TPU v7x, 32 devices: a whole 2x2x4 slice. The times are simulated.
32 devices in a mesh: grp: 2 (over y), exp: 16 (over z, x, core).
Axes of the slice: x: 2, y: 2, z: 4, core: 2. Of those that a mesh axis runs over, the one named last changes fastest.
Arguments:
- tokens: bfloat16 [4096, 2048], P(('grp', 'exp')), parts along dimension 0, may hold values from -6 to 6
- cotangent: bfloat16 [4096, 2048], P(('grp', 'exp')), parts along dimension 0, may hold values from -0.29882812 to 0.29882812
- routes: int32 [4096, 8], P(('grp', 'exp')), parts along dimension 0, may hold values from 0 to 15, all different within a row; in each aligned block of 128 rows (0 to 127, 128 to 255, ...) at most 80 rows name the same one
- combine: bfloat16 [4096, 8], P(('grp', 'exp')), parts along dimension 0, may hold values from 0.049804688 to 0.5
- doc_ids: int32 [4096], P(('grp', 'exp')), parts along dimension 0, may hold values from 0 to 3, never falling along the last dimension, each value on 1 to 1024 neighbouring positions
- w_gate: bfloat16 [16, 2048, 768], P('exp'), may hold values from -0.125 to 0.125
- w_up: bfloat16 [16, 2048, 768], P('exp'), may hold values from -0.125 to 0.125
- w_down: bfloat16 [16, 768, 2048], P('exp'), may hold values from -0.21875 to 0.21875
- proj_hidden: bfloat16 [16, 768, 64], P('exp'), may hold values from -0.21875 to 0.21875
- proj_output: bfloat16 [16, 2048, 64], P('exp'), may hold values from -6 to 6
Outputs:
- features: float32 [8, 16, 64, 64], P('grp', 'exp'), parts along dimension 0
- route_grad: float32 [4096, 8], P(('grp', 'exp')), parts along dimension 0
There are 2 independent parts, one for each index of `grp`. A program takes and returns all parts, laid end to end along the dimension named above; an argument that names none is the same for every part. Nothing has to cross between parts.
Inputs may be any that keep to these rules, and one draw needn't show every extreme that they name: `routes`: among the 128 rows of one device no expert is named more than 80 times, a bound that some block reaches; a row names 8 different experts. `doc_ids`: document ids never fall along the tokens; each of the 4 documents holds 1 to 1024 tokens, one exactly 1024.
All inputs are finite; a program needn't handle non-finite values.
Results may differ from a plain program's by a relative error of at most 0.0051.
Values may be sent and summed in bfloat16 or wider, within the bound.
No kernel may reach another device: no remote copies, remote signals or barrier semaphores. Data moves between devices by JAX's collectives and lax.ppermute only.
A program may use at most 128 MiB of HBM per device.

v0:
```python
import jax
import jax.numpy as jnp
from jax import lax
from jax.sharding import PartitionSpec as P

DOC_TOK = 512


def forward(recv_x, w_gate, w_up):
    gate_val = jnp.einsum("secd,edf->secf", recv_x, w_gate, preferred_element_type=jnp.float32)
    up_val = jnp.einsum("secd,edf->secf", recv_x, w_up, preferred_element_type=jnp.float32)
    return (jax.nn.silu(gate_val) * up_val).astype(jnp.bfloat16)


def finish(hidden, recv_dy, recv_w, w_down, proj_hidden, proj_output):
    out_val = jnp.einsum("secf,efd->secd", hidden, w_down, preferred_element_type=jnp.float32)
    slot_grad = jnp.sum(recv_dy.astype(jnp.float32) * out_val, axis=-1)
    low_side = jnp.einsum(
        "secf,efr->secr", hidden, proj_hidden, preferred_element_type=jnp.float32
    ).astype(jnp.bfloat16)
    proj_cot = jnp.einsum(
        "secd,edr->secr", recv_dy, proj_output, preferred_element_type=jnp.float32
    )
    high_side = (recv_w.astype(jnp.float32)[..., None] * proj_cot).astype(jnp.bfloat16)
    return (slot_grad, low_side, high_side)


def on_device(
    tokens, cotangent, routes, combine, doc_ids, w_gate, w_up, w_down, proj_hidden, proj_output
):
    tok_rows, chosen = routes.shape
    local_count = w_gate.shape[0]
    groups = lax.axis_size("exp")
    experts = local_count * groups
    capacity = max(2, tok_rows * chosen * 5 // (4 * experts))
    docs_count = max(2, tok_rows * groups // DOC_TOK)
    entries = tok_rows * chosen
    width = tokens.shape[1]
    flat_routes = routes.reshape(-1)
    member = (flat_routes[:, None] == jnp.arange(experts, dtype=jnp.int32)[None, :]).astype(
        jnp.int32
    )
    slot_rank = jnp.sum((jnp.cumsum(member, axis=0) - 1) * member, axis=1)
    position = flat_routes * capacity + slot_rank
    source = (
        jnp.full((experts * capacity,), -1, jnp.int32)
        .at[position]
        .set(jnp.arange(entries, dtype=jnp.int32))
    )
    filled = source >= 0
    safe_source = jnp.maximum(source, 0)
    token_of = safe_source // chosen
    send_x = jnp.where(filled[:, None], tokens[token_of], 0)
    send_dy = jnp.where(filled[:, None], cotangent[token_of], 0)
    send_w = jnp.where(filled, combine.reshape(-1)[safe_source], 0)
    send_doc = jnp.where(filled, doc_ids[token_of], -1).astype(jnp.bfloat16)
    send_x = send_x.reshape(groups, local_count, capacity, width)
    send_dy = send_dy.reshape(groups, local_count, capacity, width)
    send_w = send_w.reshape(groups, local_count, capacity)
    send_doc = send_doc.reshape(groups, local_count, capacity)
    recv_x = lax.all_to_all(send_x, "exp", split_axis=0, concat_axis=0, tiled=True)
    recv_dy = lax.all_to_all(send_dy, "exp", split_axis=0, concat_axis=0, tiled=True)
    recv_w = lax.all_to_all(send_w, "exp", split_axis=0, concat_axis=0, tiled=True)
    recv_doc = lax.all_to_all(send_doc, "exp", split_axis=0, concat_axis=0, tiled=True)
    hidden = forward(recv_x, w_gate, w_up)
    slot_grad, low_side, high_side = finish(
        hidden, recv_dy, recv_w, w_down, proj_hidden, proj_output
    )
    slot_grad, low_side, high_side, recv_doc = (slot_grad, low_side, high_side, recv_doc)
    returned = lax.all_to_all(slot_grad, "exp", split_axis=0, concat_axis=0, tiled=True)
    route_grad = returned.reshape(-1)[position].reshape(tok_rows, chosen)
    doc_table = jnp.arange(docs_count, dtype=jnp.int32).astype(jnp.bfloat16)
    onehot = (recv_doc[..., None] == doc_table).astype(jnp.bfloat16)
    spread = onehot[..., None] * low_side[..., None, :]
    feature = jnp.einsum("secdr,secq->edrq", spread, high_side, preferred_element_type=jnp.float32)
    features = jnp.transpose(feature, (1, 0, 2, 3))
    return (features, route_grad)


def solution(mesh):
    placed = (
        P(("grp", "exp"), None),
        P(("grp", "exp"), None),
        P(("grp", "exp"), None),
        P(("grp", "exp"), None),
        P(("grp", "exp")),
        P("exp", None, None),
        P("exp", None, None),
        P("exp", None, None),
        P("exp", None, None),
        P("exp", None, None),
    )
    return jax.shard_map(
        on_device,
        mesh=mesh,
        in_specs=placed,
        out_specs=(P("grp", "exp", None, None), P(("grp", "exp"), None)),
        check_vma=False,
    )
```

profile of v0, /device:TPU:0, one launch (start us, length us, event | category | flops | bytes accessed | tf_op | source)
XLA Modules:
  0.0 347.5 jit_solution(8425321726847733817)
XLA Ops:
  0.6 0.0 copy-start
  0.6 0.0 copy-start.1
  0.7 0.9 copy.35
  1.6 0.1 eq.50
  1.7 0.1 eq.46
  1.8 0.7 broadcast_multiply_fusion
  2.5 4.5 %reduce-window.6 = s32[16,8,128]{2,1,0:T(8,128)S(1)} reduce-window(s32[16,8,128]{2,1,0:T(8,128)S(1)} %fusion.51, s32[]{:T(128)} %constant.35.clone.1), window={size=1x1x128 pad=0_0x0_0x127_0}, to_apply=%region_0.0 | reduce-window | flops 2080768 | bytes 131076 | tf_op jit(solution)/shard_map/reduce-window
  7.0 0.1 slice.18
  7.1 0.1 copy.37
  7.2 0.1 copy.38
  7.3 0.1 add_add_fusion
  7.4 0.1 copy.34
  7.5 0.1 mul.60
  7.7 4.3 %scatter_custom_fusion = s32[1280]{0:T(1024)S(1)} fusion(s32[1024]{0:T(1024)S(1)} %bitcast.149, s32[1024]{0:T(1024)S(1)} %iota.16, s32[]{:T(128)} %constant.33.clone.1), kind=kCustom, calls=%fused_computation.62 | custom fusion | bytes 5124 | tf_op jit(solution)/shard_map/scatter | solution.py:48
  12.0 0.8 copy.41
  12.8 0.1 reshape.172
  12.9 8.0 %gather_fusion.2 = bf16[1280]{0:T(1024)(128)(2,1)S(1)} fusion(bf16[1024]{0:T(1024)(128)(2,1)S(1)} %reshape.172, s32[2048]{0:T(1024)S(1)} %get-tuple-element.16), kind=kCustom, calls=%fused_computation.2 | custom fusion | bytes 10240 | tf_op jit(solution)/shard_map/gather | solution.py:55
  20.9 0.0 copy-done.1
  20.9 7.6 %gather_fusion = s32[1280]{0:T(1024)S(1)} fusion(s32[128]{0:T(128)S(1)} %copy-done.1, s32[2048]{0:T(1024)S(1)} %get-tuple-element.17), kind=kCustom, calls=%fused_computation | custom fusion | bytes 15360 | tf_op jit(solution)/shard_map/gather | solution.py:56
  28.6 0.7 reshape.240
  29.3 7.4 %all-to-all-start = ((bf16[16,1,80]{2,1,0:T(2,128)(2,1)}), bf16[16,1,80]{2,1,0:T(2,128)(2,1)S(1)}, u32[]{:S(2)}, u32[]{:S(2)}) async-start(bf16[16,1,80]{2,1,0:T(2,128)(2,1)} %reshape.240), calls=%async_computation | async-start | bytes 16384 | tf_op jit(solution)/shard_map/all_to_all | solution.py:64
  36.6 0.1 broadcast_in_dim.47
  36.7 11.9 %gather_fusion.3 = bf16[1280,2048]{1,0:T(8,128)(2,1)} fusion(bf16[128,2048]{1,0:T(8,128)(2,1)} %param.11, s32[2048]{0:T(1024)S(1)} %get-tuple-element.17), kind=kCustom, calls=%fused_computation.3 | custom fusion | bytes 10490880 | tf_op jit(solution)/shard_map/gather | solution.py:54
  48.7 12.0 %gather_fusion.1 = bf16[1280,2048]{1,0:T(8,128)(2,1)} fusion(bf16[128,2048]{1,0:T(8,128)(2,1)} %param.10, s32[2048]{0:T(1024)S(1)} %get-tuple-element.17), kind=kCustom, calls=%fused_computation.1 | custom fusion | bytes 10490880 | tf_op jit(solution)/shard_map/gather | solution.py:53
  60.6 0.7 reshape.241
  61.3 0.0 all-to-all-done
  61.3 6.0 %all-to-all-start.2 = ((bf16[16,1,80]{2,1,0:T(2,128)(2,1)}), bf16[16,1,80]{2,1,0:T(2,128)(2,1)S(1)}, u32[]{:S(2)}, u32[]{:S(2)}) async-start(bf16[16,1,80]{2,1,0:T(2,128)(2,1)} %reshape.241), calls=%async_computation.2 | async-start | bytes 16384 | tf_op jit(solution)/shard_map/all_to_all | solution.py:63
  67.3 8.7 %broadcast_select_fusion.1 = (bf16[16,1,80,2048]{3,2,1,0:T(8,128)(2,1)}, bf16[16,1,80,2048]{3,2,1,0:T(8,128)(2,1)}) fusion(bf16[16,1,80,2048]{3,2,1,0:T(8,128)(2,1)} %bitcast.145, pred[16,80]{1,0:T(8,128)(4,1)S(1)} %broadcast_in_dim.47, bf16[16,1,80,2048]{3,2,1,0:T(8,128)(2,1)} %bitcast.144), kind=kLoop, calls=%fused_computation.15 | loop fusion | flops 5242880 | bytes 20972800 | tf_op jit(solution)/shard_map/jit(_where)/select_n | solution.py:53
  76.1 0.0 all-to-all-done.2
  76.1 120.8 %all_to_all.25 = bf16[16,1,80,2048]{3,2,1,0:T(8,128)(2,1)} all-to-all(bf16[16,1,80,2048]{3,2,1,0:T(8,128)(2,1)} %get-tuple-element.14), channel_id=1, replica_groups=mesh['grp'=2,'exp'=16] {'exp'}, dimensions={0} | all-to-all | bytes 10485760 | tf_op jit(solution)/shard_map/all_to_all | solution.py:61
  196.9 5.4 %all-to-all-start.3 = ((bf16[16,1,80,2048]{3,2,1,0:T(8,128)(2,1)}), bf16[16,1,80,2048]{3,2,1,0:T(8,128)(2,1)}, u32[]{:S(2)}, u32[]{:S(2)}) async-start(bf16[16,1,80,2048]{3,2,1,0:T(8,128)(2,1)} %get-tuple-element.15), calls=%async_computation.3 | async-start | bytes 10485760 | tf_op jit(solution)/shard_map/all_to_all | solution.py:62
  202.4 0.1 compare_convert_fusion
  202.5 0.0 copy-done
  202.5 0.0 copy-start.4
  202.5 6.5 %fusion.3 = f32[16,80,768]{2,1,0:T(8,128)S(1)} fusion(bf16[16,1,80,2048]{3,2,1,0:T(8,128)(2,1)} %all_to_all.25, bf16[1,2048,768]{2,1,0:T(8,128)(2,1)S(1)} %copy-done), kind=kOutput, calls=%fused_computation.10 | convolution fusion | flops 4026531840 | bytes 12320768 | tf_op jit(solution)/shard_map/secd,edf->secf/dot_general | solution.py:11
  209.0 5.8 %fusion.7 = bf16[16,1,80,768]{3,2,0,1:T(8,128)(2,1)} fusion(f32[16,80,768]{2,1,0:T(8,128)S(1)} %fusion.3, bf16[1,2048,768]{2,1,0:T(8,128)(2,1)S(1)} %copy-done.4, bf16[16,1,80,2048]{3,2,1,0:T(8,128)(2,1)S(1)} %copy-done.2), kind=kOutput, calls=%fused_computation.17 | convolution fusion | flops 4032430080 | bytes 14286848 | tf_op jit(solution)/shard_map/secd,edf->secf/dot_general | solution.py:10
  214.8 83.4 %all-to-all-done.3 = bf16[16,1,80,2048]{3,2,1,0:T(8,128)(2,1)} async-done(((bf16[16,1,80,2048]{3,2,1,0:T(8,128)(2,1)}), bf16[16,1,80,2048]{3,2,1,0:T(8,128)(2,1)}, u32[]{:S(2)}, u32[]{:S(2)}) %all-to-all-start.3) | async-done | bytes 5242912 | tf_op jit(solution)/shard_map/all_to_all | solution.py:62
  298.3 9.0 %fusion = f32[16,80]{1,0:T(8,128)} fusion(bf16[16,1,80,2048]{3,2,1,0:T(8,128)(2,1)} %all-to-all-done.3, bf16[1,768,2048]{2,1,0:T(8,128)(2,1)} %param.17, bf16[16,1,80,768]{3,2,0,1:T(8,128)(2,1)} %fusion.7), kind=kOutput, calls=%fused_computation.7 | convolution fusion | flops 4034394880 | bytes 10359808 | tf_op jit(solution)/shard_map/secf,efd->secd/dot_general | solution.py:16
  307.3 23.9 %all-to-all-start.4 = ((f32[16,1,80]{2,1,0:T(1,128)}), f32[16,1,80]{2,1,0:T(1,128)S(1)}, u32[]{:S(2)}, u32[]{:S(2)}) async-start(f32[16,1,80]{2,1,0:T(1,128)} %bitcast.43), calls=%async_computation.4 | async-start | bytes 16384 | tf_op jit(solution)/shard_map/all_to_all | solution.py:70
  331.1 2.5 fusion.27
  333.6 5.7 %fusion.39 = f32[4,1,64,64]{3,2,1,0:T(8,128)} fusion(bf16[16,1,80,2048]{3,2,1,0:T(8,128)(2,1)} %all-to-all-done.3, bf16[16,80,64]{1,2,0:T(8,128)(2,1)S(1)} %fusion.27, bf16[16,80,4]{1,0,2:T(8,128)(2,1)S(1)} %compare_convert_fusion, bf16[1,2048,64]{1,2,0:T(8,128)(2,1)} %param.19, f32[16,80]{1,0:T(8,128)S(1)} %bitcast.152), kind=kOutput, calls=%fused_computation.35 | convolution fusion | flops 377978880 | bytes 5749760 | tf_op jit(solution)/shard_map/secdr,secq->edrq/dot_general | solution.py:75
  339.3 0.0 all-to-all-done.4
  339.3 0.5 broadcast.159
  339.8 0.7 reduce.4
  340.5 0.1 reshape.178
  340.6 6.1 %gather_fusion.4 = f32[1024]{0:T(1024)S(1)} fusion(f32[1280]{0:T(1024)S(1)} %reshape.178, s32[1024]{0:T(1024)S(1)} %broadcast_clamp_fusion), kind=kCustom, calls=%fused_computation.4 | custom fusion | bytes 12288 | tf_op jit(solution)/shard_map/gather | solution.py:71
  346.7 0.1 reshape.179
  346.8 0.7 copy.46
  (19 shorter events, 0.1 us)
Async XLA Ops:
  0.6 201.9 %copy-start = (bf16[1,2048,768]{2,1,0:T(8,128)(2,1)S(1)}, bf16[1,2048,768]{2,1,0:T(8,128)(2,1)}, u32[]{:S(2)}) copy-start(bf16[1,2048,768]{2,1,0:T(8,128)(2,1)} %param.16) | copy-start | bytes 9437188
  0.6 20.3 %copy-start.1 = (s32[128]{0:T(128)S(1)}, s32[128]{0:T(128)}, u32[]{:S(2)}) copy-start(s32[128]{0:T(128)} %param.14) | copy-start | bytes 1540
  29.3 32.0 %all-to-all-start = ((bf16[16,1,80]{2,1,0:T(2,128)(2,1)}), bf16[16,1,80]{2,1,0:T(2,128)(2,1)S(1)}, u32[]{:S(2)}, u32[]{:S(2)}) async-start(bf16[16,1,80]{2,1,0:T(2,128)(2,1)} %reshape.240), calls=%async_computation | async-start | bytes 16384 | tf_op jit(solution)/shard_map/all_to_all | solution.py:64
  61.3 14.8 %all-to-all-start.2 = ((bf16[16,1,80]{2,1,0:T(2,128)(2,1)}), bf16[16,1,80]{2,1,0:T(2,128)(2,1)S(1)}, u32[]{:S(2)}, u32[]{:S(2)}) async-start(bf16[16,1,80]{2,1,0:T(2,128)(2,1)} %reshape.241), calls=%async_computation.2 | async-start | bytes 16384 | tf_op jit(solution)/shard_map/all_to_all | solution.py:63
  196.9 101.4 %all-to-all-start.3 = ((bf16[16,1,80,2048]{3,2,1,0:T(8,128)(2,1)}), bf16[16,1,80,2048]{3,2,1,0:T(8,128)(2,1)}, u32[]{:S(2)}, u32[]{:S(2)}) async-start(bf16[16,1,80,2048]{3,2,1,0:T(8,128)(2,1)} %get-tuple-element.15), calls=%async_computation.3 | async-start | bytes 10485760 | tf_op jit(solution)/shard_map/all_to_all | solution.py:62
  202.5 6.5 %copy-start.2 = (bf16[16,1,80,2048]{3,2,1,0:T(8,128)(2,1)S(1)}, bf16[16,1,80,2048]{3,2,1,0:T(8,128)(2,1)}, u32[]{:S(2)}) copy-start(bf16[16,1,80,2048]{3,2,1,0:T(8,128)(2,1)} %all_to_all.25) | copy-start | bytes 15728644
  202.5 6.5 %copy-start.4 = (bf16[1,2048,768]{2,1,0:T(8,128)(2,1)S(1)}, bf16[1,2048,768]{2,1,0:T(8,128)(2,1)}, u32[]{:S(2)}) copy-start(bf16[1,2048,768]{2,1,0:T(8,128)(2,1)} %param.15) | copy-start | bytes 9437188
  214.8 116.3 %copy-start.3 = (bf16[1,768,64]{1,2,0:T(8,128)(2,1)S(1)}, bf16[1,768,64]{1,2,0:T(8,128)(2,1)}, u32[]{:S(2)}) copy-start(bf16[1,768,64]{1,2,0:T(8,128)(2,1)} %param.18) | copy-start | bytes 294916
  307.3 32.0 %all-to-all-start.4 = ((f32[16,1,80]{2,1,0:T(1,128)}), f32[16,1,80]{2,1,0:T(1,128)S(1)}, u32[]{:S(2)}, u32[]{:S(2)}) async-start(f32[16,1,80]{2,1,0:T(1,128)} %bitcast.43), calls=%async_computation.4 | async-start | bytes 16384 | tf_op jit(solution)/shard_map/all_to_all | solution.py:70
where the time goes:
time: 348 us; the launch traced here: 347 us
  blocking collectives  121 us (35%)
  waiting for transfers between devices  83.4 us (24%)
  local copies, waits for them, and re-layouts  55.3 us (16%)
  starting transfers between devices  42.7 us (12%)
  matrix products  29.5 us (8%)
  other arithmetic  14.9 us (4%)
    all_to_all x1, blocking collectives, on_device(): lax.all_to_all(send_x, 'exp', split_axis=0, concat_axis=0, tiled=True)  121 us
    all_to_all x1, waiting for transfers between devices, on_device(): lax.all_to_all(send_dy, 'exp', split_axis=0, concat_axis=0, tiled=True)  83.4 us
    all_to_all x1, starting transfers between devices, on_device(): lax.all_to_all(slot_grad, 'exp', split_axis=0, concat_axis=0, tiled=True)  23.9 us
    gather x1, local copies, waits for them, and re-layouts, on_device(): send_x = jnp.where(filled[:, None], tokens[token_of], 0)  12 us
    gather x1, local copies, waits for them, and re-layouts, on_device(): send_dy = jnp.where(filled[:, None], cotangent[token_of], 0)  11.9 us
    dot_general x1, matrix products, finish(): jnp.einsum('secf,efd->secd', hidden, w_down, preferred_element_type=jnp.f...  9 us
    select_n x1, other arithmetic, on_device(): send_x = jnp.where(filled[:, None], tokens[token_of], 0)  8.73 us
    gather x1, local copies, waits for them, and re-layouts, on_device(): send_w = jnp.where(filled, combine.reshape(-1)[safe_source], 0)  7.97 us
  transfers between devices with their start and end apart: 4, of which 1 were waited for; matrix products, arithmetic and copies ran while one was open for 16% of the time, Pallas kernels for 0%

commit v1 on v0

v1 whole, which is shorter than its diff:
```python
import jax
import jax.numpy as jnp
from jax import lax
from jax.sharding import PartitionSpec as P

DOC_TOK = 512


def swiglu(rows, w_gate, w_up):
    gate_val = jnp.dot(rows, w_gate, preferred_element_type=jnp.float32)
    up_val = jnp.dot(rows, w_up, preferred_element_type=jnp.float32)
    return (jax.nn.silu(gate_val) * up_val).astype(jnp.bfloat16)


def finish(hidden, rows_dy, rows_w, rows_doc, w_down, proj_hidden, proj_output, docs_count):
    out_val = jnp.dot(hidden, w_down, preferred_element_type=jnp.float32)
    grad = jnp.sum(rows_dy.astype(jnp.float32) * out_val, axis=-1)
    low_side = jnp.dot(hidden, proj_hidden, preferred_element_type=jnp.float32).astype(
        jnp.bfloat16
    )
    proj_cot = jnp.dot(rows_dy, proj_output, preferred_element_type=jnp.float32)
    high_side = (rows_w.astype(jnp.float32)[:, None] * proj_cot).astype(jnp.bfloat16)
    doc_table = jnp.arange(docs_count, dtype=jnp.int32).astype(jnp.bfloat16)
    onehot = (rows_doc[:, None] == doc_table).astype(jnp.bfloat16)
    spread = onehot[:, :, None] * low_side[:, None, :]
    spread = spread.reshape(spread.shape[0], -1)
    feature = lax.dot_general(
        spread, high_side, (((0,), (0,)), ((), ())), preferred_element_type=jnp.float32
    )
    return grad, feature.reshape(docs_count, low_side.shape[1], high_side.shape[1])


def pick_own(returned, routes):
    experts = returned.shape[0]
    table = jnp.arange(experts, dtype=jnp.int32)
    hit = routes[:, :, None] == table
    return jnp.sum(jnp.where(hit, returned.T[:, None, :], 0.0), axis=-1)


def by_gather(
    tokens, cotangent, routes, combine, doc_ids, w_gate, w_up, w_down, proj_hidden, proj_output
):
    tok_rows, chosen = routes.shape
    groups = lax.axis_size("exp")
    docs_count = max(2, tok_rows * groups // DOC_TOK)
    me = lax.axis_index("exp")
    table = jnp.arange(groups, dtype=jnp.int32)
    weight = jnp.sum(
        jnp.where(routes[None, :, :] == table[:, None, None], combine[None, :, :], 0), axis=-1
    ).astype(jnp.bfloat16)
    meta = jnp.concatenate([weight, doc_ids.astype(jnp.bfloat16)[None, :]], axis=0)
    all_meta = lax.all_gather(meta, "exp")
    all_x = lax.all_gather(tokens, "exp", tiled=True)
    all_dy = lax.all_gather(cotangent, "exp", tiled=True)
    all_w = lax.dynamic_index_in_dim(all_meta, me, axis=1, keepdims=False).reshape(-1)
    all_doc = all_meta[:, groups, :].reshape(-1)
    hidden = swiglu(all_x, w_gate[0], w_up[0])
    grad, feature = finish(
        hidden, all_dy, all_w, all_doc, w_down[0], proj_hidden[0], proj_output[0], docs_count
    )
    returned = lax.all_to_all(
        grad.reshape(groups, tok_rows), "exp", split_axis=0, concat_axis=0, tiled=True
    )
    return feature[:, None], pick_own(returned, routes)


def by_routing(
    tokens, cotangent, routes, combine, doc_ids, w_gate, w_up, w_down, proj_hidden, proj_output
):
    tok_rows, chosen = routes.shape
    local_count = w_gate.shape[0]
    groups = lax.axis_size("exp")
    experts = local_count * groups
    capacity = max(2, tok_rows * chosen * 5 // (4 * experts))
    docs_count = max(2, tok_rows * groups // DOC_TOK)
    entries = tok_rows * chosen
    width = tokens.shape[1]
    flat_routes = routes.reshape(-1)
    member = (flat_routes[:, None] == jnp.arange(experts, dtype=jnp.int32)[None, :]).astype(
        jnp.int32
    )
    slot_rank = jnp.sum((jnp.cumsum(member, axis=0) - 1) * member, axis=1)
    position = flat_routes * capacity + slot_rank
    source = (
        jnp.full((experts * capacity,), -1, jnp.int32)
        .at[position]
        .set(jnp.arange(entries, dtype=jnp.int32))
    )
    filled = source >= 0
    safe_source = jnp.maximum(source, 0)
    token_of = safe_source // chosen
    send_x = jnp.where(filled[:, None], tokens[token_of], 0)
    send_dy = jnp.where(filled[:, None], cotangent[token_of], 0)
    send_w = jnp.where(filled, combine.reshape(-1)[safe_source], 0)
    send_doc = jnp.where(filled, doc_ids[token_of], -1).astype(jnp.bfloat16)

    def exchange(array):
        array = array.reshape((groups, local_count, capacity) + array.shape[1:])
        return lax.all_to_all(array, "exp", split_axis=0, concat_axis=0, tiled=True)

    recv_x, recv_dy, recv_w, recv_doc = (
        exchange(send_x),
        exchange(send_dy),
        exchange(send_w),
        exchange(send_doc),
    )
    slots = groups * capacity
    grads, feats = [], []
    for e in range(local_count):
        hidden = swiglu(recv_x[:, e].reshape(slots, width), w_gate[e], w_up[e])
        grad, feature = finish(
            hidden,
            recv_dy[:, e].reshape(slots, width),
            recv_w[:, e].reshape(slots),
            recv_doc[:, e].reshape(slots),
            w_down[e],
            proj_hidden[e],
            proj_output[e],
            docs_count,
        )
        grads.append(grad.reshape(groups, capacity))
        feats.append(feature)
    slot_grad = jnp.stack(grads, axis=1)
    returned = lax.all_to_all(slot_grad, "exp", split_axis=0, concat_axis=0, tiled=True)
    route_grad = returned.reshape(-1)[position].reshape(tok_rows, chosen)
    return jnp.stack(feats, axis=1), route_grad


def on_device(tokens, cotangent, routes, combine, doc_ids, w_gate, *rest):
    tok_rows, chosen = routes.shape
    experts = w_gate.shape[0] * lax.axis_size("exp")
    dense = w_gate.shape[0] == 1 and 4 * chosen >= experts
    plan = by_gather if dense else by_routing
    return plan(tokens, cotangent, routes, combine, doc_ids, w_gate, *rest)


def solution(mesh):
    placed = (
        P(("grp", "exp"), None),
        P(("grp", "exp"), None),
        P(("grp", "exp"), None),
        P(("grp", "exp"), None),
        P(("grp", "exp")),
        P("exp", None, None),
        P("exp", None, None),
        P("exp", None, None),
        P("exp", None, None),
        P("exp", None, None),
    )
    return jax.shard_map(
        on_device,
        mesh=mesh,
        in_specs=placed,
        out_specs=(P("grp", "exp", None, None), P(("grp", "exp"), None)),
        check_vma=False,
    )
```

time: 348 us -> 196 us (0.56)
  blocking collectives: 121 us -> 23.9 us
  local copies, waits for them, and re-layouts: 55.3 us -> 3.96 us
  starting transfers between devices: 42.7 us -> 3.64 us
  waiting for transfers between devices: 83.4 us -> 112 us
  between operations: 0.89 us -> 14.1 us
  other arithmetic: 14.9 us -> 2.11 us
  matrix products: 29.5 us -> 35.8 us
    all_to_all x1 -> x0, blocking collectives: 121 us -> none  [on_device(): lax.all_to_all(send_x, 'exp', split_axis=0, concat_axis=0, tiled=True)]
    all_gather x0 -> x2, waiting for transfers between devices: none -> 111 us  [the longest x1 58.4 us: by_gather(): all_dy = lax.all_gather(cotangent, 'exp', tiled=True)]
    all_to_all x4 -> x1, waiting for transfers between devices: 83.4 us -> 0.37 us  [by_gather(): lax.all_to_all(grad.reshape(groups, tok_rows), 'exp', split_axis=0, conca...]
    gather x5 -> x0, local copies, waits for them, and re-layouts: 45.6 us -> none  [the longest x1 12 us: on_device(): send_x = jnp.where(filled[:, None], tokens[token_of], 0)]
    all_to_all x4 -> x1, starting transfers between devices: 42.7 us -> 3.56 us  [by_gather(): lax.all_to_all(grad.reshape(groups, tok_rows), 'exp', split_axis=0, conca...]
    all_gather x0 -> x1, blocking collectives: none -> 23.9 us  [by_gather(): all_meta = lax.all_gather(meta, 'exp')]
    select_n x3 -> x0, other arithmetic: 8.75 us -> none  [the longest x1 8.73 us: on_device(): send_x = jnp.where(filled[:, None], tokens[token_of], 0)]
    dot_general x5, matrix products: 29.5 us -> 35.8 us  [the longest x1 11.5 us: finish(): out_val = jnp.dot(hidden, w_down, preferred_element_type=jnp.float32)]
  transfers between devices with their start and end apart: 4 -> 3, of which waited for: 1 -> 3; matrix products, arithmetic and copies ran while one was open for 16% -> 14% of each run, Pallas kernels for 0% -> 0%
where the time goes in v1:
time: 196 us; the launch traced here: 195 us
  waiting for transfers between devices  112 us (57%)
  matrix products  35.8 us (18%)
  blocking collectives  23.9 us (12%)
  between operations  14.1 us (7%)
  local copies, waits for them, and re-layouts  3.96 us (2%)
  starting transfers between devices  3.64 us (2%)
  other arithmetic  2.11 us (1%)
    all_gather x1, waiting for transfers between devices, by_gather(): all_dy = lax.all_gather(cotangent, 'exp', tiled=True)  58.4 us
    all_gather x1, waiting for transfers between devices, by_gather(): all_x = lax.all_gather(tokens, 'exp', tiled=True)  52.4 us
    all_gather x1, blocking collectives, by_gather(): all_meta = lax.all_gather(meta, 'exp')  23.9 us
    dot_general x1, matrix products, finish(): out_val = jnp.dot(hidden, w_down, preferred_element_type=jnp.float32)  11.5 us
    dot_general x1, matrix products, swiglu(): gate_val = jnp.dot(rows, w_gate, preferred_element_type=jnp.float32)  9.85 us
    dot_general x1, matrix products, swiglu(): up_val = jnp.dot(rows, w_up, preferred_element_type=jnp.float32)  7.38 us
    dot_general x1, matrix products, finish(): lax.dot_general(spread, high_side, (((0,), (0,)), ((), ())), preferred_el...  6 us
    unnamed x14, local copies, waits for them, and re-layouts  3.96 us
  transfers between devices with their start and end apart: 3, of which 3 were waited for; matrix products, arithmetic and copies ran while one was open for 14% of the time, Pallas kernels for 0%

profile of v1, /device:TPU:0, one launch (start us, length us, event | category | flops | bytes accessed | tf_op | source)
XLA Modules:
  0.0 195.4 jit_solution(6743250790378883952)
XLA Ops:
  7.2 0.0 copy-start
  7.2 0.0 all-gather.5.cloned.1.call-start
  7.2 0.7 all-gather.5.cloned.1.call-update
  7.9 0.0 all-gather.7.cloned.1.call-start
  8.0 2.2 %copy.38 = bf16[128,2048]{0,1:T(8,128)(2,1)} copy(bf16[128,2048]{1,0:T(8,128)(2,1)} %param.11) | data formatting | bytes 1048576 | tf_op args[1]
  10.2 0.0 all-gather.7.cloned.1.call-update
  10.2 0.7 fusion.15
  10.9 0.7 convert_bitcast_fusion
  11.6 23.9 %all-gather.1 = bf16[16,17,128]{2,1,0:T(8,128)(2,1)S(1)} all-gather(bf16[1,17,128]{2,1,0:T(8,128)(2,1)S(1)} %maximum_bitcast_fusion), channel_id=2, replica_groups=mesh['grp'=2,'exp'=16] {'exp'}, dimensions={0}, use_global_device_ids=true | all-gather | bytes 73984 | tf_op jit(solution)/shard_map/all_gather | solution.py:52
  35.6 0.1 compare_convert_fusion
  35.6 52.4 %all-gather.5.cloned.1.call-done = bf16[2048,2048]{1,0:T(8,128)(2,1)} async-done(((bf16[128,2048]{1,0:T(8,128)(2,1)}), bf16[2048,2048]{1,0:T(8,128)(2,1)}) %all-gather.5.cloned.1.call-update) | async-done | bytes 8388624 | tf_op jit(solution)/shard_map/all_gather | solution.py:53
  88.0 0.0 copy-done
  88.0 0.0 copy-start.4
  88.0 0.0 copy-start.5
  88.0 9.8 %fusion.2 = f32[2048,768]{1,0:T(8,128)S(1)} fusion(bf16[2048,2048]{1,0:T(8,128)(2,1)} %all-gather.5.cloned.1.call-done, bf16[1,2048,768]{2,1,0:T(8,128)(2,1)S(1)} %copy-done), kind=kOutput, calls=%fused_computation.4 | convolution fusion | flops 6442450944 | bytes 17825792 | tf_op jit(solution)/shard_map/dot_general | solution.py:10
  97.9 0.0 copy-done.4
  97.9 0.0 copy-done.5
  97.9 0.0 copy-start.2
  97.9 7.4 %multiply_convert_fusion = bf16[2048,768]{1,0:T(8,128)(2,1)S(1)} fusion(f32[2048,768]{1,0:T(8,128)S(1)} %fusion.2, bf16[2048,2048]{1,0:T(8,128)(2,1)S(1)} %copy-done.4, bf16[1,2048,768]{2,1,0:T(8,128)(2,1)S(1)} %copy-done.5), kind=kOutput, calls=%fused_computation.1 | convolution fusion | flops 6451888128 | bytes 20971520 | tf_op jit(solution)/shard_map/dot_general | solution.py:11
  105.3 0.0 copy-start.1
  105.3 1.7 copy-done.1
  107.0 0.0 copy-done.2
  107.0 1.1 convolution_convert_fusion
  108.1 58.4 %all-gather.7.cloned.1.call-done = bf16[2048,2048]{0,1:T(8,128)(2,1)} async-done(((bf16[128,2048]{0,1:T(8,128)(2,1)}), bf16[2048,2048]{0,1:T(8,128)(2,1)}) %all-gather.7.cloned.1.call-update) | async-done | bytes 8388624 | tf_op jit(solution)/shard_map/all_gather | solution.py:54
  166.5 11.5 %multiply_reduce_fusion = f32[2048]{0:T(1024)} fusion(bf16[2048,2048]{0,1:T(8,128)(2,1)} %all-gather.7.cloned.1.call-done, bf16[2048,768]{1,0:T(8,128)(2,1)} %copy-done.1, bf16[1,768,2048]{2,1,0:T(8,128)(2,1)} %param.17), kind=kOutput, calls=%fused_computation | convolution fusion | flops 6455031808 | bytes 14688256 | tf_op jit(solution)/shard_map/dot_general | solution.py:16
  178.0 0.0 copy-start.3
  178.0 3.6 %all-to-all-start = ((f32[16,1,128]{2,1,0:T(1,128)}), f32[16,1,128]{2,1,0:T(1,128)S(1)}, u32[]{:S(2)}, u32[]{:S(2)}) async-start(f32[16,1,128]{2,1,0:T(1,128)} %bitcast.16), calls=%async_computation | async-start | bytes 16384 | tf_op jit(solution)/shard_map/all_to_all | solution.py:61
  181.6 6.0 %convolution_bitcast_fusion = f32[4,1,64,64]{3,2,1,0:T(8,128)} fusion(bf16[2048,2048]{0,1:T(8,128)(2,1)} %all-gather.7.cloned.1.call-done, bf16[2048,64]{0,1:T(8,128)(2,1)S(1)} %convolution_convert_fusion, bf16[2048,4]{0,1:T(4,128)(2,1)S(1)} %compare_convert_fusion, bf16[1,2048,64]{1,2,0:T(8,128)(2,1)} %param.19, f32[2048]{0:T(1024)S(1)} %bitcast.50), kind=kOutput, calls=%fused_computation.10 | convolution fusion | flops 604766208 | bytes 9003008 | tf_op jit(solution)/shard_map/dot_general | solution.py:27
  187.6 0.4 all-to-all-done
  188.0 0.0 copy-done.3
  188.0 0.6 select_reduce_fusion
  (4 shorter events, 0.0 us)
Async XLA Ops:
  7.2 80.8 %copy-start = (bf16[1,2048,768]{2,1,0:T(8,128)(2,1)S(1)}, bf16[1,2048,768]{2,1,0:T(8,128)(2,1)}, u32[]{:S(2)}) copy-start(bf16[1,2048,768]{2,1,0:T(8,128)(2,1)} %param.15) | copy-start | bytes 9437188
  7.2 80.8 %all-gather.5.cloned.1.call-start = ((), (), s32[]{:S(2)}) async-start(), calls=%async_computation.1 | async-start | bytes 8912896 | tf_op jit(solution)/shard_map/all_gather | solution.py:53
  7.9 158.6 %all-gather.7.cloned.1.call-start = ((), (), s32[]{:S(2)}) async-start(), calls=%async_computation.2 | async-start | bytes 8912896 | tf_op jit(solution)/shard_map/all_gather | solution.py:54
  88.0 9.9 %copy-start.4 = (bf16[2048,2048]{1,0:T(8,128)(2,1)S(1)}, bf16[2048,2048]{1,0:T(8,128)(2,1)}, u32[]{:S(2)}) copy-start(bf16[2048,2048]{1,0:T(8,128)(2,1)} %all-gather.5.cloned.1.call-done) | copy-start | bytes 25165828
  88.0 9.9 %copy-start.5 = (bf16[1,2048,768]{2,1,0:T(8,128)(2,1)S(1)}, bf16[1,2048,768]{2,1,0:T(8,128)(2,1)}, u32[]{:S(2)}) copy-start(bf16[1,2048,768]{2,1,0:T(8,128)(2,1)} %param.16) | copy-start | bytes 9437188
  97.9 9.1 %copy-start.2 = (bf16[1,768,64]{1,2,0:T(8,128)(2,1)S(1)}, bf16[1,768,64]{1,2,0:T(8,128)(2,1)}, u32[]{:S(2)}) copy-start(bf16[1,768,64]{1,2,0:T(8,128)(2,1)} %param.18) | copy-start | bytes 294916
  105.3 1.7 copy-start.1
  178.0 9.9 %copy-start.3 = (s32[128,8]{0,1:T(8,128)S(1)}, s32[128,8]{0,1:T(8,128)}, u32[]{:S(2)}) copy-start(s32[128,8]{0,1:T(8,128)} %param.12) | copy-start | bytes 12292
  178.0 9.9 %all-to-all-start = ((f32[16,1,128]{2,1,0:T(1,128)}), f32[16,1,128]{2,1,0:T(1,128)S(1)}, u32[]{:S(2)}, u32[]{:S(2)}) async-start(f32[16,1,128]{2,1,0:T(1,128)} %bitcast.16), calls=%async_computation | async-start | bytes 16384 | tf_op jit(solution)/shard_map/all_to_all | solution.py:61
Sparse Core Ops, SparseCore 0:
  10.2 77.7 all-gather.4
  90.1 76.3 all-gather.6

commit v2 on v1

--- a/solution.py
+++ b/solution.py
@@ -1,5 +1,6 @@
 import jax
 import jax.numpy as jnp
+import numpy as np
 from jax import lax
 from jax.sharding import PartitionSpec as P
 
@@ -37,30 +38,95 @@
     return jnp.sum(jnp.where(hit, returned.T[:, None, :], 0.0), axis=-1)
 
 
-def by_gather(
+def by_ring(
     tokens, cotangent, routes, combine, doc_ids, w_gate, w_up, w_down, proj_hidden, proj_output
 ):
     tok_rows, chosen = routes.shape
     groups = lax.axis_size("exp")
     docs_count = max(2, tok_rows * groups // DOC_TOK)
+    chips = groups // 2
+    half = chips // 2
+    ring = list(range(0, chips, 2)) + list(range(chips - 1, 0, -2))
+    onward = []
+    for place in range(chips):
+        onward.append((2 * ring[place], 2 * ring[(place + 1) % chips]))
+        onward.append((2 * ring[place] + 1, 2 * ring[place - 1] + 1))
+    across = [(i, i ^ 1) for i in range(groups)]
+
+    def hop(block):
+        return lax.ppermute(block, "exp", onward)
+
+    def swap(block):
+        return lax.ppermute(block, "exp", across)
+
+    orders = np.zeros((groups, groups), np.int32)
+    for place in range(chips):
+        for core in range(2):
+            way = 1 - 2 * core
+
+            def owner(steps, which):
+                return 2 * ring[(place + steps) % chips] + which
+
+            order = [owner(0, core), owner(0, 1 - core)]
+            for step in range(1, half + 1):
+                near, far = -step * way, step * way
+                if step < half:
+                    order += [owner(near, core), owner(near, 1 - core)]
+                    order += [owner(far, 1 - core), owner(far, core)]
+                else:
+                    order += [owner(near, core), owner(far, 1 - core)]
+            orders[owner(0, core)] = order
     me = lax.axis_index("exp")
+    mine = lax.dynamic_index_in_dim(jnp.asarray(orders), me, axis=0, keepdims=False)
+    owned = mine[:, None] == jnp.arange(groups, dtype=jnp.int32)
+
     table = jnp.arange(groups, dtype=jnp.int32)
     weight = jnp.sum(
         jnp.where(routes[None, :, :] == table[:, None, None], combine[None, :, :], 0), axis=-1
     ).astype(jnp.bfloat16)
-    meta = jnp.concatenate([weight, doc_ids.astype(jnp.bfloat16)[None, :]], axis=0)
-    all_meta = lax.all_gather(meta, "exp")
-    all_x = lax.all_gather(tokens, "exp", tiled=True)
-    all_dy = lax.all_gather(cotangent, "exp", tiled=True)
-    all_w = lax.dynamic_index_in_dim(all_meta, me, axis=1, keepdims=False).reshape(-1)
-    all_doc = all_meta[:, groups, :].reshape(-1)
-    hidden = swiglu(all_x, w_gate[0], w_up[0])
-    grad, feature = finish(
-        hidden, all_dy, all_w, all_doc, w_down[0], proj_hidden[0], proj_output[0], docs_count
-    )
-    returned = lax.all_to_all(
-        grad.reshape(groups, tok_rows), "exp", split_axis=0, concat_axis=0, tiled=True
-    )
+    own_doc = jnp.broadcast_to(doc_ids.astype(jnp.bfloat16)[None, :], weight.shape)
+    meta = lax.all_to_all(
+        jnp.stack([weight, own_doc], axis=1), "exp", split_axis=0, concat_axis=0, tiled=True
+    )
+    meta = jnp.sum(
+        jnp.where(owned[:, :, None, None], meta[None].astype(jnp.float32), 0.0), axis=1
+    ).astype(jnp.bfloat16)
+
+    sets = [[(tokens, cotangent)]]
+    last = [(tokens, cotangent)]
+    beside = tuple(swap(block) for block in last[0])
+    sets[0].append(beside)
+    last.append(beside)
+    for step in range(1, half + 1):
+        if step == half:
+            last = last[:1]
+        x_in = [hop(pair[0]) for pair in last]
+        dy_in = [hop(pair[1]) for pair in last]
+        last = list(zip(x_in, dy_in))
+        sets.append(last + [(swap(pair[0]), swap(pair[1])) for pair in last])
+
+    grads, feature, begin = [], 0.0, 0
+    for blocks in sets:
+        x = jnp.concatenate([pair[0] for pair in blocks], axis=0)
+        dy = jnp.concatenate([pair[1] for pair in blocks], axis=0)
+        part = meta[begin : begin + len(blocks)]
+        begin += len(blocks)
+        hidden = swiglu(x, w_gate[0], w_up[0])
+        grad, term = finish(
+            hidden,
+            dy,
+            part[:, 0].reshape(-1),
+            part[:, 1].reshape(-1),
+            w_down[0],
+            proj_hidden[0],
+            proj_output[0],
+            docs_count,
+        )
+        grads.append(grad.reshape(len(blocks), tok_rows))
+        feature = feature + term
+    grads = jnp.concatenate(grads, axis=0)
+    grads = jnp.sum(jnp.where(owned[:, :, None], grads[:, None, :], 0.0), axis=0)
+    returned = lax.all_to_all(grads, "exp", split_axis=0, concat_axis=0, tiled=True)
     return feature[:, None], pick_own(returned, routes)
 
 
@@ -129,8 +195,8 @@
 def on_device(tokens, cotangent, routes, combine, doc_ids, w_gate, *rest):
     tok_rows, chosen = routes.shape
     experts = w_gate.shape[0] * lax.axis_size("exp")
-    dense = w_gate.shape[0] == 1 and 4 * chosen >= experts
-    plan = by_gather if dense else by_routing
+    dense = w_gate.shape[0] == 1 and 4 * chosen >= experts and experts % 4 == 0
+    plan = by_ring if dense else by_routing
     return plan(tokens, cotangent, routes, combine, doc_ids, w_gate, *rest)
 
 

time: 196 us -> 159 us (0.81)
  waiting for transfers between devices: 112 us -> 30.9 us
  local copies, waits for them, and re-layouts: 3.96 us -> 42.2 us
  blocking collectives: 23.9 us -> 0 us
  starting transfers between devices: 3.64 us -> 25.7 us
  matrix products: 35.8 us -> 52.6 us
  between operations: 14.1 us -> 1.19 us
  other arithmetic: 2.11 us -> 4.87 us
    all_gather x2 -> x0, waiting for transfers between devices: 111 us -> none  [the longest x1 58.4 us: by_gather(): all_dy = lax.all_gather(cotangent, 'exp', tiled=True)]
    ppermute x0 -> x30, waiting for transfers between devices: none -> 27.5 us  [the longest x14 27.5 us: hop(): return lax.ppermute(block, 'exp', onward)]
    unnamed x14 -> x74, local copies, waits for them, and re-layouts: 3.96 us -> 30.9 us
    all_gather x1 -> x0, blocking collectives: 23.9 us -> none  [by_gather(): all_meta = lax.all_gather(meta, 'exp')]
    ppermute x0 -> x30, starting transfers between devices: none -> 17.2 us  [the longest x14 14 us: hop(): return lax.ppermute(block, 'exp', onward)]
    concatenate x0 -> x11, local copies, waits for them, and re-layouts: none -> 10 us  [the longest x5 5.77 us: by_ring(): dy = jnp.concatenate([pair[1] for pair in blocks], axis=0)]
    dot_general x1 -> x5, matrix products: 6 us -> 15.1 us  [finish(): lax.dot_general(spread, high_side, (((0,), (0,)), ((), ())), preferred_el...]
    dot_general x1 -> x5, matrix products: 11.5 us -> 16.5 us  [finish(): out_val = jnp.dot(hidden, w_down, preferred_element_type=jnp.float32)]
  transfers between devices with their start and end apart: 3 -> 32, of which waited for: 3 -> 7; matrix products, arithmetic and copies ran while one was open for 14% -> 61% of each run, Pallas kernels for 0% -> 0%
where the time goes in v2:
time: 159 us; the launch traced here: 157 us
  matrix products  52.6 us (33%)
  local copies, waits for them, and re-layouts  42.2 us (27%)
  waiting for transfers between devices  30.9 us (19%)
  starting transfers between devices  25.7 us (16%)
  other arithmetic  4.87 us (3%)
    unnamed x74, local copies, waits for them, and re-layouts  30.9 us
    ppermute x14, waiting for transfers between devices, hop(): return lax.ppermute(block, 'exp', onward)  27.5 us
    dot_general x5, matrix products, finish(): out_val = jnp.dot(hidden, w_down, preferred_element_type=jnp.float32)  16.5 us
    dot_general x5, matrix products, finish(): lax.dot_general(spread, high_side, (((0,), (0,)), ((), ())), preferred_el...  15.1 us
    ppermute x14, starting transfers between devices, hop(): return lax.ppermute(block, 'exp', onward)  14 us
    dot_general x5, matrix products, swiglu(): gate_val = jnp.dot(rows, w_gate, preferred_element_type=jnp.float32)  8.77 us
    dot_general x5, matrix products, swiglu(): up_val = jnp.dot(rows, w_up, preferred_element_type=jnp.float32)  7.76 us
    concatenate x5, local copies, waits for them, and re-layouts, by_ring(): dy = jnp.concatenate([pair[1] for pair in blocks], axis=0)  5.77 us
  transfers between devices with their start and end apart: 32, of which 7 were waited for; matrix products, arithmetic and copies ran while one was open for 61% of the time, Pallas kernels for 0%

profile of v2, /device:TPU:0, one launch (start us, length us, event | category | flops | bytes accessed | tf_op | source)
XLA Modules:
  0.0 157.5 jit_solution(16477200371548394537)
XLA Ops:
  0.6 3.1 %collective-permute-start.2 = (bf16[128,2048]{1,0:T(8,128)(2,1)}, bf16[128,2048]{1,0:T(8,128)(2,1)}, u32[]{:S(2)}, u32[]{:S(2)}) collective-permute-start(bf16[128,2048]{1,0:T(8,128)(2,1)} %param.11), channel_id=1, source_target_pairs={{0,4},{1,3},{4,8},{5,1},{8,12},{9,5},{12,14},{13,9},{14,10},{15,13... | collective-permute-start | bytes 1572872 | tf_op jit(solution)/shard_map/ppermute | solution.py:57
  3.7 1.6 %collective-permute-start.6 = (bf16[128,2048]{1,0:T(8,128)(2,1)}, bf16[128,2048]{1,0:T(8,128)(2,1)}, u32[]{:S(2)}, u32[]{:S(2)}) collective-permute-start(bf16[128,2048]{1,0:T(8,128)(2,1)} %param.12), channel_id=1, source_target_pairs={{0,4},{1,3},{4,8},{5,1},{8,12},{9,5},{12,14},{13,9},{14,10},{15,13... | collective-permute-start | bytes 1572872 | tf_op jit(solution)/shard_map/ppermute | solution.py:57
  7.3 5.0 %all-to-all-start = ((bf16[16,2,128]{2,1,0:T(2,128)(2,1)}), bf16[16,2,128]{2,1,0:T(2,128)(2,1)S(1)}, u32[]{:S(2)}, u32[]{:S(2)}) async-start(bf16[16,2,128]{2,1,0:T(2,128)(2,1)} %copy.32), calls=%async_computation | async-start | bytes 16384 | tf_op jit(solution)/shard_map/all_to_all | solution.py:88
  12.3 1.9 %constant_dynamic-update-slice_fusion.1 = bf16[256,2048]{1,0:T(8,128)(2,1)} fusion(bf16[128,2048]{1,0:T(8,128)(2,1)} %param.11), kind=kLoop, calls=%fused_computation.97 | loop fusion | bytes 1048576
  14.2 1.9 %constant_dynamic-update-slice_fusion.3 = bf16[256,2048]{1,0:T(8,128)(2,1)} fusion(bf16[128,2048]{1,0:T(8,128)(2,1)} %param.12), kind=kLoop, calls=%fused_computation.99 | loop fusion | bytes 1048576
  16.9 3.3 %all-to-all-done = bf16[16,2,128]{2,1,0:T(2,128)(2,1)S(1)} async-done(((bf16[16,2,128]{2,1,0:T(2,128)(2,1)}), bf16[16,2,128]{2,1,0:T(2,128)(2,1)S(1)}, u32[]{:S(2)}, u32[]{:S(2)}) %all-to-all-start) | async-done | bytes 8224 | tf_op jit(solution)/shard_map/all_to_all | solution.py:88
  22.3 1.9 %constant_dynamic-update-slice_fusion = bf16[256,2048]{1,0:T(8,128)(2,1)} fusion(bf16[256,2048]{1,0:T(8,128)(2,1)} %constant_dynamic-update-slice_fusion.1, bf16[128,2048]{1,0:T(8,128)(2,1)} %collective-permute-done), kind=kLoop, calls=%fused_computation.96 | loop fusion | bytes 1048576 | tf_op jit(solution)/shard_map/concatenate | solution.py:110
  24.2 2.3 %fusion.28 = f32[256,768]{1,0:T(8,128)S(1)} fusion(bf16[256,2048]{1,0:T(8,128)(2,1)} %constant_dynamic-update-slice_fusion, bf16[1,2048,768]{2,1,0:T(8,128)(2,1)S(1)} %copy-done), kind=kOutput, calls=%fused_computation.31 | convolution fusion | flops 805306368 | bytes 4980736 | tf_op jit(solution)/shard_map/dot_general | solution.py:11
  28.2 1.1 constant_dynamic-update-slice_fusion.2
  29.4 1.7 %multiply_reduce_fusion.4 = f32[256]{0:T(256)} fusion(bf16[256,2048]{1,0:T(8,128)(2,1)S(1)} %constant_dynamic-update-slice_fusion.2, bf16[256,768]{1,0:T(8,128)(2,1)S(1)} %multiply_convert_fusion.4, bf16[1,768,2048]{2,1,0:T(8,128)(2,1)S(1)} %copy-done.24), kind=kOutput, calls=%fused_computation.34 | convolution fusion | flops 806878976 | bytes 4588544 | tf_op jit(solution)/shard_map/dot_general | solution.py:17
  32.7 1.5 collective-permute-start.14
  35.4 1.9 %constant_dynamic-update-slice_fusion.11 = bf16[512,2048]{1,0:T(8,128)(2,1)} fusion(bf16[128,2048]{1,0:T(8,128)(2,1)} %collective-permute-done.6), kind=kLoop, calls=%fused_computation.107 | loop fusion | bytes 1048576
  37.9 3.8 %collective-permute-done.3 = bf16[128,2048]{1,0:T(8,128)(2,1)S(1)} collective-permute-done((bf16[128,2048]{1,0:T(8,128)(2,1)}, bf16[128,2048]{1,0:T(8,128)(2,1)S(1)}, u32[]{:S(2)}, u32[]{:S(2)}) %collective-permute-start.3) | collective-permute-done | bytes 524320 | tf_op jit(solution)/shard_map/ppermute | solution.py:57
  42.2 10.8 %collective-permute-done.14 = bf16[128,2048]{1,0:T(8,128)(2,1)} collective-permute-done((bf16[128,2048]{1,0:T(8,128)(2,1)}, bf16[128,2048]{1,0:T(8,128)(2,1)}, u32[]{:S(2)}, u32[]{:S(2)}) %collective-permute-start.14) | collective-permute-done | bytes 524320 | tf_op jit(solution)/shard_map/ppermute | solution.py:57
  53.5 1.9 %constant_dynamic-update-slice_fusion.19 = bf16[512,2048]{1,0:T(8,128)(2,1)} fusion(bf16[128,2048]{1,0:T(8,128)(2,1)} %collective-permute-done.14), kind=kLoop, calls=%fused_computation.115 | loop fusion | bytes 1048576
  59.5 1.8 %fusion.26 = f32[512,768]{1,0:T(8,128)S(1)} fusion(bf16[512,2048]{1,0:T(8,128)(2,1)S(1)} %constant_dynamic-update-slice_fusion.4, bf16[1,2048,768]{2,1,0:T(8,128)(2,1)S(1)} %copy-done), kind=kOutput, calls=%fused_computation.29 | convolution fusion | flops 1610612736 | bytes 6815744 | tf_op jit(solution)/shard_map/dot_general | solution.py:11
  61.3 1.9 %multiply_convert_fusion.2 = bf16[512,768]{1,0:T(8,128)(2,1)S(1)} fusion(f32[512,768]{1,0:T(8,128)S(1)} %fusion.26, bf16[512,2048]{1,0:T(8,128)(2,1)S(1)} %constant_dynamic-update-slice_fusion.4, bf16[1,2048,768]{2,1,0:T(8,128)(2,1)S(1)} %copy-done.21), kind=kOutput, calls=%fused_computation.37 | convolution fusion | flops 1612972032 | bytes 7602176 | tf_op jit(solution)/shard_map/dot_general | solution.py:12
  63.3 2.1 %constant_dynamic-update-slice_fusion.23 = bf16[512,2048]{1,0:T(8,128)(2,1)} fusion(bf16[128,2048]{1,0:T(8,128)(2,1)} %collective-permute-done.18), kind=kLoop, calls=%fused_computation.119 | loop fusion | bytes 1048576
  65.7 4.2 %collective-permute-done.22 = bf16[128,2048]{1,0:T(8,128)(2,1)} collective-permute-done((bf16[128,2048]{1,0:T(8,128)(2,1)}, bf16[128,2048]{1,0:T(8,128)(2,1)}, u32[]{:S(2)}, u32[]{:S(2)}) %collective-permute-start.22) | collective-permute-done | bytes 524320 | tf_op jit(solution)/shard_map/ppermute | solution.py:57
  70.4 1.9 %constant_dynamic-update-slice_fusion.27 = bf16[512,2048]{1,0:T(8,128)(2,1)} fusion(bf16[128,2048]{1,0:T(8,128)(2,1)} %collective-permute-done.22), kind=kLoop, calls=%fused_computation.123 | loop fusion | bytes 1048576
  73.4 2.1 %collective-permute-done.15 = bf16[128,2048]{1,0:T(8,128)(2,1)} collective-permute-done((bf16[128,2048]{1,0:T(8,128)(2,1)S(1)}, bf16[128,2048]{1,0:T(8,128)(2,1)}, u32[]{:S(2)}, u32[]{:S(2)}) %collective-permute-start.15) | collective-permute-done | bytes 524320 | tf_op jit(solution)/shard_map/ppermute | solution.py:57
  75.5 1.9 %constant_dynamic-update-slice_fusion.18 = bf16[512,2048]{1,0:T(8,128)(2,1)} fusion(bf16[512,2048]{1,0:T(8,128)(2,1)} %constant_dynamic-update-slice_fusion.19, bf16[128,2048]{1,0:T(8,128)(2,1)} %collective-permute-done.15), kind=kLoop, calls=%fused_computation.114 | loop fusion | bytes 1048576
  77.9 1.4 convolution_convert_fusion.2
  80.5 3.3 %fusion.49 = f32[4,64,64]{2,1,0:T(8,128)} fusion(bf16[512,2048]{1,0:T(8,128)(2,1)} %constant_dynamic-update-slice_fusion.8, bf16[1,2048,64]{1,2,0:T(8,128)(2,1)S(1)} %copy-done.1, bf16[512,64]{0,1:T(8,128)(2,1)} %convolution_convert_fusion.2, bf16[512,4]{0,1:T(4,128)(2,1)S(1)} %get-tuple-element.29, f32[512]{0:T(512)} %bitcast.192), kind=kOutput, calls=%fused_computation.65 | convolution fusion | flops 151191552 | bytes 2496512 | tf_op jit(solution)/shard_map/dot_general | solution.py:28
  83.9 1.9 %constant_dynamic-update-slice_fusion.17 = bf16[512,2048]{1,0:T(8,128)(2,1)} fusion(bf16[512,2048]{1,0:T(8,128)(2,1)} %constant_dynamic-update-slice_fusion.18, bf16[128,2048]{1,0:T(8,128)(2,1)} %collective-permute-done.16), kind=kLoop, calls=%fused_computation.113 | loop fusion | bytes 1048576
  85.8 5.4 %multiply_reduce_fusion.2 = f32[512]{0:T(512)} fusion(bf16[512,2048]{1,0:T(8,128)(2,1)} %constant_dynamic-update-slice_fusion.8, bf16[512,768]{1,0:T(8,128)(2,1)} %copy-done.7, bf16[1,768,2048]{2,1,0:T(8,128)(2,1)} %param.18), kind=kOutput, calls=%fused_computation.2 | convolution fusion | flops 1613757952 | bytes 6031360 | tf_op jit(solution)/shard_map/dot_general | solution.py:17
  91.2 1.2 collective-permute-start.26
  92.5 1.8 %fusion.24 = f32[512,768]{1,0:T(8,128)S(1)} fusion(bf16[512,2048]{1,0:T(8,128)(2,1)S(1)} %constant_dynamic-update-slice_fusion.12, bf16[1,2048,768]{2,1,0:T(8,128)(2,1)S(1)} %copy-done), kind=kOutput, calls=%fused_computation.27 | convolution fusion | flops 1610612736 | bytes 6815744 | tf_op jit(solution)/shard_map/dot_general | solution.py:11
  94.4 1.9 %multiply_convert_fusion.1 = bf16[512,768]{1,0:T(8,128)(2,1)S(1)} fusion(f32[512,768]{1,0:T(8,128)S(1)} %fusion.24, bf16[512,2048]{1,0:T(8,128)(2,1)S(1)} %constant_dynamic-update-slice_fusion.12, bf16[1,2048,768]{2,1,0:T(8,128)(2,1)S(1)} %copy-done.22), kind=kOutput, calls=%fused_computation.36 | convolution fusion | flops 1612972032 | bytes 7602176 | tf_op jit(solution)/shard_map/dot_general | solution.py:12
  96.3 4.4 %collective-permute-done.26 = bf16[128,2048]{1,0:T(8,128)(2,1)} collective-permute-done((bf16[128,2048]{1,0:T(8,128)(2,1)}, bf16[128,2048]{1,0:T(8,128)(2,1)}, u32[]{:S(2)}, u32[]{:S(2)}) %collective-permute-start.26) | collective-permute-done | bytes 524320 | tf_op jit(solution)/shard_map/ppermute | solution.py:57
  100.7 1.2 collective-permute-start.28
  101.9 1.9 %constant_dynamic-update-slice_fusion.29 = bf16[256,2048]{1,0:T(8,128)(2,1)} fusion(bf16[128,2048]{1,0:T(8,128)(2,1)} %collective-permute-done.26), kind=kLoop, calls=%fused_computation.125 | loop fusion | bytes 1048576
  103.8 1.9 %constant_dynamic-update-slice_fusion.22 = bf16[512,2048]{1,0:T(8,128)(2,1)} fusion(bf16[512,2048]{1,0:T(8,128)(2,1)} %constant_dynamic-update-slice_fusion.23, bf16[128,2048]{1,0:T(8,128)(2,1)} %collective-permute-done.19), kind=kLoop, calls=%fused_computation.118 | loop fusion | bytes 1048576
  106.2 1.9 %constant_dynamic-update-slice_fusion.26 = bf16[512,2048]{1,0:T(8,128)(2,1)} fusion(bf16[512,2048]{1,0:T(8,128)(2,1)} %constant_dynamic-update-slice_fusion.27, bf16[128,2048]{1,0:T(8,128)(2,1)} %collective-permute-done.23), kind=kLoop, calls=%fused_computation.122 | loop fusion | bytes 1048576
  108.1 2.1 %collective-permute-done.28 = bf16[128,2048]{1,0:T(8,128)(2,1)} collective-permute-done((bf16[128,2048]{1,0:T(8,128)(2,1)}, bf16[128,2048]{1,0:T(8,128)(2,1)}, u32[]{:S(2)}, u32[]{:S(2)}) %collective-permute-start.28) | collective-permute-done | bytes 524320 | tf_op jit(solution)/shard_map/ppermute | solution.py:57
  110.2 1.9 %constant_dynamic-update-slice_fusion.31 = bf16[256,2048]{1,0:T(8,128)(2,1)} fusion(bf16[128,2048]{1,0:T(8,128)(2,1)} %collective-permute-done.28), kind=kLoop, calls=%fused_computation.127 | loop fusion | bytes 1048576
  112.6 1.9 %constant_dynamic-update-slice_fusion.21 = bf16[512,2048]{1,0:T(8,128)(2,1)} fusion(bf16[512,2048]{1,0:T(8,128)(2,1)} %constant_dynamic-update-slice_fusion.22, bf16[128,2048]{1,0:T(8,128)(2,1)} %collective-permute-done.20), kind=kLoop, calls=%fused_computation.117 | loop fusion | bytes 1048576
  116.3 3.3 %fusion.50 = f32[4,64,64]{2,1,0:T(8,128)} fusion(bf16[512,2048]{1,0:T(8,128)(2,1)} %constant_dynamic-update-slice_fusion.16, bf16[1,2048,64]{1,2,0:T(8,128)(2,1)S(1)} %copy-done.1, bf16[512,64]{0,1:T(8,128)(2,1)} %convolution_convert_fusion.1, bf16[512,4]{0,1:T(4,128)(2,1)S(1)} %get-tuple-element.30, f32[512]{0:T(512)S(1)} %bitcast.191), kind=kOutput, calls=%fused_computation.66 | convolution fusion | flops 151191552 | bytes 2496512 | tf_op jit(solution)/shard_map/dot_general | solution.py:28
  119.6 1.9 %constant_dynamic-update-slice_fusion.25 = bf16[512,2048]{1,0:T(8,128)(2,1)} fusion(bf16[512,2048]{1,0:T(8,128)(2,1)} %constant_dynamic-update-slice_fusion.26, bf16[128,2048]{1,0:T(8,128)(2,1)} %collective-permute-done.24), kind=kLoop, calls=%fused_computation.121 | loop fusion | bytes 1048576
  121.5 4.8 %multiply_reduce_fusion.1 = f32[512]{0:T(512)S(1)} fusion(bf16[512,2048]{1,0:T(8,128)(2,1)} %constant_dynamic-update-slice_fusion.16, bf16[512,768]{1,0:T(8,128)(2,1)} %copy-done.8, bf16[1,768,2048]{2,1,0:T(8,128)(2,1)} %param.18), kind=kOutput, calls=%fused_computation.1 | convolution fusion | flops 1613757952 | bytes 6031360 | tf_op jit(solution)/shard_map/dot_general | solution.py:17
  127.4 1.8 %fusion.22 = f32[512,768]{1,0:T(8,128)S(1)} fusion(bf16[512,2048]{1,0:T(8,128)(2,1)S(1)} %constant_dynamic-update-slice_fusion.20, bf16[1,2048,768]{2,1,0:T(8,128)(2,1)S(1)} %copy-done), kind=kOutput, calls=%fused_computation.25 | convolution fusion | flops 1610612736 | bytes 6815744 | tf_op jit(solution)/shard_map/dot_general | solution.py:11
  129.3 1.9 %multiply_convert_fusion = bf16[512,768]{1,0:T(8,128)(2,1)S(1)} fusion(f32[512,768]{1,0:T(8,128)S(1)} %fusion.22, bf16[512,2048]{1,0:T(8,128)(2,1)S(1)} %constant_dynamic-update-slice_fusion.20, bf16[1,2048,768]{2,1,0:T(8,128)(2,1)S(1)} %copy-done.23), kind=kOutput, calls=%fused_computation.35 | convolution fusion | flops 1612972032 | bytes 7602176 | tf_op jit(solution)/shard_map/dot_general | solution.py:12
  136.3 1.9 %constant_dynamic-update-slice_fusion.24 = bf16[512,2048]{1,0:T(8,128)(2,1)} fusion(bf16[512,2048]{1,0:T(8,128)(2,1)} %constant_dynamic-update-slice_fusion.25, bf16[128,2048]{1,0:T(8,128)(2,1)} %collective-permute-done.25), kind=kLoop, calls=%fused_computation.120 | loop fusion | bytes 1048576 | tf_op jit(solution)/shard_map/concatenate | solution.py:111
  138.2 3.6 %multiply_reduce_fusion = f32[512]{0:T(512)S(1)} fusion(bf16[512,2048]{1,0:T(8,128)(2,1)} %constant_dynamic-update-slice_fusion.24, bf16[512,768]{1,0:T(8,128)(2,1)S(1)} %multiply_convert_fusion, bf16[1,768,2048]{2,1,0:T(8,128)(2,1)S(1)} %copy-done.25), kind=kOutput, calls=%fused_computation | convolution fusion | flops 1613757952 | bytes 6031360 | tf_op jit(solution)/shard_map/dot_general | solution.py:17
  144.8 3.5 %all-to-all-start.1 = ((f32[16,1,128]{2,1,0:T(1,128)}), f32[16,1,128]{2,1,0:T(1,128)S(1)}, u32[]{:S(2)}, u32[]{:S(2)}) async-start(f32[16,1,128]{2,1,0:T(1,128)} %bitcast.40), calls=%async_computation.1 | async-start | bytes 16384 | tf_op jit(solution)/shard_map/all_to_all | solution.py:129
  148.3 3.3 %fusion.51 = f32[4,64,64]{2,1,0:T(8,128)} fusion(bf16[512,2048]{1,0:T(8,128)(2,1)} %constant_dynamic-update-slice_fusion.24, bf16[1,2048,64]{1,2,0:T(8,128)(2,1)S(1)} %copy-done.1, bf16[512,64]{0,1:T(8,128)(2,1)S(1)} %copy-done.11, bf16[512,4]{0,1:T(4,128)(2,1)S(1)} %get-tuple-element.31, f32[512]{0:T(512)} %bitcast.190), kind=kOutput, calls=%fused_computation.67 | convolution fusion | flops 151191552 | bytes 2496512 | tf_op jit(solution)/shard_map/dot_general | solution.py:28
  151.6 2.7 %fusion.38 = f32[4,64,64]{2,1,0:T(8,128)} fusion(f32[4,64,64]{2,1,0:T(8,128)} %fusion.51, f32[4,64,64]{2,1,0:T(8,128)} %fusion.50, f32[4,64,64]{2,1,0:T(8,128)} %fusion.49, bf16[256,2048]{1,0:T(8,128)(2,1)} %copy-done.4, bf16[1,2048,64]{1,2,0:T(8,128)(2,1)S(1)} %copy-done.1, bf16[256,64]{0,1:T(8,128)(2,1)S(1)} %convolution_convert_fusion.4, ...), kind=kOutput, calls=%fused_computation.45 | convolution fusion | flops 75644928 | bytes 1608704 | tf_op jit(solution)/shard_map/dot_general | solution.py:28
  154.3 2.6 %fusion.36 = f32[4,1,64,64]{3,2,1,0:T(8,128)} fusion(f32[4,64,64]{2,1,0:T(8,128)} %fusion.38, bf16[256,2048]{1,0:T(8,128)(2,1)} %copy-done.6, bf16[1,2048,64]{1,2,0:T(8,128)(2,1)S(1)} %copy-done.1, bf16[256,64]{0,1:T(8,128)(2,1)S(1)} %copy-done.12, bf16[256,4]{0,1:T(4,128)(2,1)S(1)} %copy-done.17, f32[256]{0:T(256)} %bitcast.197), kind=kOutput, calls=%fused_computation.42 | convolution fusion | flops 75612160 | bytes 1477632 | tf_op jit(solution)/shard_map/dot_general | solution.py:28
  (142 shorter events, 31.6 us)
Async XLA Ops:
  0.6 23.6 %copy-start = (bf16[1,2048,768]{2,1,0:T(8,128)(2,1)S(1)}, bf16[1,2048,768]{2,1,0:T(8,128)(2,1)}, u32[]{:S(2)}) copy-start(bf16[1,2048,768]{2,1,0:T(8,128)(2,1)} %param.16) | copy-start | bytes 9437188
  0.6 25.9 %collective-permute-start.2 = (bf16[128,2048]{1,0:T(8,128)(2,1)}, bf16[128,2048]{1,0:T(8,128)(2,1)}, u32[]{:S(2)}, u32[]{:S(2)}) collective-permute-start(bf16[128,2048]{1,0:T(8,128)(2,1)} %param.11), channel_id=1, source_target_pairs={{0,4},{1,3},{4,8},{5,1},{8,12},{9,5},{12,14},{13,9},{14,10},{15,13... | collective-permute-start | bytes 1572872 | tf_op jit(solution)/shard_map/ppermute | solution.py:57
  3.7 18.6 %collective-permute-start = (bf16[128,2048]{1,0:T(8,128)(2,1)}, bf16[128,2048]{1,0:T(8,128)(2,1)}, u32[]{:S(2)}, u32[]{:S(2)}) collective-permute-start(bf16[128,2048]{1,0:T(8,128)(2,1)} %param.11), channel_id=1, source_target_pairs={{0,1},{1,0},{2,3},{3,2},{4,5},{5,4},{6,7},{7,6},{8,9},{9,8},{10,11... | collective-permute-start | bytes 1572872 | tf_op jit(solution)/shard_map/ppermute | solution.py:60
  3.7 29.0 %collective-permute-start.6 = (bf16[128,2048]{1,0:T(8,128)(2,1)}, bf16[128,2048]{1,0:T(8,128)(2,1)}, u32[]{:S(2)}, u32[]{:S(2)}) collective-permute-start(bf16[128,2048]{1,0:T(8,128)(2,1)} %param.12), channel_id=1, source_target_pairs={{0,4},{1,3},{4,8},{5,1},{8,12},{9,5},{12,14},{13,9},{14,10},{15,13... | collective-permute-start | bytes 1572872 | tf_op jit(solution)/shard_map/ppermute | solution.py:57
  5.3 22.9 %collective-permute-start.1 = (bf16[128,2048]{1,0:T(8,128)(2,1)}, bf16[128,2048]{1,0:T(8,128)(2,1)}, u32[]{:S(2)}, u32[]{:S(2)}) collective-permute-start(bf16[128,2048]{1,0:T(8,128)(2,1)} %param.12), channel_id=1, source_target_pairs={{0,1},{1,0},{2,3},{3,2},{4,5},{5,4},{6,7},{7,6},{8,9},{9,8},{10,11... | collective-permute-start | bytes 1572872 | tf_op jit(solution)/shard_map/ppermute | solution.py:60
  7.3 12.9 %all-to-all-start = ((bf16[16,2,128]{2,1,0:T(2,128)(2,1)}), bf16[16,2,128]{2,1,0:T(2,128)(2,1)S(1)}, u32[]{:S(2)}, u32[]{:S(2)}) async-start(bf16[16,2,128]{2,1,0:T(2,128)(2,1)} %copy.32), calls=%async_computation | async-start | bytes 16384 | tf_op jit(solution)/shard_map/all_to_all | solution.py:88
  24.2 3.0 %copy-start.10 = (bf16[256,2048]{1,0:T(8,128)(2,1)S(1)}, bf16[256,2048]{1,0:T(8,128)(2,1)}, u32[]{:S(2)}) copy-start(bf16[256,2048]{1,0:T(8,128)(2,1)} %constant_dynamic-update-slice_fusion) | copy-start | bytes 3145732
  24.2 3.0 %copy-start.21 = (bf16[1,2048,768]{2,1,0:T(8,128)(2,1)S(1)}, bf16[1,2048,768]{2,1,0:T(8,128)(2,1)}, u32[]{:S(2)}) copy-start(bf16[1,2048,768]{2,1,0:T(8,128)(2,1)} %param.17) | copy-start | bytes 9437188
  26.6 2.8 %copy-start.24 = (bf16[1,768,2048]{2,1,0:T(8,128)(2,1)S(1)}, bf16[1,768,2048]{2,1,0:T(8,128)(2,1)}, u32[]{:S(2)}) copy-start(bf16[1,768,2048]{2,1,0:T(8,128)(2,1)} %param.18) | copy-start | bytes 9437188
  26.6 10.7 %collective-permute-start.10 = (bf16[128,2048]{1,0:T(8,128)(2,1)}, bf16[128,2048]{1,0:T(8,128)(2,1)S(1)}, u32[]{:S(2)}, u32[]{:S(2)}) collective-permute-start(bf16[128,2048]{1,0:T(8,128)(2,1)} %collective-permute-done.2), channel_id=1, source_target_pairs={{0,4},{1,3},{4,8},{5,1},{8,12},{9,5},{12,14},{13,9},{14,10},{15,13... | collective-permute-start | bytes 1572872 | tf_op jit(solution)/shard_map/ppermute | solution.py:57
  31.3 10.3 %collective-permute-start.3 = (bf16[128,2048]{1,0:T(8,128)(2,1)}, bf16[128,2048]{1,0:T(8,128)(2,1)S(1)}, u32[]{:S(2)}, u32[]{:S(2)}) collective-permute-start(bf16[128,2048]{1,0:T(8,128)(2,1)} %collective-permute-done), channel_id=1, source_target_pairs={{0,4},{1,3},{4,8},{5,1},{8,12},{9,5},{12,14},{13,9},{14,10},{15,13... | collective-permute-start | bytes 1572872 | tf_op jit(solution)/shard_map/ppermute | solution.py:57
  32.0 23.6 %collective-permute-start.7 = (bf16[128,2048]{1,0:T(8,128)(2,1)}, bf16[128,2048]{1,0:T(8,128)(2,1)S(1)}, u32[]{:S(2)}, u32[]{:S(2)}) collective-permute-start(bf16[128,2048]{1,0:T(8,128)(2,1)} %collective-permute-done.1), channel_id=1, source_target_pairs={{0,4},{1,3},{4,8},{5,1},{8,12},{9,5},{12,14},{13,9},{14,10},{15,13... | collective-permute-start | bytes 1572872 | tf_op jit(solution)/shard_map/ppermute | solution.py:57
  32.7 20.3 %collective-permute-start.14 = (bf16[128,2048]{1,0:T(8,128)(2,1)}, bf16[128,2048]{1,0:T(8,128)(2,1)}, u32[]{:S(2)}, u32[]{:S(2)}) collective-permute-start(bf16[128,2048]{1,0:T(8,128)(2,1)} %collective-permute-done.6), channel_id=1, source_target_pairs={{0,4},{1,3},{4,8},{5,1},{8,12},{9,5},{12,14},{13,9},{14,10},{15,13... | collective-permute-start | bytes 1572872 | tf_op jit(solution)/shard_map/ppermute | solution.py:57
  35.3 20.2 %collective-permute-start.4 = (bf16[128,2048]{1,0:T(8,128)(2,1)}, bf16[128,2048]{1,0:T(8,128)(2,1)S(1)}, u32[]{:S(2)}, u32[]{:S(2)}) collective-permute-start(bf16[128,2048]{1,0:T(8,128)(2,1)} %collective-permute-done.2), channel_id=1, source_target_pairs={{0,1},{1,0},{2,3},{3,2},{4,5},{5,4},{6,7},{7,6},{8,9},{9,8},{10,11... | collective-permute-start | bytes 1572872 | tf_op jit(solution)/shard_map/ppermute | solution.py:60
  37.3 19.8 %collective-permute-start.8 = (bf16[128,2048]{1,0:T(8,128)(2,1)}, bf16[128,2048]{1,0:T(8,128)(2,1)S(1)}, u32[]{:S(2)}, u32[]{:S(2)}) collective-permute-start(bf16[128,2048]{1,0:T(8,128)(2,1)} %collective-permute-done.6), channel_id=1, source_target_pairs={{0,1},{1,0},{2,3},{3,2},{4,5},{5,4},{6,7},{7,6},{8,9},{9,8},{10,11... | collective-permute-start | bytes 1572872 | tf_op jit(solution)/shard_map/ppermute | solution.py:60
  41.7 21.5 %collective-permute-start.18 = (bf16[128,2048]{1,0:T(8,128)(2,1)S(1)}, bf16[128,2048]{1,0:T(8,128)(2,1)}, u32[]{:S(2)}, u32[]{:S(2)}) collective-permute-start(bf16[128,2048]{1,0:T(8,128)(2,1)S(1)} %collective-permute-done.10), channel_id=1, source_target_pairs={{0,4},{1,3},{4,8},{5,1},{8,12},{9,5},{12,14},{13,9},{14,10},{15,13... | collective-permute-start | bytes 1572872 | tf_op jit(solution)/shard_map/ppermute | solution.py:57
  53.0 12.4 %collective-permute-start.11 = (bf16[128,2048]{1,0:T(8,128)(2,1)S(1)}, bf16[128,2048]{1,0:T(8,128)(2,1)}, u32[]{:S(2)}, u32[]{:S(2)}) collective-permute-start(bf16[128,2048]{1,0:T(8,128)(2,1)S(1)} %collective-permute-done.3), channel_id=1, source_target_pairs={{0,4},{1,3},{4,8},{5,1},{8,12},{9,5},{12,14},{13,9},{14,10},{15,13... | collective-permute-start | bytes 1572872 | tf_op jit(solution)/shard_map/ppermute | solution.py:57
  55.5 3.3 %collective-permute-start.5 = (bf16[128,2048]{1,0:T(8,128)(2,1)S(1)}, bf16[128,2048]{1,0:T(8,128)(2,1)S(1)}, u32[]{:S(2)}, u32[]{:S(2)}) collective-permute-start(bf16[128,2048]{1,0:T(8,128)(2,1)S(1)} %collective-permute-done.3), channel_id=1, source_target_pairs={{0,1},{1,0},{2,3},{3,2},{4,5},{5,4},{6,7},{7,6},{8,9},{9,8},{10,11... | collective-permute-start | bytes 1572872 | tf_op jit(solution)/shard_map/ppermute | solution.py:60
  55.6 14.2 %collective-permute-start.22 = (bf16[128,2048]{1,0:T(8,128)(2,1)}, bf16[128,2048]{1,0:T(8,128)(2,1)}, u32[]{:S(2)}, u32[]{:S(2)}) collective-permute-start(bf16[128,2048]{1,0:T(8,128)(2,1)} %collective-permute-done.14), channel_id=1, source_target_pairs={{0,4},{1,3},{4,8},{5,1},{8,12},{9,5},{12,14},{13,9},{14,10},{15,13... | collective-permute-start | bytes 1572872 | tf_op jit(solution)/shard_map/ppermute | solution.py:57
  57.1 18.4 %collective-permute-start.15 = (bf16[128,2048]{1,0:T(8,128)(2,1)S(1)}, bf16[128,2048]{1,0:T(8,128)(2,1)}, u32[]{:S(2)}, u32[]{:S(2)}) collective-permute-start(bf16[128,2048]{1,0:T(8,128)(2,1)S(1)} %collective-permute-done.7), channel_id=1, source_target_pairs={{0,4},{1,3},{4,8},{5,1},{8,12},{9,5},{12,14},{13,9},{14,10},{15,13... | collective-permute-start | bytes 1572872 | tf_op jit(solution)/shard_map/ppermute | solution.py:57
  58.8 18.6 %collective-permute-start.12 = (bf16[128,2048]{1,0:T(8,128)(2,1)S(1)}, bf16[128,2048]{1,0:T(8,128)(2,1)S(1)}, u32[]{:S(2)}, u32[]{:S(2)}) collective-permute-start(bf16[128,2048]{1,0:T(8,128)(2,1)S(1)} %collective-permute-done.10), channel_id=1, source_target_pairs={{0,1},{1,0},{2,3},{3,2},{4,5},{5,4},{6,7},{7,6},{8,9},{9,8},{10,11... | collective-permute-start | bytes 1572872 | tf_op jit(solution)/shard_map/ppermute | solution.py:60
  63.2 14.7 %copy-start.7 = (bf16[512,768]{1,0:T(8,128)(2,1)}, bf16[512,768]{1,0:T(8,128)(2,1)S(1)}, u32[]{:S(2)}) copy-start(bf16[512,768]{1,0:T(8,128)(2,1)S(1)} %multiply_convert_fusion.2) | copy-start | bytes 2359300
  63.2 20.6 %collective-permute-start.16 = (bf16[128,2048]{1,0:T(8,128)(2,1)}, bf16[128,2048]{1,0:T(8,128)(2,1)}, u32[]{:S(2)}, u32[]{:S(2)}) collective-permute-start(bf16[128,2048]{1,0:T(8,128)(2,1)} %collective-permute-done.14), channel_id=1, source_target_pairs={{0,1},{1,0},{2,3},{3,2},{4,5},{5,4},{6,7},{7,6},{8,9},{9,8},{10,11... | collective-permute-start | bytes 1572872 | tf_op jit(solution)/shard_map/ppermute | solution.py:60
  65.4 13.9 %collective-permute-start.9 = (bf16[128,2048]{1,0:T(8,128)(2,1)S(1)}, bf16[128,2048]{1,0:T(8,128)(2,1)S(1)}, u32[]{:S(2)}, u32[]{:S(2)}) collective-permute-start(bf16[128,2048]{1,0:T(8,128)(2,1)S(1)} %collective-permute-done.7), channel_id=1, source_target_pairs={{0,1},{1,0},{2,3},{3,2},{4,5},{5,4},{6,7},{7,6},{8,9},{9,8},{10,11... | collective-permute-start | bytes 1572872 | tf_op jit(solution)/shard_map/ppermute | solution.py:60
  69.9 34.0 %collective-permute-start.19 = (bf16[128,2048]{1,0:T(8,128)(2,1)}, bf16[128,2048]{1,0:T(8,128)(2,1)}, u32[]{:S(2)}, u32[]{:S(2)}) collective-permute-start(bf16[128,2048]{1,0:T(8,128)(2,1)} %collective-permute-done.11), channel_id=1, source_target_pairs={{0,4},{1,3},{4,8},{5,1},{8,12},{9,5},{12,14},{13,9},{14,10},{15,13... | collective-permute-start | bytes 1572872 | tf_op jit(solution)/shard_map/ppermute | solution.py:57
  73.3 7.2 %copy-start.1 = (bf16[1,2048,64]{1,2,0:T(8,128)(2,1)S(1)}, bf16[1,2048,64]{1,2,0:T(8,128)(2,1)}, u32[]{:S(2)}) copy-start(bf16[1,2048,64]{1,2,0:T(8,128)(2,1)} %param.20) | copy-start | bytes 786436
  75.5 36.6 %collective-permute-start.20 = (bf16[128,2048]{1,0:T(8,128)(2,1)}, bf16[128,2048]{1,0:T(8,128)(2,1)}, u32[]{:S(2)}, u32[]{:S(2)}) collective-permute-start(bf16[128,2048]{1,0:T(8,128)(2,1)} %collective-permute-done.18), channel_id=1, source_target_pairs={{0,1},{1,0},{2,3},{3,2},{4,5},{5,4},{6,7},{7,6},{8,9},{9,8},{10,11... | collective-permute-start | bytes 1572872 | tf_op jit(solution)/shard_map/ppermute | solution.py:60
  77.4 28.4 %collective-permute-start.23 = (bf16[128,2048]{1,0:T(8,128)(2,1)}, bf16[128,2048]{1,0:T(8,128)(2,1)}, u32[]{:S(2)}, u32[]{:S(2)}) collective-permute-start(bf16[128,2048]{1,0:T(8,128)(2,1)} %collective-permute-done.15), channel_id=1, source_target_pairs={{0,4},{1,3},{4,8},{5,1},{8,12},{9,5},{12,14},{13,9},{14,10},{15,13... | collective-permute-start | bytes 1572872 | tf_op jit(solution)/shard_map/ppermute | solution.py:57
  79.3 40.3 %collective-permute-start.24 = (bf16[128,2048]{1,0:T(8,128)(2,1)}, bf16[128,2048]{1,0:T(8,128)(2,1)}, u32[]{:S(2)}, u32[]{:S(2)}) collective-permute-start(bf16[128,2048]{1,0:T(8,128)(2,1)} %collective-permute-done.22), channel_id=1, source_target_pairs={{0,1},{1,0},{2,3},{3,2},{4,5},{5,4},{6,7},{7,6},{8,9},{9,8},{10,11... | collective-permute-start | bytes 1572872 | tf_op jit(solution)/shard_map/ppermute | solution.py:60
  83.8 7.5 %collective-permute-start.13 = (bf16[128,2048]{1,0:T(8,128)(2,1)}, bf16[128,2048]{1,0:T(8,128)(2,1)S(1)}, u32[]{:S(2)}, u32[]{:S(2)}) collective-permute-start(bf16[128,2048]{1,0:T(8,128)(2,1)} %collective-permute-done.11), channel_id=1, source_target_pairs={{0,1},{1,0},{2,3},{3,2},{4,5},{5,4},{6,7},{7,6},{8,9},{9,8},{10,11... | collective-permute-start | bytes 1572872 | tf_op jit(solution)/shard_map/ppermute | solution.py:60
  85.8 6.6 %copy-start.15 = (bf16[512,2048]{1,0:T(8,128)(2,1)S(1)}, bf16[512,2048]{1,0:T(8,128)(2,1)}, u32[]{:S(2)}) copy-start(bf16[512,2048]{1,0:T(8,128)(2,1)} %copy-done.14) | copy-start | bytes 6291460
  91.2 9.5 %collective-permute-start.26 = (bf16[128,2048]{1,0:T(8,128)(2,1)}, bf16[128,2048]{1,0:T(8,128)(2,1)}, u32[]{:S(2)}, u32[]{:S(2)}) collective-permute-start(bf16[128,2048]{1,0:T(8,128)(2,1)} %collective-permute-done.18), channel_id=1, source_target_pairs={{0,4},{1,3},{4,8},{5,1},{8,12},{9,5},{12,14},{13,9},{14,10},{15,13... | collective-permute-start | bytes 1572872 | tf_op jit(solution)/shard_map/ppermute | solution.py:57
  96.3 18.2 %copy-start.8 = (bf16[512,768]{1,0:T(8,128)(2,1)}, bf16[512,768]{1,0:T(8,128)(2,1)S(1)}, u32[]{:S(2)}) copy-start(bf16[512,768]{1,0:T(8,128)(2,1)S(1)} %multiply_convert_fusion.1) | copy-start | bytes 2359300
  100.7 9.5 %collective-permute-start.28 = (bf16[128,2048]{1,0:T(8,128)(2,1)}, bf16[128,2048]{1,0:T(8,128)(2,1)}, u32[]{:S(2)}, u32[]{:S(2)}) collective-permute-start(bf16[128,2048]{1,0:T(8,128)(2,1)} %collective-permute-done.22), channel_id=1, source_target_pairs={{0,4},{1,3},{4,8},{5,1},{8,12},{9,5},{12,14},{13,9},{14,10},{15,13... | collective-permute-start | bytes 1572872 | tf_op jit(solution)/shard_map/ppermute | solution.py:57
  103.8 11.7 %collective-permute-start.17 = (bf16[128,2048]{1,0:T(8,128)(2,1)}, bf16[128,2048]{1,0:T(8,128)(2,1)S(1)}, u32[]{:S(2)}, u32[]{:S(2)}) collective-permute-start(bf16[128,2048]{1,0:T(8,128)(2,1)} %collective-permute-done.15), channel_id=1, source_target_pairs={{0,1},{1,0},{2,3},{3,2},{4,5},{5,4},{6,7},{7,6},{8,9},{9,8},{10,11... | collective-permute-start | bytes 1572872 | tf_op jit(solution)/shard_map/ppermute | solution.py:60
  105.7 20.6 %collective-permute-start.21 = (bf16[128,2048]{1,0:T(8,128)(2,1)}, bf16[128,2048]{1,0:T(8,128)(2,1)}, u32[]{:S(2)}, u32[]{:S(2)}) collective-permute-start(bf16[128,2048]{1,0:T(8,128)(2,1)} %collective-permute-done.19), channel_id=1, source_target_pairs={{0,1},{1,0},{2,3},{3,2},{4,5},{5,4},{6,7},{7,6},{8,9},{9,8},{10,11... | collective-permute-start | bytes 1572872 | tf_op jit(solution)/shard_map/ppermute | solution.py:60
  108.1 8.2 %copy-start.18 = (f32[4,1,128]{2,1,0:T(1,128)S(1)}, f32[4,1,128]{2,1,0:T(1,128)}, u32[]{:S(2)}) copy-start(f32[4,1,128]{2,1,0:T(1,128)} %get-tuple-element.22) | copy-start | bytes 6148
  110.2 26.0 %collective-permute-start.25 = (bf16[128,2048]{1,0:T(8,128)(2,1)}, bf16[128,2048]{1,0:T(8,128)(2,1)}, u32[]{:S(2)}, u32[]{:S(2)}) collective-permute-start(bf16[128,2048]{1,0:T(8,128)(2,1)} %collective-permute-done.23), channel_id=1, source_target_pairs={{0,1},{1,0},{2,3},{3,2},{4,5},{5,4},{6,7},{7,6},{8,9},{9,8},{10,11... | collective-permute-start | bytes 1572872 | tf_op jit(solution)/shard_map/ppermute | solution.py:60
  112.1 19.1 %collective-permute-start.27 = (bf16[128,2048]{1,0:T(8,128)(2,1)}, bf16[128,2048]{1,0:T(8,128)(2,1)}, u32[]{:S(2)}, u32[]{:S(2)}) collective-permute-start(bf16[128,2048]{1,0:T(8,128)(2,1)} %collective-permute-done.26), channel_id=1, source_target_pairs={{0,1},{1,0},{2,3},{3,2},{4,5},{5,4},{6,7},{7,6},{8,9},{9,8},{10,11... | collective-permute-start | bytes 1572872 | tf_op jit(solution)/shard_map/ppermute | solution.py:60
  115.5 26.3 %collective-permute-start.29 = (bf16[128,2048]{1,0:T(8,128)(2,1)}, bf16[128,2048]{1,0:T(8,128)(2,1)}, u32[]{:S(2)}, u32[]{:S(2)}) collective-permute-start(bf16[128,2048]{1,0:T(8,128)(2,1)} %collective-permute-done.28), channel_id=1, source_target_pairs={{0,1},{1,0},{2,3},{3,2},{4,5},{5,4},{6,7},{7,6},{8,9},{9,8},{10,11... | collective-permute-start | bytes 1572872 | tf_op jit(solution)/shard_map/ppermute | solution.py:60
  121.5 4.8 %copy-start.13 = (bf16[512,2048]{1,0:T(8,128)(2,1)S(1)}, bf16[512,2048]{1,0:T(8,128)(2,1)}, u32[]{:S(2)}) copy-start(bf16[512,2048]{1,0:T(8,128)(2,1)} %constant_dynamic-update-slice_fusion.21) | copy-start | bytes 6291460
  133.3 4.8 %copy-start.25 = (bf16[1,768,2048]{2,1,0:T(8,128)(2,1)S(1)}, bf16[1,768,2048]{2,1,0:T(8,128)(2,1)}, u32[]{:S(2)}) copy-start(bf16[1,768,2048]{2,1,0:T(8,128)(2,1)} %param.18) | copy-start | bytes 9437188
  138.2 3.6 %copy-start.5 = (bf16[256,2048]{1,0:T(8,128)(2,1)S(1)}, bf16[256,2048]{1,0:T(8,128)(2,1)}, u32[]{:S(2)}) copy-start(bf16[256,2048]{1,0:T(8,128)(2,1)} %constant_dynamic-update-slice_fusion.31) | copy-start | bytes 3145732
  142.9 5.4 %copy-start.11 = (bf16[512,64]{0,1:T(8,128)(2,1)S(1)}, bf16[512,64]{0,1:T(8,128)(2,1)}, u32[]{:S(2)}) copy-start(bf16[512,64]{0,1:T(8,128)(2,1)} %convolution_convert_fusion) | copy-start | bytes 196612
  144.8 12.0 %all-to-all-start.1 = ((f32[16,1,128]{2,1,0:T(1,128)}), f32[16,1,128]{2,1,0:T(1,128)S(1)}, u32[]{:S(2)}, u32[]{:S(2)}) async-start(f32[16,1,128]{2,1,0:T(1,128)} %bitcast.40), calls=%async_computation.1 | async-start | bytes 16384 | tf_op jit(solution)/shard_map/all_to_all | solution.py:129
  148.3 6.0 %copy-start.12 = (bf16[256,64]{0,1:T(8,128)(2,1)S(1)}, bf16[256,64]{0,1:T(8,128)(2,1)}, u32[]{:S(2)}) copy-start(bf16[256,64]{0,1:T(8,128)(2,1)} %convolution_convert_fusion.3) | copy-start | bytes 98308
  148.3 5.9 %copy-start.17 = (bf16[256,4]{0,1:T(4,128)(2,1)S(1)}, bf16[256,4]{0,1:T(4,128)(2,1)}, u32[]{:S(2)}) copy-start(bf16[256,4]{0,1:T(4,128)(2,1)} %get-tuple-element.27) | copy-start | bytes 6148
  151.6 5.3 %copy-start.16 = (s32[128,8]{0,1:T(8,128)S(1)}, s32[128,8]{0,1:T(8,128)}, u32[]{:S(2)}) copy-start(s32[128,8]{0,1:T(8,128)} %param.13) | copy-start | bytes 12292
  (10 other events, 16.7 us)

commit v3 on v2

--- a/solution.py
+++ b/solution.py
@@ -92,25 +92,21 @@
         jnp.where(owned[:, :, None, None], meta[None].astype(jnp.float32), 0.0), axis=1
     ).astype(jnp.bfloat16)
 
-    sets = [[(tokens, cotangent)]]
-    last = [(tokens, cotangent)]
-    beside = tuple(swap(block) for block in last[0])
-    sets[0].append(beside)
-    last.append(beside)
-    for step in range(1, half + 1):
-        if step == half:
-            last = last[:1]
-        x_in = [hop(pair[0]) for pair in last]
-        dy_in = [hop(pair[1]) for pair in last]
-        last = list(zip(x_in, dy_in))
-        sets.append(last + [(swap(pair[0]), swap(pair[1])) for pair in last])
-
-    grads, feature, begin = [], 0.0, 0
-    for blocks in sets:
-        x = jnp.concatenate([pair[0] for pair in blocks], axis=0)
-        dy = jnp.concatenate([pair[1] for pair in blocks], axis=0)
-        part = meta[begin : begin + len(blocks)]
-        begin += len(blocks)
+    x, dy = tokens, cotangent
+    x_beside, dy_beside = swap(x), swap(dy)
+    sets = [(jnp.concatenate([x, x_beside]), jnp.concatenate([dy, dy_beside]))]
+    x = jnp.concatenate([hop(x), hop(x_beside)])
+    dy = jnp.concatenate([hop(dy), hop(dy_beside)])
+    for step in range(1, half):
+        sets += [(x, dy), (swap(x), swap(dy))]
+        if step < half - 1:
+            x, dy = hop(x), hop(dy)
+    x, dy = hop(x[:tok_rows]), hop(dy[:tok_rows])
+    sets.append((jnp.concatenate([x, swap(x)]), jnp.concatenate([dy, swap(dy)])))
+
+    grads, feature = [], 0.0
+    for begin, (x, dy) in enumerate(sets):
+        part = meta[2 * begin : 2 * begin + 2]
         hidden = swiglu(x, w_gate[0], w_up[0])
         grad, term = finish(
             hidden,
@@ -122,7 +118,7 @@
             proj_output[0],
             docs_count,
         )
-        grads.append(grad.reshape(len(blocks), tok_rows))
+        grads.append(grad.reshape(2, tok_rows))
         feature = feature + term
     grads = jnp.concatenate(grads, axis=0)
     grads = jnp.sum(jnp.where(owned[:, :, None], grads[:, None, :], 0.0), axis=0)

time: 159 us -> 155 us (0.975)
  matrix products: 52.6 us -> 80.3 us
  local copies, waits for them, and re-layouts: 42.2 us -> 25.3 us
  waiting for transfers between devices: 30.9 us -> 21.7 us
  starting transfers between devices: 25.7 us -> 21 us
    unnamed x74 -> x66, local copies, waits for them, and re-layouts: 30.9 us -> 11.3 us
    ppermute x14 -> x10, waiting for transfers between devices: 27.5 us -> 17 us  [hop(): return lax.ppermute(block, 'exp', onward)]
    dot_general x5 -> x8, matrix products: 7.76 us -> 16.3 us  [swiglu(): up_val = jnp.dot(rows, w_up, preferred_element_type=jnp.float32)]
    dot_general x5 -> x8, matrix products: 8.77 us -> 16.8 us  [swiglu(): gate_val = jnp.dot(rows, w_gate, preferred_element_type=jnp.float32)]
    dot_general x5 -> x8, matrix products: 16.5 us -> 22.2 us  [finish(): out_val = jnp.dot(hidden, w_down, preferred_element_type=jnp.float32)]
    dot_general x5 -> x8, matrix products: 15.1 us -> 20.6 us  [finish(): lax.dot_general(spread, high_side, (((0,), (0,)), ((), ())), preferred_el...]
    ppermute x14 -> x10, starting transfers between devices: 14 us -> 8.79 us  [hop(): return lax.ppermute(block, 'exp', onward)]
    slice x0 -> x2, local copies, waits for them, and re-layouts: none -> 4.15 us  [by_ring(): x, dy = (hop(x[:tok_rows]), hop(dy[:tok_rows]))]
  transfers between devices with their start and end apart: 32 -> 22, of which waited for: 7 -> 4; matrix products, arithmetic and copies ran while one was open for 61% -> 68% of each run, Pallas kernels for 0% -> 0%
where the time goes in v3:
time: 155 us; the launch traced here: 154 us
  matrix products  80.3 us (52%)
  local copies, waits for them, and re-layouts  25.3 us (16%)
  waiting for transfers between devices  21.7 us (14%)
  starting transfers between devices  21 us (14%)
  other arithmetic  4.23 us (3%)
    dot_general x8, matrix products, finish(): out_val = jnp.dot(hidden, w_down, preferred_element_type=jnp.float32)  22.2 us
    dot_general x8, matrix products, finish(): lax.dot_general(spread, high_side, (((0,), (0,)), ((), ())), preferred_el...  20.6 us
    ppermute x10, waiting for transfers between devices, hop(): return lax.ppermute(block, 'exp', onward)  17 us
    dot_general x8, matrix products, swiglu(): gate_val = jnp.dot(rows, w_gate, preferred_element_type=jnp.float32)  16.8 us
    dot_general x8, matrix products, swiglu(): up_val = jnp.dot(rows, w_up, preferred_element_type=jnp.float32)  16.3 us
    unnamed x66, local copies, waits for them, and re-layouts  11.3 us
    ppermute x10, starting transfers between devices, hop(): return lax.ppermute(block, 'exp', onward)  8.79 us
    all_to_all x1, starting transfers between devices, by_ring(): lax.all_to_all(jnp.stack([weight, own_doc], axis=1), 'exp', split_axis=0,...  4.94 us
  transfers between devices with their start and end apart: 22, of which 4 were waited for; matrix products, arithmetic and copies ran while one was open for 68% of the time, Pallas kernels for 0%

profile of v3, /device:TPU:0, one launch (start us, length us, event | category | flops | bytes accessed | tf_op | source)
XLA Modules:
  0.0 153.9 jit_solution(9219570424530309089)
XLA Ops:
  1.2 2.6 %collective-permute-start.2 = (bf16[128,2048]{1,0:T(8,128)(2,1)}, bf16[128,2048]{1,0:T(8,128)(2,1)}, u32[]{:S(2)}, u32[]{:S(2)}) collective-permute-start(bf16[128,2048]{1,0:T(8,128)(2,1)} %param.11), channel_id=1, source_target_pairs={{0,4},{1,3},{4,8},{5,1},{8,12},{9,5},{12,14},{13,9},{14,10},{15,13... | collective-permute-start | bytes 1572872 | tf_op jit(solution)/shard_map/ppermute | solution.py:57
  3.9 1.5 collective-permute-start.4
  7.4 4.9 %all-to-all-start = ((bf16[16,2,128]{2,1,0:T(2,128)(2,1)}), bf16[16,2,128]{2,1,0:T(2,128)(2,1)S(1)}, u32[]{:S(2)}, u32[]{:S(2)}) async-start(bf16[16,2,128]{2,1,0:T(2,128)(2,1)} %copy.32), calls=%async_computation | async-start | bytes 16384 | tf_op jit(solution)/shard_map/all_to_all | solution.py:88
  12.3 1.9 %constant_dynamic-update-slice_fusion.1 = bf16[256,2048]{1,0:T(8,128)(2,1)} fusion(bf16[128,2048]{1,0:T(8,128)(2,1)} %param.11), kind=kLoop, calls=%fused_computation.169 | loop fusion | bytes 1048576
  14.3 1.9 %constant_dynamic-update-slice_fusion.3 = bf16[256,2048]{1,0:T(8,128)(2,1)} fusion(bf16[128,2048]{1,0:T(8,128)(2,1)} %param.12), kind=kLoop, calls=%fused_computation.171 | loop fusion | bytes 1048576
  16.9 3.4 %all-to-all-done = bf16[16,2,128]{2,1,0:T(2,128)(2,1)S(1)} async-done(((bf16[16,2,128]{2,1,0:T(2,128)(2,1)}), bf16[16,2,128]{2,1,0:T(2,128)(2,1)S(1)}, u32[]{:S(2)}, u32[]{:S(2)}) %all-to-all-start) | async-done | bytes 8224 | tf_op jit(solution)/shard_map/all_to_all | solution.py:88
  21.8 2.0 %constant_dynamic-update-slice_fusion = bf16[256,2048]{1,0:T(8,128)(2,1)} fusion(bf16[256,2048]{1,0:T(8,128)(2,1)} %constant_dynamic-update-slice_fusion.1, bf16[128,2048]{1,0:T(8,128)(2,1)} %collective-permute-done), kind=kLoop, calls=%fused_computation.168 | loop fusion | bytes 1048576 | tf_op jit(solution)/shard_map/concatenate | solution.py:97
  23.8 2.3 %fusion.46 = f32[256,768]{1,0:T(8,128)S(1)} fusion(bf16[256,2048]{1,0:T(8,128)(2,1)} %constant_dynamic-update-slice_fusion, bf16[1,2048,768]{2,1,0:T(8,128)(2,1)S(1)} %copy-done), kind=kOutput, calls=%fused_computation.46 | convolution fusion | flops 805306368 | bytes 4980736 | tf_op jit(solution)/shard_map/dot_general | solution.py:11
  28.5 1.6 %multiply_reduce_fusion.7 = f32[256]{0:T(256)} fusion(bf16[256,2048]{1,0:T(8,128)(2,1)S(1)} %constant_dynamic-update-slice_fusion.2, bf16[256,768]{1,0:T(8,128)(2,1)S(1)} %multiply_convert_fusion.7, bf16[1,768,2048]{2,1,0:T(8,128)(2,1)S(1)} %copy-done.26), kind=kOutput, calls=%fused_computation.55 | convolution fusion | flops 806878976 | bytes 4588544 | tf_op jit(solution)/shard_map/dot_general | solution.py:17
  31.5 1.9 %constant_dynamic-update-slice_fusion.5 = bf16[256,2048]{1,0:T(8,128)(2,1)} fusion(bf16[128,2048]{1,0:T(8,128)(2,1)} %collective-permute-done.2), kind=kLoop, calls=%fused_computation.173 | loop fusion | bytes 1048576
  33.4 1.9 %constant_dynamic-update-slice_fusion.7 = bf16[256,2048]{1,0:T(8,128)(2,1)} fusion(bf16[128,2048]{1,0:T(8,128)(2,1)} %collective-permute-done.4), kind=kLoop, calls=%fused_computation.175 | loop fusion | bytes 1048576
  35.3 2.6 %fusion.65 = f32[4,64,64]{2,1,0:T(8,128)} fusion(bf16[256,2048]{1,0:T(8,128)(2,1)} %copy-done.4, bf16[1,2048,64]{1,2,0:T(8,128)(2,1)S(1)} %copy-done.1, bf16[256,64]{0,1:T(8,128)(2,1)S(1)} %convolution_convert_fusion.7, bf16[256,4]{0,1:T(4,128)(2,1)} %get-tuple-element.43, f32[256]{0:T(256)} %bitcast.292), kind=kOutput, calls=%fused_computation.104 | convolution fusion | flops 75595776 | bytes 1412096 | tf_op jit(solution)/shard_map/dot_general | solution.py:28
  37.9 7.4 %collective-permute-done.5 = bf16[128,2048]{1,0:T(8,128)(2,1)} collective-permute-done((bf16[128,2048]{1,0:T(8,128)(2,1)}, bf16[128,2048]{1,0:T(8,128)(2,1)}, u32[]{:S(2)}, u32[]{:S(2)}) %collective-permute-start.5) | collective-permute-done | bytes 524320 | tf_op jit(solution)/shard_map/ppermute | solution.py:57
  45.3 1.9 %constant_dynamic-update-slice_fusion.6 = bf16[256,2048]{1,0:T(8,128)(2,1)} fusion(bf16[256,2048]{1,0:T(8,128)(2,1)} %constant_dynamic-update-slice_fusion.7, bf16[128,2048]{1,0:T(8,128)(2,1)} %collective-permute-done.5), kind=kLoop, calls=%fused_computation.174 | loop fusion | bytes 1048576 | tf_op jit(solution)/shard_map/concatenate | solution.py:99
  47.7 2.2 %constant_dynamic-update-slice_fusion.4 = bf16[256,2048]{1,0:T(8,128)(2,1)} fusion(bf16[256,2048]{1,0:T(8,128)(2,1)} %constant_dynamic-update-slice_fusion.5, bf16[128,2048]{1,0:T(8,128)(2,1)} %collective-permute-done.3), kind=kLoop, calls=%fused_computation.172 | loop fusion | bytes 1048576 | tf_op jit(solution)/shard_map/concatenate | solution.py:98
  49.9 2.2 %fusion.44 = f32[256,768]{1,0:T(8,128)S(1)} fusion(bf16[256,2048]{1,0:T(8,128)(2,1)} %constant_dynamic-update-slice_fusion.4, bf16[1,2048,768]{2,1,0:T(8,128)(2,1)S(1)} %copy-done), kind=kOutput, calls=%fused_computation.44 | convolution fusion | flops 805306368 | bytes 4980736 | tf_op jit(solution)/shard_map/dot_general | solution.py:11
  53.6 2.3 %multiply_convert_fusion.6 = bf16[256,768]{1,0:T(8,128)(2,1)S(1)} fusion(f32[256,768]{1,0:T(8,128)S(1)} %fusion.44, bf16[256,2048]{1,0:T(8,128)(2,1)} %constant_dynamic-update-slice_fusion.4, bf16[1,2048,768]{2,1,0:T(8,128)(2,1)S(1)} %copy-done.22), kind=kOutput, calls=%fused_computation.102 | convolution fusion | flops 806486016 | bytes 5373952 | tf_op jit(solution)/shard_map/dot_general | solution.py:12
  56.9 2.6 %convolution_add_fusion.6 = f32[4,64,64]{2,1,0:T(8,128)} fusion(f32[4,64,64]{2,1,0:T(8,128)} %fusion.65, bf16[256,2048]{1,0:T(8,128)(2,1)} %constant_dynamic-update-slice_fusion.6, bf16[1,2048,64]{1,2,0:T(8,128)(2,1)S(1)} %copy-done.1, bf16[256,64]{0,1:T(8,128)(2,1)S(1)} %convolution_convert_fusion.6, bf16[256,4]{0,1:T(4,128)(2,1)} %get-tuple-element.37, ...), kind=kOutput, calls=%fused_computation.63 | convolution fusion | flops 75612160 | bytes 1477632 | tf_op jit(solution)/shard_map/dot_general | solution.py:28
  59.5 3.9 %multiply_reduce_fusion.6 = f32[256]{0:T(256)} fusion(bf16[256,2048]{1,0:T(8,128)(2,1)} %constant_dynamic-update-slice_fusion.6, bf16[256,768]{1,0:T(8,128)(2,1)} %copy-done.8, bf16[1,768,2048]{2,1,0:T(8,128)(2,1)} %param.18), kind=kOutput, calls=%fused_computation.54 | convolution fusion | flops 806878976 | bytes 4588544 | tf_op jit(solution)/shard_map/dot_general | solution.py:17
  63.9 9.6 %collective-permute-done.8 = bf16[256,2048]{1,0:T(8,128)(2,1)} collective-permute-done((bf16[256,2048]{1,0:T(8,128)(2,1)}, bf16[256,2048]{1,0:T(8,128)(2,1)}, u32[]{:S(2)}, u32[]{:S(2)}) %collective-permute-start.8) | collective-permute-done | bytes 1048608 | tf_op jit(solution)/shard_map/ppermute | solution.py:57
  74.1 2.2 %fusion.42 = f32[256,768]{1,0:T(8,128)S(1)} fusion(bf16[256,2048]{1,0:T(8,128)(2,1)} %collective-permute-done.6, bf16[1,2048,768]{2,1,0:T(8,128)(2,1)S(1)} %copy-done), kind=kOutput, calls=%fused_computation.42 | convolution fusion | flops 805306368 | bytes 4980736 | tf_op jit(solution)/shard_map/dot_general | solution.py:11
  76.3 2.2 %multiply_convert_fusion.5 = bf16[256,768]{1,0:T(8,128)(2,1)S(1)} fusion(f32[256,768]{1,0:T(8,128)S(1)} %fusion.42, bf16[256,2048]{1,0:T(8,128)(2,1)} %collective-permute-done.6, bf16[1,2048,768]{2,1,0:T(8,128)(2,1)S(1)} %copy-done.23), kind=kOutput, calls=%fused_computation.101 | convolution fusion | flops 806486016 | bytes 5373952 | tf_op jit(solution)/shard_map/dot_general | solution.py:12
  78.8 2.2 %fusion.40 = f32[256,768]{1,0:T(8,128)S(1)} fusion(bf16[256,2048]{1,0:T(8,128)(2,1)} %collective-permute-done.8, bf16[1,2048,768]{2,1,0:T(8,128)(2,1)S(1)} %copy-done), kind=kOutput, calls=%fused_computation.40 | convolution fusion | flops 805306368 | bytes 4980736 | tf_op jit(solution)/shard_map/dot_general | solution.py:11
  81.0 3.0 %multiply_convert_fusion.4 = bf16[256,768]{1,0:T(8,128)(2,1)} fusion(f32[256,768]{1,0:T(8,128)S(1)} %fusion.40, bf16[256,2048]{1,0:T(8,128)(2,1)} %collective-permute-done.8, bf16[1,2048,768]{2,1,0:T(8,128)(2,1)S(1)} %copy-done.23), kind=kOutput, calls=%fused_computation.100 | convolution fusion | flops 806486016 | bytes 5373952 | tf_op jit(solution)/shard_map/dot_general | solution.py:12
  84.0 2.6 %convolution_add_fusion.5 = f32[4,64,64]{2,1,0:T(8,128)} fusion(f32[4,64,64]{2,1,0:T(8,128)} %convolution_add_fusion.6, bf16[256,2048]{1,0:T(8,128)(2,1)} %collective-permute-done.7, bf16[1,2048,64]{1,2,0:T(8,128)(2,1)S(1)} %copy-done.1, bf16[256,64]{0,1:T(8,128)(2,1)S(1)} %convolution_convert_fusion.5, bf16[256,4]{0,1:T(4,128)(2,1)} %get-tuple-element.38, ...), kind=kOutput, calls=%fused_computation.62 | convolution fusion | flops 75612160 | bytes 1477632 | tf_op jit(solution)/shard_map/dot_general | solution.py:28
  86.6 1.4 convolution_convert_fusion.4
  88.6 3.9 %multiply_reduce_fusion.4 = f32[256]{0:T(256)} fusion(bf16[256,2048]{1,0:T(8,128)(2,1)} %collective-permute-done.9, bf16[256,768]{1,0:T(8,128)(2,1)} %multiply_convert_fusion.4, bf16[1,768,2048]{2,1,0:T(8,128)(2,1)} %param.18), kind=kOutput, calls=%fused_computation.52 | convolution fusion | flops 806878976 | bytes 4588544 | tf_op jit(solution)/shard_map/dot_general | solution.py:17
  92.6 2.9 %multiply_reduce_fusion.5 = f32[256]{0:T(256)} fusion(bf16[256,2048]{1,0:T(8,128)(2,1)} %collective-permute-done.7, bf16[256,768]{1,0:T(8,128)(2,1)S(1)} %copy-done.7, bf16[1,768,2048]{2,1,0:T(8,128)(2,1)S(1)} %copy-done.27), kind=kOutput, calls=%fused_computation.53 | convolution fusion | flops 806878976 | bytes 4588544 | tf_op jit(solution)/shard_map/dot_general | solution.py:17
  95.5 2.6 %convolution_add_fusion.4 = f32[4,64,64]{2,1,0:T(8,128)} fusion(f32[4,64,64]{2,1,0:T(8,128)} %convolution_add_fusion.5, bf16[256,2048]{1,0:T(8,128)(2,1)} %collective-permute-done.9, bf16[1,2048,64]{1,2,0:T(8,128)(2,1)S(1)} %copy-done.1, bf16[256,64]{0,1:T(8,128)(2,1)S(1)} %convolution_convert_fusion.4, bf16[256,4]{0,1:T(4,128)(2,1)} %get-tuple-element.39, ...), kind=kOutput, calls=%fused_computation.61 | convolution fusion | flops 75612160 | bytes 1477632 | tf_op jit(solution)/shard_map/dot_general | solution.py:28
  98.1 1.9 %slice.113 = bf16[128,2048]{1,0:T(8,128)(2,1)} slice(bf16[256,2048]{1,0:T(8,128)(2,1)} %collective-permute-done.13), slice={[0:128], [0:2048]} | slice | bytes 1048576 | tf_op jit(solution)/shard_map/slice | solution.py:104
  100.6 2.3 %slice.111 = bf16[128,2048]{1,0:T(8,128)(2,1)} slice(bf16[256,2048]{1,0:T(8,128)(2,1)} %collective-permute-done.12), slice={[0:128], [0:2048]} | slice | bytes 1048576 | tf_op jit(solution)/shard_map/slice | solution.py:104
  103.6 2.2 %fusion.36 = f32[256,768]{1,0:T(8,128)S(1)} fusion(bf16[256,2048]{1,0:T(8,128)(2,1)} %collective-permute-done.12, bf16[1,2048,768]{2,1,0:T(8,128)(2,1)S(1)} %copy-done), kind=kOutput, calls=%fused_computation.36 | convolution fusion | flops 805306368 | bytes 4980736 | tf_op jit(solution)/shard_map/dot_general | solution.py:11
  105.8 2.2 %multiply_convert_fusion.2 = bf16[256,768]{1,0:T(8,128)(2,1)S(1)} fusion(f32[256,768]{1,0:T(8,128)S(1)} %fusion.36, bf16[256,2048]{1,0:T(8,128)(2,1)} %collective-permute-done.12, bf16[1,2048,768]{2,1,0:T(8,128)(2,1)S(1)} %copy-done.24), kind=kOutput, calls=%fused_computation.98 | convolution fusion | flops 806486016 | bytes 5373952 | tf_op jit(solution)/shard_map/dot_general | solution.py:12
  108.7 2.5 %fusion.38 = f32[256,768]{1,0:T(8,128)S(1)} fusion(bf16[256,2048]{1,0:T(8,128)(2,1)} %collective-permute-done.10, bf16[1,2048,768]{2,1,0:T(8,128)(2,1)S(1)} %copy-done), kind=kOutput, calls=%fused_computation.38 | convolution fusion | flops 805306368 | bytes 4980736 | tf_op jit(solution)/shard_map/dot_general | solution.py:11
  111.2 2.9 %multiply_reduce_fusion.2 = f32[256]{0:T(256)} fusion(bf16[256,2048]{1,0:T(8,128)(2,1)} %collective-permute-done.13, bf16[256,768]{1,0:T(8,128)(2,1)S(1)} %multiply_convert_fusion.2, bf16[1,768,2048]{2,1,0:T(8,128)(2,1)S(1)} %copy-done.28), kind=kOutput, calls=%fused_computation.50 | convolution fusion | flops 806878976 | bytes 4588544 | tf_op jit(solution)/shard_map/dot_general | solution.py:17
  114.1 2.3 %multiply_convert_fusion.3 = bf16[256,768]{1,0:T(8,128)(2,1)S(1)} fusion(f32[256,768]{1,0:T(8,128)S(1)} %fusion.38, bf16[256,2048]{1,0:T(8,128)(2,1)} %collective-permute-done.10, bf16[1,2048,768]{2,1,0:T(8,128)(2,1)S(1)} %copy-done.24), kind=kOutput, calls=%fused_computation.99 | convolution fusion | flops 806486016 | bytes 5373952 | tf_op jit(solution)/shard_map/dot_general | solution.py:12
  116.4 2.9 %multiply_reduce_fusion.3 = f32[256]{0:T(256)} fusion(bf16[256,2048]{1,0:T(8,128)(2,1)} %collective-permute-done.11, bf16[256,768]{1,0:T(8,128)(2,1)S(1)} %multiply_convert_fusion.3, bf16[1,768,2048]{2,1,0:T(8,128)(2,1)S(1)} %copy-done.28), kind=kOutput, calls=%fused_computation.51 | convolution fusion | flops 806878976 | bytes 4588544 | tf_op jit(solution)/shard_map/dot_general | solution.py:17
  120.4 2.6 %convolution_add_fusion.3 = f32[4,64,64]{2,1,0:T(8,128)} fusion(f32[4,64,64]{2,1,0:T(8,128)} %convolution_add_fusion.4, bf16[256,2048]{1,0:T(8,128)(2,1)} %collective-permute-done.11, bf16[1,2048,64]{1,2,0:T(8,128)(2,1)S(1)} %copy-done.1, bf16[256,64]{0,1:T(8,128)(2,1)} %convolution_convert_fusion.3, bf16[256,4]{0,1:T(4,128)(2,1)} %get-tuple-element.40, ...), kind=kOutput, calls=%fused_computation.60 | convolution fusion | flops 75612160 | bytes 1477632 | tf_op jit(solution)/shard_map/dot_general | solution.py:28
  123.0 2.6 %convolution_add_fusion.2 = f32[4,64,64]{2,1,0:T(8,128)} fusion(f32[4,64,64]{2,1,0:T(8,128)} %convolution_add_fusion.3, bf16[256,2048]{1,0:T(8,128)(2,1)} %collective-permute-done.13, bf16[1,2048,64]{1,2,0:T(8,128)(2,1)S(1)} %copy-done.1, bf16[256,64]{0,1:T(8,128)(2,1)S(1)} %convolution_convert_fusion.2, bf16[256,4]{0,1:T(4,128)(2,1)S(1)} %get-tuple-element.41, ...), kind=kOutput, calls=%fused_computation.59 | convolution fusion | flops 75612160 | bytes 1477632 | tf_op jit(solution)/shard_map/dot_general | solution.py:28
  128.3 1.2 constant_dynamic-update-slice_fusion.8
  132.5 1.7 %multiply_reduce_fusion = f32[256]{0:T(256)} fusion(bf16[256,2048]{1,0:T(8,128)(2,1)S(1)} %constant_dynamic-update-slice_fusion.10, bf16[256,768]{1,0:T(8,128)(2,1)S(1)} %multiply_convert_fusion, bf16[1,768,2048]{2,1,0:T(8,128)(2,1)S(1)} %copy-done.29), kind=kOutput, calls=%fused_computation.48 | convolution fusion | flops 806878976 | bytes 4588544 | tf_op jit(solution)/shard_map/dot_general | solution.py:17
  134.1 2.2 %fusion.34 = f32[256,768]{1,0:T(8,128)S(1)} fusion(bf16[256,2048]{1,0:T(8,128)(2,1)} %collective-permute-done.14, bf16[1,2048,768]{2,1,0:T(8,128)(2,1)S(1)} %copy-done), kind=kOutput, calls=%fused_computation.34 | convolution fusion | flops 805306368 | bytes 4980736 | tf_op jit(solution)/shard_map/dot_general | solution.py:11
  136.3 2.2 %multiply_convert_fusion.1 = bf16[256,768]{1,0:T(8,128)(2,1)S(1)} fusion(f32[256,768]{1,0:T(8,128)S(1)} %fusion.34, bf16[256,2048]{1,0:T(8,128)(2,1)} %collective-permute-done.14, bf16[1,2048,768]{2,1,0:T(8,128)(2,1)S(1)} %copy-done.25), kind=kOutput, calls=%fused_computation.97 | convolution fusion | flops 806486016 | bytes 5373952 | tf_op jit(solution)/shard_map/dot_general | solution.py:12
  139.6 2.3 %multiply_reduce_fusion.1 = f32[256]{0:T(256)S(1)} fusion(bf16[256,2048]{1,0:T(8,128)(2,1)} %collective-permute-done.15, bf16[256,768]{1,0:T(8,128)(2,1)S(1)} %multiply_convert_fusion.1, bf16[1,768,2048]{2,1,0:T(8,128)(2,1)S(1)} %copy-done.29), kind=kOutput, calls=%fused_computation.49 | convolution fusion | flops 806878976 | bytes 4588544 | tf_op jit(solution)/shard_map/dot_general | solution.py:17
  142.7 4.1 %all-to-all-start.1 = ((f32[16,1,128]{2,1,0:T(1,128)}), f32[16,1,128]{2,1,0:T(1,128)S(1)}, u32[]{:S(2)}, u32[]{:S(2)}) async-start(f32[16,1,128]{2,1,0:T(1,128)} %bitcast.58), calls=%async_computation.1 | async-start | bytes 16384 | tf_op jit(solution)/shard_map/all_to_all | solution.py:125
  146.9 2.6 %convolution_add_fusion.1 = f32[4,64,64]{2,1,0:T(8,128)} fusion(f32[4,64,64]{2,1,0:T(8,128)} %convolution_add_fusion.2, bf16[256,2048]{1,0:T(8,128)(2,1)} %collective-permute-done.15, bf16[1,2048,64]{1,2,0:T(8,128)(2,1)S(1)} %copy-done.1, bf16[256,64]{0,1:T(8,128)(2,1)S(1)} %copy-done.10, bf16[256,4]{0,1:T(4,128)(2,1)S(1)} %get-tuple-element.42, ...), kind=kOutput, calls=%fused_computation.58 | convolution fusion | flops 75612160 | bytes 1477632 | tf_op jit(solution)/shard_map/dot_general | solution.py:28
  149.5 2.6 %fusion.48 = f32[4,1,64,64]{3,2,1,0:T(8,128)} fusion(f32[4,64,64]{2,1,0:T(8,128)} %convolution_add_fusion.1, bf16[256,2048]{1,0:T(8,128)(2,1)} %copy-done.5, bf16[1,2048,64]{1,2,0:T(8,128)(2,1)S(1)} %copy-done.1, bf16[256,64]{0,1:T(8,128)(2,1)S(1)} %convolution_convert_fusion, bf16[256,4]{0,1:T(4,128)(2,1)S(1)} %get-tuple-element.36, f32[256]{0:T(256)S(1)} %bitcast.293), kind=kOutput, calls=%fused_computation.57 | convolution fusion | flops 75612160 | bytes 1477632 | tf_op jit(solution)/shard_map/dot_general | solution.py:28
  152.0 1.2 all-to-all-done.1
  (125 shorter events, 24.3 us)
Async XLA Ops:
  0.6 23.2 %copy-start = (bf16[1,2048,768]{2,1,0:T(8,128)(2,1)S(1)}, bf16[1,2048,768]{2,1,0:T(8,128)(2,1)}, u32[]{:S(2)}) copy-start(bf16[1,2048,768]{2,1,0:T(8,128)(2,1)} %param.16) | copy-start | bytes 9437188
  0.6 21.1 %collective-permute-start = (bf16[128,2048]{1,0:T(8,128)(2,1)}, bf16[128,2048]{1,0:T(8,128)(2,1)}, u32[]{:S(2)}, u32[]{:S(2)}) collective-permute-start(bf16[128,2048]{1,0:T(8,128)(2,1)} %param.11), channel_id=1, source_target_pairs={{0,1},{1,0},{2,3},{3,2},{4,5},{5,4},{6,7},{7,6},{8,9},{9,8},{10,11... | collective-permute-start | bytes 1572872 | tf_op jit(solution)/shard_map/ppermute | solution.py:60
  1.2 30.4 %collective-permute-start.2 = (bf16[128,2048]{1,0:T(8,128)(2,1)}, bf16[128,2048]{1,0:T(8,128)(2,1)}, u32[]{:S(2)}, u32[]{:S(2)}) collective-permute-start(bf16[128,2048]{1,0:T(8,128)(2,1)} %param.11), channel_id=1, source_target_pairs={{0,4},{1,3},{4,8},{5,1},{8,12},{9,5},{12,14},{13,9},{14,10},{15,13... | collective-permute-start | bytes 1572872 | tf_op jit(solution)/shard_map/ppermute | solution.py:57
  3.8 23.4 %collective-permute-start.1 = (bf16[128,2048]{1,0:T(8,128)(2,1)}, bf16[128,2048]{1,0:T(8,128)(2,1)}, u32[]{:S(2)}, u32[]{:S(2)}) collective-permute-start(bf16[128,2048]{1,0:T(8,128)(2,1)} %param.12), channel_id=1, source_target_pairs={{0,1},{1,0},{2,3},{3,2},{4,5},{5,4},{6,7},{7,6},{8,9},{9,8},{10,11... | collective-permute-start | bytes 1572872 | tf_op jit(solution)/shard_map/ppermute | solution.py:60
  3.9 29.6 %collective-permute-start.4 = (bf16[128,2048]{1,0:T(8,128)(2,1)}, bf16[128,2048]{1,0:T(8,128)(2,1)}, u32[]{:S(2)}, u32[]{:S(2)}) collective-permute-start(bf16[128,2048]{1,0:T(8,128)(2,1)} %param.12), channel_id=1, source_target_pairs={{0,4},{1,3},{4,8},{5,1},{8,12},{9,5},{12,14},{13,9},{14,10},{15,13... | collective-permute-start | bytes 1572872 | tf_op jit(solution)/shard_map/ppermute | solution.py:57
  7.4 12.9 %all-to-all-start = ((bf16[16,2,128]{2,1,0:T(2,128)(2,1)}), bf16[16,2,128]{2,1,0:T(2,128)(2,1)S(1)}, u32[]{:S(2)}, u32[]{:S(2)}) async-start(bf16[16,2,128]{2,1,0:T(2,128)(2,1)} %copy.32), calls=%async_computation | async-start | bytes 16384 | tf_op jit(solution)/shard_map/all_to_all | solution.py:88
  21.8 4.4 %copy-start.21 = (bf16[1,2048,768]{2,1,0:T(8,128)(2,1)S(1)}, bf16[1,2048,768]{2,1,0:T(8,128)(2,1)}, u32[]{:S(2)}) copy-start(bf16[1,2048,768]{2,1,0:T(8,128)(2,1)} %param.17) | copy-start | bytes 9437188
  23.8 2.3 %copy-start.9 = (bf16[256,2048]{1,0:T(8,128)(2,1)S(1)}, bf16[256,2048]{1,0:T(8,128)(2,1)}, u32[]{:S(2)}) copy-start(bf16[256,2048]{1,0:T(8,128)(2,1)} %constant_dynamic-update-slice_fusion) | copy-start | bytes 3145732
  26.1 2.4 %copy-start.26 = (bf16[1,768,2048]{2,1,0:T(8,128)(2,1)S(1)}, bf16[1,768,2048]{2,1,0:T(8,128)(2,1)}, u32[]{:S(2)}) copy-start(bf16[1,768,2048]{2,1,0:T(8,128)(2,1)} %param.18) | copy-start | bytes 9437188
  27.2 4.1 %copy-start.2 = (bf16[1,768,64]{1,2,0:T(8,128)(2,1)S(1)}, bf16[1,768,64]{1,2,0:T(8,128)(2,1)}, u32[]{:S(2)}) copy-start(bf16[1,768,64]{1,2,0:T(8,128)(2,1)} %param.19) | copy-start | bytes 294916
  28.5 4.9 %copy-start.4 = (bf16[256,2048]{1,0:T(8,128)(2,1)}, bf16[256,2048]{1,0:T(8,128)(2,1)S(1)}, u32[]{:S(2)}) copy-start(bf16[256,2048]{1,0:T(8,128)(2,1)S(1)} %constant_dynamic-update-slice_fusion.2) | copy-start | bytes 3145732
  28.5 6.8 %copy-start.1 = (bf16[1,2048,64]{1,2,0:T(8,128)(2,1)S(1)}, bf16[1,2048,64]{1,2,0:T(8,128)(2,1)}, u32[]{:S(2)}) copy-start(bf16[1,2048,64]{1,2,0:T(8,128)(2,1)} %param.20) | copy-start | bytes 786436
  30.2 17.5 %collective-permute-start.3 = (bf16[128,2048]{1,0:T(8,128)(2,1)}, bf16[128,2048]{1,0:T(8,128)(2,1)}, u32[]{:S(2)}, u32[]{:S(2)}) collective-permute-start(bf16[128,2048]{1,0:T(8,128)(2,1)} %collective-permute-done), channel_id=1, source_target_pairs={{0,4},{1,3},{4,8},{5,1},{8,12},{9,5},{12,14},{13,9},{14,10},{15,13... | collective-permute-start | bytes 1572872 | tf_op jit(solution)/shard_map/ppermute | solution.py:57
  30.7 14.6 %collective-permute-start.5 = (bf16[128,2048]{1,0:T(8,128)(2,1)}, bf16[128,2048]{1,0:T(8,128)(2,1)}, u32[]{:S(2)}, u32[]{:S(2)}) collective-permute-start(bf16[128,2048]{1,0:T(8,128)(2,1)} %collective-permute-done.1), channel_id=1, source_target_pairs={{0,4},{1,3},{4,8},{5,1},{8,12},{9,5},{12,14},{13,9},{14,10},{15,13... | collective-permute-start | bytes 1572872 | tf_op jit(solution)/shard_map/ppermute | solution.py:57
  47.2 6.4 %copy-start.22 = (bf16[1,2048,768]{2,1,0:T(8,128)(2,1)S(1)}, bf16[1,2048,768]{2,1,0:T(8,128)(2,1)}, u32[]{:S(2)}) copy-start(bf16[1,2048,768]{2,1,0:T(8,128)(2,1)} %param.17) | copy-start | bytes 9437188
  47.2 16.2 %collective-permute-start.9 = (bf16[256,2048]{1,0:T(8,128)(2,1)}, bf16[256,2048]{1,0:T(8,128)(2,1)}, u32[]{:S(2)}, u32[]{:S(2)}) collective-permute-start(bf16[256,2048]{1,0:T(8,128)(2,1)} %constant_dynamic-update-slice_fusion.6), channel_id=1, source_target_pairs={{0,4},{1,3},{4,8},{5,1},{8,12},{9,5},{12,14},{13,9},{14,10},{15,13... | collective-permute-start | bytes 3145736 | tf_op jit(solution)/shard_map/ppermute | solution.py:57
  47.7 36.3 %collective-permute-start.7 = (bf16[256,2048]{1,0:T(8,128)(2,1)}, bf16[256,2048]{1,0:T(8,128)(2,1)}, u32[]{:S(2)}, u32[]{:S(2)}) collective-permute-start(bf16[256,2048]{1,0:T(8,128)(2,1)} %constant_dynamic-update-slice_fusion.6), channel_id=1, source_target_pairs={{0,1},{1,0},{2,3},{3,2},{4,5},{5,4},{6,7},{7,6},{8,9},{9,8},{10,11... | collective-permute-start | bytes 3145736 | tf_op jit(solution)/shard_map/ppermute | solution.py:60
  52.1 21.5 %collective-permute-start.8 = (bf16[256,2048]{1,0:T(8,128)(2,1)}, bf16[256,2048]{1,0:T(8,128)(2,1)}, u32[]{:S(2)}, u32[]{:S(2)}) collective-permute-start(bf16[256,2048]{1,0:T(8,128)(2,1)} %constant_dynamic-update-slice_fusion.4), channel_id=1, source_target_pairs={{0,4},{1,3},{4,8},{5,1},{8,12},{9,5},{12,14},{13,9},{14,10},{15,13... | collective-permute-start | bytes 3145736 | tf_op jit(solution)/shard_map/ppermute | solution.py:57
  52.7 21.3 %collective-permute-start.6 = (bf16[256,2048]{1,0:T(8,128)(2,1)}, bf16[256,2048]{1,0:T(8,128)(2,1)}, u32[]{:S(2)}, u32[]{:S(2)}) collective-permute-start(bf16[256,2048]{1,0:T(8,128)(2,1)} %constant_dynamic-update-slice_fusion.4), channel_id=1, source_target_pairs={{0,1},{1,0},{2,3},{3,2},{4,5},{5,4},{6,7},{7,6},{8,9},{9,8},{10,11... | collective-permute-start | bytes 3145736 | tf_op jit(solution)/shard_map/ppermute | solution.py:60
  63.4 12.9 %copy-start.23 = (bf16[1,2048,768]{2,1,0:T(8,128)(2,1)S(1)}, bf16[1,2048,768]{2,1,0:T(8,128)(2,1)}, u32[]{:S(2)}) copy-start(bf16[1,2048,768]{2,1,0:T(8,128)(2,1)} %param.17) | copy-start | bytes 9437188
  63.4 34.7 %collective-permute-start.13 = (bf16[256,2048]{1,0:T(8,128)(2,1)}, bf16[256,2048]{1,0:T(8,128)(2,1)}, u32[]{:S(2)}, u32[]{:S(2)}) collective-permute-start(bf16[256,2048]{1,0:T(8,128)(2,1)} %collective-permute-done.9), channel_id=1, source_target_pairs={{0,4},{1,3},{4,8},{5,1},{8,12},{9,5},{12,14},{13,9},{14,10},{15,13... | collective-permute-start | bytes 3145736 | tf_op jit(solution)/shard_map/ppermute | solution.py:57
  73.6 27.0 %collective-permute-start.12 = (bf16[256,2048]{1,0:T(8,128)(2,1)}, bf16[256,2048]{1,0:T(8,128)(2,1)}, u32[]{:S(2)}, u32[]{:S(2)}) collective-permute-start(bf16[256,2048]{1,0:T(8,128)(2,1)} %collective-permute-done.8), channel_id=1, source_target_pairs={{0,4},{1,3},{4,8},{5,1},{8,12},{9,5},{12,14},{13,9},{14,10},{15,13... | collective-permute-start | bytes 3145736 | tf_op jit(solution)/shard_map/ppermute | solution.py:57
  78.5 5.5 %copy-start.6 = (bf16[256,768]{1,0:T(8,128)(2,1)}, bf16[256,768]{1,0:T(8,128)(2,1)S(1)}, u32[]{:S(2)}) copy-start(bf16[256,768]{1,0:T(8,128)(2,1)S(1)} %multiply_convert_fusion.5) | copy-start | bytes 1179652
  86.6 5.9 %copy-start.7 = (bf16[256,768]{1,0:T(8,128)(2,1)S(1)}, bf16[256,768]{1,0:T(8,128)(2,1)}, u32[]{:S(2)}) copy-start(bf16[256,768]{1,0:T(8,128)(2,1)} %copy-done.6) | copy-start | bytes 1179652
  86.6 5.9 %copy-start.27 = (bf16[1,768,2048]{2,1,0:T(8,128)(2,1)S(1)}, bf16[1,768,2048]{2,1,0:T(8,128)(2,1)}, u32[]{:S(2)}) copy-start(bf16[1,768,2048]{2,1,0:T(8,128)(2,1)} %param.18) | copy-start | bytes 9437188
  88.0 28.4 %collective-permute-start.11 = (bf16[256,2048]{1,0:T(8,128)(2,1)}, bf16[256,2048]{1,0:T(8,128)(2,1)}, u32[]{:S(2)}, u32[]{:S(2)}) collective-permute-start(bf16[256,2048]{1,0:T(8,128)(2,1)} %collective-permute-done.9), channel_id=1, source_target_pairs={{0,1},{1,0},{2,3},{3,2},{4,5},{5,4},{6,7},{7,6},{8,9},{9,8},{10,11... | collective-permute-start | bytes 3145736 | tf_op jit(solution)/shard_map/ppermute | solution.py:60
  88.1 20.0 %collective-permute-start.10 = (bf16[256,2048]{1,0:T(8,128)(2,1)}, bf16[256,2048]{1,0:T(8,128)(2,1)}, u32[]{:S(2)}, u32[]{:S(2)}) collective-permute-start(bf16[256,2048]{1,0:T(8,128)(2,1)} %collective-permute-done.8), channel_id=1, source_target_pairs={{0,1},{1,0},{2,3},{3,2},{4,5},{5,4},{6,7},{7,6},{8,9},{9,8},{10,11... | collective-permute-start | bytes 3145736 | tf_op jit(solution)/shard_map/ppermute | solution.py:60
  100.0 5.9 %copy-start.24 = (bf16[1,2048,768]{2,1,0:T(8,128)(2,1)S(1)}, bf16[1,2048,768]{2,1,0:T(8,128)(2,1)}, u32[]{:S(2)}) copy-start(bf16[1,2048,768]{2,1,0:T(8,128)(2,1)} %param.17) | copy-start | bytes 9437188
  100.0 25.6 %collective-permute-start.18 = (bf16[128,2048]{1,0:T(8,128)(2,1)}, bf16[128,2048]{1,0:T(8,128)(2,1)}, u32[]{:S(2)}, u32[]{:S(2)}) collective-permute-start(bf16[128,2048]{1,0:T(8,128)(2,1)} %slice.113), channel_id=1, source_target_pairs={{0,4},{1,3},{4,8},{5,1},{8,12},{9,5},{12,14},{13,9},{14,10},{15,13... | collective-permute-start | bytes 1572872 | tf_op jit(solution)/shard_map/ppermute | solution.py:57
  102.8 20.2 %collective-permute-start.16 = (bf16[128,2048]{1,0:T(8,128)(2,1)}, bf16[128,2048]{1,0:T(8,128)(2,1)}, u32[]{:S(2)}, u32[]{:S(2)}) collective-permute-start(bf16[128,2048]{1,0:T(8,128)(2,1)} %slice.111), channel_id=1, source_target_pairs={{0,4},{1,3},{4,8},{5,1},{8,12},{9,5},{12,14},{13,9},{14,10},{15,13... | collective-permute-start | bytes 1572872 | tf_op jit(solution)/shard_map/ppermute | solution.py:57
  103.6 35.9 %collective-permute-start.15 = (bf16[256,2048]{1,0:T(8,128)(2,1)}, bf16[256,2048]{1,0:T(8,128)(2,1)}, u32[]{:S(2)}, u32[]{:S(2)}) collective-permute-start(bf16[256,2048]{1,0:T(8,128)(2,1)} %collective-permute-done.13), channel_id=1, source_target_pairs={{0,1},{1,0},{2,3},{3,2},{4,5},{5,4},{6,7},{7,6},{8,9},{9,8},{10,11... | collective-permute-start | bytes 3145736 | tf_op jit(solution)/shard_map/ppermute | solution.py:60
  108.1 3.1 %copy-start.28 = (bf16[1,768,2048]{2,1,0:T(8,128)(2,1)S(1)}, bf16[1,768,2048]{2,1,0:T(8,128)(2,1)}, u32[]{:S(2)}) copy-start(bf16[1,768,2048]{2,1,0:T(8,128)(2,1)} %param.18) | copy-start | bytes 9437188
  108.1 26.0 %collective-permute-start.14 = (bf16[256,2048]{1,0:T(8,128)(2,1)}, bf16[256,2048]{1,0:T(8,128)(2,1)}, u32[]{:S(2)}, u32[]{:S(2)}) collective-permute-start(bf16[256,2048]{1,0:T(8,128)(2,1)} %collective-permute-done.12), channel_id=1, source_target_pairs={{0,1},{1,0},{2,3},{3,2},{4,5},{5,4},{6,7},{7,6},{8,9},{9,8},{10,11... | collective-permute-start | bytes 3145736 | tf_op jit(solution)/shard_map/ppermute | solution.py:60
  123.0 5.3 %collective-permute-start.17 = (bf16[128,2048]{1,0:T(8,128)(2,1)}, bf16[128,2048]{1,0:T(8,128)(2,1)}, u32[]{:S(2)}, u32[]{:S(2)}) collective-permute-start(bf16[128,2048]{1,0:T(8,128)(2,1)} %collective-permute-done.16), channel_id=1, source_target_pairs={{0,1},{1,0},{2,3},{3,2},{4,5},{5,4},{6,7},{7,6},{8,9},{9,8},{10,11... | collective-permute-start | bytes 1572872 | tf_op jit(solution)/shard_map/ppermute | solution.py:60
  125.6 6.2 %collective-permute-start.19 = (bf16[128,2048]{1,0:T(8,128)(2,1)}, bf16[128,2048]{1,0:T(8,128)(2,1)S(1)}, u32[]{:S(2)}, u32[]{:S(2)}) collective-permute-start(bf16[128,2048]{1,0:T(8,128)(2,1)} %collective-permute-done.18), channel_id=1, source_target_pairs={{0,1},{1,0},{2,3},{3,2},{4,5},{5,4},{6,7},{7,6},{8,9},{9,8},{10,11... | collective-permute-start | bytes 1572872 | tf_op jit(solution)/shard_map/ppermute | solution.py:60
  132.5 3.9 %copy-start.5 = (bf16[256,2048]{1,0:T(8,128)(2,1)}, bf16[256,2048]{1,0:T(8,128)(2,1)S(1)}, u32[]{:S(2)}) copy-start(bf16[256,2048]{1,0:T(8,128)(2,1)S(1)} %constant_dynamic-update-slice_fusion.10) | copy-start | bytes 3145732
  138.6 8.3 %copy-start.13 = (f32[2,1,128]{2,1,0:T(1,128)S(1)}, f32[2,1,128]{2,1,0:T(1,128)}, u32[]{:S(2)}) copy-start(f32[2,1,128]{2,1,0:T(1,128)} %get-tuple-element.35) | copy-start | bytes 3076
  139.5 2.4 %copy-start.14 = (f32[256]{0:T(256)S(1)}, f32[256]{0:T(256)}, u32[]{:S(2)}) copy-start(f32[256]{0:T(256)} %multiply_reduce_fusion.7) | copy-start | bytes 3076
  139.5 2.4 %copy-start.15 = (f32[256]{0:T(256)S(1)}, f32[256]{0:T(256)}, u32[]{:S(2)}) copy-start(f32[256]{0:T(256)} %multiply_reduce_fusion.6) | copy-start | bytes 3076
  139.5 2.4 %copy-start.16 = (f32[256]{0:T(256)S(1)}, f32[256]{0:T(256)}, u32[]{:S(2)}) copy-start(f32[256]{0:T(256)} %multiply_reduce_fusion.4) | copy-start | bytes 3076
  139.5 2.5 %copy-start.17 = (f32[256]{0:T(256)S(1)}, f32[256]{0:T(256)}, u32[]{:S(2)}) copy-start(f32[256]{0:T(256)} %multiply_reduce_fusion.5) | copy-start | bytes 3076
  139.5 2.5 %copy-start.18 = (f32[256]{0:T(256)S(1)}, f32[256]{0:T(256)}, u32[]{:S(2)}) copy-start(f32[256]{0:T(256)} %multiply_reduce_fusion.2) | copy-start | bytes 3076
  139.5 2.5 %copy-start.19 = (f32[256]{0:T(256)S(1)}, f32[256]{0:T(256)}, u32[]{:S(2)}) copy-start(f32[256]{0:T(256)} %multiply_reduce_fusion.3) | copy-start | bytes 3076
  139.5 2.5 %copy-start.20 = (f32[256]{0:T(256)S(1)}, f32[256]{0:T(256)}, u32[]{:S(2)}) copy-start(f32[256]{0:T(256)} %multiply_reduce_fusion) | copy-start | bytes 3076
  139.5 7.4 %copy-start.10 = (bf16[256,64]{0,1:T(8,128)(2,1)S(1)}, bf16[256,64]{0,1:T(8,128)(2,1)}, u32[]{:S(2)}) copy-start(bf16[256,64]{0,1:T(8,128)(2,1)} %convolution_convert_fusion.1) | copy-start | bytes 98308
  139.5 9.9 %copy-start.12 = (f32[2,1,128]{2,1,0:T(1,128)S(1)}, f32[2,1,128]{2,1,0:T(1,128)}, u32[]{:S(2)}) copy-start(f32[2,1,128]{2,1,0:T(1,128)} %get-tuple-element.20) | copy-start | bytes 3076
  139.5 13.7 %copy-start.11 = (s32[128,8]{0,1:T(8,128)S(1)}, s32[128,8]{0,1:T(8,128)}, u32[]{:S(2)}) copy-start(s32[128,8]{0,1:T(8,128)} %param.13) | copy-start | bytes 12292
  142.7 10.5 %all-to-all-start.1 = ((f32[16,1,128]{2,1,0:T(1,128)}), f32[16,1,128]{2,1,0:T(1,128)S(1)}, u32[]{:S(2)}, u32[]{:S(2)}) async-start(f32[16,1,128]{2,1,0:T(1,128)} %bitcast.58), calls=%async_computation.1 | async-start | bytes 16384 | tf_op jit(solution)/shard_map/all_to_all | solution.py:125
  (4 other events, 6.1 us)

commit v4 on v3

--- a/solution.py
+++ b/solution.py
@@ -1,7 +1,11 @@
+import functools
+
 import jax
 import jax.numpy as jnp
 import numpy as np
 from jax import lax
+from jax.experimental import pallas as pl
+from jax.experimental.pallas import tpu as pltpu
 from jax.sharding import PartitionSpec as P
 
 DOC_TOK = 512
@@ -36,6 +40,137 @@
     table = jnp.arange(experts, dtype=jnp.int32)
     hit = routes[:, :, None] == table
     return jnp.sum(jnp.where(hit, returned.T[:, None, :], 0.0), axis=-1)
+
+
+def rows_kernel(blocks, begin, first, *refs):
+    order, meta = refs[:2]
+    x_in, dy_in = refs[2 : 2 + blocks], refs[2 + blocks : 2 + 2 * blocks]
+    w_gate, w_up, w_down, low_proj, high_proj = refs[2 + 2 * blocks : 7 + 2 * blocks]
+    grads, feat, x_all, dy_all, low_sum, grad_sum, sems = refs[-7:]
+    tile = pl.program_id(0)
+    rows = x_in[0].shape[0]
+    across = (((1,), (1,)), ((), ()))
+
+    @pl.when(tile == 0)
+    def _():
+        copies = []
+        for i in range(blocks):
+            place = pl.ds(i * rows, rows)
+            copies.append(pltpu.make_async_copy(x_in[i], x_all.at[place], sems.at[2 * i]))
+            copies.append(pltpu.make_async_copy(dy_in[i], dy_all.at[place], sems.at[2 * i + 1]))
+        for copy in copies:
+            copy.start()
+        low_sum[...] = jnp.zeros_like(low_sum)
+        grad_sum[...] = jnp.zeros_like(grad_sum)
+        if first:
+            grads[...] = jnp.zeros_like(grads)
+            feat[...] = jnp.zeros_like(feat)
+        else:
+            grads_in, feat_in = refs[7 + 2 * blocks : 9 + 2 * blocks]
+            grads[...] = grads_in[...]
+            feat[...] = feat_in[...]
+        for copy in copies:
+            copy.wait()
+
+    gate_val = jnp.dot(x_all[...], w_gate[...], preferred_element_type=jnp.float32)
+    up_val = jnp.dot(x_all[...], w_up[...], preferred_element_type=jnp.float32)
+    hidden = (jax.nn.silu(gate_val) * up_val).astype(jnp.bfloat16)
+    back = lax.dot_general(dy_all[...], w_down[...], across, preferred_element_type=jnp.float32)
+    terms = hidden.astype(jnp.float32) * back
+    lanes = grad_sum.shape[1]
+    for cut in range(0, terms.shape[1], lanes):
+        grad_sum[...] += terms[:, cut : cut + lanes]
+    low_sum[...] += lax.dot_general(
+        hidden, low_proj[...], across, preferred_element_type=jnp.float32
+    )
+
+    @pl.when(tile == pl.num_programs(0) - 1)
+    def _():
+        proj_cot = lax.dot_general(
+            dy_all[...], high_proj[...], across, preferred_element_type=jnp.float32
+        )
+        rank = proj_cot.shape[1]
+        width = low_sum.shape[1]
+        doc_of = lax.broadcasted_iota(jnp.int32, (rows, width), 1) // rank
+        spread, high_side = [], []
+        for i in range(blocks):
+            place = slice(i * rows, (i + 1) * rows)
+            owner = order[begin + i]
+            facts = meta[pl.ds(owner, 1), :]
+            weight = jnp.transpose(jnp.broadcast_to(facts[:, :rows], (rows, rows)))
+            doc = jnp.transpose(jnp.broadcast_to(facts[:, rows:], (rows, rows)))
+            doc = jnp.concatenate([doc] * (width // rows), axis=1).astype(jnp.int32)
+            high_side.append((weight[:, :rank] * proj_cot[place]).astype(jnp.bfloat16))
+            low_side = jnp.where(doc == doc_of, low_sum[place, :], 0.0)
+            spread.append(low_side.astype(jnp.bfloat16))
+            grads[pl.ds(owner, 1), :] = jnp.sum(
+                jnp.transpose(grad_sum[place, :]), axis=0, keepdims=True
+            )
+        feat[...] += lax.dot_general(
+            jnp.concatenate(spread, axis=0),
+            jnp.concatenate(high_side, axis=0),
+            (((0,), (0,)), ((), ())),
+            preferred_element_type=jnp.float32,
+        )
+
+
+def work(begin, order, meta, x_in, dy_in, weights, sums, after):
+    w_gate, w_up, w_down, low_proj, high_proj = weights
+    blocks = len(x_in)
+    rows, width = x_in[0].shape
+    hidden = w_gate.shape[2]
+    tile = 256 if hidden % 256 == 0 else hidden
+    groups = order.shape[0]
+    low_width, rank = low_proj.shape[0], high_proj.shape[0]
+    anywhere = pl.BlockSpec(memory_space=pl.ANY)
+
+    def whole(shape):
+        return pl.BlockSpec(shape, lambda j: (0,) * len(shape))
+
+    sum_shapes = ((groups, rows), (low_width, rank))
+    call = pl.pallas_call(
+        functools.partial(rows_kernel, blocks, begin, not sums),
+        grid=(hidden // tile,),
+        out_shape=[jax.ShapeDtypeStruct(shape, jnp.float32) for shape in sum_shapes],
+        in_specs=[pl.BlockSpec(memory_space=pltpu.SMEM), whole(meta.shape)]
+        + [anywhere] * (2 * blocks)
+        + [
+            pl.BlockSpec((None, width, tile), lambda j: (0, 0, j)),
+            pl.BlockSpec((None, width, tile), lambda j: (0, 0, j)),
+            pl.BlockSpec((None, tile, width), lambda j: (0, j, 0)),
+            pl.BlockSpec((low_width, tile), lambda j: (0, j)),
+            whole(high_proj.shape),
+        ]
+        + [whole(shape) for shape in sum_shapes[: len(sums)]]
+        + [anywhere] * len(after),
+        out_specs=[whole(shape) for shape in sum_shapes],
+        scratch_shapes=[
+            pltpu.VMEM((blocks * rows, width), jnp.bfloat16),
+            pltpu.VMEM((blocks * rows, width), jnp.bfloat16),
+            pltpu.VMEM((blocks * rows, low_width), jnp.float32),
+            pltpu.VMEM((blocks * rows, 128), jnp.float32),
+            pltpu.SemaphoreType.DMA((2 * blocks,)),
+        ],
+        compiler_params=pltpu.CompilerParams(vmem_limit_bytes=60 * 1024 * 1024),
+        cost_estimate=pl.CostEstimate(
+            flops=6 * blocks * rows * width * hidden,
+            bytes_accessed=6 * width * hidden + 4 * blocks * rows * width,
+            transcendentals=blocks * rows * hidden,
+        ),
+    )
+    return call(order, meta, *x_in, *dy_in, *weights, *sums, *after)
+
+
+def facts_kernel(routes, combine, doc_ids, after, out):
+    groups, rows = out.shape[0], routes.shape[1]
+    expert = lax.broadcasted_iota(jnp.int32, (groups, rows), 0)
+    weight = jnp.zeros((groups, rows), jnp.float32)
+    for k in range(routes.shape[0]):
+        share = combine[k : k + 1, :].astype(jnp.float32)
+        weight += jnp.where(routes[k : k + 1, :] == expert, share, 0.0)
+    out[:, :rows] = weight.astype(out.dtype)
+    doc = jnp.broadcast_to(doc_ids[...], (groups, rows)).astype(jnp.float32)
+    out[:, rows:] = doc.astype(out.dtype)
 
 
 def by_ring(
@@ -70,60 +205,61 @@
             order = [owner(0, core), owner(0, 1 - core)]
             for step in range(1, half + 1):
                 near, far = -step * way, step * way
+                order += [owner(near, core), owner(far, 1 - core)]
                 if step < half:
-                    order += [owner(near, core), owner(near, 1 - core)]
-                    order += [owner(far, 1 - core), owner(far, core)]
-                else:
-                    order += [owner(near, core), owner(far, 1 - core)]
+                    order += [owner(near, 1 - core), owner(far, core)]
             orders[owner(0, core)] = order
     me = lax.axis_index("exp")
-    mine = lax.dynamic_index_in_dim(jnp.asarray(orders), me, axis=0, keepdims=False)
-    owned = mine[:, None] == jnp.arange(groups, dtype=jnp.int32)
-
-    table = jnp.arange(groups, dtype=jnp.int32)
-    weight = jnp.sum(
-        jnp.where(routes[None, :, :] == table[:, None, None], combine[None, :, :], 0), axis=-1
-    ).astype(jnp.bfloat16)
-    own_doc = jnp.broadcast_to(doc_ids.astype(jnp.bfloat16)[None, :], weight.shape)
-    meta = lax.all_to_all(
-        jnp.stack([weight, own_doc], axis=1), "exp", split_axis=0, concat_axis=0, tiled=True
-    )
-    meta = jnp.sum(
-        jnp.where(owned[:, :, None, None], meta[None].astype(jnp.float32), 0.0), axis=1
-    ).astype(jnp.bfloat16)
-
-    x, dy = tokens, cotangent
-    x_beside, dy_beside = swap(x), swap(dy)
-    sets = [(jnp.concatenate([x, x_beside]), jnp.concatenate([dy, dy_beside]))]
-    x = jnp.concatenate([hop(x), hop(x_beside)])
-    dy = jnp.concatenate([hop(dy), hop(dy_beside)])
-    for step in range(1, half):
-        sets += [(x, dy), (swap(x), swap(dy))]
-        if step < half - 1:
-            x, dy = hop(x), hop(dy)
-    x, dy = hop(x[:tok_rows]), hop(dy[:tok_rows])
-    sets.append((jnp.concatenate([x, swap(x)]), jnp.concatenate([dy, swap(dy)])))
-
-    grads, feature = [], 0.0
-    for begin, (x, dy) in enumerate(sets):
-        part = meta[2 * begin : 2 * begin + 2]
-        hidden = swiglu(x, w_gate[0], w_up[0])
-        grad, term = finish(
-            hidden,
-            dy,
-            part[:, 0].reshape(-1),
-            part[:, 1].reshape(-1),
-            w_down[0],
-            proj_hidden[0],
-            proj_output[0],
-            docs_count,
+    order = lax.dynamic_index_in_dim(jnp.asarray(orders), me, axis=0, keepdims=False)
+
+    own = (tokens, cotangent)
+    beside = (swap(tokens), swap(cotangent))
+    near = [(own, beside)]
+    far = []
+    for step in range(1, half + 1):
+        pairs = near[-1] if step < half else near[-1][:1]
+        arrived = tuple((hop(x), hop(dy)) for x, dy in pairs)
+        near.append(arrived)
+        far.append(tuple((swap(x), swap(dy)) for x, dy in arrived))
+
+    facts = pl.pallas_call(
+        facts_kernel,
+        out_shape=jax.ShapeDtypeStruct((groups, 2 * tok_rows), jnp.bfloat16),
+        in_specs=[pl.BlockSpec(memory_space=pltpu.VMEM)] * 3
+        + [pl.BlockSpec(memory_space=pl.ANY)],
+        out_specs=pl.BlockSpec(memory_space=pltpu.VMEM),
+    )(routes.T, combine.T, doc_ids[None, :], beside[0])
+    meta = lax.all_to_all(facts, "exp", split_axis=0, concat_axis=0, tiled=True)
+    meta = meta.astype(jnp.float32)
+
+    low_proj = jnp.concatenate([proj_hidden[0].T] * docs_count, axis=0)
+    weights = (w_gate, w_up, w_down, low_proj, proj_output[0].T)
+    jobs = [((own, beside), near[1][0][1])]
+    for step in range(1, half + 1):
+        for side in range(len(near[step])):
+            if step == half:
+                after = None
+            elif side == 0:
+                after = near[step][1][1]
+            else:
+                after = near[step + 1][0][1 if step + 1 < half else 0]
+            jobs.append(((near[step][side], far[step - 1][side]), after))
+    sums = []
+    for i, (pair, after) in enumerate(jobs):
+        sums = work(
+            2 * i,
+            order,
+            meta,
+            [block[0] for block in pair],
+            [block[1] for block in pair],
+            weights,
+            sums,
+            [] if after is None else [after],
         )
-        grads.append(grad.reshape(2, tok_rows))
-        feature = feature + term
-    grads = jnp.concatenate(grads, axis=0)
-    grads = jnp.sum(jnp.where(owned[:, :, None], grads[:, None, :], 0.0), axis=0)
+    grads, feature = sums
     returned = lax.all_to_all(grads, "exp", split_axis=0, concat_axis=0, tiled=True)
-    return feature[:, None], pick_own(returned, routes)
+    rank = proj_output.shape[2]
+    return feature.reshape(docs_count, 1, rank, rank), pick_own(returned, routes)
 
 
 def by_routing(

time: 155 us -> 162 us (1.045)
  matrix products: 80.3 us -> 0 us
  Pallas kernels: 0 us -> 76.8 us
  local copies, waits for them, and re-layouts: 25.3 us -> 4.91 us
  starting transfers between devices: 21 us -> 31.8 us
  blocking collectives: 0 us -> 10.4 us
  waiting for transfers between devices: 21.7 us -> 31.7 us
    dot_general x40 -> x0, matrix products: 80.3 us -> none  [the longest x8 22.2 us: finish(): out_val = jnp.dot(hidden, w_down, preferred_element_type=jnp.float32)]
    pallas_call x0 -> x9, Pallas kernels: none -> 76.8 us  [the longest x8 75.5 us: work(): return call(order, meta, *x_in, *dy_in, *weights, *sums, *after)]
    ppermute x10 -> x14, starting transfers between devices: 8.79 us -> 23.3 us  [hop(): return lax.ppermute(block, 'exp', onward)]
    all_to_all x0 -> x1, blocking collectives: none -> 10.4 us  [by_ring(): lax.all_to_all(grads, 'exp', split_axis=0, concat_axis=0, tiled=True)]
    ppermute x10 -> x14, waiting for transfers between devices: 17 us -> 25.7 us  [hop(): return lax.ppermute(block, 'exp', onward)]
    concatenate x7 -> x0, local copies, waits for them, and re-layouts: 8.58 us -> none  [the longest x2 3.19 us: by_ring(): sets = [(jnp.concatenate([x, x_beside]), jnp.concatenate([dy, dy_beside]))]]
    unnamed x66 -> x44, local copies, waits for them, and re-layouts: 11.3 us -> 3.19 us
    all_to_all x2 -> x1, starting transfers between devices: 9.08 us -> 4.9 us  [by_ring(): meta = lax.all_to_all(facts, 'exp', split_axis=0, concat_axis=0, tiled=True)]
  transfers between devices with their start and end apart: 22 -> 31, of which waited for: 4 -> 8; matrix products, arithmetic and copies ran while one was open for 68% -> 4% of each run, Pallas kernels for 0% -> 42%
where the time goes in v4:
time: 162 us; the launch traced here: 161 us
  Pallas kernels  76.8 us (47%)
  starting transfers between devices  31.8 us (20%)
  waiting for transfers between devices  31.7 us (20%)
  blocking collectives  10.4 us (6%)
  local copies, waits for them, and re-layouts  4.91 us (3%)
  other arithmetic  4.42 us (3%)
    pallas_call x8, Pallas kernels, work(): return call(order, meta, *x_in, *dy_in, *weights, *sums, *after)  75.5 us
    ppermute x14, waiting for transfers between devices, hop(): return lax.ppermute(block, 'exp', onward)  25.7 us
    ppermute x14, starting transfers between devices, hop(): return lax.ppermute(block, 'exp', onward)  23.3 us
    all_to_all x1, blocking collectives, by_ring(): lax.all_to_all(grads, 'exp', split_axis=0, concat_axis=0, tiled=True)  10.4 us
    all_to_all x1, waiting for transfers between devices, by_ring(): meta = lax.all_to_all(facts, 'exp', split_axis=0, concat_axis=0, tiled=True)  5.97 us
    all_to_all x1, starting transfers between devices, by_ring(): meta = lax.all_to_all(facts, 'exp', split_axis=0, concat_axis=0, tiled=True)  4.9 us
    ppermute x16, starting transfers between devices, swap(): return lax.ppermute(block, 'exp', across)  3.57 us
  transfers between devices with their start and end apart: 31, of which 8 were waited for; matrix products, arithmetic and copies ran while one was open for 4% of the time, Pallas kernels for 42%

profile of v4, /device:TPU:0, one launch (start us, length us, event | category | flops | bytes accessed | tf_op | source)
XLA Modules:
  0.0 160.9 jit_solution(13942307255049803672)
XLA Ops:
  0.6 0.5 collective-permute-start.15
  1.2 3.0 %collective-permute-start.6 = (bf16[128,2048]{1,0:T(8,128)(2,1)}, bf16[128,2048]{1,0:T(8,128)(2,1)S(1)}, u32[]{:S(2)}, u32[]{:S(2)}) collective-permute-start(bf16[128,2048]{1,0:T(8,128)(2,1)} %refs_4_.1), channel_id=1, source_target_pairs={{0,4},{1,3},{4,8},{5,1},{8,12},{9,5},{12,14},{13,9},{14,10},{15,13... | collective-permute-start | bytes 1572872 | tf_op jit(solution)/shard_map/ppermute | solution.py:192
  4.2 1.6 collective-permute-start.1
  5.8 1.6 collective-permute-start.16
  7.4 1.5 collective-permute-start.11
  8.9 2.6 %collective-permute-done.6.refs_11_.refs_4_ = bf16[128,2048]{1,0:T(8,128)(2,1)S(1)} collective-permute-done((bf16[128,2048]{1,0:T(8,128)(2,1)}, bf16[128,2048]{1,0:T(8,128)(2,1)S(1)}, u32[]{:S(2)}, u32[]{:S(2)}) %collective-permute-start.6) | collective-permute-done | bytes 524320 | tf_op jit(solution)/shard_map/ppermute | solution.py:192
  11.5 5.6 %collective-permute-done.1.refs_2_ = bf16[128,2048]{1,0:T(8,128)(2,1)S(1)} collective-permute-done((bf16[128,2048]{1,0:T(8,128)(2,1)}, bf16[128,2048]{1,0:T(8,128)(2,1)S(1)}, u32[]{:S(2)}, u32[]{:S(2)}) %collective-permute-start.1) | collective-permute-done | bytes 524320 | tf_op jit(solution)/shard_map/ppermute | solution.py:192
  17.1 2.1 %collective-permute-start.7 = (bf16[128,2048]{1,0:T(8,128)(2,1)S(1)}, bf16[128,2048]{1,0:T(8,128)(2,1)S(1)}, u32[]{:S(2)}, u32[]{:S(2)}) collective-permute-start(bf16[128,2048]{1,0:T(8,128)(2,1)S(1)} %collective-permute-done.6.refs_11_.refs_4_), channel_id=1, source_target_pairs={{0,4},{1,3},{4,8},{5,1},{8,12},{9,5},{12,14},{13,9},{14,10},{15,13... | collective-permute-start | bytes 1572872 | tf_op jit(solution)/shard_map/ppermute | solution.py:192
  19.2 3.5 %collective-permute-done.16.refs_13_.refs_4_ = bf16[128,2048]{1,0:T(8,128)(2,1)S(1)} collective-permute-done((bf16[128,2048]{1,0:T(8,128)(2,1)S(1)}, bf16[128,2048]{1,0:T(8,128)(2,1)S(1)}, u32[]{:S(2)}, u32[]{:S(2)}) %collective-permute-start.16) | collective-permute-done | bytes 524320 | tf_op jit(solution)/shard_map/ppermute | solution.py:192
  22.8 2.1 %collective-permute-start.2 = (bf16[128,2048]{1,0:T(8,128)(2,1)S(1)}, bf16[128,2048]{1,0:T(8,128)(2,1)}, u32[]{:S(2)}, u32[]{:S(2)}) collective-permute-start(bf16[128,2048]{1,0:T(8,128)(2,1)S(1)} %collective-permute-done.1.refs_2_), channel_id=1, source_target_pairs={{0,4},{1,3},{4,8},{5,1},{8,12},{9,5},{12,14},{13,9},{14,10},{15,13... | collective-permute-start | bytes 1572872 | tf_op jit(solution)/shard_map/ppermute | solution.py:192
  24.9 3.6 %collective-permute-done.11.refs_2_ = bf16[128,2048]{1,0:T(8,128)(2,1)} collective-permute-done((bf16[128,2048]{1,0:T(8,128)(2,1)S(1)}, bf16[128,2048]{1,0:T(8,128)(2,1)}, u32[]{:S(2)}, u32[]{:S(2)}) %collective-permute-start.11) | collective-permute-done | bytes 524320 | tf_op jit(solution)/shard_map/ppermute | solution.py:192
  28.5 0.5 collective-permute-start.27
  29.0 2.2 %collective-permute-start.17 = (bf16[128,2048]{1,0:T(8,128)(2,1)S(1)}, bf16[128,2048]{1,0:T(8,128)(2,1)S(1)}, u32[]{:S(2)}, u32[]{:S(2)}) collective-permute-start(bf16[128,2048]{1,0:T(8,128)(2,1)S(1)} %collective-permute-done.16.refs_13_.refs_4_), channel_id=1, source_target_pairs={{0,4},{1,3},{4,8},{5,1},{8,12},{9,5},{12,14},{13,9},{14,10},{15,13... | collective-permute-start | bytes 1572872 | tf_op jit(solution)/shard_map/ppermute | solution.py:192
  31.2 2.8 %collective-permute-done.7.refs_13_.refs_4_ = bf16[128,2048]{1,0:T(8,128)(2,1)S(1)} collective-permute-done((bf16[128,2048]{1,0:T(8,128)(2,1)S(1)}, bf16[128,2048]{1,0:T(8,128)(2,1)S(1)}, u32[]{:S(2)}, u32[]{:S(2)}) %collective-permute-start.7) | collective-permute-done | bytes 524320 | tf_op jit(solution)/shard_map/ppermute | solution.py:192
  34.0 5.7 %collective-permute-done.2.refs_2_ = bf16[128,2048]{1,0:T(8,128)(2,1)} collective-permute-done((bf16[128,2048]{1,0:T(8,128)(2,1)S(1)}, bf16[128,2048]{1,0:T(8,128)(2,1)}, u32[]{:S(2)}, u32[]{:S(2)}) %collective-permute-start.2) | collective-permute-done | bytes 524320 | tf_op jit(solution)/shard_map/ppermute | solution.py:192
  39.7 2.1 %collective-permute-start.12 = (bf16[128,2048]{1,0:T(8,128)(2,1)}, bf16[128,2048]{1,0:T(8,128)(2,1)}, u32[]{:S(2)}, u32[]{:S(2)}) collective-permute-start(bf16[128,2048]{1,0:T(8,128)(2,1)} %collective-permute-done.11.refs_2_), channel_id=1, source_target_pairs={{0,4},{1,3},{4,8},{5,1},{8,12},{9,5},{12,14},{13,9},{14,10},{15,13... | collective-permute-start | bytes 1572872 | tf_op jit(solution)/shard_map/ppermute | solution.py:192
  41.9 1.6 %collective-permute-start.8 = (bf16[128,2048]{1,0:T(8,128)(2,1)S(1)}, bf16[128,2048]{1,0:T(8,128)(2,1)S(1)}, u32[]{:S(2)}, u32[]{:S(2)}) collective-permute-start(bf16[128,2048]{1,0:T(8,128)(2,1)S(1)} %collective-permute-done.7.refs_13_.refs_4_), channel_id=1, source_target_pairs={{0,4},{1,3},{4,8},{5,1},{8,12},{9,5},{12,14},{13,9},{14,10},{15,13... | collective-permute-start | bytes 1572872 | tf_op jit(solution)/shard_map/ppermute | solution.py:192
  43.5 1.7 %collective-permute-done.17.refs_13_.refs_4_ = bf16[128,2048]{1,0:T(8,128)(2,1)S(1)} collective-permute-done((bf16[128,2048]{1,0:T(8,128)(2,1)S(1)}, bf16[128,2048]{1,0:T(8,128)(2,1)S(1)}, u32[]{:S(2)}, u32[]{:S(2)}) %collective-permute-start.17) | collective-permute-done | bytes 524320 | tf_op jit(solution)/shard_map/ppermute | solution.py:192
  45.2 2.1 %collective-permute-start.3 = (bf16[128,2048]{1,0:T(8,128)(2,1)}, bf16[128,2048]{1,0:T(8,128)(2,1)}, u32[]{:S(2)}, u32[]{:S(2)}) collective-permute-start(bf16[128,2048]{1,0:T(8,128)(2,1)} %collective-permute-done.2.refs_2_), channel_id=1, source_target_pairs={{0,4},{1,3},{4,8},{5,1},{8,12},{9,5},{12,14},{13,9},{14,10},{15,13... | collective-permute-start | bytes 1572872 | tf_op jit(solution)/shard_map/ppermute | solution.py:192
  47.3 1.9 %pad_maximum_fusion.refs_9_ = bf16[256,768]{1,0:T(8,128)(2,1)} fusion(bf16[64,768]{1,0:T(8,128)(2,1)} %bitcast.32), kind=kLoop, calls=%fused_computation | loop fusion | flops 1572864 | bytes 491520 | tf_op jit(solution)/shard_map/concatenate | solution.py:235
  49.2 1.3 shard_map.122
  50.5 0.5 broadcast.2
  51.0 1.3 reduce
  52.4 0.6 reshape.17
  53.0 4.9 %all-to-all-start = ((bf16[16,2,128]{2,1,0:T(2,128)(2,1)}), bf16[16,2,128]{2,1,0:T(2,128)(2,1)S(1)}, u32[]{:S(2)}, u32[]{:S(2)}) async-start(bf16[16,2,128]{2,1,0:T(2,128)(2,1)} %reshape.17), calls=%async_computation | async-start | bytes 16384 | tf_op jit(solution)/shard_map/all_to_all | solution.py:232
  57.9 0.5 collective-permute-start.23
  58.5 1.2 dynamic-slice_bitcast_fusion.refs_0_
  59.7 6.0 %all-to-all-done = bf16[16,2,128]{2,1,0:T(2,128)(2,1)S(1)} async-done(((bf16[16,2,128]{2,1,0:T(2,128)(2,1)}), bf16[16,2,128]{2,1,0:T(2,128)(2,1)S(1)}, u32[]{:S(2)}, u32[]{:S(2)}) %all-to-all-start) | async-done | bytes 8224 | tf_op jit(solution)/shard_map/all_to_all | solution.py:232
  65.7 0.6 collective-permute-start.18
  66.2 0.6 bitcast_convert_fusion.refs_1_
  66.8 0.6 collective-permute-start.13
  67.4 9.4 %shard_map.123 = (f32[16,128]{1,0:T(8,128)}, f32[256,64]{1,0:T(8,128)}) custom-call(s32[16]{0:T(128)} %dynamic-slice_bitcast_fusion.refs_0_, f32[16,256]{1,0:T(8,128)} %bitcast_convert_fusion.refs_1_, bf16[128,2048]{1,0:T(8,128)(2,1)} %refs_2_.1, bf16[128,2048]{1,0:T(8,128)(2,1)} %copy-done.7, bf16[128,2048]{1,0:T(8,128)(2,1)} %refs_4_.1, ...), custom_call_target="tpu_custom_call" | custom-call | flops 2415919104 | bytes 11534336 | tf_op jit(solution)/shard_map/pallas_call | solution.py:161
  76.9 0.8 collective-permute-start.9
  77.8 1.5 collective-permute-start.4
  79.2 9.4 %shard_map.124 = (f32[16,128]{1,0:T(8,128)}, f32[256,64]{1,0:T(8,128)}) custom-call(s32[16]{0:T(128)} %dynamic-slice_bitcast_fusion.refs_0_, f32[16,256]{1,0:T(8,128)} %bitcast_convert_fusion.refs_1_, bf16[128,2048]{1,0:T(8,128)(2,1)} %copy-done.8, bf16[128,2048]{1,0:T(8,128)(2,1)} %copy-done.11, bf16[128,2048]{1,0:T(8,128)(2,1)} %copy-done.3, ...), custom_call_target="tpu_custom_call" | custom-call | flops 2415919104 | bytes 11534336 | tf_op jit(solution)/shard_map/pallas_call | solution.py:161
  88.7 0.7 collective-permute-start.20
  89.4 9.4 %shard_map.125 = (f32[16,128]{1,0:T(8,128)}, f32[256,64]{1,0:T(8,128)}) custom-call(s32[16]{0:T(128)} %dynamic-slice_bitcast_fusion.refs_0_, f32[16,256]{1,0:T(8,128)} %bitcast_convert_fusion.refs_1_, bf16[128,2048]{1,0:T(8,128)(2,1)} %collective-permute-done.11.refs_2_, bf16[128,2048]{1,0:T(8,128)(2,1)} %copy-done.12, bf16[128,2048]{1,0:T(8,128)(2,1)} %copy-done, ...), custom_call_target="tpu_custom_call" | custom-call | flops 2415919104 | bytes 11534336 | tf_op jit(solution)/shard_map/pallas_call | solution.py:161
  99.1 0.4 collective-permute-start.14
  99.5 9.4 %shard_map.126 = (f32[16,128]{1,0:T(8,128)}, f32[256,64]{1,0:T(8,128)}) custom-call(s32[16]{0:T(128)} %dynamic-slice_bitcast_fusion.refs_0_, f32[16,256]{1,0:T(8,128)} %bitcast_convert_fusion.refs_1_, bf16[128,2048]{1,0:T(8,128)(2,1)} %collective-permute-done.2.refs_2_, bf16[128,2048]{1,0:T(8,128)(2,1)} %collective-permute-done.24.refs_3_, ...), custom_call_target="tpu_custom_call" | custom-call | flops 2415919104 | bytes 11534336 | tf_op jit(solution)/shard_map/pallas_call | solution.py:161
  109.5 9.4 %shard_map.127 = (f32[16,128]{1,0:T(8,128)}, f32[256,64]{1,0:T(8,128)}) custom-call(s32[16]{0:T(128)} %dynamic-slice_bitcast_fusion.refs_0_, f32[16,256]{1,0:T(8,128)} %bitcast_convert_fusion.refs_1_, bf16[128,2048]{1,0:T(8,128)(2,1)} %collective-permute-done.12.refs_2_, bf16[128,2048]{1,0:T(8,128)(2,1)} %collective-permute-done.22.refs_3_, ...), custom_call_target="tpu_custom_call" | custom-call | flops 2415919104 | bytes 11534336 | tf_op jit(solution)/shard_map/pallas_call | solution.py:161
  119.0 0.8 copy-done.16
  119.8 9.4 %shard_map.128 = (f32[16,128]{1,0:T(8,128)}, f32[256,64]{1,0:T(8,128)}) custom-call(s32[16]{0:T(128)} %dynamic-slice_bitcast_fusion.refs_0_, f32[16,256]{1,0:T(8,128)} %bitcast_convert_fusion.refs_1_, bf16[128,2048]{1,0:T(8,128)(2,1)} %collective-permute-done.3.refs_2_, bf16[128,2048]{1,0:T(8,128)(2,1)} %copy-done.16, bf16[128,2048]{1,0:T(8,128)(2,1)} %copy-done.4, ...), custom_call_target="tpu_custom_call" | custom-call | flops 2415919104 | bytes 11534336 | tf_op jit(solution)/shard_map/pallas_call | solution.py:161
  129.2 0.8 copy-done.17
  130.2 9.4 %shard_map.129 = (f32[16,128]{1,0:T(8,128)}, f32[256,64]{1,0:T(8,128)}) custom-call(s32[16]{0:T(128)} %dynamic-slice_bitcast_fusion.refs_0_, f32[16,256]{1,0:T(8,128)} %bitcast_convert_fusion.refs_1_, bf16[128,2048]{1,0:T(8,128)(2,1)} %collective-permute-done.13.refs_2_, bf16[128,2048]{1,0:T(8,128)(2,1)} %copy-done.19, bf16[128,2048]{1,0:T(8,128)(2,1)} %copy-done.5, ...), custom_call_target="tpu_custom_call" | custom-call | flops 2415919104 | bytes 11534336 | tf_op jit(solution)/shard_map/pallas_call | solution.py:161
  139.7 0.8 copy-done.18
  140.4 9.4 %shard_map.130 = (f32[16,128]{1,0:T(8,128)}, f32[256,64]{1,0:T(8,128)}) custom-call(s32[16]{0:T(128)} %dynamic-slice_bitcast_fusion.refs_0_, f32[16,256]{1,0:T(8,128)} %bitcast_convert_fusion.refs_1_, bf16[128,2048]{1,0:T(8,128)(2,1)} %copy-done.6, bf16[128,2048]{1,0:T(8,128)(2,1)} %collective-permute-done.5.refs_3_, bf16[128,2048]{1,0:T(8,128)(2,1)} %copy-done.15, ...), custom_call_target="tpu_custom_call" | custom-call | flops 2415919104 | bytes 11534336 | tf_op jit(solution)/shard_map/pallas_call | solution.py:161
  149.9 10.4 %all_to_all.21 = f32[16,1,128]{2,1,0:T(1,128)S(1)} all-to-all(f32[16,1,128]{2,1,0:T(1,128)} %bitcast.36), channel_id=1, replica_groups=mesh['grp'=2,'exp'=16] {'exp'}, dimensions={0} | all-to-all | bytes 16384 | tf_op jit(solution)/shard_map/all_to_all | solution.py:260
  160.3 0.6 select_reduce_fusion
  (74 shorter events, 1.3 us)
Async XLA Ops:
  0.6 5.2 %collective-permute-start.15 = (bf16[128,2048]{1,0:T(8,128)(2,1)}, bf16[128,2048]{1,0:T(8,128)(2,1)S(1)}, u32[]{:S(2)}, u32[]{:S(2)}) collective-permute-start(bf16[128,2048]{1,0:T(8,128)(2,1)} %refs_4_.1), channel_id=1, source_target_pairs={{0,1},{1,0},{2,3},{3,2},{4,5},{5,4},{6,7},{7,6},{8,9},{9,8},{10,11... | collective-permute-start | bytes 1572872 | tf_op jit(solution)/shard_map/ppermute | solution.py:195
  1.1 6.2 %collective-permute-start = (bf16[128,2048]{1,0:T(8,128)(2,1)}, bf16[128,2048]{1,0:T(8,128)(2,1)S(1)}, u32[]{:S(2)}, u32[]{:S(2)}) collective-permute-start(bf16[128,2048]{1,0:T(8,128)(2,1)} %refs_2_.1), channel_id=1, source_target_pairs={{0,1},{1,0},{2,3},{3,2},{4,5},{5,4},{6,7},{7,6},{8,9},{9,8},{10,11... | collective-permute-start | bytes 1572872 | tf_op jit(solution)/shard_map/ppermute | solution.py:195
  1.2 10.3 %collective-permute-start.6 = (bf16[128,2048]{1,0:T(8,128)(2,1)}, bf16[128,2048]{1,0:T(8,128)(2,1)S(1)}, u32[]{:S(2)}, u32[]{:S(2)}) collective-permute-start(bf16[128,2048]{1,0:T(8,128)(2,1)} %refs_4_.1), channel_id=1, source_target_pairs={{0,4},{1,3},{4,8},{5,1},{8,12},{9,5},{12,14},{13,9},{14,10},{15,13... | collective-permute-start | bytes 1572872 | tf_op jit(solution)/shard_map/ppermute | solution.py:192
  4.2 12.9 %collective-permute-start.1 = (bf16[128,2048]{1,0:T(8,128)(2,1)}, bf16[128,2048]{1,0:T(8,128)(2,1)S(1)}, u32[]{:S(2)}, u32[]{:S(2)}) collective-permute-start(bf16[128,2048]{1,0:T(8,128)(2,1)} %refs_2_.1), channel_id=1, source_target_pairs={{0,4},{1,3},{4,8},{5,1},{8,12},{9,5},{12,14},{13,9},{14,10},{15,13... | collective-permute-start | bytes 1572872 | tf_op jit(solution)/shard_map/ppermute | solution.py:192
  5.8 23.2 %copy-start.9 = (bf16[128,2048]{1,0:T(8,128)(2,1)}, bf16[128,2048]{1,0:T(8,128)(2,1)S(1)}, u32[]{:S(2)}) copy-start(bf16[128,2048]{1,0:T(8,128)(2,1)S(1)} %collective-permute-done.15.refs_5_) | copy-start | bytes 1572868
  5.8 16.9 %collective-permute-start.16 = (bf16[128,2048]{1,0:T(8,128)(2,1)S(1)}, bf16[128,2048]{1,0:T(8,128)(2,1)S(1)}, u32[]{:S(2)}, u32[]{:S(2)}) collective-permute-start(bf16[128,2048]{1,0:T(8,128)(2,1)S(1)} %collective-permute-done.15.refs_5_), channel_id=1, source_target_pairs={{0,4},{1,3},{4,8},{5,1},{8,12},{9,5},{12,14},{13,9},{14,10},{15,13... | collective-permute-start | bytes 1572872 | tf_op jit(solution)/shard_map/ppermute | solution.py:192
  7.4 41.8 %copy-start.7 = (bf16[128,2048]{1,0:T(8,128)(2,1)}, bf16[128,2048]{1,0:T(8,128)(2,1)S(1)}, u32[]{:S(2)}) copy-start(bf16[128,2048]{1,0:T(8,128)(2,1)S(1)} %collective-permute-done.after.refs_3_) | copy-start | bytes 1572868
  7.4 21.1 %collective-permute-start.11 = (bf16[128,2048]{1,0:T(8,128)(2,1)S(1)}, bf16[128,2048]{1,0:T(8,128)(2,1)}, u32[]{:S(2)}, u32[]{:S(2)}) collective-permute-start(bf16[128,2048]{1,0:T(8,128)(2,1)S(1)} %collective-permute-done.after.refs_3_), channel_id=1, source_target_pairs={{0,4},{1,3},{4,8},{5,1},{8,12},{9,5},{12,14},{13,9},{14,10},{15,13... | collective-permute-start | bytes 1572872 | tf_op jit(solution)/shard_map/ppermute | solution.py:192
  11.5 55.9 %copy-start.3 = (bf16[128,2048]{1,0:T(8,128)(2,1)}, bf16[128,2048]{1,0:T(8,128)(2,1)S(1)}, u32[]{:S(2)}) copy-start(bf16[128,2048]{1,0:T(8,128)(2,1)S(1)} %collective-permute-done.6.refs_11_.refs_4_) | copy-start | bytes 1572868
  11.5 17.0 %collective-permute-start.29 = (bf16[128,2048]{1,0:T(8,128)(2,1)S(1)}, bf16[128,2048]{1,0:T(8,128)(2,1)S(1)}, u32[]{:S(2)}, u32[]{:S(2)}) collective-permute-start(bf16[128,2048]{1,0:T(8,128)(2,1)S(1)} %collective-permute-done.6.refs_11_.refs_4_), channel_id=1, source_target_pairs={{0,1},{1,0},{2,3},{3,2},{4,5},{5,4},{6,7},{7,6},{8,9},{9,8},{10,11... | collective-permute-start | bytes 1572872 | tf_op jit(solution)/shard_map/ppermute | solution.py:195
  17.1 24.7 %copy-start.8 = (bf16[128,2048]{1,0:T(8,128)(2,1)}, bf16[128,2048]{1,0:T(8,128)(2,1)S(1)}, u32[]{:S(2)}) copy-start(bf16[128,2048]{1,0:T(8,128)(2,1)S(1)} %collective-permute-done.1.refs_2_) | copy-start | bytes 1572868
  17.1 11.9 %collective-permute-start.28 = (bf16[128,2048]{1,0:T(8,128)(2,1)S(1)}, bf16[128,2048]{1,0:T(8,128)(2,1)S(1)}, u32[]{:S(2)}, u32[]{:S(2)}) collective-permute-start(bf16[128,2048]{1,0:T(8,128)(2,1)S(1)} %collective-permute-done.1.refs_2_), channel_id=1, source_target_pairs={{0,1},{1,0},{2,3},{3,2},{4,5},{5,4},{6,7},{7,6},{8,9},{9,8},{10,11... | collective-permute-start | bytes 1572872 | tf_op jit(solution)/shard_map/ppermute | solution.py:195
  17.1 16.8 %collective-permute-start.7 = (bf16[128,2048]{1,0:T(8,128)(2,1)S(1)}, bf16[128,2048]{1,0:T(8,128)(2,1)S(1)}, u32[]{:S(2)}, u32[]{:S(2)}) collective-permute-start(bf16[128,2048]{1,0:T(8,128)(2,1)S(1)} %collective-permute-done.6.refs_11_.refs_4_), channel_id=1, source_target_pairs={{0,4},{1,3},{4,8},{5,1},{8,12},{9,5},{12,14},{13,9},{14,10},{15,13... | collective-permute-start | bytes 1572872 | tf_op jit(solution)/shard_map/ppermute | solution.py:192
  22.7 54.1 %copy-start = (bf16[128,2048]{1,0:T(8,128)(2,1)}, bf16[128,2048]{1,0:T(8,128)(2,1)S(1)}, u32[]{:S(2)}) copy-start(bf16[128,2048]{1,0:T(8,128)(2,1)S(1)} %collective-permute-done.16.refs_13_.refs_4_) | copy-start | bytes 1572868
  22.8 17.0 %collective-permute-start.2 = (bf16[128,2048]{1,0:T(8,128)(2,1)S(1)}, bf16[128,2048]{1,0:T(8,128)(2,1)}, u32[]{:S(2)}, u32[]{:S(2)}) collective-permute-start(bf16[128,2048]{1,0:T(8,128)(2,1)S(1)} %collective-permute-done.1.refs_2_), channel_id=1, source_target_pairs={{0,4},{1,3},{4,8},{5,1},{8,12},{9,5},{12,14},{13,9},{14,10},{15,13... | collective-permute-start | bytes 1572872 | tf_op jit(solution)/shard_map/ppermute | solution.py:192
  28.5 13.3 %collective-permute-start.26 = (bf16[128,2048]{1,0:T(8,128)(2,1)}, bf16[128,2048]{1,0:T(8,128)(2,1)S(1)}, u32[]{:S(2)}, u32[]{:S(2)}) collective-permute-start(bf16[128,2048]{1,0:T(8,128)(2,1)} %collective-permute-done.11.refs_2_), channel_id=1, source_target_pairs={{0,1},{1,0},{2,3},{3,2},{4,5},{5,4},{6,7},{7,6},{8,9},{9,8},{10,11... | collective-permute-start | bytes 1572872 | tf_op jit(solution)/shard_map/ppermute | solution.py:195
  28.5 16.7 %copy-start.10 = (bf16[128,2048]{1,0:T(8,128)(2,1)}, bf16[128,2048]{1,0:T(8,128)(2,1)S(1)}, u32[]{:S(2)}) copy-start(bf16[128,2048]{1,0:T(8,128)(2,1)S(1)} %collective-permute-done.29.refs_5_) | copy-start | bytes 1572868
  28.5 13.4 %collective-permute-start.27 = (bf16[128,2048]{1,0:T(8,128)(2,1)S(1)}, bf16[128,2048]{1,0:T(8,128)(2,1)S(1)}, u32[]{:S(2)}, u32[]{:S(2)}) collective-permute-start(bf16[128,2048]{1,0:T(8,128)(2,1)S(1)} %collective-permute-done.16.refs_13_.refs_4_), channel_id=1, source_target_pairs={{0,1},{1,0},{2,3},{3,2},{4,5},{5,4},{6,7},{7,6},{8,9},{9,8},{10,11... | collective-permute-start | bytes 1572872 | tf_op jit(solution)/shard_map/ppermute | solution.py:195
  29.0 18.3 %copy-start.11 = (bf16[128,2048]{1,0:T(8,128)(2,1)}, bf16[128,2048]{1,0:T(8,128)(2,1)S(1)}, u32[]{:S(2)}) copy-start(bf16[128,2048]{1,0:T(8,128)(2,1)S(1)} %collective-permute-done.28.refs_3_) | copy-start | bytes 1572868
  29.0 16.2 %collective-permute-start.17 = (bf16[128,2048]{1,0:T(8,128)(2,1)S(1)}, bf16[128,2048]{1,0:T(8,128)(2,1)S(1)}, u32[]{:S(2)}, u32[]{:S(2)}) collective-permute-start(bf16[128,2048]{1,0:T(8,128)(2,1)S(1)} %collective-permute-done.16.refs_13_.refs_4_), channel_id=1, source_target_pairs={{0,4},{1,3},{4,8},{5,1},{8,12},{9,5},{12,14},{13,9},{14,10},{15,13... | collective-permute-start | bytes 1572872 | tf_op jit(solution)/shard_map/ppermute | solution.py:192
  34.0 42.9 %copy-start.1 = (bf16[128,2048]{1,0:T(8,128)(2,1)}, bf16[128,2048]{1,0:T(8,128)(2,1)S(1)}, u32[]{:S(2)}) copy-start(bf16[128,2048]{1,0:T(8,128)(2,1)S(1)} %collective-permute-done.7.refs_13_.refs_4_) | copy-start | bytes 1572868
  34.0 23.9 %collective-permute-start.25 = (bf16[128,2048]{1,0:T(8,128)(2,1)S(1)}, bf16[128,2048]{1,0:T(8,128)(2,1)}, u32[]{:S(2)}, u32[]{:S(2)}) collective-permute-start(bf16[128,2048]{1,0:T(8,128)(2,1)S(1)} %collective-permute-done.7.refs_13_.refs_4_), channel_id=1, source_target_pairs={{0,1},{1,0},{2,3},{3,2},{4,5},{5,4},{6,7},{7,6},{8,9},{9,8},{10,11... | collective-permute-start | bytes 1572872 | tf_op jit(solution)/shard_map/ppermute | solution.py:195
  39.7 18.7 %collective-permute-start.12 = (bf16[128,2048]{1,0:T(8,128)(2,1)}, bf16[128,2048]{1,0:T(8,128)(2,1)}, u32[]{:S(2)}, u32[]{:S(2)}) collective-permute-start(bf16[128,2048]{1,0:T(8,128)(2,1)} %collective-permute-done.11.refs_2_), channel_id=1, source_target_pairs={{0,4},{1,3},{4,8},{5,1},{8,12},{9,5},{12,14},{13,9},{14,10},{15,13... | collective-permute-start | bytes 1572872 | tf_op jit(solution)/shard_map/ppermute | solution.py:192
  41.8 5.5 %copy-start.12 = (bf16[128,2048]{1,0:T(8,128)(2,1)}, bf16[128,2048]{1,0:T(8,128)(2,1)S(1)}, u32[]{:S(2)}) copy-start(bf16[128,2048]{1,0:T(8,128)(2,1)S(1)} %collective-permute-done.26.refs_3_) | copy-start | bytes 1572868
  41.8 23.9 %collective-permute-start.24 = (bf16[128,2048]{1,0:T(8,128)(2,1)}, bf16[128,2048]{1,0:T(8,128)(2,1)}, u32[]{:S(2)}, u32[]{:S(2)}) collective-permute-start(bf16[128,2048]{1,0:T(8,128)(2,1)} %collective-permute-done.2.refs_2_), channel_id=1, source_target_pairs={{0,1},{1,0},{2,3},{3,2},{4,5},{5,4},{6,7},{7,6},{8,9},{9,8},{10,11... | collective-permute-start | bytes 1572872 | tf_op jit(solution)/shard_map/ppermute | solution.py:195
  41.8 5.5 %copy-start.13 = (bf16[128,2048]{1,0:T(8,128)(2,1)}, bf16[128,2048]{1,0:T(8,128)(2,1)S(1)}, u32[]{:S(2)}) copy-start(bf16[128,2048]{1,0:T(8,128)(2,1)S(1)} %collective-permute-done.27.refs_5_) | copy-start | bytes 1572868
  41.9 25.0 %collective-permute-start.8 = (bf16[128,2048]{1,0:T(8,128)(2,1)S(1)}, bf16[128,2048]{1,0:T(8,128)(2,1)S(1)}, u32[]{:S(2)}, u32[]{:S(2)}) collective-permute-start(bf16[128,2048]{1,0:T(8,128)(2,1)S(1)} %collective-permute-done.7.refs_13_.refs_4_), channel_id=1, source_target_pairs={{0,4},{1,3},{4,8},{5,1},{8,12},{9,5},{12,14},{13,9},{14,10},{15,13... | collective-permute-start | bytes 1572872 | tf_op jit(solution)/shard_map/ppermute | solution.py:192
  45.2 31.7 %copy-start.2 = (bf16[128,2048]{1,0:T(8,128)(2,1)}, bf16[128,2048]{1,0:T(8,128)(2,1)S(1)}, u32[]{:S(2)}) copy-start(bf16[128,2048]{1,0:T(8,128)(2,1)S(1)} %collective-permute-done.17.refs_13_.refs_4_) | copy-start | bytes 1572868
  45.2 22.2 %collective-permute-start.3 = (bf16[128,2048]{1,0:T(8,128)(2,1)}, bf16[128,2048]{1,0:T(8,128)(2,1)}, u32[]{:S(2)}, u32[]{:S(2)}) collective-permute-start(bf16[128,2048]{1,0:T(8,128)(2,1)} %collective-permute-done.2.refs_2_), channel_id=1, source_target_pairs={{0,4},{1,3},{4,8},{5,1},{8,12},{9,5},{12,14},{13,9},{14,10},{15,13... | collective-permute-start | bytes 1572872 | tf_op jit(solution)/shard_map/ppermute | solution.py:192
  53.0 12.7 %all-to-all-start = ((bf16[16,2,128]{2,1,0:T(2,128)(2,1)}), bf16[16,2,128]{2,1,0:T(2,128)(2,1)S(1)}, u32[]{:S(2)}, u32[]{:S(2)}) async-start(bf16[16,2,128]{2,1,0:T(2,128)(2,1)} %reshape.17), calls=%async_computation | async-start | bytes 16384 | tf_op jit(solution)/shard_map/all_to_all | solution.py:232
  57.9 19.0 %collective-permute-start.23 = (bf16[128,2048]{1,0:T(8,128)(2,1)S(1)}, bf16[128,2048]{1,0:T(8,128)(2,1)S(1)}, u32[]{:S(2)}, u32[]{:S(2)}) collective-permute-start(bf16[128,2048]{1,0:T(8,128)(2,1)S(1)} %collective-permute-done.17.refs_13_.refs_4_), channel_id=1, source_target_pairs={{0,1},{1,0},{2,3},{3,2},{4,5},{5,4},{6,7},{7,6},{8,9},{9,8},{10,11... | collective-permute-start | bytes 1572872 | tf_op jit(solution)/shard_map/ppermute | solution.py:195
  58.4 19.4 %collective-permute-start.22 = (bf16[128,2048]{1,0:T(8,128)(2,1)}, bf16[128,2048]{1,0:T(8,128)(2,1)}, u32[]{:S(2)}, u32[]{:S(2)}) collective-permute-start(bf16[128,2048]{1,0:T(8,128)(2,1)} %collective-permute-done.12.refs_2_), channel_id=1, source_target_pairs={{0,1},{1,0},{2,3},{3,2},{4,5},{5,4},{6,7},{7,6},{8,9},{9,8},{10,11... | collective-permute-start | bytes 1572872 | tf_op jit(solution)/shard_map/ppermute | solution.py:195
  65.7 23.0 %collective-permute-start.18 = (bf16[128,2048]{1,0:T(8,128)(2,1)S(1)}, bf16[128,2048]{1,0:T(8,128)(2,1)S(1)}, u32[]{:S(2)}, u32[]{:S(2)}) collective-permute-start(bf16[128,2048]{1,0:T(8,128)(2,1)S(1)} %collective-permute-done.17.refs_13_.refs_4_), channel_id=1, source_target_pairs={{0,4},{1,3},{4,8},{5,1},{8,12},{9,5},{12,14},{13,9},{14,10},{15,13... | collective-permute-start | bytes 1572872 | tf_op jit(solution)/shard_map/ppermute | solution.py:192
  66.8 10.1 %copy-start.4 = (bf16[128,2048]{1,0:T(8,128)(2,1)}, bf16[128,2048]{1,0:T(8,128)(2,1)S(1)}, u32[]{:S(2)}) copy-start(bf16[128,2048]{1,0:T(8,128)(2,1)S(1)} %collective-permute-done.8.refs_13_.refs_4_) | copy-start | bytes 1572868
  66.8 32.2 %collective-permute-start.13 = (bf16[128,2048]{1,0:T(8,128)(2,1)}, bf16[128,2048]{1,0:T(8,128)(2,1)}, u32[]{:S(2)}, u32[]{:S(2)}) collective-permute-start(bf16[128,2048]{1,0:T(8,128)(2,1)} %collective-permute-done.12.refs_2_), channel_id=1, source_target_pairs={{0,4},{1,3},{4,8},{5,1},{8,12},{9,5},{12,14},{13,9},{14,10},{15,13... | collective-permute-start | bytes 1572872 | tf_op jit(solution)/shard_map/ppermute | solution.py:192
  67.4 31.4 %collective-permute-start.21 = (bf16[128,2048]{1,0:T(8,128)(2,1)S(1)}, bf16[128,2048]{1,0:T(8,128)(2,1)}, u32[]{:S(2)}, u32[]{:S(2)}) collective-permute-start(bf16[128,2048]{1,0:T(8,128)(2,1)S(1)} %collective-permute-done.8.refs_13_.refs_4_), channel_id=1, source_target_pairs={{0,1},{1,0},{2,3},{3,2},{4,5},{5,4},{6,7},{7,6},{8,9},{9,8},{10,11... | collective-permute-start | bytes 1572872 | tf_op jit(solution)/shard_map/ppermute | solution.py:195
  76.9 11.7 %copy-start.14 = (bf16[128,2048]{1,0:T(8,128)(2,1)}, bf16[128,2048]{1,0:T(8,128)(2,1)S(1)}, u32[]{:S(2)}) copy-start(bf16[128,2048]{1,0:T(8,128)(2,1)S(1)} %collective-permute-done.23.refs_5_) | copy-start | bytes 1572868
  76.9 32.0 %collective-permute-start.9 = (bf16[128,2048]{1,0:T(8,128)(2,1)S(1)}, bf16[128,2048]{1,0:T(8,128)(2,1)S(1)}, u32[]{:S(2)}, u32[]{:S(2)}) collective-permute-start(bf16[128,2048]{1,0:T(8,128)(2,1)S(1)} %collective-permute-done.8.refs_13_.refs_4_), channel_id=1, source_target_pairs={{0,4},{1,3},{4,8},{5,1},{8,12},{9,5},{12,14},{13,9},{14,10},{15,13... | collective-permute-start | bytes 1572872 | tf_op jit(solution)/shard_map/ppermute | solution.py:192
  77.8 31.3 %collective-permute-start.4 = (bf16[128,2048]{1,0:T(8,128)(2,1)}, bf16[128,2048]{1,0:T(8,128)(2,1)S(1)}, u32[]{:S(2)}, u32[]{:S(2)}) collective-permute-start(bf16[128,2048]{1,0:T(8,128)(2,1)} %collective-permute-done.3.refs_2_), channel_id=1, source_target_pairs={{0,4},{1,3},{4,8},{5,1},{8,12},{9,5},{12,14},{13,9},{14,10},{15,13... | collective-permute-start | bytes 1572872 | tf_op jit(solution)/shard_map/ppermute | solution.py:192
  88.7 10.2 %copy-start.5 = (bf16[128,2048]{1,0:T(8,128)(2,1)}, bf16[128,2048]{1,0:T(8,128)(2,1)S(1)}, u32[]{:S(2)}) copy-start(bf16[128,2048]{1,0:T(8,128)(2,1)S(1)} %collective-permute-done.18.refs_13_.refs_4_) | copy-start | bytes 1572868
  88.7 30.3 %collective-permute-start.20 = (bf16[128,2048]{1,0:T(8,128)(2,1)}, bf16[128,2048]{1,0:T(8,128)(2,1)S(1)}, u32[]{:S(2)}, u32[]{:S(2)}) collective-permute-start(bf16[128,2048]{1,0:T(8,128)(2,1)} %collective-permute-done.3.refs_2_), channel_id=1, source_target_pairs={{0,1},{1,0},{2,3},{3,2},{4,5},{5,4},{6,7},{7,6},{8,9},{9,8},{10,11... | collective-permute-start | bytes 1572872 | tf_op jit(solution)/shard_map/ppermute | solution.py:195
  98.9 30.3 %collective-permute-start.19 = (bf16[128,2048]{1,0:T(8,128)(2,1)S(1)}, bf16[128,2048]{1,0:T(8,128)(2,1)S(1)}, u32[]{:S(2)}, u32[]{:S(2)}) collective-permute-start(bf16[128,2048]{1,0:T(8,128)(2,1)S(1)} %collective-permute-done.18.refs_13_.refs_4_), channel_id=1, source_target_pairs={{0,1},{1,0},{2,3},{3,2},{4,5},{5,4},{6,7},{7,6},{8,9},{9,8},{10,11... | collective-permute-start | bytes 1572872 | tf_op jit(solution)/shard_map/ppermute | solution.py:195
  99.1 30.1 %collective-permute-start.14 = (bf16[128,2048]{1,0:T(8,128)(2,1)}, bf16[128,2048]{1,0:T(8,128)(2,1)S(1)}, u32[]{:S(2)}, u32[]{:S(2)}) collective-permute-start(bf16[128,2048]{1,0:T(8,128)(2,1)} %collective-permute-done.13.refs_2_), channel_id=1, source_target_pairs={{0,1},{1,0},{2,3},{3,2},{4,5},{5,4},{6,7},{7,6},{8,9},{9,8},{10,11... | collective-permute-start | bytes 1572872 | tf_op jit(solution)/shard_map/ppermute | solution.py:195
  108.9 10.0 %copy-start.15 = (bf16[128,2048]{1,0:T(8,128)(2,1)}, bf16[128,2048]{1,0:T(8,128)(2,1)S(1)}, u32[]{:S(2)}) copy-start(bf16[128,2048]{1,0:T(8,128)(2,1)S(1)} %collective-permute-done.9.refs_4_) | copy-start | bytes 1572868
  108.9 30.7 %collective-permute-start.10 = (bf16[128,2048]{1,0:T(8,128)(2,1)S(1)}, bf16[128,2048]{1,0:T(8,128)(2,1)S(1)}, u32[]{:S(2)}, u32[]{:S(2)}) collective-permute-start(bf16[128,2048]{1,0:T(8,128)(2,1)S(1)} %collective-permute-done.9.refs_4_), channel_id=1, source_target_pairs={{0,1},{1,0},{2,3},{3,2},{4,5},{5,4},{6,7},{7,6},{8,9},{9,8},{10,11... | collective-permute-start | bytes 1572872 | tf_op jit(solution)/shard_map/ppermute | solution.py:195
  109.1 9.8 %copy-start.6 = (bf16[128,2048]{1,0:T(8,128)(2,1)}, bf16[128,2048]{1,0:T(8,128)(2,1)S(1)}, u32[]{:S(2)}) copy-start(bf16[128,2048]{1,0:T(8,128)(2,1)S(1)} %collective-permute-done.4.refs_13_.refs_2_) | copy-start | bytes 1572868
  109.1 30.5 %collective-permute-start.5 = (bf16[128,2048]{1,0:T(8,128)(2,1)S(1)}, bf16[128,2048]{1,0:T(8,128)(2,1)}, u32[]{:S(2)}, u32[]{:S(2)}) collective-permute-start(bf16[128,2048]{1,0:T(8,128)(2,1)S(1)} %collective-permute-done.4.refs_13_.refs_2_), channel_id=1, source_target_pairs={{0,1},{1,0},{2,3},{3,2},{4,5},{5,4},{6,7},{7,6},{8,9},{9,8},{10,11... | collective-permute-start | bytes 1572872 | tf_op jit(solution)/shard_map/ppermute | solution.py:195
  140.4 19.9 %copy-start.20 = (s32[128,8]{0,1:T(8,128)S(1)}, s32[128,8]{0,1:T(8,128)}, u32[]{:S(2)}) copy-start(s32[128,8]{0,1:T(8,128)} %param.13) | copy-start | bytes 12292
  (4 other events, 3.3 us)

commit v5 on v3

--- a/solution.py
+++ b/solution.py
@@ -1,7 +1,11 @@
+import functools
+
 import jax
 import jax.numpy as jnp
 import numpy as np
 from jax import lax
+from jax.experimental import pallas as pl
+from jax.experimental.pallas import tpu as pltpu
 from jax.sharding import PartitionSpec as P
 
 DOC_TOK = 512
@@ -36,6 +40,127 @@
     table = jnp.arange(experts, dtype=jnp.int32)
     hit = routes[:, :, None] == table
     return jnp.sum(jnp.where(hit, returned.T[:, None, :], 0.0), axis=-1)
+
+
+def rows_kernel(blocks, first, *refs):
+    order, facts = refs[:2]
+    block_in = refs[2 : 2 + blocks]
+    w_gate, w_up, w_down, low_proj, high_proj = refs[2 + blocks : 7 + blocks]
+    grads, feat, x_all, dy_all, low_sum, grad_sum = refs[-6:]
+    rows = block_in[0].shape[0] // 2
+    across = (((1,), (1,)), ((), ()))
+    for i in range(blocks):
+        x_all[i * rows : (i + 1) * rows, :] = block_in[i][:rows, :]
+        dy_all[i * rows : (i + 1) * rows, :] = block_in[i][rows:, :]
+    low_sum[...] = jnp.zeros_like(low_sum)
+    grad_sum[...] = jnp.zeros_like(grad_sum)
+    units = w_gate.shape[2]
+    tile = 256 if units % 256 == 0 else units
+    lanes = grad_sum.shape[1]
+
+    @pl.loop(0, units // tile)
+    def _(j):
+        part = pl.ds(pl.multiple_of(j * tile, tile), tile)
+        gate_val = jnp.dot(x_all[...], w_gate[0, :, part], preferred_element_type=jnp.float32)
+        up_val = jnp.dot(x_all[...], w_up[0, :, part], preferred_element_type=jnp.float32)
+        hidden = (jax.nn.silu(gate_val) * up_val).astype(jnp.bfloat16)
+        back = lax.dot_general(
+            dy_all[...], w_down[0, part, :], across, preferred_element_type=jnp.float32
+        )
+        terms = hidden.astype(jnp.float32) * back
+        for cut in range(0, tile, lanes):
+            grad_sum[...] += terms[:, cut : cut + lanes]
+        low_sum[...] += lax.dot_general(
+            hidden, low_proj[:, part], across, preferred_element_type=jnp.float32
+        )
+
+    proj_cot = lax.dot_general(
+        dy_all[...], high_proj[...], across, preferred_element_type=jnp.float32
+    )
+    rank = proj_cot.shape[1]
+    width = low_sum.shape[1]
+    doc_of = lax.broadcasted_iota(jnp.int32, (rows, width), 1) // rank
+    if first:
+        grads[...] = jnp.zeros_like(grads)
+    else:
+        grads_in, feat_in = refs[7 + blocks : 9 + blocks]
+        grads[...] = grads_in[...]
+    spread, high_side = [], []
+    for i in range(blocks):
+        place = slice(i * rows, (i + 1) * rows)
+        owner = order[i]
+        weight = jnp.transpose(jnp.broadcast_to(facts[owner, 0:1, :], (rows, rows)))
+        doc = jnp.transpose(jnp.broadcast_to(facts[owner, 1:2, :], (rows, rows)))
+        doc = jnp.concatenate([doc] * (width // rows), axis=1).astype(jnp.int32)
+        high_side.append((weight[:, :rank] * proj_cot[place]).astype(jnp.bfloat16))
+        low_side = jnp.where(doc == doc_of, low_sum[place, :], 0.0)
+        spread.append(low_side.astype(jnp.bfloat16))
+        grads[owner, :, :] = jnp.broadcast_to(
+            jnp.sum(jnp.transpose(grad_sum[place, :]), axis=0, keepdims=True), (8, rows)
+        )
+    feature = lax.dot_general(
+        jnp.concatenate(spread, axis=0),
+        jnp.concatenate(high_side, axis=0),
+        (((0,), (0,)), ((), ())),
+        preferred_element_type=jnp.float32,
+    )
+    feat[...] = feature if first else feat_in[...] + feature
+
+
+def work(order, facts, block_in, weights, sums):
+    units = weights[0].shape[2]
+    low_width, rank = weights[3].shape[0], weights[4].shape[0]
+    blocks = len(block_in)
+    rows, width = block_in[0].shape[0] // 2, block_in[0].shape[1]
+    inside = pl.BlockSpec(memory_space=pltpu.VMEM)
+    call = pl.pallas_call(
+        functools.partial(rows_kernel, blocks, not sums),
+        out_shape=[
+            jax.ShapeDtypeStruct(facts.shape, jnp.float32),
+            jax.ShapeDtypeStruct((low_width, rank), jnp.float32),
+        ],
+        in_specs=[pl.BlockSpec(memory_space=pltpu.SMEM)]
+        + [inside] * (1 + blocks + len(weights) + len(sums)),
+        out_specs=[inside] * 2,
+        scratch_shapes=[
+            pltpu.VMEM((blocks * rows, width), jnp.bfloat16),
+            pltpu.VMEM((blocks * rows, width), jnp.bfloat16),
+            pltpu.VMEM((blocks * rows, low_width), jnp.float32),
+            pltpu.VMEM((blocks * rows, 128), jnp.float32),
+        ],
+        compiler_params=pltpu.CompilerParams(vmem_limit_bytes=16 * 1024 * 1024),
+        cost_estimate=pl.CostEstimate(
+            flops=6 * blocks * rows * width * units,
+            bytes_accessed=4 * blocks * rows * width,
+            transcendentals=blocks * rows * units,
+        ),
+    )
+    return call(order, facts, *block_in, *weights, *sums)
+
+
+def facts_kernel(routes, combine, doc_ids, out):
+    groups, lines, rows = out.shape
+    expert = lax.broadcasted_iota(jnp.int32, (groups, rows), 0)
+    weight = jnp.zeros((groups, rows), jnp.float32)
+    for k in range(routes.shape[0]):
+        share = combine[k : k + 1, :].astype(jnp.float32)
+        weight += jnp.where(routes[k : k + 1, :] == expert, share, 0.0)
+    line = lax.broadcasted_iota(jnp.int32, (lines, rows), 0)
+    doc = doc_ids[...].astype(jnp.float32)
+    for e in range(groups):
+        out[e] = jnp.where(line == 0, weight[e : e + 1, :], doc)
+
+
+def stack_kernel(top, bottom, out, sems):
+    rows = top.shape[0]
+    copies = [
+        pltpu.make_async_copy(top, out.at[:rows], sems.at[0]),
+        pltpu.make_async_copy(bottom, out.at[rows:], sems.at[1]),
+    ]
+    for copy in copies:
+        copy.start()
+    for copy in copies:
+        copy.wait()
 
 
 def by_ring(
@@ -70,60 +195,61 @@
             order = [owner(0, core), owner(0, 1 - core)]
             for step in range(1, half + 1):
                 near, far = -step * way, step * way
+                order += [owner(near, core), owner(far, 1 - core)]
                 if step < half:
-                    order += [owner(near, core), owner(near, 1 - core)]
-                    order += [owner(far, 1 - core), owner(far, core)]
-                else:
-                    order += [owner(near, core), owner(far, 1 - core)]
+                    order += [owner(near, 1 - core), owner(far, core)]
             orders[owner(0, core)] = order
     me = lax.axis_index("exp")
-    mine = lax.dynamic_index_in_dim(jnp.asarray(orders), me, axis=0, keepdims=False)
-    owned = mine[:, None] == jnp.arange(groups, dtype=jnp.int32)
-
-    table = jnp.arange(groups, dtype=jnp.int32)
-    weight = jnp.sum(
-        jnp.where(routes[None, :, :] == table[:, None, None], combine[None, :, :], 0), axis=-1
-    ).astype(jnp.bfloat16)
-    own_doc = jnp.broadcast_to(doc_ids.astype(jnp.bfloat16)[None, :], weight.shape)
-    meta = lax.all_to_all(
-        jnp.stack([weight, own_doc], axis=1), "exp", split_axis=0, concat_axis=0, tiled=True
-    )
-    meta = jnp.sum(
-        jnp.where(owned[:, :, None, None], meta[None].astype(jnp.float32), 0.0), axis=1
-    ).astype(jnp.bfloat16)
-
-    x, dy = tokens, cotangent
-    x_beside, dy_beside = swap(x), swap(dy)
-    sets = [(jnp.concatenate([x, x_beside]), jnp.concatenate([dy, dy_beside]))]
-    x = jnp.concatenate([hop(x), hop(x_beside)])
-    dy = jnp.concatenate([hop(dy), hop(dy_beside)])
-    for step in range(1, half):
-        sets += [(x, dy), (swap(x), swap(dy))]
-        if step < half - 1:
-            x, dy = hop(x), hop(dy)
-    x, dy = hop(x[:tok_rows]), hop(dy[:tok_rows])
-    sets.append((jnp.concatenate([x, swap(x)]), jnp.concatenate([dy, swap(dy)])))
-
-    grads, feature = [], 0.0
-    for begin, (x, dy) in enumerate(sets):
-        part = meta[2 * begin : 2 * begin + 2]
-        hidden = swiglu(x, w_gate[0], w_up[0])
-        grad, term = finish(
-            hidden,
-            dy,
-            part[:, 0].reshape(-1),
-            part[:, 1].reshape(-1),
-            w_down[0],
-            proj_hidden[0],
-            proj_output[0],
-            docs_count,
-        )
-        grads.append(grad.reshape(2, tok_rows))
-        feature = feature + term
-    grads = jnp.concatenate(grads, axis=0)
-    grads = jnp.sum(jnp.where(owned[:, :, None], grads[:, None, :], 0.0), axis=0)
+    order = lax.dynamic_index_in_dim(jnp.asarray(orders), me, axis=0, keepdims=False)
+
+    rows, width = tokens.shape
+    own = pl.pallas_call(
+        stack_kernel,
+        out_shape=jax.ShapeDtypeStruct((2 * rows, width), tokens.dtype),
+        in_specs=[pl.BlockSpec(memory_space=pl.ANY)] * 2,
+        out_specs=pl.BlockSpec(memory_space=pltpu.VMEM),
+        scratch_shapes=[pltpu.SemaphoreType.DMA((2,))],
+    )(tokens, cotangent)
+    beside = swap(own)
+
+    facts = pl.pallas_call(
+        facts_kernel,
+        out_shape=jax.ShapeDtypeStruct((groups, 8, rows), jnp.float32),
+        in_specs=[pl.BlockSpec(memory_space=pltpu.VMEM)] * 3,
+        out_specs=pl.BlockSpec(memory_space=pltpu.VMEM),
+    )(routes.T, combine.T, doc_ids[None, :])
+    facts = lax.all_to_all(facts, "exp", split_axis=0, concat_axis=0, tiled=True)
+
+    low_proj = jnp.concatenate([proj_hidden[0].T] * docs_count, axis=0)
+    weights = (w_gate, w_up, w_down, low_proj, proj_output[0].T)
+    sums, done = [], 0
+    jobs = [(own, beside)]
+
+    def behind(block):
+        nonlocal sums, done
+        job = jobs.pop(0)
+        sums = work(order[done : done + len(job)], facts, job, weights, sums)
+        done += len(job)
+        if block is None:
+            return None
+        sums, block = lax.optimization_barrier((sums, block))
+        return block
+
+    near, other = own, beside
+    for step in range(1, half + 1):
+        near = hop(near)
+        if step > 1:
+            near = behind(near)
+        jobs.append((near, swap(near)))
+        if step < half:
+            other = behind(hop(other))
+            jobs.append((other, swap(other)))
+    while jobs:
+        behind(None)
+    grads, feature = sums
     returned = lax.all_to_all(grads, "exp", split_axis=0, concat_axis=0, tiled=True)
-    return feature[:, None], pick_own(returned, routes)
+    rank = proj_output.shape[2]
+    return feature.reshape(docs_count, 1, rank, rank), pick_own(returned[:, 0, :], routes)
 
 
 def by_routing(

time: 155 us -> 129 us (0.83)
  matrix products: 80.3 us -> 0 us
  Pallas kernels: 0 us -> 43.1 us
  waiting for transfers between devices: 21.7 us -> 48.4 us
  local copies, waits for them, and re-layouts: 25.3 us -> 8.64 us
  blocking collectives: 0 us -> 9.83 us
  starting transfers between devices: 21 us -> 15.8 us
  other arithmetic: 4.23 us -> 1.72 us
    dot_general x40 -> x0, matrix products: 80.3 us -> none  [the longest x8 22.2 us: finish(): out_val = jnp.dot(hidden, w_down, preferred_element_type=jnp.float32)]
    pallas_call x0 -> x10, Pallas kernels: none -> 43.1 us  [the longest x8 39.5 us: work(): return call(order, facts, *block_in, *weights, *sums)]
    ppermute x10 -> x7, waiting for transfers between devices: 17 us -> 31.8 us  [hop(): return lax.ppermute(block, 'exp', onward)]
    all_to_all x2 -> x1, waiting for transfers between devices: 4.61 us -> 16.6 us  [by_ring(): lax.all_to_all(facts, 'exp', split_axis=0, concat_axis=0, tiled=True)]
    all_to_all x0 -> x1, blocking collectives: none -> 9.83 us  [by_ring(): lax.all_to_all(grads, 'exp', split_axis=0, concat_axis=0, tiled=True)]
    concatenate x7 -> x0, local copies, waits for them, and re-layouts: 8.58 us -> none  [the longest x2 3.19 us: by_ring(): sets = [(jnp.concatenate([x, x_beside]), jnp.concatenate([dy, dy_beside]))]]
    all_to_all x2 -> x1, starting transfers between devices: 9.08 us -> 4.9 us  [by_ring(): lax.all_to_all(facts, 'exp', split_axis=0, concat_axis=0, tiled=True)]
    slice x2, local copies, waits for them, and re-layouts: 4.15 us -> 0.08 us  [the longest x1 0.08 us: behind(): sums = work(order[done:done + len(job)], facts, job, weights, sums)]
  transfers between devices with their start and end apart: 22 -> 16, of which waited for: 4 -> 6; matrix products, arithmetic and copies ran while one was open for 68% -> 1% of each run, Pallas kernels for 0% -> 28%
where the time goes in v5:
time: 129 us; the launch traced here: 128 us
  waiting for transfers between devices  48.4 us (38%)
  Pallas kernels  43.1 us (33%)
  starting transfers between devices  15.8 us (12%)
  blocking collectives  9.83 us (8%)
  local copies, waits for them, and re-layouts  8.64 us (7%)
  other arithmetic  1.72 us (1%)
    pallas_call x8, Pallas kernels, work(): return call(order, facts, *block_in, *weights, *sums)  39.5 us
    ppermute x7, waiting for transfers between devices, hop(): return lax.ppermute(block, 'exp', onward)  31.8 us
    all_to_all x1, waiting for transfers between devices, by_ring(): lax.all_to_all(facts, 'exp', split_axis=0, concat_axis=0, tiled=True)  16.6 us
    ppermute x7, starting transfers between devices, hop(): return lax.ppermute(block, 'exp', onward)  9.95 us
    all_to_all x1, blocking collectives, by_ring(): lax.all_to_all(grads, 'exp', split_axis=0, concat_axis=0, tiled=True)  9.83 us
    unnamed x20, local copies, waits for them, and re-layouts  7.86 us
    all_to_all x1, starting transfers between devices, by_ring(): lax.all_to_all(facts, 'exp', split_axis=0, concat_axis=0, tiled=True)  4.9 us
  transfers between devices with their start and end apart: 16, of which 6 were waited for; matrix products, arithmetic and copies ran while one was open for 1% of the time, Pallas kernels for 28%

profile of v5, /device:TPU:0, one launch (start us, length us, event | category | flops | bytes accessed | tf_op | source)
XLA Modules:
  0.0 128.3 jit_solution(10239292803296757061)
XLA Ops:
  0.6 2.2 %shard_map.123.refs_2_ = bf16[256,2048]{1,0:T(8,128)(2,1)} custom-call(bf16[128,2048]{1,0:T(8,128)(2,1)} %top.1, bf16[128,2048]{1,0:T(8,128)(2,1)} %bottom.1), custom_call_target="tpu_custom_call" | custom-call | tf_op jit(solution)/shard_map/pallas_call | solution.py:206
  2.8 0.5 collective-permute-start.2
  3.3 2.6 %collective-permute-start = (bf16[256,2048]{1,0:T(8,128)(2,1)}, bf16[256,2048]{1,0:T(8,128)(2,1)}, u32[]{:S(2)}, u32[]{:S(2)}) collective-permute-start(bf16[256,2048]{1,0:T(8,128)(2,1)} %shard_map.123.refs_2_), channel_id=1, source_target_pairs={{0,4},{1,3},{4,8},{5,1},{8,12},{9,5},{12,14},{13,9},{14,10},{15,13... | collective-permute-start | bytes 3145736 | tf_op jit(solution)/shard_map/ppermute | solution.py:182
  6.0 0.0 collective-permute-done.2.refs_3_
  6.0 2.9 %collective-permute-start.3 = (bf16[256,2048]{1,0:T(8,128)(2,1)}, bf16[256,2048]{1,0:T(8,128)(2,1)S(1)}, u32[]{:S(2)}, u32[]{:S(2)}) collective-permute-start(bf16[256,2048]{1,0:T(8,128)(2,1)} %collective-permute-done.2.refs_3_), channel_id=1, source_target_pairs={{0,4},{1,3},{4,8},{5,1},{8,12},{9,5},{12,14},{13,9},{14,10},{15,13... | collective-permute-start | bytes 3145736 | tf_op jit(solution)/shard_map/ppermute | solution.py:182
  8.9 10.1 %collective-permute-done.refs_2_ = bf16[256,2048]{1,0:T(8,128)(2,1)} collective-permute-done((bf16[256,2048]{1,0:T(8,128)(2,1)}, bf16[256,2048]{1,0:T(8,128)(2,1)}, u32[]{:S(2)}, u32[]{:S(2)}) %collective-permute-start) | collective-permute-done | bytes 1048608 | tf_op jit(solution)/shard_map/ppermute | solution.py:182
  19.0 2.1 %collective-permute-start.4 = (bf16[256,2048]{1,0:T(8,128)(2,1)}, bf16[256,2048]{1,0:T(8,128)(2,1)S(1)}, u32[]{:S(2)}, u32[]{:S(2)}) collective-permute-start(bf16[256,2048]{1,0:T(8,128)(2,1)} %collective-permute-done.refs_2_), channel_id=1, source_target_pairs={{0,4},{1,3},{4,8},{5,1},{8,12},{9,5},{12,14},{13,9},{14,10},{15,13... | collective-permute-start | bytes 3145736 | tf_op jit(solution)/shard_map/ppermute | solution.py:182
  21.1 1.4 %shard_map.122 = f32[16,8,128]{2,1,0:T(8,128)} custom-call(s32[8,128]{1,0:T(8,128)} %bitcast.41, bf16[8,128]{1,0:T(8,128)(2,1)} %bitcast.42, s32[1,128]{1,0:T(1,128)} %bitcast.43), custom_call_target="tpu_custom_call" | custom-call | tf_op jit(solution)/shard_map/pallas_call | solution.py:215
  22.5 4.9 %all-to-all-start = ((f32[16,8,128]{2,1,0:T(8,128)}), f32[16,8,128]{2,1,0:T(8,128)S(1)}, u32[]{:S(2)}, u32[]{:S(2)}) async-start(f32[16,8,128]{2,1,0:T(8,128)} %shard_map.122), calls=%async_computation | async-start | bytes 131072 | tf_op jit(solution)/shard_map/all_to_all | solution.py:221
  27.4 0.7 constant_dynamic-slice_fusion
  28.1 0.1 slice_bitcast_fusion
  28.1 1.1 pad_maximum_fusion.refs_7_
  29.2 16.6 %all-to-all-done.refs_1_ = f32[16,8,128]{2,1,0:T(8,128)S(1)} async-done(((f32[16,8,128]{2,1,0:T(8,128)}), f32[16,8,128]{2,1,0:T(8,128)S(1)}, u32[]{:S(2)}, u32[]{:S(2)}) %all-to-all-start) | async-done | bytes 65568 | tf_op jit(solution)/shard_map/all_to_all | solution.py:221
  45.9 1.9 %copy-done = bf16[1,2048,768]{2,1,0:T(8,128)(2,1)S(1)} copy-done((bf16[1,2048,768]{2,1,0:T(8,128)(2,1)S(1)}, bf16[1,2048,768]{2,1,0:T(8,128)(2,1)}, u32[]{:S(2)}) %copy-start) | copy-done | bytes 3145752
  47.8 1.9 %copy-done.2 = bf16[1,2048,768]{2,1,0:T(8,128)(2,1)S(1)} copy-done((bf16[1,2048,768]{2,1,0:T(8,128)(2,1)S(1)}, bf16[1,2048,768]{2,1,0:T(8,128)(2,1)}, u32[]{:S(2)}) %copy-start.2) | copy-done | bytes 3145752
  49.7 1.9 %copy-done.4 = bf16[1,768,2048]{2,1,0:T(8,128)(2,1)S(1)} copy-done((bf16[1,768,2048]{2,1,0:T(8,128)(2,1)S(1)}, bf16[1,768,2048]{2,1,0:T(8,128)(2,1)}, u32[]{:S(2)}) %copy-start.4) | copy-done | bytes 3145752
  51.6 0.9 copy-done.6
  52.5 1.2 copy-done.8
  53.7 5.5 %shard_map.124 = (f32[16,8,128]{2,1,0:T(8,128)S(1)}, f32[256,64]{1,0:T(8,128)S(1)}) custom-call(s32[2]{0:T(128)S(1)} %get-tuple-element.77.refs_0_, f32[16,8,128]{2,1,0:T(8,128)S(1)} %all-to-all-done.refs_1_, bf16[256,2048]{1,0:T(8,128)(2,1)S(1)} %copy-done.8, bf16[256,2048]{1,0:T(8,128)(2,1)} %collective-permute-done.2.refs_3_, ...), custom_call_target="tpu_custom_call" | custom-call | flops 2415919104 | bytes 2097152 | tf_op jit(solution)/shard_map/pallas_call | solution.py:138
  59.2 0.0 collective-permute-done.3.refs_2_
  59.2 0.1 collective-permute-start.6
  59.3 0.2 collective-permute-start.7
  59.5 0.0 collective-permute-done.1.refs_3_
  59.6 5.6 %shard_map.125 = (f32[16,8,128]{2,1,0:T(8,128)S(1)}, f32[256,64]{1,0:T(8,128)S(1)}) custom-call(s32[2]{0:T(128)S(1)} %get-tuple-element.78.refs_0_, f32[16,8,128]{2,1,0:T(8,128)S(1)} %all-to-all-done.refs_1_, bf16[256,2048]{1,0:T(8,128)(2,1)} %collective-permute-done.refs_2_, bf16[256,2048]{1,0:T(8,128)(2,1)} %collective-permute-done.1.refs_3_, ...), custom_call_target="tpu_custom_call" | custom-call | flops 2415919104 | bytes 2097152 | tf_op jit(solution)/shard_map/pallas_call | solution.py:138
  65.2 0.0 collective-permute-done.4.refs_2_
  65.2 0.4 collective-permute-start.5
  65.6 1.7 %collective-permute-start.8 = (bf16[256,2048]{1,0:T(8,128)(2,1)S(1)}, bf16[256,2048]{1,0:T(8,128)(2,1)S(1)}, u32[]{:S(2)}, u32[]{:S(2)}) collective-permute-start(bf16[256,2048]{1,0:T(8,128)(2,1)S(1)} %collective-permute-done.4.refs_2_), channel_id=1, source_target_pairs={{0,4},{1,3},{4,8},{5,1},{8,12},{9,5},{12,14},{13,9},{14,10},{15,13... | collective-permute-start | bytes 3145736 | tf_op jit(solution)/shard_map/ppermute | solution.py:182
  67.3 4.6 %shard_map.126 = (f32[16,8,128]{2,1,0:T(8,128)S(1)}, f32[256,64]{1,0:T(8,128)S(1)}) custom-call(s32[2]{0:T(128)S(1)} %get-tuple-element.76.refs_0_, f32[16,8,128]{2,1,0:T(8,128)S(1)} %all-to-all-done.refs_1_, bf16[256,2048]{1,0:T(8,128)(2,1)S(1)} %collective-permute-done.3.refs_2_, bf16[256,2048]{1,0:T(8,128)(2,1)S(1)} %collective-permute-done.6.refs_3_, ...), custom_call_target="tpu_custom_call" | custom-call | flops 2415919104 | bytes 2097152 | tf_op jit(solution)/shard_map/pallas_call | solution.py:138
  72.0 2.2 %collective-permute-done.7.refs_2_ = bf16[256,2048]{1,0:T(8,128)(2,1)S(1)} collective-permute-done((bf16[256,2048]{1,0:T(8,128)(2,1)S(1)}, bf16[256,2048]{1,0:T(8,128)(2,1)S(1)}, u32[]{:S(2)}, u32[]{:S(2)}) %collective-permute-start.7) | collective-permute-done | bytes 1048608 | tf_op jit(solution)/shard_map/ppermute | solution.py:182
  74.2 0.2 collective-permute-start.11
  74.3 0.0 collective-permute-done.5.refs_3_
  74.3 4.6 %shard_map.127 = (f32[16,8,128]{2,1,0:T(8,128)S(1)}, f32[256,64]{1,0:T(8,128)S(1)}) custom-call(s32[2]{0:T(128)S(1)} %get-tuple-element.79.refs_0_, f32[16,8,128]{2,1,0:T(8,128)S(1)} %all-to-all-done.refs_1_, bf16[256,2048]{1,0:T(8,128)(2,1)S(1)} %collective-permute-done.4.refs_2_, bf16[256,2048]{1,0:T(8,128)(2,1)S(1)} %collective-permute-done.5.refs_3_, ...), custom_call_target="tpu_custom_call" | custom-call | flops 2415919104 | bytes 2097152 | tf_op jit(solution)/shard_map/pallas_call | solution.py:138
  79.0 6.4 %collective-permute-done.8.refs_2_ = bf16[256,2048]{1,0:T(8,128)(2,1)S(1)} collective-permute-done((bf16[256,2048]{1,0:T(8,128)(2,1)S(1)}, bf16[256,2048]{1,0:T(8,128)(2,1)S(1)}, u32[]{:S(2)}, u32[]{:S(2)}) %collective-permute-start.8) | collective-permute-done | bytes 1048608 | tf_op jit(solution)/shard_map/ppermute | solution.py:182
  85.4 0.0 collective-permute-start.9
  85.4 0.2 collective-permute-start.12
  85.6 0.0 collective-permute-done.10.refs_3_
  85.6 4.6 %shard_map.128 = (f32[16,8,128]{2,1,0:T(8,128)S(1)}, f32[256,64]{1,0:T(8,128)S(1)}) custom-call(s32[2]{0:T(128)S(1)} %get-tuple-element.75.refs_0_, f32[16,8,128]{2,1,0:T(8,128)S(1)} %all-to-all-done.refs_1_, bf16[256,2048]{1,0:T(8,128)(2,1)S(1)} %collective-permute-done.7.refs_2_, bf16[256,2048]{1,0:T(8,128)(2,1)S(1)} %collective-permute-done.10.refs_3_, ...), custom_call_target="tpu_custom_call" | custom-call | flops 2415919104 | bytes 2097152 | tf_op jit(solution)/shard_map/pallas_call | solution.py:138
  90.2 6.4 %collective-permute-done.11.refs_2_ = bf16[256,2048]{1,0:T(8,128)(2,1)S(1)} collective-permute-done((bf16[256,2048]{1,0:T(8,128)(2,1)S(1)}, bf16[256,2048]{1,0:T(8,128)(2,1)S(1)}, u32[]{:S(2)}, u32[]{:S(2)}) %collective-permute-start.11) | collective-permute-done | bytes 1048608 | tf_op jit(solution)/shard_map/ppermute | solution.py:182
  96.6 0.0 collective-permute-start.14
  96.6 0.0 collective-permute-done.9.refs_3_
  96.7 4.6 %shard_map.129 = (f32[16,8,128]{2,1,0:T(8,128)S(1)}, f32[256,64]{1,0:T(8,128)S(1)}) custom-call(s32[2]{0:T(128)S(1)} %get-tuple-element.80.refs_0_, f32[16,8,128]{2,1,0:T(8,128)S(1)} %all-to-all-done.refs_1_, bf16[256,2048]{1,0:T(8,128)(2,1)S(1)} %collective-permute-done.8.refs_2_, bf16[256,2048]{1,0:T(8,128)(2,1)S(1)} %collective-permute-done.9.refs_3_, ...), custom_call_target="tpu_custom_call" | custom-call | flops 2415919104 | bytes 2097152 | tf_op jit(solution)/shard_map/pallas_call | solution.py:138
  101.3 6.6 %collective-permute-done.12.refs_2_ = bf16[256,2048]{1,0:T(8,128)(2,1)S(1)} collective-permute-done((bf16[256,2048]{1,0:T(8,128)(2,1)S(1)}, bf16[256,2048]{1,0:T(8,128)(2,1)S(1)}, u32[]{:S(2)}, u32[]{:S(2)}) %collective-permute-start.12) | collective-permute-done | bytes 1048608 | tf_op jit(solution)/shard_map/ppermute | solution.py:182
  107.9 0.0 collective-permute-start.13
  107.9 4.6 %shard_map.130 = (f32[16,8,128]{2,1,0:T(8,128)S(1)}, f32[256,64]{1,0:T(8,128)S(1)}) custom-call(s32[2]{0:T(128)S(1)} %get-tuple-element.74.refs_0_, f32[16,8,128]{2,1,0:T(8,128)S(1)} %all-to-all-done.refs_1_, bf16[256,2048]{1,0:T(8,128)(2,1)S(1)} %collective-permute-done.11.refs_2_, bf16[256,2048]{1,0:T(8,128)(2,1)S(1)} %collective-permute-done.14.refs_3_, ...), custom_call_target="tpu_custom_call" | custom-call | flops 2415919104 | bytes 2097152 | tf_op jit(solution)/shard_map/pallas_call | solution.py:138
  112.5 0.0 copy-start.9
  112.5 5.3 %shard_map.131 = (f32[16,8,128]{2,1,0:T(8,128)S(1)}, f32[256,64]{1,0:T(8,128)}) custom-call(s32[2]{0:T(128)S(1)} %get-tuple-element.81.refs_0_, f32[16,8,128]{2,1,0:T(8,128)S(1)} %all-to-all-done.refs_1_, bf16[256,2048]{1,0:T(8,128)(2,1)S(1)} %collective-permute-done.12.refs_2_, bf16[256,2048]{1,0:T(8,128)(2,1)S(1)} %collective-permute-done.13.refs_3_, ...), custom_call_target="tpu_custom_call" | custom-call | flops 2415919104 | bytes 2097152 | tf_op jit(solution)/shard_map/pallas_call | solution.py:138
  117.8 9.8 %all_to_all.10 = f32[16,8,128]{2,1,0:T(8,128)S(1)} all-to-all(f32[16,8,128]{2,1,0:T(8,128)S(1)} %get-tuple-element.69), channel_id=1, replica_groups=mesh['grp'=2,'exp'=16] {'exp'}, dimensions={0} | all-to-all | bytes 131072 | tf_op jit(solution)/shard_map/all_to_all | solution.py:250
  127.7 0.6 select_reduce_fusion
  (20 shorter events, 0.0 us)
Async XLA Ops:
  2.8 3.2 %collective-permute-start.2 = (bf16[256,2048]{1,0:T(8,128)(2,1)}, bf16[256,2048]{1,0:T(8,128)(2,1)}, u32[]{:S(2)}, u32[]{:S(2)}) collective-permute-start(bf16[256,2048]{1,0:T(8,128)(2,1)} %shard_map.123.refs_2_), channel_id=1, source_target_pairs={{0,1},{1,0},{2,3},{3,2},{4,5},{5,4},{6,7},{7,6},{8,9},{9,8},{10,11... | collective-permute-start | bytes 3145736 | tf_op jit(solution)/shard_map/ppermute | solution.py:185
  3.3 15.6 %collective-permute-start = (bf16[256,2048]{1,0:T(8,128)(2,1)}, bf16[256,2048]{1,0:T(8,128)(2,1)}, u32[]{:S(2)}, u32[]{:S(2)}) collective-permute-start(bf16[256,2048]{1,0:T(8,128)(2,1)} %shard_map.123.refs_2_), channel_id=1, source_target_pairs={{0,4},{1,3},{4,8},{5,1},{8,12},{9,5},{12,14},{13,9},{14,10},{15,13... | collective-permute-start | bytes 3145736 | tf_op jit(solution)/shard_map/ppermute | solution.py:182
  6.0 53.3 %collective-permute-start.3 = (bf16[256,2048]{1,0:T(8,128)(2,1)}, bf16[256,2048]{1,0:T(8,128)(2,1)S(1)}, u32[]{:S(2)}, u32[]{:S(2)}) collective-permute-start(bf16[256,2048]{1,0:T(8,128)(2,1)} %collective-permute-done.2.refs_3_), channel_id=1, source_target_pairs={{0,4},{1,3},{4,8},{5,1},{8,12},{9,5},{12,14},{13,9},{14,10},{15,13... | collective-permute-start | bytes 3145736 | tf_op jit(solution)/shard_map/ppermute | solution.py:182
  19.0 40.5 %collective-permute-start.1 = (bf16[256,2048]{1,0:T(8,128)(2,1)}, bf16[256,2048]{1,0:T(8,128)(2,1)}, u32[]{:S(2)}, u32[]{:S(2)}) collective-permute-start(bf16[256,2048]{1,0:T(8,128)(2,1)} %collective-permute-done.refs_2_), channel_id=1, source_target_pairs={{0,1},{1,0},{2,3},{3,2},{4,5},{5,4},{6,7},{7,6},{8,9},{9,8},{10,11... | collective-permute-start | bytes 3145736 | tf_op jit(solution)/shard_map/ppermute | solution.py:185
  19.0 46.2 %collective-permute-start.4 = (bf16[256,2048]{1,0:T(8,128)(2,1)}, bf16[256,2048]{1,0:T(8,128)(2,1)S(1)}, u32[]{:S(2)}, u32[]{:S(2)}) collective-permute-start(bf16[256,2048]{1,0:T(8,128)(2,1)} %collective-permute-done.refs_2_), channel_id=1, source_target_pairs={{0,4},{1,3},{4,8},{5,1},{8,12},{9,5},{12,14},{13,9},{14,10},{15,13... | collective-permute-start | bytes 3145736 | tf_op jit(solution)/shard_map/ppermute | solution.py:182
  22.5 23.4 %all-to-all-start = ((f32[16,8,128]{2,1,0:T(8,128)}), f32[16,8,128]{2,1,0:T(8,128)S(1)}, u32[]{:S(2)}, u32[]{:S(2)}) async-start(f32[16,8,128]{2,1,0:T(8,128)} %shard_map.122), calls=%async_computation | async-start | bytes 131072 | tf_op jit(solution)/shard_map/all_to_all | solution.py:221
  45.9 1.9 %copy-start = (bf16[1,2048,768]{2,1,0:T(8,128)(2,1)S(1)}, bf16[1,2048,768]{2,1,0:T(8,128)(2,1)}, u32[]{:S(2)}) copy-start(bf16[1,2048,768]{2,1,0:T(8,128)(2,1)} %refs_4_.15) | copy-start | bytes 9437188
  47.8 1.9 %copy-start.2 = (bf16[1,2048,768]{2,1,0:T(8,128)(2,1)S(1)}, bf16[1,2048,768]{2,1,0:T(8,128)(2,1)}, u32[]{:S(2)}) copy-start(bf16[1,2048,768]{2,1,0:T(8,128)(2,1)} %refs_5_.15) | copy-start | bytes 9437188
  49.7 1.9 %copy-start.4 = (bf16[1,768,2048]{2,1,0:T(8,128)(2,1)S(1)}, bf16[1,768,2048]{2,1,0:T(8,128)(2,1)}, u32[]{:S(2)}) copy-start(bf16[1,768,2048]{2,1,0:T(8,128)(2,1)} %refs_6_.15) | copy-start | bytes 9437188
  51.6 0.9 copy-start.6
  52.5 1.2 copy-start.8
  53.7 5.8 %copy-start.1 = (bf16[1,2048,768]{2,1,0:T(8,128)(2,1)S(1)}, bf16[1,2048,768]{2,1,0:T(8,128)(2,1)}, u32[]{:S(2)}) copy-start(bf16[1,2048,768]{2,1,0:T(8,128)(2,1)} %refs_4_.15) | copy-start | bytes 9437188
  53.7 5.8 %copy-start.3 = (bf16[1,2048,768]{2,1,0:T(8,128)(2,1)S(1)}, bf16[1,2048,768]{2,1,0:T(8,128)(2,1)}, u32[]{:S(2)}) copy-start(bf16[1,2048,768]{2,1,0:T(8,128)(2,1)} %refs_5_.15) | copy-start | bytes 9437188
  53.7 5.8 %copy-start.5 = (bf16[1,768,2048]{2,1,0:T(8,128)(2,1)S(1)}, bf16[1,768,2048]{2,1,0:T(8,128)(2,1)}, u32[]{:S(2)}) copy-start(bf16[1,768,2048]{2,1,0:T(8,128)(2,1)} %refs_6_.15) | copy-start | bytes 9437188
  53.7 5.8 %copy-start.7 = (bf16[1,2048,64]{1,2,0:T(8,128)(2,1)S(1)}, bf16[1,2048,64]{1,2,0:T(8,128)(2,1)}, u32[]{:S(2)}) copy-start(bf16[1,2048,64]{1,2,0:T(8,128)(2,1)} %param.20) | copy-start | bytes 786436
  59.2 8.1 %collective-permute-start.6 = (bf16[256,2048]{1,0:T(8,128)(2,1)S(1)}, bf16[256,2048]{1,0:T(8,128)(2,1)S(1)}, u32[]{:S(2)}, u32[]{:S(2)}) collective-permute-start(bf16[256,2048]{1,0:T(8,128)(2,1)S(1)} %collective-permute-done.3.refs_2_), channel_id=1, source_target_pairs={{0,1},{1,0},{2,3},{3,2},{4,5},{5,4},{6,7},{7,6},{8,9},{9,8},{10,11... | collective-permute-start | bytes 3145736 | tf_op jit(solution)/shard_map/ppermute | solution.py:185
  59.3 14.9 %collective-permute-start.7 = (bf16[256,2048]{1,0:T(8,128)(2,1)S(1)}, bf16[256,2048]{1,0:T(8,128)(2,1)S(1)}, u32[]{:S(2)}, u32[]{:S(2)}) collective-permute-start(bf16[256,2048]{1,0:T(8,128)(2,1)S(1)} %collective-permute-done.3.refs_2_), channel_id=1, source_target_pairs={{0,4},{1,3},{4,8},{5,1},{8,12},{9,5},{12,14},{13,9},{14,10},{15,13... | collective-permute-start | bytes 3145736 | tf_op jit(solution)/shard_map/ppermute | solution.py:182
  65.2 9.1 %collective-permute-start.5 = (bf16[256,2048]{1,0:T(8,128)(2,1)S(1)}, bf16[256,2048]{1,0:T(8,128)(2,1)S(1)}, u32[]{:S(2)}, u32[]{:S(2)}) collective-permute-start(bf16[256,2048]{1,0:T(8,128)(2,1)S(1)} %collective-permute-done.4.refs_2_), channel_id=1, source_target_pairs={{0,1},{1,0},{2,3},{3,2},{4,5},{5,4},{6,7},{7,6},{8,9},{9,8},{10,11... | collective-permute-start | bytes 3145736 | tf_op jit(solution)/shard_map/ppermute | solution.py:185
  65.6 19.8 %collective-permute-start.8 = (bf16[256,2048]{1,0:T(8,128)(2,1)S(1)}, bf16[256,2048]{1,0:T(8,128)(2,1)S(1)}, u32[]{:S(2)}, u32[]{:S(2)}) collective-permute-start(bf16[256,2048]{1,0:T(8,128)(2,1)S(1)} %collective-permute-done.4.refs_2_), channel_id=1, source_target_pairs={{0,4},{1,3},{4,8},{5,1},{8,12},{9,5},{12,14},{13,9},{14,10},{15,13... | collective-permute-start | bytes 3145736 | tf_op jit(solution)/shard_map/ppermute | solution.py:182
  74.2 11.4 %collective-permute-start.10 = (bf16[256,2048]{1,0:T(8,128)(2,1)S(1)}, bf16[256,2048]{1,0:T(8,128)(2,1)S(1)}, u32[]{:S(2)}, u32[]{:S(2)}) collective-permute-start(bf16[256,2048]{1,0:T(8,128)(2,1)S(1)} %collective-permute-done.7.refs_2_), channel_id=1, source_target_pairs={{0,1},{1,0},{2,3},{3,2},{4,5},{5,4},{6,7},{7,6},{8,9},{9,8},{10,11... | collective-permute-start | bytes 3145736 | tf_op jit(solution)/shard_map/ppermute | solution.py:185
  74.2 22.5 %collective-permute-start.11 = (bf16[256,2048]{1,0:T(8,128)(2,1)S(1)}, bf16[256,2048]{1,0:T(8,128)(2,1)S(1)}, u32[]{:S(2)}, u32[]{:S(2)}) collective-permute-start(bf16[256,2048]{1,0:T(8,128)(2,1)S(1)} %collective-permute-done.7.refs_2_), channel_id=1, source_target_pairs={{0,4},{1,3},{4,8},{5,1},{8,12},{9,5},{12,14},{13,9},{14,10},{15,13... | collective-permute-start | bytes 3145736 | tf_op jit(solution)/shard_map/ppermute | solution.py:182
  85.4 11.2 %collective-permute-start.9 = (bf16[256,2048]{1,0:T(8,128)(2,1)S(1)}, bf16[256,2048]{1,0:T(8,128)(2,1)S(1)}, u32[]{:S(2)}, u32[]{:S(2)}) collective-permute-start(bf16[256,2048]{1,0:T(8,128)(2,1)S(1)} %collective-permute-done.8.refs_2_), channel_id=1, source_target_pairs={{0,1},{1,0},{2,3},{3,2},{4,5},{5,4},{6,7},{7,6},{8,9},{9,8},{10,11... | collective-permute-start | bytes 3145736 | tf_op jit(solution)/shard_map/ppermute | solution.py:185
  85.4 22.5 %collective-permute-start.12 = (bf16[256,2048]{1,0:T(8,128)(2,1)S(1)}, bf16[256,2048]{1,0:T(8,128)(2,1)S(1)}, u32[]{:S(2)}, u32[]{:S(2)}) collective-permute-start(bf16[256,2048]{1,0:T(8,128)(2,1)S(1)} %collective-permute-done.8.refs_2_), channel_id=1, source_target_pairs={{0,4},{1,3},{4,8},{5,1},{8,12},{9,5},{12,14},{13,9},{14,10},{15,13... | collective-permute-start | bytes 3145736 | tf_op jit(solution)/shard_map/ppermute | solution.py:182
  96.6 11.2 %collective-permute-start.14 = (bf16[256,2048]{1,0:T(8,128)(2,1)S(1)}, bf16[256,2048]{1,0:T(8,128)(2,1)S(1)}, u32[]{:S(2)}, u32[]{:S(2)}) collective-permute-start(bf16[256,2048]{1,0:T(8,128)(2,1)S(1)} %collective-permute-done.11.refs_2_), channel_id=1, source_target_pairs={{0,1},{1,0},{2,3},{3,2},{4,5},{5,4},{6,7},{7,6},{8,9},{9,8},{10,11... | collective-permute-start | bytes 3145736 | tf_op jit(solution)/shard_map/ppermute | solution.py:185
  107.9 4.6 %collective-permute-start.13 = (bf16[256,2048]{1,0:T(8,128)(2,1)S(1)}, bf16[256,2048]{1,0:T(8,128)(2,1)S(1)}, u32[]{:S(2)}, u32[]{:S(2)}) collective-permute-start(bf16[256,2048]{1,0:T(8,128)(2,1)S(1)} %collective-permute-done.12.refs_2_), channel_id=1, source_target_pairs={{0,1},{1,0},{2,3},{3,2},{4,5},{5,4},{6,7},{7,6},{8,9},{9,8},{10,11... | collective-permute-start | bytes 3145736 | tf_op jit(solution)/shard_map/ppermute | solution.py:185
  112.5 15.1 %copy-start.9 = (s32[128,8]{0,1:T(8,128)S(1)}, s32[128,8]{0,1:T(8,128)}, u32[]{:S(2)}) copy-start(s32[128,8]{0,1:T(8,128)} %param.13) | copy-start | bytes 12292

commit v6 on v5

--- a/solution.py
+++ b/solution.py
@@ -35,18 +35,11 @@
     return grad, feature.reshape(docs_count, low_side.shape[1], high_side.shape[1])
 
 
-def pick_own(returned, routes):
-    experts = returned.shape[0]
-    table = jnp.arange(experts, dtype=jnp.int32)
-    hit = routes[:, :, None] == table
-    return jnp.sum(jnp.where(hit, returned.T[:, None, :], 0.0), axis=-1)
-
-
-def rows_kernel(blocks, first, *refs):
-    order, facts = refs[:2]
+def rows_kernel(blocks, *refs):
+    order, sheet_in = refs[:2]
     block_in = refs[2 : 2 + blocks]
     w_gate, w_up, w_down, low_proj, high_proj = refs[2 + blocks : 7 + blocks]
-    grads, feat, x_all, dy_all, low_sum, grad_sum = refs[-6:]
+    sheet, low_side, proj_cot, x_all, dy_all, low_sum, grad_sum = refs[-7:]
     rows = block_in[0].shape[0] // 2
     across = (((1,), (1,)), ((), ()))
     for i in range(blocks):
@@ -54,78 +47,58 @@
         dy_all[i * rows : (i + 1) * rows, :] = block_in[i][rows:, :]
     low_sum[...] = jnp.zeros_like(low_sum)
     grad_sum[...] = jnp.zeros_like(grad_sum)
-    units = w_gate.shape[2]
+    units = w_gate.shape[1]
     tile = 256 if units % 256 == 0 else units
     lanes = grad_sum.shape[1]
 
     @pl.loop(0, units // tile)
     def _(j):
         part = pl.ds(pl.multiple_of(j * tile, tile), tile)
-        gate_val = jnp.dot(x_all[...], w_gate[0, :, part], preferred_element_type=jnp.float32)
-        up_val = jnp.dot(x_all[...], w_up[0, :, part], preferred_element_type=jnp.float32)
+        gate_val = jnp.dot(x_all[...], w_gate[:, part], preferred_element_type=jnp.float32)
+        up_val = jnp.dot(x_all[...], w_up[:, part], preferred_element_type=jnp.float32)
         hidden = (jax.nn.silu(gate_val) * up_val).astype(jnp.bfloat16)
         back = lax.dot_general(
-            dy_all[...], w_down[0, part, :], across, preferred_element_type=jnp.float32
+            dy_all[...], w_down[part, :], across, preferred_element_type=jnp.float32
         )
         terms = hidden.astype(jnp.float32) * back
         for cut in range(0, tile, lanes):
             grad_sum[...] += terms[:, cut : cut + lanes]
         low_sum[...] += lax.dot_general(
-            hidden, low_proj[:, part], across, preferred_element_type=jnp.float32
-        )
-
-    proj_cot = lax.dot_general(
-        dy_all[...], high_proj[...], across, preferred_element_type=jnp.float32
-    )
-    rank = proj_cot.shape[1]
-    width = low_sum.shape[1]
-    doc_of = lax.broadcasted_iota(jnp.int32, (rows, width), 1) // rank
-    if first:
-        grads[...] = jnp.zeros_like(grads)
-    else:
-        grads_in, feat_in = refs[7 + blocks : 9 + blocks]
-        grads[...] = grads_in[...]
-    spread, high_side = [], []
+            low_proj[:, part], hidden, across, preferred_element_type=jnp.float32
+        )
+
+    low_side[...] = low_sum[...].astype(low_side.dtype)
+    proj_cot[...] = lax.dot_general(
+        high_proj[...], dy_all[...], across, preferred_element_type=jnp.float32
+    )
+    sheet[...] = sheet_in[...]
     for i in range(blocks):
-        place = slice(i * rows, (i + 1) * rows)
-        owner = order[i]
-        weight = jnp.transpose(jnp.broadcast_to(facts[owner, 0:1, :], (rows, rows)))
-        doc = jnp.transpose(jnp.broadcast_to(facts[owner, 1:2, :], (rows, rows)))
-        doc = jnp.concatenate([doc] * (width // rows), axis=1).astype(jnp.int32)
-        high_side.append((weight[:, :rank] * proj_cot[place]).astype(jnp.bfloat16))
-        low_side = jnp.where(doc == doc_of, low_sum[place, :], 0.0)
-        spread.append(low_side.astype(jnp.bfloat16))
-        grads[owner, :, :] = jnp.broadcast_to(
-            jnp.sum(jnp.transpose(grad_sum[place, :]), axis=0, keepdims=True), (8, rows)
-        )
-    feature = lax.dot_general(
-        jnp.concatenate(spread, axis=0),
-        jnp.concatenate(high_side, axis=0),
-        (((0,), (0,)), ((), ())),
-        preferred_element_type=jnp.float32,
-    )
-    feat[...] = feature if first else feat_in[...] + feature
-
-
-def work(order, facts, block_in, weights, sums):
-    units = weights[0].shape[2]
+        total = jnp.sum(
+            jnp.transpose(grad_sum[i * rows : (i + 1) * rows, :]), axis=0, keepdims=True
+        )
+        sheet[order[i], 0:1, :] = total
+
+
+def work(order, sheet, block_in, weights):
+    units = weights[0].shape[1]
     low_width, rank = weights[3].shape[0], weights[4].shape[0]
     blocks = len(block_in)
     rows, width = block_in[0].shape[0] // 2, block_in[0].shape[1]
     inside = pl.BlockSpec(memory_space=pltpu.VMEM)
     call = pl.pallas_call(
-        functools.partial(rows_kernel, blocks, not sums),
+        functools.partial(rows_kernel, blocks),
         out_shape=[
-            jax.ShapeDtypeStruct(facts.shape, jnp.float32),
-            jax.ShapeDtypeStruct((low_width, rank), jnp.float32),
+            jax.ShapeDtypeStruct(sheet.shape, jnp.float32),
+            jax.ShapeDtypeStruct((low_width, blocks * rows), jnp.bfloat16),
+            jax.ShapeDtypeStruct((rank, blocks * rows), jnp.float32),
         ],
         in_specs=[pl.BlockSpec(memory_space=pltpu.SMEM)]
-        + [inside] * (1 + blocks + len(weights) + len(sums)),
-        out_specs=[inside] * 2,
+        + [inside] * (1 + blocks + len(weights)),
+        out_specs=[inside] * 3,
         scratch_shapes=[
             pltpu.VMEM((blocks * rows, width), jnp.bfloat16),
             pltpu.VMEM((blocks * rows, width), jnp.bfloat16),
-            pltpu.VMEM((blocks * rows, low_width), jnp.float32),
+            pltpu.VMEM((low_width, blocks * rows), jnp.float32),
             pltpu.VMEM((blocks * rows, 128), jnp.float32),
         ],
         compiler_params=pltpu.CompilerParams(vmem_limit_bytes=16 * 1024 * 1024),
@@ -135,7 +108,54 @@
             transcendentals=blocks * rows * units,
         ),
     )
-    return call(order, facts, *block_in, *weights, *sums)
+    return call(order, sheet, *block_in, *weights)
+
+
+def outcome_kernel(pieces, order, returned, routes, *refs):
+    low_in, proj_in = refs[:pieces], refs[pieces : 2 * pieces]
+    feat, route_grad = refs[-2:]
+    rows = returned.shape[2]
+    width, rank = low_in[0].shape[0], proj_in[0].shape[0]
+    doc_of = lax.broadcasted_iota(jnp.int32, (width, rows), 0) // rank
+    total = jnp.zeros(feat.shape, jnp.float32)
+    done = 0
+    for low_side, proj_cot in zip(low_in, proj_in):
+        spread, high_side = [], []
+        for i in range(low_side.shape[1] // rows):
+            place = slice(i * rows, (i + 1) * rows)
+            owner = order[done]
+            done += 1
+            weight = returned[owner, 1:2, :]
+            doc = returned[owner, 2:3, :].astype(jnp.int32)
+            high_side.append((weight * proj_cot[:, place]).astype(jnp.bfloat16))
+            low = low_side[:, place].astype(jnp.float32)
+            spread.append(jnp.where(doc == doc_of, low, 0.0).astype(jnp.bfloat16))
+        total += lax.dot_general(
+            jnp.concatenate(spread, axis=1),
+            jnp.concatenate(high_side, axis=1),
+            (((1,), (1,)), ((), ())),
+            preferred_element_type=jnp.float32,
+        )
+    feat[...] = total
+    picked = jnp.zeros(route_grad.shape, jnp.float32)
+    for e in range(returned.shape[0]):
+        picked = jnp.where(routes[...] == e, returned[e, 0:1, :], picked)
+    route_grad[...] = picked
+
+
+def load_kernel(repeat, *refs):
+    ins, outs, sems = refs[:5], refs[5:10], refs[10]
+    rank = ins[3].shape[0]
+    copies = [(src, dst) for i, (src, dst) in enumerate(zip(ins, outs)) if i != 3]
+    for i in range(repeat):
+        copies.append((ins[3], outs[3].at[i * rank : (i + 1) * rank]))
+    copies = [
+        pltpu.make_async_copy(src, dst, sems.at[i]) for i, (src, dst) in enumerate(copies)
+    ]
+    for copy in copies:
+        copy.start()
+    for copy in copies:
+        copy.wait()
 
 
 def facts_kernel(routes, combine, doc_ids, out):
@@ -148,7 +168,7 @@
     line = lax.broadcasted_iota(jnp.int32, (lines, rows), 0)
     doc = doc_ids[...].astype(jnp.float32)
     for e in range(groups):
-        out[e] = jnp.where(line == 0, weight[e : e + 1, :], doc)
+        out[e] = jnp.where(line == 1, weight[e : e + 1, :], doc)
 
 
 def stack_kernel(top, bottom, out, sems):
@@ -206,33 +226,41 @@
     own = pl.pallas_call(
         stack_kernel,
         out_shape=jax.ShapeDtypeStruct((2 * rows, width), tokens.dtype),
-        in_specs=[pl.BlockSpec(memory_space=pl.ANY)] * 2,
+        in_specs=[pl.BlockSpec(memory_space=pltpu.HBM)] * 2,
         out_specs=pl.BlockSpec(memory_space=pltpu.VMEM),
         scratch_shapes=[pltpu.SemaphoreType.DMA((2,))],
     )(tokens, cotangent)
     beside = swap(own)
 
-    facts = pl.pallas_call(
+    sheet = pl.pallas_call(
         facts_kernel,
         out_shape=jax.ShapeDtypeStruct((groups, 8, rows), jnp.float32),
         in_specs=[pl.BlockSpec(memory_space=pltpu.VMEM)] * 3,
         out_specs=pl.BlockSpec(memory_space=pltpu.VMEM),
     )(routes.T, combine.T, doc_ids[None, :])
-    facts = lax.all_to_all(facts, "exp", split_axis=0, concat_axis=0, tiled=True)
-
-    low_proj = jnp.concatenate([proj_hidden[0].T] * docs_count, axis=0)
-    weights = (w_gate, w_up, w_down, low_proj, proj_output[0].T)
-    sums, done = [], 0
+    inside = pl.BlockSpec(memory_space=pltpu.VMEM)
+    given = (w_gate[0], w_up[0], w_down[0], proj_hidden[0].T, proj_output[0].T)
+    shapes = [w.shape for w in given]
+    shapes[3] = (docs_count * shapes[3][0], shapes[3][1])
+    weights = pl.pallas_call(
+        functools.partial(load_kernel, docs_count),
+        out_shape=[jax.ShapeDtypeStruct(shape, w_gate.dtype) for shape in shapes],
+        in_specs=[pl.BlockSpec(memory_space=pltpu.HBM)] * 5,
+        out_specs=[inside] * 5,
+        scratch_shapes=[pltpu.SemaphoreType.DMA((4 + docs_count,))],
+    )(*given)
+    lows, projs, done = [], [], 0
     jobs = [(own, beside)]
 
     def behind(block):
-        nonlocal sums, done
+        nonlocal sheet, done
         job = jobs.pop(0)
-        sums = work(order[done : done + len(job)], facts, job, weights, sums)
+        sheet, low_side, proj_cot = work(order[done : done + len(job)], sheet, job, weights)
+        lows.append(low_side)
+        projs.append(proj_cot)
         done += len(job)
-        if block is None:
-            return None
-        sums, block = lax.optimization_barrier((sums, block))
+        if block is not None:
+            sheet, block = lax.optimization_barrier((sheet, block))
         return block
 
     near, other = own, beside
@@ -246,10 +274,19 @@
             jobs.append((other, swap(other)))
     while jobs:
         behind(None)
-    grads, feature = sums
-    returned = lax.all_to_all(grads, "exp", split_axis=0, concat_axis=0, tiled=True)
+    returned = lax.all_to_all(sheet, "exp", split_axis=0, concat_axis=0, tiled=True)
     rank = proj_output.shape[2]
-    return feature.reshape(docs_count, 1, rank, rank), pick_own(returned[:, 0, :], routes)
+    feature, route_grad = pl.pallas_call(
+        functools.partial(outcome_kernel, len(lows)),
+        out_shape=[
+            jax.ShapeDtypeStruct((docs_count * rank, rank), jnp.float32),
+            jax.ShapeDtypeStruct((chosen, tok_rows), jnp.float32),
+        ],
+        in_specs=[pl.BlockSpec(memory_space=pltpu.SMEM)] + [inside] * (2 + 2 * len(lows)),
+        out_specs=[inside] * 2,
+        compiler_params=pltpu.CompilerParams(vmem_limit_bytes=16 * 1024 * 1024),
+    )(order, returned, routes.T, *lows, *projs)
+    return feature.reshape(docs_count, 1, rank, rank), route_grad.T
 
 
 def by_routing(

time: 129 us -> 116 us (0.90)
  waiting for transfers between devices: 48.4 us -> 28.1 us
  Pallas kernels: 43.1 us -> 51.9 us
  blocking collectives: 9.83 us -> 11.8 us
  other arithmetic: 1.72 us -> 0 us
    all_to_all x1 -> x0, waiting for transfers between devices: 16.6 us -> none  [by_ring(): lax.all_to_all(facts, 'exp', split_axis=0, concat_axis=0, tiled=True)]
    pallas_call x8 -> x10, Pallas kernels: 39.5 us -> 48.3 us  [the longest x8 39 us: work(): return call(order, sheet, *block_in, *weights)]
    all_to_all x1 -> x0, starting transfers between devices: 4.9 us -> none  [by_ring(): lax.all_to_all(facts, 'exp', split_axis=0, concat_axis=0, tiled=True)]
    ppermute x7, starting transfers between devices: 9.95 us -> 13.8 us  [hop(): return lax.ppermute(block, 'exp', onward)]
    ppermute x7, waiting for transfers between devices: 31.8 us -> 28.1 us  [hop(): return lax.ppermute(block, 'exp', onward)]
    all_to_all x1, blocking collectives: 9.83 us -> 11.8 us  [by_ring(): lax.all_to_all(sheet, 'exp', split_axis=0, concat_axis=0, tiled=True)]
    unnamed x20 -> x26, local copies, waits for them, and re-layouts: 7.86 us -> 7.64 us
  transfers between devices with their start and end apart: 16 -> 15, of which waited for: 6 -> 5; matrix products, arithmetic and copies ran while one was open for 1% -> 1% of each run, Pallas kernels for 28% -> 38%
where the time goes in v6:
time: 116 us
  Pallas kernels  51.9 us (45%)
  waiting for transfers between devices  28.1 us (24%)
  starting transfers between devices  14.6 us (13%)
  blocking collectives  11.8 us (10%)
  local copies, waits for them, and re-layouts  8.42 us (7%)
    pallas_call x8, Pallas kernels, work(): return call(order, sheet, *block_in, *weights)  39 us
    ppermute x7, waiting for transfers between devices, hop(): return lax.ppermute(block, 'exp', onward)  28.1 us
    ppermute x7, starting transfers between devices, hop(): return lax.ppermute(block, 'exp', onward)  13.8 us
    all_to_all x1, blocking collectives, by_ring(): lax.all_to_all(sheet, 'exp', split_axis=0, concat_axis=0, tiled=True)  11.8 us
    pallas_call x1, Pallas kernels, by_ring(): pl.pallas_call(functools.partial(load_kernel, docs_count), out_shape=[jax...  7.74 us
    unnamed x26, local copies, waits for them, and re-layouts  7.64 us
  transfers between devices with their start and end apart: 15, of which 5 were waited for; matrix products, arithmetic and copies ran while one was open for 1% of the time, Pallas kernels for 38%

profile of v6, /device:TPU:0, one launch (start us, length us, event | category | flops | bytes accessed | tf_op | source)
XLA Modules:
  0.0 115.6 jit_solution(16145032928278154577)
XLA Ops:
  0.6 2.2 %shard_map.123.refs_2_ = bf16[256,2048]{1,0:T(8,128)(2,1)} custom-call(bf16[128,2048]{1,0:T(8,128)(2,1)} %top.1, bf16[128,2048]{1,0:T(8,128)(2,1)} %bottom.1), custom_call_target="tpu_custom_call" | custom-call | tf_op jit(solution)/shard_map/pallas_call | solution.py:226
  2.9 0.5 collective-permute-start
  3.4 2.6 %collective-permute-start.2 = (bf16[256,2048]{1,0:T(8,128)(2,1)}, bf16[256,2048]{1,0:T(8,128)(2,1)}, u32[]{:S(2)}, u32[]{:S(2)}) collective-permute-start(bf16[256,2048]{1,0:T(8,128)(2,1)} %shard_map.123.refs_2_), channel_id=1, source_target_pairs={{0,4},{1,3},{4,8},{5,1},{8,12},{9,5},{12,14},{13,9},{14,10},{15,13... | collective-permute-start | bytes 3145736 | tf_op jit(solution)/shard_map/ppermute | solution.py:202
  6.0 0.0 collective-permute-done.refs_3_
  6.0 2.9 %collective-permute-start.1 = (bf16[256,2048]{1,0:T(8,128)(2,1)}, bf16[256,2048]{1,0:T(8,128)(2,1)S(1)}, u32[]{:S(2)}, u32[]{:S(2)}) collective-permute-start(bf16[256,2048]{1,0:T(8,128)(2,1)} %collective-permute-done.refs_3_), channel_id=1, source_target_pairs={{0,4},{1,3},{4,8},{5,1},{8,12},{9,5},{12,14},{13,9},{14,10},{15,13... | collective-permute-start | bytes 3145736 | tf_op jit(solution)/shard_map/ppermute | solution.py:202
  9.0 10.1 %collective-permute-done.2.refs_2_ = bf16[256,2048]{1,0:T(8,128)(2,1)} collective-permute-done((bf16[256,2048]{1,0:T(8,128)(2,1)}, bf16[256,2048]{1,0:T(8,128)(2,1)}, u32[]{:S(2)}, u32[]{:S(2)}) %collective-permute-start.2) | collective-permute-done | bytes 1048608 | tf_op jit(solution)/shard_map/ppermute | solution.py:202
  19.0 0.0 collective-permute-start.3
  19.0 2.1 %collective-permute-start.4 = (bf16[256,2048]{1,0:T(8,128)(2,1)}, bf16[256,2048]{1,0:T(8,128)(2,1)S(1)}, u32[]{:S(2)}, u32[]{:S(2)}) collective-permute-start(bf16[256,2048]{1,0:T(8,128)(2,1)} %collective-permute-done.2.refs_2_), channel_id=1, source_target_pairs={{0,4},{1,3},{4,8},{5,1},{8,12},{9,5},{12,14},{13,9},{14,10},{15,13... | collective-permute-start | bytes 3145736 | tf_op jit(solution)/shard_map/ppermute | solution.py:202
  21.2 1.4 %shard_map.122.refs_1_ = f32[16,8,128]{2,1,0:T(8,128)} custom-call(s32[8,128]{1,0:T(8,128)} %bitcast.34, bf16[8,128]{1,0:T(8,128)(2,1)} %bitcast.41, s32[1,128]{1,0:T(1,128)} %bitcast.42), custom_call_target="tpu_custom_call" | custom-call | tf_op jit(solution)/shard_map/pallas_call | solution.py:235
  22.5 7.7 %shard_map.124 = (bf16[2048,768]{1,0:T(8,128)(2,1)}, bf16[2048,768]{1,0:T(8,128)(2,1)}, bf16[768,2048]{1,0:T(8,128)(2,1)}, bf16[256,768]{1,0:T(8,128)(2,1)}, bf16[64,2048]{1,0:T(8,128)(2,1)}) custom-call(bf16[2048,768]{1,0:T(8,128)(2,1)} %bitcast.36, bf16[2048,768]{1,0:T(8,128)(2,1)} %bitcast.37, bf16[768,2048]{1,0:T(8,128)(2,1)} %bitcast.38, ...), custom_call_target="tpu_custom_call" | custom-call | tf_op jit(solution)/shard_map/pallas_call | solution.py:245
  30.3 0.7 constant_dynamic-slice_fusion
  31.0 0.1 slice_bitcast_fusion
  31.0 1.9 %copy-done = bf16[2048,768]{1,0:T(8,128)(2,1)S(1)} copy-done((bf16[2048,768]{1,0:T(8,128)(2,1)S(1)}, bf16[2048,768]{1,0:T(8,128)(2,1)}, u32[]{:S(2)}) %copy-start) | copy-done | bytes 3145752
  32.9 1.9 %copy-done.2 = bf16[2048,768]{1,0:T(8,128)(2,1)S(1)} copy-done((bf16[2048,768]{1,0:T(8,128)(2,1)S(1)}, bf16[2048,768]{1,0:T(8,128)(2,1)}, u32[]{:S(2)}) %copy-start.2) | copy-done | bytes 3145752
  34.8 1.9 %copy-done.4 = bf16[768,2048]{1,0:T(8,128)(2,1)S(1)} copy-done((bf16[768,2048]{1,0:T(8,128)(2,1)S(1)}, bf16[768,2048]{1,0:T(8,128)(2,1)}, u32[]{:S(2)}) %copy-start.4) | copy-done | bytes 3145752
  36.7 1.0 copy-done.6
  37.7 0.9 copy-done.8
  38.7 5.5 %shard_map.125 = (f32[16,8,128]{2,1,0:T(8,128)S(1)}, bf16[256,256]{1,0:T(8,128)(2,1)S(1)}, f32[64,256]{1,0:T(8,128)S(1)}) custom-call(s32[2]{0:T(128)S(1)} %get-tuple-element.92.refs_0_, f32[16,8,128]{2,1,0:T(8,128)S(1)} %copy-done.11, bf16[256,2048]{1,0:T(8,128)(2,1)S(1)} %copy-done.10, bf16[256,2048]{1,0:T(8,128)(2,1)} %collective-permute-done.refs_3_, ...), custom_call_target="tpu_custom_call" | custom-call | flops 2415919104 | bytes 2097152 | tf_op jit(solution)/shard_map/pallas_call | solution.py:111
  44.2 0.0 collective-permute-done.1.refs_2_
  44.2 0.2 collective-permute-start.5
  44.4 1.5 %collective-permute-start.6 = (bf16[256,2048]{1,0:T(8,128)(2,1)S(1)}, bf16[256,2048]{1,0:T(8,128)(2,1)S(1)}, u32[]{:S(2)}, u32[]{:S(2)}) collective-permute-start(bf16[256,2048]{1,0:T(8,128)(2,1)S(1)} %collective-permute-done.1.refs_2_), channel_id=1, source_target_pairs={{0,4},{1,3},{4,8},{5,1},{8,12},{9,5},{12,14},{13,9},{14,10},{15,13... | collective-permute-start | bytes 3145736 | tf_op jit(solution)/shard_map/ppermute | solution.py:202
  45.9 0.0 collective-permute-done.3.refs_3_
  45.9 5.7 %shard_map.126 = (f32[16,8,128]{2,1,0:T(8,128)S(1)}, bf16[256,256]{1,0:T(8,128)(2,1)S(1)}, f32[64,256]{1,0:T(8,128)S(1)}) custom-call(s32[2]{0:T(128)S(1)} %get-tuple-element.93.refs_0_, f32[16,8,128]{2,1,0:T(8,128)S(1)} %get-tuple-element.51.refs_1_, bf16[256,2048]{1,0:T(8,128)(2,1)} %collective-permute-done.2.refs_2_, ...), custom_call_target="tpu_custom_call" | custom-call | flops 2415919104 | bytes 2097152 | tf_op jit(solution)/shard_map/pallas_call | solution.py:111
  51.6 0.1 collective-permute-start.7
  51.7 1.6 %collective-permute-start.8 = (bf16[256,2048]{1,0:T(8,128)(2,1)S(1)}, bf16[256,2048]{1,0:T(8,128)(2,1)S(1)}, u32[]{:S(2)}, u32[]{:S(2)}) collective-permute-start(bf16[256,2048]{1,0:T(8,128)(2,1)S(1)} %collective-permute-done.4.refs_2_), channel_id=1, source_target_pairs={{0,4},{1,3},{4,8},{5,1},{8,12},{9,5},{12,14},{13,9},{14,10},{15,13... | collective-permute-start | bytes 3145736 | tf_op jit(solution)/shard_map/ppermute | solution.py:202
  53.3 0.0 collective-permute-done.5.refs_3_
  53.3 4.6 %shard_map.127 = (f32[16,8,128]{2,1,0:T(8,128)S(1)}, bf16[256,256]{1,0:T(8,128)(2,1)S(1)}, f32[64,256]{1,0:T(8,128)S(1)}) custom-call(s32[2]{0:T(128)S(1)} %get-tuple-element.94.refs_0_, f32[16,8,128]{2,1,0:T(8,128)S(1)} %get-tuple-element.53.refs_1_, bf16[256,2048]{1,0:T(8,128)(2,1)S(1)} %collective-permute-done.1.refs_2_, ...), custom_call_target="tpu_custom_call" | custom-call | flops 2415919104 | bytes 2097152 | tf_op jit(solution)/shard_map/pallas_call | solution.py:111
  57.9 1.2 %collective-permute-done.6.refs_2_ = bf16[256,2048]{1,0:T(8,128)(2,1)S(1)} collective-permute-done((bf16[256,2048]{1,0:T(8,128)(2,1)S(1)}, bf16[256,2048]{1,0:T(8,128)(2,1)S(1)}, u32[]{:S(2)}, u32[]{:S(2)}) %collective-permute-start.6) | collective-permute-done | bytes 1048608 | tf_op jit(solution)/shard_map/ppermute | solution.py:202
  59.2 0.0 collective-permute-start.9
  59.2 1.5 %collective-permute-start.10 = (bf16[256,2048]{1,0:T(8,128)(2,1)S(1)}, bf16[256,2048]{1,0:T(8,128)(2,1)S(1)}, u32[]{:S(2)}, u32[]{:S(2)}) collective-permute-start(bf16[256,2048]{1,0:T(8,128)(2,1)S(1)} %collective-permute-done.6.refs_2_), channel_id=1, source_target_pairs={{0,4},{1,3},{4,8},{5,1},{8,12},{9,5},{12,14},{13,9},{14,10},{15,13... | collective-permute-start | bytes 3145736 | tf_op jit(solution)/shard_map/ppermute | solution.py:202
  60.7 0.0 collective-permute-done.7.refs_3_
  60.7 4.6 %shard_map.128 = (f32[16,8,128]{2,1,0:T(8,128)S(1)}, bf16[256,256]{1,0:T(8,128)(2,1)S(1)}, f32[64,256]{1,0:T(8,128)S(1)}) custom-call(s32[2]{0:T(128)S(1)} %get-tuple-element.95.refs_0_, f32[16,8,128]{2,1,0:T(8,128)S(1)} %get-tuple-element.56.refs_1_, bf16[256,2048]{1,0:T(8,128)(2,1)S(1)} %collective-permute-done.4.refs_2_, ...), custom_call_target="tpu_custom_call" | custom-call | flops 2415919104 | bytes 2097152 | tf_op jit(solution)/shard_map/pallas_call | solution.py:111
  65.3 5.1 %collective-permute-done.8.refs_2_ = bf16[256,2048]{1,0:T(8,128)(2,1)S(1)} collective-permute-done((bf16[256,2048]{1,0:T(8,128)(2,1)S(1)}, bf16[256,2048]{1,0:T(8,128)(2,1)S(1)}, u32[]{:S(2)}, u32[]{:S(2)}) %collective-permute-start.8) | collective-permute-done | bytes 1048608 | tf_op jit(solution)/shard_map/ppermute | solution.py:202
  70.4 0.0 collective-permute-start.11
  70.4 1.5 %collective-permute-start.12 = (bf16[256,2048]{1,0:T(8,128)(2,1)S(1)}, bf16[256,2048]{1,0:T(8,128)(2,1)S(1)}, u32[]{:S(2)}, u32[]{:S(2)}) collective-permute-start(bf16[256,2048]{1,0:T(8,128)(2,1)S(1)} %collective-permute-done.8.refs_2_), channel_id=1, source_target_pairs={{0,4},{1,3},{4,8},{5,1},{8,12},{9,5},{12,14},{13,9},{14,10},{15,13... | collective-permute-start | bytes 3145736 | tf_op jit(solution)/shard_map/ppermute | solution.py:202
  71.9 0.0 collective-permute-done.9.refs_3_
  71.9 4.6 %shard_map.129 = (f32[16,8,128]{2,1,0:T(8,128)S(1)}, bf16[256,256]{1,0:T(8,128)(2,1)S(1)}, f32[64,256]{1,0:T(8,128)S(1)}) custom-call(s32[2]{0:T(128)S(1)} %get-tuple-element.96.refs_0_, f32[16,8,128]{2,1,0:T(8,128)S(1)} %get-tuple-element.59.refs_1_, bf16[256,2048]{1,0:T(8,128)(2,1)S(1)} %collective-permute-done.6.refs_2_, ...), custom_call_target="tpu_custom_call" | custom-call | flops 2415919104 | bytes 2097152 | tf_op jit(solution)/shard_map/pallas_call | solution.py:111
  76.6 5.1 %collective-permute-done.10.refs_2_ = bf16[256,2048]{1,0:T(8,128)(2,1)S(1)} collective-permute-done((bf16[256,2048]{1,0:T(8,128)(2,1)S(1)}, bf16[256,2048]{1,0:T(8,128)(2,1)S(1)}, u32[]{:S(2)}, u32[]{:S(2)}) %collective-permute-start.10) | collective-permute-done | bytes 1048608 | tf_op jit(solution)/shard_map/ppermute | solution.py:202
  81.7 0.0 collective-permute-start.13
  81.7 0.0 collective-permute-done.11.refs_3_
  81.7 4.6 %shard_map.130 = (f32[16,8,128]{2,1,0:T(8,128)S(1)}, bf16[256,256]{1,0:T(8,128)(2,1)S(1)}, f32[64,256]{1,0:T(8,128)S(1)}) custom-call(s32[2]{0:T(128)S(1)} %get-tuple-element.97.refs_0_, f32[16,8,128]{2,1,0:T(8,128)S(1)} %get-tuple-element.62.refs_1_, bf16[256,2048]{1,0:T(8,128)(2,1)S(1)} %collective-permute-done.8.refs_2_, ...), custom_call_target="tpu_custom_call" | custom-call | flops 2415919104 | bytes 2097152 | tf_op jit(solution)/shard_map/pallas_call | solution.py:111
  86.3 6.6 %collective-permute-done.12.refs_2_ = bf16[256,2048]{1,0:T(8,128)(2,1)S(1)} collective-permute-done((bf16[256,2048]{1,0:T(8,128)(2,1)S(1)}, bf16[256,2048]{1,0:T(8,128)(2,1)S(1)}, u32[]{:S(2)}, u32[]{:S(2)}) %collective-permute-start.12) | collective-permute-done | bytes 1048608 | tf_op jit(solution)/shard_map/ppermute | solution.py:202
  92.9 4.6 %shard_map.131 = (f32[16,8,128]{2,1,0:T(8,128)S(1)}, bf16[256,256]{1,0:T(8,128)(2,1)S(1)}, f32[64,256]{1,0:T(8,128)S(1)}) custom-call(s32[2]{0:T(128)S(1)} %get-tuple-element.98.refs_0_, f32[16,8,128]{2,1,0:T(8,128)S(1)} %get-tuple-element.65.refs_1_, bf16[256,2048]{1,0:T(8,128)(2,1)S(1)} %collective-permute-done.10.refs_2_, ...), custom_call_target="tpu_custom_call" | custom-call | flops 2415919104 | bytes 2097152 | tf_op jit(solution)/shard_map/pallas_call | solution.py:111
  97.5 0.0 collective-permute-done.14.refs_3_
  97.5 0.0 copy-start.12
  97.6 4.6 %shard_map.132 = (f32[16,8,128]{2,1,0:T(8,128)S(1)}, bf16[256,256]{1,0:T(8,128)(2,1)S(1)}, f32[64,256]{1,0:T(8,128)S(1)}) custom-call(s32[2]{0:T(128)S(1)} %get-tuple-element.99.refs_0_, f32[16,8,128]{2,1,0:T(8,128)S(1)} %get-tuple-element.67.refs_1_, bf16[256,2048]{1,0:T(8,128)(2,1)S(1)} %collective-permute-done.12.refs_2_, ...), custom_call_target="tpu_custom_call" | custom-call | flops 2415919104 | bytes 2097152 | tf_op jit(solution)/shard_map/pallas_call | solution.py:111
  102.2 11.8 %all_to_all.5.returned = f32[16,8,128]{2,1,0:T(8,128)S(1)} all-to-all(f32[16,8,128]{2,1,0:T(8,128)S(1)} %get-tuple-element.69), channel_id=1, replica_groups=mesh['grp'=2,'exp'=16] {'exp'}, dimensions={0} | all-to-all | bytes 131072 | tf_op jit(solution)/shard_map/all_to_all | solution.py:277
  114.0 1.6 %shard_map.133 = (f32[256,64]{1,0:T(8,128)}, f32[8,128]{1,0:T(8,128)}) custom-call(s32[16]{0:T(128)S(1)} %get-tuple-element.91.order, f32[16,8,128]{2,1,0:T(8,128)S(1)} %all_to_all.5.returned, s32[8,128]{1,0:T(8,128)S(1)} %bitcast.35, bf16[256,256]{1,0:T(8,128)(2,1)S(1)} %get-tuple-element.70.refs_0_, bf16[256,256]{1,0:T(8,128)(2,1)S(1)} %get-tuple-element.71.refs_1_, ...), custom_call_target="tpu_custom_call" | custom-call | tf_op jit(solution)/shard_map/pallas_call | solution.py:279
  (23 shorter events, 0.0 us)
Async XLA Ops:
  2.9 3.2 %collective-permute-start = (bf16[256,2048]{1,0:T(8,128)(2,1)}, bf16[256,2048]{1,0:T(8,128)(2,1)}, u32[]{:S(2)}, u32[]{:S(2)}) collective-permute-start(bf16[256,2048]{1,0:T(8,128)(2,1)} %shard_map.123.refs_2_), channel_id=1, source_target_pairs={{0,1},{1,0},{2,3},{3,2},{4,5},{5,4},{6,7},{7,6},{8,9},{9,8},{10,11... | collective-permute-start | bytes 3145736 | tf_op jit(solution)/shard_map/ppermute | solution.py:205
  3.4 15.6 %collective-permute-start.2 = (bf16[256,2048]{1,0:T(8,128)(2,1)}, bf16[256,2048]{1,0:T(8,128)(2,1)}, u32[]{:S(2)}, u32[]{:S(2)}) collective-permute-start(bf16[256,2048]{1,0:T(8,128)(2,1)} %shard_map.123.refs_2_), channel_id=1, source_target_pairs={{0,4},{1,3},{4,8},{5,1},{8,12},{9,5},{12,14},{13,9},{14,10},{15,13... | collective-permute-start | bytes 3145736 | tf_op jit(solution)/shard_map/ppermute | solution.py:202
  6.0 38.1 %collective-permute-start.1 = (bf16[256,2048]{1,0:T(8,128)(2,1)}, bf16[256,2048]{1,0:T(8,128)(2,1)S(1)}, u32[]{:S(2)}, u32[]{:S(2)}) collective-permute-start(bf16[256,2048]{1,0:T(8,128)(2,1)} %collective-permute-done.refs_3_), channel_id=1, source_target_pairs={{0,4},{1,3},{4,8},{5,1},{8,12},{9,5},{12,14},{13,9},{14,10},{15,13... | collective-permute-start | bytes 3145736 | tf_op jit(solution)/shard_map/ppermute | solution.py:202
  19.0 26.8 %collective-permute-start.3 = (bf16[256,2048]{1,0:T(8,128)(2,1)}, bf16[256,2048]{1,0:T(8,128)(2,1)}, u32[]{:S(2)}, u32[]{:S(2)}) collective-permute-start(bf16[256,2048]{1,0:T(8,128)(2,1)} %collective-permute-done.2.refs_2_), channel_id=1, source_target_pairs={{0,1},{1,0},{2,3},{3,2},{4,5},{5,4},{6,7},{7,6},{8,9},{9,8},{10,11... | collective-permute-start | bytes 3145736 | tf_op jit(solution)/shard_map/ppermute | solution.py:205
  19.0 32.5 %collective-permute-start.4 = (bf16[256,2048]{1,0:T(8,128)(2,1)}, bf16[256,2048]{1,0:T(8,128)(2,1)S(1)}, u32[]{:S(2)}, u32[]{:S(2)}) collective-permute-start(bf16[256,2048]{1,0:T(8,128)(2,1)} %collective-permute-done.2.refs_2_), channel_id=1, source_target_pairs={{0,4},{1,3},{4,8},{5,1},{8,12},{9,5},{12,14},{13,9},{14,10},{15,13... | collective-permute-start | bytes 3145736 | tf_op jit(solution)/shard_map/ppermute | solution.py:202
  22.5 8.5 %copy-start.10 = (bf16[256,2048]{1,0:T(8,128)(2,1)S(1)}, bf16[256,2048]{1,0:T(8,128)(2,1)}, u32[]{:S(2)}) copy-start(bf16[256,2048]{1,0:T(8,128)(2,1)} %shard_map.123.refs_2_) | copy-start | bytes 3145732
  22.5 8.5 %copy-start.11 = (f32[16,8,128]{2,1,0:T(8,128)S(1)}, f32[16,8,128]{2,1,0:T(8,128)}, u32[]{:S(2)}) copy-start(f32[16,8,128]{2,1,0:T(8,128)} %shard_map.122.refs_1_) | copy-start | bytes 196612
  31.0 1.9 %copy-start = (bf16[2048,768]{1,0:T(8,128)(2,1)S(1)}, bf16[2048,768]{1,0:T(8,128)(2,1)}, u32[]{:S(2)}) copy-start(bf16[2048,768]{1,0:T(8,128)(2,1)} %get-tuple-element.45.refs_4_) | copy-start | bytes 9437188
  32.9 1.9 %copy-start.2 = (bf16[2048,768]{1,0:T(8,128)(2,1)S(1)}, bf16[2048,768]{1,0:T(8,128)(2,1)}, u32[]{:S(2)}) copy-start(bf16[2048,768]{1,0:T(8,128)(2,1)} %get-tuple-element.46.refs_5_) | copy-start | bytes 9437188
  34.8 1.9 %copy-start.4 = (bf16[768,2048]{1,0:T(8,128)(2,1)S(1)}, bf16[768,2048]{1,0:T(8,128)(2,1)}, u32[]{:S(2)}) copy-start(bf16[768,2048]{1,0:T(8,128)(2,1)} %get-tuple-element.47.refs_6_) | copy-start | bytes 9437188
  36.7 1.0 copy-start.6
  37.7 0.9 copy-start.8
  38.7 7.2 %copy-start.1 = (bf16[2048,768]{1,0:T(8,128)(2,1)S(1)}, bf16[2048,768]{1,0:T(8,128)(2,1)}, u32[]{:S(2)}) copy-start(bf16[2048,768]{1,0:T(8,128)(2,1)} %get-tuple-element.45.refs_4_) | copy-start | bytes 9437188
  38.7 7.2 %copy-start.3 = (bf16[2048,768]{1,0:T(8,128)(2,1)S(1)}, bf16[2048,768]{1,0:T(8,128)(2,1)}, u32[]{:S(2)}) copy-start(bf16[2048,768]{1,0:T(8,128)(2,1)} %get-tuple-element.46.refs_5_) | copy-start | bytes 9437188
  38.7 7.2 %copy-start.5 = (bf16[768,2048]{1,0:T(8,128)(2,1)S(1)}, bf16[768,2048]{1,0:T(8,128)(2,1)}, u32[]{:S(2)}) copy-start(bf16[768,2048]{1,0:T(8,128)(2,1)} %get-tuple-element.47.refs_6_) | copy-start | bytes 9437188
  38.7 7.2 %copy-start.7 = (bf16[256,768]{1,0:T(8,128)(2,1)S(1)}, bf16[256,768]{1,0:T(8,128)(2,1)}, u32[]{:S(2)}) copy-start(bf16[256,768]{1,0:T(8,128)(2,1)} %get-tuple-element.48.refs_7_) | copy-start | bytes 1179652
  38.7 7.2 %copy-start.9 = (bf16[64,2048]{1,0:T(8,128)(2,1)S(1)}, bf16[64,2048]{1,0:T(8,128)(2,1)}, u32[]{:S(2)}) copy-start(bf16[64,2048]{1,0:T(8,128)(2,1)} %get-tuple-element.49.refs_8_) | copy-start | bytes 786436
  44.2 9.1 %collective-permute-start.5 = (bf16[256,2048]{1,0:T(8,128)(2,1)S(1)}, bf16[256,2048]{1,0:T(8,128)(2,1)S(1)}, u32[]{:S(2)}, u32[]{:S(2)}) collective-permute-start(bf16[256,2048]{1,0:T(8,128)(2,1)S(1)} %collective-permute-done.1.refs_2_), channel_id=1, source_target_pairs={{0,1},{1,0},{2,3},{3,2},{4,5},{5,4},{6,7},{7,6},{8,9},{9,8},{10,11... | collective-permute-start | bytes 3145736 | tf_op jit(solution)/shard_map/ppermute | solution.py:205
  44.4 14.8 %collective-permute-start.6 = (bf16[256,2048]{1,0:T(8,128)(2,1)S(1)}, bf16[256,2048]{1,0:T(8,128)(2,1)S(1)}, u32[]{:S(2)}, u32[]{:S(2)}) collective-permute-start(bf16[256,2048]{1,0:T(8,128)(2,1)S(1)} %collective-permute-done.1.refs_2_), channel_id=1, source_target_pairs={{0,4},{1,3},{4,8},{5,1},{8,12},{9,5},{12,14},{13,9},{14,10},{15,13... | collective-permute-start | bytes 3145736 | tf_op jit(solution)/shard_map/ppermute | solution.py:202
  51.6 9.1 %collective-permute-start.7 = (bf16[256,2048]{1,0:T(8,128)(2,1)S(1)}, bf16[256,2048]{1,0:T(8,128)(2,1)S(1)}, u32[]{:S(2)}, u32[]{:S(2)}) collective-permute-start(bf16[256,2048]{1,0:T(8,128)(2,1)S(1)} %collective-permute-done.4.refs_2_), channel_id=1, source_target_pairs={{0,1},{1,0},{2,3},{3,2},{4,5},{5,4},{6,7},{7,6},{8,9},{9,8},{10,11... | collective-permute-start | bytes 3145736 | tf_op jit(solution)/shard_map/ppermute | solution.py:205
  51.7 18.8 %collective-permute-start.8 = (bf16[256,2048]{1,0:T(8,128)(2,1)S(1)}, bf16[256,2048]{1,0:T(8,128)(2,1)S(1)}, u32[]{:S(2)}, u32[]{:S(2)}) collective-permute-start(bf16[256,2048]{1,0:T(8,128)(2,1)S(1)} %collective-permute-done.4.refs_2_), channel_id=1, source_target_pairs={{0,4},{1,3},{4,8},{5,1},{8,12},{9,5},{12,14},{13,9},{14,10},{15,13... | collective-permute-start | bytes 3145736 | tf_op jit(solution)/shard_map/ppermute | solution.py:202
  59.2 12.7 %collective-permute-start.9 = (bf16[256,2048]{1,0:T(8,128)(2,1)S(1)}, bf16[256,2048]{1,0:T(8,128)(2,1)S(1)}, u32[]{:S(2)}, u32[]{:S(2)}) collective-permute-start(bf16[256,2048]{1,0:T(8,128)(2,1)S(1)} %collective-permute-done.6.refs_2_), channel_id=1, source_target_pairs={{0,1},{1,0},{2,3},{3,2},{4,5},{5,4},{6,7},{7,6},{8,9},{9,8},{10,11... | collective-permute-start | bytes 3145736 | tf_op jit(solution)/shard_map/ppermute | solution.py:205
  59.2 22.5 %collective-permute-start.10 = (bf16[256,2048]{1,0:T(8,128)(2,1)S(1)}, bf16[256,2048]{1,0:T(8,128)(2,1)S(1)}, u32[]{:S(2)}, u32[]{:S(2)}) collective-permute-start(bf16[256,2048]{1,0:T(8,128)(2,1)S(1)} %collective-permute-done.6.refs_2_), channel_id=1, source_target_pairs={{0,4},{1,3},{4,8},{5,1},{8,12},{9,5},{12,14},{13,9},{14,10},{15,13... | collective-permute-start | bytes 3145736 | tf_op jit(solution)/shard_map/ppermute | solution.py:202
  70.4 11.2 %collective-permute-start.11 = (bf16[256,2048]{1,0:T(8,128)(2,1)S(1)}, bf16[256,2048]{1,0:T(8,128)(2,1)S(1)}, u32[]{:S(2)}, u32[]{:S(2)}) collective-permute-start(bf16[256,2048]{1,0:T(8,128)(2,1)S(1)} %collective-permute-done.8.refs_2_), channel_id=1, source_target_pairs={{0,1},{1,0},{2,3},{3,2},{4,5},{5,4},{6,7},{7,6},{8,9},{9,8},{10,11... | collective-permute-start | bytes 3145736 | tf_op jit(solution)/shard_map/ppermute | solution.py:205
  70.4 22.5 %collective-permute-start.12 = (bf16[256,2048]{1,0:T(8,128)(2,1)S(1)}, bf16[256,2048]{1,0:T(8,128)(2,1)S(1)}, u32[]{:S(2)}, u32[]{:S(2)}) collective-permute-start(bf16[256,2048]{1,0:T(8,128)(2,1)S(1)} %collective-permute-done.8.refs_2_), channel_id=1, source_target_pairs={{0,4},{1,3},{4,8},{5,1},{8,12},{9,5},{12,14},{13,9},{14,10},{15,13... | collective-permute-start | bytes 3145736 | tf_op jit(solution)/shard_map/ppermute | solution.py:202
  81.7 11.2 %collective-permute-start.13 = (bf16[256,2048]{1,0:T(8,128)(2,1)S(1)}, bf16[256,2048]{1,0:T(8,128)(2,1)S(1)}, u32[]{:S(2)}, u32[]{:S(2)}) collective-permute-start(bf16[256,2048]{1,0:T(8,128)(2,1)S(1)} %collective-permute-done.10.refs_2_), channel_id=1, source_target_pairs={{0,1},{1,0},{2,3},{3,2},{4,5},{5,4},{6,7},{7,6},{8,9},{9,8},{10,11... | collective-permute-start | bytes 3145736 | tf_op jit(solution)/shard_map/ppermute | solution.py:205
  92.9 4.6 %collective-permute-start.14 = (bf16[256,2048]{1,0:T(8,128)(2,1)S(1)}, bf16[256,2048]{1,0:T(8,128)(2,1)S(1)}, u32[]{:S(2)}, u32[]{:S(2)}) collective-permute-start(bf16[256,2048]{1,0:T(8,128)(2,1)S(1)} %collective-permute-done.12.refs_2_), channel_id=1, source_target_pairs={{0,1},{1,0},{2,3},{3,2},{4,5},{5,4},{6,7},{7,6},{8,9},{9,8},{10,11... | collective-permute-start | bytes 3145736 | tf_op jit(solution)/shard_map/ppermute | solution.py:205
  97.5 16.4 %copy-start.12 = (s32[128,8]{0,1:T(8,128)S(1)}, s32[128,8]{0,1:T(8,128)}, u32[]{:S(2)}) copy-start(s32[128,8]{0,1:T(8,128)} %param.13) | copy-start | bytes 12292

commit v7 on v6

--- a/solution.py
+++ b/solution.py
@@ -9,6 +9,7 @@
 from jax.sharding import PartitionSpec as P
 
 DOC_TOK = 512
+LOAD_MIB = 40
 
 
 def swiglu(rows, w_gate, w_up):
@@ -35,25 +36,43 @@
     return grad, feature.reshape(docs_count, low_side.shape[1], high_side.shape[1])
 
 
-def rows_kernel(blocks, *refs):
+def rows_kernel(blocks, load, *refs):
     order, sheet_in = refs[:2]
     block_in = refs[2 : 2 + blocks]
-    w_gate, w_up, w_down, low_proj, high_proj = refs[2 + blocks : 7 + blocks]
-    sheet, low_side, proj_cot, x_all, dy_all, low_sum, grad_sum = refs[-7:]
+    given = refs[2 + blocks : 7 + blocks]
+    sheet, low_side, proj_cot = refs[7 + blocks : 10 + blocks]
+    x_all, dy_all, low_sum, grad_sum = refs[-5:-1] if load else refs[-4:]
+    w_gate, w_up, w_down, low_proj, high_proj = refs[10 + blocks : 15 + blocks] if load else given
     rows = block_in[0].shape[0] // 2
     across = (((1,), (1,)), ((), ()))
+    units = w_gate.shape[1]
+    tile = 256 if units % 256 == 0 else units
+    tiles = units // tile
+    lanes = grad_sum.shape[1]
+    copies = []
+    if load:
+        rank = given[3].shape[0]
+        for j in range(tiles):
+            part = pl.ds(j * tile, tile)
+            copies.append((given[0].at[:, part], w_gate.at[:, part]))
+            copies.append((given[1].at[:, part], w_up.at[:, part]))
+            copies.append((given[2].at[part, :], w_down.at[part, :]))
+        for i in range(low_proj.shape[0] // rank):
+            copies.append((given[3], low_proj.at[pl.ds(i * rank, rank), :]))
+        copies.append((given[4], high_proj))
+        copies = [
+            pltpu.make_async_copy(src, dst, refs[-1].at[i]) for i, (src, dst) in enumerate(copies)
+        ]
+        for copy in copies[3 * tiles :] + copies[: 3 * tiles]:
+            copy.start()
     for i in range(blocks):
         x_all[i * rows : (i + 1) * rows, :] = block_in[i][:rows, :]
         dy_all[i * rows : (i + 1) * rows, :] = block_in[i][rows:, :]
     low_sum[...] = jnp.zeros_like(low_sum)
     grad_sum[...] = jnp.zeros_like(grad_sum)
-    units = w_gate.shape[1]
-    tile = 256 if units % 256 == 0 else units
-    lanes = grad_sum.shape[1]
-
-    @pl.loop(0, units // tile)
-    def _(j):
-        part = pl.ds(pl.multiple_of(j * tile, tile), tile)
+
+    def one_tile(j):
+        part = pl.ds(j * tile, tile)
         gate_val = jnp.dot(x_all[...], w_gate[:, part], preferred_element_type=jnp.float32)
         up_val = jnp.dot(x_all[...], w_up[:, part], preferred_element_type=jnp.float32)
         hidden = (jax.nn.silu(gate_val) * up_val).astype(jnp.bfloat16)
@@ -67,41 +86,65 @@
             low_proj[:, part], hidden, across, preferred_element_type=jnp.float32
         )
 
+    for copy in copies[3 * tiles :]:
+        copy.wait()
+    for j in range(tiles):
+        for copy in copies[3 * j : 3 * j + 3] if load else []:
+            copy.wait()
+        one_tile(j)
+
     low_side[...] = low_sum[...].astype(low_side.dtype)
     proj_cot[...] = lax.dot_general(
         high_proj[...], dy_all[...], across, preferred_element_type=jnp.float32
     )
-    sheet[...] = sheet_in[...]
+    own_lines = sheet.shape[0] == blocks
+    if not own_lines:
+        sheet[...] = sheet_in[...]
     for i in range(blocks):
         total = jnp.sum(
             jnp.transpose(grad_sum[i * rows : (i + 1) * rows, :]), axis=0, keepdims=True
         )
-        sheet[order[i], 0:1, :] = total
-
-
-def work(order, sheet, block_in, weights):
-    units = weights[0].shape[1]
-    low_width, rank = weights[3].shape[0], weights[4].shape[0]
+        if own_lines:
+            sheet[i] = jnp.broadcast_to(total, sheet.shape[1:])
+        else:
+            sheet[order[i], 0:1, :] = total
+
+
+def work(order, sheet, block_in, weights, load=0, apart=False):
+    width, units = weights[0].shape
+    low_width, rank = weights[3].shape[0] * max(load, 1), weights[4].shape[0]
     blocks = len(block_in)
-    rows, width = block_in[0].shape[0] // 2, block_in[0].shape[1]
+    rows = block_in[0].shape[0] // 2
     inside = pl.BlockSpec(memory_space=pltpu.VMEM)
+    loaded = []
+    if load:
+        shapes = [w.shape for w in weights]
+        shapes[3] = (low_width, units)
+        loaded = [jax.ShapeDtypeStruct(shape, weights[0].dtype) for shape in shapes]
+    tiles = units // 256 if units % 256 == 0 else 1
+    lines = (blocks if apart else sheet.shape[0],) + sheet.shape[1:]
     call = pl.pallas_call(
-        functools.partial(rows_kernel, blocks),
+        functools.partial(rows_kernel, blocks, load > 0),
         out_shape=[
-            jax.ShapeDtypeStruct(sheet.shape, jnp.float32),
+            jax.ShapeDtypeStruct(lines, jnp.float32),
             jax.ShapeDtypeStruct((low_width, blocks * rows), jnp.bfloat16),
             jax.ShapeDtypeStruct((rank, blocks * rows), jnp.float32),
-        ],
+        ]
+        + loaded,
         in_specs=[pl.BlockSpec(memory_space=pltpu.SMEM)]
-        + [inside] * (1 + blocks + len(weights)),
-        out_specs=[inside] * 3,
+        + [inside] * (1 + blocks)
+        + [pl.BlockSpec(memory_space=pl.ANY) if load else inside] * len(weights),
+        out_specs=[inside] * (3 + len(loaded)),
         scratch_shapes=[
             pltpu.VMEM((blocks * rows, width), jnp.bfloat16),
             pltpu.VMEM((blocks * rows, width), jnp.bfloat16),
             pltpu.VMEM((low_width, blocks * rows), jnp.float32),
             pltpu.VMEM((blocks * rows, 128), jnp.float32),
-        ],
-        compiler_params=pltpu.CompilerParams(vmem_limit_bytes=16 * 1024 * 1024),
+        ]
+        + ([pltpu.SemaphoreType.DMA((3 * tiles + load + 1,))] if load else []),
+        compiler_params=pltpu.CompilerParams(
+            vmem_limit_bytes=(LOAD_MIB if load else 16) * 1024 * 1024
+        ),
         cost_estimate=pl.CostEstimate(
             flops=6 * blocks * rows * width * units,
             bytes_accessed=4 * blocks * rows * width,
@@ -111,8 +154,9 @@
     return call(order, sheet, *block_in, *weights)
 
 
-def outcome_kernel(pieces, order, returned, routes, *refs):
+def outcome_kernel(pieces, order, source, returned, routes, *refs):
     low_in, proj_in = refs[:pieces], refs[pieces : 2 * pieces]
+    late = refs[2 * pieces : -2]
     feat, route_grad = refs[-2:]
     rows = returned.shape[2]
     width, rank = low_in[0].shape[0], proj_in[0].shape[0]
@@ -140,22 +184,10 @@
     picked = jnp.zeros(route_grad.shape, jnp.float32)
     for e in range(returned.shape[0]):
         picked = jnp.where(routes[...] == e, returned[e, 0:1, :], picked)
+    for i in range(len(late)):
+        sender = source[source.shape[0] - len(late) + i]
+        picked = jnp.where(routes[...] == sender, late[i][0, 0:1, :], picked)
     route_grad[...] = picked
-
-
-def load_kernel(repeat, *refs):
-    ins, outs, sems = refs[:5], refs[5:10], refs[10]
-    rank = ins[3].shape[0]
-    copies = [(src, dst) for i, (src, dst) in enumerate(zip(ins, outs)) if i != 3]
-    for i in range(repeat):
-        copies.append((ins[3], outs[3].at[i * rank : (i + 1) * rank]))
-    copies = [
-        pltpu.make_async_copy(src, dst, sems.at[i]) for i, (src, dst) in enumerate(copies)
-    ]
-    for copy in copies:
-        copy.start()
-    for copy in copies:
-        copy.wait()
 
 
 def facts_kernel(routes, combine, doc_ids, out):
@@ -204,23 +236,33 @@
     def swap(block):
         return lax.ppermute(block, "exp", across)
 
-    orders = np.zeros((groups, groups), np.int32)
+    arrivals = [(c, step) for step in range(1, half + 1) for c in ("ab" if step < half else "a")]
+    jobs = [[("a", 0, False), ("a", 0, True)]]
+    for i, (c, step) in enumerate(arrivals):
+        job = [(c, step, False)]
+        if i > 0:
+            job.append(arrivals[i - 1] + (True,))
+        if i == 1:
+            job.append(arrivals[0] + (False,))
+        if i != 0:
+            jobs.append(job)
+    jobs.append([arrivals[-1] + (True,)])
+    blocks_of = [block for job in jobs for block in job]
+
+    orders = np.zeros((groups, 2 * groups), np.int32)
     for place in range(chips):
         for core in range(2):
-            way = 1 - 2 * core
-
-            def owner(steps, which):
-                return 2 * ring[(place + steps) % chips] + which
-
-            order = [owner(0, core), owner(0, 1 - core)]
-            for step in range(1, half + 1):
-                near, far = -step * way, step * way
-                order += [owner(near, core), owner(far, 1 - core)]
-                if step < half:
-                    order += [owner(near, 1 - core), owner(far, core)]
-            orders[owner(0, core)] = order
-    me = lax.axis_index("exp")
-    order = lax.dynamic_index_in_dim(jnp.asarray(orders), me, axis=0, keepdims=False)
+            me = 2 * ring[place] + core
+            for i, (c, step, handed) in enumerate(blocks_of):
+                first = core if (c == "a") != handed else 1 - core
+                way = (1 if core == 1 else -1) * (-1 if handed else 1)
+                owner = 2 * ring[(place + way * step) % chips] + first
+                orders[me, i] = owner
+                orders[owner, groups + i] = me
+    mine = lax.dynamic_index_in_dim(
+        jnp.asarray(orders), lax.axis_index("exp"), axis=0, keepdims=False
+    )
+    order, source = mine[:groups], mine[groups:]
 
     rows, width = tokens.shape
     own = pl.pallas_call(
@@ -240,41 +282,49 @@
     )(routes.T, combine.T, doc_ids[None, :])
     inside = pl.BlockSpec(memory_space=pltpu.VMEM)
     given = (w_gate[0], w_up[0], w_down[0], proj_hidden[0].T, proj_output[0].T)
-    shapes = [w.shape for w in given]
-    shapes[3] = (docs_count * shapes[3][0], shapes[3][1])
-    weights = pl.pallas_call(
-        functools.partial(load_kernel, docs_count),
-        out_shape=[jax.ShapeDtypeStruct(shape, w_gate.dtype) for shape in shapes],
-        in_specs=[pl.BlockSpec(memory_space=pltpu.HBM)] * 5,
-        out_specs=[inside] * 5,
-        scratch_shapes=[pltpu.SemaphoreType.DMA((4 + docs_count,))],
-    )(*given)
+    weights = None
     lows, projs, done = [], [], 0
-    jobs = [(own, beside)]
-
-    def behind(block):
-        nonlocal sheet, done
+    held = {("a", 0, False): own, ("a", 0, True): beside}
+
+    def take(apart=False):
+        nonlocal sheet, weights, done
         job = jobs.pop(0)
-        sheet, low_side, proj_cot = work(order[done : done + len(job)], sheet, job, weights)
+        share, blocks = order[done : done + len(job)], [held[name] for name in job]
+        if weights is None:
+            lines, low_side, proj_cot, *weights = work(
+                share, sheet, blocks, given, load=docs_count
+            )
+        else:
+            lines, low_side, proj_cot = work(share, sheet, blocks, weights, apart=apart)
         lows.append(low_side)
         projs.append(proj_cot)
         done += len(job)
-        if block is not None:
-            sheet, block = lax.optimization_barrier((sheet, block))
-        return block
-
-    near, other = own, beside
-    for step in range(1, half + 1):
-        near = hop(near)
-        if step > 1:
-            near = behind(near)
-        jobs.append((near, swap(near)))
-        if step < half:
-            other = behind(hop(other))
-            jobs.append((other, swap(other)))
+        if not apart:
+            sheet = lines
+            return low_side
+        for i in range(len(job)):
+            spot = done - len(job) + i
+            back = [(d, int(orders[d, spot])) for d in range(groups)]
+            late.append(lax.ppermute(lines[i : i + 1], "exp", back))
+        return low_side
+
+    def tie(one, other):
+        return lax.optimization_barrier((one, other))
+
+    late = []
+    chain = {"a": own, "b": beside}
+    for i, (c, step) in enumerate(arrivals):
+        block = hop(chain[c])
+        if i != 1:
+            lows[-1:], block = tie([take(apart=i == len(arrivals) - 1)], block)
+        if i == len(arrivals) - 1:
+            returned, block = tie(returned, block)
+        chain[c] = held[(c, step, False)] = block
+        held[(c, step, True)] = swap(block)
+        if i == len(arrivals) - 2:
+            returned = lax.all_to_all(sheet, "exp", split_axis=0, concat_axis=0, tiled=True)
     while jobs:
-        behind(None)
-    returned = lax.all_to_all(sheet, "exp", split_axis=0, concat_axis=0, tiled=True)
+        take(apart=True)
     rank = proj_output.shape[2]
     feature, route_grad = pl.pallas_call(
         functools.partial(outcome_kernel, len(lows)),
@@ -282,10 +332,11 @@
             jax.ShapeDtypeStruct((docs_count * rank, rank), jnp.float32),
             jax.ShapeDtypeStruct((chosen, tok_rows), jnp.float32),
         ],
-        in_specs=[pl.BlockSpec(memory_space=pltpu.SMEM)] + [inside] * (2 + 2 * len(lows)),
+        in_specs=[pl.BlockSpec(memory_space=pltpu.SMEM)] * 2
+        + [inside] * (2 + 2 * len(lows) + len(late)),
         out_specs=[inside] * 2,
         compiler_params=pltpu.CompilerParams(vmem_limit_bytes=16 * 1024 * 1024),
-    )(order, returned, routes.T, *lows, *projs)
+    )(order, source, returned, routes.T, *lows, *projs, *late)
     return feature.reshape(docs_count, 1, rank, rank), route_grad.T
 
 
@@ -354,7 +405,7 @@
 def on_device(tokens, cotangent, routes, combine, doc_ids, w_gate, *rest):
     tok_rows, chosen = routes.shape
     experts = w_gate.shape[0] * lax.axis_size("exp")
-    dense = w_gate.shape[0] == 1 and 4 * chosen >= experts and experts % 4 == 0
+    dense = w_gate.shape[0] == 1 and 4 * chosen >= experts and experts >= 8 and experts % 4 == 0
     plan = by_ring if dense else by_routing
     return plan(tokens, cotangent, routes, combine, doc_ids, w_gate, *rest)
 

time: 116 us -> 126 us (1.086)
  starting transfers between devices: 14.6 us -> 30.4 us
  local copies, waits for them, and re-layouts: 8.42 us -> 21.8 us
  blocking collectives: 11.8 us -> 0 us
  Pallas kernels: 51.9 us -> 44.8 us
    unnamed x26 -> x86, local copies, waits for them, and re-layouts: 7.64 us -> 19.6 us
    all_to_all x1 -> x0, blocking collectives: 11.8 us -> none  [by_ring(): lax.all_to_all(sheet, 'exp', split_axis=0, concat_axis=0, tiled=True)]
    ppermute x0 -> x5, starting transfers between devices: none -> 8.59 us  [take(): late.append(lax.ppermute(lines[i:i + 1], 'exp', back))]
    pallas_call x1 -> x0, Pallas kernels: 7.74 us -> none  [by_ring(): pl.pallas_call(functools.partial(load_kernel, docs_count), out_shape=[jax...]
    all_to_all x0 -> x1, starting transfers between devices: none -> 6.6 us  [by_ring(): lax.all_to_all(sheet, 'exp', split_axis=0, concat_axis=0, tiled=True)]
    ppermute x7, waiting for transfers between devices: 28.1 us -> 21.7 us  [hop(): return lax.ppermute(block, 'exp', onward)]
    ppermute x0 -> x5, waiting for transfers between devices: none -> 5.63 us  [take(): late.append(lax.ppermute(lines[i:i + 1], 'exp', back))]
    slice x1 -> x6, local copies, waits for them, and re-layouts: 0.08 us -> 1.49 us  [the longest x3 1.41 us: take(): share, blocks = (order[done:done + len(job)], [held[name] for name in job])]
  transfers between devices with their start and end apart: 15 -> 21, of which waited for: 5 -> 7; matrix products, arithmetic and copies ran while one was open for 1% -> 2% of each run, Pallas kernels for 38% -> 32%
where the time goes in v7:
time: 126 us; the launch traced here: 125 us
  Pallas kernels  44.8 us (36%)
  starting transfers between devices  30.4 us (24%)
  waiting for transfers between devices  27.4 us (22%)
  local copies, waits for them, and re-layouts  21.8 us (17%)
    pallas_call x8, Pallas kernels, work(): return call(order, sheet, *block_in, *weights)  39.2 us
    ppermute x7, waiting for transfers between devices, hop(): return lax.ppermute(block, 'exp', onward)  21.7 us
    unnamed x86, local copies, waits for them, and re-layouts  19.6 us
    ppermute x7, starting transfers between devices, hop(): return lax.ppermute(block, 'exp', onward)  14.3 us
    ppermute x5, starting transfers between devices, take(): late.append(lax.ppermute(lines[i:i + 1], 'exp', back))  8.59 us
    all_to_all x1, starting transfers between devices, by_ring(): lax.all_to_all(sheet, 'exp', split_axis=0, concat_axis=0, tiled=True)  6.6 us
    ppermute x5, waiting for transfers between devices, take(): late.append(lax.ppermute(lines[i:i + 1], 'exp', back))  5.63 us
  transfers between devices with their start and end apart: 21, of which 7 were waited for; matrix products, arithmetic and copies ran while one was open for 2% of the time, Pallas kernels for 32%

profile of v7, /device:TPU:0, one launch (start us, length us, event | category | flops | bytes accessed | tf_op | source)
XLA Modules:
  0.0 125.4 jit_solution(9009115299987978679)
XLA Ops:
  0.6 2.3 %shard_map.123.refs_2_ = bf16[256,2048]{1,0:T(8,128)(2,1)} custom-call(bf16[128,2048]{1,0:T(8,128)(2,1)} %top.1, bf16[128,2048]{1,0:T(8,128)(2,1)} %bottom.1), custom_call_target="tpu_custom_call" | custom-call | tf_op jit(solution)/shard_map/pallas_call | solution.py:268
  3.4 2.6 %collective-permute-start.2 = (bf16[256,2048]{1,0:T(8,128)(2,1)}, bf16[256,2048]{1,0:T(8,128)(2,1)}, u32[]{:S(2)}, u32[]{:S(2)}) collective-permute-start(bf16[256,2048]{1,0:T(8,128)(2,1)} %shard_map.123.refs_2_), channel_id=1, source_target_pairs={{0,4},{1,3},{4,8},{5,1},{8,12},{9,5},{12,14},{13,9},{14,10},{15,13... | collective-permute-start | bytes 3145736 | tf_op jit(solution)/shard_map/ppermute | solution.py:234
  6.1 1.4 %shard_map.122.refs_1_ = f32[16,8,128]{2,1,0:T(8,128)} custom-call(s32[8,128]{1,0:T(8,128)} %bitcast.37, bf16[8,128]{1,0:T(8,128)(2,1)} %bitcast.42, s32[1,128]{1,0:T(1,128)} %bitcast.43), custom_call_target="tpu_custom_call" | custom-call | tf_op jit(solution)/shard_map/pallas_call | solution.py:277
  7.4 0.7 constant_dynamic-slice_fusion
  8.2 1.6 %collective-permute-start.1 = (bf16[256,2048]{1,0:T(8,128)(2,1)}, bf16[256,2048]{1,0:T(8,128)(2,1)S(1)}, u32[]{:S(2)}, u32[]{:S(2)}) collective-permute-start(bf16[256,2048]{1,0:T(8,128)(2,1)} %collective-permute-done.refs_3_), channel_id=1, source_target_pairs={{0,4},{1,3},{4,8},{5,1},{8,12},{9,5},{12,14},{13,9},{14,10},{15,13... | collective-permute-start | bytes 3145736 | tf_op jit(solution)/shard_map/ppermute | solution.py:234
  9.8 1.2 copy-done.9
  11.0 0.8 copy-done.13
  11.9 0.9 copy-done.14
  12.8 0.9 copy-done.27
  13.7 7.8 %shard_map.124 = (f32[16,8,128]{2,1,0:T(8,128)S(1)}, bf16[256,256]{1,0:T(8,128)(2,1)S(1)}, f32[64,256]{1,0:T(8,128)S(1)}, bf16[2048,768]{1,0:T(8,128)(2,1)S(1)},...) custom-call(s32[2]{0:T(128)S(1)} %get-tuple-element.100.refs_0_, ...), custom_call_target="tpu_custom_call" | custom-call | flops 2415919104 | bytes 2097152 | tf_op jit(solution)/shard_map/pallas_call | solution.py:154
  21.6 1.6 %collective-permute-start.4 = (bf16[256,2048]{1,0:T(8,128)(2,1)}, bf16[256,2048]{1,0:T(8,128)(2,1)S(1)}, u32[]{:S(2)}, u32[]{:S(2)}) collective-permute-start(bf16[256,2048]{1,0:T(8,128)(2,1)} %collective-permute-done.2.refs_4_), channel_id=1, source_target_pairs={{0,4},{1,3},{4,8},{5,1},{8,12},{9,5},{12,14},{13,9},{14,10},{15,13... | collective-permute-start | bytes 3145736 | tf_op jit(solution)/shard_map/ppermute | solution.py:234
  23.2 7.0 %collective-permute-done.1.refs_2_ = bf16[256,2048]{1,0:T(8,128)(2,1)S(1)} collective-permute-done((bf16[256,2048]{1,0:T(8,128)(2,1)}, bf16[256,2048]{1,0:T(8,128)(2,1)S(1)}, u32[]{:S(2)}, u32[]{:S(2)}) %collective-permute-start.1) | collective-permute-done | bytes 1048608 | tf_op jit(solution)/shard_map/ppermute | solution.py:234
  30.3 2.1 %collective-permute-start.6 = (bf16[256,2048]{1,0:T(8,128)(2,1)S(1)}, bf16[256,2048]{1,0:T(8,128)(2,1)S(1)}, u32[]{:S(2)}, u32[]{:S(2)}) collective-permute-start(bf16[256,2048]{1,0:T(8,128)(2,1)S(1)} %collective-permute-done.1.refs_2_), channel_id=1, source_target_pairs={{0,4},{1,3},{4,8},{5,1},{8,12},{9,5},{12,14},{13,9},{14,10},{15,13... | collective-permute-start | bytes 3145736 | tf_op jit(solution)/shard_map/ppermute | solution.py:234
  32.4 6.0 %shard_map.125 = (f32[16,8,128]{2,1,0:T(8,128)S(1)}, bf16[256,384]{1,0:T(8,128)(2,1)S(1)}, f32[64,384]{1,0:T(8,128)S(1)}) custom-call(s32[3]{0:T(128)S(1)} %slice_bitcast_fusion.3.refs_0_, f32[16,8,128]{2,1,0:T(8,128)S(1)} %get-tuple-element.47.refs_1_, bf16[256,2048]{1,0:T(8,128)(2,1)S(1)} %collective-permute-done.1.refs_2_, ...), custom_call_target="tpu_custom_call" | custom-call | flops 3623878656 | bytes 3145728 | tf_op jit(solution)/shard_map/pallas_call | solution.py:154
  38.4 3.0 %collective-permute-done.4.refs_2_ = bf16[256,2048]{1,0:T(8,128)(2,1)S(1)} collective-permute-done((bf16[256,2048]{1,0:T(8,128)(2,1)}, bf16[256,2048]{1,0:T(8,128)(2,1)S(1)}, u32[]{:S(2)}, u32[]{:S(2)}) %collective-permute-start.4) | collective-permute-done | bytes 1048608 | tf_op jit(solution)/shard_map/ppermute | solution.py:234
  41.5 2.1 %collective-permute-start.8 = (bf16[256,2048]{1,0:T(8,128)(2,1)S(1)}, bf16[256,2048]{1,0:T(8,128)(2,1)}, u32[]{:S(2)}, u32[]{:S(2)}) collective-permute-start(bf16[256,2048]{1,0:T(8,128)(2,1)S(1)} %collective-permute-done.4.refs_2_), channel_id=1, source_target_pairs={{0,4},{1,3},{4,8},{5,1},{8,12},{9,5},{12,14},{13,9},{14,10},{15,13... | collective-permute-start | bytes 3145736 | tf_op jit(solution)/shard_map/ppermute | solution.py:234
  43.6 3.9 %shard_map.126 = (f32[16,8,128]{2,1,0:T(8,128)S(1)}, bf16[256,256]{1,0:T(8,128)(2,1)S(1)}, f32[64,256]{1,0:T(8,128)S(1)}) custom-call(s32[2]{0:T(128)S(1)} %get-tuple-element.101.refs_0_, f32[16,8,128]{2,1,0:T(8,128)S(1)} %get-tuple-element.55.refs_1_, bf16[256,2048]{1,0:T(8,128)(2,1)S(1)} %collective-permute-done.4.refs_2_, ...), custom_call_target="tpu_custom_call" | custom-call | flops 2415919104 | bytes 2097152 | tf_op jit(solution)/shard_map/pallas_call | solution.py:154
  47.5 0.6 copy-done.19
  48.8 3.9 %collective-permute-done.6.refs_2_ = bf16[256,2048]{1,0:T(8,128)(2,1)S(1)} collective-permute-done((bf16[256,2048]{1,0:T(8,128)(2,1)S(1)}, bf16[256,2048]{1,0:T(8,128)(2,1)S(1)}, u32[]{:S(2)}, u32[]{:S(2)}) %collective-permute-start.6) | collective-permute-done | bytes 1048608 | tf_op jit(solution)/shard_map/ppermute | solution.py:234
  52.7 2.1 %collective-permute-start.10 = (bf16[256,2048]{1,0:T(8,128)(2,1)S(1)}, bf16[256,2048]{1,0:T(8,128)(2,1)}, u32[]{:S(2)}, u32[]{:S(2)}) collective-permute-start(bf16[256,2048]{1,0:T(8,128)(2,1)S(1)} %collective-permute-done.6.refs_2_), channel_id=1, source_target_pairs={{0,4},{1,3},{4,8},{5,1},{8,12},{9,5},{12,14},{13,9},{14,10},{15,13... | collective-permute-start | bytes 3145736 | tf_op jit(solution)/shard_map/ppermute | solution.py:234
  54.8 3.9 %shard_map.127 = (f32[16,8,128]{2,1,0:T(8,128)S(1)}, bf16[256,256]{1,0:T(8,128)(2,1)S(1)}, f32[64,256]{1,0:T(8,128)S(1)}) custom-call(s32[2]{0:T(128)S(1)} %get-tuple-element.102.refs_0_, f32[16,8,128]{2,1,0:T(8,128)S(1)} %get-tuple-element.58.refs_1_, bf16[256,2048]{1,0:T(8,128)(2,1)S(1)} %collective-permute-done.6.refs_2_, ...), custom_call_target="tpu_custom_call" | custom-call | flops 2415919104 | bytes 2097152 | tf_op jit(solution)/shard_map/pallas_call | solution.py:154
  58.7 0.7 copy-done.21
  59.4 4.6 %collective-permute-done.8.refs_2_ = bf16[256,2048]{1,0:T(8,128)(2,1)} collective-permute-done((bf16[256,2048]{1,0:T(8,128)(2,1)S(1)}, bf16[256,2048]{1,0:T(8,128)(2,1)}, u32[]{:S(2)}, u32[]{:S(2)}) %collective-permute-start.8) | collective-permute-done | bytes 1048608 | tf_op jit(solution)/shard_map/ppermute | solution.py:234
  64.0 2.1 %collective-permute-start.12 = (bf16[256,2048]{1,0:T(8,128)(2,1)}, bf16[256,2048]{1,0:T(8,128)(2,1)}, u32[]{:S(2)}, u32[]{:S(2)}) collective-permute-start(bf16[256,2048]{1,0:T(8,128)(2,1)} %collective-permute-done.8.refs_2_), channel_id=1, source_target_pairs={{0,4},{1,3},{4,8},{5,1},{8,12},{9,5},{12,14},{13,9},{14,10},{15,13... | collective-permute-start | bytes 3145736 | tf_op jit(solution)/shard_map/ppermute | solution.py:234
  66.2 4.6 %shard_map.128 = (f32[16,8,128]{2,1,0:T(8,128)S(1)}, bf16[256,256]{1,0:T(8,128)(2,1)S(1)}, f32[64,256]{1,0:T(8,128)S(1)}) custom-call(s32[2]{0:T(128)S(1)} %get-tuple-element.103.refs_0_, f32[16,8,128]{2,1,0:T(8,128)S(1)} %get-tuple-element.61.refs_1_, bf16[256,2048]{1,0:T(8,128)(2,1)} %collective-permute-done.8.refs_2_, ...), custom_call_target="tpu_custom_call" | custom-call | flops 2415919104 | bytes 2097152 | tf_op jit(solution)/shard_map/pallas_call | solution.py:154
  70.8 0.6 copy-done.23
  72.1 3.2 %collective-permute-done.10.refs_2_ = bf16[256,2048]{1,0:T(8,128)(2,1)} collective-permute-done((bf16[256,2048]{1,0:T(8,128)(2,1)S(1)}, bf16[256,2048]{1,0:T(8,128)(2,1)}, u32[]{:S(2)}, u32[]{:S(2)}) %collective-permute-start.10) | collective-permute-done | bytes 1048608 | tf_op jit(solution)/shard_map/ppermute | solution.py:234
  75.3 6.6 %all-to-all-start = ((f32[16,8,128]{2,1,0:T(8,128)}), f32[16,8,128]{2,1,0:T(8,128)}, u32[]{:S(2)}, u32[]{:S(2)}) async-start(f32[16,8,128]{2,1,0:T(8,128)} %copy-done.10), calls=%async_computation | async-start | bytes 131072 | tf_op jit(solution)/shard_map/all_to_all | solution.py:325
  81.9 1.9 %copy-done.1 = bf16[2048,768]{1,0:T(8,128)(2,1)S(1)} copy-done((bf16[2048,768]{1,0:T(8,128)(2,1)S(1)}, bf16[2048,768]{1,0:T(8,128)(2,1)}, u32[]{:S(2)}) %copy-start.1) | copy-done | bytes 3145752
  83.8 1.9 %copy-done.4 = bf16[768,2048]{1,0:T(8,128)(2,1)S(1)} copy-done((bf16[768,2048]{1,0:T(8,128)(2,1)S(1)}, bf16[768,2048]{1,0:T(8,128)(2,1)}, u32[]{:S(2)}) %copy-start.4) | copy-done | bytes 3145752
  85.7 0.9 copy-done.7
  86.6 0.8 copy-done.11
  87.5 4.9 %shard_map.129 = (f32[2,8,128]{2,1,0:T(8,128)S(1)}, bf16[256,256]{1,0:T(8,128)(2,1)S(1)}, f32[64,256]{1,0:T(8,128)S(1)}) custom-call(s32[2]{0:T(128)S(1)} %get-tuple-element.99.refs_0_, f32[16,8,128]{2,1,0:T(8,128)S(1)} %copy-done.11, bf16[256,2048]{1,0:T(8,128)(2,1)} %collective-permute-done.10.refs_2_, bf16[256,2048]{1,0:T(8,128)(2,1)} %collective-permute-done.11.refs_3_, ...), custom_call_target="tpu_custom_call" | custom-call | flops 2415919104 | bytes 2097152 | tf_op jit(solution)/shard_map/pallas_call | solution.py:154
  92.3 0.6 copy-done.25
  93.0 0.6 copy-done.38
  94.0 1.3 %slice.98 = s32[1,1]{1,0:T(1,128)} slice(s32[1,32]{1,0:T(1,128)} %copy-done.41), slice={[0:1], [15:16]} | slice | bytes 8 | tf_op jit(solution)/shard_map/slice | solution.py:292
  95.2 3.4 %collective-permute-start.15 = (f32[1,8,128]{2,1,0:T(8,128)S(1)}, f32[1,8,128]{2,1,0:T(8,128)S(1)}, u32[]{:S(2)}, u32[]{:S(2)}) collective-permute-start(f32[1,8,128]{2,1,0:T(8,128)S(1)} %get-tuple-element.97), channel_id=1, source_target_pairs={{0,11},{1,12},{2,15},{3,8},{4,7},{5,14},{6,13},{7,4},{8,3},{9,10},... | collective-permute-start | bytes 12296 | tf_op jit(solution)/shard_map/ppermute | solution.py:308
  98.7 1.2 collective-permute-start.16
  99.9 1.9 %copy-done.2 = bf16[2048,768]{1,0:T(8,128)(2,1)S(1)} copy-done((bf16[2048,768]{1,0:T(8,128)(2,1)S(1)}, bf16[2048,768]{1,0:T(8,128)(2,1)}, u32[]{:S(2)}) %copy-start.2) | copy-done | bytes 3145752
  101.8 1.9 %copy-done.5 = bf16[768,2048]{1,0:T(8,128)(2,1)S(1)} copy-done((bf16[768,2048]{1,0:T(8,128)(2,1)S(1)}, bf16[768,2048]{1,0:T(8,128)(2,1)}, u32[]{:S(2)}) %copy-start.5) | copy-done | bytes 3145752
  103.7 0.9 copy-done.8
  104.6 0.8 copy-done.12
  105.5 4.9 %shard_map.130 = (f32[2,8,128]{2,1,0:T(8,128)S(1)}, bf16[256,256]{1,0:T(8,128)(2,1)S(1)}, f32[64,256]{1,0:T(8,128)S(1)}) custom-call(s32[2]{0:T(128)S(1)} %get-tuple-element.98.refs_0_, f32[16,8,128]{2,1,0:T(8,128)S(1)} %copy-done.12, bf16[256,2048]{1,0:T(8,128)(2,1)} %collective-permute-done.12.refs_2_, bf16[256,2048]{1,0:T(8,128)(2,1)} %collective-permute-done.13.refs_3_, ...), custom_call_target="tpu_custom_call" | custom-call | flops 2415919104 | bytes 2097152 | tf_op jit(solution)/shard_map/pallas_call | solution.py:154
  110.3 2.4 %collective-permute-start.17 = (f32[1,8,128]{2,1,0:T(8,128)S(1)}, f32[1,8,128]{2,1,0:T(8,128)S(1)}, u32[]{:S(2)}, u32[]{:S(2)}) collective-permute-start(f32[1,8,128]{2,1,0:T(8,128)S(1)} %get-tuple-element.95), channel_id=1, source_target_pairs={{0,14},{1,15},{2,12},{3,13},{4,10},{5,11},{6,8},{7,9},{8,6},{9,7},... | collective-permute-start | bytes 12296 | tf_op jit(solution)/shard_map/ppermute | solution.py:308
  112.8 1.5 %collective-permute-start.18 = (f32[1,8,128]{2,1,0:T(8,128)S(1)}, f32[1,8,128]{2,1,0:T(8,128)S(1)}, u32[]{:S(2)}, u32[]{:S(2)}) collective-permute-start(f32[1,8,128]{2,1,0:T(8,128)S(1)} %get-tuple-element.94), channel_id=1, source_target_pairs={{0,12},{1,11},{2,8},{3,15},{4,14},{5,7},{6,4},{7,13},{8,10},{9,3},... | collective-permute-start | bytes 12296 | tf_op jit(solution)/shard_map/ppermute | solution.py:308
  114.4 3.2 %shard_map.131 = (f32[1,8,128]{2,1,0:T(8,128)S(1)}, bf16[256,128]{1,0:T(8,128)(2,1)S(1)}, f32[64,128]{1,0:T(8,128)S(1)}) custom-call(s32[1]{0:T(128)} %bitcast.19.refs_0_, f32[16,8,128]{2,1,0:T(8,128)S(1)} %copy-done.12, bf16[256,2048]{1,0:T(8,128)(2,1)S(1)} %collective-permute-done.14.refs_2_, ...), custom_call_target="tpu_custom_call" | custom-call | flops 1207959552 | bytes 1048576 | tf_op jit(solution)/shard_map/pallas_call | solution.py:154
  118.2 5.2 %collective-permute-done.19.refs_20_ = f32[1,8,128]{2,1,0:T(8,128)S(1)} collective-permute-done((f32[1,8,128]{2,1,0:T(8,128)S(1)}, f32[1,8,128]{2,1,0:T(8,128)S(1)}, u32[]{:S(2)}, u32[]{:S(2)}) %collective-permute-start.19) | collective-permute-done | bytes 4128 | tf_op jit(solution)/shard_map/ppermute | solution.py:308
  123.5 2.0 %shard_map.132 = (f32[256,64]{1,0:T(8,128)}, f32[8,128]{1,0:T(8,128)}) custom-call(s32[16]{0:T(128)S(1)} %get-tuple-element.105.order, s32[16]{0:T(128)S(1)} %get-tuple-element.104.source, f32[16,8,128]{2,1,0:T(8,128)} %all-to-all-done.returned, s32[8,128]{1,0:T(8,128)S(1)} %bitcast.38, bf16[256,256]{1,0:T(8,128)(2,1)S(1)} %copy-done.18, ...), custom_call_target="tpu_custom_call" | custom-call | tf_op jit(solution)/shard_map/pallas_call | solution.py:329
  (98 shorter events, 3.1 us)
Async XLA Ops:
  2.9 5.3 %collective-permute-start = (bf16[256,2048]{1,0:T(8,128)(2,1)}, bf16[256,2048]{1,0:T(8,128)(2,1)}, u32[]{:S(2)}, u32[]{:S(2)}) collective-permute-start(bf16[256,2048]{1,0:T(8,128)(2,1)} %shard_map.123.refs_2_), channel_id=1, source_target_pairs={{0,1},{1,0},{2,3},{3,2},{4,5},{5,4},{6,7},{7,6},{8,9},{9,8},{10,11... | collective-permute-start | bytes 3145736 | tf_op jit(solution)/shard_map/ppermute | solution.py:237
  3.4 18.1 %collective-permute-start.2 = (bf16[256,2048]{1,0:T(8,128)(2,1)}, bf16[256,2048]{1,0:T(8,128)(2,1)}, u32[]{:S(2)}, u32[]{:S(2)}) collective-permute-start(bf16[256,2048]{1,0:T(8,128)(2,1)} %shard_map.123.refs_2_), channel_id=1, source_target_pairs={{0,4},{1,3},{4,8},{5,1},{8,12},{9,5},{12,14},{13,9},{14,10},{15,13... | collective-permute-start | bytes 3145736 | tf_op jit(solution)/shard_map/ppermute | solution.py:234
  8.1 30.2 %copy-start.41 = (s32[1,32]{1,0:T(1,128)}, s32[1,32]{1,0:T(1,128)S(1)}, u32[]{:S(2)}) copy-start(s32[1,32]{1,0:T(1,128)S(1)} %constant_dynamic-slice_fusion) | copy-start | bytes 388
  8.2 22.0 %collective-permute-start.1 = (bf16[256,2048]{1,0:T(8,128)(2,1)}, bf16[256,2048]{1,0:T(8,128)(2,1)S(1)}, u32[]{:S(2)}, u32[]{:S(2)}) collective-permute-start(bf16[256,2048]{1,0:T(8,128)(2,1)} %collective-permute-done.refs_3_), channel_id=1, source_target_pairs={{0,4},{1,3},{4,8},{5,1},{8,12},{9,5},{12,14},{13,9},{14,10},{15,13... | collective-permute-start | bytes 3145736 | tf_op jit(solution)/shard_map/ppermute | solution.py:234
  21.5 16.9 %copy-start.17 = (bf16[256,256]{1,0:T(8,128)(2,1)}, bf16[256,256]{1,0:T(8,128)(2,1)S(1)}, u32[]{:S(2)}) copy-start(bf16[256,256]{1,0:T(8,128)(2,1)S(1)} %get-tuple-element.70.refs_0_) | copy-start | bytes 393220
  21.5 16.9 %copy-start.30 = (f32[64,256]{1,0:T(8,128)}, f32[64,256]{1,0:T(8,128)S(1)}, u32[]{:S(2)}) copy-start(f32[64,256]{1,0:T(8,128)S(1)} %get-tuple-element.79.refs_8_) | copy-start | bytes 196612
  21.5 44.7 %copy-start = (bf16[2048,768]{1,0:T(8,128)(2,1)}, bf16[2048,768]{1,0:T(8,128)(2,1)S(1)}, u32[]{:S(2)}) copy-start(bf16[2048,768]{1,0:T(8,128)(2,1)S(1)} %get-tuple-element.51.refs_6_.refs_5_.refs_4_) | copy-start | bytes 9437188
  21.5 44.6 %copy-start.3 = (bf16[768,2048]{1,0:T(8,128)(2,1)}, bf16[768,2048]{1,0:T(8,128)(2,1)S(1)}, u32[]{:S(2)}) copy-start(bf16[768,2048]{1,0:T(8,128)(2,1)S(1)} %get-tuple-element.52.refs_7_.refs_6_.refs_5_) | copy-start | bytes 9437188
  21.5 44.6 %copy-start.6 = (bf16[64,2048]{1,0:T(8,128)(2,1)}, bf16[64,2048]{1,0:T(8,128)(2,1)S(1)}, u32[]{:S(2)}) copy-start(bf16[64,2048]{1,0:T(8,128)(2,1)S(1)} %get-tuple-element.54.refs_9_.refs_8_.refs_7_) | copy-start | bytes 786436
  21.5 10.9 %collective-permute-start.3 = (bf16[256,2048]{1,0:T(8,128)(2,1)}, bf16[256,2048]{1,0:T(8,128)(2,1)S(1)}, u32[]{:S(2)}, u32[]{:S(2)}) collective-permute-start(bf16[256,2048]{1,0:T(8,128)(2,1)} %collective-permute-done.2.refs_4_), channel_id=1, source_target_pairs={{0,1},{1,0},{2,3},{3,2},{4,5},{5,4},{6,7},{7,6},{8,9},{9,8},{10,11... | collective-permute-start | bytes 3145736 | tf_op jit(solution)/shard_map/ppermute | solution.py:237
  21.6 19.8 %collective-permute-start.4 = (bf16[256,2048]{1,0:T(8,128)(2,1)}, bf16[256,2048]{1,0:T(8,128)(2,1)S(1)}, u32[]{:S(2)}, u32[]{:S(2)}) collective-permute-start(bf16[256,2048]{1,0:T(8,128)(2,1)} %collective-permute-done.2.refs_4_), channel_id=1, source_target_pairs={{0,4},{1,3},{4,8},{5,1},{8,12},{9,5},{12,14},{13,9},{14,10},{15,13... | collective-permute-start | bytes 3145736 | tf_op jit(solution)/shard_map/ppermute | solution.py:234
  30.2 13.3 %collective-permute-start.5 = (bf16[256,2048]{1,0:T(8,128)(2,1)S(1)}, bf16[256,2048]{1,0:T(8,128)(2,1)S(1)}, u32[]{:S(2)}, u32[]{:S(2)}) collective-permute-start(bf16[256,2048]{1,0:T(8,128)(2,1)S(1)} %collective-permute-done.1.refs_2_), channel_id=1, source_target_pairs={{0,1},{1,0},{2,3},{3,2},{4,5},{5,4},{6,7},{7,6},{8,9},{9,8},{10,11... | collective-permute-start | bytes 3145736 | tf_op jit(solution)/shard_map/ppermute | solution.py:237
  30.3 22.4 %collective-permute-start.6 = (bf16[256,2048]{1,0:T(8,128)(2,1)S(1)}, bf16[256,2048]{1,0:T(8,128)(2,1)S(1)}, u32[]{:S(2)}, u32[]{:S(2)}) collective-permute-start(bf16[256,2048]{1,0:T(8,128)(2,1)S(1)} %collective-permute-done.1.refs_2_), channel_id=1, source_target_pairs={{0,4},{1,3},{4,8},{5,1},{8,12},{9,5},{12,14},{13,9},{14,10},{15,13... | collective-permute-start | bytes 3145736 | tf_op jit(solution)/shard_map/ppermute | solution.py:234
  38.4 9.1 %copy-start.15 = (bf16[256,384]{1,0:T(8,128)(2,1)}, bf16[256,384]{1,0:T(8,128)(2,1)S(1)}, u32[]{:S(2)}) copy-start(bf16[256,384]{1,0:T(8,128)(2,1)S(1)} %get-tuple-element.71.refs_1_) | copy-start | bytes 589828
  38.4 9.1 %copy-start.28 = (f32[64,384]{1,0:T(8,128)}, f32[64,384]{1,0:T(8,128)S(1)}, u32[]{:S(2)}) copy-start(f32[64,384]{1,0:T(8,128)S(1)} %get-tuple-element.80.refs_9_) | copy-start | bytes 294916
  41.5 13.3 %collective-permute-start.7 = (bf16[256,2048]{1,0:T(8,128)(2,1)S(1)}, bf16[256,2048]{1,0:T(8,128)(2,1)S(1)}, u32[]{:S(2)}, u32[]{:S(2)}) collective-permute-start(bf16[256,2048]{1,0:T(8,128)(2,1)S(1)} %collective-permute-done.4.refs_2_), channel_id=1, source_target_pairs={{0,1},{1,0},{2,3},{3,2},{4,5},{5,4},{6,7},{7,6},{8,9},{9,8},{10,11... | collective-permute-start | bytes 3145736 | tf_op jit(solution)/shard_map/ppermute | solution.py:237
  41.5 22.6 %collective-permute-start.8 = (bf16[256,2048]{1,0:T(8,128)(2,1)S(1)}, bf16[256,2048]{1,0:T(8,128)(2,1)}, u32[]{:S(2)}, u32[]{:S(2)}) collective-permute-start(bf16[256,2048]{1,0:T(8,128)(2,1)S(1)} %collective-permute-done.4.refs_2_), channel_id=1, source_target_pairs={{0,4},{1,3},{4,8},{5,1},{8,12},{9,5},{12,14},{13,9},{14,10},{15,13... | collective-permute-start | bytes 3145736 | tf_op jit(solution)/shard_map/ppermute | solution.py:234
  52.7 13.5 %collective-permute-start.9 = (bf16[256,2048]{1,0:T(8,128)(2,1)S(1)}, bf16[256,2048]{1,0:T(8,128)(2,1)S(1)}, u32[]{:S(2)}, u32[]{:S(2)}) collective-permute-start(bf16[256,2048]{1,0:T(8,128)(2,1)S(1)} %collective-permute-done.6.refs_2_), channel_id=1, source_target_pairs={{0,1},{1,0},{2,3},{3,2},{4,5},{5,4},{6,7},{7,6},{8,9},{9,8},{10,11... | collective-permute-start | bytes 3145736 | tf_op jit(solution)/shard_map/ppermute | solution.py:237
  52.7 22.6 %collective-permute-start.10 = (bf16[256,2048]{1,0:T(8,128)(2,1)S(1)}, bf16[256,2048]{1,0:T(8,128)(2,1)}, u32[]{:S(2)}, u32[]{:S(2)}) collective-permute-start(bf16[256,2048]{1,0:T(8,128)(2,1)S(1)} %collective-permute-done.6.refs_2_), channel_id=1, source_target_pairs={{0,4},{1,3},{4,8},{5,1},{8,12},{9,5},{12,14},{13,9},{14,10},{15,13... | collective-permute-start | bytes 3145736 | tf_op jit(solution)/shard_map/ppermute | solution.py:234
  59.4 11.4 %copy-start.34 = (f32[64,256]{1,0:T(8,128)}, f32[64,256]{1,0:T(8,128)S(1)}, u32[]{:S(2)}) copy-start(f32[64,256]{1,0:T(8,128)S(1)} %get-tuple-element.82.refs_11_) | copy-start | bytes 196612
  64.0 17.9 %collective-permute-start.11 = (bf16[256,2048]{1,0:T(8,128)(2,1)}, bf16[256,2048]{1,0:T(8,128)(2,1)}, u32[]{:S(2)}, u32[]{:S(2)}) collective-permute-start(bf16[256,2048]{1,0:T(8,128)(2,1)} %collective-permute-done.8.refs_2_), channel_id=1, source_target_pairs={{0,1},{1,0},{2,3},{3,2},{4,5},{5,4},{6,7},{7,6},{8,9},{9,8},{10,11... | collective-permute-start | bytes 3145736 | tf_op jit(solution)/shard_map/ppermute | solution.py:237
  64.0 29.6 %collective-permute-start.12 = (bf16[256,2048]{1,0:T(8,128)(2,1)}, bf16[256,2048]{1,0:T(8,128)(2,1)}, u32[]{:S(2)}, u32[]{:S(2)}) collective-permute-start(bf16[256,2048]{1,0:T(8,128)(2,1)} %collective-permute-done.8.refs_2_), channel_id=1, source_target_pairs={{0,4},{1,3},{4,8},{5,1},{8,12},{9,5},{12,14},{13,9},{14,10},{15,13... | collective-permute-start | bytes 3145736 | tf_op jit(solution)/shard_map/ppermute | solution.py:234
  72.1 3.2 %copy-start.10 = (f32[16,8,128]{2,1,0:T(8,128)}, f32[16,8,128]{2,1,0:T(8,128)S(1)}, u32[]{:S(2)}) copy-start(f32[16,8,128]{2,1,0:T(8,128)S(1)} %get-tuple-element.64.refs_1_) | copy-start | bytes 196612
  75.3 24.6 %collective-permute-start.13 = (bf16[256,2048]{1,0:T(8,128)(2,1)}, bf16[256,2048]{1,0:T(8,128)(2,1)}, u32[]{:S(2)}, u32[]{:S(2)}) collective-permute-start(bf16[256,2048]{1,0:T(8,128)(2,1)} %collective-permute-done.10.refs_2_), channel_id=1, source_target_pairs={{0,1},{1,0},{2,3},{3,2},{4,5},{5,4},{6,7},{7,6},{8,9},{9,8},{10,11... | collective-permute-start | bytes 3145736 | tf_op jit(solution)/shard_map/ppermute | solution.py:237
  75.3 18.3 %all-to-all-start = ((f32[16,8,128]{2,1,0:T(8,128)}), f32[16,8,128]{2,1,0:T(8,128)}, u32[]{:S(2)}, u32[]{:S(2)}) async-start(f32[16,8,128]{2,1,0:T(8,128)} %copy-done.10), calls=%async_computation | async-start | bytes 131072 | tf_op jit(solution)/shard_map/all_to_all | solution.py:325
  81.9 1.9 %copy-start.1 = (bf16[2048,768]{1,0:T(8,128)(2,1)S(1)}, bf16[2048,768]{1,0:T(8,128)(2,1)}, u32[]{:S(2)}) copy-start(bf16[2048,768]{1,0:T(8,128)(2,1)} %copy-done) | copy-start | bytes 9437188
  83.8 1.9 %copy-start.4 = (bf16[768,2048]{1,0:T(8,128)(2,1)S(1)}, bf16[768,2048]{1,0:T(8,128)(2,1)}, u32[]{:S(2)}) copy-start(bf16[768,2048]{1,0:T(8,128)(2,1)} %copy-done.3) | copy-start | bytes 9437188
  93.6 20.6 %collective-permute-start.14 = (bf16[256,2048]{1,0:T(8,128)(2,1)}, bf16[256,2048]{1,0:T(8,128)(2,1)S(1)}, u32[]{:S(2)}, u32[]{:S(2)}) collective-permute-start(bf16[256,2048]{1,0:T(8,128)(2,1)} %collective-permute-done.12.refs_2_), channel_id=1, source_target_pairs={{0,1},{1,0},{2,3},{3,2},{4,5},{5,4},{6,7},{7,6},{8,9},{9,8},{10,11... | collective-permute-start | bytes 3145736 | tf_op jit(solution)/shard_map/ppermute | solution.py:237
  95.2 22.5 %collective-permute-start.15 = (f32[1,8,128]{2,1,0:T(8,128)S(1)}, f32[1,8,128]{2,1,0:T(8,128)S(1)}, u32[]{:S(2)}, u32[]{:S(2)}) collective-permute-start(f32[1,8,128]{2,1,0:T(8,128)S(1)} %get-tuple-element.97), channel_id=1, source_target_pairs={{0,11},{1,12},{2,15},{3,8},{4,7},{5,14},{6,13},{7,4},{8,3},{9,10},... | collective-permute-start | bytes 12296 | tf_op jit(solution)/shard_map/ppermute | solution.py:308
  98.7 19.1 %collective-permute-start.16 = (f32[1,8,128]{2,1,0:T(8,128)S(1)}, f32[1,8,128]{2,1,0:T(8,128)S(1)}, u32[]{:S(2)}, u32[]{:S(2)}) collective-permute-start(f32[1,8,128]{2,1,0:T(8,128)S(1)} %get-tuple-element.96), channel_id=1, source_target_pairs={{0,13},{1,10},{2,9},{3,14},{4,15},{5,6},{6,5},{7,12},{8,11},{9,2},... | collective-permute-start | bytes 12296 | tf_op jit(solution)/shard_map/ppermute | solution.py:308
  99.9 1.9 %copy-start.2 = (bf16[2048,768]{1,0:T(8,128)(2,1)S(1)}, bf16[2048,768]{1,0:T(8,128)(2,1)}, u32[]{:S(2)}) copy-start(bf16[2048,768]{1,0:T(8,128)(2,1)} %copy-done) | copy-start | bytes 9437188
  110.3 7.4 %collective-permute-start.17 = (f32[1,8,128]{2,1,0:T(8,128)S(1)}, f32[1,8,128]{2,1,0:T(8,128)S(1)}, u32[]{:S(2)}, u32[]{:S(2)}) collective-permute-start(f32[1,8,128]{2,1,0:T(8,128)S(1)} %get-tuple-element.95), channel_id=1, source_target_pairs={{0,14},{1,15},{2,12},{3,13},{4,10},{5,11},{6,8},{7,9},{8,6},{9,7},... | collective-permute-start | bytes 12296 | tf_op jit(solution)/shard_map/ppermute | solution.py:308
  112.8 5.4 %collective-permute-start.18 = (f32[1,8,128]{2,1,0:T(8,128)S(1)}, f32[1,8,128]{2,1,0:T(8,128)S(1)}, u32[]{:S(2)}, u32[]{:S(2)}) collective-permute-start(f32[1,8,128]{2,1,0:T(8,128)S(1)} %get-tuple-element.94), channel_id=1, source_target_pairs={{0,12},{1,11},{2,8},{3,15},{4,14},{5,7},{6,4},{7,13},{8,10},{9,3},... | collective-permute-start | bytes 12296 | tf_op jit(solution)/shard_map/ppermute | solution.py:308
  114.2 3.4 %copy-start.42 = (s32[1,32]{1,0:T(1,128)S(1)}, s32[1,32]{1,0:T(1,128)}, u32[]{:S(2)}) copy-start(s32[1,32]{1,0:T(1,128)} %copy-done.41) | copy-start | bytes 388
  114.3 9.1 %copy-start.16 = (bf16[256,384]{1,0:T(8,128)(2,1)S(1)}, bf16[256,384]{1,0:T(8,128)(2,1)}, u32[]{:S(2)}) copy-start(bf16[256,384]{1,0:T(8,128)(2,1)} %copy-done.15) | copy-start | bytes 589828
  114.3 9.1 %copy-start.18 = (bf16[256,256]{1,0:T(8,128)(2,1)S(1)}, bf16[256,256]{1,0:T(8,128)(2,1)}, u32[]{:S(2)}) copy-start(bf16[256,256]{1,0:T(8,128)(2,1)} %copy-done.17) | copy-start | bytes 393220
  114.3 9.1 %copy-start.20 = (bf16[256,256]{1,0:T(8,128)(2,1)S(1)}, bf16[256,256]{1,0:T(8,128)(2,1)}, u32[]{:S(2)}) copy-start(bf16[256,256]{1,0:T(8,128)(2,1)} %copy-done.19) | copy-start | bytes 393220
  114.3 9.1 %copy-start.22 = (bf16[256,256]{1,0:T(8,128)(2,1)S(1)}, bf16[256,256]{1,0:T(8,128)(2,1)}, u32[]{:S(2)}) copy-start(bf16[256,256]{1,0:T(8,128)(2,1)} %copy-done.21) | copy-start | bytes 393220
  114.3 9.1 %copy-start.24 = (bf16[256,256]{1,0:T(8,128)(2,1)S(1)}, bf16[256,256]{1,0:T(8,128)(2,1)}, u32[]{:S(2)}) copy-start(bf16[256,256]{1,0:T(8,128)(2,1)} %copy-done.23) | copy-start | bytes 393220
  114.3 9.1 %copy-start.26 = (bf16[256,256]{1,0:T(8,128)(2,1)S(1)}, bf16[256,256]{1,0:T(8,128)(2,1)}, u32[]{:S(2)}) copy-start(bf16[256,256]{1,0:T(8,128)(2,1)} %copy-done.25) | copy-start | bytes 393220
  114.3 9.1 %copy-start.29 = (f32[64,384]{1,0:T(8,128)S(1)}, f32[64,384]{1,0:T(8,128)}, u32[]{:S(2)}) copy-start(f32[64,384]{1,0:T(8,128)} %copy-done.28) | copy-start | bytes 294916
  114.3 9.1 %copy-start.31 = (f32[64,256]{1,0:T(8,128)S(1)}, f32[64,256]{1,0:T(8,128)}, u32[]{:S(2)}) copy-start(f32[64,256]{1,0:T(8,128)} %copy-done.30) | copy-start | bytes 196612
  114.3 9.1 %copy-start.33 = (f32[64,256]{1,0:T(8,128)S(1)}, f32[64,256]{1,0:T(8,128)}, u32[]{:S(2)}) copy-start(f32[64,256]{1,0:T(8,128)} %copy-done.32) | copy-start | bytes 196612
  114.3 9.1 %copy-start.35 = (f32[64,256]{1,0:T(8,128)S(1)}, f32[64,256]{1,0:T(8,128)}, u32[]{:S(2)}) copy-start(f32[64,256]{1,0:T(8,128)} %copy-done.34) | copy-start | bytes 196612
  114.3 9.1 %copy-start.37 = (f32[64,256]{1,0:T(8,128)S(1)}, f32[64,256]{1,0:T(8,128)}, u32[]{:S(2)}) copy-start(f32[64,256]{1,0:T(8,128)} %copy-done.36) | copy-start | bytes 196612
  114.4 9.1 %copy-start.39 = (f32[64,256]{1,0:T(8,128)S(1)}, f32[64,256]{1,0:T(8,128)}, u32[]{:S(2)}) copy-start(f32[64,256]{1,0:T(8,128)} %copy-done.38) | copy-start | bytes 196612
  114.4 9.1 %copy-start.40 = (s32[128,8]{0,1:T(8,128)S(1)}, s32[128,8]{0,1:T(8,128)}, u32[]{:S(2)}) copy-start(s32[128,8]{0,1:T(8,128)} %param.13) | copy-start | bytes 12292
  117.6 5.8 %collective-permute-start.19 = (f32[1,8,128]{2,1,0:T(8,128)S(1)}, f32[1,8,128]{2,1,0:T(8,128)S(1)}, u32[]{:S(2)}, u32[]{:S(2)}) collective-permute-start(f32[1,8,128]{2,1,0:T(8,128)S(1)} %get-tuple-element.89), channel_id=1, source_target_pairs={{0,15},{1,14},{2,13},{3,12},{4,11},{5,10},{6,9},{7,8},{8,7},{9,6},... | collective-permute-start | bytes 12296 | tf_op jit(solution)/shard_map/ppermute | solution.py:308
  (16 other events, 13.8 us)

commit v8 on v7

--- a/solution.py
+++ b/solution.py
@@ -2,7 +2,6 @@
 
 import jax
 import jax.numpy as jnp
-import numpy as np
 from jax import lax
 from jax.experimental import pallas as pl
 from jax.experimental.pallas import tpu as pltpu
@@ -36,13 +35,26 @@
     return grad, feature.reshape(docs_count, low_side.shape[1], high_side.shape[1])
 
 
-def rows_kernel(blocks, load, *refs):
-    order, sheet_in = refs[:2]
-    block_in = refs[2 : 2 + blocks]
-    given = refs[2 + blocks : 7 + blocks]
-    sheet, low_side, proj_cot = refs[7 + blocks : 10 + blocks]
+def block_owner(name, chips):
+    chain, step, handed = name
+    me = lax.axis_index("exp")
+    core, chip = lax.rem(me, 2), lax.div(me, 2)
+    turn = chips // 2
+    place = jnp.where(lax.rem(chip, 2) == 0, lax.div(chip, 2), chips - 1 - lax.div(chip, 2))
+    way = 2 * core - 1
+    place = place + (-way if handed else way) * step
+    place = lax.rem(place + chips, chips)
+    chip = jnp.where(place < turn, 2 * place, 2 * (chips - 1 - place) + 1)
+    return 2 * chip + (core if (chain == "a") != handed else 1 - core)
+
+
+def rows_kernel(names, load, *refs):
+    blocks = len(names)
+    sheet_in, block_in = refs[0], refs[1 : 1 + blocks]
+    given = refs[1 + blocks : 6 + blocks]
+    sheet, low_side, proj_cot = refs[6 + blocks : 9 + blocks]
     x_all, dy_all, low_sum, grad_sum = refs[-5:-1] if load else refs[-4:]
-    w_gate, w_up, w_down, low_proj, high_proj = refs[10 + blocks : 15 + blocks] if load else given
+    w_gate, w_up, w_down, low_proj, high_proj = refs[9 + blocks : 14 + blocks] if load else given
     rows = block_in[0].shape[0] // 2
     across = (((1,), (1,)), ((), ()))
     units = w_gate.shape[1]
@@ -97,20 +109,15 @@
     proj_cot[...] = lax.dot_general(
         high_proj[...], dy_all[...], across, preferred_element_type=jnp.float32
     )
-    own_lines = sheet.shape[0] == blocks
-    if not own_lines:
-        sheet[...] = sheet_in[...]
+    sheet[...] = sheet_in[...]
     for i in range(blocks):
         total = jnp.sum(
             jnp.transpose(grad_sum[i * rows : (i + 1) * rows, :]), axis=0, keepdims=True
         )
-        if own_lines:
-            sheet[i] = jnp.broadcast_to(total, sheet.shape[1:])
-        else:
-            sheet[order[i], 0:1, :] = total
-
-
-def work(order, sheet, block_in, weights, load=0, apart=False):
+        sheet[block_owner(names[i], sheet.shape[0] // 2), 0:1, :] = total
+
+
+def work(names, sheet, block_in, weights, load=0):
     width, units = weights[0].shape
     low_width, rank = weights[3].shape[0] * max(load, 1), weights[4].shape[0]
     blocks = len(block_in)
@@ -122,17 +129,15 @@
         shapes[3] = (low_width, units)
         loaded = [jax.ShapeDtypeStruct(shape, weights[0].dtype) for shape in shapes]
     tiles = units // 256 if units % 256 == 0 else 1
-    lines = (blocks if apart else sheet.shape[0],) + sheet.shape[1:]
     call = pl.pallas_call(
-        functools.partial(rows_kernel, blocks, load > 0),
+        functools.partial(rows_kernel, names, load > 0),
         out_shape=[
-            jax.ShapeDtypeStruct(lines, jnp.float32),
+            jax.ShapeDtypeStruct(sheet.shape, jnp.float32),
             jax.ShapeDtypeStruct((low_width, blocks * rows), jnp.bfloat16),
             jax.ShapeDtypeStruct((rank, blocks * rows), jnp.float32),
         ]
         + loaded,
-        in_specs=[pl.BlockSpec(memory_space=pltpu.SMEM)]
-        + [inside] * (1 + blocks)
+        in_specs=[inside] * (1 + blocks)
         + [pl.BlockSpec(memory_space=pl.ANY) if load else inside] * len(weights),
         out_specs=[inside] * (3 + len(loaded)),
         scratch_shapes=[
@@ -151,24 +156,21 @@
             transcendentals=blocks * rows * units,
         ),
     )
-    return call(order, sheet, *block_in, *weights)
-
-
-def outcome_kernel(pieces, order, source, returned, routes, *refs):
-    low_in, proj_in = refs[:pieces], refs[pieces : 2 * pieces]
-    late = refs[2 * pieces : -2]
+    return call(sheet, *block_in, *weights)
+
+
+def outcome_kernel(jobs, returned, routes, *refs):
+    low_in, proj_in = refs[: len(jobs)], refs[len(jobs) : 2 * len(jobs)]
     feat, route_grad = refs[-2:]
     rows = returned.shape[2]
     width, rank = low_in[0].shape[0], proj_in[0].shape[0]
     doc_of = lax.broadcasted_iota(jnp.int32, (width, rows), 0) // rank
     total = jnp.zeros(feat.shape, jnp.float32)
-    done = 0
-    for low_side, proj_cot in zip(low_in, proj_in):
+    for names, low_side, proj_cot in zip(jobs, low_in, proj_in):
         spread, high_side = [], []
-        for i in range(low_side.shape[1] // rows):
+        for i, name in enumerate(names):
             place = slice(i * rows, (i + 1) * rows)
-            owner = order[done]
-            done += 1
+            owner = block_owner(name, returned.shape[0] // 2)
             weight = returned[owner, 1:2, :]
             doc = returned[owner, 2:3, :].astype(jnp.int32)
             high_side.append((weight * proj_cot[:, place]).astype(jnp.bfloat16))
@@ -184,9 +186,6 @@
     picked = jnp.zeros(route_grad.shape, jnp.float32)
     for e in range(returned.shape[0]):
         picked = jnp.where(routes[...] == e, returned[e, 0:1, :], picked)
-    for i in range(len(late)):
-        sender = source[source.shape[0] - len(late) + i]
-        picked = jnp.where(routes[...] == sender, late[i][0, 0:1, :], picked)
     route_grad[...] = picked
 
 
@@ -237,32 +236,16 @@
         return lax.ppermute(block, "exp", across)
 
     arrivals = [(c, step) for step in range(1, half + 1) for c in ("ab" if step < half else "a")]
-    jobs = [[("a", 0, False), ("a", 0, True)]]
+    jobs = [(("a", 0, False), ("a", 0, True))]
     for i, (c, step) in enumerate(arrivals):
-        job = [(c, step, False)]
+        job = ((c, step, False),)
         if i > 0:
-            job.append(arrivals[i - 1] + (True,))
+            job += (arrivals[i - 1] + (True,),)
         if i == 1:
-            job.append(arrivals[0] + (False,))
+            job += (arrivals[0] + (False,),)
         if i != 0:
             jobs.append(job)
-    jobs.append([arrivals[-1] + (True,)])
-    blocks_of = [block for job in jobs for block in job]
-
-    orders = np.zeros((groups, 2 * groups), np.int32)
-    for place in range(chips):
-        for core in range(2):
-            me = 2 * ring[place] + core
-            for i, (c, step, handed) in enumerate(blocks_of):
-                first = core if (c == "a") != handed else 1 - core
-                way = (1 if core == 1 else -1) * (-1 if handed else 1)
-                owner = 2 * ring[(place + way * step) % chips] + first
-                orders[me, i] = owner
-                orders[owner, groups + i] = me
-    mine = lax.dynamic_index_in_dim(
-        jnp.asarray(orders), lax.axis_index("exp"), axis=0, keepdims=False
-    )
-    order, source = mine[:groups], mine[groups:]
+    jobs.append((arrivals[-1] + (True,),))
 
     rows, width = tokens.shape
     own = pl.pallas_call(
@@ -279,64 +262,50 @@
         out_shape=jax.ShapeDtypeStruct((groups, 8, rows), jnp.float32),
         in_specs=[pl.BlockSpec(memory_space=pltpu.VMEM)] * 3,
         out_specs=pl.BlockSpec(memory_space=pltpu.VMEM),
+        compiler_params=pltpu.CompilerParams(vmem_limit_bytes=8 * 1024 * 1024),
     )(routes.T, combine.T, doc_ids[None, :])
     inside = pl.BlockSpec(memory_space=pltpu.VMEM)
     given = (w_gate[0], w_up[0], w_down[0], proj_hidden[0].T, proj_output[0].T)
     weights = None
-    lows, projs, done = [], [], 0
+    lows, projs = [], []
     held = {("a", 0, False): own, ("a", 0, True): beside}
-
-    def take(apart=False):
-        nonlocal sheet, weights, done
-        job = jobs.pop(0)
-        share, blocks = order[done : done + len(job)], [held[name] for name in job]
+    todo = list(jobs)
+
+    def take():
+        nonlocal sheet, weights
+        names = todo.pop(0)
+        blocks = [held[name] for name in names]
         if weights is None:
-            lines, low_side, proj_cot, *weights = work(
-                share, sheet, blocks, given, load=docs_count
+            sheet, low_side, proj_cot, *weights = work(
+                names, sheet, blocks, given, load=docs_count
             )
         else:
-            lines, low_side, proj_cot = work(share, sheet, blocks, weights, apart=apart)
+            sheet, low_side, proj_cot = work(names, sheet, blocks, weights)
         lows.append(low_side)
         projs.append(proj_cot)
-        done += len(job)
-        if not apart:
-            sheet = lines
-            return low_side
-        for i in range(len(job)):
-            spot = done - len(job) + i
-            back = [(d, int(orders[d, spot])) for d in range(groups)]
-            late.append(lax.ppermute(lines[i : i + 1], "exp", back))
-        return low_side
-
-    def tie(one, other):
-        return lax.optimization_barrier((one, other))
-
-    late = []
+
     chain = {"a": own, "b": beside}
     for i, (c, step) in enumerate(arrivals):
         block = hop(chain[c])
         if i != 1:
-            lows[-1:], block = tie([take(apart=i == len(arrivals) - 1)], block)
-        if i == len(arrivals) - 1:
-            returned, block = tie(returned, block)
+            take()
+            sheet, block = lax.optimization_barrier((sheet, block))
         chain[c] = held[(c, step, False)] = block
         held[(c, step, True)] = swap(block)
-        if i == len(arrivals) - 2:
-            returned = lax.all_to_all(sheet, "exp", split_axis=0, concat_axis=0, tiled=True)
-    while jobs:
-        take(apart=True)
+    while todo:
+        take()
+    returned = lax.all_to_all(sheet, "exp", split_axis=0, concat_axis=0, tiled=True)
     rank = proj_output.shape[2]
     feature, route_grad = pl.pallas_call(
-        functools.partial(outcome_kernel, len(lows)),
+        functools.partial(outcome_kernel, jobs),
         out_shape=[
             jax.ShapeDtypeStruct((docs_count * rank, rank), jnp.float32),
             jax.ShapeDtypeStruct((chosen, tok_rows), jnp.float32),
         ],
-        in_specs=[pl.BlockSpec(memory_space=pltpu.SMEM)] * 2
-        + [inside] * (2 + 2 * len(lows) + len(late)),
+        in_specs=[inside] * (2 + 2 * len(lows)),
         out_specs=[inside] * 2,
         compiler_params=pltpu.CompilerParams(vmem_limit_bytes=16 * 1024 * 1024),
-    )(order, source, returned, routes.T, *lows, *projs, *late)
+    )(returned, routes.T, *lows, *projs)
     return feature.reshape(docs_count, 1, rank, rank), route_grad.T
 
 

time: 126 us -> 107 us (0.85)
  local copies, waits for them, and re-layouts: 21.8 us -> 5.09 us
  starting transfers between devices: 30.4 us -> 15 us
  blocking collectives: 0 us -> 13.3 us
  waiting for transfers between devices: 27.4 us -> 38.9 us
  Pallas kernels: 44.8 us -> 33.5 us
    ppermute x7, waiting for transfers between devices: 21.7 us -> 38.9 us  [hop(): return lax.ppermute(block, 'exp', onward)]
    unnamed x86 -> x14, local copies, waits for them, and re-layouts: 19.6 us -> 5.09 us
    all_to_all x0 -> x1, blocking collectives: none -> 13.3 us  [by_ring(): lax.all_to_all(sheet, 'exp', split_axis=0, concat_axis=0, tiled=True)]
    pallas_call x9, Pallas kernels: 41.2 us -> 31.3 us  [the longest x8 30.2 us: work(): return call(sheet, *block_in, *weights)]
    ppermute x5 -> x0, starting transfers between devices: 8.59 us -> none  [take(): late.append(lax.ppermute(lines[i:i + 1], 'exp', back))]
    all_to_all x1 -> x0, starting transfers between devices: 6.6 us -> none  [by_ring(): lax.all_to_all(sheet, 'exp', split_axis=0, concat_axis=0, tiled=True)]
    ppermute x5 -> x0, waiting for transfers between devices: 5.63 us -> none  [take(): late.append(lax.ppermute(lines[i:i + 1], 'exp', back))]
    slice x6 -> x0, local copies, waits for them, and re-layouts: 1.49 us -> none  [the longest x3 1.41 us: take(): share, blocks = (order[done:done + len(job)], [held[name] for name in job])]
  transfers between devices with their start and end apart: 21 -> 15, of which waited for: 7 -> 6; matrix products, arithmetic and copies ran while one was open for 2% -> 0% of each run, Pallas kernels for 32% -> 26%
where the time goes in v8:
time: 107 us
  waiting for transfers between devices  38.9 us (36%)
  Pallas kernels  33.5 us (31%)
  starting transfers between devices  15 us (14%)
  blocking collectives  13.3 us (12%)
  local copies, waits for them, and re-layouts  5.09 us (5%)
    ppermute x7, waiting for transfers between devices, hop(): return lax.ppermute(block, 'exp', onward)  38.9 us
    pallas_call x8, Pallas kernels, work(): return call(sheet, *block_in, *weights)  30.2 us
    ppermute x7, starting transfers between devices, hop(): return lax.ppermute(block, 'exp', onward)  14.4 us
    all_to_all x1, blocking collectives, by_ring(): lax.all_to_all(sheet, 'exp', split_axis=0, concat_axis=0, tiled=True)  13.3 us
    unnamed x14, local copies, waits for them, and re-layouts  5.09 us
    pallas_call x1, Pallas kernels, by_ring(): pl.pallas_call(stack_kernel, out_shape=jax.ShapeDtypeStruct((2 * rows, wi...  2.2 us
  transfers between devices with their start and end apart: 15, of which 6 were waited for; matrix products, arithmetic and copies ran while one was open for 0% of the time, Pallas kernels for 26%

profile of v8, /device:TPU:0, one launch (start us, length us, event | category | flops | bytes accessed | tf_op | source)
XLA Modules:
  0.0 106.5 jit_solution(5426582762574601725)
XLA Ops:
  0.6 2.2 %shard_map.114.refs_1_ = bf16[256,2048]{1,0:T(8,128)(2,1)} custom-call(bf16[128,2048]{1,0:T(8,128)(2,1)} %top.1, bf16[128,2048]{1,0:T(8,128)(2,1)} %bottom.1), custom_call_target="tpu_custom_call" | custom-call | tf_op jit(solution)/shard_map/pallas_call | solution.py:251
  2.8 0.5 collective-permute-start
  3.4 2.6 %collective-permute-start.1 = (bf16[256,2048]{1,0:T(8,128)(2,1)}, bf16[256,2048]{1,0:T(8,128)(2,1)S(1)}, u32[]{:S(2)}, u32[]{:S(2)}) collective-permute-start(bf16[256,2048]{1,0:T(8,128)(2,1)} %shard_map.114.refs_1_), channel_id=1, source_target_pairs={{0,4},{1,3},{4,8},{5,1},{8,12},{9,5},{12,14},{13,9},{14,10},{15,13... | collective-permute-start | bytes 3145736 | tf_op jit(solution)/shard_map/ppermute | solution.py:233
  6.0 0.7 copy-done.3
  6.7 0.7 copy-done.5
  7.4 0.7 copy-done.6
  8.0 0.0 collective-permute-done.refs_2_
  8.1 1.6 %collective-permute-start.2 = (bf16[256,2048]{1,0:T(8,128)(2,1)S(1)}, bf16[256,2048]{1,0:T(8,128)(2,1)S(1)}, u32[]{:S(2)}, u32[]{:S(2)}) collective-permute-start(bf16[256,2048]{1,0:T(8,128)(2,1)S(1)} %collective-permute-done.refs_2_), channel_id=1, source_target_pairs={{0,4},{1,3},{4,8},{5,1},{8,12},{9,5},{12,14},{13,9},{14,10},{15,13... | collective-permute-start | bytes 3145736 | tf_op jit(solution)/shard_map/ppermute | solution.py:233
  9.7 1.2 %copy-done = bf16[256,2048]{1,0:T(8,128)(2,1)S(1)} copy-done((bf16[256,2048]{1,0:T(8,128)(2,1)S(1)}, bf16[256,2048]{1,0:T(8,128)(2,1)}, u32[]{:S(2)}) %copy-start) | copy-done | bytes 1048600
  10.9 0.9 copy-done.1
  11.9 0.9 copy-done.2
  12.8 6.5 %shard_map.115 = (f32[16,8,128]{2,1,0:T(8,128)S(1)}, bf16[256,256]{1,0:T(8,128)(2,1)S(1)}, f32[64,256]{1,0:T(8,128)S(1)}, bf16[2048,768]{1,0:T(8,128)(2,1)S(1)},...) custom-call(f32[16,8,128]{2,1,0:T(8,128)S(1)} %shard_map.113.refs_0_, ...), custom_call_target="tpu_custom_call" | custom-call | flops 2415919104 | bytes 2097152 | tf_op jit(solution)/shard_map/pallas_call | solution.py:159
  19.2 0.0 collective-permute-done.1.refs_3_
  19.2 0.1 collective-permute-start.3
  19.3 1.7 %collective-permute-start.4 = (bf16[256,2048]{1,0:T(8,128)(2,1)S(1)}, bf16[256,2048]{1,0:T(8,128)(2,1)S(1)}, u32[]{:S(2)}, u32[]{:S(2)}) collective-permute-start(bf16[256,2048]{1,0:T(8,128)(2,1)S(1)} %collective-permute-done.1.refs_3_), channel_id=1, source_target_pairs={{0,4},{1,3},{4,8},{5,1},{8,12},{9,5},{12,14},{13,9},{14,10},{15,13... | collective-permute-start | bytes 3145736 | tf_op jit(solution)/shard_map/ppermute | solution.py:233
  21.0 9.1 %collective-permute-done.2.refs_1_ = bf16[256,2048]{1,0:T(8,128)(2,1)S(1)} collective-permute-done((bf16[256,2048]{1,0:T(8,128)(2,1)S(1)}, bf16[256,2048]{1,0:T(8,128)(2,1)S(1)}, u32[]{:S(2)}, u32[]{:S(2)}) %collective-permute-start.2) | collective-permute-done | bytes 1048608 | tf_op jit(solution)/shard_map/ppermute | solution.py:233
  30.1 0.0 collective-permute-start.5
  30.1 2.1 %collective-permute-start.6 = (bf16[256,2048]{1,0:T(8,128)(2,1)S(1)}, bf16[256,2048]{1,0:T(8,128)(2,1)S(1)}, u32[]{:S(2)}, u32[]{:S(2)}) collective-permute-start(bf16[256,2048]{1,0:T(8,128)(2,1)S(1)} %collective-permute-done.2.refs_1_), channel_id=1, source_target_pairs={{0,4},{1,3},{4,8},{5,1},{8,12},{9,5},{12,14},{13,9},{14,10},{15,13... | collective-permute-start | bytes 3145736 | tf_op jit(solution)/shard_map/ppermute | solution.py:233
  32.2 0.0 collective-permute-done.3.refs_2_
  32.2 4.6 %shard_map.116 = (f32[16,8,128]{2,1,0:T(8,128)S(1)}, bf16[256,384]{1,0:T(8,128)(2,1)S(1)}, f32[64,384]{1,0:T(8,128)S(1)}) custom-call(f32[16,8,128]{2,1,0:T(8,128)S(1)} %get-tuple-element.46.refs_0_, bf16[256,2048]{1,0:T(8,128)(2,1)S(1)} %collective-permute-done.2.refs_1_, bf16[256,2048]{1,0:T(8,128)(2,1)S(1)} %collective-permute-done.3.refs_2_, ...), custom_call_target="tpu_custom_call" | custom-call | flops 3623878656 | bytes 3145728 | tf_op jit(solution)/shard_map/pallas_call | solution.py:159
  36.9 4.5 %collective-permute-done.4.refs_1_ = bf16[256,2048]{1,0:T(8,128)(2,1)S(1)} collective-permute-done((bf16[256,2048]{1,0:T(8,128)(2,1)S(1)}, bf16[256,2048]{1,0:T(8,128)(2,1)S(1)}, u32[]{:S(2)}, u32[]{:S(2)}) %collective-permute-start.4) | collective-permute-done | bytes 1048608 | tf_op jit(solution)/shard_map/ppermute | solution.py:233
  41.4 0.0 collective-permute-start.7
  41.4 2.1 %collective-permute-start.8 = (bf16[256,2048]{1,0:T(8,128)(2,1)S(1)}, bf16[256,2048]{1,0:T(8,128)(2,1)S(1)}, u32[]{:S(2)}, u32[]{:S(2)}) collective-permute-start(bf16[256,2048]{1,0:T(8,128)(2,1)S(1)} %collective-permute-done.4.refs_1_), channel_id=1, source_target_pairs={{0,4},{1,3},{4,8},{5,1},{8,12},{9,5},{12,14},{13,9},{14,10},{15,13... | collective-permute-start | bytes 3145736 | tf_op jit(solution)/shard_map/ppermute | solution.py:233
  43.5 0.0 collective-permute-done.5.refs_2_
  43.5 3.3 %shard_map.117 = (f32[16,8,128]{2,1,0:T(8,128)S(1)}, bf16[256,256]{1,0:T(8,128)(2,1)S(1)}, f32[64,256]{1,0:T(8,128)S(1)}) custom-call(f32[16,8,128]{2,1,0:T(8,128)S(1)} %get-tuple-element.54.refs_0_, bf16[256,2048]{1,0:T(8,128)(2,1)S(1)} %collective-permute-done.4.refs_1_, bf16[256,2048]{1,0:T(8,128)(2,1)S(1)} %collective-permute-done.5.refs_2_, ...), custom_call_target="tpu_custom_call" | custom-call | flops 2415919104 | bytes 2097152 | tf_op jit(solution)/shard_map/pallas_call | solution.py:159
  46.8 5.8 %collective-permute-done.6.refs_1_ = bf16[256,2048]{1,0:T(8,128)(2,1)S(1)} collective-permute-done((bf16[256,2048]{1,0:T(8,128)(2,1)S(1)}, bf16[256,2048]{1,0:T(8,128)(2,1)S(1)}, u32[]{:S(2)}, u32[]{:S(2)}) %collective-permute-start.6) | collective-permute-done | bytes 1048608 | tf_op jit(solution)/shard_map/ppermute | solution.py:233
  52.6 0.0 collective-permute-start.9
  52.6 2.1 %collective-permute-start.10 = (bf16[256,2048]{1,0:T(8,128)(2,1)S(1)}, bf16[256,2048]{1,0:T(8,128)(2,1)S(1)}, u32[]{:S(2)}, u32[]{:S(2)}) collective-permute-start(bf16[256,2048]{1,0:T(8,128)(2,1)S(1)} %collective-permute-done.6.refs_1_), channel_id=1, source_target_pairs={{0,4},{1,3},{4,8},{5,1},{8,12},{9,5},{12,14},{13,9},{14,10},{15,13... | collective-permute-start | bytes 3145736 | tf_op jit(solution)/shard_map/ppermute | solution.py:233
  54.7 0.0 collective-permute-done.7.refs_2_
  54.7 3.3 %shard_map.118 = (f32[16,8,128]{2,1,0:T(8,128)S(1)}, bf16[256,256]{1,0:T(8,128)(2,1)S(1)}, f32[64,256]{1,0:T(8,128)S(1)}) custom-call(f32[16,8,128]{2,1,0:T(8,128)S(1)} %get-tuple-element.57.refs_0_, bf16[256,2048]{1,0:T(8,128)(2,1)S(1)} %collective-permute-done.6.refs_1_, bf16[256,2048]{1,0:T(8,128)(2,1)S(1)} %collective-permute-done.7.refs_2_, ...), custom_call_target="tpu_custom_call" | custom-call | flops 2415919104 | bytes 2097152 | tf_op jit(solution)/shard_map/pallas_call | solution.py:159
  58.0 5.8 %collective-permute-done.8.refs_1_ = bf16[256,2048]{1,0:T(8,128)(2,1)S(1)} collective-permute-done((bf16[256,2048]{1,0:T(8,128)(2,1)S(1)}, bf16[256,2048]{1,0:T(8,128)(2,1)S(1)}, u32[]{:S(2)}, u32[]{:S(2)}) %collective-permute-start.8) | collective-permute-done | bytes 1048608 | tf_op jit(solution)/shard_map/ppermute | solution.py:233
  63.8 0.0 collective-permute-start.11
  63.8 2.1 %collective-permute-start.12 = (bf16[256,2048]{1,0:T(8,128)(2,1)S(1)}, bf16[256,2048]{1,0:T(8,128)(2,1)S(1)}, u32[]{:S(2)}, u32[]{:S(2)}) collective-permute-start(bf16[256,2048]{1,0:T(8,128)(2,1)S(1)} %collective-permute-done.8.refs_1_), channel_id=1, source_target_pairs={{0,4},{1,3},{4,8},{5,1},{8,12},{9,5},{12,14},{13,9},{14,10},{15,13... | collective-permute-start | bytes 3145736 | tf_op jit(solution)/shard_map/ppermute | solution.py:233
  66.0 0.0 collective-permute-done.9.refs_2_
  66.0 3.3 %shard_map.119 = (f32[16,8,128]{2,1,0:T(8,128)S(1)}, bf16[256,256]{1,0:T(8,128)(2,1)S(1)}, f32[64,256]{1,0:T(8,128)S(1)}) custom-call(f32[16,8,128]{2,1,0:T(8,128)S(1)} %get-tuple-element.60.refs_0_, bf16[256,2048]{1,0:T(8,128)(2,1)S(1)} %collective-permute-done.8.refs_1_, bf16[256,2048]{1,0:T(8,128)(2,1)S(1)} %collective-permute-done.9.refs_2_, ...), custom_call_target="tpu_custom_call" | custom-call | flops 2415919104 | bytes 2097152 | tf_op jit(solution)/shard_map/pallas_call | solution.py:159
  69.3 5.8 %collective-permute-done.10.refs_1_ = bf16[256,2048]{1,0:T(8,128)(2,1)S(1)} collective-permute-done((bf16[256,2048]{1,0:T(8,128)(2,1)S(1)}, bf16[256,2048]{1,0:T(8,128)(2,1)S(1)}, u32[]{:S(2)}, u32[]{:S(2)}) %collective-permute-start.10) | collective-permute-done | bytes 1048608 | tf_op jit(solution)/shard_map/ppermute | solution.py:233
  75.1 0.0 collective-permute-start.13
  75.1 0.0 collective-permute-done.11.refs_2_
  75.1 3.3 %shard_map.120 = (f32[16,8,128]{2,1,0:T(8,128)S(1)}, bf16[256,256]{1,0:T(8,128)(2,1)S(1)}, f32[64,256]{1,0:T(8,128)S(1)}) custom-call(f32[16,8,128]{2,1,0:T(8,128)S(1)} %get-tuple-element.63.refs_0_, bf16[256,2048]{1,0:T(8,128)(2,1)S(1)} %collective-permute-done.10.refs_1_, bf16[256,2048]{1,0:T(8,128)(2,1)S(1)} %collective-permute-done.11.refs_2_, ...), custom_call_target="tpu_custom_call" | custom-call | flops 2415919104 | bytes 2097152 | tf_op jit(solution)/shard_map/pallas_call | solution.py:159
  78.4 7.9 %collective-permute-done.12.refs_1_ = bf16[256,2048]{1,0:T(8,128)(2,1)S(1)} collective-permute-done((bf16[256,2048]{1,0:T(8,128)(2,1)S(1)}, bf16[256,2048]{1,0:T(8,128)(2,1)S(1)}, u32[]{:S(2)}, u32[]{:S(2)}) %collective-permute-start.12) | collective-permute-done | bytes 1048608 | tf_op jit(solution)/shard_map/ppermute | solution.py:233
  86.3 0.0 collective-permute-start.14
  86.3 0.0 collective-permute-done.13.refs_2_
  86.3 3.3 %shard_map.121 = (f32[16,8,128]{2,1,0:T(8,128)S(1)}, bf16[256,256]{1,0:T(8,128)(2,1)S(1)}, f32[64,256]{1,0:T(8,128)S(1)}) custom-call(f32[16,8,128]{2,1,0:T(8,128)S(1)} %get-tuple-element.66.refs_0_, bf16[256,2048]{1,0:T(8,128)(2,1)S(1)} %collective-permute-done.12.refs_1_, bf16[256,2048]{1,0:T(8,128)(2,1)S(1)} %collective-permute-done.13.refs_2_, ...), custom_call_target="tpu_custom_call" | custom-call | flops 2415919104 | bytes 2097152 | tf_op jit(solution)/shard_map/pallas_call | solution.py:159
  89.7 0.0 collective-permute-done.14.refs_1_
  89.7 0.0 copy-start.4
  89.7 2.4 %shard_map.122 = (f32[16,8,128]{2,1,0:T(8,128)S(1)}, bf16[256,128]{1,0:T(8,128)(2,1)S(1)}, f32[64,128]{1,0:T(8,128)S(1)}) custom-call(f32[16,8,128]{2,1,0:T(8,128)S(1)} %get-tuple-element.68.refs_0_, bf16[256,2048]{1,0:T(8,128)(2,1)S(1)} %collective-permute-done.14.refs_1_, bf16[2048,768]{1,0:T(8,128)(2,1)S(1)} %get-tuple-element.48.refs_4_.refs_3_.refs_2_, ...), custom_call_target="tpu_custom_call" | custom-call | flops 1207959552 | bytes 1048576 | tf_op jit(solution)/shard_map/pallas_call | solution.py:159
  92.1 13.3 %all_to_all.5.returned = f32[16,8,128]{2,1,0:T(8,128)S(1)} all-to-all(f32[16,8,128]{2,1,0:T(8,128)S(1)} %get-tuple-element.69), channel_id=1, replica_groups=mesh['grp'=2,'exp'=16] {'exp'}, dimensions={0} | all-to-all | bytes 131072 | tf_op jit(solution)/shard_map/all_to_all | solution.py:297
  105.4 1.1 %shard_map.123 = (f32[256,64]{1,0:T(8,128)}, f32[8,128]{1,0:T(8,128)}) custom-call(f32[16,8,128]{2,1,0:T(8,128)S(1)} %all_to_all.5.returned, s32[8,128]{1,0:T(8,128)S(1)} %bitcast.19, bf16[256,256]{1,0:T(8,128)(2,1)S(1)} %get-tuple-element.70.refs_0_, bf16[256,384]{1,0:T(8,128)(2,1)S(1)} %get-tuple-element.71.refs_1_, ...), custom_call_target="tpu_custom_call" | custom-call | tf_op jit(solution)/shard_map/pallas_call | solution.py:299
  (8 shorter events, 0.0 us)
Async XLA Ops:
  2.8 5.2 %collective-permute-start = (bf16[256,2048]{1,0:T(8,128)(2,1)}, bf16[256,2048]{1,0:T(8,128)(2,1)S(1)}, u32[]{:S(2)}, u32[]{:S(2)}) collective-permute-start(bf16[256,2048]{1,0:T(8,128)(2,1)} %shard_map.114.refs_1_), channel_id=1, source_target_pairs={{0,1},{1,0},{2,3},{3,2},{4,5},{5,4},{6,7},{7,6},{8,9},{9,8},{10,11... | collective-permute-start | bytes 3145736 | tf_op jit(solution)/shard_map/ppermute | solution.py:236
  3.4 15.9 %collective-permute-start.1 = (bf16[256,2048]{1,0:T(8,128)(2,1)}, bf16[256,2048]{1,0:T(8,128)(2,1)S(1)}, u32[]{:S(2)}, u32[]{:S(2)}) collective-permute-start(bf16[256,2048]{1,0:T(8,128)(2,1)} %shard_map.114.refs_1_), channel_id=1, source_target_pairs={{0,4},{1,3},{4,8},{5,1},{8,12},{9,5},{12,14},{13,9},{14,10},{15,13... | collective-permute-start | bytes 3145736 | tf_op jit(solution)/shard_map/ppermute | solution.py:233
  6.0 0.7 copy-start.3
  6.7 0.7 copy-start.5
  7.4 0.7 copy-start.6
  8.1 22.1 %collective-permute-start.2 = (bf16[256,2048]{1,0:T(8,128)(2,1)S(1)}, bf16[256,2048]{1,0:T(8,128)(2,1)S(1)}, u32[]{:S(2)}, u32[]{:S(2)}) collective-permute-start(bf16[256,2048]{1,0:T(8,128)(2,1)S(1)} %collective-permute-done.refs_2_), channel_id=1, source_target_pairs={{0,4},{1,3},{4,8},{5,1},{8,12},{9,5},{12,14},{13,9},{14,10},{15,13... | collective-permute-start | bytes 3145736 | tf_op jit(solution)/shard_map/ppermute | solution.py:233
  9.7 1.2 %copy-start = (bf16[256,2048]{1,0:T(8,128)(2,1)S(1)}, bf16[256,2048]{1,0:T(8,128)(2,1)}, u32[]{:S(2)}) copy-start(bf16[256,2048]{1,0:T(8,128)(2,1)} %shard_map.114.refs_1_) | copy-start | bytes 3145732
  10.9 0.9 copy-start.1
  11.9 0.9 copy-start.2
  19.2 13.0 %collective-permute-start.3 = (bf16[256,2048]{1,0:T(8,128)(2,1)S(1)}, bf16[256,2048]{1,0:T(8,128)(2,1)S(1)}, u32[]{:S(2)}, u32[]{:S(2)}) collective-permute-start(bf16[256,2048]{1,0:T(8,128)(2,1)S(1)} %collective-permute-done.1.refs_3_), channel_id=1, source_target_pairs={{0,1},{1,0},{2,3},{3,2},{4,5},{5,4},{6,7},{7,6},{8,9},{9,8},{10,11... | collective-permute-start | bytes 3145736 | tf_op jit(solution)/shard_map/ppermute | solution.py:236
  19.3 22.1 %collective-permute-start.4 = (bf16[256,2048]{1,0:T(8,128)(2,1)S(1)}, bf16[256,2048]{1,0:T(8,128)(2,1)S(1)}, u32[]{:S(2)}, u32[]{:S(2)}) collective-permute-start(bf16[256,2048]{1,0:T(8,128)(2,1)S(1)} %collective-permute-done.1.refs_3_), channel_id=1, source_target_pairs={{0,4},{1,3},{4,8},{5,1},{8,12},{9,5},{12,14},{13,9},{14,10},{15,13... | collective-permute-start | bytes 3145736 | tf_op jit(solution)/shard_map/ppermute | solution.py:233
  30.1 13.3 %collective-permute-start.5 = (bf16[256,2048]{1,0:T(8,128)(2,1)S(1)}, bf16[256,2048]{1,0:T(8,128)(2,1)S(1)}, u32[]{:S(2)}, u32[]{:S(2)}) collective-permute-start(bf16[256,2048]{1,0:T(8,128)(2,1)S(1)} %collective-permute-done.2.refs_1_), channel_id=1, source_target_pairs={{0,1},{1,0},{2,3},{3,2},{4,5},{5,4},{6,7},{7,6},{8,9},{9,8},{10,11... | collective-permute-start | bytes 3145736 | tf_op jit(solution)/shard_map/ppermute | solution.py:236
  30.1 22.5 %collective-permute-start.6 = (bf16[256,2048]{1,0:T(8,128)(2,1)S(1)}, bf16[256,2048]{1,0:T(8,128)(2,1)S(1)}, u32[]{:S(2)}, u32[]{:S(2)}) collective-permute-start(bf16[256,2048]{1,0:T(8,128)(2,1)S(1)} %collective-permute-done.2.refs_1_), channel_id=1, source_target_pairs={{0,4},{1,3},{4,8},{5,1},{8,12},{9,5},{12,14},{13,9},{14,10},{15,13... | collective-permute-start | bytes 3145736 | tf_op jit(solution)/shard_map/ppermute | solution.py:233
  41.4 13.3 %collective-permute-start.7 = (bf16[256,2048]{1,0:T(8,128)(2,1)S(1)}, bf16[256,2048]{1,0:T(8,128)(2,1)S(1)}, u32[]{:S(2)}, u32[]{:S(2)}) collective-permute-start(bf16[256,2048]{1,0:T(8,128)(2,1)S(1)} %collective-permute-done.4.refs_1_), channel_id=1, source_target_pairs={{0,1},{1,0},{2,3},{3,2},{4,5},{5,4},{6,7},{7,6},{8,9},{9,8},{10,11... | collective-permute-start | bytes 3145736 | tf_op jit(solution)/shard_map/ppermute | solution.py:236
  41.4 22.5 %collective-permute-start.8 = (bf16[256,2048]{1,0:T(8,128)(2,1)S(1)}, bf16[256,2048]{1,0:T(8,128)(2,1)S(1)}, u32[]{:S(2)}, u32[]{:S(2)}) collective-permute-start(bf16[256,2048]{1,0:T(8,128)(2,1)S(1)} %collective-permute-done.4.refs_1_), channel_id=1, source_target_pairs={{0,4},{1,3},{4,8},{5,1},{8,12},{9,5},{12,14},{13,9},{14,10},{15,13... | collective-permute-start | bytes 3145736 | tf_op jit(solution)/shard_map/ppermute | solution.py:233
  52.6 13.3 %collective-permute-start.9 = (bf16[256,2048]{1,0:T(8,128)(2,1)S(1)}, bf16[256,2048]{1,0:T(8,128)(2,1)S(1)}, u32[]{:S(2)}, u32[]{:S(2)}) collective-permute-start(bf16[256,2048]{1,0:T(8,128)(2,1)S(1)} %collective-permute-done.6.refs_1_), channel_id=1, source_target_pairs={{0,1},{1,0},{2,3},{3,2},{4,5},{5,4},{6,7},{7,6},{8,9},{9,8},{10,11... | collective-permute-start | bytes 3145736 | tf_op jit(solution)/shard_map/ppermute | solution.py:236
  52.6 22.5 %collective-permute-start.10 = (bf16[256,2048]{1,0:T(8,128)(2,1)S(1)}, bf16[256,2048]{1,0:T(8,128)(2,1)S(1)}, u32[]{:S(2)}, u32[]{:S(2)}) collective-permute-start(bf16[256,2048]{1,0:T(8,128)(2,1)S(1)} %collective-permute-done.6.refs_1_), channel_id=1, source_target_pairs={{0,4},{1,3},{4,8},{5,1},{8,12},{9,5},{12,14},{13,9},{14,10},{15,13... | collective-permute-start | bytes 3145736 | tf_op jit(solution)/shard_map/ppermute | solution.py:233
  63.8 11.2 %collective-permute-start.11 = (bf16[256,2048]{1,0:T(8,128)(2,1)S(1)}, bf16[256,2048]{1,0:T(8,128)(2,1)S(1)}, u32[]{:S(2)}, u32[]{:S(2)}) collective-permute-start(bf16[256,2048]{1,0:T(8,128)(2,1)S(1)} %collective-permute-done.8.refs_1_), channel_id=1, source_target_pairs={{0,1},{1,0},{2,3},{3,2},{4,5},{5,4},{6,7},{7,6},{8,9},{9,8},{10,11... | collective-permute-start | bytes 3145736 | tf_op jit(solution)/shard_map/ppermute | solution.py:236
  63.8 22.5 %collective-permute-start.12 = (bf16[256,2048]{1,0:T(8,128)(2,1)S(1)}, bf16[256,2048]{1,0:T(8,128)(2,1)S(1)}, u32[]{:S(2)}, u32[]{:S(2)}) collective-permute-start(bf16[256,2048]{1,0:T(8,128)(2,1)S(1)} %collective-permute-done.8.refs_1_), channel_id=1, source_target_pairs={{0,4},{1,3},{4,8},{5,1},{8,12},{9,5},{12,14},{13,9},{14,10},{15,13... | collective-permute-start | bytes 3145736 | tf_op jit(solution)/shard_map/ppermute | solution.py:233
  75.1 11.2 %collective-permute-start.13 = (bf16[256,2048]{1,0:T(8,128)(2,1)S(1)}, bf16[256,2048]{1,0:T(8,128)(2,1)S(1)}, u32[]{:S(2)}, u32[]{:S(2)}) collective-permute-start(bf16[256,2048]{1,0:T(8,128)(2,1)S(1)} %collective-permute-done.10.refs_1_), channel_id=1, source_target_pairs={{0,1},{1,0},{2,3},{3,2},{4,5},{5,4},{6,7},{7,6},{8,9},{9,8},{10,11... | collective-permute-start | bytes 3145736 | tf_op jit(solution)/shard_map/ppermute | solution.py:236
  86.3 3.3 %collective-permute-start.14 = (bf16[256,2048]{1,0:T(8,128)(2,1)S(1)}, bf16[256,2048]{1,0:T(8,128)(2,1)S(1)}, u32[]{:S(2)}, u32[]{:S(2)}) collective-permute-start(bf16[256,2048]{1,0:T(8,128)(2,1)S(1)} %collective-permute-done.12.refs_1_), channel_id=1, source_target_pairs={{0,1},{1,0},{2,3},{3,2},{4,5},{5,4},{6,7},{7,6},{8,9},{9,8},{10,11... | collective-permute-start | bytes 3145736 | tf_op jit(solution)/shard_map/ppermute | solution.py:236
  89.7 15.7 %copy-start.4 = (s32[128,8]{0,1:T(8,128)S(1)}, s32[128,8]{0,1:T(8,128)}, u32[]{:S(2)}) copy-start(s32[128,8]{0,1:T(8,128)} %param.12) | copy-start | bytes 12292

commit v9 on v8

--- a/solution.py
+++ b/solution.py
@@ -50,12 +50,15 @@
 
 def rows_kernel(names, load, *refs):
     blocks = len(names)
-    sheet_in, block_in = refs[0], refs[1 : 1 + blocks]
-    given = refs[1 + blocks : 6 + blocks]
-    sheet, low_side, proj_cot = refs[6 + blocks : 9 + blocks]
+    apart = refs[1:3] if load else ()
+    refs = refs[:1] + refs[3:] if load else refs
+    whole = blocks - 1 if load else blocks
+    sheet_in, block_in = refs[0], refs[1 : 1 + whole]
+    given = refs[1 + whole : 6 + whole]
+    sheet, low_side, proj_cot = refs[6 + whole : 9 + whole]
     x_all, dy_all, low_sum, grad_sum = refs[-5:-1] if load else refs[-4:]
-    w_gate, w_up, w_down, low_proj, high_proj = refs[9 + blocks : 14 + blocks] if load else given
-    rows = block_in[0].shape[0] // 2
+    w_gate, w_up, w_down, low_proj, high_proj = refs[9 + whole : 14 + whole] if load else given
+    rows = x_all.shape[0] // blocks
     across = (((1,), (1,)), ((), ()))
     units = w_gate.shape[1]
     tile = 256 if units % 256 == 0 else units
@@ -72,14 +75,17 @@
         for i in range(low_proj.shape[0] // rank):
             copies.append((given[3], low_proj.at[pl.ds(i * rank, rank), :]))
         copies.append((given[4], high_proj))
+        copies.append((apart[0], x_all.at[:rows]))
+        copies.append((apart[1], dy_all.at[:rows]))
         copies = [
             pltpu.make_async_copy(src, dst, refs[-1].at[i]) for i, (src, dst) in enumerate(copies)
         ]
         for copy in copies[3 * tiles :] + copies[: 3 * tiles]:
             copy.start()
-    for i in range(blocks):
-        x_all[i * rows : (i + 1) * rows, :] = block_in[i][:rows, :]
-        dy_all[i * rows : (i + 1) * rows, :] = block_in[i][rows:, :]
+    for i, block in enumerate(block_in):
+        place = slice((blocks - whole + i) * rows, (blocks - whole + i + 1) * rows)
+        x_all[place, :] = block[:rows, :]
+        dy_all[place, :] = block[rows:, :]
     low_sum[...] = jnp.zeros_like(low_sum)
     grad_sum[...] = jnp.zeros_like(grad_sum)
 
@@ -117,10 +123,10 @@
         sheet[block_owner(names[i], sheet.shape[0] // 2), 0:1, :] = total
 
 
-def work(names, sheet, block_in, weights, load=0):
+def work(names, sheet, block_in, weights, apart=(), load=0):
     width, units = weights[0].shape
     low_width, rank = weights[3].shape[0] * max(load, 1), weights[4].shape[0]
-    blocks = len(block_in)
+    blocks = len(names)
     rows = block_in[0].shape[0] // 2
     inside = pl.BlockSpec(memory_space=pltpu.VMEM)
     loaded = []
@@ -137,7 +143,9 @@
             jax.ShapeDtypeStruct((rank, blocks * rows), jnp.float32),
         ]
         + loaded,
-        in_specs=[inside] * (1 + blocks)
+        in_specs=[inside]
+        + [pl.BlockSpec(memory_space=pl.ANY)] * len(apart)
+        + [inside] * len(block_in)
         + [pl.BlockSpec(memory_space=pl.ANY) if load else inside] * len(weights),
         out_specs=[inside] * (3 + len(loaded)),
         scratch_shapes=[
@@ -146,7 +154,7 @@
             pltpu.VMEM((low_width, blocks * rows), jnp.float32),
             pltpu.VMEM((blocks * rows, 128), jnp.float32),
         ]
-        + ([pltpu.SemaphoreType.DMA((3 * tiles + load + 1,))] if load else []),
+        + ([pltpu.SemaphoreType.DMA((3 * tiles + load + 3,))] if load else []),
         compiler_params=pltpu.CompilerParams(
             vmem_limit_bytes=(LOAD_MIB if load else 16) * 1024 * 1024
         ),
@@ -156,7 +164,7 @@
             transcendentals=blocks * rows * units,
         ),
     )
-    return call(sheet, *block_in, *weights)
+    return call(sheet, *apart, *block_in, *weights)
 
 
 def outcome_kernel(jobs, returned, routes, *refs):
@@ -202,16 +210,21 @@
         out[e] = jnp.where(line == 1, weight[e : e + 1, :], doc)
 
 
-def stack_kernel(top, bottom, out, sems):
+def stack_kernel(top, bottom, out):
     rows = top.shape[0]
-    copies = [
-        pltpu.make_async_copy(top, out.at[:rows], sems.at[0]),
-        pltpu.make_async_copy(bottom, out.at[rows:], sems.at[1]),
-    ]
-    for copy in copies:
-        copy.start()
-    for copy in copies:
-        copy.wait()
+    out[:rows, :] = top[...]
+    out[rows:, :] = bottom[...]
+
+
+def stack(top, bottom):
+    inside = pl.BlockSpec(memory_space=pltpu.VMEM)
+    return pl.pallas_call(
+        stack_kernel,
+        out_shape=jax.ShapeDtypeStruct((2 * top.shape[0], top.shape[1]), top.dtype),
+        in_specs=[inside] * 2,
+        out_specs=inside,
+        compiler_params=pltpu.CompilerParams(vmem_limit_bytes=8 * 1024 * 1024),
+    )(top, bottom)
 
 
 def by_ring(
@@ -247,49 +260,46 @@
             jobs.append(job)
     jobs.append((arrivals[-1] + (True,),))
 
-    rows, width = tokens.shape
-    own = pl.pallas_call(
-        stack_kernel,
-        out_shape=jax.ShapeDtypeStruct((2 * rows, width), tokens.dtype),
-        in_specs=[pl.BlockSpec(memory_space=pltpu.HBM)] * 2,
-        out_specs=pl.BlockSpec(memory_space=pltpu.VMEM),
-        scratch_shapes=[pltpu.SemaphoreType.DMA((2,))],
-    )(tokens, cotangent)
-    beside = swap(own)
-
     sheet = pl.pallas_call(
         facts_kernel,
-        out_shape=jax.ShapeDtypeStruct((groups, 8, rows), jnp.float32),
+        out_shape=jax.ShapeDtypeStruct((groups, 8, tok_rows), jnp.float32),
         in_specs=[pl.BlockSpec(memory_space=pltpu.VMEM)] * 3,
         out_specs=pl.BlockSpec(memory_space=pltpu.VMEM),
         compiler_params=pltpu.CompilerParams(vmem_limit_bytes=8 * 1024 * 1024),
     )(routes.T, combine.T, doc_ids[None, :])
+    x, dy = hop(tokens), hop(cotangent)
+    x, *own = lax.optimization_barrier((x, tokens, cotangent))
+    first = (x, dy)
+    beside = stack(swap(own[0]), swap(own[1]))
+
     inside = pl.BlockSpec(memory_space=pltpu.VMEM)
     given = (w_gate[0], w_up[0], w_down[0], proj_hidden[0].T, proj_output[0].T)
     weights = None
     lows, projs = [], []
-    held = {("a", 0, False): own, ("a", 0, True): beside}
+    held = {("a", 0, True): beside}
     todo = list(jobs)
 
     def take():
         nonlocal sheet, weights
         names = todo.pop(0)
-        blocks = [held[name] for name in names]
+        blocks = [held[name] for name in names if name in held]
         if weights is None:
             sheet, low_side, proj_cot, *weights = work(
-                names, sheet, blocks, given, load=docs_count
+                names, sheet, blocks, given, apart=(tokens, cotangent), load=docs_count
             )
         else:
             sheet, low_side, proj_cot = work(names, sheet, blocks, weights)
         lows.append(low_side)
         projs.append(proj_cot)
 
-    chain = {"a": own, "b": beside}
+    chain = {"b": beside}
     for i, (c, step) in enumerate(arrivals):
-        block = hop(chain[c])
+        block = hop(chain[c]) if i > 0 else first
         if i != 1:
             take()
             sheet, block = lax.optimization_barrier((sheet, block))
+        if i == 0:
+            block = stack(*block)
         chain[c] = held[(c, step, False)] = block
         held[(c, step, True)] = swap(block)
     while todo:

time: 107 us -> 109 us (1.019)
  starting transfers between devices: 15 us -> 17.4 us
  Pallas kernels: 33.5 us -> 31.6 us
    ppermute x7 -> x8, starting transfers between devices: 14.4 us -> 16.9 us  [hop(): return lax.ppermute(block, 'exp', onward)]
    pallas_call x10 -> x11, Pallas kernels: 32.4 us -> 30.5 us  [the longest x8 30.3 us: work(): return call(sheet, *apart, *block_in, *weights)]
    unnamed x14 -> x16, local copies, waits for them, and re-layouts: 5.09 us -> 5.95 us
    ppermute x7 -> x8, waiting for transfers between devices: 38.9 us -> 39.5 us  [hop(): return lax.ppermute(block, 'exp', onward)]
  transfers between devices with their start and end apart: 15 -> 17, of which waited for: 6 -> 7; matrix products, arithmetic and copies ran while one was open for 0% -> 0% of each run, Pallas kernels for 26% -> 26%
where the time goes in v9:
time: 109 us; the launch traced here: 108 us
  waiting for transfers between devices  39.5 us (36%)
  Pallas kernels  31.6 us (29%)
  starting transfers between devices  17.4 us (16%)
  blocking collectives  13.3 us (12%)
  local copies, waits for them, and re-layouts  5.95 us (5%)
    ppermute x8, waiting for transfers between devices, hop(): return lax.ppermute(block, 'exp', onward)  39.5 us
    pallas_call x8, Pallas kernels, work(): return call(sheet, *apart, *block_in, *weights)  30.3 us
    ppermute x8, starting transfers between devices, hop(): return lax.ppermute(block, 'exp', onward)  16.9 us
    all_to_all x1, blocking collectives, by_ring(): lax.all_to_all(sheet, 'exp', split_axis=0, concat_axis=0, tiled=True)  13.3 us
    unnamed x16, local copies, waits for them, and re-layouts  5.95 us
  transfers between devices with their start and end apart: 17, of which 7 were waited for; matrix products, arithmetic and copies ran while one was open for 0% of the time, Pallas kernels for 26%

profile of v9, /device:TPU:0, one launch (start us, length us, event | category | flops | bytes accessed | tf_op | source)
XLA Modules:
  0.0 108.5 jit_solution(11638765124824749361)
XLA Ops:
  0.6 3.1 %collective-permute-start = (bf16[128,2048]{1,0:T(8,128)(2,1)}, bf16[128,2048]{1,0:T(8,128)(2,1)S(1)}, u32[]{:S(2)}, u32[]{:S(2)}) collective-permute-start(bf16[128,2048]{1,0:T(8,128)(2,1)} %refs_1_.1), channel_id=1, source_target_pairs={{0,4},{1,3},{4,8},{5,1},{8,12},{9,5},{12,14},{13,9},{14,10},{15,13... | collective-permute-start | bytes 1572872 | tf_op jit(solution)/shard_map/ppermute | solution.py:246
  3.7 7.3 %collective-permute-done.top = bf16[128,2048]{1,0:T(8,128)(2,1)S(1)} collective-permute-done((bf16[128,2048]{1,0:T(8,128)(2,1)}, bf16[128,2048]{1,0:T(8,128)(2,1)S(1)}, u32[]{:S(2)}, u32[]{:S(2)}) %collective-permute-start) | collective-permute-done | bytes 524320 | tf_op jit(solution)/shard_map/ppermute | solution.py:246
  11.0 0.0 collective-permute-start.1
  11.0 0.5 collective-permute-start.2
  11.5 2.1 %collective-permute-start.3 = (bf16[128,2048]{1,0:T(8,128)(2,1)}, bf16[128,2048]{1,0:T(8,128)(2,1)S(1)}, u32[]{:S(2)}, u32[]{:S(2)}) collective-permute-start(bf16[128,2048]{1,0:T(8,128)(2,1)} %refs_2_.1), channel_id=1, source_target_pairs={{0,4},{1,3},{4,8},{5,1},{8,12},{9,5},{12,14},{13,9},{14,10},{15,13... | collective-permute-start | bytes 1572872 | tf_op jit(solution)/shard_map/ppermute | solution.py:246
  13.6 0.7 copy-done.4
  14.3 0.7 copy-done.6
  15.0 0.7 copy-done.7
  15.7 0.0 collective-permute-done.1.top
  15.7 0.0 collective-permute-done.2.bottom
  15.7 0.1 shard_map.114.refs_3_
  15.8 1.6 %collective-permute-start.4 = (bf16[256,2048]{1,0:T(8,128)(2,1)S(1)}, bf16[256,2048]{1,0:T(8,128)(2,1)S(1)}, u32[]{:S(2)}, u32[]{:S(2)}) collective-permute-start(bf16[256,2048]{1,0:T(8,128)(2,1)S(1)} %shard_map.114.refs_3_), channel_id=1, source_target_pairs={{0,4},{1,3},{4,8},{5,1},{8,12},{9,5},{12,14},{13,9},{14,10},{15,13... | collective-permute-start | bytes 3145736 | tf_op jit(solution)/shard_map/ppermute | solution.py:246
  17.4 1.0 copy-done
  18.4 1.0 copy-done.1
  19.5 0.9 copy-done.2
  20.4 0.9 copy-done.3
  21.3 6.6 %shard_map.115 = (f32[16,8,128]{2,1,0:T(8,128)S(1)}, bf16[256,256]{1,0:T(8,128)(2,1)S(1)}, f32[64,256]{1,0:T(8,128)S(1)}, bf16[2048,768]{1,0:T(8,128)(2,1)S(1)},...) custom-call(f32[16,8,128]{2,1,0:T(8,128)S(1)} %shard_map.113.refs_0_, ...), custom_call_target="tpu_custom_call" | custom-call | flops 2415919104 | bytes 2097152 | tf_op jit(solution)/shard_map/pallas_call | solution.py:167
  27.9 0.0 collective-permute-done.3.bottom
  27.9 0.1 shard_map.116.refs_3_
  28.0 0.1 collective-permute-start.5
  28.0 1.6 %collective-permute-start.6 = (bf16[256,2048]{1,0:T(8,128)(2,1)S(1)}, bf16[256,2048]{1,0:T(8,128)(2,1)S(1)}, u32[]{:S(2)}, u32[]{:S(2)}) collective-permute-start(bf16[256,2048]{1,0:T(8,128)(2,1)S(1)} %shard_map.116.refs_3_), channel_id=1, source_target_pairs={{0,4},{1,3},{4,8},{5,1},{8,12},{9,5},{12,14},{13,9},{14,10},{15,13... | collective-permute-start | bytes 3145736 | tf_op jit(solution)/shard_map/ppermute | solution.py:246
  29.7 2.5 %collective-permute-done.4.refs_1_ = bf16[256,2048]{1,0:T(8,128)(2,1)S(1)} collective-permute-done((bf16[256,2048]{1,0:T(8,128)(2,1)S(1)}, bf16[256,2048]{1,0:T(8,128)(2,1)S(1)}, u32[]{:S(2)}, u32[]{:S(2)}) %collective-permute-start.4) | collective-permute-done | bytes 1048608 | tf_op jit(solution)/shard_map/ppermute | solution.py:246
  32.1 2.1 %collective-permute-start.8 = (bf16[256,2048]{1,0:T(8,128)(2,1)S(1)}, bf16[256,2048]{1,0:T(8,128)(2,1)S(1)}, u32[]{:S(2)}, u32[]{:S(2)}) collective-permute-start(bf16[256,2048]{1,0:T(8,128)(2,1)S(1)} %collective-permute-done.4.refs_1_), channel_id=1, source_target_pairs={{0,4},{1,3},{4,8},{5,1},{8,12},{9,5},{12,14},{13,9},{14,10},{15,13... | collective-permute-start | bytes 3145736 | tf_op jit(solution)/shard_map/ppermute | solution.py:246
  34.2 0.0 collective-permute-done.5.refs_2_
  34.2 4.6 %shard_map.117 = (f32[16,8,128]{2,1,0:T(8,128)S(1)}, bf16[256,384]{1,0:T(8,128)(2,1)S(1)}, f32[64,384]{1,0:T(8,128)S(1)}) custom-call(f32[16,8,128]{2,1,0:T(8,128)S(1)} %get-tuple-element.53.refs_0_, bf16[256,2048]{1,0:T(8,128)(2,1)S(1)} %collective-permute-done.4.refs_1_, bf16[256,2048]{1,0:T(8,128)(2,1)S(1)} %collective-permute-done.5.refs_2_, ...), custom_call_target="tpu_custom_call" | custom-call | flops 3623878656 | bytes 3145728 | tf_op jit(solution)/shard_map/pallas_call | solution.py:167
  38.9 4.5 %collective-permute-done.6.refs_1_ = bf16[256,2048]{1,0:T(8,128)(2,1)S(1)} collective-permute-done((bf16[256,2048]{1,0:T(8,128)(2,1)S(1)}, bf16[256,2048]{1,0:T(8,128)(2,1)S(1)}, u32[]{:S(2)}, u32[]{:S(2)}) %collective-permute-start.6) | collective-permute-done | bytes 1048608 | tf_op jit(solution)/shard_map/ppermute | solution.py:246
  43.4 0.0 collective-permute-start.9
  43.4 2.1 %collective-permute-start.10 = (bf16[256,2048]{1,0:T(8,128)(2,1)S(1)}, bf16[256,2048]{1,0:T(8,128)(2,1)S(1)}, u32[]{:S(2)}, u32[]{:S(2)}) collective-permute-start(bf16[256,2048]{1,0:T(8,128)(2,1)S(1)} %collective-permute-done.6.refs_1_), channel_id=1, source_target_pairs={{0,4},{1,3},{4,8},{5,1},{8,12},{9,5},{12,14},{13,9},{14,10},{15,13... | collective-permute-start | bytes 3145736 | tf_op jit(solution)/shard_map/ppermute | solution.py:246
  45.5 3.3 %shard_map.118 = (f32[16,8,128]{2,1,0:T(8,128)S(1)}, bf16[256,256]{1,0:T(8,128)(2,1)S(1)}, f32[64,256]{1,0:T(8,128)S(1)}) custom-call(f32[16,8,128]{2,1,0:T(8,128)S(1)} %get-tuple-element.62.refs_0_, bf16[256,2048]{1,0:T(8,128)(2,1)S(1)} %collective-permute-done.6.refs_1_, bf16[256,2048]{1,0:T(8,128)(2,1)S(1)} %collective-permute-done.7.refs_2_, ...), custom_call_target="tpu_custom_call" | custom-call | flops 2415919104 | bytes 2097152 | tf_op jit(solution)/shard_map/pallas_call | solution.py:167
  48.8 5.8 %collective-permute-done.8.refs_1_ = bf16[256,2048]{1,0:T(8,128)(2,1)S(1)} collective-permute-done((bf16[256,2048]{1,0:T(8,128)(2,1)S(1)}, bf16[256,2048]{1,0:T(8,128)(2,1)S(1)}, u32[]{:S(2)}, u32[]{:S(2)}) %collective-permute-start.8) | collective-permute-done | bytes 1048608 | tf_op jit(solution)/shard_map/ppermute | solution.py:246
  54.6 0.0 collective-permute-start.11
  54.6 2.1 %collective-permute-start.12 = (bf16[256,2048]{1,0:T(8,128)(2,1)S(1)}, bf16[256,2048]{1,0:T(8,128)(2,1)S(1)}, u32[]{:S(2)}, u32[]{:S(2)}) collective-permute-start(bf16[256,2048]{1,0:T(8,128)(2,1)S(1)} %collective-permute-done.8.refs_1_), channel_id=1, source_target_pairs={{0,4},{1,3},{4,8},{5,1},{8,12},{9,5},{12,14},{13,9},{14,10},{15,13... | collective-permute-start | bytes 3145736 | tf_op jit(solution)/shard_map/ppermute | solution.py:246
  56.7 0.0 collective-permute-done.9.refs_2_
  56.7 3.3 %shard_map.119 = (f32[16,8,128]{2,1,0:T(8,128)S(1)}, bf16[256,256]{1,0:T(8,128)(2,1)S(1)}, f32[64,256]{1,0:T(8,128)S(1)}) custom-call(f32[16,8,128]{2,1,0:T(8,128)S(1)} %get-tuple-element.65.refs_0_, bf16[256,2048]{1,0:T(8,128)(2,1)S(1)} %collective-permute-done.8.refs_1_, bf16[256,2048]{1,0:T(8,128)(2,1)S(1)} %collective-permute-done.9.refs_2_, ...), custom_call_target="tpu_custom_call" | custom-call | flops 2415919104 | bytes 2097152 | tf_op jit(solution)/shard_map/pallas_call | solution.py:167
  60.0 5.8 %collective-permute-done.10.refs_1_ = bf16[256,2048]{1,0:T(8,128)(2,1)S(1)} collective-permute-done((bf16[256,2048]{1,0:T(8,128)(2,1)S(1)}, bf16[256,2048]{1,0:T(8,128)(2,1)S(1)}, u32[]{:S(2)}, u32[]{:S(2)}) %collective-permute-start.10) | collective-permute-done | bytes 1048608 | tf_op jit(solution)/shard_map/ppermute | solution.py:246
  65.8 2.1 %collective-permute-start.14 = (bf16[256,2048]{1,0:T(8,128)(2,1)S(1)}, bf16[256,2048]{1,0:T(8,128)(2,1)S(1)}, u32[]{:S(2)}, u32[]{:S(2)}) collective-permute-start(bf16[256,2048]{1,0:T(8,128)(2,1)S(1)} %collective-permute-done.10.refs_1_), channel_id=1, source_target_pairs={{0,4},{1,3},{4,8},{5,1},{8,12},{9,5},{12,14},{13,9},{14,10},{15,13... | collective-permute-start | bytes 3145736 | tf_op jit(solution)/shard_map/ppermute | solution.py:246
  67.9 0.0 collective-permute-done.11.refs_2_
  67.9 3.3 %shard_map.120 = (f32[16,8,128]{2,1,0:T(8,128)S(1)}, bf16[256,256]{1,0:T(8,128)(2,1)S(1)}, f32[64,256]{1,0:T(8,128)S(1)}) custom-call(f32[16,8,128]{2,1,0:T(8,128)S(1)} %get-tuple-element.68.refs_0_, bf16[256,2048]{1,0:T(8,128)(2,1)S(1)} %collective-permute-done.10.refs_1_, bf16[256,2048]{1,0:T(8,128)(2,1)S(1)} %collective-permute-done.11.refs_2_, ...), custom_call_target="tpu_custom_call" | custom-call | flops 2415919104 | bytes 2097152 | tf_op jit(solution)/shard_map/pallas_call | solution.py:167
  71.3 5.8 %collective-permute-done.12.refs_1_ = bf16[256,2048]{1,0:T(8,128)(2,1)S(1)} collective-permute-done((bf16[256,2048]{1,0:T(8,128)(2,1)S(1)}, bf16[256,2048]{1,0:T(8,128)(2,1)S(1)}, u32[]{:S(2)}, u32[]{:S(2)}) %collective-permute-start.12) | collective-permute-done | bytes 1048608 | tf_op jit(solution)/shard_map/ppermute | solution.py:246
  77.1 3.3 %shard_map.121 = (f32[16,8,128]{2,1,0:T(8,128)S(1)}, bf16[256,256]{1,0:T(8,128)(2,1)S(1)}, f32[64,256]{1,0:T(8,128)S(1)}) custom-call(f32[16,8,128]{2,1,0:T(8,128)S(1)} %get-tuple-element.71.refs_0_, bf16[256,2048]{1,0:T(8,128)(2,1)S(1)} %collective-permute-done.12.refs_1_, bf16[256,2048]{1,0:T(8,128)(2,1)S(1)} %collective-permute-done.13.refs_2_, ...), custom_call_target="tpu_custom_call" | custom-call | flops 2415919104 | bytes 2097152 | tf_op jit(solution)/shard_map/pallas_call | solution.py:167
  80.4 7.9 %collective-permute-done.14.refs_1_ = bf16[256,2048]{1,0:T(8,128)(2,1)S(1)} collective-permute-done((bf16[256,2048]{1,0:T(8,128)(2,1)S(1)}, bf16[256,2048]{1,0:T(8,128)(2,1)S(1)}, u32[]{:S(2)}, u32[]{:S(2)}) %collective-permute-start.14) | collective-permute-done | bytes 1048608 | tf_op jit(solution)/shard_map/ppermute | solution.py:246
  88.3 0.0 collective-permute-start.16
  88.3 0.0 collective-permute-done.15.refs_2_
  88.3 3.3 %shard_map.122 = (f32[16,8,128]{2,1,0:T(8,128)S(1)}, bf16[256,256]{1,0:T(8,128)(2,1)S(1)}, f32[64,256]{1,0:T(8,128)S(1)}) custom-call(f32[16,8,128]{2,1,0:T(8,128)S(1)} %get-tuple-element.74.refs_0_, bf16[256,2048]{1,0:T(8,128)(2,1)S(1)} %collective-permute-done.14.refs_1_, bf16[256,2048]{1,0:T(8,128)(2,1)S(1)} %collective-permute-done.15.refs_2_, ...), custom_call_target="tpu_custom_call" | custom-call | flops 2415919104 | bytes 2097152 | tf_op jit(solution)/shard_map/pallas_call | solution.py:167
  91.7 0.0 copy-start.5
  91.7 2.4 %shard_map.123 = (f32[16,8,128]{2,1,0:T(8,128)S(1)}, bf16[256,128]{1,0:T(8,128)(2,1)S(1)}, f32[64,128]{1,0:T(8,128)S(1)}) custom-call(f32[16,8,128]{2,1,0:T(8,128)S(1)} %get-tuple-element.76.refs_0_, bf16[256,2048]{1,0:T(8,128)(2,1)S(1)} %collective-permute-done.16.refs_1_, bf16[2048,768]{1,0:T(8,128)(2,1)S(1)} %get-tuple-element.56.refs_4_.refs_3_.refs_2_, ...), custom_call_target="tpu_custom_call" | custom-call | flops 1207959552 | bytes 1048576 | tf_op jit(solution)/shard_map/pallas_call | solution.py:167
  94.1 13.3 %all_to_all.5.returned = f32[16,8,128]{2,1,0:T(8,128)S(1)} all-to-all(f32[16,8,128]{2,1,0:T(8,128)S(1)} %get-tuple-element.77), channel_id=1, replica_groups=mesh['grp'=2,'exp'=16] {'exp'}, dimensions={0} | all-to-all | bytes 131072 | tf_op jit(solution)/shard_map/all_to_all | solution.py:307
  107.4 1.1 %shard_map.124 = (f32[256,64]{1,0:T(8,128)}, f32[8,128]{1,0:T(8,128)}) custom-call(f32[16,8,128]{2,1,0:T(8,128)S(1)} %all_to_all.5.returned, s32[8,128]{1,0:T(8,128)S(1)} %bitcast.19, bf16[256,256]{1,0:T(8,128)(2,1)S(1)} %get-tuple-element.78.refs_0_, bf16[256,384]{1,0:T(8,128)(2,1)S(1)} %get-tuple-element.79.refs_1_, ...), custom_call_target="tpu_custom_call" | custom-call | tf_op jit(solution)/shard_map/pallas_call | solution.py:309
  (15 shorter events, 0.0 us)
Async XLA Ops:
  0.6 10.4 %collective-permute-start = (bf16[128,2048]{1,0:T(8,128)(2,1)}, bf16[128,2048]{1,0:T(8,128)(2,1)S(1)}, u32[]{:S(2)}, u32[]{:S(2)}) collective-permute-start(bf16[128,2048]{1,0:T(8,128)(2,1)} %refs_1_.1), channel_id=1, source_target_pairs={{0,4},{1,3},{4,8},{5,1},{8,12},{9,5},{12,14},{13,9},{14,10},{15,13... | collective-permute-start | bytes 1572872 | tf_op jit(solution)/shard_map/ppermute | solution.py:246
  11.0 4.7 %collective-permute-start.1 = (bf16[128,2048]{1,0:T(8,128)(2,1)}, bf16[128,2048]{1,0:T(8,128)(2,1)S(1)}, u32[]{:S(2)}, u32[]{:S(2)}) collective-permute-start(bf16[128,2048]{1,0:T(8,128)(2,1)} %refs_1_.1), channel_id=1, source_target_pairs={{0,1},{1,0},{2,3},{3,2},{4,5},{5,4},{6,7},{7,6},{8,9},{9,8},{10,11... | collective-permute-start | bytes 1572872 | tf_op jit(solution)/shard_map/ppermute | solution.py:249
  11.0 4.7 %collective-permute-start.2 = (bf16[128,2048]{1,0:T(8,128)(2,1)}, bf16[128,2048]{1,0:T(8,128)(2,1)S(1)}, u32[]{:S(2)}, u32[]{:S(2)}) collective-permute-start(bf16[128,2048]{1,0:T(8,128)(2,1)} %refs_2_.1), channel_id=1, source_target_pairs={{0,1},{1,0},{2,3},{3,2},{4,5},{5,4},{6,7},{7,6},{8,9},{9,8},{10,11... | collective-permute-start | bytes 1572872 | tf_op jit(solution)/shard_map/ppermute | solution.py:249
  11.5 16.4 %collective-permute-start.3 = (bf16[128,2048]{1,0:T(8,128)(2,1)}, bf16[128,2048]{1,0:T(8,128)(2,1)S(1)}, u32[]{:S(2)}, u32[]{:S(2)}) collective-permute-start(bf16[128,2048]{1,0:T(8,128)(2,1)} %refs_2_.1), channel_id=1, source_target_pairs={{0,4},{1,3},{4,8},{5,1},{8,12},{9,5},{12,14},{13,9},{14,10},{15,13... | collective-permute-start | bytes 1572872 | tf_op jit(solution)/shard_map/ppermute | solution.py:246
  13.6 0.7 copy-start.4
  14.3 0.7 copy-start.6
  15.0 0.7 copy-start.7
  15.8 16.4 %collective-permute-start.4 = (bf16[256,2048]{1,0:T(8,128)(2,1)S(1)}, bf16[256,2048]{1,0:T(8,128)(2,1)S(1)}, u32[]{:S(2)}, u32[]{:S(2)}) collective-permute-start(bf16[256,2048]{1,0:T(8,128)(2,1)S(1)} %shard_map.114.refs_3_), channel_id=1, source_target_pairs={{0,4},{1,3},{4,8},{5,1},{8,12},{9,5},{12,14},{13,9},{14,10},{15,13... | collective-permute-start | bytes 3145736 | tf_op jit(solution)/shard_map/ppermute | solution.py:246
  17.4 1.0 copy-start
  18.4 1.0 copy-start.1
  19.5 0.9 copy-start.2
  20.4 0.9 copy-start.3
  28.0 6.3 %collective-permute-start.5 = (bf16[256,2048]{1,0:T(8,128)(2,1)S(1)}, bf16[256,2048]{1,0:T(8,128)(2,1)S(1)}, u32[]{:S(2)}, u32[]{:S(2)}) collective-permute-start(bf16[256,2048]{1,0:T(8,128)(2,1)S(1)} %shard_map.116.refs_3_), channel_id=1, source_target_pairs={{0,1},{1,0},{2,3},{3,2},{4,5},{5,4},{6,7},{7,6},{8,9},{9,8},{10,11... | collective-permute-start | bytes 3145736 | tf_op jit(solution)/shard_map/ppermute | solution.py:249
  28.0 15.3 %collective-permute-start.6 = (bf16[256,2048]{1,0:T(8,128)(2,1)S(1)}, bf16[256,2048]{1,0:T(8,128)(2,1)S(1)}, u32[]{:S(2)}, u32[]{:S(2)}) collective-permute-start(bf16[256,2048]{1,0:T(8,128)(2,1)S(1)} %shard_map.116.refs_3_), channel_id=1, source_target_pairs={{0,4},{1,3},{4,8},{5,1},{8,12},{9,5},{12,14},{13,9},{14,10},{15,13... | collective-permute-start | bytes 3145736 | tf_op jit(solution)/shard_map/ppermute | solution.py:246
  32.1 13.3 %collective-permute-start.7 = (bf16[256,2048]{1,0:T(8,128)(2,1)S(1)}, bf16[256,2048]{1,0:T(8,128)(2,1)S(1)}, u32[]{:S(2)}, u32[]{:S(2)}) collective-permute-start(bf16[256,2048]{1,0:T(8,128)(2,1)S(1)} %collective-permute-done.4.refs_1_), channel_id=1, source_target_pairs={{0,1},{1,0},{2,3},{3,2},{4,5},{5,4},{6,7},{7,6},{8,9},{9,8},{10,11... | collective-permute-start | bytes 3145736 | tf_op jit(solution)/shard_map/ppermute | solution.py:249
  32.1 22.5 %collective-permute-start.8 = (bf16[256,2048]{1,0:T(8,128)(2,1)S(1)}, bf16[256,2048]{1,0:T(8,128)(2,1)S(1)}, u32[]{:S(2)}, u32[]{:S(2)}) collective-permute-start(bf16[256,2048]{1,0:T(8,128)(2,1)S(1)} %collective-permute-done.4.refs_1_), channel_id=1, source_target_pairs={{0,4},{1,3},{4,8},{5,1},{8,12},{9,5},{12,14},{13,9},{14,10},{15,13... | collective-permute-start | bytes 3145736 | tf_op jit(solution)/shard_map/ppermute | solution.py:246
  43.4 13.3 %collective-permute-start.9 = (bf16[256,2048]{1,0:T(8,128)(2,1)S(1)}, bf16[256,2048]{1,0:T(8,128)(2,1)S(1)}, u32[]{:S(2)}, u32[]{:S(2)}) collective-permute-start(bf16[256,2048]{1,0:T(8,128)(2,1)S(1)} %collective-permute-done.6.refs_1_), channel_id=1, source_target_pairs={{0,1},{1,0},{2,3},{3,2},{4,5},{5,4},{6,7},{7,6},{8,9},{9,8},{10,11... | collective-permute-start | bytes 3145736 | tf_op jit(solution)/shard_map/ppermute | solution.py:249
  43.4 22.5 %collective-permute-start.10 = (bf16[256,2048]{1,0:T(8,128)(2,1)S(1)}, bf16[256,2048]{1,0:T(8,128)(2,1)S(1)}, u32[]{:S(2)}, u32[]{:S(2)}) collective-permute-start(bf16[256,2048]{1,0:T(8,128)(2,1)S(1)} %collective-permute-done.6.refs_1_), channel_id=1, source_target_pairs={{0,4},{1,3},{4,8},{5,1},{8,12},{9,5},{12,14},{13,9},{14,10},{15,13... | collective-permute-start | bytes 3145736 | tf_op jit(solution)/shard_map/ppermute | solution.py:246
  54.6 13.3 %collective-permute-start.11 = (bf16[256,2048]{1,0:T(8,128)(2,1)S(1)}, bf16[256,2048]{1,0:T(8,128)(2,1)S(1)}, u32[]{:S(2)}, u32[]{:S(2)}) collective-permute-start(bf16[256,2048]{1,0:T(8,128)(2,1)S(1)} %collective-permute-done.8.refs_1_), channel_id=1, source_target_pairs={{0,1},{1,0},{2,3},{3,2},{4,5},{5,4},{6,7},{7,6},{8,9},{9,8},{10,11... | collective-permute-start | bytes 3145736 | tf_op jit(solution)/shard_map/ppermute | solution.py:249
  54.6 22.5 %collective-permute-start.12 = (bf16[256,2048]{1,0:T(8,128)(2,1)S(1)}, bf16[256,2048]{1,0:T(8,128)(2,1)S(1)}, u32[]{:S(2)}, u32[]{:S(2)}) collective-permute-start(bf16[256,2048]{1,0:T(8,128)(2,1)S(1)} %collective-permute-done.8.refs_1_), channel_id=1, source_target_pairs={{0,4},{1,3},{4,8},{5,1},{8,12},{9,5},{12,14},{13,9},{14,10},{15,13... | collective-permute-start | bytes 3145736 | tf_op jit(solution)/shard_map/ppermute | solution.py:246
  65.8 11.2 %collective-permute-start.13 = (bf16[256,2048]{1,0:T(8,128)(2,1)S(1)}, bf16[256,2048]{1,0:T(8,128)(2,1)S(1)}, u32[]{:S(2)}, u32[]{:S(2)}) collective-permute-start(bf16[256,2048]{1,0:T(8,128)(2,1)S(1)} %collective-permute-done.10.refs_1_), channel_id=1, source_target_pairs={{0,1},{1,0},{2,3},{3,2},{4,5},{5,4},{6,7},{7,6},{8,9},{9,8},{10,11... | collective-permute-start | bytes 3145736 | tf_op jit(solution)/shard_map/ppermute | solution.py:249
  65.8 22.5 %collective-permute-start.14 = (bf16[256,2048]{1,0:T(8,128)(2,1)S(1)}, bf16[256,2048]{1,0:T(8,128)(2,1)S(1)}, u32[]{:S(2)}, u32[]{:S(2)}) collective-permute-start(bf16[256,2048]{1,0:T(8,128)(2,1)S(1)} %collective-permute-done.10.refs_1_), channel_id=1, source_target_pairs={{0,4},{1,3},{4,8},{5,1},{8,12},{9,5},{12,14},{13,9},{14,10},{15,13... | collective-permute-start | bytes 3145736 | tf_op jit(solution)/shard_map/ppermute | solution.py:246
  77.1 11.2 %collective-permute-start.15 = (bf16[256,2048]{1,0:T(8,128)(2,1)S(1)}, bf16[256,2048]{1,0:T(8,128)(2,1)S(1)}, u32[]{:S(2)}, u32[]{:S(2)}) collective-permute-start(bf16[256,2048]{1,0:T(8,128)(2,1)S(1)} %collective-permute-done.12.refs_1_), channel_id=1, source_target_pairs={{0,1},{1,0},{2,3},{3,2},{4,5},{5,4},{6,7},{7,6},{8,9},{9,8},{10,11... | collective-permute-start | bytes 3145736 | tf_op jit(solution)/shard_map/ppermute | solution.py:249
  88.3 3.3 %collective-permute-start.16 = (bf16[256,2048]{1,0:T(8,128)(2,1)S(1)}, bf16[256,2048]{1,0:T(8,128)(2,1)S(1)}, u32[]{:S(2)}, u32[]{:S(2)}) collective-permute-start(bf16[256,2048]{1,0:T(8,128)(2,1)S(1)} %collective-permute-done.14.refs_1_), channel_id=1, source_target_pairs={{0,1},{1,0},{2,3},{3,2},{4,5},{5,4},{6,7},{7,6},{8,9},{9,8},{10,11... | collective-permute-start | bytes 3145736 | tf_op jit(solution)/shard_map/ppermute | solution.py:249
  91.7 15.7 %copy-start.5 = (s32[128,8]{0,1:T(8,128)S(1)}, s32[128,8]{0,1:T(8,128)}, u32[]{:S(2)}) copy-start(s32[128,8]{0,1:T(8,128)} %param.12) | copy-start | bytes 12292

commit v10 on v9

--- a/solution.py
+++ b/solution.py
@@ -48,16 +48,24 @@
     return 2 * chip + (core if (chain == "a") != handed else 1 - core)
 
 
-def rows_kernel(names, load, *refs):
+def rows_kernel(names, load, parted, late, *refs):
     blocks = len(names)
-    apart = refs[1:3] if load else ()
-    refs = refs[:1] + refs[3:] if load else refs
-    whole = blocks - 1 if load else blocks
-    sheet_in, block_in = refs[0], refs[1 : 1 + whole]
-    given = refs[1 + whole : 6 + whole]
-    sheet, low_side, proj_cot = refs[6 + whole : 9 + whole]
-    x_all, dy_all, low_sum, grad_sum = refs[-5:-1] if load else refs[-4:]
-    w_gate, w_up, w_down, low_proj, high_proj = refs[9 + whole : 14 + whole] if load else given
+    refs = list(refs)
+
+    def some(count):
+        taken = refs[:count]
+        del refs[:count]
+        return taken
+
+    sheet_in = None if late else some(1)[0]
+    apart, block_in = some(2 if parted else 0), some(blocks - parted)
+    whole = len(block_in)
+    given = some(5)
+    sheets = some(blocks if late else 1)
+    low_side, proj_cot = some(2)
+    loaded = some(5 if load else 0)
+    x_all, dy_all, low_sum, grad_sum = some(4)
+    w_gate, w_up, w_down, low_proj, high_proj = loaded if load else given
     rows = x_all.shape[0] // blocks
     across = (((1,), (1,)), ((), ()))
     units = w_gate.shape[1]
@@ -75,10 +83,11 @@
         for i in range(low_proj.shape[0] // rank):
             copies.append((given[3], low_proj.at[pl.ds(i * rank, rank), :]))
         copies.append((given[4], high_proj))
-        copies.append((apart[0], x_all.at[:rows]))
-        copies.append((apart[1], dy_all.at[:rows]))
+        if parted:
+            copies.append((apart[0], x_all.at[:rows]))
+            copies.append((apart[1], dy_all.at[:rows]))
         copies = [
-            pltpu.make_async_copy(src, dst, refs[-1].at[i]) for i, (src, dst) in enumerate(copies)
+            pltpu.make_async_copy(src, dst, refs[0].at[i]) for i, (src, dst) in enumerate(copies)
         ]
         for copy in copies[3 * tiles :] + copies[: 3 * tiles]:
             copy.start()
@@ -115,12 +124,17 @@
     proj_cot[...] = lax.dot_general(
         high_proj[...], dy_all[...], across, preferred_element_type=jnp.float32
     )
-    sheet[...] = sheet_in[...]
+    if not late:
+        sheets[0][...] = sheet_in[...]
     for i in range(blocks):
         total = jnp.sum(
             jnp.transpose(grad_sum[i * rows : (i + 1) * rows, :]), axis=0, keepdims=True
         )
-        sheet[block_owner(names[i], sheet.shape[0] // 2), 0:1, :] = total
+        if late:
+            sheets[i][...] = jnp.broadcast_to(total, sheets[i].shape)
+        else:
+            owner = block_owner(names[i], sheets[0].shape[0] // 2)
+            sheets[0][owner, 0:1, :] = total
 
 
 def work(names, sheet, block_in, weights, apart=(), load=0):
@@ -135,26 +149,28 @@
         shapes[3] = (low_width, units)
         loaded = [jax.ShapeDtypeStruct(shape, weights[0].dtype) for shape in shapes]
     tiles = units // 256 if units % 256 == 0 else 1
+    sheets = [(8, rows)] * blocks if sheet is None else [sheet.shape]
+    sheet = [] if sheet is None else [sheet]
     call = pl.pallas_call(
-        functools.partial(rows_kernel, names, load > 0),
-        out_shape=[
-            jax.ShapeDtypeStruct(sheet.shape, jnp.float32),
+        functools.partial(rows_kernel, names, load > 0, len(apart) > 0, not sheet),
+        out_shape=[jax.ShapeDtypeStruct(shape, jnp.float32) for shape in sheets]
+        + [
             jax.ShapeDtypeStruct((low_width, blocks * rows), jnp.bfloat16),
             jax.ShapeDtypeStruct((rank, blocks * rows), jnp.float32),
         ]
         + loaded,
-        in_specs=[inside]
+        in_specs=[inside] * len(sheet)
         + [pl.BlockSpec(memory_space=pl.ANY)] * len(apart)
         + [inside] * len(block_in)
         + [pl.BlockSpec(memory_space=pl.ANY) if load else inside] * len(weights),
-        out_specs=[inside] * (3 + len(loaded)),
+        out_specs=[inside] * (len(sheets) + 2 + len(loaded)),
         scratch_shapes=[
             pltpu.VMEM((blocks * rows, width), jnp.bfloat16),
             pltpu.VMEM((blocks * rows, width), jnp.bfloat16),
             pltpu.VMEM((low_width, blocks * rows), jnp.float32),
             pltpu.VMEM((blocks * rows, 128), jnp.float32),
         ]
-        + ([pltpu.SemaphoreType.DMA((3 * tiles + load + 3,))] if load else []),
+        + ([pltpu.SemaphoreType.DMA((3 * tiles + load + 1 + len(apart),))] if load else []),
         compiler_params=pltpu.CompilerParams(
             vmem_limit_bytes=(LOAD_MIB if load else 16) * 1024 * 1024
         ),
@@ -164,11 +180,14 @@
             transcendentals=blocks * rows * units,
         ),
     )
-    return call(sheet, *apart, *block_in, *weights)
-
-
-def outcome_kernel(jobs, returned, routes, *refs):
+    results = call(*sheet, *apart, *block_in, *weights)
+    cut = len(sheets)
+    return results[:cut], results[cut], results[cut + 1], results[cut + 2 :]
+
+
+def outcome_kernel(jobs, senders, returned, routes, *refs):
     low_in, proj_in = refs[: len(jobs)], refs[len(jobs) : 2 * len(jobs)]
+    late = refs[2 * len(jobs) : -2]
     feat, route_grad = refs[-2:]
     rows = returned.shape[2]
     width, rank = low_in[0].shape[0], proj_in[0].shape[0]
@@ -194,6 +213,9 @@
     picked = jnp.zeros(route_grad.shape, jnp.float32)
     for e in range(returned.shape[0]):
         picked = jnp.where(routes[...] == e, returned[e, 0:1, :], picked)
+    for name, lines in zip(senders, late):
+        sender = block_owner(name, returned.shape[0] // 2)
+        picked = jnp.where(routes[...] == sender, lines[0:1, :], picked)
     route_grad[...] = picked
 
 
@@ -267,55 +289,80 @@
         out_specs=pl.BlockSpec(memory_space=pltpu.VMEM),
         compiler_params=pltpu.CompilerParams(vmem_limit_bytes=8 * 1024 * 1024),
     )(routes.T, combine.T, doc_ids[None, :])
-    x, dy = hop(tokens), hop(cotangent)
-    x, *own = lax.optimization_barrier((x, tokens, cotangent))
-    first = (x, dy)
-    beside = stack(swap(own[0]), swap(own[1]))
+    first = (hop(tokens), hop(cotangent))
+    beside = stack(swap(tokens), swap(cotangent))
 
     inside = pl.BlockSpec(memory_space=pltpu.VMEM)
     given = (w_gate[0], w_up[0], w_down[0], proj_hidden[0].T, proj_output[0].T)
     weights = None
-    lows, projs = [], []
+    lows, projs, late, senders = [], [], [], []
     held = {("a", 0, True): beside}
     todo = list(jobs)
 
-    def take():
+    def back(name):
+        chain, step, handed = name
+        pairs = []
+        for place in range(chips):
+            for core in range(2):
+                way = (2 * core - 1) * (-1 if handed else 1)
+                owner = 2 * ring[(place + way * step) % chips]
+                owner += core if (chain == "a") != handed else 1 - core
+                pairs.append((2 * ring[place] + core, owner))
+        if 0 < step < half and (chain == "a") != handed:
+            return pairs, ("b" if chain == "a" else "a", step, not handed)
+        return pairs, name
+
+    def take(direct=False, load=False):
         nonlocal sheet, weights
         names = todo.pop(0)
         blocks = [held[name] for name in names if name in held]
-        if weights is None:
-            sheet, low_side, proj_cot, *weights = work(
-                names, sheet, blocks, given, apart=(tokens, cotangent), load=docs_count
-            )
-        else:
-            sheet, low_side, proj_cot = work(names, sheet, blocks, weights)
+        apart = () if len(blocks) == len(names) else (tokens, cotangent)
+        sheets, low_side, proj_cot, loaded = work(
+            names,
+            None if direct else sheet,
+            blocks,
+            given if load else weights,
+            apart=apart,
+            load=docs_count if load else 0,
+        )
+        weights = loaded if load else weights
         lows.append(low_side)
         projs.append(proj_cot)
+        if not direct:
+            (sheet,) = sheets
+            return
+        for name, lines in zip(names, sheets):
+            pairs, sender = back(name)
+            late.append(lax.ppermute(lines, "exp", pairs))
+            senders.append(sender)
 
     chain = {"b": beside}
+    end = len(arrivals) - 1
     for i, (c, step) in enumerate(arrivals):
         block = hop(chain[c]) if i > 0 else first
         if i != 1:
-            take()
-            sheet, block = lax.optimization_barrier((sheet, block))
+            take(direct=i == end, load=i in (0, end))
+            lows[-1:], block = lax.optimization_barrier((lows[-1:], block))
         if i == 0:
             block = stack(*block)
+        if i == end - 1:
+            returned = lax.all_to_all(sheet, "exp", split_axis=0, concat_axis=0, tiled=True)
+            returned, block = lax.optimization_barrier((returned, block))
         chain[c] = held[(c, step, False)] = block
         held[(c, step, True)] = swap(block)
     while todo:
-        take()
-    returned = lax.all_to_all(sheet, "exp", split_axis=0, concat_axis=0, tiled=True)
+        take(direct=True)
     rank = proj_output.shape[2]
     feature, route_grad = pl.pallas_call(
-        functools.partial(outcome_kernel, jobs),
+        functools.partial(outcome_kernel, jobs, senders),
         out_shape=[
             jax.ShapeDtypeStruct((docs_count * rank, rank), jnp.float32),
             jax.ShapeDtypeStruct((chosen, tok_rows), jnp.float32),
         ],
-        in_specs=[inside] * (2 + 2 * len(lows)),
+        in_specs=[inside] * (2 + 2 * len(lows) + len(late)),
         out_specs=[inside] * 2,
         compiler_params=pltpu.CompilerParams(vmem_limit_bytes=16 * 1024 * 1024),
-    )(returned, routes.T, *lows, *projs)
+    )(returned, routes.T, *lows, *projs, *late)
     return feature.reshape(docs_count, 1, rank, rank), route_grad.T
 
 

time: 109 us -> 119 us (1.092)
  blocking collectives: 13.3 us -> 0 us
  starting transfers between devices: 17.4 us -> 29.5 us
  Pallas kernels: 31.6 us -> 38 us
  local copies, waits for them, and re-layouts: 5.95 us -> 10.5 us
    ppermute x8, waiting for transfers between devices: 39.5 us -> 20 us  [hop(): return lax.ppermute(block, 'exp', onward)]
    all_to_all x0 -> x1, waiting for transfers between devices: none -> 14.8 us  [by_ring(): lax.all_to_all(sheet, 'exp', split_axis=0, concat_axis=0, tiled=True)]
    all_to_all x1 -> x0, blocking collectives: 13.3 us -> none  [by_ring(): lax.all_to_all(sheet, 'exp', split_axis=0, concat_axis=0, tiled=True)]
    ppermute x0 -> x5, starting transfers between devices: none -> 7.14 us  [take(): late.append(lax.ppermute(lines, 'exp', pairs))]
    pallas_call x9, Pallas kernels: 31.4 us -> 37.8 us  [the longest x8 35.9 us: work(): results = call(*sheet, *apart, *block_in, *weights)]
    all_to_all x0 -> x1, starting transfers between devices: none -> 4.95 us  [by_ring(): lax.all_to_all(sheet, 'exp', split_axis=0, concat_axis=0, tiled=True)]
    ppermute x0 -> x5, waiting for transfers between devices: none -> 4.54 us  [take(): late.append(lax.ppermute(lines, 'exp', pairs))]
    unnamed x16 -> x62, local copies, waits for them, and re-layouts: 5.95 us -> 10.5 us
  transfers between devices with their start and end apart: 17 -> 23, of which waited for: 7 -> 7; matrix products, arithmetic and copies ran while one was open for 0% -> 0% of each run, Pallas kernels for 26% -> 30%
where the time goes in v10:
time: 119 us; the launch traced here: 118 us
  waiting for transfers between devices  39.4 us (33%)
  Pallas kernels  38 us (32%)
  starting transfers between devices  29.5 us (25%)
  local copies, waits for them, and re-layouts  10.5 us (9%)
    pallas_call x8, Pallas kernels, work(): results = call(*sheet, *apart, *block_in, *weights)  35.9 us
    ppermute x8, waiting for transfers between devices, hop(): return lax.ppermute(block, 'exp', onward)  20 us
    ppermute x8, starting transfers between devices, hop(): return lax.ppermute(block, 'exp', onward)  16.2 us
    all_to_all x1, waiting for transfers between devices, by_ring(): lax.all_to_all(sheet, 'exp', split_axis=0, concat_axis=0, tiled=True)  14.8 us
    unnamed x62, local copies, waits for them, and re-layouts  10.5 us
    ppermute x5, starting transfers between devices, take(): late.append(lax.ppermute(lines, 'exp', pairs))  7.14 us
    all_to_all x1, starting transfers between devices, by_ring(): lax.all_to_all(sheet, 'exp', split_axis=0, concat_axis=0, tiled=True)  4.95 us
    ppermute x5, waiting for transfers between devices, take(): late.append(lax.ppermute(lines, 'exp', pairs))  4.54 us
  transfers between devices with their start and end apart: 23, of which 7 were waited for; matrix products, arithmetic and copies ran while one was open for 0% of the time, Pallas kernels for 30%

profile of v10, /device:TPU:0, one launch (start us, length us, event | category | flops | bytes accessed | tf_op | source)
XLA Modules:
  0.0 118.3 jit_solution(4983609735022194078)
XLA Ops:
  0.6 0.5 collective-permute-start
  1.1 0.1 collective-permute-start.1
  1.2 3.0 %collective-permute-start.3 = (bf16[128,2048]{1,0:T(8,128)(2,1)}, bf16[128,2048]{1,0:T(8,128)(2,1)S(1)}, u32[]{:S(2)}, u32[]{:S(2)}) collective-permute-start(bf16[128,2048]{1,0:T(8,128)(2,1)} %refs_1_.1), channel_id=1, source_target_pairs={{0,4},{1,3},{4,8},{5,1},{8,12},{9,5},{12,14},{13,9},{14,10},{15,13... | collective-permute-start | bytes 1572872 | tf_op jit(solution)/shard_map/ppermute | solution.py:268
  4.2 1.6 %collective-permute-start.4 = (bf16[128,2048]{1,0:T(8,128)(2,1)}, bf16[128,2048]{1,0:T(8,128)(2,1)S(1)}, u32[]{:S(2)}, u32[]{:S(2)}) collective-permute-start(bf16[128,2048]{1,0:T(8,128)(2,1)} %refs_2_.1), channel_id=1, source_target_pairs={{0,4},{1,3},{4,8},{5,1},{8,12},{9,5},{12,14},{13,9},{14,10},{15,13... | collective-permute-start | bytes 1572872 | tf_op jit(solution)/shard_map/ppermute | solution.py:268
  5.8 0.7 copy-done.27
  6.5 0.7 copy-done.29
  7.2 0.7 copy-done.30
  8.0 1.6 %collective-permute-start.2 = (bf16[256,2048]{1,0:T(8,128)(2,1)S(1)}, bf16[256,2048]{1,0:T(8,128)(2,1)S(1)}, u32[]{:S(2)}, u32[]{:S(2)}) collective-permute-start(bf16[256,2048]{1,0:T(8,128)(2,1)S(1)} %shard_map.114.refs_3_), channel_id=1, source_target_pairs={{0,4},{1,3},{4,8},{5,1},{8,12},{9,5},{12,14},{13,9},{14,10},{15,13... | collective-permute-start | bytes 3145736 | tf_op jit(solution)/shard_map/ppermute | solution.py:268
  9.6 0.9 copy-done
  10.5 1.0 copy-done.2
  11.6 1.0 copy-done.3
  12.6 0.9 copy-done.4
  13.5 6.6 %shard_map.115 = (f32[16,8,128]{2,1,0:T(8,128)S(1)}, bf16[256,256]{1,0:T(8,128)(2,1)S(1)}, f32[64,256]{1,0:T(8,128)S(1)}, bf16[2048,768]{1,0:T(8,128)(2,1)S(1)},...) custom-call(f32[16,8,128]{2,1,0:T(8,128)S(1)} %shard_map.113.refs_0_, ...), custom_call_target="tpu_custom_call" | custom-call | flops 2415919104 | bytes 2097152 | tf_op jit(solution)/shard_map/pallas_call | solution.py:183
  20.2 0.1 collective-permute-start.5
  20.3 1.5 %collective-permute-start.6 = (bf16[256,2048]{1,0:T(8,128)(2,1)S(1)}, bf16[256,2048]{1,0:T(8,128)(2,1)S(1)}, u32[]{:S(2)}, u32[]{:S(2)}) collective-permute-start(bf16[256,2048]{1,0:T(8,128)(2,1)S(1)} %shard_map.116.refs_3_), channel_id=1, source_target_pairs={{0,4},{1,3},{4,8},{5,1},{8,12},{9,5},{12,14},{13,9},{14,10},{15,13... | collective-permute-start | bytes 3145736 | tf_op jit(solution)/shard_map/ppermute | solution.py:268
  21.8 6.5 %collective-permute-done.2.refs_1_ = bf16[256,2048]{1,0:T(8,128)(2,1)S(1)} collective-permute-done((bf16[256,2048]{1,0:T(8,128)(2,1)S(1)}, bf16[256,2048]{1,0:T(8,128)(2,1)S(1)}, u32[]{:S(2)}, u32[]{:S(2)}) %collective-permute-start.2) | collective-permute-done | bytes 1048608 | tf_op jit(solution)/shard_map/ppermute | solution.py:268
  28.4 2.1 %collective-permute-start.8 = (bf16[256,2048]{1,0:T(8,128)(2,1)S(1)}, bf16[256,2048]{1,0:T(8,128)(2,1)S(1)}, u32[]{:S(2)}, u32[]{:S(2)}) collective-permute-start(bf16[256,2048]{1,0:T(8,128)(2,1)S(1)} %collective-permute-done.2.refs_1_), channel_id=1, source_target_pairs={{0,4},{1,3},{4,8},{5,1},{8,12},{9,5},{12,14},{13,9},{14,10},{15,13... | collective-permute-start | bytes 3145736 | tf_op jit(solution)/shard_map/ppermute | solution.py:268
  30.5 4.6 %shard_map.117 = (f32[16,8,128]{2,1,0:T(8,128)S(1)}, bf16[256,384]{1,0:T(8,128)(2,1)S(1)}, f32[64,384]{1,0:T(8,128)S(1)}) custom-call(f32[16,8,128]{2,1,0:T(8,128)S(1)} %get-tuple-element.55.refs_0_, bf16[256,2048]{1,0:T(8,128)(2,1)S(1)} %collective-permute-done.2.refs_1_, bf16[256,2048]{1,0:T(8,128)(2,1)S(1)} %collective-permute-done.5.refs_2_, ...), custom_call_target="tpu_custom_call" | custom-call | flops 3623878656 | bytes 3145728 | tf_op jit(solution)/shard_map/pallas_call | solution.py:183
  35.2 4.4 %collective-permute-done.6.refs_1_ = bf16[256,2048]{1,0:T(8,128)(2,1)S(1)} collective-permute-done((bf16[256,2048]{1,0:T(8,128)(2,1)S(1)}, bf16[256,2048]{1,0:T(8,128)(2,1)S(1)}, u32[]{:S(2)}, u32[]{:S(2)}) %collective-permute-start.6) | collective-permute-done | bytes 1048608 | tf_op jit(solution)/shard_map/ppermute | solution.py:268
  39.6 2.1 %collective-permute-start.10 = (bf16[256,2048]{1,0:T(8,128)(2,1)S(1)}, bf16[256,2048]{1,0:T(8,128)(2,1)S(1)}, u32[]{:S(2)}, u32[]{:S(2)}) collective-permute-start(bf16[256,2048]{1,0:T(8,128)(2,1)S(1)} %collective-permute-done.6.refs_1_), channel_id=1, source_target_pairs={{0,4},{1,3},{4,8},{5,1},{8,12},{9,5},{12,14},{13,9},{14,10},{15,13... | collective-permute-start | bytes 3145736 | tf_op jit(solution)/shard_map/ppermute | solution.py:268
  41.7 3.3 %shard_map.118 = (f32[16,8,128]{2,1,0:T(8,128)S(1)}, bf16[256,256]{1,0:T(8,128)(2,1)S(1)}, f32[64,256]{1,0:T(8,128)S(1)}) custom-call(f32[16,8,128]{2,1,0:T(8,128)S(1)} %get-tuple-element.64.refs_0_, bf16[256,2048]{1,0:T(8,128)(2,1)S(1)} %collective-permute-done.6.refs_1_, bf16[256,2048]{1,0:T(8,128)(2,1)S(1)} %collective-permute-done.7.refs_2_, ...), custom_call_target="tpu_custom_call" | custom-call | flops 2415919104 | bytes 2097152 | tf_op jit(solution)/shard_map/pallas_call | solution.py:183
  45.1 0.6 copy-done.10
  45.7 0.6 copy-done.20
  46.3 4.5 %collective-permute-done.8.refs_1_ = bf16[256,2048]{1,0:T(8,128)(2,1)S(1)} collective-permute-done((bf16[256,2048]{1,0:T(8,128)(2,1)S(1)}, bf16[256,2048]{1,0:T(8,128)(2,1)S(1)}, u32[]{:S(2)}, u32[]{:S(2)}) %collective-permute-start.8) | collective-permute-done | bytes 1048608 | tf_op jit(solution)/shard_map/ppermute | solution.py:268
  50.8 2.1 %collective-permute-start.12 = (bf16[256,2048]{1,0:T(8,128)(2,1)S(1)}, bf16[256,2048]{1,0:T(8,128)(2,1)S(1)}, u32[]{:S(2)}, u32[]{:S(2)}) collective-permute-start(bf16[256,2048]{1,0:T(8,128)(2,1)S(1)} %collective-permute-done.8.refs_1_), channel_id=1, source_target_pairs={{0,4},{1,3},{4,8},{5,1},{8,12},{9,5},{12,14},{13,9},{14,10},{15,13... | collective-permute-start | bytes 3145736 | tf_op jit(solution)/shard_map/ppermute | solution.py:268
  53.0 3.3 %shard_map.119 = (f32[16,8,128]{2,1,0:T(8,128)S(1)}, bf16[256,256]{1,0:T(8,128)(2,1)S(1)}, f32[64,256]{1,0:T(8,128)S(1)}) custom-call(f32[16,8,128]{2,1,0:T(8,128)S(1)} %get-tuple-element.67.refs_0_, bf16[256,2048]{1,0:T(8,128)(2,1)S(1)} %collective-permute-done.8.refs_1_, bf16[256,2048]{1,0:T(8,128)(2,1)S(1)} %collective-permute-done.9.refs_2_, ...), custom_call_target="tpu_custom_call" | custom-call | flops 2415919104 | bytes 2097152 | tf_op jit(solution)/shard_map/pallas_call | solution.py:183
  56.3 0.7 copy-done.12
  57.0 0.6 copy-done.22
  57.6 4.5 %collective-permute-done.10.refs_1_ = bf16[256,2048]{1,0:T(8,128)(2,1)S(1)} collective-permute-done((bf16[256,2048]{1,0:T(8,128)(2,1)S(1)}, bf16[256,2048]{1,0:T(8,128)(2,1)S(1)}, u32[]{:S(2)}, u32[]{:S(2)}) %collective-permute-start.10) | collective-permute-done | bytes 1048608 | tf_op jit(solution)/shard_map/ppermute | solution.py:268
  62.1 2.1 %collective-permute-start.14 = (bf16[256,2048]{1,0:T(8,128)(2,1)S(1)}, bf16[256,2048]{1,0:T(8,128)(2,1)}, u32[]{:S(2)}, u32[]{:S(2)}) collective-permute-start(bf16[256,2048]{1,0:T(8,128)(2,1)S(1)} %collective-permute-done.10.refs_1_), channel_id=1, source_target_pairs={{0,4},{1,3},{4,8},{5,1},{8,12},{9,5},{12,14},{13,9},{14,10},{15,13... | collective-permute-start | bytes 3145736 | tf_op jit(solution)/shard_map/ppermute | solution.py:268
  64.2 3.3 %shard_map.120 = (f32[16,8,128]{2,1,0:T(8,128)S(1)}, bf16[256,256]{1,0:T(8,128)(2,1)S(1)}, f32[64,256]{1,0:T(8,128)S(1)}) custom-call(f32[16,8,128]{2,1,0:T(8,128)S(1)} %get-tuple-element.70.refs_0_, bf16[256,2048]{1,0:T(8,128)(2,1)S(1)} %collective-permute-done.10.refs_1_, bf16[256,2048]{1,0:T(8,128)(2,1)S(1)} %collective-permute-done.11.refs_2_, ...), custom_call_target="tpu_custom_call" | custom-call | flops 2415919104 | bytes 2097152 | tf_op jit(solution)/shard_map/pallas_call | solution.py:183
  67.5 0.7 copy-done.14
  68.2 0.6 copy-done.24
  68.8 0.6 copy-done.26
  69.4 4.9 %all-to-all-start = ((f32[16,8,128]{2,1,0:T(8,128)}), f32[16,8,128]{2,1,0:T(8,128)}, u32[]{:S(2)}, u32[]{:S(2)}) async-start(f32[16,8,128]{2,1,0:T(8,128)} %copy-done.26), calls=%async_computation | async-start | bytes 131072 | tf_op jit(solution)/shard_map/all_to_all | solution.py:349
  74.4 14.8 %all-to-all-done.returned = f32[16,8,128]{2,1,0:T(8,128)} async-done(((f32[16,8,128]{2,1,0:T(8,128)}), f32[16,8,128]{2,1,0:T(8,128)}, u32[]{:S(2)}, u32[]{:S(2)}) %all-to-all-start) | async-done | bytes 65568 | tf_op jit(solution)/shard_map/all_to_all | solution.py:349
  89.2 7.7 %shard_map.121 = (f32[8,128]{1,0:T(8,128)S(1)}, f32[8,128]{1,0:T(8,128)S(1)}, bf16[256,256]{1,0:T(8,128)(2,1)S(1)}, f32[64,256]{1,0:T(8,128)S(1)}, bf16[2048,768...) custom-call(bf16[256,2048]{1,0:T(8,128)(2,1)S(1)} %collective-permut, ...), custom_call_target="tpu_custom_call" | custom-call | flops 2415919104 | bytes 2097152 | tf_op jit(solution)/shard_map/pallas_call | solution.py:183
  96.9 0.6 collective-permute-start.16
  97.5 0.3 collective-permute-start.17
  97.8 1.9 %collective-permute-start.18 = (f32[8,128]{1,0:T(8,128)S(1)}, f32[8,128]{1,0:T(8,128)S(1)}, u32[]{:S(2)}, u32[]{:S(2)}) collective-permute-start(f32[8,128]{1,0:T(8,128)S(1)} %get-tuple-element.102), channel_id=1, source_target_pairs={{0,13},{1,10},{4,15},{5,6},{8,11},{9,2},{12,7},{13,0},{14,3},{15,4... | collective-permute-start | bytes 12296 | tf_op jit(solution)/shard_map/ppermute | solution.py:336
  99.7 4.6 %shard_map.122 = (f32[8,128]{1,0:T(8,128)S(1)}, f32[8,128]{1,0:T(8,128)S(1)}, bf16[256,256]{1,0:T(8,128)(2,1)S(1)}, f32[64,256]{1,0:T(8,128)S(1)}) custom-call(bf16[256,2048]{1,0:T(8,128)(2,1)} %collective-permute-done.14.refs_0_, bf16[256,2048]{1,0:T(8,128)(2,1)S(1)} %collective-permute-done.15.refs_1_, ...), custom_call_target="tpu_custom_call" | custom-call | flops 2415919104 | bytes 2097152 | tf_op jit(solution)/shard_map/pallas_call | solution.py:183
  104.3 2.4 %collective-permute-start.19 = (f32[8,128]{1,0:T(8,128)S(1)}, f32[8,128]{1,0:T(8,128)S(1)}, u32[]{:S(2)}, u32[]{:S(2)}) collective-permute-start(f32[8,128]{1,0:T(8,128)S(1)} %get-tuple-element.103), channel_id=1, source_target_pairs={{0,14},{1,15},{4,10},{5,11},{8,6},{9,7},{12,2},{13,3},{14,0},{15,1... | collective-permute-start | bytes 12296 | tf_op jit(solution)/shard_map/ppermute | solution.py:336
  106.8 1.2 %collective-permute-start.20 = (f32[8,128]{1,0:T(8,128)S(1)}, f32[8,128]{1,0:T(8,128)S(1)}, u32[]{:S(2)}, u32[]{:S(2)}) collective-permute-start(f32[8,128]{1,0:T(8,128)S(1)} %get-tuple-element.104), channel_id=1, source_target_pairs={{0,12},{1,11},{4,14},{5,7},{8,10},{9,3},{12,6},{13,1},{14,2},{15,5... | collective-permute-start | bytes 12296 | tf_op jit(solution)/shard_map/ppermute | solution.py:336
  108.1 2.4 %shard_map.123 = (f32[8,128]{1,0:T(8,128)S(1)}, bf16[256,128]{1,0:T(8,128)(2,1)S(1)}, f32[64,128]{1,0:T(8,128)S(1)}) custom-call(bf16[256,2048]{1,0:T(8,128)(2,1)S(1)} %collective-permute-done.16.refs_0_, bf16[2048,768]{1,0:T(8,128)(2,1)S(1)} %get-tuple-element.86.refs_2_.refs_1_, bf16[2048,768]{1,0:T(8,128)(2,1)S(1)} %get-tuple-element.87.refs_3_.refs_2_, ...), custom_call_target="tpu_custom_call" | custom-call | flops 1207959552 | bytes 1048576 | tf_op jit(solution)/shard_map/pallas_call | solution.py:183
  110.5 1.2 %collective-permute-start.21 = (f32[8,128]{1,0:T(8,128)S(1)}, f32[8,128]{1,0:T(8,128)S(1)}, u32[]{:S(2)}, u32[]{:S(2)}) collective-permute-start(f32[8,128]{1,0:T(8,128)S(1)} %get-tuple-element.105), channel_id=1, source_target_pairs={{0,15},{1,14},{4,11},{5,10},{8,7},{9,6},{12,3},{13,2},{14,1},{15,0... | collective-permute-start | bytes 12296 | tf_op jit(solution)/shard_map/ppermute | solution.py:336
  111.7 0.8 collective-permute-done.20.refs_19_
  112.5 3.8 %collective-permute-done.21.refs_20_ = f32[8,128]{1,0:T(8,128)S(1)} collective-permute-done((f32[8,128]{1,0:T(8,128)S(1)}, f32[8,128]{1,0:T(8,128)S(1)}, u32[]{:S(2)}, u32[]{:S(2)}) %collective-permute-start.21) | collective-permute-done | bytes 4128 | tf_op jit(solution)/shard_map/ppermute | solution.py:336
  116.4 2.0 %shard_map.124 = (f32[256,64]{1,0:T(8,128)}, f32[8,128]{1,0:T(8,128)}) custom-call(f32[16,8,128]{2,1,0:T(8,128)} %all-to-all-done.returned, s32[8,128]{1,0:T(8,128)S(1)} %bitcast.21, bf16[256,256]{1,0:T(8,128)(2,1)S(1)} %copy-done.9, bf16[256,384]{1,0:T(8,128)(2,1)S(1)} %copy-done.7, bf16[256,256]{1,0:T(8,128)(2,1)S(1)} %copy-done.11, ...), custom_call_target="tpu_custom_call" | custom-call | tf_op jit(solution)/shard_map/pallas_call | solution.py:356
  (72 shorter events, 0.3 us)
Async XLA Ops:
  0.6 7.2 %collective-permute-start = (bf16[128,2048]{1,0:T(8,128)(2,1)}, bf16[128,2048]{1,0:T(8,128)(2,1)S(1)}, u32[]{:S(2)}, u32[]{:S(2)}) collective-permute-start(bf16[128,2048]{1,0:T(8,128)(2,1)} %refs_1_.1), channel_id=1, source_target_pairs={{0,1},{1,0},{2,3},{3,2},{4,5},{5,4},{6,7},{7,6},{8,9},{9,8},{10,11... | collective-permute-start | bytes 1572872 | tf_op jit(solution)/shard_map/ppermute | solution.py:271
  1.1 6.7 %collective-permute-start.1 = (bf16[128,2048]{1,0:T(8,128)(2,1)}, bf16[128,2048]{1,0:T(8,128)(2,1)S(1)}, u32[]{:S(2)}, u32[]{:S(2)}) collective-permute-start(bf16[128,2048]{1,0:T(8,128)(2,1)} %refs_2_.1), channel_id=1, source_target_pairs={{0,1},{1,0},{2,3},{3,2},{4,5},{5,4},{6,7},{7,6},{8,9},{9,8},{10,11... | collective-permute-start | bytes 1572872 | tf_op jit(solution)/shard_map/ppermute | solution.py:271
  1.2 18.9 %collective-permute-start.3 = (bf16[128,2048]{1,0:T(8,128)(2,1)}, bf16[128,2048]{1,0:T(8,128)(2,1)S(1)}, u32[]{:S(2)}, u32[]{:S(2)}) collective-permute-start(bf16[128,2048]{1,0:T(8,128)(2,1)} %refs_1_.1), channel_id=1, source_target_pairs={{0,4},{1,3},{4,8},{5,1},{8,12},{9,5},{12,14},{13,9},{14,10},{15,13... | collective-permute-start | bytes 1572872 | tf_op jit(solution)/shard_map/ppermute | solution.py:268
  4.2 15.9 %collective-permute-start.4 = (bf16[128,2048]{1,0:T(8,128)(2,1)}, bf16[128,2048]{1,0:T(8,128)(2,1)S(1)}, u32[]{:S(2)}, u32[]{:S(2)}) collective-permute-start(bf16[128,2048]{1,0:T(8,128)(2,1)} %refs_2_.1), channel_id=1, source_target_pairs={{0,4},{1,3},{4,8},{5,1},{8,12},{9,5},{12,14},{13,9},{14,10},{15,13... | collective-permute-start | bytes 1572872 | tf_op jit(solution)/shard_map/ppermute | solution.py:268
  5.8 0.7 copy-start.27
  6.5 0.7 copy-start.29
  8.0 20.4 %collective-permute-start.2 = (bf16[256,2048]{1,0:T(8,128)(2,1)S(1)}, bf16[256,2048]{1,0:T(8,128)(2,1)S(1)}, u32[]{:S(2)}, u32[]{:S(2)}) collective-permute-start(bf16[256,2048]{1,0:T(8,128)(2,1)S(1)} %shard_map.114.refs_3_), channel_id=1, source_target_pairs={{0,4},{1,3},{4,8},{5,1},{8,12},{9,5},{12,14},{13,9},{14,10},{15,13... | collective-permute-start | bytes 3145736 | tf_op jit(solution)/shard_map/ppermute | solution.py:268
  9.6 0.9 copy-start
  10.5 1.0 copy-start.2
  11.6 1.0 copy-start.3
  12.6 0.9 copy-start.4
  20.1 15.0 %copy-start.8 = (bf16[256,256]{1,0:T(8,128)(2,1)}, bf16[256,256]{1,0:T(8,128)(2,1)S(1)}, u32[]{:S(2)}) copy-start(bf16[256,256]{1,0:T(8,128)(2,1)S(1)} %get-tuple-element.77.refs_0_) | copy-start | bytes 393220
  20.1 15.0 %copy-start.18 = (f32[64,256]{1,0:T(8,128)}, f32[64,256]{1,0:T(8,128)S(1)}, u32[]{:S(2)}) copy-start(f32[64,256]{1,0:T(8,128)S(1)} %get-tuple-element.93.refs_8_) | copy-start | bytes 196612
  20.2 10.3 %collective-permute-start.5 = (bf16[256,2048]{1,0:T(8,128)(2,1)S(1)}, bf16[256,2048]{1,0:T(8,128)(2,1)S(1)}, u32[]{:S(2)}, u32[]{:S(2)}) collective-permute-start(bf16[256,2048]{1,0:T(8,128)(2,1)S(1)} %shard_map.116.refs_3_), channel_id=1, source_target_pairs={{0,1},{1,0},{2,3},{3,2},{4,5},{5,4},{6,7},{7,6},{8,9},{9,8},{10,11... | collective-permute-start | bytes 3145736 | tf_op jit(solution)/shard_map/ppermute | solution.py:271
  20.3 19.3 %collective-permute-start.6 = (bf16[256,2048]{1,0:T(8,128)(2,1)S(1)}, bf16[256,2048]{1,0:T(8,128)(2,1)S(1)}, u32[]{:S(2)}, u32[]{:S(2)}) collective-permute-start(bf16[256,2048]{1,0:T(8,128)(2,1)S(1)} %shard_map.116.refs_3_), channel_id=1, source_target_pairs={{0,4},{1,3},{4,8},{5,1},{8,12},{9,5},{12,14},{13,9},{14,10},{15,13... | collective-permute-start | bytes 3145736 | tf_op jit(solution)/shard_map/ppermute | solution.py:268
  28.4 13.4 %collective-permute-start.7 = (bf16[256,2048]{1,0:T(8,128)(2,1)S(1)}, bf16[256,2048]{1,0:T(8,128)(2,1)S(1)}, u32[]{:S(2)}, u32[]{:S(2)}) collective-permute-start(bf16[256,2048]{1,0:T(8,128)(2,1)S(1)} %collective-permute-done.2.refs_1_), channel_id=1, source_target_pairs={{0,1},{1,0},{2,3},{3,2},{4,5},{5,4},{6,7},{7,6},{8,9},{9,8},{10,11... | collective-permute-start | bytes 3145736 | tf_op jit(solution)/shard_map/ppermute | solution.py:271
  28.4 22.5 %collective-permute-start.8 = (bf16[256,2048]{1,0:T(8,128)(2,1)S(1)}, bf16[256,2048]{1,0:T(8,128)(2,1)S(1)}, u32[]{:S(2)}, u32[]{:S(2)}) collective-permute-start(bf16[256,2048]{1,0:T(8,128)(2,1)S(1)} %collective-permute-done.2.refs_1_), channel_id=1, source_target_pairs={{0,4},{1,3},{4,8},{5,1},{8,12},{9,5},{12,14},{13,9},{14,10},{15,13... | collective-permute-start | bytes 3145736 | tf_op jit(solution)/shard_map/ppermute | solution.py:268
  35.1 9.9 %copy-start.6 = (bf16[256,384]{1,0:T(8,128)(2,1)}, bf16[256,384]{1,0:T(8,128)(2,1)S(1)}, u32[]{:S(2)}) copy-start(bf16[256,384]{1,0:T(8,128)(2,1)S(1)} %get-tuple-element.78.refs_1_) | copy-start | bytes 589828
  35.1 9.9 %copy-start.16 = (f32[64,384]{1,0:T(8,128)}, f32[64,384]{1,0:T(8,128)S(1)}, u32[]{:S(2)}) copy-start(f32[64,384]{1,0:T(8,128)S(1)} %get-tuple-element.94.refs_9_) | copy-start | bytes 294916
  39.6 13.4 %collective-permute-start.9 = (bf16[256,2048]{1,0:T(8,128)(2,1)S(1)}, bf16[256,2048]{1,0:T(8,128)(2,1)S(1)}, u32[]{:S(2)}, u32[]{:S(2)}) collective-permute-start(bf16[256,2048]{1,0:T(8,128)(2,1)S(1)} %collective-permute-done.6.refs_1_), channel_id=1, source_target_pairs={{0,1},{1,0},{2,3},{3,2},{4,5},{5,4},{6,7},{7,6},{8,9},{9,8},{10,11... | collective-permute-start | bytes 3145736 | tf_op jit(solution)/shard_map/ppermute | solution.py:271
  39.6 22.5 %collective-permute-start.10 = (bf16[256,2048]{1,0:T(8,128)(2,1)S(1)}, bf16[256,2048]{1,0:T(8,128)(2,1)S(1)}, u32[]{:S(2)}, u32[]{:S(2)}) collective-permute-start(bf16[256,2048]{1,0:T(8,128)(2,1)S(1)} %collective-permute-done.6.refs_1_), channel_id=1, source_target_pairs={{0,4},{1,3},{4,8},{5,1},{8,12},{9,5},{12,14},{13,9},{14,10},{15,13... | collective-permute-start | bytes 3145736 | tf_op jit(solution)/shard_map/ppermute | solution.py:268
  50.8 13.4 %collective-permute-start.11 = (bf16[256,2048]{1,0:T(8,128)(2,1)S(1)}, bf16[256,2048]{1,0:T(8,128)(2,1)S(1)}, u32[]{:S(2)}, u32[]{:S(2)}) collective-permute-start(bf16[256,2048]{1,0:T(8,128)(2,1)S(1)} %collective-permute-done.8.refs_1_), channel_id=1, source_target_pairs={{0,1},{1,0},{2,3},{3,2},{4,5},{5,4},{6,7},{7,6},{8,9},{9,8},{10,11... | collective-permute-start | bytes 3145736 | tf_op jit(solution)/shard_map/ppermute | solution.py:271
  50.8 23.5 %collective-permute-start.12 = (bf16[256,2048]{1,0:T(8,128)(2,1)S(1)}, bf16[256,2048]{1,0:T(8,128)(2,1)S(1)}, u32[]{:S(2)}, u32[]{:S(2)}) collective-permute-start(bf16[256,2048]{1,0:T(8,128)(2,1)S(1)} %collective-permute-done.8.refs_1_), channel_id=1, source_target_pairs={{0,4},{1,3},{4,8},{5,1},{8,12},{9,5},{12,14},{13,9},{14,10},{15,13... | collective-permute-start | bytes 3145736 | tf_op jit(solution)/shard_map/ppermute | solution.py:268
  56.3 0.7 copy-start.12
  62.1 27.1 %collective-permute-start.13 = (bf16[256,2048]{1,0:T(8,128)(2,1)S(1)}, bf16[256,2048]{1,0:T(8,128)(2,1)}, u32[]{:S(2)}, u32[]{:S(2)}) collective-permute-start(bf16[256,2048]{1,0:T(8,128)(2,1)S(1)} %collective-permute-done.10.refs_1_), channel_id=1, source_target_pairs={{0,1},{1,0},{2,3},{3,2},{4,5},{5,4},{6,7},{7,6},{8,9},{9,8},{10,11... | collective-permute-start | bytes 3145736 | tf_op jit(solution)/shard_map/ppermute | solution.py:271
  62.1 34.8 %collective-permute-start.14 = (bf16[256,2048]{1,0:T(8,128)(2,1)S(1)}, bf16[256,2048]{1,0:T(8,128)(2,1)}, u32[]{:S(2)}, u32[]{:S(2)}) collective-permute-start(bf16[256,2048]{1,0:T(8,128)(2,1)S(1)} %collective-permute-done.10.refs_1_), channel_id=1, source_target_pairs={{0,4},{1,3},{4,8},{5,1},{8,12},{9,5},{12,14},{13,9},{14,10},{15,13... | collective-permute-start | bytes 3145736 | tf_op jit(solution)/shard_map/ppermute | solution.py:268
  64.2 25.0 %copy-start.1 = (bf16[1,2048,64]{1,2,0:T(8,128)(2,1)S(1)}, bf16[1,2048,64]{1,2,0:T(8,128)(2,1)}, u32[]{:S(2)}) copy-start(bf16[1,2048,64]{1,2,0:T(8,128)(2,1)} %param.19) | copy-start | bytes 786436
  64.2 25.0 %copy-start.5 = (bf16[1,768,64]{1,2,0:T(8,128)(2,1)S(1)}, bf16[1,768,64]{1,2,0:T(8,128)(2,1)}, u32[]{:S(2)}) copy-start(bf16[1,768,64]{1,2,0:T(8,128)(2,1)} %param.18) | copy-start | bytes 294916
  67.5 0.7 copy-start.14
  69.4 19.8 %all-to-all-start = ((f32[16,8,128]{2,1,0:T(8,128)}), f32[16,8,128]{2,1,0:T(8,128)}, u32[]{:S(2)}, u32[]{:S(2)}) async-start(f32[16,8,128]{2,1,0:T(8,128)} %copy-done.26), calls=%async_computation | async-start | bytes 131072 | tf_op jit(solution)/shard_map/all_to_all | solution.py:349
  89.2 10.6 %collective-permute-start.15 = (bf16[256,2048]{1,0:T(8,128)(2,1)S(1)}, bf16[256,2048]{1,0:T(8,128)(2,1)S(1)}, u32[]{:S(2)}, u32[]{:S(2)}) collective-permute-start(bf16[256,2048]{1,0:T(8,128)(2,1)S(1)} %collective-permute-done.12.refs_0_), channel_id=1, source_target_pairs={{0,1},{1,0},{2,3},{3,2},{4,5},{5,4},{6,7},{7,6},{8,9},{9,8},{10,11... | collective-permute-start | bytes 3145736 | tf_op jit(solution)/shard_map/ppermute | solution.py:271
  96.9 11.1 %collective-permute-start.16 = (bf16[256,2048]{1,0:T(8,128)(2,1)}, bf16[256,2048]{1,0:T(8,128)(2,1)S(1)}, u32[]{:S(2)}, u32[]{:S(2)}) collective-permute-start(bf16[256,2048]{1,0:T(8,128)(2,1)} %collective-permute-done.14.refs_0_), channel_id=1, source_target_pairs={{0,1},{1,0},{2,3},{3,2},{4,5},{5,4},{6,7},{7,6},{8,9},{9,8},{10,11... | collective-permute-start | bytes 3145736 | tf_op jit(solution)/shard_map/ppermute | solution.py:271
  97.5 14.2 %collective-permute-start.17 = (f32[8,128]{1,0:T(8,128)S(1)}, f32[8,128]{1,0:T(8,128)S(1)}, u32[]{:S(2)}, u32[]{:S(2)}) collective-permute-start(f32[8,128]{1,0:T(8,128)S(1)} %get-tuple-element.101), channel_id=1, source_target_pairs={{0,11},{1,12},{4,7},{5,14},{8,3},{9,10},{12,1},{13,6},{14,5},{15,2... | collective-permute-start | bytes 12296 | tf_op jit(solution)/shard_map/ppermute | solution.py:336
  97.8 13.9 %collective-permute-start.18 = (f32[8,128]{1,0:T(8,128)S(1)}, f32[8,128]{1,0:T(8,128)S(1)}, u32[]{:S(2)}, u32[]{:S(2)}) collective-permute-start(f32[8,128]{1,0:T(8,128)S(1)} %get-tuple-element.102), channel_id=1, source_target_pairs={{0,13},{1,10},{4,15},{5,6},{8,11},{9,2},{12,7},{13,0},{14,3},{15,4... | collective-permute-start | bytes 12296 | tf_op jit(solution)/shard_map/ppermute | solution.py:336
  104.3 7.4 %collective-permute-start.19 = (f32[8,128]{1,0:T(8,128)S(1)}, f32[8,128]{1,0:T(8,128)S(1)}, u32[]{:S(2)}, u32[]{:S(2)}) collective-permute-start(f32[8,128]{1,0:T(8,128)S(1)} %get-tuple-element.103), channel_id=1, source_target_pairs={{0,14},{1,15},{4,10},{5,11},{8,6},{9,7},{12,2},{13,3},{14,0},{15,1... | collective-permute-start | bytes 12296 | tf_op jit(solution)/shard_map/ppermute | solution.py:336
  106.7 9.5 %copy-start.7 = (bf16[256,384]{1,0:T(8,128)(2,1)S(1)}, bf16[256,384]{1,0:T(8,128)(2,1)}, u32[]{:S(2)}) copy-start(bf16[256,384]{1,0:T(8,128)(2,1)} %copy-done.6) | copy-start | bytes 589828
  106.7 9.5 %copy-start.9 = (bf16[256,256]{1,0:T(8,128)(2,1)S(1)}, bf16[256,256]{1,0:T(8,128)(2,1)}, u32[]{:S(2)}) copy-start(bf16[256,256]{1,0:T(8,128)(2,1)} %copy-done.8) | copy-start | bytes 393220
  106.7 9.5 %copy-start.11 = (bf16[256,256]{1,0:T(8,128)(2,1)S(1)}, bf16[256,256]{1,0:T(8,128)(2,1)}, u32[]{:S(2)}) copy-start(bf16[256,256]{1,0:T(8,128)(2,1)} %copy-done.10) | copy-start | bytes 393220
  106.7 9.6 %copy-start.13 = (bf16[256,256]{1,0:T(8,128)(2,1)S(1)}, bf16[256,256]{1,0:T(8,128)(2,1)}, u32[]{:S(2)}) copy-start(bf16[256,256]{1,0:T(8,128)(2,1)} %copy-done.12) | copy-start | bytes 393220
  106.7 9.6 %copy-start.15 = (bf16[256,256]{1,0:T(8,128)(2,1)S(1)}, bf16[256,256]{1,0:T(8,128)(2,1)}, u32[]{:S(2)}) copy-start(bf16[256,256]{1,0:T(8,128)(2,1)} %copy-done.14) | copy-start | bytes 393220
  106.7 9.6 %copy-start.17 = (f32[64,384]{1,0:T(8,128)S(1)}, f32[64,384]{1,0:T(8,128)}, u32[]{:S(2)}) copy-start(f32[64,384]{1,0:T(8,128)} %copy-done.16) | copy-start | bytes 294916
  106.7 9.6 %copy-start.19 = (f32[64,256]{1,0:T(8,128)S(1)}, f32[64,256]{1,0:T(8,128)}, u32[]{:S(2)}) copy-start(f32[64,256]{1,0:T(8,128)} %copy-done.18) | copy-start | bytes 196612
  106.8 9.6 %copy-start.21 = (f32[64,256]{1,0:T(8,128)S(1)}, f32[64,256]{1,0:T(8,128)}, u32[]{:S(2)}) copy-start(f32[64,256]{1,0:T(8,128)} %copy-done.20) | copy-start | bytes 196612
  106.8 9.6 %copy-start.23 = (f32[64,256]{1,0:T(8,128)S(1)}, f32[64,256]{1,0:T(8,128)}, u32[]{:S(2)}) copy-start(f32[64,256]{1,0:T(8,128)} %copy-done.22) | copy-start | bytes 196612
  106.8 9.6 %copy-start.25 = (f32[64,256]{1,0:T(8,128)S(1)}, f32[64,256]{1,0:T(8,128)}, u32[]{:S(2)}) copy-start(f32[64,256]{1,0:T(8,128)} %copy-done.24) | copy-start | bytes 196612
  106.8 9.6 %copy-start.28 = (s32[128,8]{0,1:T(8,128)S(1)}, s32[128,8]{0,1:T(8,128)}, u32[]{:S(2)}) copy-start(s32[128,8]{0,1:T(8,128)} %param.12) | copy-start | bytes 12292
  106.8 5.7 %collective-permute-start.20 = (f32[8,128]{1,0:T(8,128)S(1)}, f32[8,128]{1,0:T(8,128)S(1)}, u32[]{:S(2)}, u32[]{:S(2)}) collective-permute-start(f32[8,128]{1,0:T(8,128)S(1)} %get-tuple-element.104), channel_id=1, source_target_pairs={{0,12},{1,11},{4,14},{5,7},{8,10},{9,3},{12,6},{13,1},{14,2},{15,5... | collective-permute-start | bytes 12296 | tf_op jit(solution)/shard_map/ppermute | solution.py:336
  110.5 5.8 %collective-permute-start.21 = (f32[8,128]{1,0:T(8,128)S(1)}, f32[8,128]{1,0:T(8,128)S(1)}, u32[]{:S(2)}, u32[]{:S(2)}) collective-permute-start(f32[8,128]{1,0:T(8,128)S(1)} %get-tuple-element.105), channel_id=1, source_target_pairs={{0,15},{1,14},{4,11},{5,10},{8,7},{9,6},{12,3},{13,2},{14,1},{15,0... | collective-permute-start | bytes 12296 | tf_op jit(solution)/shard_map/ppermute | solution.py:336
  (6 other events, 3.8 us)

commit v11 on v9

--- a/solution.py
+++ b/solution.py
@@ -267,10 +267,8 @@
         out_specs=pl.BlockSpec(memory_space=pltpu.VMEM),
         compiler_params=pltpu.CompilerParams(vmem_limit_bytes=8 * 1024 * 1024),
     )(routes.T, combine.T, doc_ids[None, :])
-    x, dy = hop(tokens), hop(cotangent)
-    x, *own = lax.optimization_barrier((x, tokens, cotangent))
-    first = (x, dy)
-    beside = stack(swap(own[0]), swap(own[1]))
+    first = (hop(tokens), hop(cotangent))
+    beside = stack(swap(tokens), swap(cotangent))
 
     inside = pl.BlockSpec(memory_space=pltpu.VMEM)
     given = (w_gate[0], w_up[0], w_down[0], proj_hidden[0].T, proj_output[0].T)

time: 109 us -> 105 us (0.963)
  waiting for transfers between devices: 39.5 us -> 36.3 us
    ppermute x8, waiting for transfers between devices: 39.5 us -> 36.3 us  [hop(): return lax.ppermute(block, 'exp', onward)]
  transfers between devices with their start and end apart: 17 -> 17, of which waited for: 7 -> 6; matrix products, arithmetic and copies ran while one was open for 0% -> 0% of each run, Pallas kernels for 26% -> 27%
where the time goes in v11:
time: 105 us
  waiting for transfers between devices  36.3 us (35%)
  Pallas kernels  31.6 us (30%)
  starting transfers between devices  16.9 us (16%)
  blocking collectives  13.3 us (13%)
  local copies, waits for them, and re-layouts  5.95 us (6%)
    ppermute x8, waiting for transfers between devices, hop(): return lax.ppermute(block, 'exp', onward)  36.3 us
    pallas_call x8, Pallas kernels, work(): return call(sheet, *apart, *block_in, *weights)  30.3 us
    ppermute x8, starting transfers between devices, hop(): return lax.ppermute(block, 'exp', onward)  16.2 us
    all_to_all x1, blocking collectives, by_ring(): lax.all_to_all(sheet, 'exp', split_axis=0, concat_axis=0, tiled=True)  13.3 us
    unnamed x16, local copies, waits for them, and re-layouts  5.95 us
  transfers between devices with their start and end apart: 17, of which 6 were waited for; matrix products, arithmetic and copies ran while one was open for 0% of the time, Pallas kernels for 27%

profile of v11, /device:TPU:0, one launch (start us, length us, event | category | flops | bytes accessed | tf_op | source)
XLA Modules:
  0.0 104.7 jit_solution(3713426097317323147)
XLA Ops:
  0.6 0.5 collective-permute-start
  1.1 0.1 collective-permute-start.1
  1.2 3.0 %collective-permute-start.2 = (bf16[128,2048]{1,0:T(8,128)(2,1)}, bf16[128,2048]{1,0:T(8,128)(2,1)S(1)}, u32[]{:S(2)}, u32[]{:S(2)}) collective-permute-start(bf16[128,2048]{1,0:T(8,128)(2,1)} %refs_1_.1), channel_id=1, source_target_pairs={{0,4},{1,3},{4,8},{5,1},{8,12},{9,5},{12,14},{13,9},{14,10},{15,13... | collective-permute-start | bytes 1572872 | tf_op jit(solution)/shard_map/ppermute | solution.py:246
  4.2 1.6 %collective-permute-start.3 = (bf16[128,2048]{1,0:T(8,128)(2,1)}, bf16[128,2048]{1,0:T(8,128)(2,1)S(1)}, u32[]{:S(2)}, u32[]{:S(2)}) collective-permute-start(bf16[128,2048]{1,0:T(8,128)(2,1)} %refs_2_.1), channel_id=1, source_target_pairs={{0,4},{1,3},{4,8},{5,1},{8,12},{9,5},{12,14},{13,9},{14,10},{15,13... | collective-permute-start | bytes 1572872 | tf_op jit(solution)/shard_map/ppermute | solution.py:246
  5.8 0.7 copy-done.4
  6.5 0.7 copy-done.6
  7.2 0.7 copy-done.7
  7.9 0.0 collective-permute-done.top
  7.9 0.0 collective-permute-done.1.bottom
  7.9 0.1 shard_map.114.refs_3_
  8.0 1.6 %collective-permute-start.4 = (bf16[256,2048]{1,0:T(8,128)(2,1)S(1)}, bf16[256,2048]{1,0:T(8,128)(2,1)S(1)}, u32[]{:S(2)}, u32[]{:S(2)}) collective-permute-start(bf16[256,2048]{1,0:T(8,128)(2,1)S(1)} %shard_map.114.refs_3_), channel_id=1, source_target_pairs={{0,4},{1,3},{4,8},{5,1},{8,12},{9,5},{12,14},{13,9},{14,10},{15,13... | collective-permute-start | bytes 3145736 | tf_op jit(solution)/shard_map/ppermute | solution.py:246
  9.6 1.0 copy-done
  10.6 1.0 copy-done.1
  11.7 0.9 copy-done.2
  12.6 0.9 copy-done.3
  13.5 6.6 %shard_map.115 = (f32[16,8,128]{2,1,0:T(8,128)S(1)}, bf16[256,256]{1,0:T(8,128)(2,1)S(1)}, f32[64,256]{1,0:T(8,128)S(1)}, bf16[2048,768]{1,0:T(8,128)(2,1)S(1)},...) custom-call(f32[16,8,128]{2,1,0:T(8,128)S(1)} %shard_map.113.refs_0_, ...), custom_call_target="tpu_custom_call" | custom-call | flops 2415919104 | bytes 2097152 | tf_op jit(solution)/shard_map/pallas_call | solution.py:167
  20.1 0.0 collective-permute-done.2.top
  20.1 0.1 shard_map.116.refs_3_
  20.2 0.1 collective-permute-start.5
  20.3 1.5 %collective-permute-start.6 = (bf16[256,2048]{1,0:T(8,128)(2,1)S(1)}, bf16[256,2048]{1,0:T(8,128)(2,1)S(1)}, u32[]{:S(2)}, u32[]{:S(2)}) collective-permute-start(bf16[256,2048]{1,0:T(8,128)(2,1)S(1)} %shard_map.116.refs_3_), channel_id=1, source_target_pairs={{0,4},{1,3},{4,8},{5,1},{8,12},{9,5},{12,14},{13,9},{14,10},{15,13... | collective-permute-start | bytes 3145736 | tf_op jit(solution)/shard_map/ppermute | solution.py:246
  21.8 6.6 %collective-permute-done.4.refs_1_ = bf16[256,2048]{1,0:T(8,128)(2,1)S(1)} collective-permute-done((bf16[256,2048]{1,0:T(8,128)(2,1)S(1)}, bf16[256,2048]{1,0:T(8,128)(2,1)S(1)}, u32[]{:S(2)}, u32[]{:S(2)}) %collective-permute-start.4) | collective-permute-done | bytes 1048608 | tf_op jit(solution)/shard_map/ppermute | solution.py:246
  28.4 0.0 collective-permute-start.7
  28.4 2.1 %collective-permute-start.8 = (bf16[256,2048]{1,0:T(8,128)(2,1)S(1)}, bf16[256,2048]{1,0:T(8,128)(2,1)S(1)}, u32[]{:S(2)}, u32[]{:S(2)}) collective-permute-start(bf16[256,2048]{1,0:T(8,128)(2,1)S(1)} %collective-permute-done.4.refs_1_), channel_id=1, source_target_pairs={{0,4},{1,3},{4,8},{5,1},{8,12},{9,5},{12,14},{13,9},{14,10},{15,13... | collective-permute-start | bytes 3145736 | tf_op jit(solution)/shard_map/ppermute | solution.py:246
  30.5 4.6 %shard_map.117 = (f32[16,8,128]{2,1,0:T(8,128)S(1)}, bf16[256,384]{1,0:T(8,128)(2,1)S(1)}, f32[64,384]{1,0:T(8,128)S(1)}) custom-call(f32[16,8,128]{2,1,0:T(8,128)S(1)} %get-tuple-element.47.refs_0_, bf16[256,2048]{1,0:T(8,128)(2,1)S(1)} %collective-permute-done.4.refs_1_, bf16[256,2048]{1,0:T(8,128)(2,1)S(1)} %collective-permute-done.5.refs_2_, ...), custom_call_target="tpu_custom_call" | custom-call | flops 3623878656 | bytes 3145728 | tf_op jit(solution)/shard_map/pallas_call | solution.py:167
  35.1 4.5 %collective-permute-done.6.refs_1_ = bf16[256,2048]{1,0:T(8,128)(2,1)S(1)} collective-permute-done((bf16[256,2048]{1,0:T(8,128)(2,1)S(1)}, bf16[256,2048]{1,0:T(8,128)(2,1)S(1)}, u32[]{:S(2)}, u32[]{:S(2)}) %collective-permute-start.6) | collective-permute-done | bytes 1048608 | tf_op jit(solution)/shard_map/ppermute | solution.py:246
  39.6 0.0 collective-permute-start.9
  39.6 2.1 %collective-permute-start.10 = (bf16[256,2048]{1,0:T(8,128)(2,1)S(1)}, bf16[256,2048]{1,0:T(8,128)(2,1)S(1)}, u32[]{:S(2)}, u32[]{:S(2)}) collective-permute-start(bf16[256,2048]{1,0:T(8,128)(2,1)S(1)} %collective-permute-done.6.refs_1_), channel_id=1, source_target_pairs={{0,4},{1,3},{4,8},{5,1},{8,12},{9,5},{12,14},{13,9},{14,10},{15,13... | collective-permute-start | bytes 3145736 | tf_op jit(solution)/shard_map/ppermute | solution.py:246
  41.7 3.3 %shard_map.118 = (f32[16,8,128]{2,1,0:T(8,128)S(1)}, bf16[256,256]{1,0:T(8,128)(2,1)S(1)}, f32[64,256]{1,0:T(8,128)S(1)}) custom-call(f32[16,8,128]{2,1,0:T(8,128)S(1)} %get-tuple-element.56.refs_0_, bf16[256,2048]{1,0:T(8,128)(2,1)S(1)} %collective-permute-done.6.refs_1_, bf16[256,2048]{1,0:T(8,128)(2,1)S(1)} %collective-permute-done.7.refs_2_, ...), custom_call_target="tpu_custom_call" | custom-call | flops 2415919104 | bytes 2097152 | tf_op jit(solution)/shard_map/pallas_call | solution.py:167
  45.0 5.8 %collective-permute-done.8.refs_1_ = bf16[256,2048]{1,0:T(8,128)(2,1)S(1)} collective-permute-done((bf16[256,2048]{1,0:T(8,128)(2,1)S(1)}, bf16[256,2048]{1,0:T(8,128)(2,1)S(1)}, u32[]{:S(2)}, u32[]{:S(2)}) %collective-permute-start.8) | collective-permute-done | bytes 1048608 | tf_op jit(solution)/shard_map/ppermute | solution.py:246
  50.8 0.0 collective-permute-start.11
  50.8 2.1 %collective-permute-start.12 = (bf16[256,2048]{1,0:T(8,128)(2,1)S(1)}, bf16[256,2048]{1,0:T(8,128)(2,1)S(1)}, u32[]{:S(2)}, u32[]{:S(2)}) collective-permute-start(bf16[256,2048]{1,0:T(8,128)(2,1)S(1)} %collective-permute-done.8.refs_1_), channel_id=1, source_target_pairs={{0,4},{1,3},{4,8},{5,1},{8,12},{9,5},{12,14},{13,9},{14,10},{15,13... | collective-permute-start | bytes 3145736 | tf_op jit(solution)/shard_map/ppermute | solution.py:246
  53.0 0.0 collective-permute-done.9.refs_2_
  53.0 3.3 %shard_map.119 = (f32[16,8,128]{2,1,0:T(8,128)S(1)}, bf16[256,256]{1,0:T(8,128)(2,1)S(1)}, f32[64,256]{1,0:T(8,128)S(1)}) custom-call(f32[16,8,128]{2,1,0:T(8,128)S(1)} %get-tuple-element.59.refs_0_, bf16[256,2048]{1,0:T(8,128)(2,1)S(1)} %collective-permute-done.8.refs_1_, bf16[256,2048]{1,0:T(8,128)(2,1)S(1)} %collective-permute-done.9.refs_2_, ...), custom_call_target="tpu_custom_call" | custom-call | flops 2415919104 | bytes 2097152 | tf_op jit(solution)/shard_map/pallas_call | solution.py:167
  56.3 5.8 %collective-permute-done.10.refs_1_ = bf16[256,2048]{1,0:T(8,128)(2,1)S(1)} collective-permute-done((bf16[256,2048]{1,0:T(8,128)(2,1)S(1)}, bf16[256,2048]{1,0:T(8,128)(2,1)S(1)}, u32[]{:S(2)}, u32[]{:S(2)}) %collective-permute-start.10) | collective-permute-done | bytes 1048608 | tf_op jit(solution)/shard_map/ppermute | solution.py:246
  62.1 2.1 %collective-permute-start.14 = (bf16[256,2048]{1,0:T(8,128)(2,1)S(1)}, bf16[256,2048]{1,0:T(8,128)(2,1)S(1)}, u32[]{:S(2)}, u32[]{:S(2)}) collective-permute-start(bf16[256,2048]{1,0:T(8,128)(2,1)S(1)} %collective-permute-done.10.refs_1_), channel_id=1, source_target_pairs={{0,4},{1,3},{4,8},{5,1},{8,12},{9,5},{12,14},{13,9},{14,10},{15,13... | collective-permute-start | bytes 3145736 | tf_op jit(solution)/shard_map/ppermute | solution.py:246
  64.2 0.0 collective-permute-done.11.refs_2_
  64.2 3.3 %shard_map.120 = (f32[16,8,128]{2,1,0:T(8,128)S(1)}, bf16[256,256]{1,0:T(8,128)(2,1)S(1)}, f32[64,256]{1,0:T(8,128)S(1)}) custom-call(f32[16,8,128]{2,1,0:T(8,128)S(1)} %get-tuple-element.62.refs_0_, bf16[256,2048]{1,0:T(8,128)(2,1)S(1)} %collective-permute-done.10.refs_1_, bf16[256,2048]{1,0:T(8,128)(2,1)S(1)} %collective-permute-done.11.refs_2_, ...), custom_call_target="tpu_custom_call" | custom-call | flops 2415919104 | bytes 2097152 | tf_op jit(solution)/shard_map/pallas_call | solution.py:167
  67.5 5.8 %collective-permute-done.12.refs_1_ = bf16[256,2048]{1,0:T(8,128)(2,1)S(1)} collective-permute-done((bf16[256,2048]{1,0:T(8,128)(2,1)S(1)}, bf16[256,2048]{1,0:T(8,128)(2,1)S(1)}, u32[]{:S(2)}, u32[]{:S(2)}) %collective-permute-start.12) | collective-permute-done | bytes 1048608 | tf_op jit(solution)/shard_map/ppermute | solution.py:246
  73.3 0.0 collective-permute-start.15
  73.3 3.3 %shard_map.121 = (f32[16,8,128]{2,1,0:T(8,128)S(1)}, bf16[256,256]{1,0:T(8,128)(2,1)S(1)}, f32[64,256]{1,0:T(8,128)S(1)}) custom-call(f32[16,8,128]{2,1,0:T(8,128)S(1)} %get-tuple-element.65.refs_0_, bf16[256,2048]{1,0:T(8,128)(2,1)S(1)} %collective-permute-done.12.refs_1_, bf16[256,2048]{1,0:T(8,128)(2,1)S(1)} %collective-permute-done.13.refs_2_, ...), custom_call_target="tpu_custom_call" | custom-call | flops 2415919104 | bytes 2097152 | tf_op jit(solution)/shard_map/pallas_call | solution.py:167
  76.6 7.9 %collective-permute-done.14.refs_1_ = bf16[256,2048]{1,0:T(8,128)(2,1)S(1)} collective-permute-done((bf16[256,2048]{1,0:T(8,128)(2,1)S(1)}, bf16[256,2048]{1,0:T(8,128)(2,1)S(1)}, u32[]{:S(2)}, u32[]{:S(2)}) %collective-permute-start.14) | collective-permute-done | bytes 1048608 | tf_op jit(solution)/shard_map/ppermute | solution.py:246
  84.5 0.0 collective-permute-start.16
  84.5 0.0 collective-permute-done.15.refs_2_
  84.5 3.3 %shard_map.122 = (f32[16,8,128]{2,1,0:T(8,128)S(1)}, bf16[256,256]{1,0:T(8,128)(2,1)S(1)}, f32[64,256]{1,0:T(8,128)S(1)}) custom-call(f32[16,8,128]{2,1,0:T(8,128)S(1)} %get-tuple-element.68.refs_0_, bf16[256,2048]{1,0:T(8,128)(2,1)S(1)} %collective-permute-done.14.refs_1_, bf16[256,2048]{1,0:T(8,128)(2,1)S(1)} %collective-permute-done.15.refs_2_, ...), custom_call_target="tpu_custom_call" | custom-call | flops 2415919104 | bytes 2097152 | tf_op jit(solution)/shard_map/pallas_call | solution.py:167
  87.9 0.0 copy-start.5
  87.9 2.4 %shard_map.123 = (f32[16,8,128]{2,1,0:T(8,128)S(1)}, bf16[256,128]{1,0:T(8,128)(2,1)S(1)}, f32[64,128]{1,0:T(8,128)S(1)}) custom-call(f32[16,8,128]{2,1,0:T(8,128)S(1)} %get-tuple-element.70.refs_0_, bf16[256,2048]{1,0:T(8,128)(2,1)S(1)} %collective-permute-done.16.refs_1_, bf16[2048,768]{1,0:T(8,128)(2,1)S(1)} %get-tuple-element.50.refs_4_.refs_3_.refs_2_, ...), custom_call_target="tpu_custom_call" | custom-call | flops 1207959552 | bytes 1048576 | tf_op jit(solution)/shard_map/pallas_call | solution.py:167
  90.3 13.3 %all_to_all.5.returned = f32[16,8,128]{2,1,0:T(8,128)S(1)} all-to-all(f32[16,8,128]{2,1,0:T(8,128)S(1)} %get-tuple-element.71), channel_id=1, replica_groups=mesh['grp'=2,'exp'=16] {'exp'}, dimensions={0} | all-to-all | bytes 131072 | tf_op jit(solution)/shard_map/all_to_all | solution.py:305
  103.6 1.1 %shard_map.124 = (f32[256,64]{1,0:T(8,128)}, f32[8,128]{1,0:T(8,128)}) custom-call(f32[16,8,128]{2,1,0:T(8,128)S(1)} %all_to_all.5.returned, s32[8,128]{1,0:T(8,128)S(1)} %bitcast.19, bf16[256,256]{1,0:T(8,128)(2,1)S(1)} %get-tuple-element.72.refs_0_, bf16[256,384]{1,0:T(8,128)(2,1)S(1)} %get-tuple-element.73.refs_1_, ...), custom_call_target="tpu_custom_call" | custom-call | tf_op jit(solution)/shard_map/pallas_call | solution.py:307
  (15 shorter events, 0.0 us)
Async XLA Ops:
  0.6 7.2 %collective-permute-start = (bf16[128,2048]{1,0:T(8,128)(2,1)}, bf16[128,2048]{1,0:T(8,128)(2,1)S(1)}, u32[]{:S(2)}, u32[]{:S(2)}) collective-permute-start(bf16[128,2048]{1,0:T(8,128)(2,1)} %refs_1_.1), channel_id=1, source_target_pairs={{0,1},{1,0},{2,3},{3,2},{4,5},{5,4},{6,7},{7,6},{8,9},{9,8},{10,11... | collective-permute-start | bytes 1572872 | tf_op jit(solution)/shard_map/ppermute | solution.py:249
  1.1 6.7 %collective-permute-start.1 = (bf16[128,2048]{1,0:T(8,128)(2,1)}, bf16[128,2048]{1,0:T(8,128)(2,1)S(1)}, u32[]{:S(2)}, u32[]{:S(2)}) collective-permute-start(bf16[128,2048]{1,0:T(8,128)(2,1)} %refs_2_.1), channel_id=1, source_target_pairs={{0,1},{1,0},{2,3},{3,2},{4,5},{5,4},{6,7},{7,6},{8,9},{9,8},{10,11... | collective-permute-start | bytes 1572872 | tf_op jit(solution)/shard_map/ppermute | solution.py:249
  1.2 18.8 %collective-permute-start.2 = (bf16[128,2048]{1,0:T(8,128)(2,1)}, bf16[128,2048]{1,0:T(8,128)(2,1)S(1)}, u32[]{:S(2)}, u32[]{:S(2)}) collective-permute-start(bf16[128,2048]{1,0:T(8,128)(2,1)} %refs_1_.1), channel_id=1, source_target_pairs={{0,4},{1,3},{4,8},{5,1},{8,12},{9,5},{12,14},{13,9},{14,10},{15,13... | collective-permute-start | bytes 1572872 | tf_op jit(solution)/shard_map/ppermute | solution.py:246
  4.2 15.9 %collective-permute-start.3 = (bf16[128,2048]{1,0:T(8,128)(2,1)}, bf16[128,2048]{1,0:T(8,128)(2,1)S(1)}, u32[]{:S(2)}, u32[]{:S(2)}) collective-permute-start(bf16[128,2048]{1,0:T(8,128)(2,1)} %refs_2_.1), channel_id=1, source_target_pairs={{0,4},{1,3},{4,8},{5,1},{8,12},{9,5},{12,14},{13,9},{14,10},{15,13... | collective-permute-start | bytes 1572872 | tf_op jit(solution)/shard_map/ppermute | solution.py:246
  5.8 0.7 copy-start.4
  6.5 0.7 copy-start.6
  7.2 0.7 copy-start.7
  8.0 20.4 %collective-permute-start.4 = (bf16[256,2048]{1,0:T(8,128)(2,1)S(1)}, bf16[256,2048]{1,0:T(8,128)(2,1)S(1)}, u32[]{:S(2)}, u32[]{:S(2)}) collective-permute-start(bf16[256,2048]{1,0:T(8,128)(2,1)S(1)} %shard_map.114.refs_3_), channel_id=1, source_target_pairs={{0,4},{1,3},{4,8},{5,1},{8,12},{9,5},{12,14},{13,9},{14,10},{15,13... | collective-permute-start | bytes 3145736 | tf_op jit(solution)/shard_map/ppermute | solution.py:246
  9.6 1.0 copy-start
  10.6 1.0 copy-start.1
  11.7 0.9 copy-start.2
  12.6 0.9 copy-start.3
  20.2 10.3 %collective-permute-start.5 = (bf16[256,2048]{1,0:T(8,128)(2,1)S(1)}, bf16[256,2048]{1,0:T(8,128)(2,1)S(1)}, u32[]{:S(2)}, u32[]{:S(2)}) collective-permute-start(bf16[256,2048]{1,0:T(8,128)(2,1)S(1)} %shard_map.116.refs_3_), channel_id=1, source_target_pairs={{0,1},{1,0},{2,3},{3,2},{4,5},{5,4},{6,7},{7,6},{8,9},{9,8},{10,11... | collective-permute-start | bytes 3145736 | tf_op jit(solution)/shard_map/ppermute | solution.py:249
  20.3 19.3 %collective-permute-start.6 = (bf16[256,2048]{1,0:T(8,128)(2,1)S(1)}, bf16[256,2048]{1,0:T(8,128)(2,1)S(1)}, u32[]{:S(2)}, u32[]{:S(2)}) collective-permute-start(bf16[256,2048]{1,0:T(8,128)(2,1)S(1)} %shard_map.116.refs_3_), channel_id=1, source_target_pairs={{0,4},{1,3},{4,8},{5,1},{8,12},{9,5},{12,14},{13,9},{14,10},{15,13... | collective-permute-start | bytes 3145736 | tf_op jit(solution)/shard_map/ppermute | solution.py:246
  28.4 13.4 %collective-permute-start.7 = (bf16[256,2048]{1,0:T(8,128)(2,1)S(1)}, bf16[256,2048]{1,0:T(8,128)(2,1)S(1)}, u32[]{:S(2)}, u32[]{:S(2)}) collective-permute-start(bf16[256,2048]{1,0:T(8,128)(2,1)S(1)} %collective-permute-done.4.refs_1_), channel_id=1, source_target_pairs={{0,1},{1,0},{2,3},{3,2},{4,5},{5,4},{6,7},{7,6},{8,9},{9,8},{10,11... | collective-permute-start | bytes 3145736 | tf_op jit(solution)/shard_map/ppermute | solution.py:249
  28.4 22.5 %collective-permute-start.8 = (bf16[256,2048]{1,0:T(8,128)(2,1)S(1)}, bf16[256,2048]{1,0:T(8,128)(2,1)S(1)}, u32[]{:S(2)}, u32[]{:S(2)}) collective-permute-start(bf16[256,2048]{1,0:T(8,128)(2,1)S(1)} %collective-permute-done.4.refs_1_), channel_id=1, source_target_pairs={{0,4},{1,3},{4,8},{5,1},{8,12},{9,5},{12,14},{13,9},{14,10},{15,13... | collective-permute-start | bytes 3145736 | tf_op jit(solution)/shard_map/ppermute | solution.py:246
  39.6 13.4 %collective-permute-start.9 = (bf16[256,2048]{1,0:T(8,128)(2,1)S(1)}, bf16[256,2048]{1,0:T(8,128)(2,1)S(1)}, u32[]{:S(2)}, u32[]{:S(2)}) collective-permute-start(bf16[256,2048]{1,0:T(8,128)(2,1)S(1)} %collective-permute-done.6.refs_1_), channel_id=1, source_target_pairs={{0,1},{1,0},{2,3},{3,2},{4,5},{5,4},{6,7},{7,6},{8,9},{9,8},{10,11... | collective-permute-start | bytes 3145736 | tf_op jit(solution)/shard_map/ppermute | solution.py:249
  39.6 22.5 %collective-permute-start.10 = (bf16[256,2048]{1,0:T(8,128)(2,1)S(1)}, bf16[256,2048]{1,0:T(8,128)(2,1)S(1)}, u32[]{:S(2)}, u32[]{:S(2)}) collective-permute-start(bf16[256,2048]{1,0:T(8,128)(2,1)S(1)} %collective-permute-done.6.refs_1_), channel_id=1, source_target_pairs={{0,4},{1,3},{4,8},{5,1},{8,12},{9,5},{12,14},{13,9},{14,10},{15,13... | collective-permute-start | bytes 3145736 | tf_op jit(solution)/shard_map/ppermute | solution.py:246
  50.8 13.4 %collective-permute-start.11 = (bf16[256,2048]{1,0:T(8,128)(2,1)S(1)}, bf16[256,2048]{1,0:T(8,128)(2,1)S(1)}, u32[]{:S(2)}, u32[]{:S(2)}) collective-permute-start(bf16[256,2048]{1,0:T(8,128)(2,1)S(1)} %collective-permute-done.8.refs_1_), channel_id=1, source_target_pairs={{0,1},{1,0},{2,3},{3,2},{4,5},{5,4},{6,7},{7,6},{8,9},{9,8},{10,11... | collective-permute-start | bytes 3145736 | tf_op jit(solution)/shard_map/ppermute | solution.py:249
  50.8 22.5 %collective-permute-start.12 = (bf16[256,2048]{1,0:T(8,128)(2,1)S(1)}, bf16[256,2048]{1,0:T(8,128)(2,1)S(1)}, u32[]{:S(2)}, u32[]{:S(2)}) collective-permute-start(bf16[256,2048]{1,0:T(8,128)(2,1)S(1)} %collective-permute-done.8.refs_1_), channel_id=1, source_target_pairs={{0,4},{1,3},{4,8},{5,1},{8,12},{9,5},{12,14},{13,9},{14,10},{15,13... | collective-permute-start | bytes 3145736 | tf_op jit(solution)/shard_map/ppermute | solution.py:246
  62.1 11.2 %collective-permute-start.13 = (bf16[256,2048]{1,0:T(8,128)(2,1)S(1)}, bf16[256,2048]{1,0:T(8,128)(2,1)S(1)}, u32[]{:S(2)}, u32[]{:S(2)}) collective-permute-start(bf16[256,2048]{1,0:T(8,128)(2,1)S(1)} %collective-permute-done.10.refs_1_), channel_id=1, source_target_pairs={{0,1},{1,0},{2,3},{3,2},{4,5},{5,4},{6,7},{7,6},{8,9},{9,8},{10,11... | collective-permute-start | bytes 3145736 | tf_op jit(solution)/shard_map/ppermute | solution.py:249
  62.1 22.5 %collective-permute-start.14 = (bf16[256,2048]{1,0:T(8,128)(2,1)S(1)}, bf16[256,2048]{1,0:T(8,128)(2,1)S(1)}, u32[]{:S(2)}, u32[]{:S(2)}) collective-permute-start(bf16[256,2048]{1,0:T(8,128)(2,1)S(1)} %collective-permute-done.10.refs_1_), channel_id=1, source_target_pairs={{0,4},{1,3},{4,8},{5,1},{8,12},{9,5},{12,14},{13,9},{14,10},{15,13... | collective-permute-start | bytes 3145736 | tf_op jit(solution)/shard_map/ppermute | solution.py:246
  73.3 11.2 %collective-permute-start.15 = (bf16[256,2048]{1,0:T(8,128)(2,1)S(1)}, bf16[256,2048]{1,0:T(8,128)(2,1)S(1)}, u32[]{:S(2)}, u32[]{:S(2)}) collective-permute-start(bf16[256,2048]{1,0:T(8,128)(2,1)S(1)} %collective-permute-done.12.refs_1_), channel_id=1, source_target_pairs={{0,1},{1,0},{2,3},{3,2},{4,5},{5,4},{6,7},{7,6},{8,9},{9,8},{10,11... | collective-permute-start | bytes 3145736 | tf_op jit(solution)/shard_map/ppermute | solution.py:249
  84.5 3.3 %collective-permute-start.16 = (bf16[256,2048]{1,0:T(8,128)(2,1)S(1)}, bf16[256,2048]{1,0:T(8,128)(2,1)S(1)}, u32[]{:S(2)}, u32[]{:S(2)}) collective-permute-start(bf16[256,2048]{1,0:T(8,128)(2,1)S(1)} %collective-permute-done.14.refs_1_), channel_id=1, source_target_pairs={{0,1},{1,0},{2,3},{3,2},{4,5},{5,4},{6,7},{7,6},{8,9},{9,8},{10,11... | collective-permute-start | bytes 3145736 | tf_op jit(solution)/shard_map/ppermute | solution.py:249
  87.9 15.7 %copy-start.5 = (s32[128,8]{0,1:T(8,128)S(1)}, s32[128,8]{0,1:T(8,128)}, u32[]{:S(2)}) copy-start(s32[128,8]{0,1:T(8,128)} %param.12) | copy-start | bytes 12292

commit v12 on v11

--- a/solution.py
+++ b/solution.py
@@ -167,6 +167,114 @@
     return call(sheet, *apart, *block_in, *weights)
 
 
+def front_kernel(*refs):
+    blocks = len(refs) - 7
+    x_in = refs[:blocks]
+    w_gate, w_up, low_proj, hidden, low_side, x_all, low_sum = refs[blocks:]
+    rows = x_in[0].shape[0]
+    for i in range(blocks):
+        x_all[i * rows : (i + 1) * rows, :] = x_in[i][...]
+    units = w_gate.shape[1]
+    tile = 256 if units % 256 == 0 else units
+    for cut in range(0, units, tile):
+        part = pl.ds(cut, tile)
+        gate_val = jnp.dot(x_all[...], w_gate[:, part], preferred_element_type=jnp.float32)
+        up_val = jnp.dot(x_all[...], w_up[:, part], preferred_element_type=jnp.float32)
+        piece = (jax.nn.silu(gate_val) * up_val).astype(jnp.bfloat16)
+        hidden[:, part] = piece
+        low = lax.dot_general(
+            low_proj[:, part],
+            piece,
+            (((1,), (1,)), ((), ())),
+            preferred_element_type=jnp.float32,
+        )
+        low_sum[...] = low if cut == 0 else low_sum[...] + low
+    low_side[...] = low_sum[...].astype(low_side.dtype)
+
+
+def front(x_in, weights):
+    w_gate, w_up, _, low_proj, _ = weights
+    rows, width = len(x_in) * x_in[0].shape[0], x_in[0].shape[1]
+    units = w_gate.shape[1]
+    inside = pl.BlockSpec(memory_space=pltpu.VMEM)
+    return pl.pallas_call(
+        front_kernel,
+        out_shape=[
+            jax.ShapeDtypeStruct((rows, units), jnp.bfloat16),
+            jax.ShapeDtypeStruct((low_proj.shape[0], rows), jnp.bfloat16),
+        ],
+        in_specs=[inside] * (len(x_in) + 3),
+        out_specs=[inside] * 2,
+        scratch_shapes=[
+            pltpu.VMEM((rows, width), jnp.bfloat16),
+            pltpu.VMEM((low_proj.shape[0], rows), jnp.float32),
+        ],
+        compiler_params=pltpu.CompilerParams(vmem_limit_bytes=16 * 1024 * 1024),
+        cost_estimate=pl.CostEstimate(
+            flops=4 * rows * width * units,
+            bytes_accessed=2 * rows * width,
+            transcendentals=rows * units,
+        ),
+    )(*x_in, w_gate, w_up, low_proj)
+
+
+def back_kernel(names, *refs):
+    blocks = len(names)
+    sheet_in, dy_in = refs[0], refs[1 : 1 + blocks]
+    hidden, w_down, high_proj, sheet, proj_cot, dy_all, grad_sum = refs[1 + blocks :]
+    rows = dy_in[0].shape[0]
+    across = (((1,), (1,)), ((), ()))
+    for i in range(blocks):
+        dy_all[i * rows : (i + 1) * rows, :] = dy_in[i][...]
+    units, lanes = hidden.shape[1], grad_sum.shape[1]
+    tile = 256 if units % 256 == 0 else units
+    for cut in range(0, units, tile):
+        part = pl.ds(cut, tile)
+        back = lax.dot_general(
+            dy_all[...], w_down[part, :], across, preferred_element_type=jnp.float32
+        )
+        terms = hidden[:, part].astype(jnp.float32) * back
+        total = terms[:, :lanes]
+        for spot in range(lanes, tile, lanes):
+            total += terms[:, spot : spot + lanes]
+        grad_sum[...] = total if cut == 0 else grad_sum[...] + total
+    proj_cot[...] = lax.dot_general(
+        high_proj[...], dy_all[...], across, preferred_element_type=jnp.float32
+    )
+    sheet[...] = sheet_in[...]
+    for i in range(blocks):
+        total = jnp.sum(
+            jnp.transpose(grad_sum[i * rows : (i + 1) * rows, :]), axis=0, keepdims=True
+        )
+        sheet[block_owner(names[i], sheet.shape[0] // 2), 0:1, :] = total
+
+
+def finish_late(names, sheet, dy_in, hidden, weights):
+    _, _, w_down, _, high_proj = weights
+    rows, width = len(dy_in) * dy_in[0].shape[0], dy_in[0].shape[1]
+    units = hidden.shape[1]
+    inside = pl.BlockSpec(memory_space=pltpu.VMEM)
+    return pl.pallas_call(
+        functools.partial(back_kernel, names),
+        out_shape=[
+            jax.ShapeDtypeStruct(sheet.shape, jnp.float32),
+            jax.ShapeDtypeStruct((high_proj.shape[0], rows), jnp.float32),
+        ],
+        in_specs=[inside] * (len(dy_in) + 4),
+        out_specs=[inside] * 2,
+        scratch_shapes=[
+            pltpu.VMEM((rows, width), jnp.bfloat16),
+            pltpu.VMEM((rows, 128), jnp.float32),
+        ],
+        compiler_params=pltpu.CompilerParams(vmem_limit_bytes=16 * 1024 * 1024),
+        cost_estimate=pl.CostEstimate(
+            flops=2 * rows * width * units,
+            bytes_accessed=2 * rows * width,
+            transcendentals=0,
+        ),
+    )(sheet, *dy_in, hidden, w_down, high_proj)
+
+
 def outcome_kernel(jobs, returned, routes, *refs):
     low_in, proj_in = refs[: len(jobs)], refs[len(jobs) : 2 * len(jobs)]
     feat, route_grad = refs[-2:]
@@ -227,6 +335,24 @@
     )(top, bottom)
 
 
+def split_kernel(cuts, block, *parts):
+    for (begin, count), part in zip(cuts, parts):
+        part[...] = block[begin : begin + count, :]
+
+
+def split(block, cuts):
+    inside = pl.BlockSpec(memory_space=pltpu.VMEM)
+    return pl.pallas_call(
+        functools.partial(split_kernel, cuts),
+        out_shape=[
+            jax.ShapeDtypeStruct((count, block.shape[1]), block.dtype) for _, count in cuts
+        ],
+        in_specs=[inside],
+        out_specs=[inside] * len(cuts),
+        compiler_params=pltpu.CompilerParams(vmem_limit_bytes=8 * 1024 * 1024),
+    )(block)
+
+
 def by_ring(
     tokens, cotangent, routes, combine, doc_ids, w_gate, w_up, w_down, proj_hidden, proj_output
 ):
@@ -256,9 +382,10 @@
             job += (arrivals[i - 1] + (True,),)
         if i == 1:
             job += (arrivals[0] + (False,),)
-        if i != 0:
+        if i == len(arrivals) - 1:
+            jobs += [job[1:], (job[0], (c, step, True))]
+        elif i != 0:
             jobs.append(job)
-    jobs.append((arrivals[-1] + (True,),))
 
     sheet = pl.pallas_call(
         facts_kernel,
@@ -291,7 +418,7 @@
         projs.append(proj_cot)
 
     chain = {"b": beside}
-    for i, (c, step) in enumerate(arrivals):
+    for i, (c, step) in enumerate(arrivals[:-1]):
         block = hop(chain[c]) if i > 0 else first
         if i != 1:
             take()
@@ -300,8 +427,19 @@
             block = stack(*block)
         chain[c] = held[(c, step, False)] = block
         held[(c, step, True)] = swap(block)
-    while todo:
-        take()
+    cut = tok_rows // 2
+    *x, dy = split(chain["a"], ((0, cut), (cut, cut), (tok_rows, tok_rows)))
+    dy, _ = lax.optimization_barrier((dy, chain["b"]))
+    x, dy = [hop(part) for part in x], hop(dy)
+    take()
+    sheet, x = lax.optimization_barrier((sheet, x))
+    hidden, low_side = front(x + [swap(part) for part in x], weights)
+    hidden, dy = lax.optimization_barrier((hidden, dy))
+    dy_beside = swap(dy)
+    take()
+    sheet, proj_cot = finish_late(todo.pop(0), sheet, [dy, dy_beside], hidden, weights)
+    lows.append(low_side)
+    projs.append(proj_cot)
     returned = lax.all_to_all(sheet, "exp", split_axis=0, concat_axis=0, tiled=True)
     rank = proj_output.shape[2]
     feature, route_grad = pl.pallas_call(

time: 105 us -> 103 us (0.981)
  waiting for transfers between devices: 36.3 us -> 29.6 us
  starting transfers between devices: 16.9 us -> 21.1 us
    ppermute x8 -> x10, waiting for transfers between devices: 36.3 us -> 28.1 us  [hop(): return lax.ppermute(block, 'exp', onward)]
    pallas_call x0 -> x3, Pallas kernels: none -> 3.9 us  [the longest x1 2.45 us: front(): pl.pallas_call(front_kernel, out_shape=[jax.ShapeDtypeStruct((rows, units...]
    ppermute x8 -> x10, starting transfers between devices: 16.2 us -> 19.9 us  [hop(): return lax.ppermute(block, 'exp', onward)]
    pallas_call x8 -> x7, Pallas kernels: 30.3 us -> 26.9 us  [work(): return call(sheet, *apart, *block_in, *weights)]
    ppermute x9 -> x11, waiting for transfers between devices: 0.02 us -> 1.42 us  [swap(): return lax.ppermute(block, 'exp', across)]
  transfers between devices with their start and end apart: 17 -> 21, of which waited for: 6 -> 9; matrix products, arithmetic and copies ran while one was open for 0% -> 0% of each run, Pallas kernels for 27% -> 29%
where the time goes in v12:
time: 103 us
  Pallas kernels  32.1 us (31%)
  waiting for transfers between devices  29.6 us (29%)
  starting transfers between devices  21.1 us (20%)
  blocking collectives  13.3 us (13%)
  local copies, waits for them, and re-layouts  5.98 us (6%)
    ppermute x10, waiting for transfers between devices, hop(): return lax.ppermute(block, 'exp', onward)  28.1 us
    pallas_call x7, Pallas kernels, work(): return call(sheet, *apart, *block_in, *weights)  26.9 us
    ppermute x10, starting transfers between devices, hop(): return lax.ppermute(block, 'exp', onward)  19.9 us
    all_to_all x1, blocking collectives, by_ring(): lax.all_to_all(sheet, 'exp', split_axis=0, concat_axis=0, tiled=True)  13.3 us
    unnamed x16, local copies, waits for them, and re-layouts  5.98 us
    pallas_call x1, Pallas kernels, front(): pl.pallas_call(front_kernel, out_shape=[jax.ShapeDtypeStruct((rows, units...  2.45 us
  transfers between devices with their start and end apart: 21, of which 9 were waited for; matrix products, arithmetic and copies ran while one was open for 0% of the time, Pallas kernels for 29%

profile of v12, /device:TPU:0, one launch (start us, length us, event | category | flops | bytes accessed | tf_op | source)
XLA Modules:
  0.0 102.8 jit_solution(17414945096211961478)
XLA Ops:
  0.6 0.5 collective-permute-start
  1.1 0.1 collective-permute-start.1
  1.2 3.0 %collective-permute-start.2 = (bf16[128,2048]{1,0:T(8,128)(2,1)}, bf16[128,2048]{1,0:T(8,128)(2,1)S(1)}, u32[]{:S(2)}, u32[]{:S(2)}) collective-permute-start(bf16[128,2048]{1,0:T(8,128)(2,1)} %refs_1_.1), channel_id=1, source_target_pairs={{0,4},{1,3},{4,8},{5,1},{8,12},{9,5},{12,14},{13,9},{14,10},{15,13... | collective-permute-start | bytes 1572872 | tf_op jit(solution)/shard_map/ppermute | solution.py:372
  4.2 1.6 %collective-permute-start.3 = (bf16[128,2048]{1,0:T(8,128)(2,1)}, bf16[128,2048]{1,0:T(8,128)(2,1)S(1)}, u32[]{:S(2)}, u32[]{:S(2)}) collective-permute-start(bf16[128,2048]{1,0:T(8,128)(2,1)} %refs_2_.1), channel_id=1, source_target_pairs={{0,4},{1,3},{4,8},{5,1},{8,12},{9,5},{12,14},{13,9},{14,10},{15,13... | collective-permute-start | bytes 1572872 | tf_op jit(solution)/shard_map/ppermute | solution.py:372
  5.8 0.7 copy-done.4
  6.5 0.7 copy-done.6
  7.2 0.7 copy-done.7
  7.9 0.0 collective-permute-done.top
  7.9 0.1 shard_map.114.refs_3_
  8.0 1.6 %collective-permute-start.4 = (bf16[256,2048]{1,0:T(8,128)(2,1)S(1)}, bf16[256,2048]{1,0:T(8,128)(2,1)S(1)}, u32[]{:S(2)}, u32[]{:S(2)}) collective-permute-start(bf16[256,2048]{1,0:T(8,128)(2,1)S(1)} %shard_map.114.refs_3_), channel_id=1, source_target_pairs={{0,4},{1,3},{4,8},{5,1},{8,12},{9,5},{12,14},{13,9},{14,10},{15,13... | collective-permute-start | bytes 3145736 | tf_op jit(solution)/shard_map/ppermute | solution.py:372
  9.6 1.0 %copy-done = bf16[128,2048]{1,0:T(8,128)(2,1)S(1)} copy-done((bf16[128,2048]{1,0:T(8,128)(2,1)S(1)}, bf16[128,2048]{1,0:T(8,128)(2,1)}, u32[]{:S(2)}) %copy-start) | copy-done | bytes 524312
  10.6 1.0 %copy-done.1 = bf16[128,2048]{1,0:T(8,128)(2,1)S(1)} copy-done((bf16[128,2048]{1,0:T(8,128)(2,1)S(1)}, bf16[128,2048]{1,0:T(8,128)(2,1)}, u32[]{:S(2)}) %copy-start.1) | copy-done | bytes 524312
  11.7 0.9 copy-done.2
  12.6 0.9 copy-done.3
  13.5 6.6 %shard_map.115 = (f32[16,8,128]{2,1,0:T(8,128)S(1)}, bf16[256,256]{1,0:T(8,128)(2,1)S(1)}, f32[64,256]{1,0:T(8,128)S(1)}, bf16[2048,768]{1,0:T(8,128)(2,1)S(1)},...) custom-call(f32[16,8,128]{2,1,0:T(8,128)S(1)} %shard_map.113.refs_0_, ...), custom_call_target="tpu_custom_call" | custom-call | flops 2415919104 | bytes 2097152 | tf_op jit(solution)/shard_map/pallas_call | solution.py:167
  20.1 0.0 collective-permute-done.3.bottom
  20.1 0.1 shard_map.116.refs_3_
  20.2 0.1 collective-permute-start.5
  20.3 1.5 %collective-permute-start.6 = (bf16[256,2048]{1,0:T(8,128)(2,1)S(1)}, bf16[256,2048]{1,0:T(8,128)(2,1)S(1)}, u32[]{:S(2)}, u32[]{:S(2)}) collective-permute-start(bf16[256,2048]{1,0:T(8,128)(2,1)S(1)} %shard_map.116.refs_3_), channel_id=1, source_target_pairs={{0,4},{1,3},{4,8},{5,1},{8,12},{9,5},{12,14},{13,9},{14,10},{15,13... | collective-permute-start | bytes 3145736 | tf_op jit(solution)/shard_map/ppermute | solution.py:372
  21.8 6.6 %collective-permute-done.4.refs_1_ = bf16[256,2048]{1,0:T(8,128)(2,1)S(1)} collective-permute-done((bf16[256,2048]{1,0:T(8,128)(2,1)S(1)}, bf16[256,2048]{1,0:T(8,128)(2,1)S(1)}, u32[]{:S(2)}, u32[]{:S(2)}) %collective-permute-start.4) | collective-permute-done | bytes 1048608 | tf_op jit(solution)/shard_map/ppermute | solution.py:372
  28.4 2.1 %collective-permute-start.8 = (bf16[256,2048]{1,0:T(8,128)(2,1)S(1)}, bf16[256,2048]{1,0:T(8,128)(2,1)S(1)}, u32[]{:S(2)}, u32[]{:S(2)}) collective-permute-start(bf16[256,2048]{1,0:T(8,128)(2,1)S(1)} %collective-permute-done.4.refs_1_), channel_id=1, source_target_pairs={{0,4},{1,3},{4,8},{5,1},{8,12},{9,5},{12,14},{13,9},{14,10},{15,13... | collective-permute-start | bytes 3145736 | tf_op jit(solution)/shard_map/ppermute | solution.py:372
  30.5 4.6 %shard_map.117 = (f32[16,8,128]{2,1,0:T(8,128)S(1)}, bf16[256,384]{1,0:T(8,128)(2,1)S(1)}, f32[64,384]{1,0:T(8,128)S(1)}) custom-call(f32[16,8,128]{2,1,0:T(8,128)S(1)} %get-tuple-element.55.refs_0_, bf16[256,2048]{1,0:T(8,128)(2,1)S(1)} %collective-permute-done.4.refs_1_, bf16[256,2048]{1,0:T(8,128)(2,1)S(1)} %collective-permute-done.5.refs_2_, ...), custom_call_target="tpu_custom_call" | custom-call | flops 3623878656 | bytes 3145728 | tf_op jit(solution)/shard_map/pallas_call | solution.py:167
  35.1 4.5 %collective-permute-done.6.refs_1_ = bf16[256,2048]{1,0:T(8,128)(2,1)S(1)} collective-permute-done((bf16[256,2048]{1,0:T(8,128)(2,1)S(1)}, bf16[256,2048]{1,0:T(8,128)(2,1)S(1)}, u32[]{:S(2)}, u32[]{:S(2)}) %collective-permute-start.6) | collective-permute-done | bytes 1048608 | tf_op jit(solution)/shard_map/ppermute | solution.py:372
  39.6 2.1 %collective-permute-start.10 = (bf16[256,2048]{1,0:T(8,128)(2,1)S(1)}, bf16[256,2048]{1,0:T(8,128)(2,1)S(1)}, u32[]{:S(2)}, u32[]{:S(2)}) collective-permute-start(bf16[256,2048]{1,0:T(8,128)(2,1)S(1)} %collective-permute-done.6.refs_1_), channel_id=1, source_target_pairs={{0,4},{1,3},{4,8},{5,1},{8,12},{9,5},{12,14},{13,9},{14,10},{15,13... | collective-permute-start | bytes 3145736 | tf_op jit(solution)/shard_map/ppermute | solution.py:372
  41.7 3.3 %shard_map.118 = (f32[16,8,128]{2,1,0:T(8,128)S(1)}, bf16[256,256]{1,0:T(8,128)(2,1)S(1)}, f32[64,256]{1,0:T(8,128)S(1)}) custom-call(f32[16,8,128]{2,1,0:T(8,128)S(1)} %get-tuple-element.64.refs_0_, bf16[256,2048]{1,0:T(8,128)(2,1)S(1)} %collective-permute-done.6.refs_1_, bf16[256,2048]{1,0:T(8,128)(2,1)S(1)} %collective-permute-done.7.refs_2_, ...), custom_call_target="tpu_custom_call" | custom-call | flops 2415919104 | bytes 2097152 | tf_op jit(solution)/shard_map/pallas_call | solution.py:167
  45.0 5.8 %collective-permute-done.8.refs_1_ = bf16[256,2048]{1,0:T(8,128)(2,1)S(1)} collective-permute-done((bf16[256,2048]{1,0:T(8,128)(2,1)S(1)}, bf16[256,2048]{1,0:T(8,128)(2,1)S(1)}, u32[]{:S(2)}, u32[]{:S(2)}) %collective-permute-start.8) | collective-permute-done | bytes 1048608 | tf_op jit(solution)/shard_map/ppermute | solution.py:372
  50.8 2.1 %collective-permute-start.12 = (bf16[256,2048]{1,0:T(8,128)(2,1)S(1)}, bf16[256,2048]{1,0:T(8,128)(2,1)S(1)}, u32[]{:S(2)}, u32[]{:S(2)}) collective-permute-start(bf16[256,2048]{1,0:T(8,128)(2,1)S(1)} %collective-permute-done.8.refs_1_), channel_id=1, source_target_pairs={{0,4},{1,3},{4,8},{5,1},{8,12},{9,5},{12,14},{13,9},{14,10},{15,13... | collective-permute-start | bytes 3145736 | tf_op jit(solution)/shard_map/ppermute | solution.py:372
  53.0 3.3 %shard_map.119 = (f32[16,8,128]{2,1,0:T(8,128)S(1)}, bf16[256,256]{1,0:T(8,128)(2,1)S(1)}, f32[64,256]{1,0:T(8,128)S(1)}) custom-call(f32[16,8,128]{2,1,0:T(8,128)S(1)} %get-tuple-element.67.refs_0_, bf16[256,2048]{1,0:T(8,128)(2,1)S(1)} %collective-permute-done.8.refs_1_, bf16[256,2048]{1,0:T(8,128)(2,1)S(1)} %collective-permute-done.9.refs_2_, ...), custom_call_target="tpu_custom_call" | custom-call | flops 2415919104 | bytes 2097152 | tf_op jit(solution)/shard_map/pallas_call | solution.py:167
  56.3 5.8 %collective-permute-done.10.refs_1_.block = bf16[256,2048]{1,0:T(8,128)(2,1)S(1)} collective-permute-done((bf16[256,2048]{1,0:T(8,128)(2,1)S(1)}, bf16[256,2048]{1,0:T(8,128)(2,1)S(1)}, u32[]{:S(2)}, u32[]{:S(2)}) %collective-permute-start.10) | collective-permute-done | bytes 1048608 | tf_op jit(solution)/shard_map/ppermute | solution.py:372
  62.1 0.1 shard_map.122
  62.1 2.2 %collective-permute-start.14 = (bf16[64,2048]{1,0:T(8,128)(2,1)S(1)}, bf16[64,2048]{1,0:T(8,128)(2,1)S(1)}, u32[]{:S(2)}, u32[]{:S(2)}) collective-permute-start(bf16[64,2048]{1,0:T(8,128)(2,1)S(1)} %get-tuple-element.76), channel_id=1, source_target_pairs={{0,4},{1,3},{4,8},{5,1},{8,12},{9,5},{12,14},{13,9},{14,10},{15,13... | collective-permute-start | bytes 786440 | tf_op jit(solution)/shard_map/ppermute | solution.py:372
  64.3 1.6 %collective-permute-start.15 = (bf16[64,2048]{1,0:T(8,128)(2,1)S(1)}, bf16[64,2048]{1,0:T(8,128)(2,1)S(1)}, u32[]{:S(2)}, u32[]{:S(2)}) collective-permute-start(bf16[64,2048]{1,0:T(8,128)(2,1)S(1)} %get-tuple-element.77), channel_id=1, source_target_pairs={{0,4},{1,3},{4,8},{5,1},{8,12},{9,5},{12,14},{13,9},{14,10},{15,13... | collective-permute-start | bytes 786440 | tf_op jit(solution)/shard_map/ppermute | solution.py:372
  65.9 3.3 %shard_map.120 = (f32[16,8,128]{2,1,0:T(8,128)S(1)}, bf16[256,256]{1,0:T(8,128)(2,1)S(1)}, f32[64,256]{1,0:T(8,128)S(1)}) custom-call(f32[16,8,128]{2,1,0:T(8,128)S(1)} %get-tuple-element.70.refs_0_, bf16[256,2048]{1,0:T(8,128)(2,1)S(1)} %collective-permute-done.10.refs_1_.block, bf16[256,2048]{1,0:T(8,128)(2,1)S(1)} %collective-permute-done.11.refs_2_, ...), custom_call_target="tpu_custom_call" | custom-call | flops 2415919104 | bytes 2097152 | tf_op jit(solution)/shard_map/pallas_call | solution.py:167
  69.2 4.1 %collective-permute-done.12.refs_1_ = bf16[256,2048]{1,0:T(8,128)(2,1)S(1)} collective-permute-done((bf16[256,2048]{1,0:T(8,128)(2,1)S(1)}, bf16[256,2048]{1,0:T(8,128)(2,1)S(1)}, u32[]{:S(2)}, u32[]{:S(2)}) %collective-permute-start.12) | collective-permute-done | bytes 1048608 | tf_op jit(solution)/shard_map/ppermute | solution.py:372
  73.3 2.1 %collective-permute-start.19 = (bf16[128,2048]{1,0:T(8,128)(2,1)S(1)}, bf16[128,2048]{1,0:T(8,128)(2,1)S(1)}, u32[]{:S(2)}, u32[]{:S(2)}) collective-permute-start(bf16[128,2048]{1,0:T(8,128)(2,1)S(1)} %get-tuple-element.84), channel_id=1, source_target_pairs={{0,4},{1,3},{4,8},{5,1},{8,12},{9,5},{12,14},{13,9},{14,10},{15,13... | collective-permute-start | bytes 1572872 | tf_op jit(solution)/shard_map/ppermute | solution.py:372
  75.4 3.3 %shard_map.121 = (f32[16,8,128]{2,1,0:T(8,128)S(1)}, bf16[256,256]{1,0:T(8,128)(2,1)S(1)}, f32[64,256]{1,0:T(8,128)S(1)}) custom-call(f32[16,8,128]{2,1,0:T(8,128)S(1)} %get-tuple-element.73.refs_0_, bf16[256,2048]{1,0:T(8,128)(2,1)S(1)} %collective-permute-done.12.refs_1_, bf16[256,2048]{1,0:T(8,128)(2,1)S(1)} %collective-permute-done.13.refs_2_, ...), custom_call_target="tpu_custom_call" | custom-call | flops 2415919104 | bytes 2097152 | tf_op jit(solution)/shard_map/pallas_call | solution.py:167
  78.8 0.2 collective-permute-done.15.refs_1_
  78.9 0.1 collective-permute-start.17
  79.0 0.5 collective-permute-start.18
  79.4 1.0 collective-permute-done.17.refs_2_
  80.5 0.4 collective-permute-done.18.refs_3_
  80.8 2.5 %shard_map.124 = (bf16[256,768]{1,0:T(8,128)(2,1)S(1)}, bf16[256,256]{1,0:T(8,128)(2,1)S(1)}) custom-call(bf16[64,2048]{1,0:T(8,128)(2,1)S(1)} %collective-permute-done.14.refs_0_, bf16[64,2048]{1,0:T(8,128)(2,1)S(1)} %collective-permute-done.15.refs_1_, bf16[64,2048]{1,0:T(8,128)(2,1)S(1)} %collective-permute-done.17.refs_2_, ...), custom_call_target="tpu_custom_call" | custom-call | flops 1610612736 | bytes 1048576 | tf_op jit(solution)/shard_map/pallas_call | solution.py:200
  83.3 1.2 %collective-permute-done.19.refs_1_ = bf16[128,2048]{1,0:T(8,128)(2,1)S(1)} collective-permute-done((bf16[128,2048]{1,0:T(8,128)(2,1)S(1)}, bf16[128,2048]{1,0:T(8,128)(2,1)S(1)}, u32[]{:S(2)}, u32[]{:S(2)}) %collective-permute-start.19) | collective-permute-done | bytes 524320 | tf_op jit(solution)/shard_map/ppermute | solution.py:372
  84.5 2.4 %shard_map.123 = (f32[16,8,128]{2,1,0:T(8,128)S(1)}, bf16[256,128]{1,0:T(8,128)(2,1)S(1)}, f32[64,128]{1,0:T(8,128)S(1)}) custom-call(f32[16,8,128]{2,1,0:T(8,128)S(1)} %get-tuple-element.78.refs_0_, bf16[256,2048]{1,0:T(8,128)(2,1)S(1)} %collective-permute-done.16.refs_1_, bf16[2048,768]{1,0:T(8,128)(2,1)S(1)} %get-tuple-element.58.refs_4_.refs_3_.refs_2_, ...), custom_call_target="tpu_custom_call" | custom-call | flops 1207959552 | bytes 1048576 | tf_op jit(solution)/shard_map/pallas_call | solution.py:167
  87.0 0.0 copy-start.5
  87.0 1.4 %shard_map.125 = (f32[16,8,128]{2,1,0:T(8,128)S(1)}, f32[64,256]{1,0:T(8,128)S(1)}) custom-call(f32[16,8,128]{2,1,0:T(8,128)S(1)} %get-tuple-element.79.refs_0_, bf16[128,2048]{1,0:T(8,128)(2,1)S(1)} %collective-permute-done.19.refs_1_, bf16[128,2048]{1,0:T(8,128)(2,1)S(1)} %collective-permute-done.20.refs_2_, ...), custom_call_target="tpu_custom_call" | custom-call | flops 805306368 | bytes 1048576 | tf_op jit(solution)/shard_map/pallas_call | solution.py:257
  88.4 13.3 %all_to_all.5.returned = f32[16,8,128]{2,1,0:T(8,128)S(1)} all-to-all(f32[16,8,128]{2,1,0:T(8,128)S(1)} %get-tuple-element.87), channel_id=1, replica_groups=mesh['grp'=2,'exp'=16] {'exp'}, dimensions={0} | all-to-all | bytes 131072 | tf_op jit(solution)/shard_map/all_to_all | solution.py:443
  101.7 1.1 %shard_map.126 = (f32[256,64]{1,0:T(8,128)}, f32[8,128]{1,0:T(8,128)}) custom-call(f32[16,8,128]{2,1,0:T(8,128)S(1)} %all_to_all.5.returned, s32[8,128]{1,0:T(8,128)S(1)} %bitcast.19, bf16[256,256]{1,0:T(8,128)(2,1)S(1)} %get-tuple-element.88.refs_0_, bf16[256,384]{1,0:T(8,128)(2,1)S(1)} %get-tuple-element.89.refs_1_, ...), custom_call_target="tpu_custom_call" | custom-call | tf_op jit(solution)/shard_map/pallas_call | solution.py:445
  (25 shorter events, 0.1 us)
Async XLA Ops:
  0.6 7.2 %collective-permute-start = (bf16[128,2048]{1,0:T(8,128)(2,1)}, bf16[128,2048]{1,0:T(8,128)(2,1)S(1)}, u32[]{:S(2)}, u32[]{:S(2)}) collective-permute-start(bf16[128,2048]{1,0:T(8,128)(2,1)} %refs_1_.1), channel_id=1, source_target_pairs={{0,1},{1,0},{2,3},{3,2},{4,5},{5,4},{6,7},{7,6},{8,9},{9,8},{10,11... | collective-permute-start | bytes 1572872 | tf_op jit(solution)/shard_map/ppermute | solution.py:375
  1.1 6.7 %collective-permute-start.1 = (bf16[128,2048]{1,0:T(8,128)(2,1)}, bf16[128,2048]{1,0:T(8,128)(2,1)S(1)}, u32[]{:S(2)}, u32[]{:S(2)}) collective-permute-start(bf16[128,2048]{1,0:T(8,128)(2,1)} %refs_2_.1), channel_id=1, source_target_pairs={{0,1},{1,0},{2,3},{3,2},{4,5},{5,4},{6,7},{7,6},{8,9},{9,8},{10,11... | collective-permute-start | bytes 1572872 | tf_op jit(solution)/shard_map/ppermute | solution.py:375
  1.2 18.8 %collective-permute-start.2 = (bf16[128,2048]{1,0:T(8,128)(2,1)}, bf16[128,2048]{1,0:T(8,128)(2,1)S(1)}, u32[]{:S(2)}, u32[]{:S(2)}) collective-permute-start(bf16[128,2048]{1,0:T(8,128)(2,1)} %refs_1_.1), channel_id=1, source_target_pairs={{0,4},{1,3},{4,8},{5,1},{8,12},{9,5},{12,14},{13,9},{14,10},{15,13... | collective-permute-start | bytes 1572872 | tf_op jit(solution)/shard_map/ppermute | solution.py:372
  4.2 15.9 %collective-permute-start.3 = (bf16[128,2048]{1,0:T(8,128)(2,1)}, bf16[128,2048]{1,0:T(8,128)(2,1)S(1)}, u32[]{:S(2)}, u32[]{:S(2)}) collective-permute-start(bf16[128,2048]{1,0:T(8,128)(2,1)} %refs_2_.1), channel_id=1, source_target_pairs={{0,4},{1,3},{4,8},{5,1},{8,12},{9,5},{12,14},{13,9},{14,10},{15,13... | collective-permute-start | bytes 1572872 | tf_op jit(solution)/shard_map/ppermute | solution.py:372
  5.8 0.7 copy-start.4
  6.5 0.7 copy-start.6
  7.2 0.7 copy-start.7
  8.0 20.4 %collective-permute-start.4 = (bf16[256,2048]{1,0:T(8,128)(2,1)S(1)}, bf16[256,2048]{1,0:T(8,128)(2,1)S(1)}, u32[]{:S(2)}, u32[]{:S(2)}) collective-permute-start(bf16[256,2048]{1,0:T(8,128)(2,1)S(1)} %shard_map.114.refs_3_), channel_id=1, source_target_pairs={{0,4},{1,3},{4,8},{5,1},{8,12},{9,5},{12,14},{13,9},{14,10},{15,13... | collective-permute-start | bytes 3145736 | tf_op jit(solution)/shard_map/ppermute | solution.py:372
  9.6 1.0 %copy-start = (bf16[128,2048]{1,0:T(8,128)(2,1)S(1)}, bf16[128,2048]{1,0:T(8,128)(2,1)}, u32[]{:S(2)}) copy-start(bf16[128,2048]{1,0:T(8,128)(2,1)} %refs_1_.1) | copy-start | bytes 1572868
  10.6 1.0 %copy-start.1 = (bf16[128,2048]{1,0:T(8,128)(2,1)S(1)}, bf16[128,2048]{1,0:T(8,128)(2,1)}, u32[]{:S(2)}) copy-start(bf16[128,2048]{1,0:T(8,128)(2,1)} %refs_2_.1) | copy-start | bytes 1572868
  11.7 0.9 copy-start.2
  12.6 0.9 copy-start.3
  20.2 10.3 %collective-permute-start.5 = (bf16[256,2048]{1,0:T(8,128)(2,1)S(1)}, bf16[256,2048]{1,0:T(8,128)(2,1)S(1)}, u32[]{:S(2)}, u32[]{:S(2)}) collective-permute-start(bf16[256,2048]{1,0:T(8,128)(2,1)S(1)} %shard_map.116.refs_3_), channel_id=1, source_target_pairs={{0,1},{1,0},{2,3},{3,2},{4,5},{5,4},{6,7},{7,6},{8,9},{9,8},{10,11... | collective-permute-start | bytes 3145736 | tf_op jit(solution)/shard_map/ppermute | solution.py:375
  20.3 19.3 %collective-permute-start.6 = (bf16[256,2048]{1,0:T(8,128)(2,1)S(1)}, bf16[256,2048]{1,0:T(8,128)(2,1)S(1)}, u32[]{:S(2)}, u32[]{:S(2)}) collective-permute-start(bf16[256,2048]{1,0:T(8,128)(2,1)S(1)} %shard_map.116.refs_3_), channel_id=1, source_target_pairs={{0,4},{1,3},{4,8},{5,1},{8,12},{9,5},{12,14},{13,9},{14,10},{15,13... | collective-permute-start | bytes 3145736 | tf_op jit(solution)/shard_map/ppermute | solution.py:372
  28.4 13.4 %collective-permute-start.7 = (bf16[256,2048]{1,0:T(8,128)(2,1)S(1)}, bf16[256,2048]{1,0:T(8,128)(2,1)S(1)}, u32[]{:S(2)}, u32[]{:S(2)}) collective-permute-start(bf16[256,2048]{1,0:T(8,128)(2,1)S(1)} %collective-permute-done.4.refs_1_), channel_id=1, source_target_pairs={{0,1},{1,0},{2,3},{3,2},{4,5},{5,4},{6,7},{7,6},{8,9},{9,8},{10,11... | collective-permute-start | bytes 3145736 | tf_op jit(solution)/shard_map/ppermute | solution.py:375
  28.4 22.5 %collective-permute-start.8 = (bf16[256,2048]{1,0:T(8,128)(2,1)S(1)}, bf16[256,2048]{1,0:T(8,128)(2,1)S(1)}, u32[]{:S(2)}, u32[]{:S(2)}) collective-permute-start(bf16[256,2048]{1,0:T(8,128)(2,1)S(1)} %collective-permute-done.4.refs_1_), channel_id=1, source_target_pairs={{0,4},{1,3},{4,8},{5,1},{8,12},{9,5},{12,14},{13,9},{14,10},{15,13... | collective-permute-start | bytes 3145736 | tf_op jit(solution)/shard_map/ppermute | solution.py:372
  39.6 13.4 %collective-permute-start.9 = (bf16[256,2048]{1,0:T(8,128)(2,1)S(1)}, bf16[256,2048]{1,0:T(8,128)(2,1)S(1)}, u32[]{:S(2)}, u32[]{:S(2)}) collective-permute-start(bf16[256,2048]{1,0:T(8,128)(2,1)S(1)} %collective-permute-done.6.refs_1_), channel_id=1, source_target_pairs={{0,1},{1,0},{2,3},{3,2},{4,5},{5,4},{6,7},{7,6},{8,9},{9,8},{10,11... | collective-permute-start | bytes 3145736 | tf_op jit(solution)/shard_map/ppermute | solution.py:375
  39.6 22.5 %collective-permute-start.10 = (bf16[256,2048]{1,0:T(8,128)(2,1)S(1)}, bf16[256,2048]{1,0:T(8,128)(2,1)S(1)}, u32[]{:S(2)}, u32[]{:S(2)}) collective-permute-start(bf16[256,2048]{1,0:T(8,128)(2,1)S(1)} %collective-permute-done.6.refs_1_), channel_id=1, source_target_pairs={{0,4},{1,3},{4,8},{5,1},{8,12},{9,5},{12,14},{13,9},{14,10},{15,13... | collective-permute-start | bytes 3145736 | tf_op jit(solution)/shard_map/ppermute | solution.py:372
  50.8 15.1 %collective-permute-start.11 = (bf16[256,2048]{1,0:T(8,128)(2,1)S(1)}, bf16[256,2048]{1,0:T(8,128)(2,1)S(1)}, u32[]{:S(2)}, u32[]{:S(2)}) collective-permute-start(bf16[256,2048]{1,0:T(8,128)(2,1)S(1)} %collective-permute-done.8.refs_1_), channel_id=1, source_target_pairs={{0,1},{1,0},{2,3},{3,2},{4,5},{5,4},{6,7},{7,6},{8,9},{9,8},{10,11... | collective-permute-start | bytes 3145736 | tf_op jit(solution)/shard_map/ppermute | solution.py:375
  50.8 22.5 %collective-permute-start.12 = (bf16[256,2048]{1,0:T(8,128)(2,1)S(1)}, bf16[256,2048]{1,0:T(8,128)(2,1)S(1)}, u32[]{:S(2)}, u32[]{:S(2)}) collective-permute-start(bf16[256,2048]{1,0:T(8,128)(2,1)S(1)} %collective-permute-done.8.refs_1_), channel_id=1, source_target_pairs={{0,4},{1,3},{4,8},{5,1},{8,12},{9,5},{12,14},{13,9},{14,10},{15,13... | collective-permute-start | bytes 3145736 | tf_op jit(solution)/shard_map/ppermute | solution.py:372
  62.1 13.4 %collective-permute-start.13 = (bf16[256,2048]{1,0:T(8,128)(2,1)S(1)}, bf16[256,2048]{1,0:T(8,128)(2,1)S(1)}, u32[]{:S(2)}, u32[]{:S(2)}) collective-permute-start(bf16[256,2048]{1,0:T(8,128)(2,1)S(1)} %collective-permute-done.10.refs_1_.block), channel_id=1, source_target_pairs={{0,1},{1,0},{2,3},{3,2},{4,5},{5,4},{6,7},{7,6},{8,9},{9,8},{10,11... | collective-permute-start | bytes 3145736 | tf_op jit(solution)/shard_map/ppermute | solution.py:375
  62.1 16.6 %collective-permute-start.14 = (bf16[64,2048]{1,0:T(8,128)(2,1)S(1)}, bf16[64,2048]{1,0:T(8,128)(2,1)S(1)}, u32[]{:S(2)}, u32[]{:S(2)}) collective-permute-start(bf16[64,2048]{1,0:T(8,128)(2,1)S(1)} %get-tuple-element.76), channel_id=1, source_target_pairs={{0,4},{1,3},{4,8},{5,1},{8,12},{9,5},{12,14},{13,9},{14,10},{15,13... | collective-permute-start | bytes 786440 | tf_op jit(solution)/shard_map/ppermute | solution.py:372
  64.3 14.6 %collective-permute-start.15 = (bf16[64,2048]{1,0:T(8,128)(2,1)S(1)}, bf16[64,2048]{1,0:T(8,128)(2,1)S(1)}, u32[]{:S(2)}, u32[]{:S(2)}) collective-permute-start(bf16[64,2048]{1,0:T(8,128)(2,1)S(1)} %get-tuple-element.77), channel_id=1, source_target_pairs={{0,4},{1,3},{4,8},{5,1},{8,12},{9,5},{12,14},{13,9},{14,10},{15,13... | collective-permute-start | bytes 786440 | tf_op jit(solution)/shard_map/ppermute | solution.py:372
  73.3 11.2 %collective-permute-start.16 = (bf16[256,2048]{1,0:T(8,128)(2,1)S(1)}, bf16[256,2048]{1,0:T(8,128)(2,1)S(1)}, u32[]{:S(2)}, u32[]{:S(2)}) collective-permute-start(bf16[256,2048]{1,0:T(8,128)(2,1)S(1)} %collective-permute-done.12.refs_1_), channel_id=1, source_target_pairs={{0,1},{1,0},{2,3},{3,2},{4,5},{5,4},{6,7},{7,6},{8,9},{9,8},{10,11... | collective-permute-start | bytes 3145736 | tf_op jit(solution)/shard_map/ppermute | solution.py:375
  73.3 11.2 %collective-permute-start.19 = (bf16[128,2048]{1,0:T(8,128)(2,1)S(1)}, bf16[128,2048]{1,0:T(8,128)(2,1)S(1)}, u32[]{:S(2)}, u32[]{:S(2)}) collective-permute-start(bf16[128,2048]{1,0:T(8,128)(2,1)S(1)} %get-tuple-element.84), channel_id=1, source_target_pairs={{0,4},{1,3},{4,8},{5,1},{8,12},{9,5},{12,14},{13,9},{14,10},{15,13... | collective-permute-start | bytes 1572872 | tf_op jit(solution)/shard_map/ppermute | solution.py:372
  78.9 1.5 %collective-permute-start.17 = (bf16[64,2048]{1,0:T(8,128)(2,1)S(1)}, bf16[64,2048]{1,0:T(8,128)(2,1)S(1)}, u32[]{:S(2)}, u32[]{:S(2)}) collective-permute-start(bf16[64,2048]{1,0:T(8,128)(2,1)S(1)} %collective-permute-done.14.refs_0_), channel_id=1, source_target_pairs={{0,1},{1,0},{2,3},{3,2},{4,5},{5,4},{6,7},{7,6},{8,9},{9,8},{10,11... | collective-permute-start | bytes 786440 | tf_op jit(solution)/shard_map/ppermute | solution.py:375
  79.0 1.9 %collective-permute-start.18 = (bf16[64,2048]{1,0:T(8,128)(2,1)S(1)}, bf16[64,2048]{1,0:T(8,128)(2,1)S(1)}, u32[]{:S(2)}, u32[]{:S(2)}) collective-permute-start(bf16[64,2048]{1,0:T(8,128)(2,1)S(1)} %collective-permute-done.15.refs_1_), channel_id=1, source_target_pairs={{0,1},{1,0},{2,3},{3,2},{4,5},{5,4},{6,7},{7,6},{8,9},{9,8},{10,11... | collective-permute-start | bytes 786440 | tf_op jit(solution)/shard_map/ppermute | solution.py:375
  84.5 2.5 %collective-permute-start.20 = (bf16[128,2048]{1,0:T(8,128)(2,1)S(1)}, bf16[128,2048]{1,0:T(8,128)(2,1)S(1)}, u32[]{:S(2)}, u32[]{:S(2)}) collective-permute-start(bf16[128,2048]{1,0:T(8,128)(2,1)S(1)} %collective-permute-done.19.refs_1_), channel_id=1, source_target_pairs={{0,1},{1,0},{2,3},{3,2},{4,5},{5,4},{6,7},{7,6},{8,9},{9,8},{10,11... | collective-permute-start | bytes 1572872 | tf_op jit(solution)/shard_map/ppermute | solution.py:375
  87.0 14.7 %copy-start.5 = (s32[128,8]{0,1:T(8,128)S(1)}, s32[128,8]{0,1:T(8,128)}, u32[]{:S(2)}) copy-start(s32[128,8]{0,1:T(8,128)} %param.12) | copy-start | bytes 12292

commit v13 on v12

--- a/solution.py
+++ b/solution.py
@@ -82,12 +82,12 @@
         ]
         for copy in copies[3 * tiles :] + copies[: 3 * tiles]:
             copy.start()
-    for i, block in enumerate(block_in):
+    if blocks == 1:
+        x_all, dy_all = block_in[0].at[:rows, :], block_in[0].at[rows:, :]
+    for i, block in enumerate(block_in if blocks > 1 else ()):
         place = slice((blocks - whole + i) * rows, (blocks - whole + i + 1) * rows)
         x_all[place, :] = block[:rows, :]
         dy_all[place, :] = block[rows:, :]
-    low_sum[...] = jnp.zeros_like(low_sum)
-    grad_sum[...] = jnp.zeros_like(grad_sum)
 
     def one_tile(j):
         part = pl.ds(j * tile, tile)
@@ -98,11 +98,14 @@
             dy_all[...], w_down[part, :], across, preferred_element_type=jnp.float32
         )
         terms = hidden.astype(jnp.float32) * back
-        for cut in range(0, tile, lanes):
-            grad_sum[...] += terms[:, cut : cut + lanes]
-        low_sum[...] += lax.dot_general(
+        total = terms[:, :lanes]
+        for cut in range(lanes, tile, lanes):
+            total += terms[:, cut : cut + lanes]
+        grad_sum[...] = total if j == 0 else grad_sum[...] + total
+        low = lax.dot_general(
             low_proj[:, part], hidden, across, preferred_element_type=jnp.float32
         )
+        low_sum[...] = low if j == 0 else low_sum[...] + low
 
     for copy in copies[3 * tiles :]:
         copy.wait()
@@ -281,9 +284,8 @@
     rows = returned.shape[2]
     width, rank = low_in[0].shape[0], proj_in[0].shape[0]
     doc_of = lax.broadcasted_iota(jnp.int32, (width, rows), 0) // rank
-    total = jnp.zeros(feat.shape, jnp.float32)
+    spread, high_side = [], []
     for names, low_side, proj_cot in zip(jobs, low_in, proj_in):
-        spread, high_side = [], []
         for i, name in enumerate(names):
             place = slice(i * rows, (i + 1) * rows)
             owner = block_owner(name, returned.shape[0] // 2)
@@ -292,13 +294,12 @@
             high_side.append((weight * proj_cot[:, place]).astype(jnp.bfloat16))
             low = low_side[:, place].astype(jnp.float32)
             spread.append(jnp.where(doc == doc_of, low, 0.0).astype(jnp.bfloat16))
-        total += lax.dot_general(
-            jnp.concatenate(spread, axis=1),
-            jnp.concatenate(high_side, axis=1),
-            (((1,), (1,)), ((), ())),
-            preferred_element_type=jnp.float32,
-        )
-    feat[...] = total
+    feat[...] = lax.dot_general(
+        jnp.concatenate(spread, axis=1),
+        jnp.concatenate(high_side, axis=1),
+        (((1,), (1,)), ((), ())),
+        preferred_element_type=jnp.float32,
+    )
     picked = jnp.zeros(route_grad.shape, jnp.float32)
     for e in range(returned.shape[0]):
         picked = jnp.where(routes[...] == e, returned[e, 0:1, :], picked)
@@ -389,7 +390,7 @@
 
     sheet = pl.pallas_call(
         facts_kernel,
-        out_shape=jax.ShapeDtypeStruct((groups, 8, tok_rows), jnp.float32),
+        out_shape=jax.ShapeDtypeStruct((groups, 4, tok_rows), jnp.float32),
         in_specs=[pl.BlockSpec(memory_space=pltpu.VMEM)] * 3,
         out_specs=pl.BlockSpec(memory_space=pltpu.VMEM),
         compiler_params=pltpu.CompilerParams(vmem_limit_bytes=8 * 1024 * 1024),

time: 103 us -> 103 us (level)
  no operation moved by 1% of the time
where the time goes in v13:
time: 103 us
  Pallas kernels  32.1 us (31%)
  waiting for transfers between devices  29.6 us (29%)
  starting transfers between devices  21.1 us (20%)
  blocking collectives  13 us (13%)
  local copies, waits for them, and re-layouts  5.98 us (6%)
    ppermute x10, waiting for transfers between devices, hop(): return lax.ppermute(block, 'exp', onward)  28.1 us
    pallas_call x7, Pallas kernels, work(): return call(sheet, *apart, *block_in, *weights)  26.9 us
    ppermute x10, starting transfers between devices, hop(): return lax.ppermute(block, 'exp', onward)  19.9 us
    all_to_all x1, blocking collectives, by_ring(): lax.all_to_all(sheet, 'exp', split_axis=0, concat_axis=0, tiled=True)  13 us
    unnamed x16, local copies, waits for them, and re-layouts  5.98 us
    pallas_call x1, Pallas kernels, front(): pl.pallas_call(front_kernel, out_shape=[jax.ShapeDtypeStruct((rows, units...  2.45 us
  transfers between devices with their start and end apart: 21, of which 9 were waited for; matrix products, arithmetic and copies ran while one was open for 0% of the time, Pallas kernels for 29%

profile of v13, /device:TPU:0, one launch (start us, length us, event | category | flops | bytes accessed | tf_op | source)
XLA Modules:
  0.0 102.5 jit_solution(4532766891420448264)
XLA Ops:
  0.6 0.5 collective-permute-start
  1.1 0.1 collective-permute-start.1
  1.2 3.0 %collective-permute-start.2 = (bf16[128,2048]{1,0:T(8,128)(2,1)}, bf16[128,2048]{1,0:T(8,128)(2,1)S(1)}, u32[]{:S(2)}, u32[]{:S(2)}) collective-permute-start(bf16[128,2048]{1,0:T(8,128)(2,1)} %refs_1_.1), channel_id=1, source_target_pairs={{0,4},{1,3},{4,8},{5,1},{8,12},{9,5},{12,14},{13,9},{14,10},{15,13... | collective-permute-start | bytes 1572872 | tf_op jit(solution)/shard_map/ppermute | solution.py:373
  4.2 1.6 %collective-permute-start.3 = (bf16[128,2048]{1,0:T(8,128)(2,1)}, bf16[128,2048]{1,0:T(8,128)(2,1)S(1)}, u32[]{:S(2)}, u32[]{:S(2)}) collective-permute-start(bf16[128,2048]{1,0:T(8,128)(2,1)} %refs_2_.1), channel_id=1, source_target_pairs={{0,4},{1,3},{4,8},{5,1},{8,12},{9,5},{12,14},{13,9},{14,10},{15,13... | collective-permute-start | bytes 1572872 | tf_op jit(solution)/shard_map/ppermute | solution.py:373
  5.8 0.7 copy-done.4
  6.5 0.7 copy-done.6
  7.2 0.7 copy-done.7
  7.9 0.0 collective-permute-done.top
  7.9 0.1 shard_map.114.refs_3_
  8.0 1.6 %collective-permute-start.4 = (bf16[256,2048]{1,0:T(8,128)(2,1)S(1)}, bf16[256,2048]{1,0:T(8,128)(2,1)S(1)}, u32[]{:S(2)}, u32[]{:S(2)}) collective-permute-start(bf16[256,2048]{1,0:T(8,128)(2,1)S(1)} %shard_map.114.refs_3_), channel_id=1, source_target_pairs={{0,4},{1,3},{4,8},{5,1},{8,12},{9,5},{12,14},{13,9},{14,10},{15,13... | collective-permute-start | bytes 3145736 | tf_op jit(solution)/shard_map/ppermute | solution.py:373
  9.6 1.0 %copy-done = bf16[128,2048]{1,0:T(8,128)(2,1)S(1)} copy-done((bf16[128,2048]{1,0:T(8,128)(2,1)S(1)}, bf16[128,2048]{1,0:T(8,128)(2,1)}, u32[]{:S(2)}) %copy-start) | copy-done | bytes 524312
  10.6 1.0 %copy-done.1 = bf16[128,2048]{1,0:T(8,128)(2,1)S(1)} copy-done((bf16[128,2048]{1,0:T(8,128)(2,1)S(1)}, bf16[128,2048]{1,0:T(8,128)(2,1)}, u32[]{:S(2)}) %copy-start.1) | copy-done | bytes 524312
  11.7 0.9 copy-done.2
  12.6 0.9 copy-done.3
  13.5 6.6 %shard_map.115 = (f32[16,4,128]{2,1,0:T(4,128)S(1)}, bf16[256,256]{1,0:T(8,128)(2,1)S(1)}, f32[64,256]{1,0:T(8,128)S(1)}, bf16[2048,768]{1,0:T(8,128)(2,1)S(1)},...) custom-call(f32[16,4,128]{2,1,0:T(4,128)S(1)} %shard_map.113.refs_0_, ...), custom_call_target="tpu_custom_call" | custom-call | flops 2415919104 | bytes 2097152 | tf_op jit(solution)/shard_map/pallas_call | solution.py:170
  20.1 0.0 collective-permute-done.2.top
  20.1 0.1 shard_map.116.refs_3_
  20.2 0.1 collective-permute-start.5
  20.3 1.5 %collective-permute-start.6 = (bf16[256,2048]{1,0:T(8,128)(2,1)S(1)}, bf16[256,2048]{1,0:T(8,128)(2,1)S(1)}, u32[]{:S(2)}, u32[]{:S(2)}) collective-permute-start(bf16[256,2048]{1,0:T(8,128)(2,1)S(1)} %shard_map.116.refs_3_), channel_id=1, source_target_pairs={{0,4},{1,3},{4,8},{5,1},{8,12},{9,5},{12,14},{13,9},{14,10},{15,13... | collective-permute-start | bytes 3145736 | tf_op jit(solution)/shard_map/ppermute | solution.py:373
  21.8 6.6 %collective-permute-done.4.refs_1_ = bf16[256,2048]{1,0:T(8,128)(2,1)S(1)} collective-permute-done((bf16[256,2048]{1,0:T(8,128)(2,1)S(1)}, bf16[256,2048]{1,0:T(8,128)(2,1)S(1)}, u32[]{:S(2)}, u32[]{:S(2)}) %collective-permute-start.4) | collective-permute-done | bytes 1048608 | tf_op jit(solution)/shard_map/ppermute | solution.py:373
  28.4 2.1 %collective-permute-start.8 = (bf16[256,2048]{1,0:T(8,128)(2,1)S(1)}, bf16[256,2048]{1,0:T(8,128)(2,1)S(1)}, u32[]{:S(2)}, u32[]{:S(2)}) collective-permute-start(bf16[256,2048]{1,0:T(8,128)(2,1)S(1)} %collective-permute-done.4.refs_1_), channel_id=1, source_target_pairs={{0,4},{1,3},{4,8},{5,1},{8,12},{9,5},{12,14},{13,9},{14,10},{15,13... | collective-permute-start | bytes 3145736 | tf_op jit(solution)/shard_map/ppermute | solution.py:373
  30.5 4.6 %shard_map.117 = (f32[16,4,128]{2,1,0:T(4,128)S(1)}, bf16[256,384]{1,0:T(8,128)(2,1)S(1)}, f32[64,384]{1,0:T(8,128)S(1)}) custom-call(f32[16,4,128]{2,1,0:T(4,128)S(1)} %get-tuple-element.55.refs_0_, bf16[256,2048]{1,0:T(8,128)(2,1)S(1)} %collective-permute-done.4.refs_1_, bf16[256,2048]{1,0:T(8,128)(2,1)S(1)} %collective-permute-done.5.refs_2_, ...), custom_call_target="tpu_custom_call" | custom-call | flops 3623878656 | bytes 3145728 | tf_op jit(solution)/shard_map/pallas_call | solution.py:170
  35.1 4.5 %collective-permute-done.6.refs_1_ = bf16[256,2048]{1,0:T(8,128)(2,1)S(1)} collective-permute-done((bf16[256,2048]{1,0:T(8,128)(2,1)S(1)}, bf16[256,2048]{1,0:T(8,128)(2,1)S(1)}, u32[]{:S(2)}, u32[]{:S(2)}) %collective-permute-start.6) | collective-permute-done | bytes 1048608 | tf_op jit(solution)/shard_map/ppermute | solution.py:373
  39.6 2.1 %collective-permute-start.10 = (bf16[256,2048]{1,0:T(8,128)(2,1)S(1)}, bf16[256,2048]{1,0:T(8,128)(2,1)S(1)}, u32[]{:S(2)}, u32[]{:S(2)}) collective-permute-start(bf16[256,2048]{1,0:T(8,128)(2,1)S(1)} %collective-permute-done.6.refs_1_), channel_id=1, source_target_pairs={{0,4},{1,3},{4,8},{5,1},{8,12},{9,5},{12,14},{13,9},{14,10},{15,13... | collective-permute-start | bytes 3145736 | tf_op jit(solution)/shard_map/ppermute | solution.py:373
  41.7 3.3 %shard_map.118 = (f32[16,4,128]{2,1,0:T(4,128)S(1)}, bf16[256,256]{1,0:T(8,128)(2,1)S(1)}, f32[64,256]{1,0:T(8,128)S(1)}) custom-call(f32[16,4,128]{2,1,0:T(4,128)S(1)} %get-tuple-element.64.refs_0_, bf16[256,2048]{1,0:T(8,128)(2,1)S(1)} %collective-permute-done.6.refs_1_, bf16[256,2048]{1,0:T(8,128)(2,1)S(1)} %collective-permute-done.7.refs_2_, ...), custom_call_target="tpu_custom_call" | custom-call | flops 2415919104 | bytes 2097152 | tf_op jit(solution)/shard_map/pallas_call | solution.py:170
  45.0 5.8 %collective-permute-done.8.refs_1_ = bf16[256,2048]{1,0:T(8,128)(2,1)S(1)} collective-permute-done((bf16[256,2048]{1,0:T(8,128)(2,1)S(1)}, bf16[256,2048]{1,0:T(8,128)(2,1)S(1)}, u32[]{:S(2)}, u32[]{:S(2)}) %collective-permute-start.8) | collective-permute-done | bytes 1048608 | tf_op jit(solution)/shard_map/ppermute | solution.py:373
  50.8 2.1 %collective-permute-start.12 = (bf16[256,2048]{1,0:T(8,128)(2,1)S(1)}, bf16[256,2048]{1,0:T(8,128)(2,1)S(1)}, u32[]{:S(2)}, u32[]{:S(2)}) collective-permute-start(bf16[256,2048]{1,0:T(8,128)(2,1)S(1)} %collective-permute-done.8.refs_1_), channel_id=1, source_target_pairs={{0,4},{1,3},{4,8},{5,1},{8,12},{9,5},{12,14},{13,9},{14,10},{15,13... | collective-permute-start | bytes 3145736 | tf_op jit(solution)/shard_map/ppermute | solution.py:373
  53.0 3.3 %shard_map.119 = (f32[16,4,128]{2,1,0:T(4,128)S(1)}, bf16[256,256]{1,0:T(8,128)(2,1)S(1)}, f32[64,256]{1,0:T(8,128)S(1)}) custom-call(f32[16,4,128]{2,1,0:T(4,128)S(1)} %get-tuple-element.67.refs_0_, bf16[256,2048]{1,0:T(8,128)(2,1)S(1)} %collective-permute-done.8.refs_1_, bf16[256,2048]{1,0:T(8,128)(2,1)S(1)} %collective-permute-done.9.refs_2_, ...), custom_call_target="tpu_custom_call" | custom-call | flops 2415919104 | bytes 2097152 | tf_op jit(solution)/shard_map/pallas_call | solution.py:170
  56.3 5.8 %collective-permute-done.10.refs_1_.block = bf16[256,2048]{1,0:T(8,128)(2,1)S(1)} collective-permute-done((bf16[256,2048]{1,0:T(8,128)(2,1)S(1)}, bf16[256,2048]{1,0:T(8,128)(2,1)S(1)}, u32[]{:S(2)}, u32[]{:S(2)}) %collective-permute-start.10) | collective-permute-done | bytes 1048608 | tf_op jit(solution)/shard_map/ppermute | solution.py:373
  62.1 0.1 shard_map.122
  62.1 2.2 %collective-permute-start.14 = (bf16[64,2048]{1,0:T(8,128)(2,1)S(1)}, bf16[64,2048]{1,0:T(8,128)(2,1)S(1)}, u32[]{:S(2)}, u32[]{:S(2)}) collective-permute-start(bf16[64,2048]{1,0:T(8,128)(2,1)S(1)} %get-tuple-element.76), channel_id=1, source_target_pairs={{0,4},{1,3},{4,8},{5,1},{8,12},{9,5},{12,14},{13,9},{14,10},{15,13... | collective-permute-start | bytes 786440 | tf_op jit(solution)/shard_map/ppermute | solution.py:373
  64.3 1.6 %collective-permute-start.15 = (bf16[64,2048]{1,0:T(8,128)(2,1)S(1)}, bf16[64,2048]{1,0:T(8,128)(2,1)S(1)}, u32[]{:S(2)}, u32[]{:S(2)}) collective-permute-start(bf16[64,2048]{1,0:T(8,128)(2,1)S(1)} %get-tuple-element.77), channel_id=1, source_target_pairs={{0,4},{1,3},{4,8},{5,1},{8,12},{9,5},{12,14},{13,9},{14,10},{15,13... | collective-permute-start | bytes 786440 | tf_op jit(solution)/shard_map/ppermute | solution.py:373
  65.9 3.3 %shard_map.120 = (f32[16,4,128]{2,1,0:T(4,128)S(1)}, bf16[256,256]{1,0:T(8,128)(2,1)S(1)}, f32[64,256]{1,0:T(8,128)S(1)}) custom-call(f32[16,4,128]{2,1,0:T(4,128)S(1)} %get-tuple-element.70.refs_0_, bf16[256,2048]{1,0:T(8,128)(2,1)S(1)} %collective-permute-done.10.refs_1_.block, bf16[256,2048]{1,0:T(8,128)(2,1)S(1)} %collective-permute-done.11.refs_2_, ...), custom_call_target="tpu_custom_call" | custom-call | flops 2415919104 | bytes 2097152 | tf_op jit(solution)/shard_map/pallas_call | solution.py:170
  69.2 4.1 %collective-permute-done.12.refs_1_ = bf16[256,2048]{1,0:T(8,128)(2,1)S(1)} collective-permute-done((bf16[256,2048]{1,0:T(8,128)(2,1)S(1)}, bf16[256,2048]{1,0:T(8,128)(2,1)S(1)}, u32[]{:S(2)}, u32[]{:S(2)}) %collective-permute-start.12) | collective-permute-done | bytes 1048608 | tf_op jit(solution)/shard_map/ppermute | solution.py:373
  73.3 2.1 %collective-permute-start.19 = (bf16[128,2048]{1,0:T(8,128)(2,1)S(1)}, bf16[128,2048]{1,0:T(8,128)(2,1)S(1)}, u32[]{:S(2)}, u32[]{:S(2)}) collective-permute-start(bf16[128,2048]{1,0:T(8,128)(2,1)S(1)} %get-tuple-element.84), channel_id=1, source_target_pairs={{0,4},{1,3},{4,8},{5,1},{8,12},{9,5},{12,14},{13,9},{14,10},{15,13... | collective-permute-start | bytes 1572872 | tf_op jit(solution)/shard_map/ppermute | solution.py:373
  75.4 3.3 %shard_map.121 = (f32[16,4,128]{2,1,0:T(4,128)S(1)}, bf16[256,256]{1,0:T(8,128)(2,1)S(1)}, f32[64,256]{1,0:T(8,128)S(1)}) custom-call(f32[16,4,128]{2,1,0:T(4,128)S(1)} %get-tuple-element.73.refs_0_, bf16[256,2048]{1,0:T(8,128)(2,1)S(1)} %collective-permute-done.12.refs_1_, bf16[256,2048]{1,0:T(8,128)(2,1)S(1)} %collective-permute-done.13.refs_2_, ...), custom_call_target="tpu_custom_call" | custom-call | flops 2415919104 | bytes 2097152 | tf_op jit(solution)/shard_map/pallas_call | solution.py:170
  78.8 0.2 collective-permute-done.15.refs_1_
  78.9 0.1 collective-permute-start.17
  79.0 0.5 collective-permute-start.18
  79.4 1.0 collective-permute-done.17.refs_2_
  80.5 0.4 collective-permute-done.18.refs_3_
  80.8 2.5 %shard_map.124 = (bf16[256,768]{1,0:T(8,128)(2,1)S(1)}, bf16[256,256]{1,0:T(8,128)(2,1)S(1)}) custom-call(bf16[64,2048]{1,0:T(8,128)(2,1)S(1)} %collective-permute-done.14.refs_0_, bf16[64,2048]{1,0:T(8,128)(2,1)S(1)} %collective-permute-done.15.refs_1_, bf16[64,2048]{1,0:T(8,128)(2,1)S(1)} %collective-permute-done.17.refs_2_, ...), custom_call_target="tpu_custom_call" | custom-call | flops 1610612736 | bytes 1048576 | tf_op jit(solution)/shard_map/pallas_call | solution.py:203
  83.3 1.2 %collective-permute-done.19.refs_1_ = bf16[128,2048]{1,0:T(8,128)(2,1)S(1)} collective-permute-done((bf16[128,2048]{1,0:T(8,128)(2,1)S(1)}, bf16[128,2048]{1,0:T(8,128)(2,1)S(1)}, u32[]{:S(2)}, u32[]{:S(2)}) %collective-permute-start.19) | collective-permute-done | bytes 524320 | tf_op jit(solution)/shard_map/ppermute | solution.py:373
  84.5 2.4 %shard_map.123 = (f32[16,4,128]{2,1,0:T(4,128)S(1)}, bf16[256,128]{1,0:T(8,128)(2,1)S(1)}, f32[64,128]{1,0:T(8,128)S(1)}) custom-call(f32[16,4,128]{2,1,0:T(4,128)S(1)} %get-tuple-element.78.refs_0_, bf16[256,2048]{1,0:T(8,128)(2,1)S(1)} %collective-permute-done.16.refs_1_, bf16[2048,768]{1,0:T(8,128)(2,1)S(1)} %get-tuple-element.58.refs_4_.refs_3_.refs_2_, ...), custom_call_target="tpu_custom_call" | custom-call | flops 1207959552 | bytes 1048576 | tf_op jit(solution)/shard_map/pallas_call | solution.py:170
  87.0 0.0 copy-start.5
  87.0 1.4 %shard_map.125 = (f32[16,4,128]{2,1,0:T(4,128)S(1)}, f32[64,256]{1,0:T(8,128)S(1)}) custom-call(f32[16,4,128]{2,1,0:T(4,128)S(1)} %get-tuple-element.79.refs_0_, bf16[128,2048]{1,0:T(8,128)(2,1)S(1)} %collective-permute-done.19.refs_1_, bf16[128,2048]{1,0:T(8,128)(2,1)S(1)} %collective-permute-done.20.refs_2_, ...), custom_call_target="tpu_custom_call" | custom-call | flops 805306368 | bytes 1048576 | tf_op jit(solution)/shard_map/pallas_call | solution.py:260
  88.4 13.0 %all_to_all.5.returned = f32[16,4,128]{2,1,0:T(4,128)S(1)} all-to-all(f32[16,4,128]{2,1,0:T(4,128)S(1)} %get-tuple-element.87), channel_id=1, replica_groups=mesh['grp'=2,'exp'=16] {'exp'}, dimensions={0} | all-to-all | bytes 65536 | tf_op jit(solution)/shard_map/all_to_all | solution.py:444
  101.4 1.1 %shard_map.126 = (f32[256,64]{1,0:T(8,128)}, f32[8,128]{1,0:T(8,128)}) custom-call(f32[16,4,128]{2,1,0:T(4,128)S(1)} %all_to_all.5.returned, s32[8,128]{1,0:T(8,128)S(1)} %bitcast.19, bf16[256,256]{1,0:T(8,128)(2,1)S(1)} %get-tuple-element.88.refs_0_, bf16[256,384]{1,0:T(8,128)(2,1)S(1)} %get-tuple-element.89.refs_1_, ...), custom_call_target="tpu_custom_call" | custom-call | tf_op jit(solution)/shard_map/pallas_call | solution.py:446
  (25 shorter events, 0.1 us)
Async XLA Ops:
  0.6 7.2 %collective-permute-start = (bf16[128,2048]{1,0:T(8,128)(2,1)}, bf16[128,2048]{1,0:T(8,128)(2,1)S(1)}, u32[]{:S(2)}, u32[]{:S(2)}) collective-permute-start(bf16[128,2048]{1,0:T(8,128)(2,1)} %refs_1_.1), channel_id=1, source_target_pairs={{0,1},{1,0},{2,3},{3,2},{4,5},{5,4},{6,7},{7,6},{8,9},{9,8},{10,11... | collective-permute-start | bytes 1572872 | tf_op jit(solution)/shard_map/ppermute | solution.py:376
  1.1 6.7 %collective-permute-start.1 = (bf16[128,2048]{1,0:T(8,128)(2,1)}, bf16[128,2048]{1,0:T(8,128)(2,1)S(1)}, u32[]{:S(2)}, u32[]{:S(2)}) collective-permute-start(bf16[128,2048]{1,0:T(8,128)(2,1)} %refs_2_.1), channel_id=1, source_target_pairs={{0,1},{1,0},{2,3},{3,2},{4,5},{5,4},{6,7},{7,6},{8,9},{9,8},{10,11... | collective-permute-start | bytes 1572872 | tf_op jit(solution)/shard_map/ppermute | solution.py:376
  1.2 18.8 %collective-permute-start.2 = (bf16[128,2048]{1,0:T(8,128)(2,1)}, bf16[128,2048]{1,0:T(8,128)(2,1)S(1)}, u32[]{:S(2)}, u32[]{:S(2)}) collective-permute-start(bf16[128,2048]{1,0:T(8,128)(2,1)} %refs_1_.1), channel_id=1, source_target_pairs={{0,4},{1,3},{4,8},{5,1},{8,12},{9,5},{12,14},{13,9},{14,10},{15,13... | collective-permute-start | bytes 1572872 | tf_op jit(solution)/shard_map/ppermute | solution.py:373
  4.2 15.9 %collective-permute-start.3 = (bf16[128,2048]{1,0:T(8,128)(2,1)}, bf16[128,2048]{1,0:T(8,128)(2,1)S(1)}, u32[]{:S(2)}, u32[]{:S(2)}) collective-permute-start(bf16[128,2048]{1,0:T(8,128)(2,1)} %refs_2_.1), channel_id=1, source_target_pairs={{0,4},{1,3},{4,8},{5,1},{8,12},{9,5},{12,14},{13,9},{14,10},{15,13... | collective-permute-start | bytes 1572872 | tf_op jit(solution)/shard_map/ppermute | solution.py:373
  5.8 0.7 copy-start.4
  6.5 0.7 copy-start.6
  7.2 0.7 copy-start.7
  8.0 20.4 %collective-permute-start.4 = (bf16[256,2048]{1,0:T(8,128)(2,1)S(1)}, bf16[256,2048]{1,0:T(8,128)(2,1)S(1)}, u32[]{:S(2)}, u32[]{:S(2)}) collective-permute-start(bf16[256,2048]{1,0:T(8,128)(2,1)S(1)} %shard_map.114.refs_3_), channel_id=1, source_target_pairs={{0,4},{1,3},{4,8},{5,1},{8,12},{9,5},{12,14},{13,9},{14,10},{15,13... | collective-permute-start | bytes 3145736 | tf_op jit(solution)/shard_map/ppermute | solution.py:373
  9.6 1.0 %copy-start = (bf16[128,2048]{1,0:T(8,128)(2,1)S(1)}, bf16[128,2048]{1,0:T(8,128)(2,1)}, u32[]{:S(2)}) copy-start(bf16[128,2048]{1,0:T(8,128)(2,1)} %refs_1_.1) | copy-start | bytes 1572868
  10.6 1.0 %copy-start.1 = (bf16[128,2048]{1,0:T(8,128)(2,1)S(1)}, bf16[128,2048]{1,0:T(8,128)(2,1)}, u32[]{:S(2)}) copy-start(bf16[128,2048]{1,0:T(8,128)(2,1)} %refs_2_.1) | copy-start | bytes 1572868
  11.7 0.9 copy-start.2
  12.6 0.9 copy-start.3
  20.2 10.3 %collective-permute-start.5 = (bf16[256,2048]{1,0:T(8,128)(2,1)S(1)}, bf16[256,2048]{1,0:T(8,128)(2,1)S(1)}, u32[]{:S(2)}, u32[]{:S(2)}) collective-permute-start(bf16[256,2048]{1,0:T(8,128)(2,1)S(1)} %shard_map.116.refs_3_), channel_id=1, source_target_pairs={{0,1},{1,0},{2,3},{3,2},{4,5},{5,4},{6,7},{7,6},{8,9},{9,8},{10,11... | collective-permute-start | bytes 3145736 | tf_op jit(solution)/shard_map/ppermute | solution.py:376
  20.3 19.3 %collective-permute-start.6 = (bf16[256,2048]{1,0:T(8,128)(2,1)S(1)}, bf16[256,2048]{1,0:T(8,128)(2,1)S(1)}, u32[]{:S(2)}, u32[]{:S(2)}) collective-permute-start(bf16[256,2048]{1,0:T(8,128)(2,1)S(1)} %shard_map.116.refs_3_), channel_id=1, source_target_pairs={{0,4},{1,3},{4,8},{5,1},{8,12},{9,5},{12,14},{13,9},{14,10},{15,13... | collective-permute-start | bytes 3145736 | tf_op jit(solution)/shard_map/ppermute | solution.py:373
  28.4 13.4 %collective-permute-start.7 = (bf16[256,2048]{1,0:T(8,128)(2,1)S(1)}, bf16[256,2048]{1,0:T(8,128)(2,1)S(1)}, u32[]{:S(2)}, u32[]{:S(2)}) collective-permute-start(bf16[256,2048]{1,0:T(8,128)(2,1)S(1)} %collective-permute-done.4.refs_1_), channel_id=1, source_target_pairs={{0,1},{1,0},{2,3},{3,2},{4,5},{5,4},{6,7},{7,6},{8,9},{9,8},{10,11... | collective-permute-start | bytes 3145736 | tf_op jit(solution)/shard_map/ppermute | solution.py:376
  28.4 22.5 %collective-permute-start.8 = (bf16[256,2048]{1,0:T(8,128)(2,1)S(1)}, bf16[256,2048]{1,0:T(8,128)(2,1)S(1)}, u32[]{:S(2)}, u32[]{:S(2)}) collective-permute-start(bf16[256,2048]{1,0:T(8,128)(2,1)S(1)} %collective-permute-done.4.refs_1_), channel_id=1, source_target_pairs={{0,4},{1,3},{4,8},{5,1},{8,12},{9,5},{12,14},{13,9},{14,10},{15,13... | collective-permute-start | bytes 3145736 | tf_op jit(solution)/shard_map/ppermute | solution.py:373
  39.6 13.4 %collective-permute-start.9 = (bf16[256,2048]{1,0:T(8,128)(2,1)S(1)}, bf16[256,2048]{1,0:T(8,128)(2,1)S(1)}, u32[]{:S(2)}, u32[]{:S(2)}) collective-permute-start(bf16[256,2048]{1,0:T(8,128)(2,1)S(1)} %collective-permute-done.6.refs_1_), channel_id=1, source_target_pairs={{0,1},{1,0},{2,3},{3,2},{4,5},{5,4},{6,7},{7,6},{8,9},{9,8},{10,11... | collective-permute-start | bytes 3145736 | tf_op jit(solution)/shard_map/ppermute | solution.py:376
  39.6 22.5 %collective-permute-start.10 = (bf16[256,2048]{1,0:T(8,128)(2,1)S(1)}, bf16[256,2048]{1,0:T(8,128)(2,1)S(1)}, u32[]{:S(2)}, u32[]{:S(2)}) collective-permute-start(bf16[256,2048]{1,0:T(8,128)(2,1)S(1)} %collective-permute-done.6.refs_1_), channel_id=1, source_target_pairs={{0,4},{1,3},{4,8},{5,1},{8,12},{9,5},{12,14},{13,9},{14,10},{15,13... | collective-permute-start | bytes 3145736 | tf_op jit(solution)/shard_map/ppermute | solution.py:373
  50.8 15.1 %collective-permute-start.11 = (bf16[256,2048]{1,0:T(8,128)(2,1)S(1)}, bf16[256,2048]{1,0:T(8,128)(2,1)S(1)}, u32[]{:S(2)}, u32[]{:S(2)}) collective-permute-start(bf16[256,2048]{1,0:T(8,128)(2,1)S(1)} %collective-permute-done.8.refs_1_), channel_id=1, source_target_pairs={{0,1},{1,0},{2,3},{3,2},{4,5},{5,4},{6,7},{7,6},{8,9},{9,8},{10,11... | collective-permute-start | bytes 3145736 | tf_op jit(solution)/shard_map/ppermute | solution.py:376
  50.8 22.5 %collective-permute-start.12 = (bf16[256,2048]{1,0:T(8,128)(2,1)S(1)}, bf16[256,2048]{1,0:T(8,128)(2,1)S(1)}, u32[]{:S(2)}, u32[]{:S(2)}) collective-permute-start(bf16[256,2048]{1,0:T(8,128)(2,1)S(1)} %collective-permute-done.8.refs_1_), channel_id=1, source_target_pairs={{0,4},{1,3},{4,8},{5,1},{8,12},{9,5},{12,14},{13,9},{14,10},{15,13... | collective-permute-start | bytes 3145736 | tf_op jit(solution)/shard_map/ppermute | solution.py:373
  62.1 13.4 %collective-permute-start.13 = (bf16[256,2048]{1,0:T(8,128)(2,1)S(1)}, bf16[256,2048]{1,0:T(8,128)(2,1)S(1)}, u32[]{:S(2)}, u32[]{:S(2)}) collective-permute-start(bf16[256,2048]{1,0:T(8,128)(2,1)S(1)} %collective-permute-done.10.refs_1_.block), channel_id=1, source_target_pairs={{0,1},{1,0},{2,3},{3,2},{4,5},{5,4},{6,7},{7,6},{8,9},{9,8},{10,11... | collective-permute-start | bytes 3145736 | tf_op jit(solution)/shard_map/ppermute | solution.py:376
  62.1 16.6 %collective-permute-start.14 = (bf16[64,2048]{1,0:T(8,128)(2,1)S(1)}, bf16[64,2048]{1,0:T(8,128)(2,1)S(1)}, u32[]{:S(2)}, u32[]{:S(2)}) collective-permute-start(bf16[64,2048]{1,0:T(8,128)(2,1)S(1)} %get-tuple-element.76), channel_id=1, source_target_pairs={{0,4},{1,3},{4,8},{5,1},{8,12},{9,5},{12,14},{13,9},{14,10},{15,13... | collective-permute-start | bytes 786440 | tf_op jit(solution)/shard_map/ppermute | solution.py:373
  64.3 14.6 %collective-permute-start.15 = (bf16[64,2048]{1,0:T(8,128)(2,1)S(1)}, bf16[64,2048]{1,0:T(8,128)(2,1)S(1)}, u32[]{:S(2)}, u32[]{:S(2)}) collective-permute-start(bf16[64,2048]{1,0:T(8,128)(2,1)S(1)} %get-tuple-element.77), channel_id=1, source_target_pairs={{0,4},{1,3},{4,8},{5,1},{8,12},{9,5},{12,14},{13,9},{14,10},{15,13... | collective-permute-start | bytes 786440 | tf_op jit(solution)/shard_map/ppermute | solution.py:373
  73.3 11.2 %collective-permute-start.16 = (bf16[256,2048]{1,0:T(8,128)(2,1)S(1)}, bf16[256,2048]{1,0:T(8,128)(2,1)S(1)}, u32[]{:S(2)}, u32[]{:S(2)}) collective-permute-start(bf16[256,2048]{1,0:T(8,128)(2,1)S(1)} %collective-permute-done.12.refs_1_), channel_id=1, source_target_pairs={{0,1},{1,0},{2,3},{3,2},{4,5},{5,4},{6,7},{7,6},{8,9},{9,8},{10,11... | collective-permute-start | bytes 3145736 | tf_op jit(solution)/shard_map/ppermute | solution.py:376
  73.3 11.2 %collective-permute-start.19 = (bf16[128,2048]{1,0:T(8,128)(2,1)S(1)}, bf16[128,2048]{1,0:T(8,128)(2,1)S(1)}, u32[]{:S(2)}, u32[]{:S(2)}) collective-permute-start(bf16[128,2048]{1,0:T(8,128)(2,1)S(1)} %get-tuple-element.84), channel_id=1, source_target_pairs={{0,4},{1,3},{4,8},{5,1},{8,12},{9,5},{12,14},{13,9},{14,10},{15,13... | collective-permute-start | bytes 1572872 | tf_op jit(solution)/shard_map/ppermute | solution.py:373
  78.9 1.5 %collective-permute-start.17 = (bf16[64,2048]{1,0:T(8,128)(2,1)S(1)}, bf16[64,2048]{1,0:T(8,128)(2,1)S(1)}, u32[]{:S(2)}, u32[]{:S(2)}) collective-permute-start(bf16[64,2048]{1,0:T(8,128)(2,1)S(1)} %collective-permute-done.14.refs_0_), channel_id=1, source_target_pairs={{0,1},{1,0},{2,3},{3,2},{4,5},{5,4},{6,7},{7,6},{8,9},{9,8},{10,11... | collective-permute-start | bytes 786440 | tf_op jit(solution)/shard_map/ppermute | solution.py:376
  79.0 1.9 %collective-permute-start.18 = (bf16[64,2048]{1,0:T(8,128)(2,1)S(1)}, bf16[64,2048]{1,0:T(8,128)(2,1)S(1)}, u32[]{:S(2)}, u32[]{:S(2)}) collective-permute-start(bf16[64,2048]{1,0:T(8,128)(2,1)S(1)} %collective-permute-done.15.refs_1_), channel_id=1, source_target_pairs={{0,1},{1,0},{2,3},{3,2},{4,5},{5,4},{6,7},{7,6},{8,9},{9,8},{10,11... | collective-permute-start | bytes 786440 | tf_op jit(solution)/shard_map/ppermute | solution.py:376
  84.5 2.5 %collective-permute-start.20 = (bf16[128,2048]{1,0:T(8,128)(2,1)S(1)}, bf16[128,2048]{1,0:T(8,128)(2,1)S(1)}, u32[]{:S(2)}, u32[]{:S(2)}) collective-permute-start(bf16[128,2048]{1,0:T(8,128)(2,1)S(1)} %collective-permute-done.19.refs_1_), channel_id=1, source_target_pairs={{0,1},{1,0},{2,3},{3,2},{4,5},{5,4},{6,7},{7,6},{8,9},{9,8},{10,11... | collective-permute-start | bytes 1572872 | tf_op jit(solution)/shard_map/ppermute | solution.py:376
  87.0 14.4 %copy-start.5 = (s32[128,8]{0,1:T(8,128)S(1)}, s32[128,8]{0,1:T(8,128)}, u32[]{:S(2)}) copy-start(s32[128,8]{0,1:T(8,128)} %param.12) | copy-start | bytes 12292

commit v14 on v11

--- a/solution.py
+++ b/solution.py
@@ -9,6 +9,7 @@
 
 DOC_TOK = 512
 LOAD_MIB = 40
+PAIR_MIB = 38
 
 
 def swiglu(rows, w_gate, w_up):
@@ -82,7 +83,9 @@
         ]
         for copy in copies[3 * tiles :] + copies[: 3 * tiles]:
             copy.start()
-    for i, block in enumerate(block_in):
+    if blocks == 1:
+        x_all, dy_all = block_in[0].at[:rows, :], block_in[0].at[rows:, :]
+    for i, block in enumerate(block_in if blocks > 1 else ()):
         place = slice((blocks - whole + i) * rows, (blocks - whole + i + 1) * rows)
         x_all[place, :] = block[:rows, :]
         dy_all[place, :] = block[rows:, :]
@@ -167,7 +170,98 @@
     return call(sheet, *apart, *block_in, *weights)
 
 
-def outcome_kernel(jobs, returned, routes, *refs):
+def front_part(x, weights):
+    w_gate, w_up, _, low_proj, _ = weights
+    across = (((1,), (1,)), ((), ()))
+    units = w_gate.shape[1]
+    tile = 256 if units % 256 == 0 else units
+    pieces, low = [], 0.0
+    for cut in range(0, units, tile):
+        part = pl.ds(cut, tile)
+        gate_val = jnp.dot(x[...], w_gate[:, part], preferred_element_type=jnp.float32)
+        up_val = jnp.dot(x[...], w_up[:, part], preferred_element_type=jnp.float32)
+        pieces.append((jax.nn.silu(gate_val) * up_val).astype(jnp.bfloat16))
+        low += lax.dot_general(
+            low_proj[:, part], pieces[-1], across, preferred_element_type=jnp.float32
+        )
+    return pieces, low
+
+
+def back_part(dy, pieces, weights):
+    _, _, w_down, _, high_proj = weights
+    across = (((1,), (1,)), ((), ()))
+    total, cut = 0.0, 0
+    for piece in pieces:
+        part = pl.ds(cut, piece.shape[1])
+        cut += piece.shape[1]
+        back = lax.dot_general(
+            dy[...], w_down[part, :], across, preferred_element_type=jnp.float32
+        )
+        terms = piece.astype(jnp.float32) * back
+        for spot in range(0, terms.shape[1], 128):
+            total += terms[:, spot : spot + 128]
+    proj = lax.dot_general(
+        high_proj[...], dy[...], across, preferred_element_type=jnp.float32
+    )
+    return jnp.sum(jnp.transpose(total), axis=0, keepdims=True), proj
+
+
+def other_kernel(name, block, *refs):
+    weights, sheet_in, sheet, out = refs[:5], *refs[5:]
+    rows = block.shape[0] // 2
+    pieces, low = front_part(block.at[:rows, :], weights)
+    line, proj = back_part(block.at[rows:, :], pieces, weights)
+    sheet[...] = sheet_in[...]
+    sheet[block_owner(name, sheet.shape[0] // 2), 3:4, :] = line
+    out[: low.shape[0], :] = low
+    out[low.shape[0] :, :] = proj
+
+
+def front_kernel(x, *refs):
+    hidden, low_side, hidden_other, low_other = refs[10:]
+    for weights, units, low in (
+        (refs[:5], hidden, low_side),
+        (refs[5:10], hidden_other, low_other),
+    ):
+        pieces, value = front_part(x, weights)
+        low[...] = value.astype(low.dtype)
+        for i, piece in enumerate(pieces):
+            width = piece.shape[1]
+            units[:, i * width : (i + 1) * width] = piece
+
+
+def back_kernel(name, dy, hidden, hidden_other, low_other, before, *refs):
+    sheet_in, sheet, proj_cot, other = refs[10:]
+    sheet[...] = sheet_in[...]
+    owner = block_owner(name, sheet.shape[0] // 2)
+    rank = proj_cot.shape[0]
+    other[0] = before[...]
+    other[1, :rank, :] = low_other[...]
+    for which, units in enumerate((hidden, hidden_other)):
+        width = units.shape[1]
+        tile = 256 if width % 256 == 0 else width
+        pieces = [units[:, cut : cut + tile] for cut in range(0, width, tile)]
+        line, proj = back_part(dy, pieces, refs[5 * which : 5 * which + 5])
+        sheet[owner, 3 * which : 3 * which + 1, :] = line
+        if which:
+            other[1, rank:, :] = proj
+        else:
+            proj_cot[...] = proj
+
+
+def on_core(kernel, args, out_shape, flops=0):
+    inside = pl.BlockSpec(memory_space=pltpu.VMEM)
+    return pl.pallas_call(
+        kernel,
+        out_shape=out_shape,
+        in_specs=[inside] * len(args),
+        out_specs=[inside] * len(out_shape),
+        compiler_params=pltpu.CompilerParams(vmem_limit_bytes=16 * 1024 * 1024),
+        cost_estimate=pl.CostEstimate(flops=flops, bytes_accessed=2**20, transcendentals=0),
+    )(*args)
+
+
+def outcome_kernel(jobs, late, returned, routes, handed, *refs):
     low_in, proj_in = refs[: len(jobs)], refs[len(jobs) : 2 * len(jobs)]
     feat, route_grad = refs[-2:]
     rows = returned.shape[2]
@@ -190,10 +284,29 @@
             (((1,), (1,)), ((), ())),
             preferred_element_type=jnp.float32,
         )
+    spread, high_side = [], []
+    for i, (chain, step, _) in enumerate(late):
+        owner = block_owner((chain, step, True), returned.shape[0] // 2)
+        weight = returned[owner, 1:2, :]
+        doc = returned[owner, 2:3, :].astype(jnp.int32)
+        high_side.append((weight * handed[i, rank:, :]).astype(jnp.bfloat16))
+        low = handed[i, :rank, :].astype(jnp.bfloat16).astype(jnp.float32)
+        parts = [jnp.where(doc == d, low, 0.0) for d in range(width // rank)]
+        spread.append(jnp.concatenate(parts, axis=0).astype(jnp.bfloat16))
+    total += lax.dot_general(
+        jnp.concatenate(spread, axis=1),
+        jnp.concatenate(high_side, axis=1),
+        (((1,), (1,)), ((), ())),
+        preferred_element_type=jnp.float32,
+    )
     feat[...] = total
     picked = jnp.zeros(route_grad.shape, jnp.float32)
     for e in range(returned.shape[0]):
         picked = jnp.where(routes[...] == e, returned[e, 0:1, :], picked)
+    for name in late:
+        sender = block_owner(name, returned.shape[0] // 2)
+        other = sender + 1 - 2 * lax.rem(sender, 2)
+        picked = jnp.where(routes[...] == other, returned[sender, 3:4, :], picked)
     route_grad[...] = picked
 
 
@@ -225,6 +338,41 @@
         out_specs=inside,
         compiler_params=pltpu.CompilerParams(vmem_limit_bytes=8 * 1024 * 1024),
     )(top, bottom)
+
+
+def split_kernel(block, top, bottom):
+    rows = top.shape[0]
+    top[...] = block[:rows, :]
+    bottom[...] = block[rows:, :]
+
+
+def split(block):
+    half = jax.ShapeDtypeStruct((block.shape[0] // 2, block.shape[1]), block.dtype)
+    return on_core(split_kernel, (block,), [half] * 2)
+
+
+def load_kernel(*refs):
+    ins, outs, sems = refs[:5], refs[5:10], refs[10]
+    other = 1 - lax.rem(lax.axis_index("exp"), 2)
+    copies = [
+        pltpu.make_async_copy(src.at[other], dst, sems.at[i])
+        for i, (src, dst) in enumerate(zip(ins, outs))
+    ]
+    for copy in copies:
+        copy.start()
+    for copy in copies:
+        copy.wait()
+
+
+def load_other(pairs):
+    return pl.pallas_call(
+        load_kernel,
+        out_shape=[jax.ShapeDtypeStruct(w.shape[1:], w.dtype) for w in pairs],
+        in_specs=[pl.BlockSpec(memory_space=pl.ANY)] * len(pairs),
+        out_specs=[pl.BlockSpec(memory_space=pltpu.VMEM)] * len(pairs),
+        scratch_shapes=[pltpu.SemaphoreType.DMA((len(pairs),))],
+        compiler_params=pltpu.CompilerParams(vmem_limit_bytes=PAIR_MIB * 1024 * 1024),
+    )(*pairs)
 
 
 def by_ring(
@@ -256,13 +404,16 @@
             job += (arrivals[i - 1] + (True,),)
         if i == 1:
             job += (arrivals[0] + (False,),)
-        if i != 0:
+        if i == len(arrivals) - 1:
+            jobs.append(job[:1])
+        elif i == len(arrivals) - 2:
+            jobs += [job[:1], job[1:]]
+        elif i != 0:
             jobs.append(job)
-    jobs.append((arrivals[-1] + (True,),))
 
     sheet = pl.pallas_call(
         facts_kernel,
-        out_shape=jax.ShapeDtypeStruct((groups, 8, tok_rows), jnp.float32),
+        out_shape=jax.ShapeDtypeStruct((groups, 4, tok_rows), jnp.float32),
         in_specs=[pl.BlockSpec(memory_space=pltpu.VMEM)] * 3,
         out_specs=pl.BlockSpec(memory_space=pltpu.VMEM),
         compiler_params=pltpu.CompilerParams(vmem_limit_bytes=8 * 1024 * 1024),
@@ -291,29 +442,79 @@
         projs.append(proj_cot)
 
     chain = {"b": beside}
-    for i, (c, step) in enumerate(arrivals):
+    pairs = [[i, i + 1] for i in range(0, groups, 2)]
+    gathered = [
+        lax.all_gather(w, "exp", axis_index_groups=pairs, axis=0) for w in given
+    ]
+    for i, (c, step) in enumerate(arrivals[:-1]):
         block = hop(chain[c]) if i > 0 else first
         if i != 1:
             take()
             sheet, block = lax.optimization_barrier((sheet, block))
+        if i == len(arrivals) - 3:
+            sheet, gathered = lax.optimization_barrier((sheet, gathered))
+            others = load_other(gathered)
+            others, block = lax.optimization_barrier((others, block))
         if i == 0:
             block = stack(*block)
         chain[c] = held[(c, step, False)] = block
-        held[(c, step, True)] = swap(block)
-    while todo:
-        take()
+        if i < len(arrivals) - 2:
+            held[(c, step, True)] = swap(block)
+    x, dy = split(chain["a"])
+    late = (arrivals[-2] + (False,), arrivals[-1] + (False,))
+    dy, block = lax.optimization_barrier((dy, chain["b"]))
+    held[late[0]] = block
+    x, dy = hop(x), hop(dy)
+    take()
+    rank, units = proj_output.shape[2], w_gate.shape[2]
+    flops = 2 * tok_rows * tokens.shape[1] * units
+    lines = jax.ShapeDtypeStruct((2 * rank, tok_rows), jnp.float32)
+    sheet_shape = jax.ShapeDtypeStruct(sheet.shape, jnp.float32)
+    sheet, before = on_core(
+        functools.partial(other_kernel, late[0]),
+        (block, *others, sheet),
+        [sheet_shape, lines],
+        flops=3 * flops,
+    )
+    sheet, x = lax.optimization_barrier((sheet, x))
+    hidden = jax.ShapeDtypeStruct((tok_rows, units), jnp.bfloat16)
+    hidden, low_side, hidden_other, low_other = on_core(
+        front_kernel,
+        (x, *weights, *others),
+        [
+            hidden,
+            jax.ShapeDtypeStruct((docs_count * rank, tok_rows), jnp.bfloat16),
+            hidden,
+            jax.ShapeDtypeStruct((rank, tok_rows), jnp.float32),
+        ],
+        flops=4 * flops,
+    )
+    take()
+    sheet, dy = lax.optimization_barrier((sheet, dy))
+    sheet, proj_cot, other = on_core(
+        functools.partial(back_kernel, late[1]),
+        (dy, hidden, hidden_other, low_other, before, *weights, *others, sheet),
+        [
+            sheet_shape,
+            jax.ShapeDtypeStruct((rank, tok_rows), jnp.float32),
+            jax.ShapeDtypeStruct((2,) + lines.shape, jnp.float32),
+        ],
+        flops=2 * flops,
+    )
+    lows.append(low_side)
+    projs.append(proj_cot)
+    handed = swap(other)
     returned = lax.all_to_all(sheet, "exp", split_axis=0, concat_axis=0, tiled=True)
-    rank = proj_output.shape[2]
     feature, route_grad = pl.pallas_call(
-        functools.partial(outcome_kernel, jobs),
+        functools.partial(outcome_kernel, jobs, late),
         out_shape=[
             jax.ShapeDtypeStruct((docs_count * rank, rank), jnp.float32),
             jax.ShapeDtypeStruct((chosen, tok_rows), jnp.float32),
         ],
-        in_specs=[inside] * (2 + 2 * len(lows)),
+        in_specs=[inside] * (3 + 2 * len(lows)),
         out_specs=[inside] * 2,
         compiler_params=pltpu.CompilerParams(vmem_limit_bytes=16 * 1024 * 1024),
-    )(returned, routes.T, *lows, *projs)
+    )(returned, routes.T, handed, *lows, *projs)
     return feature.reshape(docs_count, 1, rank, rank), route_grad.T
 
 

time: 105 us -> 123 us (1.17)
  Pallas kernels: 31.6 us -> 47.1 us
  waiting for transfers between devices: 36.3 us -> 20.8 us
  between operations: 0.74 us -> 14.2 us
  starting transfers between devices: 16.9 us -> 18.8 us
  blocking collectives: 13.3 us -> 15.1 us
    ppermute x8 -> x9, waiting for transfers between devices: 36.3 us -> 18.7 us  [hop(): return lax.ppermute(block, 'exp', onward)]
    pallas_call x2 -> x7, Pallas kernels: 1.13 us -> 15.6 us  [the longest x4 10.5 us: on_core(): pl.pallas_call(kernel, out_shape=out_shape, in_specs=[inside] * len(args)...]
    all_gather x0 -> x2, blocking collectives: none -> 5.03 us  [by_ring(): lax.all_gather(w, 'exp', axis_index_groups=pairs, axis=0)]
    all_to_all x1, blocking collectives: 13.3 us -> 10.1 us  [by_ring(): lax.all_to_all(sheet, 'exp', split_axis=0, concat_axis=0, tiled=True)]
    unnamed x0 -> x3, waiting for transfers between devices: none -> 2.06 us
    ppermute x8 -> x9, starting transfers between devices: 16.2 us -> 17.7 us  [hop(): return lax.ppermute(block, 'exp', onward)]
    pallas_call x8 -> x7, Pallas kernels: 30.3 us -> 31.3 us  [work(): return call(sheet, *apart, *block_in, *weights)]
    unnamed x16 -> x62, local copies, waits for them, and re-layouts: 5.95 us -> 6.4 us
  transfers between devices with their start and end apart: 17 -> 20, of which waited for: 6 -> 3; matrix products, arithmetic and copies ran while one was open for 0% -> 0% of each run, Pallas kernels for 27% -> 35%
where the time goes in v14:
time: 123 us; the launch traced here: 122 us
  Pallas kernels  47.1 us (38%)
  waiting for transfers between devices  20.8 us (17%)
  starting transfers between devices  18.8 us (15%)
  blocking collectives  15.1 us (12%)
  between operations  14.2 us (12%)
  local copies, waits for them, and re-layouts  6.4 us (5%)
    pallas_call x7, Pallas kernels, work(): return call(sheet, *apart, *block_in, *weights)  31.3 us
    ppermute x9, waiting for transfers between devices, hop(): return lax.ppermute(block, 'exp', onward)  18.7 us
    ppermute x9, starting transfers between devices, hop(): return lax.ppermute(block, 'exp', onward)  17.7 us
    pallas_call x4, Pallas kernels, on_core(): pl.pallas_call(kernel, out_shape=out_shape, in_specs=[inside] * len(args)...  10.5 us
    all_to_all x1, blocking collectives, by_ring(): lax.all_to_all(sheet, 'exp', split_axis=0, concat_axis=0, tiled=True)  10.1 us
    unnamed x62, local copies, waits for them, and re-layouts  6.4 us
    all_gather x2, blocking collectives, by_ring(): lax.all_gather(w, 'exp', axis_index_groups=pairs, axis=0)  5.03 us
    pallas_call x1, Pallas kernels, load_other(): pl.pallas_call(load_kernel, out_shape=[jax.ShapeDtypeStruct(w.shape[1:],...  3.95 us
  transfers between devices with their start and end apart: 20, of which 3 were waited for; matrix products, arithmetic and copies ran while one was open for 0% of the time, Pallas kernels for 35%

profile of v14, /device:TPU:0, one launch (start us, length us, event | category | flops | bytes accessed | tf_op | source)
XLA Modules:
  0.0 122.3 jit_solution(17580841433481951092)
XLA Ops:
  7.2 0.7 all-gather.10.cloned.1.call-update
  7.9 0.0 all-gather.6.cloned.1.call-start
  7.9 0.7 all-gather.6.cloned.1.call-update
  8.7 0.0 all-gather.8.cloned.1.call-start
  8.7 0.7 all-gather.8.cloned.1.call-update
  9.4 0.5 collective-permute-start
  9.9 0.1 collective-permute-start.1
  10.0 3.0 %collective-permute-start.2 = (bf16[128,2048]{1,0:T(8,128)(2,1)}, bf16[128,2048]{1,0:T(8,128)(2,1)S(1)}, u32[]{:S(2)}, u32[]{:S(2)}) collective-permute-start(bf16[128,2048]{1,0:T(8,128)(2,1)} %refs_1_.1), channel_id=1, source_target_pairs={{0,4},{1,3},{4,8},{5,1},{8,12},{9,5},{12,14},{13,9},{14,10},{15,13... | collective-permute-start | bytes 1572872 | tf_op jit(solution)/shard_map/ppermute | solution.py:394
  13.0 1.6 %collective-permute-start.3 = (bf16[128,2048]{1,0:T(8,128)(2,1)}, bf16[128,2048]{1,0:T(8,128)(2,1)S(1)}, u32[]{:S(2)}, u32[]{:S(2)}) collective-permute-start(bf16[128,2048]{1,0:T(8,128)(2,1)} %refs_2_.1), channel_id=1, source_target_pairs={{0,4},{1,3},{4,8},{5,1},{8,12},{9,5},{12,14},{13,9},{14,10},{15,13... | collective-permute-start | bytes 1572872 | tf_op jit(solution)/shard_map/ppermute | solution.py:394
  14.6 0.1 shard_map.114.refs_3_
  14.7 1.6 %collective-permute-start.4 = (bf16[256,2048]{1,0:T(8,128)(2,1)S(1)}, bf16[256,2048]{1,0:T(8,128)(2,1)S(1)}, u32[]{:S(2)}, u32[]{:S(2)}) collective-permute-start(bf16[256,2048]{1,0:T(8,128)(2,1)S(1)} %shard_map.114.refs_3_), channel_id=1, source_target_pairs={{0,4},{1,3},{4,8},{5,1},{8,12},{9,5},{12,14},{13,9},{14,10},{15,13... | collective-permute-start | bytes 3145736 | tf_op jit(solution)/shard_map/ppermute | solution.py:394
  16.3 0.9 copy-done.7
  17.3 0.9 copy-done.9
  18.2 7.8 %shard_map.115 = (f32[16,4,128]{2,1,0:T(4,128)S(1)}, bf16[256,256]{1,0:T(8,128)(2,1)S(1)}, f32[64,256]{1,0:T(8,128)S(1)}, bf16[2048,768]{1,0:T(8,128)(2,1)S(1)},...) custom-call(f32[16,4,128]{2,1,0:T(4,128)S(1)} %shard_map.113.refs_0_, ...), custom_call_target="tpu_custom_call" | custom-call | flops 2415919104 | bytes 2097152 | tf_op jit(solution)/shard_map/pallas_call | solution.py:170
  26.1 0.1 shard_map.116.refs_3_
  26.2 0.1 collective-permute-start.5
  26.2 2.0 %collective-permute-start.6 = (bf16[256,2048]{1,0:T(8,128)(2,1)S(1)}, bf16[256,2048]{1,0:T(8,128)(2,1)S(1)}, u32[]{:S(2)}, u32[]{:S(2)}) collective-permute-start(bf16[256,2048]{1,0:T(8,128)(2,1)S(1)} %shard_map.116.refs_3_), channel_id=1, source_target_pairs={{0,4},{1,3},{4,8},{5,1},{8,12},{9,5},{12,14},{13,9},{14,10},{15,13... | collective-permute-start | bytes 3145736 | tf_op jit(solution)/shard_map/ppermute | solution.py:394
  28.2 8.9 %collective-permute-done.4.refs_1_ = bf16[256,2048]{1,0:T(8,128)(2,1)S(1)} collective-permute-done((bf16[256,2048]{1,0:T(8,128)(2,1)S(1)}, bf16[256,2048]{1,0:T(8,128)(2,1)S(1)}, u32[]{:S(2)}, u32[]{:S(2)}) %collective-permute-start.4) | collective-permute-done | bytes 1048608 | tf_op jit(solution)/shard_map/ppermute | solution.py:394
  37.2 2.1 %collective-permute-start.8 = (bf16[256,2048]{1,0:T(8,128)(2,1)S(1)}, bf16[256,2048]{1,0:T(8,128)(2,1)}, u32[]{:S(2)}, u32[]{:S(2)}) collective-permute-start(bf16[256,2048]{1,0:T(8,128)(2,1)S(1)} %collective-permute-done.4.refs_1_), channel_id=1, source_target_pairs={{0,4},{1,3},{4,8},{5,1},{8,12},{9,5},{12,14},{13,9},{14,10},{15,13... | collective-permute-start | bytes 3145736 | tf_op jit(solution)/shard_map/ppermute | solution.py:394
  39.3 4.6 %shard_map.117 = (f32[16,4,128]{2,1,0:T(4,128)S(1)}, bf16[256,384]{1,0:T(8,128)(2,1)S(1)}, f32[64,384]{1,0:T(8,128)S(1)}) custom-call(f32[16,4,128]{2,1,0:T(4,128)S(1)} %get-tuple-element.76.refs_0_, bf16[256,2048]{1,0:T(8,128)(2,1)S(1)} %collective-permute-done.4.refs_1_, bf16[256,2048]{1,0:T(8,128)(2,1)S(1)} %collective-permute-done.5.refs_2_, ...), custom_call_target="tpu_custom_call" | custom-call | flops 3623878656 | bytes 3145728 | tf_op jit(solution)/shard_map/pallas_call | solution.py:170
  43.9 0.6 copy-done.18
  44.6 3.8 %collective-permute-done.6.refs_1_ = bf16[256,2048]{1,0:T(8,128)(2,1)S(1)} collective-permute-done((bf16[256,2048]{1,0:T(8,128)(2,1)S(1)}, bf16[256,2048]{1,0:T(8,128)(2,1)S(1)}, u32[]{:S(2)}, u32[]{:S(2)}) %collective-permute-start.6) | collective-permute-done | bytes 1048608 | tf_op jit(solution)/shard_map/ppermute | solution.py:394
  48.4 2.1 %collective-permute-start.10 = (bf16[256,2048]{1,0:T(8,128)(2,1)S(1)}, bf16[256,2048]{1,0:T(8,128)(2,1)}, u32[]{:S(2)}, u32[]{:S(2)}) collective-permute-start(bf16[256,2048]{1,0:T(8,128)(2,1)S(1)} %collective-permute-done.6.refs_1_), channel_id=1, source_target_pairs={{0,4},{1,3},{4,8},{5,1},{8,12},{9,5},{12,14},{13,9},{14,10},{15,13... | collective-permute-start | bytes 3145736 | tf_op jit(solution)/shard_map/ppermute | solution.py:394
  50.5 3.3 %shard_map.118 = (f32[16,4,128]{2,1,0:T(4,128)S(1)}, bf16[256,256]{1,0:T(8,128)(2,1)S(1)}, f32[64,256]{1,0:T(8,128)S(1)}) custom-call(f32[16,4,128]{2,1,0:T(4,128)S(1)} %get-tuple-element.85.refs_0_, bf16[256,2048]{1,0:T(8,128)(2,1)S(1)} %collective-permute-done.6.refs_1_, bf16[256,2048]{1,0:T(8,128)(2,1)S(1)} %collective-permute-done.7.refs_2_, ...), custom_call_target="tpu_custom_call" | custom-call | flops 2415919104 | bytes 2097152 | tf_op jit(solution)/shard_map/pallas_call | solution.py:170
  53.9 5.9 %collective-permute-done.8.refs_1_ = bf16[256,2048]{1,0:T(8,128)(2,1)} collective-permute-done((bf16[256,2048]{1,0:T(8,128)(2,1)S(1)}, bf16[256,2048]{1,0:T(8,128)(2,1)}, u32[]{:S(2)}, u32[]{:S(2)}) %collective-permute-start.8) | collective-permute-done | bytes 1048608 | tf_op jit(solution)/shard_map/ppermute | solution.py:394
  59.7 2.1 %collective-permute-start.12 = (bf16[256,2048]{1,0:T(8,128)(2,1)}, bf16[256,2048]{1,0:T(8,128)(2,1)}, u32[]{:S(2)}, u32[]{:S(2)}) collective-permute-start(bf16[256,2048]{1,0:T(8,128)(2,1)} %collective-permute-done.8.refs_1_), channel_id=1, source_target_pairs={{0,4},{1,3},{4,8},{5,1},{8,12},{9,5},{12,14},{13,9},{14,10},{15,13... | collective-permute-start | bytes 3145736 | tf_op jit(solution)/shard_map/ppermute | solution.py:394
  61.8 2.2 %all-gather = bf16[128,768]{1,0:T(8,128)(2,1)} all-gather(bf16[64,768]{1,0:T(8,128)(2,1)S(1)} %bitcast.23), channel_id=2, replica_groups={{0,1},{2,3},{4,5},{6,7},{8,9},{10,11},{12,13},{14,15},{16,17},{18,19},{..., dimensions={0}, use_global_device_ids=true | all-gather | bytes 294912 | tf_op jit(solution)/shard_map/all_gather | solution.py:447
  64.0 2.9 %all-gather.1 = bf16[128,2048]{1,0:T(8,128)(2,1)} all-gather(bf16[64,2048]{1,0:T(8,128)(2,1)S(1)} %bitcast.20), channel_id=3, replica_groups={{0,1},{2,3},{4,5},{6,7},{8,9},{10,11},{12,13},{14,15},{16,17},{18,19},{..., dimensions={0}, use_global_device_ids=true | all-gather | bytes 786432 | tf_op jit(solution)/shard_map/all_gather | solution.py:447
  66.9 4.6 %shard_map.119 = (f32[16,4,128]{2,1,0:T(4,128)S(1)}, bf16[256,256]{1,0:T(8,128)(2,1)S(1)}, f32[64,256]{1,0:T(8,128)S(1)}) custom-call(f32[16,4,128]{2,1,0:T(4,128)S(1)} %get-tuple-element.88.refs_0_, bf16[256,2048]{1,0:T(8,128)(2,1)} %collective-permute-done.8.refs_1_, bf16[256,2048]{1,0:T(8,128)(2,1)S(1)} %collective-permute-done.9.refs_2_, ...), custom_call_target="tpu_custom_call" | custom-call | flops 2415919104 | bytes 2097152 | tf_op jit(solution)/shard_map/pallas_call | solution.py:170
  71.5 0.6 copy-done.16
  72.1 0.6 copy-done.24
  72.7 0.6 copy-done.26
  73.4 1.0 copy-done.6
  74.4 0.9 copy-done.8
  75.3 4.0 %shard_map.120 = (bf16[2048,768]{1,0:T(8,128)(2,1)S(1)}, bf16[2048,768]{1,0:T(8,128)(2,1)S(1)}, bf16[768,2048]{1,0:T(8,128)(2,1)S(1)}, bf16[64,768]{1,0:T(8,128)(2,1)S(1)}, bf16[64,2048]{1,0:T(8,128)(2,1)S(1)}) custom-call(bf16[2,2048,768]{2,1,0:T(8,128)(2,1)} %all-gather.6.cloned.1.call-done.refs_0_, ...), custom_call_target="tpu_custom_call" | custom-call | tf_op jit(solution)/shard_map/pallas_call | solution.py:368
  79.3 0.2 collective-permute-start.14
  79.5 1.8 %shard_map.121 = (bf16[128,2048]{1,0:T(8,128)(2,1)S(1)}, bf16[128,2048]{1,0:T(8,128)(2,1)S(1)}) custom-call(bf16[256,2048]{1,0:T(8,128)(2,1)} %collective-permute-done.10.block.refs_1_), custom_call_target="tpu_custom_call" | custom-call | bytes 1048576 | tf_op jit(solution)/shard_map/pallas_call | solution.py:254
  81.3 1.5 %collective-permute-start.13 = (bf16[128,2048]{1,0:T(8,128)(2,1)S(1)}, bf16[128,2048]{1,0:T(8,128)(2,1)S(1)}, u32[]{:S(2)}, u32[]{:S(2)}) collective-permute-start(bf16[128,2048]{1,0:T(8,128)(2,1)S(1)} %get-tuple-element.117), channel_id=1, source_target_pairs={{0,4},{1,3},{4,8},{5,1},{8,12},{9,5},{12,14},{13,9},{14,10},{15,13... | collective-permute-start | bytes 1572872 | tf_op jit(solution)/shard_map/ppermute | solution.py:394
  82.9 4.9 %shard_map.122 = (f32[16,4,128]{2,1,0:T(4,128)S(1)}, bf16[256,256]{1,0:T(8,128)(2,1)S(1)}, f32[64,256]{1,0:T(8,128)S(1)}) custom-call(f32[16,4,128]{2,1,0:T(4,128)S(1)} %copy-done.27, bf16[256,2048]{1,0:T(8,128)(2,1)} %collective-permute-done.10.block.refs_1_, bf16[256,2048]{1,0:T(8,128)(2,1)} %collective-permute-done.11.refs_2_, ...), custom_call_target="tpu_custom_call" | custom-call | flops 2415919104 | bytes 2097152 | tf_op jit(solution)/shard_map/pallas_call | solution.py:170
  87.8 1.7 %collective-permute-start.15 = (bf16[128,2048]{1,0:T(8,128)(2,1)S(1)}, bf16[128,2048]{1,0:T(8,128)(2,1)S(1)}, u32[]{:S(2)}, u32[]{:S(2)}) collective-permute-start(bf16[128,2048]{1,0:T(8,128)(2,1)S(1)} %get-tuple-element.120), channel_id=1, source_target_pairs={{0,4},{1,3},{4,8},{5,1},{8,12},{9,5},{12,14},{13,9},{14,10},{15,13... | collective-permute-start | bytes 1572872 | tf_op jit(solution)/shard_map/ppermute | solution.py:394
  89.4 3.7 %shard_map.123 = (f32[16,4,128]{2,1,0:T(4,128)S(1)}, bf16[256,128]{1,0:T(8,128)(2,1)S(1)}, f32[64,128]{1,0:T(8,128)S(1)}) custom-call(f32[16,4,128]{2,1,0:T(4,128)S(1)} %get-tuple-element.114.refs_0_, bf16[256,2048]{1,0:T(8,128)(2,1)} %collective-permute-done.12.refs_1_.block, bf16[2048,768]{1,0:T(8,128)(2,1)S(1)} %get-tuple-element.79.refs_4_.refs_3_.refs_2_.refs_0_, ...), custom_call_target="tpu_custom_call" | custom-call | flops 1207959552 | bytes 1048576 | tf_op jit(solution)/shard_map/pallas_call | solution.py:170
  93.1 3.6 %shard_map.124 = (f32[16,4,128]{2,1,0:T(4,128)S(1)}, f32[128,128]{1,0:T(8,128)S(1)}) custom-call(bf16[256,2048]{1,0:T(8,128)(2,1)} %collective-permute-done.12.refs_1_.block, bf16[2048,768]{1,0:T(8,128)(2,1)S(1)} %get-tuple-element.109.refs_0_.refs_5_, bf16[2048,768]{1,0:T(8,128)(2,1)S(1)} %get-tuple-element.110.refs_1_.refs_6_, ...), custom_call_target="tpu_custom_call" | custom-call | flops 1207959552 | bytes 1048576 | tf_op jit(solution)/shard_map/pallas_call | solution.py:254
  96.7 2.5 %shard_map.126 = (bf16[128,768]{1,0:T(8,128)(2,1)S(1)}, bf16[256,128]{1,0:T(8,128)(2,1)S(1)}, bf16[128,768]{1,0:T(8,128)(2,1)S(1)}, f32[64,128]{1,0:T(8,128)S(1)}) custom-call(bf16[128,2048]{1,0:T(8,128)(2,1)S(1)} %collective-permute-done.13.x, bf16[2048,768]{1,0:T(8,128)(2,1)S(1)} %get-tuple-element.79.refs_4_.refs_3_.refs_2_.refs_0_, ...), custom_call_target="tpu_custom_call" | custom-call | flops 1610612736 | bytes 1048576 | tf_op jit(solution)/shard_map/pallas_call | solution.py:254
  99.3 2.5 %shard_map.125 = (f32[16,4,128]{2,1,0:T(4,128)S(1)}, bf16[256,128]{1,0:T(8,128)(2,1)S(1)}, f32[64,128]{1,0:T(8,128)S(1)}) custom-call(f32[16,4,128]{2,1,0:T(4,128)S(1)} %get-tuple-element.118.refs_0_, bf16[256,2048]{1,0:T(8,128)(2,1)S(1)} %collective-permute-done.14.refs_1_, bf16[2048,768]{1,0:T(8,128)(2,1)S(1)} %get-tuple-element.79.refs_4_.refs_3_.refs_2_.refs_0_, ...), custom_call_target="tpu_custom_call" | custom-call | flops 1207959552 | bytes 1048576 | tf_op jit(solution)/shard_map/pallas_call | solution.py:170
  101.9 2.5 %shard_map.127 = (f32[16,4,128]{2,1,0:T(4,128)S(1)}, f32[64,128]{1,0:T(8,128)S(1)}, f32[2,128,128]{2,1,0:T(8,128)S(1)}) custom-call(bf16[128,2048]{1,0:T(8,128)(2,1)S(1)} %collective-permute-done.15.dy, bf16[128,768]{1,0:T(8,128)(2,1)S(1)} %get-tuple-element.123.hidden, bf16[128,768]{1,0:T(8,128)(2,1)S(1)} %get-tuple-element.124.hidden_other, ...), custom_call_target="tpu_custom_call" | custom-call | flops 805306368 | bytes 1048576 | tf_op jit(solution)/shard_map/pallas_call | solution.py:254
  104.4 0.1 collective-permute-start.16
  104.5 10.1 %all_to_all.5.returned = f32[16,4,128]{2,1,0:T(4,128)S(1)} all-to-all(f32[16,4,128]{2,1,0:T(4,128)S(1)} %get-tuple-element.128), channel_id=1, replica_groups=mesh['grp'=2,'exp'=16] {'exp'}, dimensions={0} | all-to-all | bytes 65536 | tf_op jit(solution)/shard_map/all_to_all | solution.py:507
  114.7 1.1 shard_map.128
  (76 shorter events, 0.3 us)
Async XLA Ops:
  7.2 66.2 %all-gather.10.cloned.1.call-start = ((), (), s32[]{:S(2)}) async-start(), calls=%async_computation.3 | async-start | bytes 9437184 | tf_op jit(solution)/shard_map/all_gather | solution.py:447
  7.9 65.4 %all-gather.6.cloned.1.call-start = ((), (), s32[]{:S(2)}) async-start(), calls=%async_computation.1 | async-start | bytes 9437184 | tf_op jit(solution)/shard_map/all_gather | solution.py:447
  8.6 7.7 %copy-start.28 = (s32[128,8]{0,1:T(8,128)S(1)}, s32[128,8]{0,1:T(8,128)}, u32[]{:S(2)}) copy-start(s32[128,8]{0,1:T(8,128)} %param.12) | copy-start | bytes 12292
  8.7 7.6 %copy-start.29 = (bf16[128,8]{0,1:T(8,128)(2,1)S(1)}, bf16[128,8]{0,1:T(8,128)(2,1)}, u32[]{:S(2)}) copy-start(bf16[128,8]{0,1:T(8,128)(2,1)} %param.13) | copy-start | bytes 6148
  8.7 7.6 %copy-start.30 = (s32[128]{0:T(128)S(1)}, s32[128]{0:T(128)}, u32[]{:S(2)}) copy-start(s32[128]{0:T(128)} %param.14) | copy-start | bytes 1540
  8.7 64.7 %all-gather.8.cloned.1.call-start = ((), (), s32[]{:S(2)}) async-start(), calls=%async_computation.2 | async-start | bytes 9437184 | tf_op jit(solution)/shard_map/all_gather | solution.py:447
  9.4 5.2 %collective-permute-start = (bf16[128,2048]{1,0:T(8,128)(2,1)}, bf16[128,2048]{1,0:T(8,128)(2,1)S(1)}, u32[]{:S(2)}, u32[]{:S(2)}) collective-permute-start(bf16[128,2048]{1,0:T(8,128)(2,1)} %refs_1_.1), channel_id=1, source_target_pairs={{0,1},{1,0},{2,3},{3,2},{4,5},{5,4},{6,7},{7,6},{8,9},{9,8},{10,11... | collective-permute-start | bytes 1572872 | tf_op jit(solution)/shard_map/ppermute | solution.py:397
  9.9 4.7 %collective-permute-start.1 = (bf16[128,2048]{1,0:T(8,128)(2,1)}, bf16[128,2048]{1,0:T(8,128)(2,1)S(1)}, u32[]{:S(2)}, u32[]{:S(2)}) collective-permute-start(bf16[128,2048]{1,0:T(8,128)(2,1)} %refs_2_.1), channel_id=1, source_target_pairs={{0,1},{1,0},{2,3},{3,2},{4,5},{5,4},{6,7},{7,6},{8,9},{9,8},{10,11... | collective-permute-start | bytes 1572872 | tf_op jit(solution)/shard_map/ppermute | solution.py:397
  10.0 16.1 %collective-permute-start.2 = (bf16[128,2048]{1,0:T(8,128)(2,1)}, bf16[128,2048]{1,0:T(8,128)(2,1)S(1)}, u32[]{:S(2)}, u32[]{:S(2)}) collective-permute-start(bf16[128,2048]{1,0:T(8,128)(2,1)} %refs_1_.1), channel_id=1, source_target_pairs={{0,4},{1,3},{4,8},{5,1},{8,12},{9,5},{12,14},{13,9},{14,10},{15,13... | collective-permute-start | bytes 1572872 | tf_op jit(solution)/shard_map/ppermute | solution.py:394
  13.0 13.1 %collective-permute-start.3 = (bf16[128,2048]{1,0:T(8,128)(2,1)}, bf16[128,2048]{1,0:T(8,128)(2,1)S(1)}, u32[]{:S(2)}, u32[]{:S(2)}) collective-permute-start(bf16[128,2048]{1,0:T(8,128)(2,1)} %refs_2_.1), channel_id=1, source_target_pairs={{0,4},{1,3},{4,8},{5,1},{8,12},{9,5},{12,14},{13,9},{14,10},{15,13... | collective-permute-start | bytes 1572872 | tf_op jit(solution)/shard_map/ppermute | solution.py:394
  14.7 22.5 %collective-permute-start.4 = (bf16[256,2048]{1,0:T(8,128)(2,1)S(1)}, bf16[256,2048]{1,0:T(8,128)(2,1)S(1)}, u32[]{:S(2)}, u32[]{:S(2)}) collective-permute-start(bf16[256,2048]{1,0:T(8,128)(2,1)S(1)} %shard_map.114.refs_3_), channel_id=1, source_target_pairs={{0,4},{1,3},{4,8},{5,1},{8,12},{9,5},{12,14},{13,9},{14,10},{15,13... | collective-permute-start | bytes 3145736 | tf_op jit(solution)/shard_map/ppermute | solution.py:394
  16.3 1.0 copy-start.7
  17.3 0.9 copy-start.9
  26.0 17.9 %copy-start.12 = (bf16[256,256]{1,0:T(8,128)(2,1)}, bf16[256,256]{1,0:T(8,128)(2,1)S(1)}, u32[]{:S(2)}) copy-start(bf16[256,256]{1,0:T(8,128)(2,1)S(1)} %get-tuple-element.130.refs_0_) | copy-start | bytes 393220
  26.0 17.9 %copy-start.20 = (f32[64,256]{1,0:T(8,128)}, f32[64,256]{1,0:T(8,128)S(1)}, u32[]{:S(2)}) copy-start(f32[64,256]{1,0:T(8,128)S(1)} %get-tuple-element.138.refs_8_) | copy-start | bytes 196612
  26.0 40.8 %copy-start = (bf16[2048,768]{1,0:T(8,128)(2,1)}, bf16[2048,768]{1,0:T(8,128)(2,1)S(1)}, u32[]{:S(2)}) copy-start(bf16[2048,768]{1,0:T(8,128)(2,1)S(1)} %get-tuple-element.80.refs_5_.refs_4_.refs_3_.refs_1_) | copy-start | bytes 9437188
  26.0 40.8 %copy-start.2 = (bf16[768,2048]{1,0:T(8,128)(2,1)}, bf16[768,2048]{1,0:T(8,128)(2,1)S(1)}, u32[]{:S(2)}) copy-start(bf16[768,2048]{1,0:T(8,128)(2,1)S(1)} %get-tuple-element.81.refs_6_.refs_5_.refs_4_.refs_2_) | copy-start | bytes 9437188
  26.1 40.8 %copy-start.4 = (bf16[64,2048]{1,0:T(8,128)(2,1)}, bf16[64,2048]{1,0:T(8,128)(2,1)S(1)}, u32[]{:S(2)}) copy-start(bf16[64,2048]{1,0:T(8,128)(2,1)S(1)} %get-tuple-element.83.refs_8_.refs_7_.refs_6_.refs_4_) | copy-start | bytes 786436
  26.2 13.1 %collective-permute-start.5 = (bf16[256,2048]{1,0:T(8,128)(2,1)S(1)}, bf16[256,2048]{1,0:T(8,128)(2,1)S(1)}, u32[]{:S(2)}, u32[]{:S(2)}) collective-permute-start(bf16[256,2048]{1,0:T(8,128)(2,1)S(1)} %shard_map.116.refs_3_), channel_id=1, source_target_pairs={{0,1},{1,0},{2,3},{3,2},{4,5},{5,4},{6,7},{7,6},{8,9},{9,8},{10,11... | collective-permute-start | bytes 3145736 | tf_op jit(solution)/shard_map/ppermute | solution.py:397
  26.2 22.1 %collective-permute-start.6 = (bf16[256,2048]{1,0:T(8,128)(2,1)S(1)}, bf16[256,2048]{1,0:T(8,128)(2,1)S(1)}, u32[]{:S(2)}, u32[]{:S(2)}) collective-permute-start(bf16[256,2048]{1,0:T(8,128)(2,1)S(1)} %shard_map.116.refs_3_), channel_id=1, source_target_pairs={{0,4},{1,3},{4,8},{5,1},{8,12},{9,5},{12,14},{13,9},{14,10},{15,13... | collective-permute-start | bytes 3145736 | tf_op jit(solution)/shard_map/ppermute | solution.py:394
  37.1 13.3 %collective-permute-start.7 = (bf16[256,2048]{1,0:T(8,128)(2,1)S(1)}, bf16[256,2048]{1,0:T(8,128)(2,1)S(1)}, u32[]{:S(2)}, u32[]{:S(2)}) collective-permute-start(bf16[256,2048]{1,0:T(8,128)(2,1)S(1)} %collective-permute-done.4.refs_1_), channel_id=1, source_target_pairs={{0,1},{1,0},{2,3},{3,2},{4,5},{5,4},{6,7},{7,6},{8,9},{9,8},{10,11... | collective-permute-start | bytes 3145736 | tf_op jit(solution)/shard_map/ppermute | solution.py:397
  37.2 22.6 %collective-permute-start.8 = (bf16[256,2048]{1,0:T(8,128)(2,1)S(1)}, bf16[256,2048]{1,0:T(8,128)(2,1)}, u32[]{:S(2)}, u32[]{:S(2)}) collective-permute-start(bf16[256,2048]{1,0:T(8,128)(2,1)S(1)} %collective-permute-done.4.refs_1_), channel_id=1, source_target_pairs={{0,4},{1,3},{4,8},{5,1},{8,12},{9,5},{12,14},{13,9},{14,10},{15,13... | collective-permute-start | bytes 3145736 | tf_op jit(solution)/shard_map/ppermute | solution.py:394
  44.5 9.3 %copy-start.10 = (bf16[256,384]{1,0:T(8,128)(2,1)}, bf16[256,384]{1,0:T(8,128)(2,1)S(1)}, u32[]{:S(2)}) copy-start(bf16[256,384]{1,0:T(8,128)(2,1)S(1)} %get-tuple-element.131.refs_1_) | copy-start | bytes 589828
  48.4 18.5 %collective-permute-start.9 = (bf16[256,2048]{1,0:T(8,128)(2,1)S(1)}, bf16[256,2048]{1,0:T(8,128)(2,1)S(1)}, u32[]{:S(2)}, u32[]{:S(2)}) collective-permute-start(bf16[256,2048]{1,0:T(8,128)(2,1)S(1)} %collective-permute-done.6.refs_1_), channel_id=1, source_target_pairs={{0,1},{1,0},{2,3},{3,2},{4,5},{5,4},{6,7},{7,6},{8,9},{9,8},{10,11... | collective-permute-start | bytes 3145736 | tf_op jit(solution)/shard_map/ppermute | solution.py:397
  48.4 25.0 %collective-permute-start.10 = (bf16[256,2048]{1,0:T(8,128)(2,1)S(1)}, bf16[256,2048]{1,0:T(8,128)(2,1)}, u32[]{:S(2)}, u32[]{:S(2)}) collective-permute-start(bf16[256,2048]{1,0:T(8,128)(2,1)S(1)} %collective-permute-done.6.refs_1_), channel_id=1, source_target_pairs={{0,4},{1,3},{4,8},{5,1},{8,12},{9,5},{12,14},{13,9},{14,10},{15,13... | collective-permute-start | bytes 3145736 | tf_op jit(solution)/shard_map/ppermute | solution.py:394
  53.8 13.0 %copy-start.14 = (bf16[256,256]{1,0:T(8,128)(2,1)}, bf16[256,256]{1,0:T(8,128)(2,1)S(1)}, u32[]{:S(2)}) copy-start(bf16[256,256]{1,0:T(8,128)(2,1)S(1)} %get-tuple-element.132.refs_2_) | copy-start | bytes 393220
  53.8 17.6 %copy-start.22 = (f32[64,256]{1,0:T(8,128)}, f32[64,256]{1,0:T(8,128)S(1)}, u32[]{:S(2)}) copy-start(f32[64,256]{1,0:T(8,128)S(1)} %get-tuple-element.140.refs_10_) | copy-start | bytes 196612
  59.7 23.1 %collective-permute-start.11 = (bf16[256,2048]{1,0:T(8,128)(2,1)}, bf16[256,2048]{1,0:T(8,128)(2,1)}, u32[]{:S(2)}, u32[]{:S(2)}) collective-permute-start(bf16[256,2048]{1,0:T(8,128)(2,1)} %collective-permute-done.8.refs_1_), channel_id=1, source_target_pairs={{0,1},{1,0},{2,3},{3,2},{4,5},{5,4},{6,7},{7,6},{8,9},{9,8},{10,11... | collective-permute-start | bytes 3145736 | tf_op jit(solution)/shard_map/ppermute | solution.py:397
  59.7 28.0 %collective-permute-start.12 = (bf16[256,2048]{1,0:T(8,128)(2,1)}, bf16[256,2048]{1,0:T(8,128)(2,1)}, u32[]{:S(2)}, u32[]{:S(2)}) collective-permute-start(bf16[256,2048]{1,0:T(8,128)(2,1)} %collective-permute-done.8.refs_1_), channel_id=1, source_target_pairs={{0,4},{1,3},{4,8},{5,1},{8,12},{9,5},{12,14},{13,9},{14,10},{15,13... | collective-permute-start | bytes 3145736 | tf_op jit(solution)/shard_map/ppermute | solution.py:394
  71.5 0.7 copy-start.16
  73.4 1.0 copy-start.6
  74.4 0.9 copy-start.8
  75.3 7.5 %copy-start.1 = (bf16[2048,768]{1,0:T(8,128)(2,1)S(1)}, bf16[2048,768]{1,0:T(8,128)(2,1)}, u32[]{:S(2)}) copy-start(bf16[2048,768]{1,0:T(8,128)(2,1)} %copy-done) | copy-start | bytes 9437188
  75.3 7.5 %copy-start.3 = (bf16[768,2048]{1,0:T(8,128)(2,1)S(1)}, bf16[768,2048]{1,0:T(8,128)(2,1)}, u32[]{:S(2)}) copy-start(bf16[768,2048]{1,0:T(8,128)(2,1)} %copy-done.2) | copy-start | bytes 9437188
  75.3 7.5 %copy-start.5 = (bf16[64,2048]{1,0:T(8,128)(2,1)S(1)}, bf16[64,2048]{1,0:T(8,128)(2,1)}, u32[]{:S(2)}) copy-start(bf16[64,2048]{1,0:T(8,128)(2,1)} %copy-done.4) | copy-start | bytes 786436
  75.3 7.5 %copy-start.27 = (f32[16,4,128]{2,1,0:T(4,128)S(1)}, f32[16,4,128]{2,1,0:T(4,128)}, u32[]{:S(2)}) copy-start(f32[16,4,128]{2,1,0:T(4,128)} %copy-done.26) | copy-start | bytes 98308
  79.3 20.0 %collective-permute-start.14 = (bf16[256,2048]{1,0:T(8,128)(2,1)}, bf16[256,2048]{1,0:T(8,128)(2,1)S(1)}, u32[]{:S(2)}, u32[]{:S(2)}) collective-permute-start(bf16[256,2048]{1,0:T(8,128)(2,1)} %collective-permute-done.10.block.refs_1_), channel_id=1, source_target_pairs={{0,1},{1,0},{2,3},{3,2},{4,5},{5,4},{6,7},{7,6},{8,9},{9,8},{10,11... | collective-permute-start | bytes 3145736 | tf_op jit(solution)/shard_map/ppermute | solution.py:397
  81.3 15.4 %collective-permute-start.13 = (bf16[128,2048]{1,0:T(8,128)(2,1)S(1)}, bf16[128,2048]{1,0:T(8,128)(2,1)S(1)}, u32[]{:S(2)}, u32[]{:S(2)}) collective-permute-start(bf16[128,2048]{1,0:T(8,128)(2,1)S(1)} %get-tuple-element.117), channel_id=1, source_target_pairs={{0,4},{1,3},{4,8},{5,1},{8,12},{9,5},{12,14},{13,9},{14,10},{15,13... | collective-permute-start | bytes 1572872 | tf_op jit(solution)/shard_map/ppermute | solution.py:394
  87.8 14.0 %collective-permute-start.15 = (bf16[128,2048]{1,0:T(8,128)(2,1)S(1)}, bf16[128,2048]{1,0:T(8,128)(2,1)S(1)}, u32[]{:S(2)}, u32[]{:S(2)}) collective-permute-start(bf16[128,2048]{1,0:T(8,128)(2,1)S(1)} %get-tuple-element.120), channel_id=1, source_target_pairs={{0,4},{1,3},{4,8},{5,1},{8,12},{9,5},{12,14},{13,9},{14,10},{15,13... | collective-permute-start | bytes 1572872 | tf_op jit(solution)/shard_map/ppermute | solution.py:394
  101.8 12.8 %copy-start.11 = (bf16[256,384]{1,0:T(8,128)(2,1)S(1)}, bf16[256,384]{1,0:T(8,128)(2,1)}, u32[]{:S(2)}) copy-start(bf16[256,384]{1,0:T(8,128)(2,1)} %copy-done.10) | copy-start | bytes 589828
  101.8 12.8 %copy-start.13 = (bf16[256,256]{1,0:T(8,128)(2,1)S(1)}, bf16[256,256]{1,0:T(8,128)(2,1)}, u32[]{:S(2)}) copy-start(bf16[256,256]{1,0:T(8,128)(2,1)} %copy-done.12) | copy-start | bytes 393220
  101.8 12.8 %copy-start.15 = (bf16[256,256]{1,0:T(8,128)(2,1)S(1)}, bf16[256,256]{1,0:T(8,128)(2,1)}, u32[]{:S(2)}) copy-start(bf16[256,256]{1,0:T(8,128)(2,1)} %copy-done.14) | copy-start | bytes 393220
  101.8 12.8 %copy-start.17 = (bf16[256,256]{1,0:T(8,128)(2,1)S(1)}, bf16[256,256]{1,0:T(8,128)(2,1)}, u32[]{:S(2)}) copy-start(bf16[256,256]{1,0:T(8,128)(2,1)} %copy-done.16) | copy-start | bytes 393220
  101.8 12.8 %copy-start.19 = (f32[64,384]{1,0:T(8,128)S(1)}, f32[64,384]{1,0:T(8,128)}, u32[]{:S(2)}) copy-start(f32[64,384]{1,0:T(8,128)} %copy-done.18) | copy-start | bytes 294916
  101.8 12.8 %copy-start.21 = (f32[64,256]{1,0:T(8,128)S(1)}, f32[64,256]{1,0:T(8,128)}, u32[]{:S(2)}) copy-start(f32[64,256]{1,0:T(8,128)} %copy-done.20) | copy-start | bytes 196612
  101.8 12.8 %copy-start.23 = (f32[64,256]{1,0:T(8,128)S(1)}, f32[64,256]{1,0:T(8,128)}, u32[]{:S(2)}) copy-start(f32[64,256]{1,0:T(8,128)} %copy-done.22) | copy-start | bytes 196612
  101.9 12.8 %copy-start.25 = (f32[64,256]{1,0:T(8,128)S(1)}, f32[64,256]{1,0:T(8,128)}, u32[]{:S(2)}) copy-start(f32[64,256]{1,0:T(8,128)} %copy-done.24) | copy-start | bytes 196612
  104.4 10.2 %collective-permute-start.16 = (f32[2,128,128]{2,1,0:T(8,128)S(1)}, f32[2,128,128]{2,1,0:T(8,128)S(1)}, u32[]{:S(2)}, u32[]{:S(2)}) collective-permute-start(f32[2,128,128]{2,1,0:T(8,128)S(1)} %get-tuple-element.129), channel_id=1, source_target_pairs={{0,1},{1,0},{2,3},{3,2},{4,5},{5,4},{6,7},{7,6},{8,9},{9,8},{10,11... | collective-permute-start | bytes 393224 | tf_op jit(solution)/shard_map/ppermute | solution.py:397
  (3 other events, 1.8 us)
Sparse Core Ops, SparseCore 0:
  9.5 20.9 all-gather.9
  32.1 18.0 all-gather.5
  51.7 18.0 all-gather.7

commit v15 on v13

--- a/solution.py
+++ b/solution.py
@@ -171,12 +171,13 @@
 
 
 def front_kernel(*refs):
-    blocks = len(refs) - 7
+    blocks = len(refs) - 8
     x_in = refs[:blocks]
-    w_gate, w_up, low_proj, hidden, low_side, x_all, low_sum = refs[blocks:]
-    rows = x_in[0].shape[0]
-    for i in range(blocks):
-        x_all[i * rows : (i + 1) * rows, :] = x_in[i][...]
+    w_gate, w_up, low_proj, hidden, low_first, low_last, x_all, low_sum = refs[blocks:]
+    begin = 0
+    for x in x_in:
+        x_all[begin : begin + x.shape[0], :] = x[...]
+        begin += x.shape[0]
     units = w_gate.shape[1]
     tile = 256 if units % 256 == 0 else units
     for cut in range(0, units, tile):
@@ -192,22 +193,25 @@
             preferred_element_type=jnp.float32,
         )
         low_sum[...] = low if cut == 0 else low_sum[...] + low
-    low_side[...] = low_sum[...].astype(low_side.dtype)
-
-
-def front(x_in, weights):
+    cut = low_first.shape[1]
+    low_first[...] = low_sum[:, :cut].astype(low_first.dtype)
+    low_last[...] = low_sum[:, cut:].astype(low_last.dtype)
+
+
+def front(x_in, weights, last):
     w_gate, w_up, _, low_proj, _ = weights
-    rows, width = len(x_in) * x_in[0].shape[0], x_in[0].shape[1]
+    rows, width = sum(x.shape[0] for x in x_in), x_in[0].shape[1]
     units = w_gate.shape[1]
     inside = pl.BlockSpec(memory_space=pltpu.VMEM)
     return pl.pallas_call(
         front_kernel,
         out_shape=[
             jax.ShapeDtypeStruct((rows, units), jnp.bfloat16),
-            jax.ShapeDtypeStruct((low_proj.shape[0], rows), jnp.bfloat16),
+            jax.ShapeDtypeStruct((low_proj.shape[0], rows - last), jnp.bfloat16),
+            jax.ShapeDtypeStruct((low_proj.shape[0], last), jnp.bfloat16),
         ],
         in_specs=[inside] * (len(x_in) + 3),
-        out_specs=[inside] * 2,
+        out_specs=[inside] * 3,
         scratch_shapes=[
             pltpu.VMEM((rows, width), jnp.bfloat16),
             pltpu.VMEM((low_proj.shape[0], rows), jnp.float32),
@@ -221,7 +225,7 @@
     )(*x_in, w_gate, w_up, low_proj)
 
 
-def back_kernel(names, *refs):
+def back_kernel(names, begin, *refs):
     blocks = len(names)
     sheet_in, dy_in = refs[0], refs[1 : 1 + blocks]
     hidden, w_down, high_proj, sheet, proj_cot, dy_all, grad_sum = refs[1 + blocks :]
@@ -236,7 +240,7 @@
         back = lax.dot_general(
             dy_all[...], w_down[part, :], across, preferred_element_type=jnp.float32
         )
-        terms = hidden[:, part].astype(jnp.float32) * back
+        terms = hidden[begin : begin + blocks * rows, part].astype(jnp.float32) * back
         total = terms[:, :lanes]
         for spot in range(lanes, tile, lanes):
             total += terms[:, spot : spot + lanes]
@@ -252,13 +256,13 @@
         sheet[block_owner(names[i], sheet.shape[0] // 2), 0:1, :] = total
 
 
-def finish_late(names, sheet, dy_in, hidden, weights):
+def finish_late(names, sheet, dy_in, hidden, begin, weights):
     _, _, w_down, _, high_proj = weights
     rows, width = len(dy_in) * dy_in[0].shape[0], dy_in[0].shape[1]
     units = hidden.shape[1]
     inside = pl.BlockSpec(memory_space=pltpu.VMEM)
     return pl.pallas_call(
-        functools.partial(back_kernel, names),
+        functools.partial(back_kernel, names, begin),
         out_shape=[
             jax.ShapeDtypeStruct(sheet.shape, jnp.float32),
             jax.ShapeDtypeStruct((high_proj.shape[0], rows), jnp.float32),
@@ -384,7 +388,7 @@
         if i == 1:
             job += (arrivals[0] + (False,),)
         if i == len(arrivals) - 1:
-            jobs += [job[1:], (job[0], (c, step, True))]
+            jobs += [(job[1], job[0]), ((c, step, True),)]
         elif i != 0:
             jobs.append(job)
 
@@ -427,19 +431,29 @@
         if i == 0:
             block = stack(*block)
         chain[c] = held[(c, step, False)] = block
-        held[(c, step, True)] = swap(block)
+        if i < len(arrivals) - 2:
+            held[(c, step, True)] = swap(block)
     cut = tok_rows // 2
-    *x, dy = split(chain["a"], ((0, cut), (cut, cut), (tok_rows, tok_rows)))
+    cuts = ((0, cut), (cut, cut), (tok_rows, tok_rows))
+    *x, dy = split(chain["a"], cuts)
     dy, _ = lax.optimization_barrier((dy, chain["b"]))
     x, dy = [hop(part) for part in x], hop(dy)
+    *x_before, dy_before = split(chain["b"], ((0, tok_rows), (tok_rows, tok_rows)))
+    x_before, dy_before = [swap(part) for part in x_before], swap(dy_before)
     take()
     sheet, x = lax.optimization_barrier((sheet, x))
-    hidden, low_side = front(x + [swap(part) for part in x], weights)
+    hidden, low_first, low_last = front(
+        x_before + x + [swap(part) for part in x], weights, tok_rows
+    )
     hidden, dy = lax.optimization_barrier((hidden, dy))
     dy_beside = swap(dy)
-    take()
-    sheet, proj_cot = finish_late(todo.pop(0), sheet, [dy, dy_beside], hidden, weights)
-    lows.append(low_side)
+    sheet, proj_cot = finish_late(todo.pop(0), sheet, [dy_before, dy], hidden, 0, weights)
+    lows.append(low_first)
+    projs.append(proj_cot)
+    sheet, proj_cot = finish_late(
+        todo.pop(0), sheet, [dy_beside], hidden, 2 * tok_rows, weights
+    )
+    lows.append(low_last)
     projs.append(proj_cot)
     returned = lax.all_to_all(sheet, "exp", split_axis=0, concat_axis=0, tiled=True)
     rank = proj_output.shape[2]

time: 103 us -> 102 us (level)
    pallas_call x7 -> x6, Pallas kernels: 26.9 us -> 24.5 us  [work(): return call(sheet, *apart, *block_in, *weights)]
    pallas_call x1 -> x2, Pallas kernels: 1.38 us -> 2.75 us  [finish_late(): pl.pallas_call(functools.partial(back_kernel, names, begin), out_shape=[j...]
    ppermute x10, waiting for transfers between devices: 28.1 us -> 26.9 us  [hop(): return lax.ppermute(block, 'exp', onward)]
  transfers between devices with their start and end apart: 21 -> 22, of which waited for: 9 -> 9; matrix products, arithmetic and copies ran while one was open for 0% -> 0% of each run, Pallas kernels for 29% -> 29%
where the time goes in v15:
time: 102 us
  Pallas kernels  31.9 us (31%)
  waiting for transfers between devices  28.7 us (28%)
  starting transfers between devices  21.6 us (21%)
  blocking collectives  12.9 us (13%)
  local copies, waits for them, and re-layouts  5.95 us (6%)
    ppermute x10, waiting for transfers between devices, hop(): return lax.ppermute(block, 'exp', onward)  26.9 us
    pallas_call x6, Pallas kernels, work(): return call(sheet, *apart, *block_in, *weights)  24.5 us
    ppermute x10, starting transfers between devices, hop(): return lax.ppermute(block, 'exp', onward)  20.2 us
    all_to_all x1, blocking collectives, by_ring(): lax.all_to_all(sheet, 'exp', split_axis=0, concat_axis=0, tiled=True)  12.9 us
    unnamed x16, local copies, waits for them, and re-layouts  5.95 us
    pallas_call x1, Pallas kernels, front(): pl.pallas_call(front_kernel, out_shape=[jax.ShapeDtypeStruct((rows, units...  3.2 us
    pallas_call x2, Pallas kernels, finish_late(): pl.pallas_call(functools.partial(back_kernel, names, begin), out_shape=[j...  2.75 us
  transfers between devices with their start and end apart: 22, of which 9 were waited for; matrix products, arithmetic and copies ran while one was open for 0% of the time, Pallas kernels for 29%

profile of v15, /device:TPU:0, one launch (start us, length us, event | category | flops | bytes accessed | tf_op | source)
XLA Modules:
  0.0 101.8 jit_solution(5806050126757263902)
XLA Ops:
  0.6 0.5 collective-permute-start
  1.1 0.1 collective-permute-start.1
  1.2 3.0 %collective-permute-start.2 = (bf16[128,2048]{1,0:T(8,128)(2,1)}, bf16[128,2048]{1,0:T(8,128)(2,1)S(1)}, u32[]{:S(2)}, u32[]{:S(2)}) collective-permute-start(bf16[128,2048]{1,0:T(8,128)(2,1)} %refs_1_.1), channel_id=1, source_target_pairs={{0,4},{1,3},{4,8},{5,1},{8,12},{9,5},{12,14},{13,9},{14,10},{15,13... | collective-permute-start | bytes 1572872 | tf_op jit(solution)/shard_map/ppermute | solution.py:377
  4.2 1.6 %collective-permute-start.3 = (bf16[128,2048]{1,0:T(8,128)(2,1)}, bf16[128,2048]{1,0:T(8,128)(2,1)S(1)}, u32[]{:S(2)}, u32[]{:S(2)}) collective-permute-start(bf16[128,2048]{1,0:T(8,128)(2,1)} %refs_2_.1), channel_id=1, source_target_pairs={{0,4},{1,3},{4,8},{5,1},{8,12},{9,5},{12,14},{13,9},{14,10},{15,13... | collective-permute-start | bytes 1572872 | tf_op jit(solution)/shard_map/ppermute | solution.py:377
  5.8 0.7 copy-done.4
  6.5 0.7 copy-done.6
  7.2 0.7 copy-done.7
  7.9 0.1 shard_map.114.refs_3_
  8.0 1.6 %collective-permute-start.4 = (bf16[256,2048]{1,0:T(8,128)(2,1)S(1)}, bf16[256,2048]{1,0:T(8,128)(2,1)S(1)}, u32[]{:S(2)}, u32[]{:S(2)}) collective-permute-start(bf16[256,2048]{1,0:T(8,128)(2,1)S(1)} %shard_map.114.refs_3_), channel_id=1, source_target_pairs={{0,4},{1,3},{4,8},{5,1},{8,12},{9,5},{12,14},{13,9},{14,10},{15,13... | collective-permute-start | bytes 3145736 | tf_op jit(solution)/shard_map/ppermute | solution.py:377
  9.6 1.0 %copy-done = bf16[128,2048]{1,0:T(8,128)(2,1)S(1)} copy-done((bf16[128,2048]{1,0:T(8,128)(2,1)S(1)}, bf16[128,2048]{1,0:T(8,128)(2,1)}, u32[]{:S(2)}) %copy-start) | copy-done | bytes 524312
  10.6 1.0 %copy-done.1 = bf16[128,2048]{1,0:T(8,128)(2,1)S(1)} copy-done((bf16[128,2048]{1,0:T(8,128)(2,1)S(1)}, bf16[128,2048]{1,0:T(8,128)(2,1)}, u32[]{:S(2)}) %copy-start.1) | copy-done | bytes 524312
  11.7 0.9 copy-done.2
  12.6 0.9 copy-done.3
  13.5 6.6 %shard_map.115 = (f32[16,4,128]{2,1,0:T(4,128)S(1)}, bf16[256,256]{1,0:T(8,128)(2,1)S(1)}, f32[64,256]{1,0:T(8,128)S(1)}, bf16[2048,768]{1,0:T(8,128)(2,1)S(1)},...) custom-call(f32[16,4,128]{2,1,0:T(4,128)S(1)} %shard_map.113.refs_0_, ...), custom_call_target="tpu_custom_call" | custom-call | flops 2415919104 | bytes 2097152 | tf_op jit(solution)/shard_map/pallas_call | solution.py:170
  20.1 0.1 shard_map.116.refs_3_
  20.2 0.1 collective-permute-start.5
  20.3 1.5 %collective-permute-start.6 = (bf16[256,2048]{1,0:T(8,128)(2,1)S(1)}, bf16[256,2048]{1,0:T(8,128)(2,1)S(1)}, u32[]{:S(2)}, u32[]{:S(2)}) collective-permute-start(bf16[256,2048]{1,0:T(8,128)(2,1)S(1)} %shard_map.116.refs_3_), channel_id=1, source_target_pairs={{0,4},{1,3},{4,8},{5,1},{8,12},{9,5},{12,14},{13,9},{14,10},{15,13... | collective-permute-start | bytes 3145736 | tf_op jit(solution)/shard_map/ppermute | solution.py:377
  21.8 6.6 %collective-permute-done.4.refs_1_ = bf16[256,2048]{1,0:T(8,128)(2,1)S(1)} collective-permute-done((bf16[256,2048]{1,0:T(8,128)(2,1)S(1)}, bf16[256,2048]{1,0:T(8,128)(2,1)S(1)}, u32[]{:S(2)}, u32[]{:S(2)}) %collective-permute-start.4) | collective-permute-done | bytes 1048608 | tf_op jit(solution)/shard_map/ppermute | solution.py:377
  28.4 2.1 %collective-permute-start.8 = (bf16[256,2048]{1,0:T(8,128)(2,1)S(1)}, bf16[256,2048]{1,0:T(8,128)(2,1)S(1)}, u32[]{:S(2)}, u32[]{:S(2)}) collective-permute-start(bf16[256,2048]{1,0:T(8,128)(2,1)S(1)} %collective-permute-done.4.refs_1_), channel_id=1, source_target_pairs={{0,4},{1,3},{4,8},{5,1},{8,12},{9,5},{12,14},{13,9},{14,10},{15,13... | collective-permute-start | bytes 3145736 | tf_op jit(solution)/shard_map/ppermute | solution.py:377
  30.5 4.6 %shard_map.117 = (f32[16,4,128]{2,1,0:T(4,128)S(1)}, bf16[256,384]{1,0:T(8,128)(2,1)S(1)}, f32[64,384]{1,0:T(8,128)S(1)}) custom-call(f32[16,4,128]{2,1,0:T(4,128)S(1)} %get-tuple-element.57.refs_0_, bf16[256,2048]{1,0:T(8,128)(2,1)S(1)} %collective-permute-done.4.refs_1_, bf16[256,2048]{1,0:T(8,128)(2,1)S(1)} %collective-permute-done.5.refs_2_, ...), custom_call_target="tpu_custom_call" | custom-call | flops 3623878656 | bytes 3145728 | tf_op jit(solution)/shard_map/pallas_call | solution.py:170
  35.1 4.5 %collective-permute-done.6.refs_1_ = bf16[256,2048]{1,0:T(8,128)(2,1)S(1)} collective-permute-done((bf16[256,2048]{1,0:T(8,128)(2,1)S(1)}, bf16[256,2048]{1,0:T(8,128)(2,1)S(1)}, u32[]{:S(2)}, u32[]{:S(2)}) %collective-permute-start.6) | collective-permute-done | bytes 1048608 | tf_op jit(solution)/shard_map/ppermute | solution.py:377
  39.6 2.1 %collective-permute-start.10 = (bf16[256,2048]{1,0:T(8,128)(2,1)S(1)}, bf16[256,2048]{1,0:T(8,128)(2,1)S(1)}, u32[]{:S(2)}, u32[]{:S(2)}) collective-permute-start(bf16[256,2048]{1,0:T(8,128)(2,1)S(1)} %collective-permute-done.6.refs_1_), channel_id=1, source_target_pairs={{0,4},{1,3},{4,8},{5,1},{8,12},{9,5},{12,14},{13,9},{14,10},{15,13... | collective-permute-start | bytes 3145736 | tf_op jit(solution)/shard_map/ppermute | solution.py:377
  41.7 3.3 %shard_map.118 = (f32[16,4,128]{2,1,0:T(4,128)S(1)}, bf16[256,256]{1,0:T(8,128)(2,1)S(1)}, f32[64,256]{1,0:T(8,128)S(1)}) custom-call(f32[16,4,128]{2,1,0:T(4,128)S(1)} %get-tuple-element.66.refs_0_, bf16[256,2048]{1,0:T(8,128)(2,1)S(1)} %collective-permute-done.6.refs_1_, bf16[256,2048]{1,0:T(8,128)(2,1)S(1)} %collective-permute-done.7.refs_2_, ...), custom_call_target="tpu_custom_call" | custom-call | flops 2415919104 | bytes 2097152 | tf_op jit(solution)/shard_map/pallas_call | solution.py:170
  45.0 5.8 %collective-permute-done.8.refs_1_ = bf16[256,2048]{1,0:T(8,128)(2,1)S(1)} collective-permute-done((bf16[256,2048]{1,0:T(8,128)(2,1)S(1)}, bf16[256,2048]{1,0:T(8,128)(2,1)S(1)}, u32[]{:S(2)}, u32[]{:S(2)}) %collective-permute-start.8) | collective-permute-done | bytes 1048608 | tf_op jit(solution)/shard_map/ppermute | solution.py:377
  50.8 2.1 %collective-permute-start.12 = (bf16[256,2048]{1,0:T(8,128)(2,1)S(1)}, bf16[256,2048]{1,0:T(8,128)(2,1)S(1)}, u32[]{:S(2)}, u32[]{:S(2)}) collective-permute-start(bf16[256,2048]{1,0:T(8,128)(2,1)S(1)} %collective-permute-done.8.refs_1_), channel_id=1, source_target_pairs={{0,4},{1,3},{4,8},{5,1},{8,12},{9,5},{12,14},{13,9},{14,10},{15,13... | collective-permute-start | bytes 3145736 | tf_op jit(solution)/shard_map/ppermute | solution.py:377
  53.0 3.3 %shard_map.119 = (f32[16,4,128]{2,1,0:T(4,128)S(1)}, bf16[256,256]{1,0:T(8,128)(2,1)S(1)}, f32[64,256]{1,0:T(8,128)S(1)}) custom-call(f32[16,4,128]{2,1,0:T(4,128)S(1)} %get-tuple-element.69.refs_0_, bf16[256,2048]{1,0:T(8,128)(2,1)S(1)} %collective-permute-done.8.refs_1_, bf16[256,2048]{1,0:T(8,128)(2,1)S(1)} %collective-permute-done.9.refs_2_, ...), custom_call_target="tpu_custom_call" | custom-call | flops 2415919104 | bytes 2097152 | tf_op jit(solution)/shard_map/pallas_call | solution.py:170
  56.3 5.8 %collective-permute-done.10.refs_1_.block = bf16[256,2048]{1,0:T(8,128)(2,1)S(1)} collective-permute-done((bf16[256,2048]{1,0:T(8,128)(2,1)S(1)}, bf16[256,2048]{1,0:T(8,128)(2,1)S(1)}, u32[]{:S(2)}, u32[]{:S(2)}) %collective-permute-start.10) | collective-permute-done | bytes 1048608 | tf_op jit(solution)/shard_map/ppermute | solution.py:377
  62.1 0.1 shard_map.122
  62.1 2.2 %collective-permute-start.14 = (bf16[64,2048]{1,0:T(8,128)(2,1)S(1)}, bf16[64,2048]{1,0:T(8,128)(2,1)S(1)}, u32[]{:S(2)}, u32[]{:S(2)}) collective-permute-start(bf16[64,2048]{1,0:T(8,128)(2,1)S(1)} %get-tuple-element.78), channel_id=1, source_target_pairs={{0,4},{1,3},{4,8},{5,1},{8,12},{9,5},{12,14},{13,9},{14,10},{15,13... | collective-permute-start | bytes 786440 | tf_op jit(solution)/shard_map/ppermute | solution.py:377
  64.3 1.6 %collective-permute-start.15 = (bf16[64,2048]{1,0:T(8,128)(2,1)S(1)}, bf16[64,2048]{1,0:T(8,128)(2,1)S(1)}, u32[]{:S(2)}, u32[]{:S(2)}) collective-permute-start(bf16[64,2048]{1,0:T(8,128)(2,1)S(1)} %get-tuple-element.79), channel_id=1, source_target_pairs={{0,4},{1,3},{4,8},{5,1},{8,12},{9,5},{12,14},{13,9},{14,10},{15,13... | collective-permute-start | bytes 786440 | tf_op jit(solution)/shard_map/ppermute | solution.py:377
  65.9 3.3 %shard_map.120 = (f32[16,4,128]{2,1,0:T(4,128)S(1)}, bf16[256,256]{1,0:T(8,128)(2,1)S(1)}, f32[64,256]{1,0:T(8,128)S(1)}) custom-call(f32[16,4,128]{2,1,0:T(4,128)S(1)} %get-tuple-element.72.refs_0_, bf16[256,2048]{1,0:T(8,128)(2,1)S(1)} %collective-permute-done.10.refs_1_.block, bf16[256,2048]{1,0:T(8,128)(2,1)S(1)} %collective-permute-done.11.refs_2_, ...), custom_call_target="tpu_custom_call" | custom-call | flops 2415919104 | bytes 2097152 | tf_op jit(solution)/shard_map/pallas_call | solution.py:170
  69.2 4.1 %collective-permute-done.12.refs_1_.block = bf16[256,2048]{1,0:T(8,128)(2,1)S(1)} collective-permute-done((bf16[256,2048]{1,0:T(8,128)(2,1)S(1)}, bf16[256,2048]{1,0:T(8,128)(2,1)S(1)}, u32[]{:S(2)}, u32[]{:S(2)}) %collective-permute-start.12) | collective-permute-done | bytes 1048608 | tf_op jit(solution)/shard_map/ppermute | solution.py:377
  73.3 0.1 shard_map.123
  73.4 0.1 collective-permute-start.17
  73.5 2.4 %collective-permute-start.20 = (bf16[128,2048]{1,0:T(8,128)(2,1)S(1)}, bf16[128,2048]{1,0:T(8,128)(2,1)S(1)}, u32[]{:S(2)}, u32[]{:S(2)}) collective-permute-start(bf16[128,2048]{1,0:T(8,128)(2,1)S(1)} %get-tuple-element.87), channel_id=1, source_target_pairs={{0,4},{1,3},{4,8},{5,1},{8,12},{9,5},{12,14},{13,9},{14,10},{15,13... | collective-permute-start | bytes 1572872 | tf_op jit(solution)/shard_map/ppermute | solution.py:377
  75.8 3.3 %shard_map.121 = (f32[16,4,128]{2,1,0:T(4,128)S(1)}, bf16[256,256]{1,0:T(8,128)(2,1)S(1)}, f32[64,256]{1,0:T(8,128)S(1)}) custom-call(f32[16,4,128]{2,1,0:T(4,128)S(1)} %get-tuple-element.75.refs_0_, bf16[256,2048]{1,0:T(8,128)(2,1)S(1)} %collective-permute-done.12.refs_1_.block, bf16[256,2048]{1,0:T(8,128)(2,1)S(1)} %collective-permute-done.13.refs_2_, ...), custom_call_target="tpu_custom_call" | custom-call | flops 2415919104 | bytes 2097152 | tf_op jit(solution)/shard_map/pallas_call | solution.py:170
  79.2 0.1 collective-permute-start.18
  79.3 0.5 collective-permute-start.19
  79.8 0.1 collective-permute-start.16
  79.9 0.9 collective-permute-done.18.refs_3_
  80.8 0.4 collective-permute-done.19.refs_4_
  81.2 3.2 %shard_map.124 = (bf16[384,768]{1,0:T(8,128)(2,1)S(1)}, bf16[256,256]{1,0:T(8,128)(2,1)S(1)}, bf16[256,128]{1,0:T(8,128)(2,1)S(1)}) custom-call(bf16[128,2048]{1,0:T(8,128)(2,1)S(1)} %collective-permute-done.17.refs_0_, bf16[64,2048]{1,0:T(8,128)(2,1)S(1)} %collective-permute-done.14.refs_1_, bf16[64,2048]{1,0:T(8,128)(2,1)S(1)} %collective-permute-done.15.refs_2_, ...), custom_call_target="tpu_custom_call" | custom-call | flops 2415919104 | bytes 1572864 | tf_op jit(solution)/shard_map/pallas_call | solution.py:206
  84.4 0.2 collective-permute-done.20.refs_2_
  84.6 1.4 %shard_map.125 = (f32[16,4,128]{2,1,0:T(4,128)S(1)}, f32[64,256]{1,0:T(8,128)S(1)}) custom-call(f32[16,4,128]{2,1,0:T(4,128)S(1)} %get-tuple-element.80.refs_0_, bf16[128,2048]{1,0:T(8,128)(2,1)S(1)} %collective-permute-done.16.refs_1_, bf16[128,2048]{1,0:T(8,128)(2,1)S(1)} %collective-permute-done.20.refs_2_, ...), custom_call_target="tpu_custom_call" | custom-call | flops 805306368 | bytes 1048576 | tf_op jit(solution)/shard_map/pallas_call | solution.py:264
  86.0 0.5 collective-permute-done.21.refs_1_
  86.5 1.4 %shard_map.126 = (f32[16,4,128]{2,1,0:T(4,128)S(1)}, f32[64,128]{1,0:T(8,128)S(1)}) custom-call(f32[16,4,128]{2,1,0:T(4,128)S(1)} %get-tuple-element.90.refs_0_, bf16[128,2048]{1,0:T(8,128)(2,1)S(1)} %collective-permute-done.21.refs_1_, bf16[384,768]{1,0:T(8,128)(2,1)S(1)} %get-tuple-element.89.refs_3_.refs_2_, ...), custom_call_target="tpu_custom_call" | custom-call | flops 402653184 | bytes 524288 | tf_op jit(solution)/shard_map/pallas_call | solution.py:264
  87.8 12.9 %all_to_all.5.returned = f32[16,4,128]{2,1,0:T(4,128)S(1)} all-to-all(f32[16,4,128]{2,1,0:T(4,128)S(1)} %get-tuple-element.91), channel_id=1, replica_groups=mesh['grp'=2,'exp'=16] {'exp'}, dimensions={0} | all-to-all | bytes 65536 | tf_op jit(solution)/shard_map/all_to_all | solution.py:458
  100.7 1.1 %shard_map.127 = (f32[256,64]{1,0:T(8,128)}, f32[8,128]{1,0:T(8,128)}) custom-call(f32[16,4,128]{2,1,0:T(4,128)S(1)} %all_to_all.5.returned, s32[8,128]{1,0:T(8,128)S(1)} %bitcast.19, bf16[256,256]{1,0:T(8,128)(2,1)S(1)} %get-tuple-element.92.refs_0_, bf16[256,384]{1,0:T(8,128)(2,1)S(1)} %get-tuple-element.93.refs_1_, ...), custom_call_target="tpu_custom_call" | custom-call | tf_op jit(solution)/shard_map/pallas_call | solution.py:460
  (28 shorter events, 0.1 us)
Async XLA Ops:
  0.6 7.2 %collective-permute-start = (bf16[128,2048]{1,0:T(8,128)(2,1)}, bf16[128,2048]{1,0:T(8,128)(2,1)S(1)}, u32[]{:S(2)}, u32[]{:S(2)}) collective-permute-start(bf16[128,2048]{1,0:T(8,128)(2,1)} %refs_1_.1), channel_id=1, source_target_pairs={{0,1},{1,0},{2,3},{3,2},{4,5},{5,4},{6,7},{7,6},{8,9},{9,8},{10,11... | collective-permute-start | bytes 1572872 | tf_op jit(solution)/shard_map/ppermute | solution.py:380
  1.1 6.7 %collective-permute-start.1 = (bf16[128,2048]{1,0:T(8,128)(2,1)}, bf16[128,2048]{1,0:T(8,128)(2,1)S(1)}, u32[]{:S(2)}, u32[]{:S(2)}) collective-permute-start(bf16[128,2048]{1,0:T(8,128)(2,1)} %refs_2_.1), channel_id=1, source_target_pairs={{0,1},{1,0},{2,3},{3,2},{4,5},{5,4},{6,7},{7,6},{8,9},{9,8},{10,11... | collective-permute-start | bytes 1572872 | tf_op jit(solution)/shard_map/ppermute | solution.py:380
  1.2 18.8 %collective-permute-start.2 = (bf16[128,2048]{1,0:T(8,128)(2,1)}, bf16[128,2048]{1,0:T(8,128)(2,1)S(1)}, u32[]{:S(2)}, u32[]{:S(2)}) collective-permute-start(bf16[128,2048]{1,0:T(8,128)(2,1)} %refs_1_.1), channel_id=1, source_target_pairs={{0,4},{1,3},{4,8},{5,1},{8,12},{9,5},{12,14},{13,9},{14,10},{15,13... | collective-permute-start | bytes 1572872 | tf_op jit(solution)/shard_map/ppermute | solution.py:377
  4.2 15.9 %collective-permute-start.3 = (bf16[128,2048]{1,0:T(8,128)(2,1)}, bf16[128,2048]{1,0:T(8,128)(2,1)S(1)}, u32[]{:S(2)}, u32[]{:S(2)}) collective-permute-start(bf16[128,2048]{1,0:T(8,128)(2,1)} %refs_2_.1), channel_id=1, source_target_pairs={{0,4},{1,3},{4,8},{5,1},{8,12},{9,5},{12,14},{13,9},{14,10},{15,13... | collective-permute-start | bytes 1572872 | tf_op jit(solution)/shard_map/ppermute | solution.py:377
  5.8 0.7 copy-start.4
  6.5 0.7 copy-start.6
  7.2 0.7 copy-start.7
  8.0 20.4 %collective-permute-start.4 = (bf16[256,2048]{1,0:T(8,128)(2,1)S(1)}, bf16[256,2048]{1,0:T(8,128)(2,1)S(1)}, u32[]{:S(2)}, u32[]{:S(2)}) collective-permute-start(bf16[256,2048]{1,0:T(8,128)(2,1)S(1)} %shard_map.114.refs_3_), channel_id=1, source_target_pairs={{0,4},{1,3},{4,8},{5,1},{8,12},{9,5},{12,14},{13,9},{14,10},{15,13... | collective-permute-start | bytes 3145736 | tf_op jit(solution)/shard_map/ppermute | solution.py:377
  9.6 1.0 %copy-start = (bf16[128,2048]{1,0:T(8,128)(2,1)S(1)}, bf16[128,2048]{1,0:T(8,128)(2,1)}, u32[]{:S(2)}) copy-start(bf16[128,2048]{1,0:T(8,128)(2,1)} %refs_1_.1) | copy-start | bytes 1572868
  10.6 1.0 %copy-start.1 = (bf16[128,2048]{1,0:T(8,128)(2,1)S(1)}, bf16[128,2048]{1,0:T(8,128)(2,1)}, u32[]{:S(2)}) copy-start(bf16[128,2048]{1,0:T(8,128)(2,1)} %refs_2_.1) | copy-start | bytes 1572868
  11.7 0.9 copy-start.2
  12.6 0.9 copy-start.3
  20.2 10.3 %collective-permute-start.5 = (bf16[256,2048]{1,0:T(8,128)(2,1)S(1)}, bf16[256,2048]{1,0:T(8,128)(2,1)S(1)}, u32[]{:S(2)}, u32[]{:S(2)}) collective-permute-start(bf16[256,2048]{1,0:T(8,128)(2,1)S(1)} %shard_map.116.refs_3_), channel_id=1, source_target_pairs={{0,1},{1,0},{2,3},{3,2},{4,5},{5,4},{6,7},{7,6},{8,9},{9,8},{10,11... | collective-permute-start | bytes 3145736 | tf_op jit(solution)/shard_map/ppermute | solution.py:380
  20.3 19.3 %collective-permute-start.6 = (bf16[256,2048]{1,0:T(8,128)(2,1)S(1)}, bf16[256,2048]{1,0:T(8,128)(2,1)S(1)}, u32[]{:S(2)}, u32[]{:S(2)}) collective-permute-start(bf16[256,2048]{1,0:T(8,128)(2,1)S(1)} %shard_map.116.refs_3_), channel_id=1, source_target_pairs={{0,4},{1,3},{4,8},{5,1},{8,12},{9,5},{12,14},{13,9},{14,10},{15,13... | collective-permute-start | bytes 3145736 | tf_op jit(solution)/shard_map/ppermute | solution.py:377
  28.4 13.4 %collective-permute-start.7 = (bf16[256,2048]{1,0:T(8,128)(2,1)S(1)}, bf16[256,2048]{1,0:T(8,128)(2,1)S(1)}, u32[]{:S(2)}, u32[]{:S(2)}) collective-permute-start(bf16[256,2048]{1,0:T(8,128)(2,1)S(1)} %collective-permute-done.4.refs_1_), channel_id=1, source_target_pairs={{0,1},{1,0},{2,3},{3,2},{4,5},{5,4},{6,7},{7,6},{8,9},{9,8},{10,11... | collective-permute-start | bytes 3145736 | tf_op jit(solution)/shard_map/ppermute | solution.py:380
  28.4 22.5 %collective-permute-start.8 = (bf16[256,2048]{1,0:T(8,128)(2,1)S(1)}, bf16[256,2048]{1,0:T(8,128)(2,1)S(1)}, u32[]{:S(2)}, u32[]{:S(2)}) collective-permute-start(bf16[256,2048]{1,0:T(8,128)(2,1)S(1)} %collective-permute-done.4.refs_1_), channel_id=1, source_target_pairs={{0,4},{1,3},{4,8},{5,1},{8,12},{9,5},{12,14},{13,9},{14,10},{15,13... | collective-permute-start | bytes 3145736 | tf_op jit(solution)/shard_map/ppermute | solution.py:377
  39.6 13.4 %collective-permute-start.9 = (bf16[256,2048]{1,0:T(8,128)(2,1)S(1)}, bf16[256,2048]{1,0:T(8,128)(2,1)S(1)}, u32[]{:S(2)}, u32[]{:S(2)}) collective-permute-start(bf16[256,2048]{1,0:T(8,128)(2,1)S(1)} %collective-permute-done.6.refs_1_), channel_id=1, source_target_pairs={{0,1},{1,0},{2,3},{3,2},{4,5},{5,4},{6,7},{7,6},{8,9},{9,8},{10,11... | collective-permute-start | bytes 3145736 | tf_op jit(solution)/shard_map/ppermute | solution.py:380
  39.6 22.5 %collective-permute-start.10 = (bf16[256,2048]{1,0:T(8,128)(2,1)S(1)}, bf16[256,2048]{1,0:T(8,128)(2,1)S(1)}, u32[]{:S(2)}, u32[]{:S(2)}) collective-permute-start(bf16[256,2048]{1,0:T(8,128)(2,1)S(1)} %collective-permute-done.6.refs_1_), channel_id=1, source_target_pairs={{0,4},{1,3},{4,8},{5,1},{8,12},{9,5},{12,14},{13,9},{14,10},{15,13... | collective-permute-start | bytes 3145736 | tf_op jit(solution)/shard_map/ppermute | solution.py:377
  50.8 15.1 %collective-permute-start.11 = (bf16[256,2048]{1,0:T(8,128)(2,1)S(1)}, bf16[256,2048]{1,0:T(8,128)(2,1)S(1)}, u32[]{:S(2)}, u32[]{:S(2)}) collective-permute-start(bf16[256,2048]{1,0:T(8,128)(2,1)S(1)} %collective-permute-done.8.refs_1_), channel_id=1, source_target_pairs={{0,1},{1,0},{2,3},{3,2},{4,5},{5,4},{6,7},{7,6},{8,9},{9,8},{10,11... | collective-permute-start | bytes 3145736 | tf_op jit(solution)/shard_map/ppermute | solution.py:380
  50.8 22.5 %collective-permute-start.12 = (bf16[256,2048]{1,0:T(8,128)(2,1)S(1)}, bf16[256,2048]{1,0:T(8,128)(2,1)S(1)}, u32[]{:S(2)}, u32[]{:S(2)}) collective-permute-start(bf16[256,2048]{1,0:T(8,128)(2,1)S(1)} %collective-permute-done.8.refs_1_), channel_id=1, source_target_pairs={{0,4},{1,3},{4,8},{5,1},{8,12},{9,5},{12,14},{13,9},{14,10},{15,13... | collective-permute-start | bytes 3145736 | tf_op jit(solution)/shard_map/ppermute | solution.py:377
  62.1 13.8 %collective-permute-start.13 = (bf16[256,2048]{1,0:T(8,128)(2,1)S(1)}, bf16[256,2048]{1,0:T(8,128)(2,1)S(1)}, u32[]{:S(2)}, u32[]{:S(2)}) collective-permute-start(bf16[256,2048]{1,0:T(8,128)(2,1)S(1)} %collective-permute-done.10.refs_1_.block), channel_id=1, source_target_pairs={{0,1},{1,0},{2,3},{3,2},{4,5},{5,4},{6,7},{7,6},{8,9},{9,8},{10,11... | collective-permute-start | bytes 3145736 | tf_op jit(solution)/shard_map/ppermute | solution.py:380
  62.1 17.0 %collective-permute-start.14 = (bf16[64,2048]{1,0:T(8,128)(2,1)S(1)}, bf16[64,2048]{1,0:T(8,128)(2,1)S(1)}, u32[]{:S(2)}, u32[]{:S(2)}) collective-permute-start(bf16[64,2048]{1,0:T(8,128)(2,1)S(1)} %get-tuple-element.78), channel_id=1, source_target_pairs={{0,4},{1,3},{4,8},{5,1},{8,12},{9,5},{12,14},{13,9},{14,10},{15,13... | collective-permute-start | bytes 786440 | tf_op jit(solution)/shard_map/ppermute | solution.py:377
  64.3 14.9 %collective-permute-start.15 = (bf16[64,2048]{1,0:T(8,128)(2,1)S(1)}, bf16[64,2048]{1,0:T(8,128)(2,1)S(1)}, u32[]{:S(2)}, u32[]{:S(2)}) collective-permute-start(bf16[64,2048]{1,0:T(8,128)(2,1)S(1)} %get-tuple-element.79), channel_id=1, source_target_pairs={{0,4},{1,3},{4,8},{5,1},{8,12},{9,5},{12,14},{13,9},{14,10},{15,13... | collective-permute-start | bytes 786440 | tf_op jit(solution)/shard_map/ppermute | solution.py:377
  73.4 7.8 %collective-permute-start.17 = (bf16[128,2048]{1,0:T(8,128)(2,1)S(1)}, bf16[128,2048]{1,0:T(8,128)(2,1)S(1)}, u32[]{:S(2)}, u32[]{:S(2)}) collective-permute-start(bf16[128,2048]{1,0:T(8,128)(2,1)S(1)} %get-tuple-element.82), channel_id=1, source_target_pairs={{0,1},{1,0},{2,3},{3,2},{4,5},{5,4},{6,7},{7,6},{8,9},{9,8},{10,11... | collective-permute-start | bytes 1572872 | tf_op jit(solution)/shard_map/ppermute | solution.py:380
  73.5 11.1 %collective-permute-start.20 = (bf16[128,2048]{1,0:T(8,128)(2,1)S(1)}, bf16[128,2048]{1,0:T(8,128)(2,1)S(1)}, u32[]{:S(2)}, u32[]{:S(2)}) collective-permute-start(bf16[128,2048]{1,0:T(8,128)(2,1)S(1)} %get-tuple-element.87), channel_id=1, source_target_pairs={{0,4},{1,3},{4,8},{5,1},{8,12},{9,5},{12,14},{13,9},{14,10},{15,13... | collective-permute-start | bytes 1572872 | tf_op jit(solution)/shard_map/ppermute | solution.py:377
  79.2 1.6 %collective-permute-start.18 = (bf16[64,2048]{1,0:T(8,128)(2,1)S(1)}, bf16[64,2048]{1,0:T(8,128)(2,1)S(1)}, u32[]{:S(2)}, u32[]{:S(2)}) collective-permute-start(bf16[64,2048]{1,0:T(8,128)(2,1)S(1)} %collective-permute-done.14.refs_1_), channel_id=1, source_target_pairs={{0,1},{1,0},{2,3},{3,2},{4,5},{5,4},{6,7},{7,6},{8,9},{9,8},{10,11... | collective-permute-start | bytes 786440 | tf_op jit(solution)/shard_map/ppermute | solution.py:380
  79.3 1.9 %collective-permute-start.19 = (bf16[64,2048]{1,0:T(8,128)(2,1)S(1)}, bf16[64,2048]{1,0:T(8,128)(2,1)S(1)}, u32[]{:S(2)}, u32[]{:S(2)}) collective-permute-start(bf16[64,2048]{1,0:T(8,128)(2,1)S(1)} %collective-permute-done.15.refs_2_), channel_id=1, source_target_pairs={{0,1},{1,0},{2,3},{3,2},{4,5},{5,4},{6,7},{7,6},{8,9},{9,8},{10,11... | collective-permute-start | bytes 786440 | tf_op jit(solution)/shard_map/ppermute | solution.py:380
  79.8 4.8 %collective-permute-start.16 = (bf16[128,2048]{1,0:T(8,128)(2,1)S(1)}, bf16[128,2048]{1,0:T(8,128)(2,1)S(1)}, u32[]{:S(2)}, u32[]{:S(2)}) collective-permute-start(bf16[128,2048]{1,0:T(8,128)(2,1)S(1)} %get-tuple-element.81), channel_id=1, source_target_pairs={{0,1},{1,0},{2,3},{3,2},{4,5},{5,4},{6,7},{7,6},{8,9},{9,8},{10,11... | collective-permute-start | bytes 1572872 | tf_op jit(solution)/shard_map/ppermute | solution.py:380
  84.5 1.9 %collective-permute-start.21 = (bf16[128,2048]{1,0:T(8,128)(2,1)S(1)}, bf16[128,2048]{1,0:T(8,128)(2,1)S(1)}, u32[]{:S(2)}, u32[]{:S(2)}) collective-permute-start(bf16[128,2048]{1,0:T(8,128)(2,1)S(1)} %collective-permute-done.20.refs_2_), channel_id=1, source_target_pairs={{0,1},{1,0},{2,3},{3,2},{4,5},{5,4},{6,7},{7,6},{8,9},{9,8},{10,11... | collective-permute-start | bytes 1572872 | tf_op jit(solution)/shard_map/ppermute | solution.py:380
  86.0 14.7 %copy-start.5 = (s32[128,8]{0,1:T(8,128)S(1)}, s32[128,8]{0,1:T(8,128)}, u32[]{:S(2)}) copy-start(s32[128,8]{0,1:T(8,128)} %param.12) | copy-start | bytes 12292

commit v16 on v15

--- a/solution.py
+++ b/solution.py
@@ -225,61 +225,67 @@
     )(*x_in, w_gate, w_up, low_proj)
 
 
-def back_kernel(names, begin, *refs):
+def fold(product):
+    total = product[:, :128]
+    for spot in range(128, product.shape[1], 128):
+        total += product[:, spot : spot + 128]
+    return total
+
+
+def enter(sheet, name, total):
+    sheet[block_owner(name, sheet.shape[0] // 2), 0:1, :] = jnp.sum(
+        jnp.transpose(total), axis=0, keepdims=True
+    )
+
+
+def out_kernel(names, *refs):
     blocks = len(names)
     sheet_in, dy_in = refs[0], refs[1 : 1 + blocks]
-    hidden, w_down, high_proj, sheet, proj_cot, dy_all, grad_sum = refs[1 + blocks :]
+    hidden, w_down, high_proj, sheet, proj_cot, rest = refs[1 + blocks :]
     rows = dy_in[0].shape[0]
     across = (((1,), (1,)), ((), ()))
-    for i in range(blocks):
-        dy_all[i * rows : (i + 1) * rows, :] = dy_in[i][...]
-    units, lanes = hidden.shape[1], grad_sum.shape[1]
-    tile = 256 if units % 256 == 0 else units
-    for cut in range(0, units, tile):
+    width = w_down.shape[1]
+    tile = 512 if width % 512 == 0 else width
+    totals = [0.0] * blocks
+    for cut in range(0, width, tile):
         part = pl.ds(cut, tile)
-        back = lax.dot_general(
-            dy_all[...], w_down[part, :], across, preferred_element_type=jnp.float32
-        )
-        terms = hidden[begin : begin + blocks * rows, part].astype(jnp.float32) * back
-        total = terms[:, :lanes]
-        for spot in range(lanes, tile, lanes):
-            total += terms[:, spot : spot + lanes]
-        grad_sum[...] = total if cut == 0 else grad_sum[...] + total
-    proj_cot[...] = lax.dot_general(
-        high_proj[...], dy_all[...], across, preferred_element_type=jnp.float32
-    )
+        out_val = jnp.dot(hidden[...], w_down[:, part], preferred_element_type=jnp.float32)
+        for i in range(blocks):
+            dy = dy_in[i][:, part].astype(jnp.float32)
+            totals[i] += fold(dy * out_val[i * rows : (i + 1) * rows, :])
+        rest[:, part] = out_val[blocks * rows :, :]
     sheet[...] = sheet_in[...]
     for i in range(blocks):
-        total = jnp.sum(
-            jnp.transpose(grad_sum[i * rows : (i + 1) * rows, :]), axis=0, keepdims=True
+        enter(sheet, names[i], totals[i])
+        proj_cot[:, i * rows : (i + 1) * rows] = lax.dot_general(
+            high_proj[...], dy_in[i][...], across, preferred_element_type=jnp.float32
         )
-        sheet[block_owner(names[i], sheet.shape[0] // 2), 0:1, :] = total
-
-
-def finish_late(names, sheet, dy_in, hidden, begin, weights):
-    _, _, w_down, _, high_proj = weights
-    rows, width = len(dy_in) * dy_in[0].shape[0], dy_in[0].shape[1]
-    units = hidden.shape[1]
+
+
+def last_kernel(name, sheet_in, dy, out_val, high_proj, sheet, proj_cot):
+    width = dy.shape[1]
+    tile = 512 if width % 512 == 0 else width
+    total = 0.0
+    for cut in range(0, width, tile):
+        part = pl.ds(cut, tile)
+        total += fold(dy[:, part].astype(jnp.float32) * out_val[:, part])
+    sheet[...] = sheet_in[...]
+    enter(sheet, name, total)
+    proj_cot[...] = lax.dot_general(
+        high_proj[...], dy[...], (((1,), (1,)), ((), ())), preferred_element_type=jnp.float32
+    )
+
+
+def on_core(kernel, args, out_shape, flops=0):
     inside = pl.BlockSpec(memory_space=pltpu.VMEM)
     return pl.pallas_call(
-        functools.partial(back_kernel, names, begin),
-        out_shape=[
-            jax.ShapeDtypeStruct(sheet.shape, jnp.float32),
-            jax.ShapeDtypeStruct((high_proj.shape[0], rows), jnp.float32),
-        ],
-        in_specs=[inside] * (len(dy_in) + 4),
-        out_specs=[inside] * 2,
-        scratch_shapes=[
-            pltpu.VMEM((rows, width), jnp.bfloat16),
-            pltpu.VMEM((rows, 128), jnp.float32),
-        ],
+        kernel,
+        out_shape=[jax.ShapeDtypeStruct(shape, jnp.float32) for shape in out_shape],
+        in_specs=[inside] * len(args),
+        out_specs=[inside] * len(out_shape),
         compiler_params=pltpu.CompilerParams(vmem_limit_bytes=16 * 1024 * 1024),
-        cost_estimate=pl.CostEstimate(
-            flops=2 * rows * width * units,
-            bytes_accessed=2 * rows * width,
-            transcendentals=0,
-        ),
-    )(sheet, *dy_in, hidden, w_down, high_proj)
+        cost_estimate=pl.CostEstimate(flops=flops, bytes_accessed=2**20, transcendentals=0),
+    )(*args)
 
 
 def outcome_kernel(jobs, returned, routes, *refs):
@@ -447,16 +453,24 @@
     )
     hidden, dy = lax.optimization_barrier((hidden, dy))
     dy_beside = swap(dy)
-    sheet, proj_cot = finish_late(todo.pop(0), sheet, [dy_before, dy], hidden, 0, weights)
+    rank = proj_output.shape[2]
+    sheet, proj_cot, out_val = on_core(
+        functools.partial(out_kernel, todo.pop(0)),
+        (sheet, dy_before, dy, hidden, weights[2], weights[4]),
+        [sheet.shape, (rank, 2 * tok_rows), tokens.shape],
+        flops=6 * tok_rows * hidden.shape[1] * tokens.shape[1],
+    )
     lows.append(low_first)
     projs.append(proj_cot)
-    sheet, proj_cot = finish_late(
-        todo.pop(0), sheet, [dy_beside], hidden, 2 * tok_rows, weights
+    ((name,),) = todo
+    sheet, proj_cot = on_core(
+        functools.partial(last_kernel, name),
+        (sheet, dy_beside, out_val, weights[4]),
+        [sheet.shape, (rank, tok_rows)],
     )
     lows.append(low_last)
     projs.append(proj_cot)
     returned = lax.all_to_all(sheet, "exp", split_axis=0, concat_axis=0, tiled=True)
-    rank = proj_output.shape[2]
     feature, route_grad = pl.pallas_call(
         functools.partial(outcome_kernel, jobs),
         out_shape=[

time: 102 us -> 101 us (level)
  no operation moved by 1% of the time
where the time goes in v16:
time: 101 us
  Pallas kernels  31.1 us (31%)
  waiting for transfers between devices  28.4 us (28%)
  starting transfers between devices  21.6 us (21%)
  blocking collectives  12.9 us (13%)
  local copies, waits for them, and re-layouts  5.95 us (6%)
    ppermute x10, waiting for transfers between devices, hop(): return lax.ppermute(block, 'exp', onward)  26.9 us
    pallas_call x6, Pallas kernels, work(): return call(sheet, *apart, *block_in, *weights)  24.5 us
    ppermute x10, starting transfers between devices, hop(): return lax.ppermute(block, 'exp', onward)  20.2 us
    all_to_all x1, blocking collectives, by_ring(): lax.all_to_all(sheet, 'exp', split_axis=0, concat_axis=0, tiled=True)  12.9 us
    unnamed x16, local copies, waits for them, and re-layouts  5.95 us
    pallas_call x1, Pallas kernels, front(): pl.pallas_call(front_kernel, out_shape=[jax.ShapeDtypeStruct((rows, units...  3.19 us
  transfers between devices with their start and end apart: 22, of which 9 were waited for; matrix products, arithmetic and copies ran while one was open for 0% of the time, Pallas kernels for 29%

profile of v16, /device:TPU:0, one launch (start us, length us, event | category | flops | bytes accessed | tf_op | source)
XLA Modules:
  0.0 100.8 jit_solution(10545521383094845794)
XLA Ops:
  0.6 0.5 collective-permute-start
  1.1 0.1 collective-permute-start.1
  1.2 3.0 %collective-permute-start.2 = (bf16[128,2048]{1,0:T(8,128)(2,1)}, bf16[128,2048]{1,0:T(8,128)(2,1)S(1)}, u32[]{:S(2)}, u32[]{:S(2)}) collective-permute-start(bf16[128,2048]{1,0:T(8,128)(2,1)} %refs_1_.1), channel_id=1, source_target_pairs={{0,4},{1,3},{4,8},{5,1},{8,12},{9,5},{12,14},{13,9},{14,10},{15,13... | collective-permute-start | bytes 1572872 | tf_op jit(solution)/shard_map/ppermute | solution.py:383
  4.2 1.6 %collective-permute-start.3 = (bf16[128,2048]{1,0:T(8,128)(2,1)}, bf16[128,2048]{1,0:T(8,128)(2,1)S(1)}, u32[]{:S(2)}, u32[]{:S(2)}) collective-permute-start(bf16[128,2048]{1,0:T(8,128)(2,1)} %refs_2_.1), channel_id=1, source_target_pairs={{0,4},{1,3},{4,8},{5,1},{8,12},{9,5},{12,14},{13,9},{14,10},{15,13... | collective-permute-start | bytes 1572872 | tf_op jit(solution)/shard_map/ppermute | solution.py:383
  5.8 0.7 copy-done.4
  6.5 0.7 copy-done.6
  7.2 0.7 copy-done.7
  7.9 0.1 shard_map.114.refs_3_
  8.0 1.6 %collective-permute-start.4 = (bf16[256,2048]{1,0:T(8,128)(2,1)S(1)}, bf16[256,2048]{1,0:T(8,128)(2,1)S(1)}, u32[]{:S(2)}, u32[]{:S(2)}) collective-permute-start(bf16[256,2048]{1,0:T(8,128)(2,1)S(1)} %shard_map.114.refs_3_), channel_id=1, source_target_pairs={{0,4},{1,3},{4,8},{5,1},{8,12},{9,5},{12,14},{13,9},{14,10},{15,13... | collective-permute-start | bytes 3145736 | tf_op jit(solution)/shard_map/ppermute | solution.py:383
  9.6 1.0 %copy-done = bf16[128,2048]{1,0:T(8,128)(2,1)S(1)} copy-done((bf16[128,2048]{1,0:T(8,128)(2,1)S(1)}, bf16[128,2048]{1,0:T(8,128)(2,1)}, u32[]{:S(2)}) %copy-start) | copy-done | bytes 524312
  10.6 1.0 %copy-done.1 = bf16[128,2048]{1,0:T(8,128)(2,1)S(1)} copy-done((bf16[128,2048]{1,0:T(8,128)(2,1)S(1)}, bf16[128,2048]{1,0:T(8,128)(2,1)}, u32[]{:S(2)}) %copy-start.1) | copy-done | bytes 524312
  11.7 0.9 copy-done.2
  12.6 0.9 copy-done.3
  13.5 6.6 %shard_map.115 = (f32[16,4,128]{2,1,0:T(4,128)S(1)}, bf16[256,256]{1,0:T(8,128)(2,1)S(1)}, f32[64,256]{1,0:T(8,128)S(1)}, bf16[2048,768]{1,0:T(8,128)(2,1)S(1)},...) custom-call(f32[16,4,128]{2,1,0:T(4,128)S(1)} %shard_map.113.refs_0_, ...), custom_call_target="tpu_custom_call" | custom-call | flops 2415919104 | bytes 2097152 | tf_op jit(solution)/shard_map/pallas_call | solution.py:170
  20.1 0.1 shard_map.116.refs_3_
  20.2 0.1 collective-permute-start.5
  20.3 1.5 %collective-permute-start.6 = (bf16[256,2048]{1,0:T(8,128)(2,1)S(1)}, bf16[256,2048]{1,0:T(8,128)(2,1)S(1)}, u32[]{:S(2)}, u32[]{:S(2)}) collective-permute-start(bf16[256,2048]{1,0:T(8,128)(2,1)S(1)} %shard_map.116.refs_3_), channel_id=1, source_target_pairs={{0,4},{1,3},{4,8},{5,1},{8,12},{9,5},{12,14},{13,9},{14,10},{15,13... | collective-permute-start | bytes 3145736 | tf_op jit(solution)/shard_map/ppermute | solution.py:383
  21.8 6.6 %collective-permute-done.4.refs_1_ = bf16[256,2048]{1,0:T(8,128)(2,1)S(1)} collective-permute-done((bf16[256,2048]{1,0:T(8,128)(2,1)S(1)}, bf16[256,2048]{1,0:T(8,128)(2,1)S(1)}, u32[]{:S(2)}, u32[]{:S(2)}) %collective-permute-start.4) | collective-permute-done | bytes 1048608 | tf_op jit(solution)/shard_map/ppermute | solution.py:383
  28.4 2.1 %collective-permute-start.8 = (bf16[256,2048]{1,0:T(8,128)(2,1)S(1)}, bf16[256,2048]{1,0:T(8,128)(2,1)S(1)}, u32[]{:S(2)}, u32[]{:S(2)}) collective-permute-start(bf16[256,2048]{1,0:T(8,128)(2,1)S(1)} %collective-permute-done.4.refs_1_), channel_id=1, source_target_pairs={{0,4},{1,3},{4,8},{5,1},{8,12},{9,5},{12,14},{13,9},{14,10},{15,13... | collective-permute-start | bytes 3145736 | tf_op jit(solution)/shard_map/ppermute | solution.py:383
  30.5 4.6 %shard_map.117 = (f32[16,4,128]{2,1,0:T(4,128)S(1)}, bf16[256,384]{1,0:T(8,128)(2,1)S(1)}, f32[64,384]{1,0:T(8,128)S(1)}) custom-call(f32[16,4,128]{2,1,0:T(4,128)S(1)} %get-tuple-element.58.refs_0_, bf16[256,2048]{1,0:T(8,128)(2,1)S(1)} %collective-permute-done.4.refs_1_, bf16[256,2048]{1,0:T(8,128)(2,1)S(1)} %collective-permute-done.5.refs_2_, ...), custom_call_target="tpu_custom_call" | custom-call | flops 3623878656 | bytes 3145728 | tf_op jit(solution)/shard_map/pallas_call | solution.py:170
  35.1 4.5 %collective-permute-done.6.refs_1_ = bf16[256,2048]{1,0:T(8,128)(2,1)S(1)} collective-permute-done((bf16[256,2048]{1,0:T(8,128)(2,1)S(1)}, bf16[256,2048]{1,0:T(8,128)(2,1)S(1)}, u32[]{:S(2)}, u32[]{:S(2)}) %collective-permute-start.6) | collective-permute-done | bytes 1048608 | tf_op jit(solution)/shard_map/ppermute | solution.py:383
  39.6 2.1 %collective-permute-start.10 = (bf16[256,2048]{1,0:T(8,128)(2,1)S(1)}, bf16[256,2048]{1,0:T(8,128)(2,1)S(1)}, u32[]{:S(2)}, u32[]{:S(2)}) collective-permute-start(bf16[256,2048]{1,0:T(8,128)(2,1)S(1)} %collective-permute-done.6.refs_1_), channel_id=1, source_target_pairs={{0,4},{1,3},{4,8},{5,1},{8,12},{9,5},{12,14},{13,9},{14,10},{15,13... | collective-permute-start | bytes 3145736 | tf_op jit(solution)/shard_map/ppermute | solution.py:383
  41.7 3.3 %shard_map.118 = (f32[16,4,128]{2,1,0:T(4,128)S(1)}, bf16[256,256]{1,0:T(8,128)(2,1)S(1)}, f32[64,256]{1,0:T(8,128)S(1)}) custom-call(f32[16,4,128]{2,1,0:T(4,128)S(1)} %get-tuple-element.67.refs_0_, bf16[256,2048]{1,0:T(8,128)(2,1)S(1)} %collective-permute-done.6.refs_1_, bf16[256,2048]{1,0:T(8,128)(2,1)S(1)} %collective-permute-done.7.refs_2_, ...), custom_call_target="tpu_custom_call" | custom-call | flops 2415919104 | bytes 2097152 | tf_op jit(solution)/shard_map/pallas_call | solution.py:170
  45.0 5.8 %collective-permute-done.8.refs_1_ = bf16[256,2048]{1,0:T(8,128)(2,1)S(1)} collective-permute-done((bf16[256,2048]{1,0:T(8,128)(2,1)S(1)}, bf16[256,2048]{1,0:T(8,128)(2,1)S(1)}, u32[]{:S(2)}, u32[]{:S(2)}) %collective-permute-start.8) | collective-permute-done | bytes 1048608 | tf_op jit(solution)/shard_map/ppermute | solution.py:383
  50.8 2.1 %collective-permute-start.12 = (bf16[256,2048]{1,0:T(8,128)(2,1)S(1)}, bf16[256,2048]{1,0:T(8,128)(2,1)S(1)}, u32[]{:S(2)}, u32[]{:S(2)}) collective-permute-start(bf16[256,2048]{1,0:T(8,128)(2,1)S(1)} %collective-permute-done.8.refs_1_), channel_id=1, source_target_pairs={{0,4},{1,3},{4,8},{5,1},{8,12},{9,5},{12,14},{13,9},{14,10},{15,13... | collective-permute-start | bytes 3145736 | tf_op jit(solution)/shard_map/ppermute | solution.py:383
  53.0 3.3 %shard_map.119 = (f32[16,4,128]{2,1,0:T(4,128)S(1)}, bf16[256,256]{1,0:T(8,128)(2,1)S(1)}, f32[64,256]{1,0:T(8,128)S(1)}) custom-call(f32[16,4,128]{2,1,0:T(4,128)S(1)} %get-tuple-element.70.refs_0_, bf16[256,2048]{1,0:T(8,128)(2,1)S(1)} %collective-permute-done.8.refs_1_, bf16[256,2048]{1,0:T(8,128)(2,1)S(1)} %collective-permute-done.9.refs_2_, ...), custom_call_target="tpu_custom_call" | custom-call | flops 2415919104 | bytes 2097152 | tf_op jit(solution)/shard_map/pallas_call | solution.py:170
  56.3 5.8 %collective-permute-done.10.refs_1_.block = bf16[256,2048]{1,0:T(8,128)(2,1)S(1)} collective-permute-done((bf16[256,2048]{1,0:T(8,128)(2,1)S(1)}, bf16[256,2048]{1,0:T(8,128)(2,1)S(1)}, u32[]{:S(2)}, u32[]{:S(2)}) %collective-permute-start.10) | collective-permute-done | bytes 1048608 | tf_op jit(solution)/shard_map/ppermute | solution.py:383
  62.1 0.1 shard_map.122
  62.1 2.2 %collective-permute-start.14 = (bf16[64,2048]{1,0:T(8,128)(2,1)S(1)}, bf16[64,2048]{1,0:T(8,128)(2,1)S(1)}, u32[]{:S(2)}, u32[]{:S(2)}) collective-permute-start(bf16[64,2048]{1,0:T(8,128)(2,1)S(1)} %get-tuple-element.79), channel_id=1, source_target_pairs={{0,4},{1,3},{4,8},{5,1},{8,12},{9,5},{12,14},{13,9},{14,10},{15,13... | collective-permute-start | bytes 786440 | tf_op jit(solution)/shard_map/ppermute | solution.py:383
  64.3 1.6 %collective-permute-start.15 = (bf16[64,2048]{1,0:T(8,128)(2,1)S(1)}, bf16[64,2048]{1,0:T(8,128)(2,1)S(1)}, u32[]{:S(2)}, u32[]{:S(2)}) collective-permute-start(bf16[64,2048]{1,0:T(8,128)(2,1)S(1)} %get-tuple-element.80), channel_id=1, source_target_pairs={{0,4},{1,3},{4,8},{5,1},{8,12},{9,5},{12,14},{13,9},{14,10},{15,13... | collective-permute-start | bytes 786440 | tf_op jit(solution)/shard_map/ppermute | solution.py:383
  65.9 3.3 %shard_map.120 = (f32[16,4,128]{2,1,0:T(4,128)S(1)}, bf16[256,256]{1,0:T(8,128)(2,1)S(1)}, f32[64,256]{1,0:T(8,128)S(1)}) custom-call(f32[16,4,128]{2,1,0:T(4,128)S(1)} %get-tuple-element.73.refs_0_, bf16[256,2048]{1,0:T(8,128)(2,1)S(1)} %collective-permute-done.10.refs_1_.block, bf16[256,2048]{1,0:T(8,128)(2,1)S(1)} %collective-permute-done.11.refs_2_, ...), custom_call_target="tpu_custom_call" | custom-call | flops 2415919104 | bytes 2097152 | tf_op jit(solution)/shard_map/pallas_call | solution.py:170
  69.2 4.1 %collective-permute-done.12.refs_1_.block = bf16[256,2048]{1,0:T(8,128)(2,1)S(1)} collective-permute-done((bf16[256,2048]{1,0:T(8,128)(2,1)S(1)}, bf16[256,2048]{1,0:T(8,128)(2,1)S(1)}, u32[]{:S(2)}, u32[]{:S(2)}) %collective-permute-start.12) | collective-permute-done | bytes 1048608 | tf_op jit(solution)/shard_map/ppermute | solution.py:383
  73.3 0.1 shard_map.123
  73.4 0.1 collective-permute-start.17
  73.5 2.4 %collective-permute-start.20 = (bf16[128,2048]{1,0:T(8,128)(2,1)S(1)}, bf16[128,2048]{1,0:T(8,128)(2,1)S(1)}, u32[]{:S(2)}, u32[]{:S(2)}) collective-permute-start(bf16[128,2048]{1,0:T(8,128)(2,1)S(1)} %get-tuple-element.88), channel_id=1, source_target_pairs={{0,4},{1,3},{4,8},{5,1},{8,12},{9,5},{12,14},{13,9},{14,10},{15,13... | collective-permute-start | bytes 1572872 | tf_op jit(solution)/shard_map/ppermute | solution.py:383
  75.8 3.3 %shard_map.121 = (f32[16,4,128]{2,1,0:T(4,128)S(1)}, bf16[256,256]{1,0:T(8,128)(2,1)S(1)}, f32[64,256]{1,0:T(8,128)S(1)}) custom-call(f32[16,4,128]{2,1,0:T(4,128)S(1)} %get-tuple-element.76.refs_0_, bf16[256,2048]{1,0:T(8,128)(2,1)S(1)} %collective-permute-done.12.refs_1_.block, bf16[256,2048]{1,0:T(8,128)(2,1)S(1)} %collective-permute-done.13.refs_2_, ...), custom_call_target="tpu_custom_call" | custom-call | flops 2415919104 | bytes 2097152 | tf_op jit(solution)/shard_map/pallas_call | solution.py:170
  79.2 0.1 collective-permute-start.18
  79.3 0.5 collective-permute-start.19
  79.8 0.1 collective-permute-start.16
  79.9 0.9 collective-permute-done.18.refs_3_
  80.8 0.4 collective-permute-done.19.refs_4_
  81.2 3.2 %shard_map.124 = (bf16[384,768]{1,0:T(8,128)(2,1)S(1)}, bf16[256,256]{1,0:T(8,128)(2,1)S(1)}, bf16[256,128]{1,0:T(8,128)(2,1)S(1)}) custom-call(bf16[128,2048]{1,0:T(8,128)(2,1)S(1)} %collective-permute-done.17.refs_0_, bf16[64,2048]{1,0:T(8,128)(2,1)S(1)} %collective-permute-done.14.refs_1_, bf16[64,2048]{1,0:T(8,128)(2,1)S(1)} %collective-permute-done.15.refs_2_, ...), custom_call_target="tpu_custom_call" | custom-call | flops 2415919104 | bytes 1572864 | tf_op jit(solution)/shard_map/pallas_call | solution.py:206
  84.4 0.2 collective-permute-done.20.refs_2_
  84.6 1.7 %shard_map.125 = (f32[16,4,128]{2,1,0:T(4,128)S(1)}, f32[64,256]{1,0:T(8,128)S(1)}, f32[128,2048]{1,0:T(8,128)S(1)}) custom-call(f32[16,4,128]{2,1,0:T(4,128)S(1)} %get-tuple-element.81.refs_0_, bf16[128,2048]{1,0:T(8,128)(2,1)S(1)} %collective-permute-done.16.refs_1_, bf16[128,2048]{1,0:T(8,128)(2,1)S(1)} %collective-permute-done.20.refs_2_, ...), custom_call_target="tpu_custom_call" | custom-call | flops 1207959552 | bytes 1048576 | tf_op jit(solution)/shard_map/pallas_call | solution.py:281
  86.3 0.1 collective-permute-done.21.dy
  86.5 0.3 shard_map.126
  86.8 12.9 %all_to_all.5.returned = f32[16,4,128]{2,1,0:T(4,128)S(1)} all-to-all(f32[16,4,128]{2,1,0:T(4,128)S(1)} %get-tuple-element.93), channel_id=1, replica_groups=mesh['grp'=2,'exp'=16] {'exp'}, dimensions={0} | all-to-all | bytes 65536 | tf_op jit(solution)/shard_map/all_to_all | solution.py:473
  99.7 1.1 %shard_map.127 = (f32[256,64]{1,0:T(8,128)}, f32[8,128]{1,0:T(8,128)}) custom-call(f32[16,4,128]{2,1,0:T(4,128)S(1)} %all_to_all.5.returned, s32[8,128]{1,0:T(8,128)S(1)} %bitcast.19, bf16[256,256]{1,0:T(8,128)(2,1)S(1)} %get-tuple-element.94.refs_0_, bf16[256,384]{1,0:T(8,128)(2,1)S(1)} %get-tuple-element.95.refs_1_, ...), custom_call_target="tpu_custom_call" | custom-call | tf_op jit(solution)/shard_map/pallas_call | solution.py:474
  (28 shorter events, 0.1 us)
Async XLA Ops:
  0.6 7.2 %collective-permute-start = (bf16[128,2048]{1,0:T(8,128)(2,1)}, bf16[128,2048]{1,0:T(8,128)(2,1)S(1)}, u32[]{:S(2)}, u32[]{:S(2)}) collective-permute-start(bf16[128,2048]{1,0:T(8,128)(2,1)} %refs_1_.1), channel_id=1, source_target_pairs={{0,1},{1,0},{2,3},{3,2},{4,5},{5,4},{6,7},{7,6},{8,9},{9,8},{10,11... | collective-permute-start | bytes 1572872 | tf_op jit(solution)/shard_map/ppermute | solution.py:386
  1.1 6.7 %collective-permute-start.1 = (bf16[128,2048]{1,0:T(8,128)(2,1)}, bf16[128,2048]{1,0:T(8,128)(2,1)S(1)}, u32[]{:S(2)}, u32[]{:S(2)}) collective-permute-start(bf16[128,2048]{1,0:T(8,128)(2,1)} %refs_2_.1), channel_id=1, source_target_pairs={{0,1},{1,0},{2,3},{3,2},{4,5},{5,4},{6,7},{7,6},{8,9},{9,8},{10,11... | collective-permute-start | bytes 1572872 | tf_op jit(solution)/shard_map/ppermute | solution.py:386
  1.2 18.8 %collective-permute-start.2 = (bf16[128,2048]{1,0:T(8,128)(2,1)}, bf16[128,2048]{1,0:T(8,128)(2,1)S(1)}, u32[]{:S(2)}, u32[]{:S(2)}) collective-permute-start(bf16[128,2048]{1,0:T(8,128)(2,1)} %refs_1_.1), channel_id=1, source_target_pairs={{0,4},{1,3},{4,8},{5,1},{8,12},{9,5},{12,14},{13,9},{14,10},{15,13... | collective-permute-start | bytes 1572872 | tf_op jit(solution)/shard_map/ppermute | solution.py:383
  4.2 15.9 %collective-permute-start.3 = (bf16[128,2048]{1,0:T(8,128)(2,1)}, bf16[128,2048]{1,0:T(8,128)(2,1)S(1)}, u32[]{:S(2)}, u32[]{:S(2)}) collective-permute-start(bf16[128,2048]{1,0:T(8,128)(2,1)} %refs_2_.1), channel_id=1, source_target_pairs={{0,4},{1,3},{4,8},{5,1},{8,12},{9,5},{12,14},{13,9},{14,10},{15,13... | collective-permute-start | bytes 1572872 | tf_op jit(solution)/shard_map/ppermute | solution.py:383
  5.8 0.7 copy-start.4
  6.5 0.7 copy-start.6
  7.2 0.7 copy-start.7
  8.0 20.4 %collective-permute-start.4 = (bf16[256,2048]{1,0:T(8,128)(2,1)S(1)}, bf16[256,2048]{1,0:T(8,128)(2,1)S(1)}, u32[]{:S(2)}, u32[]{:S(2)}) collective-permute-start(bf16[256,2048]{1,0:T(8,128)(2,1)S(1)} %shard_map.114.refs_3_), channel_id=1, source_target_pairs={{0,4},{1,3},{4,8},{5,1},{8,12},{9,5},{12,14},{13,9},{14,10},{15,13... | collective-permute-start | bytes 3145736 | tf_op jit(solution)/shard_map/ppermute | solution.py:383
  9.6 1.0 %copy-start = (bf16[128,2048]{1,0:T(8,128)(2,1)S(1)}, bf16[128,2048]{1,0:T(8,128)(2,1)}, u32[]{:S(2)}) copy-start(bf16[128,2048]{1,0:T(8,128)(2,1)} %refs_1_.1) | copy-start | bytes 1572868
  10.6 1.0 %copy-start.1 = (bf16[128,2048]{1,0:T(8,128)(2,1)S(1)}, bf16[128,2048]{1,0:T(8,128)(2,1)}, u32[]{:S(2)}) copy-start(bf16[128,2048]{1,0:T(8,128)(2,1)} %refs_2_.1) | copy-start | bytes 1572868
  11.7 0.9 copy-start.2
  12.6 0.9 copy-start.3
  20.2 10.3 %collective-permute-start.5 = (bf16[256,2048]{1,0:T(8,128)(2,1)S(1)}, bf16[256,2048]{1,0:T(8,128)(2,1)S(1)}, u32[]{:S(2)}, u32[]{:S(2)}) collective-permute-start(bf16[256,2048]{1,0:T(8,128)(2,1)S(1)} %shard_map.116.refs_3_), channel_id=1, source_target_pairs={{0,1},{1,0},{2,3},{3,2},{4,5},{5,4},{6,7},{7,6},{8,9},{9,8},{10,11... | collective-permute-start | bytes 3145736 | tf_op jit(solution)/shard_map/ppermute | solution.py:386
  20.3 19.3 %collective-permute-start.6 = (bf16[256,2048]{1,0:T(8,128)(2,1)S(1)}, bf16[256,2048]{1,0:T(8,128)(2,1)S(1)}, u32[]{:S(2)}, u32[]{:S(2)}) collective-permute-start(bf16[256,2048]{1,0:T(8,128)(2,1)S(1)} %shard_map.116.refs_3_), channel_id=1, source_target_pairs={{0,4},{1,3},{4,8},{5,1},{8,12},{9,5},{12,14},{13,9},{14,10},{15,13... | collective-permute-start | bytes 3145736 | tf_op jit(solution)/shard_map/ppermute | solution.py:383
  28.4 13.4 %collective-permute-start.7 = (bf16[256,2048]{1,0:T(8,128)(2,1)S(1)}, bf16[256,2048]{1,0:T(8,128)(2,1)S(1)}, u32[]{:S(2)}, u32[]{:S(2)}) collective-permute-start(bf16[256,2048]{1,0:T(8,128)(2,1)S(1)} %collective-permute-done.4.refs_1_), channel_id=1, source_target_pairs={{0,1},{1,0},{2,3},{3,2},{4,5},{5,4},{6,7},{7,6},{8,9},{9,8},{10,11... | collective-permute-start | bytes 3145736 | tf_op jit(solution)/shard_map/ppermute | solution.py:386
  28.4 22.5 %collective-permute-start.8 = (bf16[256,2048]{1,0:T(8,128)(2,1)S(1)}, bf16[256,2048]{1,0:T(8,128)(2,1)S(1)}, u32[]{:S(2)}, u32[]{:S(2)}) collective-permute-start(bf16[256,2048]{1,0:T(8,128)(2,1)S(1)} %collective-permute-done.4.refs_1_), channel_id=1, source_target_pairs={{0,4},{1,3},{4,8},{5,1},{8,12},{9,5},{12,14},{13,9},{14,10},{15,13... | collective-permute-start | bytes 3145736 | tf_op jit(solution)/shard_map/ppermute | solution.py:383
  39.6 13.4 %collective-permute-start.9 = (bf16[256,2048]{1,0:T(8,128)(2,1)S(1)}, bf16[256,2048]{1,0:T(8,128)(2,1)S(1)}, u32[]{:S(2)}, u32[]{:S(2)}) collective-permute-start(bf16[256,2048]{1,0:T(8,128)(2,1)S(1)} %collective-permute-done.6.refs_1_), channel_id=1, source_target_pairs={{0,1},{1,0},{2,3},{3,2},{4,5},{5,4},{6,7},{7,6},{8,9},{9,8},{10,11... | collective-permute-start | bytes 3145736 | tf_op jit(solution)/shard_map/ppermute | solution.py:386
  39.6 22.5 %collective-permute-start.10 = (bf16[256,2048]{1,0:T(8,128)(2,1)S(1)}, bf16[256,2048]{1,0:T(8,128)(2,1)S(1)}, u32[]{:S(2)}, u32[]{:S(2)}) collective-permute-start(bf16[256,2048]{1,0:T(8,128)(2,1)S(1)} %collective-permute-done.6.refs_1_), channel_id=1, source_target_pairs={{0,4},{1,3},{4,8},{5,1},{8,12},{9,5},{12,14},{13,9},{14,10},{15,13... | collective-permute-start | bytes 3145736 | tf_op jit(solution)/shard_map/ppermute | solution.py:383
  50.8 15.1 %collective-permute-start.11 = (bf16[256,2048]{1,0:T(8,128)(2,1)S(1)}, bf16[256,2048]{1,0:T(8,128)(2,1)S(1)}, u32[]{:S(2)}, u32[]{:S(2)}) collective-permute-start(bf16[256,2048]{1,0:T(8,128)(2,1)S(1)} %collective-permute-done.8.refs_1_), channel_id=1, source_target_pairs={{0,1},{1,0},{2,3},{3,2},{4,5},{5,4},{6,7},{7,6},{8,9},{9,8},{10,11... | collective-permute-start | bytes 3145736 | tf_op jit(solution)/shard_map/ppermute | solution.py:386
  50.8 22.5 %collective-permute-start.12 = (bf16[256,2048]{1,0:T(8,128)(2,1)S(1)}, bf16[256,2048]{1,0:T(8,128)(2,1)S(1)}, u32[]{:S(2)}, u32[]{:S(2)}) collective-permute-start(bf16[256,2048]{1,0:T(8,128)(2,1)S(1)} %collective-permute-done.8.refs_1_), channel_id=1, source_target_pairs={{0,4},{1,3},{4,8},{5,1},{8,12},{9,5},{12,14},{13,9},{14,10},{15,13... | collective-permute-start | bytes 3145736 | tf_op jit(solution)/shard_map/ppermute | solution.py:383
  62.1 13.8 %collective-permute-start.13 = (bf16[256,2048]{1,0:T(8,128)(2,1)S(1)}, bf16[256,2048]{1,0:T(8,128)(2,1)S(1)}, u32[]{:S(2)}, u32[]{:S(2)}) collective-permute-start(bf16[256,2048]{1,0:T(8,128)(2,1)S(1)} %collective-permute-done.10.refs_1_.block), channel_id=1, source_target_pairs={{0,1},{1,0},{2,3},{3,2},{4,5},{5,4},{6,7},{7,6},{8,9},{9,8},{10,11... | collective-permute-start | bytes 3145736 | tf_op jit(solution)/shard_map/ppermute | solution.py:386
  62.1 17.0 %collective-permute-start.14 = (bf16[64,2048]{1,0:T(8,128)(2,1)S(1)}, bf16[64,2048]{1,0:T(8,128)(2,1)S(1)}, u32[]{:S(2)}, u32[]{:S(2)}) collective-permute-start(bf16[64,2048]{1,0:T(8,128)(2,1)S(1)} %get-tuple-element.79), channel_id=1, source_target_pairs={{0,4},{1,3},{4,8},{5,1},{8,12},{9,5},{12,14},{13,9},{14,10},{15,13... | collective-permute-start | bytes 786440 | tf_op jit(solution)/shard_map/ppermute | solution.py:383
  64.3 14.9 %collective-permute-start.15 = (bf16[64,2048]{1,0:T(8,128)(2,1)S(1)}, bf16[64,2048]{1,0:T(8,128)(2,1)S(1)}, u32[]{:S(2)}, u32[]{:S(2)}) collective-permute-start(bf16[64,2048]{1,0:T(8,128)(2,1)S(1)} %get-tuple-element.80), channel_id=1, source_target_pairs={{0,4},{1,3},{4,8},{5,1},{8,12},{9,5},{12,14},{13,9},{14,10},{15,13... | collective-permute-start | bytes 786440 | tf_op jit(solution)/shard_map/ppermute | solution.py:383
  73.4 7.8 %collective-permute-start.17 = (bf16[128,2048]{1,0:T(8,128)(2,1)S(1)}, bf16[128,2048]{1,0:T(8,128)(2,1)S(1)}, u32[]{:S(2)}, u32[]{:S(2)}) collective-permute-start(bf16[128,2048]{1,0:T(8,128)(2,1)S(1)} %get-tuple-element.83), channel_id=1, source_target_pairs={{0,1},{1,0},{2,3},{3,2},{4,5},{5,4},{6,7},{7,6},{8,9},{9,8},{10,11... | collective-permute-start | bytes 1572872 | tf_op jit(solution)/shard_map/ppermute | solution.py:386
  73.5 11.1 %collective-permute-start.20 = (bf16[128,2048]{1,0:T(8,128)(2,1)S(1)}, bf16[128,2048]{1,0:T(8,128)(2,1)S(1)}, u32[]{:S(2)}, u32[]{:S(2)}) collective-permute-start(bf16[128,2048]{1,0:T(8,128)(2,1)S(1)} %get-tuple-element.88), channel_id=1, source_target_pairs={{0,4},{1,3},{4,8},{5,1},{8,12},{9,5},{12,14},{13,9},{14,10},{15,13... | collective-permute-start | bytes 1572872 | tf_op jit(solution)/shard_map/ppermute | solution.py:383
  79.2 1.6 %collective-permute-start.18 = (bf16[64,2048]{1,0:T(8,128)(2,1)S(1)}, bf16[64,2048]{1,0:T(8,128)(2,1)S(1)}, u32[]{:S(2)}, u32[]{:S(2)}) collective-permute-start(bf16[64,2048]{1,0:T(8,128)(2,1)S(1)} %collective-permute-done.14.refs_1_), channel_id=1, source_target_pairs={{0,1},{1,0},{2,3},{3,2},{4,5},{5,4},{6,7},{7,6},{8,9},{9,8},{10,11... | collective-permute-start | bytes 786440 | tf_op jit(solution)/shard_map/ppermute | solution.py:386
  79.3 1.9 %collective-permute-start.19 = (bf16[64,2048]{1,0:T(8,128)(2,1)S(1)}, bf16[64,2048]{1,0:T(8,128)(2,1)S(1)}, u32[]{:S(2)}, u32[]{:S(2)}) collective-permute-start(bf16[64,2048]{1,0:T(8,128)(2,1)S(1)} %collective-permute-done.15.refs_2_), channel_id=1, source_target_pairs={{0,1},{1,0},{2,3},{3,2},{4,5},{5,4},{6,7},{7,6},{8,9},{9,8},{10,11... | collective-permute-start | bytes 786440 | tf_op jit(solution)/shard_map/ppermute | solution.py:386
  79.8 4.8 %collective-permute-start.16 = (bf16[128,2048]{1,0:T(8,128)(2,1)S(1)}, bf16[128,2048]{1,0:T(8,128)(2,1)S(1)}, u32[]{:S(2)}, u32[]{:S(2)}) collective-permute-start(bf16[128,2048]{1,0:T(8,128)(2,1)S(1)} %get-tuple-element.82), channel_id=1, source_target_pairs={{0,1},{1,0},{2,3},{3,2},{4,5},{5,4},{6,7},{7,6},{8,9},{9,8},{10,11... | collective-permute-start | bytes 1572872 | tf_op jit(solution)/shard_map/ppermute | solution.py:386
  84.5 15.1 %copy-start.5 = (s32[128,8]{0,1:T(8,128)S(1)}, s32[128,8]{0,1:T(8,128)}, u32[]{:S(2)}) copy-start(s32[128,8]{0,1:T(8,128)} %param.12) | copy-start | bytes 12292
  84.5 1.9 %collective-permute-start.21 = (bf16[128,2048]{1,0:T(8,128)(2,1)S(1)}, bf16[128,2048]{1,0:T(8,128)(2,1)S(1)}, u32[]{:S(2)}, u32[]{:S(2)}) collective-permute-start(bf16[128,2048]{1,0:T(8,128)(2,1)S(1)} %collective-permute-done.20.refs_2_), channel_id=1, source_target_pairs={{0,1},{1,0},{2,3},{3,2},{4,5},{5,4},{6,7},{7,6},{8,9},{9,8},{10,11... | collective-permute-start | bytes 1572872 | tf_op jit(solution)/shard_map/ppermute | solution.py:386

commit v17 on v16

--- a/solution.py
+++ b/solution.py
@@ -292,24 +292,25 @@
     low_in, proj_in = refs[: len(jobs)], refs[len(jobs) : 2 * len(jobs)]
     feat, route_grad = refs[-2:]
     rows = returned.shape[2]
-    width, rank = low_in[0].shape[0], proj_in[0].shape[0]
-    doc_of = lax.broadcasted_iota(jnp.int32, (width, rows), 0) // rank
-    spread, high_side = [], []
-    for names, low_side, proj_cot in zip(jobs, low_in, proj_in):
+    docs, rank = feat.shape[0], feat.shape[2]
+    low_side, high_side = [], []
+    for names, low, proj_cot in zip(jobs, low_in, proj_in):
+        low_side.append(low[...])
         for i, name in enumerate(names):
             place = slice(i * rows, (i + 1) * rows)
             owner = block_owner(name, returned.shape[0] // 2)
             weight = returned[owner, 1:2, :]
             doc = returned[owner, 2:3, :].astype(jnp.int32)
-            high_side.append((weight * proj_cot[:, place]).astype(jnp.bfloat16))
-            low = low_side[:, place].astype(jnp.float32)
-            spread.append(jnp.where(doc == doc_of, low, 0.0).astype(jnp.bfloat16))
-    feat[...] = lax.dot_general(
-        jnp.concatenate(spread, axis=1),
+            parts = [jnp.where(doc == d, weight, 0.0) * proj_cot[:, place] for d in range(docs)]
+            high_side.append(jnp.concatenate(parts, axis=0).astype(jnp.bfloat16))
+    total = lax.dot_general(
+        jnp.concatenate(low_side, axis=1),
         jnp.concatenate(high_side, axis=1),
         (((1,), (1,)), ((), ())),
         preferred_element_type=jnp.float32,
     )
+    for d in range(docs):
+        feat[d] = total[:, d * rank : (d + 1) * rank]
     picked = jnp.zeros(route_grad.shape, jnp.float32)
     for e in range(returned.shape[0]):
         picked = jnp.where(routes[...] == e, returned[e, 0:1, :], picked)
@@ -421,7 +422,7 @@
         blocks = [held[name] for name in names if name in held]
         if weights is None:
             sheet, low_side, proj_cot, *weights = work(
-                names, sheet, blocks, given, apart=(tokens, cotangent), load=docs_count
+                names, sheet, blocks, given, apart=(tokens, cotangent), load=1
             )
         else:
             sheet, low_side, proj_cot = work(names, sheet, blocks, weights)
@@ -474,14 +475,14 @@
     feature, route_grad = pl.pallas_call(
         functools.partial(outcome_kernel, jobs),
         out_shape=[
-            jax.ShapeDtypeStruct((docs_count * rank, rank), jnp.float32),
+            jax.ShapeDtypeStruct((docs_count, rank, rank), jnp.float32),
             jax.ShapeDtypeStruct((chosen, tok_rows), jnp.float32),
         ],
         in_specs=[inside] * (2 + 2 * len(lows)),
         out_specs=[inside] * 2,
         compiler_params=pltpu.CompilerParams(vmem_limit_bytes=16 * 1024 * 1024),
     )(returned, routes.T, *lows, *projs)
-    return feature.reshape(docs_count, 1, rank, rank), route_grad.T
+    return feature[:, None], route_grad.T
 
 
 def by_routing(

time: 101 us -> 101 us (level)
  waiting for transfers between devices: 28.4 us -> 30.4 us
  Pallas kernels: 31.1 us -> 29.5 us
    ppermute x10, waiting for transfers between devices: 26.9 us -> 28.8 us  [hop(): return lax.ppermute(block, 'exp', onward)]
    pallas_call x6, Pallas kernels: 24.5 us -> 23 us  [work(): return call(sheet, *apart, *block_in, *weights)]
  transfers between devices with their start and end apart: 22 -> 22, of which waited for: 9 -> 10; matrix products, arithmetic and copies ran while one was open for 0% -> 0% of each run, Pallas kernels for 29% -> 28%
where the time goes in v17:
time: 101 us
  waiting for transfers between devices  30.4 us (30%)
  Pallas kernels  29.5 us (29%)
  starting transfers between devices  21.2 us (21%)
  blocking collectives  12.9 us (13%)
  local copies, waits for them, and re-layouts  5.95 us (6%)
    ppermute x10, waiting for transfers between devices, hop(): return lax.ppermute(block, 'exp', onward)  28.8 us
    pallas_call x6, Pallas kernels, work(): return call(sheet, *apart, *block_in, *weights)  23 us
    ppermute x10, starting transfers between devices, hop(): return lax.ppermute(block, 'exp', onward)  20 us
    all_to_all x1, blocking collectives, by_ring(): lax.all_to_all(sheet, 'exp', split_axis=0, concat_axis=0, tiled=True)  12.9 us
    unnamed x16, local copies, waits for them, and re-layouts  5.95 us
    pallas_call x1, Pallas kernels, front(): pl.pallas_call(front_kernel, out_shape=[jax.ShapeDtypeStruct((rows, units...  3.08 us
  transfers between devices with their start and end apart: 22, of which 10 were waited for; matrix products, arithmetic and copies ran while one was open for 0% of the time, Pallas kernels for 28%

profile of v17, /device:TPU:0, one launch (start us, length us, event | category | flops | bytes accessed | tf_op | source)
XLA Modules:
  0.0 100.8 jit_solution(6592978749761587054)
XLA Ops:
  0.6 0.5 collective-permute-start
  1.1 0.1 collective-permute-start.1
  1.2 3.0 %collective-permute-start.2 = (bf16[128,2048]{1,0:T(8,128)(2,1)}, bf16[128,2048]{1,0:T(8,128)(2,1)S(1)}, u32[]{:S(2)}, u32[]{:S(2)}) collective-permute-start(bf16[128,2048]{1,0:T(8,128)(2,1)} %refs_1_.1), channel_id=1, source_target_pairs={{0,4},{1,3},{4,8},{5,1},{8,12},{9,5},{12,14},{13,9},{14,10},{15,13... | collective-permute-start | bytes 1572872 | tf_op jit(solution)/shard_map/ppermute | solution.py:384
  4.2 1.6 %collective-permute-start.3 = (bf16[128,2048]{1,0:T(8,128)(2,1)}, bf16[128,2048]{1,0:T(8,128)(2,1)S(1)}, u32[]{:S(2)}, u32[]{:S(2)}) collective-permute-start(bf16[128,2048]{1,0:T(8,128)(2,1)} %refs_2_.1), channel_id=1, source_target_pairs={{0,4},{1,3},{4,8},{5,1},{8,12},{9,5},{12,14},{13,9},{14,10},{15,13... | collective-permute-start | bytes 1572872 | tf_op jit(solution)/shard_map/ppermute | solution.py:384
  5.8 0.7 copy-done.4
  6.5 0.7 copy-done.6
  7.2 0.7 copy-done.7
  7.9 0.1 shard_map.114.refs_3_
  8.0 1.6 %collective-permute-start.4 = (bf16[256,2048]{1,0:T(8,128)(2,1)S(1)}, bf16[256,2048]{1,0:T(8,128)(2,1)S(1)}, u32[]{:S(2)}, u32[]{:S(2)}) collective-permute-start(bf16[256,2048]{1,0:T(8,128)(2,1)S(1)} %shard_map.114.refs_3_), channel_id=1, source_target_pairs={{0,4},{1,3},{4,8},{5,1},{8,12},{9,5},{12,14},{13,9},{14,10},{15,13... | collective-permute-start | bytes 3145736 | tf_op jit(solution)/shard_map/ppermute | solution.py:384
  9.6 1.0 %copy-done = bf16[128,2048]{1,0:T(8,128)(2,1)S(1)} copy-done((bf16[128,2048]{1,0:T(8,128)(2,1)S(1)}, bf16[128,2048]{1,0:T(8,128)(2,1)}, u32[]{:S(2)}) %copy-start) | copy-done | bytes 524312
  10.6 1.0 %copy-done.1 = bf16[128,2048]{1,0:T(8,128)(2,1)S(1)} copy-done((bf16[128,2048]{1,0:T(8,128)(2,1)S(1)}, bf16[128,2048]{1,0:T(8,128)(2,1)}, u32[]{:S(2)}) %copy-start.1) | copy-done | bytes 524312
  11.7 0.9 copy-done.2
  12.6 0.9 copy-done.3
  13.5 6.1 %shard_map.115 = (f32[16,4,128]{2,1,0:T(4,128)S(1)}, bf16[64,256]{1,0:T(8,128)(2,1)S(1)}, f32[64,256]{1,0:T(8,128)S(1)}, bf16[2048,768]{1,0:T(8,128)(2,1)S(1)}, ...) custom-call(f32[16,4,128]{2,1,0:T(4,128)S(1)} %shard_map.113.refs_0_, ...), custom_call_target="tpu_custom_call" | custom-call | flops 2415919104 | bytes 2097152 | tf_op jit(solution)/shard_map/pallas_call | solution.py:170
  19.6 0.1 shard_map.116.refs_3_
  19.7 0.1 collective-permute-start.5
  19.8 1.5 %collective-permute-start.6 = (bf16[256,2048]{1,0:T(8,128)(2,1)S(1)}, bf16[256,2048]{1,0:T(8,128)(2,1)S(1)}, u32[]{:S(2)}, u32[]{:S(2)}) collective-permute-start(bf16[256,2048]{1,0:T(8,128)(2,1)S(1)} %shard_map.116.refs_3_), channel_id=1, source_target_pairs={{0,4},{1,3},{4,8},{5,1},{8,12},{9,5},{12,14},{13,9},{14,10},{15,13... | collective-permute-start | bytes 3145736 | tf_op jit(solution)/shard_map/ppermute | solution.py:384
  21.3 7.1 %collective-permute-done.4.refs_1_ = bf16[256,2048]{1,0:T(8,128)(2,1)S(1)} collective-permute-done((bf16[256,2048]{1,0:T(8,128)(2,1)S(1)}, bf16[256,2048]{1,0:T(8,128)(2,1)S(1)}, u32[]{:S(2)}, u32[]{:S(2)}) %collective-permute-start.4) | collective-permute-done | bytes 1048608 | tf_op jit(solution)/shard_map/ppermute | solution.py:384
  28.4 2.1 %collective-permute-start.8 = (bf16[256,2048]{1,0:T(8,128)(2,1)S(1)}, bf16[256,2048]{1,0:T(8,128)(2,1)S(1)}, u32[]{:S(2)}, u32[]{:S(2)}) collective-permute-start(bf16[256,2048]{1,0:T(8,128)(2,1)S(1)} %collective-permute-done.4.refs_1_), channel_id=1, source_target_pairs={{0,4},{1,3},{4,8},{5,1},{8,12},{9,5},{12,14},{13,9},{14,10},{15,13... | collective-permute-start | bytes 3145736 | tf_op jit(solution)/shard_map/ppermute | solution.py:384
  30.5 4.7 %shard_map.117 = (f32[16,4,128]{2,1,0:T(4,128)S(1)}, bf16[64,384]{1,0:T(8,128)(2,1)S(1)}, f32[64,384]{1,0:T(8,128)S(1)}) custom-call(f32[16,4,128]{2,1,0:T(4,128)S(1)} %get-tuple-element.58.refs_0_, bf16[256,2048]{1,0:T(8,128)(2,1)S(1)} %collective-permute-done.4.refs_1_, bf16[256,2048]{1,0:T(8,128)(2,1)S(1)} %collective-permute-done.5.refs_2_, ...), custom_call_target="tpu_custom_call" | custom-call | flops 3623878656 | bytes 3145728 | tf_op jit(solution)/shard_map/pallas_call | solution.py:170
  35.2 4.4 %collective-permute-done.6.refs_1_ = bf16[256,2048]{1,0:T(8,128)(2,1)S(1)} collective-permute-done((bf16[256,2048]{1,0:T(8,128)(2,1)S(1)}, bf16[256,2048]{1,0:T(8,128)(2,1)S(1)}, u32[]{:S(2)}, u32[]{:S(2)}) %collective-permute-start.6) | collective-permute-done | bytes 1048608 | tf_op jit(solution)/shard_map/ppermute | solution.py:384
  39.6 2.1 %collective-permute-start.10 = (bf16[256,2048]{1,0:T(8,128)(2,1)S(1)}, bf16[256,2048]{1,0:T(8,128)(2,1)S(1)}, u32[]{:S(2)}, u32[]{:S(2)}) collective-permute-start(bf16[256,2048]{1,0:T(8,128)(2,1)S(1)} %collective-permute-done.6.refs_1_), channel_id=1, source_target_pairs={{0,4},{1,3},{4,8},{5,1},{8,12},{9,5},{12,14},{13,9},{14,10},{15,13... | collective-permute-start | bytes 3145736 | tf_op jit(solution)/shard_map/ppermute | solution.py:384
  41.7 3.0 %shard_map.118 = (f32[16,4,128]{2,1,0:T(4,128)S(1)}, bf16[64,256]{1,0:T(8,128)(2,1)S(1)}, f32[64,256]{1,0:T(8,128)S(1)}) custom-call(f32[16,4,128]{2,1,0:T(4,128)S(1)} %get-tuple-element.67.refs_0_, bf16[256,2048]{1,0:T(8,128)(2,1)S(1)} %collective-permute-done.6.refs_1_, bf16[256,2048]{1,0:T(8,128)(2,1)S(1)} %collective-permute-done.7.refs_2_, ...), custom_call_target="tpu_custom_call" | custom-call | flops 2415919104 | bytes 2097152 | tf_op jit(solution)/shard_map/pallas_call | solution.py:170
  44.8 6.1 %collective-permute-done.8.refs_1_ = bf16[256,2048]{1,0:T(8,128)(2,1)S(1)} collective-permute-done((bf16[256,2048]{1,0:T(8,128)(2,1)S(1)}, bf16[256,2048]{1,0:T(8,128)(2,1)S(1)}, u32[]{:S(2)}, u32[]{:S(2)}) %collective-permute-start.8) | collective-permute-done | bytes 1048608 | tf_op jit(solution)/shard_map/ppermute | solution.py:384
  50.8 2.1 %collective-permute-start.12 = (bf16[256,2048]{1,0:T(8,128)(2,1)S(1)}, bf16[256,2048]{1,0:T(8,128)(2,1)S(1)}, u32[]{:S(2)}, u32[]{:S(2)}) collective-permute-start(bf16[256,2048]{1,0:T(8,128)(2,1)S(1)} %collective-permute-done.8.refs_1_), channel_id=1, source_target_pairs={{0,4},{1,3},{4,8},{5,1},{8,12},{9,5},{12,14},{13,9},{14,10},{15,13... | collective-permute-start | bytes 3145736 | tf_op jit(solution)/shard_map/ppermute | solution.py:384
  53.0 3.0 %shard_map.119 = (f32[16,4,128]{2,1,0:T(4,128)S(1)}, bf16[64,256]{1,0:T(8,128)(2,1)S(1)}, f32[64,256]{1,0:T(8,128)S(1)}) custom-call(f32[16,4,128]{2,1,0:T(4,128)S(1)} %get-tuple-element.70.refs_0_, bf16[256,2048]{1,0:T(8,128)(2,1)S(1)} %collective-permute-done.8.refs_1_, bf16[256,2048]{1,0:T(8,128)(2,1)S(1)} %collective-permute-done.9.refs_2_, ...), custom_call_target="tpu_custom_call" | custom-call | flops 2415919104 | bytes 2097152 | tf_op jit(solution)/shard_map/pallas_call | solution.py:170
  56.0 6.1 %collective-permute-done.10.refs_1_.block = bf16[256,2048]{1,0:T(8,128)(2,1)S(1)} collective-permute-done((bf16[256,2048]{1,0:T(8,128)(2,1)S(1)}, bf16[256,2048]{1,0:T(8,128)(2,1)S(1)}, u32[]{:S(2)}, u32[]{:S(2)}) %collective-permute-start.10) | collective-permute-done | bytes 1048608 | tf_op jit(solution)/shard_map/ppermute | solution.py:384
  62.1 0.1 shard_map.122
  62.1 2.2 %collective-permute-start.14 = (bf16[64,2048]{1,0:T(8,128)(2,1)S(1)}, bf16[64,2048]{1,0:T(8,128)(2,1)S(1)}, u32[]{:S(2)}, u32[]{:S(2)}) collective-permute-start(bf16[64,2048]{1,0:T(8,128)(2,1)S(1)} %get-tuple-element.79), channel_id=1, source_target_pairs={{0,4},{1,3},{4,8},{5,1},{8,12},{9,5},{12,14},{13,9},{14,10},{15,13... | collective-permute-start | bytes 786440 | tf_op jit(solution)/shard_map/ppermute | solution.py:384
  64.3 1.6 %collective-permute-start.15 = (bf16[64,2048]{1,0:T(8,128)(2,1)S(1)}, bf16[64,2048]{1,0:T(8,128)(2,1)S(1)}, u32[]{:S(2)}, u32[]{:S(2)}) collective-permute-start(bf16[64,2048]{1,0:T(8,128)(2,1)S(1)} %get-tuple-element.80), channel_id=1, source_target_pairs={{0,4},{1,3},{4,8},{5,1},{8,12},{9,5},{12,14},{13,9},{14,10},{15,13... | collective-permute-start | bytes 786440 | tf_op jit(solution)/shard_map/ppermute | solution.py:384
  65.9 3.0 %shard_map.120 = (f32[16,4,128]{2,1,0:T(4,128)S(1)}, bf16[64,256]{1,0:T(8,128)(2,1)S(1)}, f32[64,256]{1,0:T(8,128)S(1)}) custom-call(f32[16,4,128]{2,1,0:T(4,128)S(1)} %get-tuple-element.73.refs_0_, bf16[256,2048]{1,0:T(8,128)(2,1)S(1)} %collective-permute-done.10.refs_1_.block, bf16[256,2048]{1,0:T(8,128)(2,1)S(1)} %collective-permute-done.11.refs_2_, ...), custom_call_target="tpu_custom_call" | custom-call | flops 2415919104 | bytes 2097152 | tf_op jit(solution)/shard_map/pallas_call | solution.py:170
  68.9 4.4 %collective-permute-done.12.refs_1_.block = bf16[256,2048]{1,0:T(8,128)(2,1)S(1)} collective-permute-done((bf16[256,2048]{1,0:T(8,128)(2,1)S(1)}, bf16[256,2048]{1,0:T(8,128)(2,1)S(1)}, u32[]{:S(2)}, u32[]{:S(2)}) %collective-permute-start.12) | collective-permute-done | bytes 1048608 | tf_op jit(solution)/shard_map/ppermute | solution.py:384
  73.3 0.1 shard_map.123
  73.4 0.1 collective-permute-start.17
  73.5 2.2 %collective-permute-start.20 = (bf16[128,2048]{1,0:T(8,128)(2,1)S(1)}, bf16[128,2048]{1,0:T(8,128)(2,1)S(1)}, u32[]{:S(2)}, u32[]{:S(2)}) collective-permute-start(bf16[128,2048]{1,0:T(8,128)(2,1)S(1)} %get-tuple-element.88), channel_id=1, source_target_pairs={{0,4},{1,3},{4,8},{5,1},{8,12},{9,5},{12,14},{13,9},{14,10},{15,13... | collective-permute-start | bytes 1572872 | tf_op jit(solution)/shard_map/ppermute | solution.py:384
  75.6 3.0 %shard_map.121 = (f32[16,4,128]{2,1,0:T(4,128)S(1)}, bf16[64,256]{1,0:T(8,128)(2,1)S(1)}, f32[64,256]{1,0:T(8,128)S(1)}) custom-call(f32[16,4,128]{2,1,0:T(4,128)S(1)} %get-tuple-element.76.refs_0_, bf16[256,2048]{1,0:T(8,128)(2,1)S(1)} %collective-permute-done.12.refs_1_.block, bf16[256,2048]{1,0:T(8,128)(2,1)S(1)} %collective-permute-done.13.refs_2_, ...), custom_call_target="tpu_custom_call" | custom-call | flops 2415919104 | bytes 2097152 | tf_op jit(solution)/shard_map/pallas_call | solution.py:170
  78.7 0.2 collective-permute-done.15.refs_2_
  78.9 0.5 collective-permute-start.19
  79.4 0.0 collective-permute-start.16
  79.4 1.0 %collective-permute-done.18.refs_3_ = bf16[64,2048]{1,0:T(8,128)(2,1)S(1)} collective-permute-done((bf16[64,2048]{1,0:T(8,128)(2,1)S(1)}, bf16[64,2048]{1,0:T(8,128)(2,1)S(1)}, u32[]{:S(2)}, u32[]{:S(2)}) %collective-permute-start.18) | collective-permute-done | bytes 262176 | tf_op jit(solution)/shard_map/ppermute | solution.py:387
  80.5 0.4 collective-permute-done.19.refs_4_
  80.8 3.1 %shard_map.124 = (bf16[384,768]{1,0:T(8,128)(2,1)S(1)}, bf16[64,256]{1,0:T(8,128)(2,1)S(1)}, bf16[64,128]{1,0:T(8,128)(2,1)S(1)}) custom-call(bf16[128,2048]{1,0:T(8,128)(2,1)S(1)} %collective-permute-done.17.refs_0_, bf16[64,2048]{1,0:T(8,128)(2,1)S(1)} %collective-permute-done.14.refs_1_, bf16[64,2048]{1,0:T(8,128)(2,1)S(1)} %collective-permute-done.15.refs_2_, ...), custom_call_target="tpu_custom_call" | custom-call | flops 2415919104 | bytes 1572864 | tf_op jit(solution)/shard_map/pallas_call | solution.py:206
  83.9 0.6 collective-permute-done.20.refs_2_
  84.6 1.7 %shard_map.125 = (f32[16,4,128]{2,1,0:T(4,128)S(1)}, f32[64,256]{1,0:T(8,128)S(1)}, f32[128,2048]{1,0:T(8,128)S(1)}) custom-call(f32[16,4,128]{2,1,0:T(4,128)S(1)} %get-tuple-element.81.refs_0_, bf16[128,2048]{1,0:T(8,128)(2,1)S(1)} %collective-permute-done.16.refs_1_, bf16[128,2048]{1,0:T(8,128)(2,1)S(1)} %collective-permute-done.20.refs_2_, ...), custom_call_target="tpu_custom_call" | custom-call | flops 1207959552 | bytes 1048576 | tf_op jit(solution)/shard_map/pallas_call | solution.py:281
  86.3 0.2 collective-permute-done.21.dy
  86.5 0.3 shard_map.126
  86.8 12.9 %all_to_all.5.returned = f32[16,4,128]{2,1,0:T(4,128)S(1)} all-to-all(f32[16,4,128]{2,1,0:T(4,128)S(1)} %get-tuple-element.93), channel_id=1, replica_groups=mesh['grp'=2,'exp'=16] {'exp'}, dimensions={0} | all-to-all | bytes 65536 | tf_op jit(solution)/shard_map/all_to_all | solution.py:474
  99.7 1.2 %shard_map.127 = (f32[4,64,64]{2,1,0:T(8,128)}, f32[8,128]{1,0:T(8,128)}) custom-call(f32[16,4,128]{2,1,0:T(4,128)S(1)} %all_to_all.5.returned, s32[8,128]{1,0:T(8,128)S(1)} %bitcast.19, bf16[64,256]{1,0:T(8,128)(2,1)S(1)} %get-tuple-element.94.refs_0_, bf16[64,384]{1,0:T(8,128)(2,1)S(1)} %get-tuple-element.95.refs_1_, ...), custom_call_target="tpu_custom_call" | custom-call | tf_op jit(solution)/shard_map/pallas_call | solution.py:475
  (28 shorter events, 0.1 us)
Async XLA Ops:
  0.6 7.2 %collective-permute-start = (bf16[128,2048]{1,0:T(8,128)(2,1)}, bf16[128,2048]{1,0:T(8,128)(2,1)S(1)}, u32[]{:S(2)}, u32[]{:S(2)}) collective-permute-start(bf16[128,2048]{1,0:T(8,128)(2,1)} %refs_1_.1), channel_id=1, source_target_pairs={{0,1},{1,0},{2,3},{3,2},{4,5},{5,4},{6,7},{7,6},{8,9},{9,8},{10,11... | collective-permute-start | bytes 1572872 | tf_op jit(solution)/shard_map/ppermute | solution.py:387
  1.1 6.7 %collective-permute-start.1 = (bf16[128,2048]{1,0:T(8,128)(2,1)}, bf16[128,2048]{1,0:T(8,128)(2,1)S(1)}, u32[]{:S(2)}, u32[]{:S(2)}) collective-permute-start(bf16[128,2048]{1,0:T(8,128)(2,1)} %refs_2_.1), channel_id=1, source_target_pairs={{0,1},{1,0},{2,3},{3,2},{4,5},{5,4},{6,7},{7,6},{8,9},{9,8},{10,11... | collective-permute-start | bytes 1572872 | tf_op jit(solution)/shard_map/ppermute | solution.py:387
  1.2 18.4 %collective-permute-start.2 = (bf16[128,2048]{1,0:T(8,128)(2,1)}, bf16[128,2048]{1,0:T(8,128)(2,1)S(1)}, u32[]{:S(2)}, u32[]{:S(2)}) collective-permute-start(bf16[128,2048]{1,0:T(8,128)(2,1)} %refs_1_.1), channel_id=1, source_target_pairs={{0,4},{1,3},{4,8},{5,1},{8,12},{9,5},{12,14},{13,9},{14,10},{15,13... | collective-permute-start | bytes 1572872 | tf_op jit(solution)/shard_map/ppermute | solution.py:384
  4.2 15.4 %collective-permute-start.3 = (bf16[128,2048]{1,0:T(8,128)(2,1)}, bf16[128,2048]{1,0:T(8,128)(2,1)S(1)}, u32[]{:S(2)}, u32[]{:S(2)}) collective-permute-start(bf16[128,2048]{1,0:T(8,128)(2,1)} %refs_2_.1), channel_id=1, source_target_pairs={{0,4},{1,3},{4,8},{5,1},{8,12},{9,5},{12,14},{13,9},{14,10},{15,13... | collective-permute-start | bytes 1572872 | tf_op jit(solution)/shard_map/ppermute | solution.py:384
  5.8 0.7 copy-start.4
  6.5 0.7 copy-start.6
  7.2 0.7 copy-start.7
  8.0 20.4 %collective-permute-start.4 = (bf16[256,2048]{1,0:T(8,128)(2,1)S(1)}, bf16[256,2048]{1,0:T(8,128)(2,1)S(1)}, u32[]{:S(2)}, u32[]{:S(2)}) collective-permute-start(bf16[256,2048]{1,0:T(8,128)(2,1)S(1)} %shard_map.114.refs_3_), channel_id=1, source_target_pairs={{0,4},{1,3},{4,8},{5,1},{8,12},{9,5},{12,14},{13,9},{14,10},{15,13... | collective-permute-start | bytes 3145736 | tf_op jit(solution)/shard_map/ppermute | solution.py:384
  9.6 1.0 %copy-start = (bf16[128,2048]{1,0:T(8,128)(2,1)S(1)}, bf16[128,2048]{1,0:T(8,128)(2,1)}, u32[]{:S(2)}) copy-start(bf16[128,2048]{1,0:T(8,128)(2,1)} %refs_1_.1) | copy-start | bytes 1572868
  10.6 1.0 %copy-start.1 = (bf16[128,2048]{1,0:T(8,128)(2,1)S(1)}, bf16[128,2048]{1,0:T(8,128)(2,1)}, u32[]{:S(2)}) copy-start(bf16[128,2048]{1,0:T(8,128)(2,1)} %refs_2_.1) | copy-start | bytes 1572868
  11.7 0.9 copy-start.2
  12.6 0.9 copy-start.3
  19.7 10.8 %collective-permute-start.5 = (bf16[256,2048]{1,0:T(8,128)(2,1)S(1)}, bf16[256,2048]{1,0:T(8,128)(2,1)S(1)}, u32[]{:S(2)}, u32[]{:S(2)}) collective-permute-start(bf16[256,2048]{1,0:T(8,128)(2,1)S(1)} %shard_map.116.refs_3_), channel_id=1, source_target_pairs={{0,1},{1,0},{2,3},{3,2},{4,5},{5,4},{6,7},{7,6},{8,9},{9,8},{10,11... | collective-permute-start | bytes 3145736 | tf_op jit(solution)/shard_map/ppermute | solution.py:387
  19.8 19.8 %collective-permute-start.6 = (bf16[256,2048]{1,0:T(8,128)(2,1)S(1)}, bf16[256,2048]{1,0:T(8,128)(2,1)S(1)}, u32[]{:S(2)}, u32[]{:S(2)}) collective-permute-start(bf16[256,2048]{1,0:T(8,128)(2,1)S(1)} %shard_map.116.refs_3_), channel_id=1, source_target_pairs={{0,4},{1,3},{4,8},{5,1},{8,12},{9,5},{12,14},{13,9},{14,10},{15,13... | collective-permute-start | bytes 3145736 | tf_op jit(solution)/shard_map/ppermute | solution.py:384
  28.4 13.4 %collective-permute-start.7 = (bf16[256,2048]{1,0:T(8,128)(2,1)S(1)}, bf16[256,2048]{1,0:T(8,128)(2,1)S(1)}, u32[]{:S(2)}, u32[]{:S(2)}) collective-permute-start(bf16[256,2048]{1,0:T(8,128)(2,1)S(1)} %collective-permute-done.4.refs_1_), channel_id=1, source_target_pairs={{0,1},{1,0},{2,3},{3,2},{4,5},{5,4},{6,7},{7,6},{8,9},{9,8},{10,11... | collective-permute-start | bytes 3145736 | tf_op jit(solution)/shard_map/ppermute | solution.py:387
  28.4 22.5 %collective-permute-start.8 = (bf16[256,2048]{1,0:T(8,128)(2,1)S(1)}, bf16[256,2048]{1,0:T(8,128)(2,1)S(1)}, u32[]{:S(2)}, u32[]{:S(2)}) collective-permute-start(bf16[256,2048]{1,0:T(8,128)(2,1)S(1)} %collective-permute-done.4.refs_1_), channel_id=1, source_target_pairs={{0,4},{1,3},{4,8},{5,1},{8,12},{9,5},{12,14},{13,9},{14,10},{15,13... | collective-permute-start | bytes 3145736 | tf_op jit(solution)/shard_map/ppermute | solution.py:384
  39.6 13.4 %collective-permute-start.9 = (bf16[256,2048]{1,0:T(8,128)(2,1)S(1)}, bf16[256,2048]{1,0:T(8,128)(2,1)S(1)}, u32[]{:S(2)}, u32[]{:S(2)}) collective-permute-start(bf16[256,2048]{1,0:T(8,128)(2,1)S(1)} %collective-permute-done.6.refs_1_), channel_id=1, source_target_pairs={{0,1},{1,0},{2,3},{3,2},{4,5},{5,4},{6,7},{7,6},{8,9},{9,8},{10,11... | collective-permute-start | bytes 3145736 | tf_op jit(solution)/shard_map/ppermute | solution.py:387
  39.6 22.5 %collective-permute-start.10 = (bf16[256,2048]{1,0:T(8,128)(2,1)S(1)}, bf16[256,2048]{1,0:T(8,128)(2,1)S(1)}, u32[]{:S(2)}, u32[]{:S(2)}) collective-permute-start(bf16[256,2048]{1,0:T(8,128)(2,1)S(1)} %collective-permute-done.6.refs_1_), channel_id=1, source_target_pairs={{0,4},{1,3},{4,8},{5,1},{8,12},{9,5},{12,14},{13,9},{14,10},{15,13... | collective-permute-start | bytes 3145736 | tf_op jit(solution)/shard_map/ppermute | solution.py:384
  50.8 15.1 %collective-permute-start.11 = (bf16[256,2048]{1,0:T(8,128)(2,1)S(1)}, bf16[256,2048]{1,0:T(8,128)(2,1)S(1)}, u32[]{:S(2)}, u32[]{:S(2)}) collective-permute-start(bf16[256,2048]{1,0:T(8,128)(2,1)S(1)} %collective-permute-done.8.refs_1_), channel_id=1, source_target_pairs={{0,1},{1,0},{2,3},{3,2},{4,5},{5,4},{6,7},{7,6},{8,9},{9,8},{10,11... | collective-permute-start | bytes 3145736 | tf_op jit(solution)/shard_map/ppermute | solution.py:387
  50.8 22.5 %collective-permute-start.12 = (bf16[256,2048]{1,0:T(8,128)(2,1)S(1)}, bf16[256,2048]{1,0:T(8,128)(2,1)S(1)}, u32[]{:S(2)}, u32[]{:S(2)}) collective-permute-start(bf16[256,2048]{1,0:T(8,128)(2,1)S(1)} %collective-permute-done.8.refs_1_), channel_id=1, source_target_pairs={{0,4},{1,3},{4,8},{5,1},{8,12},{9,5},{12,14},{13,9},{14,10},{15,13... | collective-permute-start | bytes 3145736 | tf_op jit(solution)/shard_map/ppermute | solution.py:384
  62.1 13.6 %collective-permute-start.13 = (bf16[256,2048]{1,0:T(8,128)(2,1)S(1)}, bf16[256,2048]{1,0:T(8,128)(2,1)S(1)}, u32[]{:S(2)}, u32[]{:S(2)}) collective-permute-start(bf16[256,2048]{1,0:T(8,128)(2,1)S(1)} %collective-permute-done.10.refs_1_.block), channel_id=1, source_target_pairs={{0,1},{1,0},{2,3},{3,2},{4,5},{5,4},{6,7},{7,6},{8,9},{9,8},{10,11... | collective-permute-start | bytes 3145736 | tf_op jit(solution)/shard_map/ppermute | solution.py:387
  62.1 16.5 %collective-permute-start.14 = (bf16[64,2048]{1,0:T(8,128)(2,1)S(1)}, bf16[64,2048]{1,0:T(8,128)(2,1)S(1)}, u32[]{:S(2)}, u32[]{:S(2)}) collective-permute-start(bf16[64,2048]{1,0:T(8,128)(2,1)S(1)} %get-tuple-element.79), channel_id=1, source_target_pairs={{0,4},{1,3},{4,8},{5,1},{8,12},{9,5},{12,14},{13,9},{14,10},{15,13... | collective-permute-start | bytes 786440 | tf_op jit(solution)/shard_map/ppermute | solution.py:384
  64.3 14.6 %collective-permute-start.15 = (bf16[64,2048]{1,0:T(8,128)(2,1)S(1)}, bf16[64,2048]{1,0:T(8,128)(2,1)S(1)}, u32[]{:S(2)}, u32[]{:S(2)}) collective-permute-start(bf16[64,2048]{1,0:T(8,128)(2,1)S(1)} %get-tuple-element.80), channel_id=1, source_target_pairs={{0,4},{1,3},{4,8},{5,1},{8,12},{9,5},{12,14},{13,9},{14,10},{15,13... | collective-permute-start | bytes 786440 | tf_op jit(solution)/shard_map/ppermute | solution.py:384
  73.4 7.5 %collective-permute-start.17 = (bf16[128,2048]{1,0:T(8,128)(2,1)S(1)}, bf16[128,2048]{1,0:T(8,128)(2,1)S(1)}, u32[]{:S(2)}, u32[]{:S(2)}) collective-permute-start(bf16[128,2048]{1,0:T(8,128)(2,1)S(1)} %get-tuple-element.83), channel_id=1, source_target_pairs={{0,1},{1,0},{2,3},{3,2},{4,5},{5,4},{6,7},{7,6},{8,9},{9,8},{10,11... | collective-permute-start | bytes 1572872 | tf_op jit(solution)/shard_map/ppermute | solution.py:387
  73.5 11.1 %collective-permute-start.20 = (bf16[128,2048]{1,0:T(8,128)(2,1)S(1)}, bf16[128,2048]{1,0:T(8,128)(2,1)S(1)}, u32[]{:S(2)}, u32[]{:S(2)}) collective-permute-start(bf16[128,2048]{1,0:T(8,128)(2,1)S(1)} %get-tuple-element.88), channel_id=1, source_target_pairs={{0,4},{1,3},{4,8},{5,1},{8,12},{9,5},{12,14},{13,9},{14,10},{15,13... | collective-permute-start | bytes 1572872 | tf_op jit(solution)/shard_map/ppermute | solution.py:384
  78.9 1.5 %collective-permute-start.18 = (bf16[64,2048]{1,0:T(8,128)(2,1)S(1)}, bf16[64,2048]{1,0:T(8,128)(2,1)S(1)}, u32[]{:S(2)}, u32[]{:S(2)}) collective-permute-start(bf16[64,2048]{1,0:T(8,128)(2,1)S(1)} %collective-permute-done.14.refs_1_), channel_id=1, source_target_pairs={{0,1},{1,0},{2,3},{3,2},{4,5},{5,4},{6,7},{7,6},{8,9},{9,8},{10,11... | collective-permute-start | bytes 786440 | tf_op jit(solution)/shard_map/ppermute | solution.py:387
  78.9 1.9 %collective-permute-start.19 = (bf16[64,2048]{1,0:T(8,128)(2,1)S(1)}, bf16[64,2048]{1,0:T(8,128)(2,1)S(1)}, u32[]{:S(2)}, u32[]{:S(2)}) collective-permute-start(bf16[64,2048]{1,0:T(8,128)(2,1)S(1)} %collective-permute-done.15.refs_2_), channel_id=1, source_target_pairs={{0,1},{1,0},{2,3},{3,2},{4,5},{5,4},{6,7},{7,6},{8,9},{9,8},{10,11... | collective-permute-start | bytes 786440 | tf_op jit(solution)/shard_map/ppermute | solution.py:387
  79.4 5.1 %collective-permute-start.16 = (bf16[128,2048]{1,0:T(8,128)(2,1)S(1)}, bf16[128,2048]{1,0:T(8,128)(2,1)S(1)}, u32[]{:S(2)}, u32[]{:S(2)}) collective-permute-start(bf16[128,2048]{1,0:T(8,128)(2,1)S(1)} %get-tuple-element.82), channel_id=1, source_target_pairs={{0,1},{1,0},{2,3},{3,2},{4,5},{5,4},{6,7},{7,6},{8,9},{9,8},{10,11... | collective-permute-start | bytes 1572872 | tf_op jit(solution)/shard_map/ppermute | solution.py:387
  84.5 15.1 %copy-start.5 = (s32[128,8]{0,1:T(8,128)S(1)}, s32[128,8]{0,1:T(8,128)}, u32[]{:S(2)}) copy-start(s32[128,8]{0,1:T(8,128)} %param.12) | copy-start | bytes 12292
  84.5 1.9 %collective-permute-start.21 = (bf16[128,2048]{1,0:T(8,128)(2,1)S(1)}, bf16[128,2048]{1,0:T(8,128)(2,1)S(1)}, u32[]{:S(2)}, u32[]{:S(2)}) collective-permute-start(bf16[128,2048]{1,0:T(8,128)(2,1)S(1)} %collective-permute-done.20.refs_2_), channel_id=1, source_target_pairs={{0,1},{1,0},{2,3},{3,2},{4,5},{5,4},{6,7},{7,6},{8,9},{9,8},{10,11... | collective-permute-start | bytes 1572872 | tf_op jit(solution)/shard_map/ppermute | solution.py:387

commit v18 on v16

--- a/solution.py
+++ b/solution.py
@@ -123,7 +123,7 @@
         total = jnp.sum(
             jnp.transpose(grad_sum[i * rows : (i + 1) * rows, :]), axis=0, keepdims=True
         )
-        sheet[block_owner(names[i], sheet.shape[0] // 2), 0:1, :] = total
+        sheet[block_owner(names[i], sheet.shape[0] // 2), :, : total.shape[1]] = total
 
 
 def work(names, sheet, block_in, weights, apart=(), load=0):
@@ -233,9 +233,8 @@
 
 
 def enter(sheet, name, total):
-    sheet[block_owner(name, sheet.shape[0] // 2), 0:1, :] = jnp.sum(
-        jnp.transpose(total), axis=0, keepdims=True
-    )
+    line = jnp.sum(jnp.transpose(total), axis=0, keepdims=True)
+    sheet[block_owner(name, sheet.shape[0] // 2), :, : line.shape[1]] = line
 
 
 def out_kernel(names, *refs):
@@ -291,19 +290,20 @@
 def outcome_kernel(jobs, returned, routes, *refs):
     low_in, proj_in = refs[: len(jobs)], refs[len(jobs) : 2 * len(jobs)]
     feat, route_grad = refs[-2:]
-    rows = returned.shape[2]
-    width, rank = low_in[0].shape[0], proj_in[0].shape[0]
-    doc_of = lax.broadcasted_iota(jnp.int32, (width, rows), 0) // rank
+    rows = returned.shape[2] // 3
+    rank = proj_in[0].shape[0]
+    docs = feat.shape[0] // rank
     spread, high_side = [], []
     for names, low_side, proj_cot in zip(jobs, low_in, proj_in):
         for i, name in enumerate(names):
             place = slice(i * rows, (i + 1) * rows)
             owner = block_owner(name, returned.shape[0] // 2)
-            weight = returned[owner, 1:2, :]
-            doc = returned[owner, 2:3, :].astype(jnp.int32)
+            weight = returned[owner, :, rows : 2 * rows]
+            doc = returned[owner, :, 2 * rows :].astype(jnp.int32)
             high_side.append((weight * proj_cot[:, place]).astype(jnp.bfloat16))
             low = low_side[:, place].astype(jnp.float32)
-            spread.append(jnp.where(doc == doc_of, low, 0.0).astype(jnp.bfloat16))
+            parts = [jnp.where(doc == d, low, 0.0) for d in range(docs)]
+            spread.append(jnp.concatenate(parts, axis=0).astype(jnp.bfloat16))
     feat[...] = lax.dot_general(
         jnp.concatenate(spread, axis=1),
         jnp.concatenate(high_side, axis=1),
@@ -312,21 +312,20 @@
     )
     picked = jnp.zeros(route_grad.shape, jnp.float32)
     for e in range(returned.shape[0]):
-        picked = jnp.where(routes[...] == e, returned[e, 0:1, :], picked)
+        picked = jnp.where(routes[...] == e, returned[e, :, :rows], picked)
     route_grad[...] = picked
 
 
 def facts_kernel(routes, combine, doc_ids, out):
-    groups, lines, rows = out.shape
+    groups, rows = out.shape[0], routes.shape[1]
     expert = lax.broadcasted_iota(jnp.int32, (groups, rows), 0)
     weight = jnp.zeros((groups, rows), jnp.float32)
     for k in range(routes.shape[0]):
         share = combine[k : k + 1, :].astype(jnp.float32)
         weight += jnp.where(routes[k : k + 1, :] == expert, share, 0.0)
-    line = lax.broadcasted_iota(jnp.int32, (lines, rows), 0)
     doc = doc_ids[...].astype(jnp.float32)
     for e in range(groups):
-        out[e] = jnp.where(line == 1, weight[e : e + 1, :], doc)
+        out[e] = jnp.concatenate([doc, weight[e : e + 1, :], doc], axis=1)
 
 
 def stack_kernel(top, bottom, out):
@@ -400,7 +399,7 @@
 
     sheet = pl.pallas_call(
         facts_kernel,
-        out_shape=jax.ShapeDtypeStruct((groups, 4, tok_rows), jnp.float32),
+        out_shape=jax.ShapeDtypeStruct((groups, 1, 3 * tok_rows), jnp.float32),
         in_specs=[pl.BlockSpec(memory_space=pltpu.VMEM)] * 3,
         out_specs=pl.BlockSpec(memory_space=pltpu.VMEM),
         compiler_params=pltpu.CompilerParams(vmem_limit_bytes=8 * 1024 * 1024),
@@ -421,7 +420,7 @@
         blocks = [held[name] for name in names if name in held]
         if weights is None:
             sheet, low_side, proj_cot, *weights = work(
-                names, sheet, blocks, given, apart=(tokens, cotangent), load=docs_count
+                names, sheet, blocks, given, apart=(tokens, cotangent), load=1
             )
         else:
             sheet, low_side, proj_cot = work(names, sheet, blocks, weights)

time: 101 us -> 101 us (level)
  waiting for transfers between devices: 28.4 us -> 30.3 us
  Pallas kernels: 31.1 us -> 29.5 us
    ppermute x10, waiting for transfers between devices: 26.9 us -> 28.8 us  [hop(): return lax.ppermute(block, 'exp', onward)]
    pallas_call x6, Pallas kernels: 24.5 us -> 23 us  [work(): return call(sheet, *apart, *block_in, *weights)]
  transfers between devices with their start and end apart: 22 -> 22, of which waited for: 9 -> 10; matrix products, arithmetic and copies ran while one was open for 0% -> 0% of each run, Pallas kernels for 29% -> 28%
where the time goes in v18:
time: 101 us
  waiting for transfers between devices  30.3 us (30%)
  Pallas kernels  29.5 us (29%)
  starting transfers between devices  21.2 us (21%)
  blocking collectives  12.8 us (13%)
  local copies, waits for them, and re-layouts  5.95 us (6%)
    ppermute x10, waiting for transfers between devices, hop(): return lax.ppermute(block, 'exp', onward)  28.8 us
    pallas_call x6, Pallas kernels, work(): return call(sheet, *apart, *block_in, *weights)  23 us
    ppermute x10, starting transfers between devices, hop(): return lax.ppermute(block, 'exp', onward)  20 us
    all_to_all x1, blocking collectives, by_ring(): lax.all_to_all(sheet, 'exp', split_axis=0, concat_axis=0, tiled=True)  12.8 us
    unnamed x16, local copies, waits for them, and re-layouts  5.95 us
    pallas_call x1, Pallas kernels, front(): pl.pallas_call(front_kernel, out_shape=[jax.ShapeDtypeStruct((rows, units...  3.09 us
    pallas_call x2, Pallas kernels, on_core(): pl.pallas_call(kernel, out_shape=[jax.ShapeDtypeStruct(shape, jnp.float32...  2.08 us
  transfers between devices with their start and end apart: 22, of which 10 were waited for; matrix products, arithmetic and copies ran while one was open for 0% of the time, Pallas kernels for 28%

profile of v18, /device:TPU:0, one launch (start us, length us, event | category | flops | bytes accessed | tf_op | source)
XLA Modules:
  0.0 100.7 jit_solution(13333264010106540579)
XLA Ops:
  0.6 0.5 collective-permute-start
  1.1 0.1 collective-permute-start.1
  1.2 3.0 %collective-permute-start.2 = (bf16[128,2048]{1,0:T(8,128)(2,1)}, bf16[128,2048]{1,0:T(8,128)(2,1)S(1)}, u32[]{:S(2)}, u32[]{:S(2)}) collective-permute-start(bf16[128,2048]{1,0:T(8,128)(2,1)} %refs_1_.1), channel_id=1, source_target_pairs={{0,4},{1,3},{4,8},{5,1},{8,12},{9,5},{12,14},{13,9},{14,10},{15,13... | collective-permute-start | bytes 1572872 | tf_op jit(solution)/shard_map/ppermute | solution.py:382
  4.2 1.6 %collective-permute-start.3 = (bf16[128,2048]{1,0:T(8,128)(2,1)}, bf16[128,2048]{1,0:T(8,128)(2,1)S(1)}, u32[]{:S(2)}, u32[]{:S(2)}) collective-permute-start(bf16[128,2048]{1,0:T(8,128)(2,1)} %refs_2_.1), channel_id=1, source_target_pairs={{0,4},{1,3},{4,8},{5,1},{8,12},{9,5},{12,14},{13,9},{14,10},{15,13... | collective-permute-start | bytes 1572872 | tf_op jit(solution)/shard_map/ppermute | solution.py:382
  5.8 0.7 copy-done.4
  6.5 0.7 copy-done.6
  7.2 0.7 copy-done.7
  7.9 0.1 shard_map.114.refs_3_
  8.0 1.6 %collective-permute-start.4 = (bf16[256,2048]{1,0:T(8,128)(2,1)S(1)}, bf16[256,2048]{1,0:T(8,128)(2,1)S(1)}, u32[]{:S(2)}, u32[]{:S(2)}) collective-permute-start(bf16[256,2048]{1,0:T(8,128)(2,1)S(1)} %shard_map.114.refs_3_), channel_id=1, source_target_pairs={{0,4},{1,3},{4,8},{5,1},{8,12},{9,5},{12,14},{13,9},{14,10},{15,13... | collective-permute-start | bytes 3145736 | tf_op jit(solution)/shard_map/ppermute | solution.py:382
  9.6 1.0 %copy-done = bf16[128,2048]{1,0:T(8,128)(2,1)S(1)} copy-done((bf16[128,2048]{1,0:T(8,128)(2,1)S(1)}, bf16[128,2048]{1,0:T(8,128)(2,1)}, u32[]{:S(2)}) %copy-start) | copy-done | bytes 524312
  10.6 1.0 %copy-done.1 = bf16[128,2048]{1,0:T(8,128)(2,1)S(1)} copy-done((bf16[128,2048]{1,0:T(8,128)(2,1)S(1)}, bf16[128,2048]{1,0:T(8,128)(2,1)}, u32[]{:S(2)}) %copy-start.1) | copy-done | bytes 524312
  11.7 0.9 copy-done.2
  12.6 0.9 copy-done.3
  13.5 6.1 %shard_map.115 = (f32[16,1,384]{2,1,0:T(1,128)S(1)}, bf16[64,256]{1,0:T(8,128)(2,1)S(1)}, f32[64,256]{1,0:T(8,128)S(1)}, bf16[2048,768]{1,0:T(8,128)(2,1)S(1)}, ...) custom-call(f32[16,1,384]{2,1,0:T(1,128)S(1)} %shard_map.113.refs_0_, ...), custom_call_target="tpu_custom_call" | custom-call | flops 2415919104 | bytes 2097152 | tf_op jit(solution)/shard_map/pallas_call | solution.py:170
  19.6 0.1 shard_map.116.refs_3_
  19.7 0.1 collective-permute-start.5
  19.8 1.5 %collective-permute-start.6 = (bf16[256,2048]{1,0:T(8,128)(2,1)S(1)}, bf16[256,2048]{1,0:T(8,128)(2,1)S(1)}, u32[]{:S(2)}, u32[]{:S(2)}) collective-permute-start(bf16[256,2048]{1,0:T(8,128)(2,1)S(1)} %shard_map.116.refs_3_), channel_id=1, source_target_pairs={{0,4},{1,3},{4,8},{5,1},{8,12},{9,5},{12,14},{13,9},{14,10},{15,13... | collective-permute-start | bytes 3145736 | tf_op jit(solution)/shard_map/ppermute | solution.py:382
  21.3 7.1 %collective-permute-done.4.refs_1_ = bf16[256,2048]{1,0:T(8,128)(2,1)S(1)} collective-permute-done((bf16[256,2048]{1,0:T(8,128)(2,1)S(1)}, bf16[256,2048]{1,0:T(8,128)(2,1)S(1)}, u32[]{:S(2)}, u32[]{:S(2)}) %collective-permute-start.4) | collective-permute-done | bytes 1048608 | tf_op jit(solution)/shard_map/ppermute | solution.py:382
  28.4 2.1 %collective-permute-start.8 = (bf16[256,2048]{1,0:T(8,128)(2,1)S(1)}, bf16[256,2048]{1,0:T(8,128)(2,1)S(1)}, u32[]{:S(2)}, u32[]{:S(2)}) collective-permute-start(bf16[256,2048]{1,0:T(8,128)(2,1)S(1)} %collective-permute-done.4.refs_1_), channel_id=1, source_target_pairs={{0,4},{1,3},{4,8},{5,1},{8,12},{9,5},{12,14},{13,9},{14,10},{15,13... | collective-permute-start | bytes 3145736 | tf_op jit(solution)/shard_map/ppermute | solution.py:382
  30.5 4.7 %shard_map.117 = (f32[16,1,384]{2,1,0:T(1,128)S(1)}, bf16[64,384]{1,0:T(8,128)(2,1)S(1)}, f32[64,384]{1,0:T(8,128)S(1)}) custom-call(f32[16,1,384]{2,1,0:T(1,128)S(1)} %get-tuple-element.58.refs_0_, bf16[256,2048]{1,0:T(8,128)(2,1)S(1)} %collective-permute-done.4.refs_1_, bf16[256,2048]{1,0:T(8,128)(2,1)S(1)} %collective-permute-done.5.refs_2_, ...), custom_call_target="tpu_custom_call" | custom-call | flops 3623878656 | bytes 3145728 | tf_op jit(solution)/shard_map/pallas_call | solution.py:170
  35.2 4.4 %collective-permute-done.6.refs_1_ = bf16[256,2048]{1,0:T(8,128)(2,1)S(1)} collective-permute-done((bf16[256,2048]{1,0:T(8,128)(2,1)S(1)}, bf16[256,2048]{1,0:T(8,128)(2,1)S(1)}, u32[]{:S(2)}, u32[]{:S(2)}) %collective-permute-start.6) | collective-permute-done | bytes 1048608 | tf_op jit(solution)/shard_map/ppermute | solution.py:382
  39.6 2.1 %collective-permute-start.10 = (bf16[256,2048]{1,0:T(8,128)(2,1)S(1)}, bf16[256,2048]{1,0:T(8,128)(2,1)S(1)}, u32[]{:S(2)}, u32[]{:S(2)}) collective-permute-start(bf16[256,2048]{1,0:T(8,128)(2,1)S(1)} %collective-permute-done.6.refs_1_), channel_id=1, source_target_pairs={{0,4},{1,3},{4,8},{5,1},{8,12},{9,5},{12,14},{13,9},{14,10},{15,13... | collective-permute-start | bytes 3145736 | tf_op jit(solution)/shard_map/ppermute | solution.py:382
  41.7 3.0 %shard_map.118 = (f32[16,1,384]{2,1,0:T(1,128)S(1)}, bf16[64,256]{1,0:T(8,128)(2,1)S(1)}, f32[64,256]{1,0:T(8,128)S(1)}) custom-call(f32[16,1,384]{2,1,0:T(1,128)S(1)} %get-tuple-element.67.refs_0_, bf16[256,2048]{1,0:T(8,128)(2,1)S(1)} %collective-permute-done.6.refs_1_, bf16[256,2048]{1,0:T(8,128)(2,1)S(1)} %collective-permute-done.7.refs_2_, ...), custom_call_target="tpu_custom_call" | custom-call | flops 2415919104 | bytes 2097152 | tf_op jit(solution)/shard_map/pallas_call | solution.py:170
  44.8 6.1 %collective-permute-done.8.refs_1_ = bf16[256,2048]{1,0:T(8,128)(2,1)S(1)} collective-permute-done((bf16[256,2048]{1,0:T(8,128)(2,1)S(1)}, bf16[256,2048]{1,0:T(8,128)(2,1)S(1)}, u32[]{:S(2)}, u32[]{:S(2)}) %collective-permute-start.8) | collective-permute-done | bytes 1048608 | tf_op jit(solution)/shard_map/ppermute | solution.py:382
  50.8 2.1 %collective-permute-start.12 = (bf16[256,2048]{1,0:T(8,128)(2,1)S(1)}, bf16[256,2048]{1,0:T(8,128)(2,1)S(1)}, u32[]{:S(2)}, u32[]{:S(2)}) collective-permute-start(bf16[256,2048]{1,0:T(8,128)(2,1)S(1)} %collective-permute-done.8.refs_1_), channel_id=1, source_target_pairs={{0,4},{1,3},{4,8},{5,1},{8,12},{9,5},{12,14},{13,9},{14,10},{15,13... | collective-permute-start | bytes 3145736 | tf_op jit(solution)/shard_map/ppermute | solution.py:382
  53.0 3.1 %shard_map.119 = (f32[16,1,384]{2,1,0:T(1,128)S(1)}, bf16[64,256]{1,0:T(8,128)(2,1)S(1)}, f32[64,256]{1,0:T(8,128)S(1)}) custom-call(f32[16,1,384]{2,1,0:T(1,128)S(1)} %get-tuple-element.70.refs_0_, bf16[256,2048]{1,0:T(8,128)(2,1)S(1)} %collective-permute-done.8.refs_1_, bf16[256,2048]{1,0:T(8,128)(2,1)S(1)} %collective-permute-done.9.refs_2_, ...), custom_call_target="tpu_custom_call" | custom-call | flops 2415919104 | bytes 2097152 | tf_op jit(solution)/shard_map/pallas_call | solution.py:170
  56.0 6.1 %collective-permute-done.10.refs_1_.block = bf16[256,2048]{1,0:T(8,128)(2,1)S(1)} collective-permute-done((bf16[256,2048]{1,0:T(8,128)(2,1)S(1)}, bf16[256,2048]{1,0:T(8,128)(2,1)S(1)}, u32[]{:S(2)}, u32[]{:S(2)}) %collective-permute-start.10) | collective-permute-done | bytes 1048608 | tf_op jit(solution)/shard_map/ppermute | solution.py:382
  62.1 0.1 shard_map.122
  62.1 2.2 %collective-permute-start.14 = (bf16[64,2048]{1,0:T(8,128)(2,1)S(1)}, bf16[64,2048]{1,0:T(8,128)(2,1)S(1)}, u32[]{:S(2)}, u32[]{:S(2)}) collective-permute-start(bf16[64,2048]{1,0:T(8,128)(2,1)S(1)} %get-tuple-element.79), channel_id=1, source_target_pairs={{0,4},{1,3},{4,8},{5,1},{8,12},{9,5},{12,14},{13,9},{14,10},{15,13... | collective-permute-start | bytes 786440 | tf_op jit(solution)/shard_map/ppermute | solution.py:382
  64.3 1.6 %collective-permute-start.15 = (bf16[64,2048]{1,0:T(8,128)(2,1)S(1)}, bf16[64,2048]{1,0:T(8,128)(2,1)S(1)}, u32[]{:S(2)}, u32[]{:S(2)}) collective-permute-start(bf16[64,2048]{1,0:T(8,128)(2,1)S(1)} %get-tuple-element.80), channel_id=1, source_target_pairs={{0,4},{1,3},{4,8},{5,1},{8,12},{9,5},{12,14},{13,9},{14,10},{15,13... | collective-permute-start | bytes 786440 | tf_op jit(solution)/shard_map/ppermute | solution.py:382
  65.9 3.0 %shard_map.120 = (f32[16,1,384]{2,1,0:T(1,128)S(1)}, bf16[64,256]{1,0:T(8,128)(2,1)S(1)}, f32[64,256]{1,0:T(8,128)S(1)}) custom-call(f32[16,1,384]{2,1,0:T(1,128)S(1)} %get-tuple-element.73.refs_0_, bf16[256,2048]{1,0:T(8,128)(2,1)S(1)} %collective-permute-done.10.refs_1_.block, bf16[256,2048]{1,0:T(8,128)(2,1)S(1)} %collective-permute-done.11.refs_2_, ...), custom_call_target="tpu_custom_call" | custom-call | flops 2415919104 | bytes 2097152 | tf_op jit(solution)/shard_map/pallas_call | solution.py:170
  68.9 4.4 %collective-permute-done.12.refs_1_.block = bf16[256,2048]{1,0:T(8,128)(2,1)S(1)} collective-permute-done((bf16[256,2048]{1,0:T(8,128)(2,1)S(1)}, bf16[256,2048]{1,0:T(8,128)(2,1)S(1)}, u32[]{:S(2)}, u32[]{:S(2)}) %collective-permute-start.12) | collective-permute-done | bytes 1048608 | tf_op jit(solution)/shard_map/ppermute | solution.py:382
  73.3 0.1 shard_map.123
  73.4 0.1 collective-permute-start.17
  73.5 2.2 %collective-permute-start.20 = (bf16[128,2048]{1,0:T(8,128)(2,1)S(1)}, bf16[128,2048]{1,0:T(8,128)(2,1)S(1)}, u32[]{:S(2)}, u32[]{:S(2)}) collective-permute-start(bf16[128,2048]{1,0:T(8,128)(2,1)S(1)} %get-tuple-element.88), channel_id=1, source_target_pairs={{0,4},{1,3},{4,8},{5,1},{8,12},{9,5},{12,14},{13,9},{14,10},{15,13... | collective-permute-start | bytes 1572872 | tf_op jit(solution)/shard_map/ppermute | solution.py:382
  75.6 3.0 %shard_map.121 = (f32[16,1,384]{2,1,0:T(1,128)S(1)}, bf16[64,256]{1,0:T(8,128)(2,1)S(1)}, f32[64,256]{1,0:T(8,128)S(1)}) custom-call(f32[16,1,384]{2,1,0:T(1,128)S(1)} %get-tuple-element.76.refs_0_, bf16[256,2048]{1,0:T(8,128)(2,1)S(1)} %collective-permute-done.12.refs_1_.block, bf16[256,2048]{1,0:T(8,128)(2,1)S(1)} %collective-permute-done.13.refs_2_, ...), custom_call_target="tpu_custom_call" | custom-call | flops 2415919104 | bytes 2097152 | tf_op jit(solution)/shard_map/pallas_call | solution.py:170
  78.7 0.2 collective-permute-done.15.refs_2_
  78.9 0.5 collective-permute-start.19
  79.4 0.0 collective-permute-start.16
  79.4 1.0 %collective-permute-done.18.refs_3_ = bf16[64,2048]{1,0:T(8,128)(2,1)S(1)} collective-permute-done((bf16[64,2048]{1,0:T(8,128)(2,1)S(1)}, bf16[64,2048]{1,0:T(8,128)(2,1)S(1)}, u32[]{:S(2)}, u32[]{:S(2)}) %collective-permute-start.18) | collective-permute-done | bytes 262176 | tf_op jit(solution)/shard_map/ppermute | solution.py:385
  80.5 0.4 collective-permute-done.19.refs_4_
  80.8 3.1 %shard_map.124 = (bf16[384,768]{1,0:T(8,128)(2,1)S(1)}, bf16[64,256]{1,0:T(8,128)(2,1)S(1)}, bf16[64,128]{1,0:T(8,128)(2,1)S(1)}) custom-call(bf16[128,2048]{1,0:T(8,128)(2,1)S(1)} %collective-permute-done.17.refs_0_, bf16[64,2048]{1,0:T(8,128)(2,1)S(1)} %collective-permute-done.14.refs_1_, bf16[64,2048]{1,0:T(8,128)(2,1)S(1)} %collective-permute-done.15.refs_2_, ...), custom_call_target="tpu_custom_call" | custom-call | flops 2415919104 | bytes 1572864 | tf_op jit(solution)/shard_map/pallas_call | solution.py:206
  83.9 0.6 collective-permute-done.20.refs_2_
  84.6 1.8 %shard_map.125 = (f32[16,1,384]{2,1,0:T(1,128)S(1)}, f32[64,256]{1,0:T(8,128)S(1)}, f32[128,2048]{1,0:T(8,128)S(1)}) custom-call(f32[16,1,384]{2,1,0:T(1,128)S(1)} %get-tuple-element.81.refs_0_, bf16[128,2048]{1,0:T(8,128)(2,1)S(1)} %collective-permute-done.16.refs_1_, bf16[128,2048]{1,0:T(8,128)(2,1)S(1)} %collective-permute-done.20.refs_2_, ...), custom_call_target="tpu_custom_call" | custom-call | flops 1207959552 | bytes 1048576 | tf_op jit(solution)/shard_map/pallas_call | solution.py:280
  86.3 0.1 collective-permute-done.21.dy
  86.5 0.3 shard_map.126
  86.8 12.8 %all_to_all.5.returned = f32[16,1,384]{2,1,0:T(1,128)S(1)} all-to-all(f32[16,1,384]{2,1,0:T(1,128)S(1)} %get-tuple-element.93), channel_id=1, replica_groups=mesh['grp'=2,'exp'=16] {'exp'}, dimensions={0} | all-to-all | bytes 49152 | tf_op jit(solution)/shard_map/all_to_all | solution.py:472
  99.6 1.1 %shard_map.127 = (f32[256,64]{1,0:T(8,128)}, f32[8,128]{1,0:T(8,128)}) custom-call(f32[16,1,384]{2,1,0:T(1,128)S(1)} %all_to_all.5.returned, s32[8,128]{1,0:T(8,128)S(1)} %bitcast.19, bf16[64,256]{1,0:T(8,128)(2,1)S(1)} %get-tuple-element.94.refs_0_, bf16[64,384]{1,0:T(8,128)(2,1)S(1)} %get-tuple-element.95.refs_1_, ...), custom_call_target="tpu_custom_call" | custom-call | tf_op jit(solution)/shard_map/pallas_call | solution.py:473
  (28 shorter events, 0.1 us)
Async XLA Ops:
  0.6 7.2 %collective-permute-start = (bf16[128,2048]{1,0:T(8,128)(2,1)}, bf16[128,2048]{1,0:T(8,128)(2,1)S(1)}, u32[]{:S(2)}, u32[]{:S(2)}) collective-permute-start(bf16[128,2048]{1,0:T(8,128)(2,1)} %refs_1_.1), channel_id=1, source_target_pairs={{0,1},{1,0},{2,3},{3,2},{4,5},{5,4},{6,7},{7,6},{8,9},{9,8},{10,11... | collective-permute-start | bytes 1572872 | tf_op jit(solution)/shard_map/ppermute | solution.py:385
  1.1 6.7 %collective-permute-start.1 = (bf16[128,2048]{1,0:T(8,128)(2,1)}, bf16[128,2048]{1,0:T(8,128)(2,1)S(1)}, u32[]{:S(2)}, u32[]{:S(2)}) collective-permute-start(bf16[128,2048]{1,0:T(8,128)(2,1)} %refs_2_.1), channel_id=1, source_target_pairs={{0,1},{1,0},{2,3},{3,2},{4,5},{5,4},{6,7},{7,6},{8,9},{9,8},{10,11... | collective-permute-start | bytes 1572872 | tf_op jit(solution)/shard_map/ppermute | solution.py:385
  1.2 18.4 %collective-permute-start.2 = (bf16[128,2048]{1,0:T(8,128)(2,1)}, bf16[128,2048]{1,0:T(8,128)(2,1)S(1)}, u32[]{:S(2)}, u32[]{:S(2)}) collective-permute-start(bf16[128,2048]{1,0:T(8,128)(2,1)} %refs_1_.1), channel_id=1, source_target_pairs={{0,4},{1,3},{4,8},{5,1},{8,12},{9,5},{12,14},{13,9},{14,10},{15,13... | collective-permute-start | bytes 1572872 | tf_op jit(solution)/shard_map/ppermute | solution.py:382
  4.2 15.4 %collective-permute-start.3 = (bf16[128,2048]{1,0:T(8,128)(2,1)}, bf16[128,2048]{1,0:T(8,128)(2,1)S(1)}, u32[]{:S(2)}, u32[]{:S(2)}) collective-permute-start(bf16[128,2048]{1,0:T(8,128)(2,1)} %refs_2_.1), channel_id=1, source_target_pairs={{0,4},{1,3},{4,8},{5,1},{8,12},{9,5},{12,14},{13,9},{14,10},{15,13... | collective-permute-start | bytes 1572872 | tf_op jit(solution)/shard_map/ppermute | solution.py:382
  5.8 0.7 copy-start.4
  6.5 0.7 copy-start.6
  7.2 0.7 copy-start.7
  8.0 20.4 %collective-permute-start.4 = (bf16[256,2048]{1,0:T(8,128)(2,1)S(1)}, bf16[256,2048]{1,0:T(8,128)(2,1)S(1)}, u32[]{:S(2)}, u32[]{:S(2)}) collective-permute-start(bf16[256,2048]{1,0:T(8,128)(2,1)S(1)} %shard_map.114.refs_3_), channel_id=1, source_target_pairs={{0,4},{1,3},{4,8},{5,1},{8,12},{9,5},{12,14},{13,9},{14,10},{15,13... | collective-permute-start | bytes 3145736 | tf_op jit(solution)/shard_map/ppermute | solution.py:382
  9.6 1.0 %copy-start = (bf16[128,2048]{1,0:T(8,128)(2,1)S(1)}, bf16[128,2048]{1,0:T(8,128)(2,1)}, u32[]{:S(2)}) copy-start(bf16[128,2048]{1,0:T(8,128)(2,1)} %refs_1_.1) | copy-start | bytes 1572868
  10.6 1.0 %copy-start.1 = (bf16[128,2048]{1,0:T(8,128)(2,1)S(1)}, bf16[128,2048]{1,0:T(8,128)(2,1)}, u32[]{:S(2)}) copy-start(bf16[128,2048]{1,0:T(8,128)(2,1)} %refs_2_.1) | copy-start | bytes 1572868
  11.7 0.9 copy-start.2
  12.6 0.9 copy-start.3
  19.7 10.8 %collective-permute-start.5 = (bf16[256,2048]{1,0:T(8,128)(2,1)S(1)}, bf16[256,2048]{1,0:T(8,128)(2,1)S(1)}, u32[]{:S(2)}, u32[]{:S(2)}) collective-permute-start(bf16[256,2048]{1,0:T(8,128)(2,1)S(1)} %shard_map.116.refs_3_), channel_id=1, source_target_pairs={{0,1},{1,0},{2,3},{3,2},{4,5},{5,4},{6,7},{7,6},{8,9},{9,8},{10,11... | collective-permute-start | bytes 3145736 | tf_op jit(solution)/shard_map/ppermute | solution.py:385
  19.8 19.8 %collective-permute-start.6 = (bf16[256,2048]{1,0:T(8,128)(2,1)S(1)}, bf16[256,2048]{1,0:T(8,128)(2,1)S(1)}, u32[]{:S(2)}, u32[]{:S(2)}) collective-permute-start(bf16[256,2048]{1,0:T(8,128)(2,1)S(1)} %shard_map.116.refs_3_), channel_id=1, source_target_pairs={{0,4},{1,3},{4,8},{5,1},{8,12},{9,5},{12,14},{13,9},{14,10},{15,13... | collective-permute-start | bytes 3145736 | tf_op jit(solution)/shard_map/ppermute | solution.py:382
  28.4 13.4 %collective-permute-start.7 = (bf16[256,2048]{1,0:T(8,128)(2,1)S(1)}, bf16[256,2048]{1,0:T(8,128)(2,1)S(1)}, u32[]{:S(2)}, u32[]{:S(2)}) collective-permute-start(bf16[256,2048]{1,0:T(8,128)(2,1)S(1)} %collective-permute-done.4.refs_1_), channel_id=1, source_target_pairs={{0,1},{1,0},{2,3},{3,2},{4,5},{5,4},{6,7},{7,6},{8,9},{9,8},{10,11... | collective-permute-start | bytes 3145736 | tf_op jit(solution)/shard_map/ppermute | solution.py:385
  28.4 22.5 %collective-permute-start.8 = (bf16[256,2048]{1,0:T(8,128)(2,1)S(1)}, bf16[256,2048]{1,0:T(8,128)(2,1)S(1)}, u32[]{:S(2)}, u32[]{:S(2)}) collective-permute-start(bf16[256,2048]{1,0:T(8,128)(2,1)S(1)} %collective-permute-done.4.refs_1_), channel_id=1, source_target_pairs={{0,4},{1,3},{4,8},{5,1},{8,12},{9,5},{12,14},{13,9},{14,10},{15,13... | collective-permute-start | bytes 3145736 | tf_op jit(solution)/shard_map/ppermute | solution.py:382
  39.6 13.4 %collective-permute-start.9 = (bf16[256,2048]{1,0:T(8,128)(2,1)S(1)}, bf16[256,2048]{1,0:T(8,128)(2,1)S(1)}, u32[]{:S(2)}, u32[]{:S(2)}) collective-permute-start(bf16[256,2048]{1,0:T(8,128)(2,1)S(1)} %collective-permute-done.6.refs_1_), channel_id=1, source_target_pairs={{0,1},{1,0},{2,3},{3,2},{4,5},{5,4},{6,7},{7,6},{8,9},{9,8},{10,11... | collective-permute-start | bytes 3145736 | tf_op jit(solution)/shard_map/ppermute | solution.py:385
  39.6 22.5 %collective-permute-start.10 = (bf16[256,2048]{1,0:T(8,128)(2,1)S(1)}, bf16[256,2048]{1,0:T(8,128)(2,1)S(1)}, u32[]{:S(2)}, u32[]{:S(2)}) collective-permute-start(bf16[256,2048]{1,0:T(8,128)(2,1)S(1)} %collective-permute-done.6.refs_1_), channel_id=1, source_target_pairs={{0,4},{1,3},{4,8},{5,1},{8,12},{9,5},{12,14},{13,9},{14,10},{15,13... | collective-permute-start | bytes 3145736 | tf_op jit(solution)/shard_map/ppermute | solution.py:382
  50.8 15.1 %collective-permute-start.11 = (bf16[256,2048]{1,0:T(8,128)(2,1)S(1)}, bf16[256,2048]{1,0:T(8,128)(2,1)S(1)}, u32[]{:S(2)}, u32[]{:S(2)}) collective-permute-start(bf16[256,2048]{1,0:T(8,128)(2,1)S(1)} %collective-permute-done.8.refs_1_), channel_id=1, source_target_pairs={{0,1},{1,0},{2,3},{3,2},{4,5},{5,4},{6,7},{7,6},{8,9},{9,8},{10,11... | collective-permute-start | bytes 3145736 | tf_op jit(solution)/shard_map/ppermute | solution.py:385
  50.8 22.5 %collective-permute-start.12 = (bf16[256,2048]{1,0:T(8,128)(2,1)S(1)}, bf16[256,2048]{1,0:T(8,128)(2,1)S(1)}, u32[]{:S(2)}, u32[]{:S(2)}) collective-permute-start(bf16[256,2048]{1,0:T(8,128)(2,1)S(1)} %collective-permute-done.8.refs_1_), channel_id=1, source_target_pairs={{0,4},{1,3},{4,8},{5,1},{8,12},{9,5},{12,14},{13,9},{14,10},{15,13... | collective-permute-start | bytes 3145736 | tf_op jit(solution)/shard_map/ppermute | solution.py:382
  62.1 13.6 %collective-permute-start.13 = (bf16[256,2048]{1,0:T(8,128)(2,1)S(1)}, bf16[256,2048]{1,0:T(8,128)(2,1)S(1)}, u32[]{:S(2)}, u32[]{:S(2)}) collective-permute-start(bf16[256,2048]{1,0:T(8,128)(2,1)S(1)} %collective-permute-done.10.refs_1_.block), channel_id=1, source_target_pairs={{0,1},{1,0},{2,3},{3,2},{4,5},{5,4},{6,7},{7,6},{8,9},{9,8},{10,11... | collective-permute-start | bytes 3145736 | tf_op jit(solution)/shard_map/ppermute | solution.py:385
  62.1 16.5 %collective-permute-start.14 = (bf16[64,2048]{1,0:T(8,128)(2,1)S(1)}, bf16[64,2048]{1,0:T(8,128)(2,1)S(1)}, u32[]{:S(2)}, u32[]{:S(2)}) collective-permute-start(bf16[64,2048]{1,0:T(8,128)(2,1)S(1)} %get-tuple-element.79), channel_id=1, source_target_pairs={{0,4},{1,3},{4,8},{5,1},{8,12},{9,5},{12,14},{13,9},{14,10},{15,13... | collective-permute-start | bytes 786440 | tf_op jit(solution)/shard_map/ppermute | solution.py:382
  64.3 14.6 %collective-permute-start.15 = (bf16[64,2048]{1,0:T(8,128)(2,1)S(1)}, bf16[64,2048]{1,0:T(8,128)(2,1)S(1)}, u32[]{:S(2)}, u32[]{:S(2)}) collective-permute-start(bf16[64,2048]{1,0:T(8,128)(2,1)S(1)} %get-tuple-element.80), channel_id=1, source_target_pairs={{0,4},{1,3},{4,8},{5,1},{8,12},{9,5},{12,14},{13,9},{14,10},{15,13... | collective-permute-start | bytes 786440 | tf_op jit(solution)/shard_map/ppermute | solution.py:382
  73.4 7.5 %collective-permute-start.17 = (bf16[128,2048]{1,0:T(8,128)(2,1)S(1)}, bf16[128,2048]{1,0:T(8,128)(2,1)S(1)}, u32[]{:S(2)}, u32[]{:S(2)}) collective-permute-start(bf16[128,2048]{1,0:T(8,128)(2,1)S(1)} %get-tuple-element.83), channel_id=1, source_target_pairs={{0,1},{1,0},{2,3},{3,2},{4,5},{5,4},{6,7},{7,6},{8,9},{9,8},{10,11... | collective-permute-start | bytes 1572872 | tf_op jit(solution)/shard_map/ppermute | solution.py:385
  73.5 11.1 %collective-permute-start.20 = (bf16[128,2048]{1,0:T(8,128)(2,1)S(1)}, bf16[128,2048]{1,0:T(8,128)(2,1)S(1)}, u32[]{:S(2)}, u32[]{:S(2)}) collective-permute-start(bf16[128,2048]{1,0:T(8,128)(2,1)S(1)} %get-tuple-element.88), channel_id=1, source_target_pairs={{0,4},{1,3},{4,8},{5,1},{8,12},{9,5},{12,14},{13,9},{14,10},{15,13... | collective-permute-start | bytes 1572872 | tf_op jit(solution)/shard_map/ppermute | solution.py:382
  78.9 1.5 %collective-permute-start.18 = (bf16[64,2048]{1,0:T(8,128)(2,1)S(1)}, bf16[64,2048]{1,0:T(8,128)(2,1)S(1)}, u32[]{:S(2)}, u32[]{:S(2)}) collective-permute-start(bf16[64,2048]{1,0:T(8,128)(2,1)S(1)} %collective-permute-done.14.refs_1_), channel_id=1, source_target_pairs={{0,1},{1,0},{2,3},{3,2},{4,5},{5,4},{6,7},{7,6},{8,9},{9,8},{10,11... | collective-permute-start | bytes 786440 | tf_op jit(solution)/shard_map/ppermute | solution.py:385
  78.9 1.9 %collective-permute-start.19 = (bf16[64,2048]{1,0:T(8,128)(2,1)S(1)}, bf16[64,2048]{1,0:T(8,128)(2,1)S(1)}, u32[]{:S(2)}, u32[]{:S(2)}) collective-permute-start(bf16[64,2048]{1,0:T(8,128)(2,1)S(1)} %collective-permute-done.15.refs_2_), channel_id=1, source_target_pairs={{0,1},{1,0},{2,3},{3,2},{4,5},{5,4},{6,7},{7,6},{8,9},{9,8},{10,11... | collective-permute-start | bytes 786440 | tf_op jit(solution)/shard_map/ppermute | solution.py:385
  79.4 5.1 %collective-permute-start.16 = (bf16[128,2048]{1,0:T(8,128)(2,1)S(1)}, bf16[128,2048]{1,0:T(8,128)(2,1)S(1)}, u32[]{:S(2)}, u32[]{:S(2)}) collective-permute-start(bf16[128,2048]{1,0:T(8,128)(2,1)S(1)} %get-tuple-element.82), channel_id=1, source_target_pairs={{0,1},{1,0},{2,3},{3,2},{4,5},{5,4},{6,7},{7,6},{8,9},{9,8},{10,11... | collective-permute-start | bytes 1572872 | tf_op jit(solution)/shard_map/ppermute | solution.py:385
  84.5 15.1 %copy-start.5 = (s32[128,8]{0,1:T(8,128)S(1)}, s32[128,8]{0,1:T(8,128)}, u32[]{:S(2)}) copy-start(s32[128,8]{0,1:T(8,128)} %param.12) | copy-start | bytes 12292
  84.5 1.9 %collective-permute-start.21 = (bf16[128,2048]{1,0:T(8,128)(2,1)S(1)}, bf16[128,2048]{1,0:T(8,128)(2,1)S(1)}, u32[]{:S(2)}, u32[]{:S(2)}) collective-permute-start(bf16[128,2048]{1,0:T(8,128)(2,1)S(1)} %collective-permute-done.20.refs_2_), channel_id=1, source_target_pairs={{0,1},{1,0},{2,3},{3,2},{4,5},{5,4},{6,7},{7,6},{8,9},{9,8},{10,11... | collective-permute-start | bytes 1572872 | tf_op jit(solution)/shard_map/ppermute | solution.py:385

commit v19 on v18

--- a/solution.py
+++ b/solution.py
@@ -170,14 +170,11 @@
     return call(sheet, *apart, *block_in, *weights)
 
 
-def front_kernel(*refs):
-    blocks = len(refs) - 8
-    x_in = refs[:blocks]
-    w_gate, w_up, low_proj, hidden, low_first, low_last, x_all, low_sum = refs[blocks:]
-    begin = 0
+def front_kernel(begin, x_in, w_gate, w_up, low_proj, hidden, low_side, x_all, low_sum):
+    rows = 0
     for x in x_in:
-        x_all[begin : begin + x.shape[0], :] = x[...]
-        begin += x.shape[0]
+        x_all[rows : rows + x.shape[0], :] = x[...]
+        rows += x.shape[0]
     units = w_gate.shape[1]
     tile = 256 if units % 256 == 0 else units
     for cut in range(0, units, tile):
@@ -185,7 +182,7 @@
         gate_val = jnp.dot(x_all[...], w_gate[:, part], preferred_element_type=jnp.float32)
         up_val = jnp.dot(x_all[...], w_up[:, part], preferred_element_type=jnp.float32)
         piece = (jax.nn.silu(gate_val) * up_val).astype(jnp.bfloat16)
-        hidden[:, part] = piece
+        hidden[begin : begin + rows, part] = piece
         low = lax.dot_general(
             low_proj[:, part],
             piece,
@@ -193,36 +190,35 @@
             preferred_element_type=jnp.float32,
         )
         low_sum[...] = low if cut == 0 else low_sum[...] + low
-    cut = low_first.shape[1]
-    low_first[...] = low_sum[:, :cut].astype(low_first.dtype)
-    low_last[...] = low_sum[:, cut:].astype(low_last.dtype)
-
-
-def front(x_in, weights, last):
+    low_side[...] = low_sum[...].astype(low_side.dtype)
+
+
+def front(x_in, weights, begin, room, held=()):
     w_gate, w_up, _, low_proj, _ = weights
     rows, width = sum(x.shape[0] for x in x_in), x_in[0].shape[1]
     units = w_gate.shape[1]
     inside = pl.BlockSpec(memory_space=pltpu.VMEM)
+    count = len(x_in)
+
+    def kernel(*refs):
+        front_kernel(begin, refs[:count], *refs[count : count + 3], *refs[-4:])
+
     return pl.pallas_call(
-        front_kernel,
+        kernel,
         out_shape=[
-            jax.ShapeDtypeStruct((rows, units), jnp.bfloat16),
-            jax.ShapeDtypeStruct((low_proj.shape[0], rows - last), jnp.bfloat16),
-            jax.ShapeDtypeStruct((low_proj.shape[0], last), jnp.bfloat16),
+            jax.ShapeDtypeStruct((room, units), jnp.bfloat16),
+            jax.ShapeDtypeStruct((low_proj.shape[0], rows), jnp.bfloat16),
         ],
-        in_specs=[inside] * (len(x_in) + 3),
-        out_specs=[inside] * 3,
+        in_specs=[inside] * (count + 3 + len(held)),
+        out_specs=[inside] * 2,
+        input_output_aliases={count + 3: 0} if held else {},
         scratch_shapes=[
             pltpu.VMEM((rows, width), jnp.bfloat16),
             pltpu.VMEM((low_proj.shape[0], rows), jnp.float32),
         ],
         compiler_params=pltpu.CompilerParams(vmem_limit_bytes=16 * 1024 * 1024),
-        cost_estimate=pl.CostEstimate(
-            flops=4 * rows * width * units,
-            bytes_accessed=2 * rows * width,
-            transcendentals=rows * units,
-        ),
-    )(*x_in, w_gate, w_up, low_proj)
+        cost_estimate=pl.CostEstimate(flops=0, bytes_accessed=0, transcendentals=0),
+    )(*x_in, w_gate, w_up, low_proj, *held)
 
 
 def fold(product):
@@ -447,9 +443,9 @@
     x_before, dy_before = [swap(part) for part in x_before], swap(dy_before)
     take()
     sheet, x = lax.optimization_barrier((sheet, x))
-    hidden, low_first, low_last = front(
-        x_before + x + [swap(part) for part in x], weights, tok_rows
-    )
+    x_beside = [swap(part) for part in x]
+    hidden, low_first = front(x_before + x, weights, 0, 3 * tok_rows)
+    hidden, low_last = front(x_beside, weights, 2 * tok_rows, 3 * tok_rows, (hidden,))
     hidden, dy = lax.optimization_barrier((hidden, dy))
     dy_beside = swap(dy)
     rank = proj_output.shape[2]

time: 101 us -> 101 us (level)
    ppermute x12, waiting for transfers between devices: 1.56 us -> 0.2 us  [swap(): return lax.ppermute(block, 'exp', across)]
    pallas_call x1 -> x2, Pallas kernels: 3.09 us -> 3.75 us  [front(): pl.pallas_call(kernel, out_shape=[jax.ShapeDtypeStruct((room, units), jnp...]
  transfers between devices with their start and end apart: 22 -> 22, of which waited for: 10 -> 7; matrix products, arithmetic and copies ran while one was open for 0% -> 0% of each run, Pallas kernels for 28% -> 29%
where the time goes in v19:
time: 101 us
  Pallas kernels  30.2 us (30%)
  waiting for transfers between devices  29.3 us (29%)
  starting transfers between devices  21.6 us (21%)
  blocking collectives  12.8 us (13%)
  local copies, waits for them, and re-layouts  5.95 us (6%)
    ppermute x10, waiting for transfers between devices, hop(): return lax.ppermute(block, 'exp', onward)  29.1 us
    pallas_call x6, Pallas kernels, work(): return call(sheet, *apart, *block_in, *weights)  23 us
    ppermute x10, starting transfers between devices, hop(): return lax.ppermute(block, 'exp', onward)  20.2 us
    all_to_all x1, blocking collectives, by_ring(): lax.all_to_all(sheet, 'exp', split_axis=0, concat_axis=0, tiled=True)  12.8 us
    unnamed x16, local copies, waits for them, and re-layouts  5.95 us
    pallas_call x2, Pallas kernels, front(): pl.pallas_call(kernel, out_shape=[jax.ShapeDtypeStruct((room, units), jnp...  3.75 us
    pallas_call x2, Pallas kernels, on_core(): pl.pallas_call(kernel, out_shape=[jax.ShapeDtypeStruct(shape, jnp.float32...  2.07 us
  transfers between devices with their start and end apart: 22, of which 7 were waited for; matrix products, arithmetic and copies ran while one was open for 0% of the time, Pallas kernels for 29%

profile of v19, /device:TPU:0, one launch (start us, length us, event | category | flops | bytes accessed | tf_op | source)
XLA Modules:
  0.0 100.7 jit_solution(591176211357313212)
XLA Ops:
  0.6 0.5 collective-permute-start
  1.1 0.1 collective-permute-start.1
  1.2 3.0 %collective-permute-start.2 = (bf16[128,2048]{1,0:T(8,128)(2,1)}, bf16[128,2048]{1,0:T(8,128)(2,1)S(1)}, u32[]{:S(2)}, u32[]{:S(2)}) collective-permute-start(bf16[128,2048]{1,0:T(8,128)(2,1)} %refs_1_.1), channel_id=1, source_target_pairs={{0,4},{1,3},{4,8},{5,1},{8,12},{9,5},{12,14},{13,9},{14,10},{15,13... | collective-permute-start | bytes 1572872 | tf_op jit(solution)/shard_map/ppermute | solution.py:378
  4.2 1.6 %collective-permute-start.3 = (bf16[128,2048]{1,0:T(8,128)(2,1)}, bf16[128,2048]{1,0:T(8,128)(2,1)S(1)}, u32[]{:S(2)}, u32[]{:S(2)}) collective-permute-start(bf16[128,2048]{1,0:T(8,128)(2,1)} %refs_2_.1), channel_id=1, source_target_pairs={{0,4},{1,3},{4,8},{5,1},{8,12},{9,5},{12,14},{13,9},{14,10},{15,13... | collective-permute-start | bytes 1572872 | tf_op jit(solution)/shard_map/ppermute | solution.py:378
  5.8 0.7 copy-done.4
  6.5 0.7 copy-done.6
  7.2 0.7 copy-done.7
  7.9 0.1 shard_map.114.refs_3_
  8.0 1.6 %collective-permute-start.4 = (bf16[256,2048]{1,0:T(8,128)(2,1)S(1)}, bf16[256,2048]{1,0:T(8,128)(2,1)S(1)}, u32[]{:S(2)}, u32[]{:S(2)}) collective-permute-start(bf16[256,2048]{1,0:T(8,128)(2,1)S(1)} %shard_map.114.refs_3_), channel_id=1, source_target_pairs={{0,4},{1,3},{4,8},{5,1},{8,12},{9,5},{12,14},{13,9},{14,10},{15,13... | collective-permute-start | bytes 3145736 | tf_op jit(solution)/shard_map/ppermute | solution.py:378
  9.6 1.0 %copy-done = bf16[128,2048]{1,0:T(8,128)(2,1)S(1)} copy-done((bf16[128,2048]{1,0:T(8,128)(2,1)S(1)}, bf16[128,2048]{1,0:T(8,128)(2,1)}, u32[]{:S(2)}) %copy-start) | copy-done | bytes 524312
  10.6 1.0 %copy-done.1 = bf16[128,2048]{1,0:T(8,128)(2,1)S(1)} copy-done((bf16[128,2048]{1,0:T(8,128)(2,1)S(1)}, bf16[128,2048]{1,0:T(8,128)(2,1)}, u32[]{:S(2)}) %copy-start.1) | copy-done | bytes 524312
  11.7 0.9 copy-done.2
  12.6 0.9 copy-done.3
  13.5 6.1 %shard_map.115 = (f32[16,1,384]{2,1,0:T(1,128)S(1)}, bf16[64,256]{1,0:T(8,128)(2,1)S(1)}, f32[64,256]{1,0:T(8,128)S(1)}, bf16[2048,768]{1,0:T(8,128)(2,1)S(1)}, ...) custom-call(f32[16,1,384]{2,1,0:T(1,128)S(1)} %shard_map.113.refs_0_, ...), custom_call_target="tpu_custom_call" | custom-call | flops 2415919104 | bytes 2097152 | tf_op jit(solution)/shard_map/pallas_call | solution.py:170
  19.6 0.1 shard_map.116.refs_3_
  19.7 0.1 collective-permute-start.5
  19.8 1.5 %collective-permute-start.6 = (bf16[256,2048]{1,0:T(8,128)(2,1)S(1)}, bf16[256,2048]{1,0:T(8,128)(2,1)S(1)}, u32[]{:S(2)}, u32[]{:S(2)}) collective-permute-start(bf16[256,2048]{1,0:T(8,128)(2,1)S(1)} %shard_map.116.refs_3_), channel_id=1, source_target_pairs={{0,4},{1,3},{4,8},{5,1},{8,12},{9,5},{12,14},{13,9},{14,10},{15,13... | collective-permute-start | bytes 3145736 | tf_op jit(solution)/shard_map/ppermute | solution.py:378
  21.3 7.1 %collective-permute-done.4.refs_1_ = bf16[256,2048]{1,0:T(8,128)(2,1)S(1)} collective-permute-done((bf16[256,2048]{1,0:T(8,128)(2,1)S(1)}, bf16[256,2048]{1,0:T(8,128)(2,1)S(1)}, u32[]{:S(2)}, u32[]{:S(2)}) %collective-permute-start.4) | collective-permute-done | bytes 1048608 | tf_op jit(solution)/shard_map/ppermute | solution.py:378
  28.4 2.1 %collective-permute-start.8 = (bf16[256,2048]{1,0:T(8,128)(2,1)S(1)}, bf16[256,2048]{1,0:T(8,128)(2,1)S(1)}, u32[]{:S(2)}, u32[]{:S(2)}) collective-permute-start(bf16[256,2048]{1,0:T(8,128)(2,1)S(1)} %collective-permute-done.4.refs_1_), channel_id=1, source_target_pairs={{0,4},{1,3},{4,8},{5,1},{8,12},{9,5},{12,14},{13,9},{14,10},{15,13... | collective-permute-start | bytes 3145736 | tf_op jit(solution)/shard_map/ppermute | solution.py:378
  30.5 4.7 %shard_map.117 = (f32[16,1,384]{2,1,0:T(1,128)S(1)}, bf16[64,384]{1,0:T(8,128)(2,1)S(1)}, f32[64,384]{1,0:T(8,128)S(1)}) custom-call(f32[16,1,384]{2,1,0:T(1,128)S(1)} %get-tuple-element.59.refs_0_, bf16[256,2048]{1,0:T(8,128)(2,1)S(1)} %collective-permute-done.4.refs_1_, bf16[256,2048]{1,0:T(8,128)(2,1)S(1)} %collective-permute-done.5.refs_2_, ...), custom_call_target="tpu_custom_call" | custom-call | flops 3623878656 | bytes 3145728 | tf_op jit(solution)/shard_map/pallas_call | solution.py:170
  35.2 4.4 %collective-permute-done.6.refs_1_ = bf16[256,2048]{1,0:T(8,128)(2,1)S(1)} collective-permute-done((bf16[256,2048]{1,0:T(8,128)(2,1)S(1)}, bf16[256,2048]{1,0:T(8,128)(2,1)S(1)}, u32[]{:S(2)}, u32[]{:S(2)}) %collective-permute-start.6) | collective-permute-done | bytes 1048608 | tf_op jit(solution)/shard_map/ppermute | solution.py:378
  39.6 2.1 %collective-permute-start.10 = (bf16[256,2048]{1,0:T(8,128)(2,1)S(1)}, bf16[256,2048]{1,0:T(8,128)(2,1)S(1)}, u32[]{:S(2)}, u32[]{:S(2)}) collective-permute-start(bf16[256,2048]{1,0:T(8,128)(2,1)S(1)} %collective-permute-done.6.refs_1_), channel_id=1, source_target_pairs={{0,4},{1,3},{4,8},{5,1},{8,12},{9,5},{12,14},{13,9},{14,10},{15,13... | collective-permute-start | bytes 3145736 | tf_op jit(solution)/shard_map/ppermute | solution.py:378
  41.7 3.0 %shard_map.118 = (f32[16,1,384]{2,1,0:T(1,128)S(1)}, bf16[64,256]{1,0:T(8,128)(2,1)S(1)}, f32[64,256]{1,0:T(8,128)S(1)}) custom-call(f32[16,1,384]{2,1,0:T(1,128)S(1)} %get-tuple-element.68.refs_0_, bf16[256,2048]{1,0:T(8,128)(2,1)S(1)} %collective-permute-done.6.refs_1_, bf16[256,2048]{1,0:T(8,128)(2,1)S(1)} %collective-permute-done.7.refs_2_, ...), custom_call_target="tpu_custom_call" | custom-call | flops 2415919104 | bytes 2097152 | tf_op jit(solution)/shard_map/pallas_call | solution.py:170
  44.8 6.1 %collective-permute-done.8.refs_1_ = bf16[256,2048]{1,0:T(8,128)(2,1)S(1)} collective-permute-done((bf16[256,2048]{1,0:T(8,128)(2,1)S(1)}, bf16[256,2048]{1,0:T(8,128)(2,1)S(1)}, u32[]{:S(2)}, u32[]{:S(2)}) %collective-permute-start.8) | collective-permute-done | bytes 1048608 | tf_op jit(solution)/shard_map/ppermute | solution.py:378
  50.8 2.1 %collective-permute-start.12 = (bf16[256,2048]{1,0:T(8,128)(2,1)S(1)}, bf16[256,2048]{1,0:T(8,128)(2,1)S(1)}, u32[]{:S(2)}, u32[]{:S(2)}) collective-permute-start(bf16[256,2048]{1,0:T(8,128)(2,1)S(1)} %collective-permute-done.8.refs_1_), channel_id=1, source_target_pairs={{0,4},{1,3},{4,8},{5,1},{8,12},{9,5},{12,14},{13,9},{14,10},{15,13... | collective-permute-start | bytes 3145736 | tf_op jit(solution)/shard_map/ppermute | solution.py:378
  53.0 3.1 %shard_map.119 = (f32[16,1,384]{2,1,0:T(1,128)S(1)}, bf16[64,256]{1,0:T(8,128)(2,1)S(1)}, f32[64,256]{1,0:T(8,128)S(1)}) custom-call(f32[16,1,384]{2,1,0:T(1,128)S(1)} %get-tuple-element.71.refs_0_, bf16[256,2048]{1,0:T(8,128)(2,1)S(1)} %collective-permute-done.8.refs_1_, bf16[256,2048]{1,0:T(8,128)(2,1)S(1)} %collective-permute-done.9.refs_2_, ...), custom_call_target="tpu_custom_call" | custom-call | flops 2415919104 | bytes 2097152 | tf_op jit(solution)/shard_map/pallas_call | solution.py:170
  56.0 6.1 %collective-permute-done.10.refs_1_.block = bf16[256,2048]{1,0:T(8,128)(2,1)S(1)} collective-permute-done((bf16[256,2048]{1,0:T(8,128)(2,1)S(1)}, bf16[256,2048]{1,0:T(8,128)(2,1)S(1)}, u32[]{:S(2)}, u32[]{:S(2)}) %collective-permute-start.10) | collective-permute-done | bytes 1048608 | tf_op jit(solution)/shard_map/ppermute | solution.py:378
  62.1 0.1 shard_map.122
  62.1 2.2 %collective-permute-start.14 = (bf16[64,2048]{1,0:T(8,128)(2,1)S(1)}, bf16[64,2048]{1,0:T(8,128)(2,1)S(1)}, u32[]{:S(2)}, u32[]{:S(2)}) collective-permute-start(bf16[64,2048]{1,0:T(8,128)(2,1)S(1)} %get-tuple-element.80), channel_id=1, source_target_pairs={{0,4},{1,3},{4,8},{5,1},{8,12},{9,5},{12,14},{13,9},{14,10},{15,13... | collective-permute-start | bytes 786440 | tf_op jit(solution)/shard_map/ppermute | solution.py:378
  64.3 1.6 %collective-permute-start.15 = (bf16[64,2048]{1,0:T(8,128)(2,1)S(1)}, bf16[64,2048]{1,0:T(8,128)(2,1)S(1)}, u32[]{:S(2)}, u32[]{:S(2)}) collective-permute-start(bf16[64,2048]{1,0:T(8,128)(2,1)S(1)} %get-tuple-element.81), channel_id=1, source_target_pairs={{0,4},{1,3},{4,8},{5,1},{8,12},{9,5},{12,14},{13,9},{14,10},{15,13... | collective-permute-start | bytes 786440 | tf_op jit(solution)/shard_map/ppermute | solution.py:378
  65.9 3.0 %shard_map.120 = (f32[16,1,384]{2,1,0:T(1,128)S(1)}, bf16[64,256]{1,0:T(8,128)(2,1)S(1)}, f32[64,256]{1,0:T(8,128)S(1)}) custom-call(f32[16,1,384]{2,1,0:T(1,128)S(1)} %get-tuple-element.74.refs_0_, bf16[256,2048]{1,0:T(8,128)(2,1)S(1)} %collective-permute-done.10.refs_1_.block, bf16[256,2048]{1,0:T(8,128)(2,1)S(1)} %collective-permute-done.11.refs_2_, ...), custom_call_target="tpu_custom_call" | custom-call | flops 2415919104 | bytes 2097152 | tf_op jit(solution)/shard_map/pallas_call | solution.py:170
  68.9 4.4 %collective-permute-done.12.refs_1_.block = bf16[256,2048]{1,0:T(8,128)(2,1)S(1)} collective-permute-done((bf16[256,2048]{1,0:T(8,128)(2,1)S(1)}, bf16[256,2048]{1,0:T(8,128)(2,1)S(1)}, u32[]{:S(2)}, u32[]{:S(2)}) %collective-permute-start.12) | collective-permute-done | bytes 1048608 | tf_op jit(solution)/shard_map/ppermute | solution.py:378
  73.3 0.1 shard_map.123
  73.4 0.1 collective-permute-start.19
  73.5 2.4 %collective-permute-start.20 = (bf16[128,2048]{1,0:T(8,128)(2,1)S(1)}, bf16[128,2048]{1,0:T(8,128)(2,1)S(1)}, u32[]{:S(2)}, u32[]{:S(2)}) collective-permute-start(bf16[128,2048]{1,0:T(8,128)(2,1)S(1)} %get-tuple-element.90), channel_id=1, source_target_pairs={{0,4},{1,3},{4,8},{5,1},{8,12},{9,5},{12,14},{13,9},{14,10},{15,13... | collective-permute-start | bytes 1572872 | tf_op jit(solution)/shard_map/ppermute | solution.py:378
  75.8 3.1 %shard_map.121 = (f32[16,1,384]{2,1,0:T(1,128)S(1)}, bf16[64,256]{1,0:T(8,128)(2,1)S(1)}, f32[64,256]{1,0:T(8,128)S(1)}) custom-call(f32[16,1,384]{2,1,0:T(1,128)S(1)} %get-tuple-element.77.refs_0_, bf16[256,2048]{1,0:T(8,128)(2,1)S(1)} %collective-permute-done.12.refs_1_.block, bf16[256,2048]{1,0:T(8,128)(2,1)S(1)} %collective-permute-done.13.refs_2_, ...), custom_call_target="tpu_custom_call" | custom-call | flops 2415919104 | bytes 2097152 | tf_op jit(solution)/shard_map/pallas_call | solution.py:170
  78.9 0.0 collective-permute-done.15.refs_2_
  78.9 0.1 collective-permute-start.17
  79.0 0.5 collective-permute-start.18
  79.5 0.1 collective-permute-start.16
  79.6 2.3 %shard_map.124 = (bf16[384,768]{1,0:T(8,128)(2,1)S(1)}, bf16[64,256]{1,0:T(8,128)(2,1)S(1)}) custom-call(bf16[128,2048]{1,0:T(8,128)(2,1)S(1)} %collective-permute-done.19.refs_0_, bf16[64,2048]{1,0:T(8,128)(2,1)S(1)} %collective-permute-done.14.refs_1_, bf16[64,2048]{1,0:T(8,128)(2,1)S(1)} %collective-permute-done.15.refs_2_, ...), custom_call_target="tpu_custom_call" | custom-call | tf_op jit(solution)/shard_map/pallas_call | solution.py:206
  81.9 1.5 %shard_map.125 = (bf16[384,768]{1,0:T(8,128)(2,1)S(1)}, bf16[64,128]{1,0:T(8,128)(2,1)S(1)}) custom-call(bf16[64,2048]{1,0:T(8,128)(2,1)S(1)} %collective-permute-done.17.refs_0_, bf16[64,2048]{1,0:T(8,128)(2,1)S(1)} %collective-permute-done.18.refs_1_, ...), custom_call_target="tpu_custom_call", output_to_operand_aliasing={{0}: (5, {})} | custom-call | tf_op jit(solution)/shard_map/pallas_call | solution.py:206
  83.4 1.2 %collective-permute-done.20.refs_2_ = bf16[128,2048]{1,0:T(8,128)(2,1)S(1)} collective-permute-done((bf16[128,2048]{1,0:T(8,128)(2,1)S(1)}, bf16[128,2048]{1,0:T(8,128)(2,1)S(1)}, u32[]{:S(2)}, u32[]{:S(2)}) %collective-permute-start.20) | collective-permute-done | bytes 524320 | tf_op jit(solution)/shard_map/ppermute | solution.py:378
  84.6 1.7 %shard_map.126 = (f32[16,1,384]{2,1,0:T(1,128)S(1)}, f32[64,256]{1,0:T(8,128)S(1)}, f32[128,2048]{1,0:T(8,128)S(1)}) custom-call(f32[16,1,384]{2,1,0:T(1,128)S(1)} %get-tuple-element.82.refs_0_, bf16[128,2048]{1,0:T(8,128)(2,1)S(1)} %collective-permute-done.16.refs_1_, bf16[128,2048]{1,0:T(8,128)(2,1)S(1)} %collective-permute-done.20.refs_2_, ...), custom_call_target="tpu_custom_call" | custom-call | flops 1207959552 | bytes 1048576 | tf_op jit(solution)/shard_map/pallas_call | solution.py:276
  86.3 0.2 collective-permute-done.21.dy
  86.5 0.3 shard_map.127
  86.8 12.8 %all_to_all.5.returned = f32[16,1,384]{2,1,0:T(1,128)S(1)} all-to-all(f32[16,1,384]{2,1,0:T(1,128)S(1)} %get-tuple-element.95), channel_id=1, replica_groups=mesh['grp'=2,'exp'=16] {'exp'}, dimensions={0} | all-to-all | bytes 49152 | tf_op jit(solution)/shard_map/all_to_all | solution.py:468
  99.6 1.1 %shard_map.128 = (f32[256,64]{1,0:T(8,128)}, f32[8,128]{1,0:T(8,128)}) custom-call(f32[16,1,384]{2,1,0:T(1,128)S(1)} %all_to_all.5.returned, s32[8,128]{1,0:T(8,128)S(1)} %bitcast.19, bf16[64,256]{1,0:T(8,128)(2,1)S(1)} %get-tuple-element.96.refs_0_, bf16[64,384]{1,0:T(8,128)(2,1)S(1)} %get-tuple-element.97.refs_1_, ...), custom_call_target="tpu_custom_call" | custom-call | tf_op jit(solution)/shard_map/pallas_call | solution.py:469
  (29 shorter events, 0.1 us)
Async XLA Ops:
  0.6 7.2 %collective-permute-start = (bf16[128,2048]{1,0:T(8,128)(2,1)}, bf16[128,2048]{1,0:T(8,128)(2,1)S(1)}, u32[]{:S(2)}, u32[]{:S(2)}) collective-permute-start(bf16[128,2048]{1,0:T(8,128)(2,1)} %refs_1_.1), channel_id=1, source_target_pairs={{0,1},{1,0},{2,3},{3,2},{4,5},{5,4},{6,7},{7,6},{8,9},{9,8},{10,11... | collective-permute-start | bytes 1572872 | tf_op jit(solution)/shard_map/ppermute | solution.py:381
  1.1 6.7 %collective-permute-start.1 = (bf16[128,2048]{1,0:T(8,128)(2,1)}, bf16[128,2048]{1,0:T(8,128)(2,1)S(1)}, u32[]{:S(2)}, u32[]{:S(2)}) collective-permute-start(bf16[128,2048]{1,0:T(8,128)(2,1)} %refs_2_.1), channel_id=1, source_target_pairs={{0,1},{1,0},{2,3},{3,2},{4,5},{5,4},{6,7},{7,6},{8,9},{9,8},{10,11... | collective-permute-start | bytes 1572872 | tf_op jit(solution)/shard_map/ppermute | solution.py:381
  1.2 18.4 %collective-permute-start.2 = (bf16[128,2048]{1,0:T(8,128)(2,1)}, bf16[128,2048]{1,0:T(8,128)(2,1)S(1)}, u32[]{:S(2)}, u32[]{:S(2)}) collective-permute-start(bf16[128,2048]{1,0:T(8,128)(2,1)} %refs_1_.1), channel_id=1, source_target_pairs={{0,4},{1,3},{4,8},{5,1},{8,12},{9,5},{12,14},{13,9},{14,10},{15,13... | collective-permute-start | bytes 1572872 | tf_op jit(solution)/shard_map/ppermute | solution.py:378
  4.2 15.4 %collective-permute-start.3 = (bf16[128,2048]{1,0:T(8,128)(2,1)}, bf16[128,2048]{1,0:T(8,128)(2,1)S(1)}, u32[]{:S(2)}, u32[]{:S(2)}) collective-permute-start(bf16[128,2048]{1,0:T(8,128)(2,1)} %refs_2_.1), channel_id=1, source_target_pairs={{0,4},{1,3},{4,8},{5,1},{8,12},{9,5},{12,14},{13,9},{14,10},{15,13... | collective-permute-start | bytes 1572872 | tf_op jit(solution)/shard_map/ppermute | solution.py:378
  5.8 0.7 copy-start.4
  6.5 0.7 copy-start.6
  7.2 0.7 copy-start.7
  8.0 20.4 %collective-permute-start.4 = (bf16[256,2048]{1,0:T(8,128)(2,1)S(1)}, bf16[256,2048]{1,0:T(8,128)(2,1)S(1)}, u32[]{:S(2)}, u32[]{:S(2)}) collective-permute-start(bf16[256,2048]{1,0:T(8,128)(2,1)S(1)} %shard_map.114.refs_3_), channel_id=1, source_target_pairs={{0,4},{1,3},{4,8},{5,1},{8,12},{9,5},{12,14},{13,9},{14,10},{15,13... | collective-permute-start | bytes 3145736 | tf_op jit(solution)/shard_map/ppermute | solution.py:378
  9.6 1.0 %copy-start = (bf16[128,2048]{1,0:T(8,128)(2,1)S(1)}, bf16[128,2048]{1,0:T(8,128)(2,1)}, u32[]{:S(2)}) copy-start(bf16[128,2048]{1,0:T(8,128)(2,1)} %refs_1_.1) | copy-start | bytes 1572868
  10.6 1.0 %copy-start.1 = (bf16[128,2048]{1,0:T(8,128)(2,1)S(1)}, bf16[128,2048]{1,0:T(8,128)(2,1)}, u32[]{:S(2)}) copy-start(bf16[128,2048]{1,0:T(8,128)(2,1)} %refs_2_.1) | copy-start | bytes 1572868
  11.7 0.9 copy-start.2
  12.6 0.9 copy-start.3
  19.7 10.8 %collective-permute-start.5 = (bf16[256,2048]{1,0:T(8,128)(2,1)S(1)}, bf16[256,2048]{1,0:T(8,128)(2,1)S(1)}, u32[]{:S(2)}, u32[]{:S(2)}) collective-permute-start(bf16[256,2048]{1,0:T(8,128)(2,1)S(1)} %shard_map.116.refs_3_), channel_id=1, source_target_pairs={{0,1},{1,0},{2,3},{3,2},{4,5},{5,4},{6,7},{7,6},{8,9},{9,8},{10,11... | collective-permute-start | bytes 3145736 | tf_op jit(solution)/shard_map/ppermute | solution.py:381
  19.8 19.8 %collective-permute-start.6 = (bf16[256,2048]{1,0:T(8,128)(2,1)S(1)}, bf16[256,2048]{1,0:T(8,128)(2,1)S(1)}, u32[]{:S(2)}, u32[]{:S(2)}) collective-permute-start(bf16[256,2048]{1,0:T(8,128)(2,1)S(1)} %shard_map.116.refs_3_), channel_id=1, source_target_pairs={{0,4},{1,3},{4,8},{5,1},{8,12},{9,5},{12,14},{13,9},{14,10},{15,13... | collective-permute-start | bytes 3145736 | tf_op jit(solution)/shard_map/ppermute | solution.py:378
  28.4 13.4 %collective-permute-start.7 = (bf16[256,2048]{1,0:T(8,128)(2,1)S(1)}, bf16[256,2048]{1,0:T(8,128)(2,1)S(1)}, u32[]{:S(2)}, u32[]{:S(2)}) collective-permute-start(bf16[256,2048]{1,0:T(8,128)(2,1)S(1)} %collective-permute-done.4.refs_1_), channel_id=1, source_target_pairs={{0,1},{1,0},{2,3},{3,2},{4,5},{5,4},{6,7},{7,6},{8,9},{9,8},{10,11... | collective-permute-start | bytes 3145736 | tf_op jit(solution)/shard_map/ppermute | solution.py:381
  28.4 22.5 %collective-permute-start.8 = (bf16[256,2048]{1,0:T(8,128)(2,1)S(1)}, bf16[256,2048]{1,0:T(8,128)(2,1)S(1)}, u32[]{:S(2)}, u32[]{:S(2)}) collective-permute-start(bf16[256,2048]{1,0:T(8,128)(2,1)S(1)} %collective-permute-done.4.refs_1_), channel_id=1, source_target_pairs={{0,4},{1,3},{4,8},{5,1},{8,12},{9,5},{12,14},{13,9},{14,10},{15,13... | collective-permute-start | bytes 3145736 | tf_op jit(solution)/shard_map/ppermute | solution.py:378
  39.6 13.4 %collective-permute-start.9 = (bf16[256,2048]{1,0:T(8,128)(2,1)S(1)}, bf16[256,2048]{1,0:T(8,128)(2,1)S(1)}, u32[]{:S(2)}, u32[]{:S(2)}) collective-permute-start(bf16[256,2048]{1,0:T(8,128)(2,1)S(1)} %collective-permute-done.6.refs_1_), channel_id=1, source_target_pairs={{0,1},{1,0},{2,3},{3,2},{4,5},{5,4},{6,7},{7,6},{8,9},{9,8},{10,11... | collective-permute-start | bytes 3145736 | tf_op jit(solution)/shard_map/ppermute | solution.py:381
  39.6 22.5 %collective-permute-start.10 = (bf16[256,2048]{1,0:T(8,128)(2,1)S(1)}, bf16[256,2048]{1,0:T(8,128)(2,1)S(1)}, u32[]{:S(2)}, u32[]{:S(2)}) collective-permute-start(bf16[256,2048]{1,0:T(8,128)(2,1)S(1)} %collective-permute-done.6.refs_1_), channel_id=1, source_target_pairs={{0,4},{1,3},{4,8},{5,1},{8,12},{9,5},{12,14},{13,9},{14,10},{15,13... | collective-permute-start | bytes 3145736 | tf_op jit(solution)/shard_map/ppermute | solution.py:378
  50.8 15.1 %collective-permute-start.11 = (bf16[256,2048]{1,0:T(8,128)(2,1)S(1)}, bf16[256,2048]{1,0:T(8,128)(2,1)S(1)}, u32[]{:S(2)}, u32[]{:S(2)}) collective-permute-start(bf16[256,2048]{1,0:T(8,128)(2,1)S(1)} %collective-permute-done.8.refs_1_), channel_id=1, source_target_pairs={{0,1},{1,0},{2,3},{3,2},{4,5},{5,4},{6,7},{7,6},{8,9},{9,8},{10,11... | collective-permute-start | bytes 3145736 | tf_op jit(solution)/shard_map/ppermute | solution.py:381
  50.8 22.5 %collective-permute-start.12 = (bf16[256,2048]{1,0:T(8,128)(2,1)S(1)}, bf16[256,2048]{1,0:T(8,128)(2,1)S(1)}, u32[]{:S(2)}, u32[]{:S(2)}) collective-permute-start(bf16[256,2048]{1,0:T(8,128)(2,1)S(1)} %collective-permute-done.8.refs_1_), channel_id=1, source_target_pairs={{0,4},{1,3},{4,8},{5,1},{8,12},{9,5},{12,14},{13,9},{14,10},{15,13... | collective-permute-start | bytes 3145736 | tf_op jit(solution)/shard_map/ppermute | solution.py:378
  62.1 13.8 %collective-permute-start.13 = (bf16[256,2048]{1,0:T(8,128)(2,1)S(1)}, bf16[256,2048]{1,0:T(8,128)(2,1)S(1)}, u32[]{:S(2)}, u32[]{:S(2)}) collective-permute-start(bf16[256,2048]{1,0:T(8,128)(2,1)S(1)} %collective-permute-done.10.refs_1_.block), channel_id=1, source_target_pairs={{0,1},{1,0},{2,3},{3,2},{4,5},{5,4},{6,7},{7,6},{8,9},{9,8},{10,11... | collective-permute-start | bytes 3145736 | tf_op jit(solution)/shard_map/ppermute | solution.py:381
  62.1 16.8 %collective-permute-start.14 = (bf16[64,2048]{1,0:T(8,128)(2,1)S(1)}, bf16[64,2048]{1,0:T(8,128)(2,1)S(1)}, u32[]{:S(2)}, u32[]{:S(2)}) collective-permute-start(bf16[64,2048]{1,0:T(8,128)(2,1)S(1)} %get-tuple-element.80), channel_id=1, source_target_pairs={{0,4},{1,3},{4,8},{5,1},{8,12},{9,5},{12,14},{13,9},{14,10},{15,13... | collective-permute-start | bytes 786440 | tf_op jit(solution)/shard_map/ppermute | solution.py:378
  64.3 14.6 %collective-permute-start.15 = (bf16[64,2048]{1,0:T(8,128)(2,1)S(1)}, bf16[64,2048]{1,0:T(8,128)(2,1)S(1)}, u32[]{:S(2)}, u32[]{:S(2)}) collective-permute-start(bf16[64,2048]{1,0:T(8,128)(2,1)S(1)} %get-tuple-element.81), channel_id=1, source_target_pairs={{0,4},{1,3},{4,8},{5,1},{8,12},{9,5},{12,14},{13,9},{14,10},{15,13... | collective-permute-start | bytes 786440 | tf_op jit(solution)/shard_map/ppermute | solution.py:378
  73.4 6.2 %collective-permute-start.19 = (bf16[128,2048]{1,0:T(8,128)(2,1)S(1)}, bf16[128,2048]{1,0:T(8,128)(2,1)S(1)}, u32[]{:S(2)}, u32[]{:S(2)}) collective-permute-start(bf16[128,2048]{1,0:T(8,128)(2,1)S(1)} %get-tuple-element.86), channel_id=1, source_target_pairs={{0,1},{1,0},{2,3},{3,2},{4,5},{5,4},{6,7},{7,6},{8,9},{9,8},{10,11... | collective-permute-start | bytes 1572872 | tf_op jit(solution)/shard_map/ppermute | solution.py:381
  73.5 11.1 %collective-permute-start.20 = (bf16[128,2048]{1,0:T(8,128)(2,1)S(1)}, bf16[128,2048]{1,0:T(8,128)(2,1)S(1)}, u32[]{:S(2)}, u32[]{:S(2)}) collective-permute-start(bf16[128,2048]{1,0:T(8,128)(2,1)S(1)} %get-tuple-element.90), channel_id=1, source_target_pairs={{0,4},{1,3},{4,8},{5,1},{8,12},{9,5},{12,14},{13,9},{14,10},{15,13... | collective-permute-start | bytes 1572872 | tf_op jit(solution)/shard_map/ppermute | solution.py:378
  78.9 2.9 %collective-permute-start.17 = (bf16[64,2048]{1,0:T(8,128)(2,1)S(1)}, bf16[64,2048]{1,0:T(8,128)(2,1)S(1)}, u32[]{:S(2)}, u32[]{:S(2)}) collective-permute-start(bf16[64,2048]{1,0:T(8,128)(2,1)S(1)} %collective-permute-done.14.refs_1_), channel_id=1, source_target_pairs={{0,1},{1,0},{2,3},{3,2},{4,5},{5,4},{6,7},{7,6},{8,9},{9,8},{10,11... | collective-permute-start | bytes 786440 | tf_op jit(solution)/shard_map/ppermute | solution.py:381
  79.0 2.9 %collective-permute-start.18 = (bf16[64,2048]{1,0:T(8,128)(2,1)S(1)}, bf16[64,2048]{1,0:T(8,128)(2,1)S(1)}, u32[]{:S(2)}, u32[]{:S(2)}) collective-permute-start(bf16[64,2048]{1,0:T(8,128)(2,1)S(1)} %collective-permute-done.15.refs_2_), channel_id=1, source_target_pairs={{0,1},{1,0},{2,3},{3,2},{4,5},{5,4},{6,7},{7,6},{8,9},{9,8},{10,11... | collective-permute-start | bytes 786440 | tf_op jit(solution)/shard_map/ppermute | solution.py:381
  79.5 5.0 %collective-permute-start.16 = (bf16[128,2048]{1,0:T(8,128)(2,1)S(1)}, bf16[128,2048]{1,0:T(8,128)(2,1)S(1)}, u32[]{:S(2)}, u32[]{:S(2)}) collective-permute-start(bf16[128,2048]{1,0:T(8,128)(2,1)S(1)} %get-tuple-element.83), channel_id=1, source_target_pairs={{0,1},{1,0},{2,3},{3,2},{4,5},{5,4},{6,7},{7,6},{8,9},{9,8},{10,11... | collective-permute-start | bytes 1572872 | tf_op jit(solution)/shard_map/ppermute | solution.py:381
  84.5 15.1 %copy-start.5 = (s32[128,8]{0,1:T(8,128)S(1)}, s32[128,8]{0,1:T(8,128)}, u32[]{:S(2)}) copy-start(s32[128,8]{0,1:T(8,128)} %param.12) | copy-start | bytes 12292
  84.5 1.9 %collective-permute-start.21 = (bf16[128,2048]{1,0:T(8,128)(2,1)S(1)}, bf16[128,2048]{1,0:T(8,128)(2,1)S(1)}, u32[]{:S(2)}, u32[]{:S(2)}) collective-permute-start(bf16[128,2048]{1,0:T(8,128)(2,1)S(1)} %collective-permute-done.20.refs_2_), channel_id=1, source_target_pairs={{0,1},{1,0},{2,3},{3,2},{4,5},{5,4},{6,7},{7,6},{8,9},{9,8},{10,11... | collective-permute-start | bytes 1572872 | tf_op jit(solution)/shard_map/ppermute | solution.py:381

commit v20 on v18

--- a/solution.py
+++ b/solution.py
@@ -244,7 +244,7 @@
     rows = dy_in[0].shape[0]
     across = (((1,), (1,)), ((), ()))
     width = w_down.shape[1]
-    tile = 512 if width % 512 == 0 else width
+    tile = 256 if width % 256 == 0 else width
     totals = [0.0] * blocks
     for cut in range(0, width, tile):
         part = pl.ds(cut, tile)

time: 101 us -> 101 us (level)
  no operation moved by 1% of the time
where the time goes in v20:
time: 101 us
  waiting for transfers between devices  30.3 us (30%)
  Pallas kernels  29.5 us (29%)
  starting transfers between devices  21.2 us (21%)
  blocking collectives  12.8 us (13%)
  local copies, waits for them, and re-layouts  5.95 us (6%)
    ppermute x10, waiting for transfers between devices, hop(): return lax.ppermute(block, 'exp', onward)  28.8 us
    pallas_call x6, Pallas kernels, work(): return call(sheet, *apart, *block_in, *weights)  23 us
    ppermute x10, starting transfers between devices, hop(): return lax.ppermute(block, 'exp', onward)  20 us
    all_to_all x1, blocking collectives, by_ring(): lax.all_to_all(sheet, 'exp', split_axis=0, concat_axis=0, tiled=True)  12.8 us
    unnamed x16, local copies, waits for them, and re-layouts  5.95 us
    pallas_call x1, Pallas kernels, front(): pl.pallas_call(front_kernel, out_shape=[jax.ShapeDtypeStruct((rows, units...  3.09 us
    pallas_call x2, Pallas kernels, on_core(): pl.pallas_call(kernel, out_shape=[jax.ShapeDtypeStruct(shape, jnp.float32...  2.08 us
  transfers between devices with their start and end apart: 22, of which 10 were waited for; matrix products, arithmetic and copies ran while one was open for 0% of the time, Pallas kernels for 28%

profile of v20, /device:TPU:0, one launch (start us, length us, event | category | flops | bytes accessed | tf_op | source)
XLA Modules:
  0.0 100.7 jit_solution(7159804696107366178)
XLA Ops:
  0.6 0.5 collective-permute-start
  1.1 0.1 collective-permute-start.1
  1.2 3.0 %collective-permute-start.2 = (bf16[128,2048]{1,0:T(8,128)(2,1)}, bf16[128,2048]{1,0:T(8,128)(2,1)S(1)}, u32[]{:S(2)}, u32[]{:S(2)}) collective-permute-start(bf16[128,2048]{1,0:T(8,128)(2,1)} %refs_1_.1), channel_id=1, source_target_pairs={{0,4},{1,3},{4,8},{5,1},{8,12},{9,5},{12,14},{13,9},{14,10},{15,13... | collective-permute-start | bytes 1572872 | tf_op jit(solution)/shard_map/ppermute | solution.py:382
  4.2 1.6 %collective-permute-start.3 = (bf16[128,2048]{1,0:T(8,128)(2,1)}, bf16[128,2048]{1,0:T(8,128)(2,1)S(1)}, u32[]{:S(2)}, u32[]{:S(2)}) collective-permute-start(bf16[128,2048]{1,0:T(8,128)(2,1)} %refs_2_.1), channel_id=1, source_target_pairs={{0,4},{1,3},{4,8},{5,1},{8,12},{9,5},{12,14},{13,9},{14,10},{15,13... | collective-permute-start | bytes 1572872 | tf_op jit(solution)/shard_map/ppermute | solution.py:382
  5.8 0.7 copy-done.4
  6.5 0.7 copy-done.6
  7.2 0.7 copy-done.7
  7.9 0.1 shard_map.114.refs_3_
  8.0 1.6 %collective-permute-start.4 = (bf16[256,2048]{1,0:T(8,128)(2,1)S(1)}, bf16[256,2048]{1,0:T(8,128)(2,1)S(1)}, u32[]{:S(2)}, u32[]{:S(2)}) collective-permute-start(bf16[256,2048]{1,0:T(8,128)(2,1)S(1)} %shard_map.114.refs_3_), channel_id=1, source_target_pairs={{0,4},{1,3},{4,8},{5,1},{8,12},{9,5},{12,14},{13,9},{14,10},{15,13... | collective-permute-start | bytes 3145736 | tf_op jit(solution)/shard_map/ppermute | solution.py:382
  9.6 1.0 %copy-done = bf16[128,2048]{1,0:T(8,128)(2,1)S(1)} copy-done((bf16[128,2048]{1,0:T(8,128)(2,1)S(1)}, bf16[128,2048]{1,0:T(8,128)(2,1)}, u32[]{:S(2)}) %copy-start) | copy-done | bytes 524312
  10.6 1.0 %copy-done.1 = bf16[128,2048]{1,0:T(8,128)(2,1)S(1)} copy-done((bf16[128,2048]{1,0:T(8,128)(2,1)S(1)}, bf16[128,2048]{1,0:T(8,128)(2,1)}, u32[]{:S(2)}) %copy-start.1) | copy-done | bytes 524312
  11.7 0.9 copy-done.2
  12.6 0.9 copy-done.3
  13.5 6.1 %shard_map.115 = (f32[16,1,384]{2,1,0:T(1,128)S(1)}, bf16[64,256]{1,0:T(8,128)(2,1)S(1)}, f32[64,256]{1,0:T(8,128)S(1)}, bf16[2048,768]{1,0:T(8,128)(2,1)S(1)}, ...) custom-call(f32[16,1,384]{2,1,0:T(1,128)S(1)} %shard_map.113.refs_0_, ...), custom_call_target="tpu_custom_call" | custom-call | flops 2415919104 | bytes 2097152 | tf_op jit(solution)/shard_map/pallas_call | solution.py:170
  19.6 0.1 shard_map.116.refs_3_
  19.7 0.1 collective-permute-start.5
  19.8 1.5 %collective-permute-start.6 = (bf16[256,2048]{1,0:T(8,128)(2,1)S(1)}, bf16[256,2048]{1,0:T(8,128)(2,1)S(1)}, u32[]{:S(2)}, u32[]{:S(2)}) collective-permute-start(bf16[256,2048]{1,0:T(8,128)(2,1)S(1)} %shard_map.116.refs_3_), channel_id=1, source_target_pairs={{0,4},{1,3},{4,8},{5,1},{8,12},{9,5},{12,14},{13,9},{14,10},{15,13... | collective-permute-start | bytes 3145736 | tf_op jit(solution)/shard_map/ppermute | solution.py:382
  21.3 7.1 %collective-permute-done.4.refs_1_ = bf16[256,2048]{1,0:T(8,128)(2,1)S(1)} collective-permute-done((bf16[256,2048]{1,0:T(8,128)(2,1)S(1)}, bf16[256,2048]{1,0:T(8,128)(2,1)S(1)}, u32[]{:S(2)}, u32[]{:S(2)}) %collective-permute-start.4) | collective-permute-done | bytes 1048608 | tf_op jit(solution)/shard_map/ppermute | solution.py:382
  28.4 2.1 %collective-permute-start.8 = (bf16[256,2048]{1,0:T(8,128)(2,1)S(1)}, bf16[256,2048]{1,0:T(8,128)(2,1)S(1)}, u32[]{:S(2)}, u32[]{:S(2)}) collective-permute-start(bf16[256,2048]{1,0:T(8,128)(2,1)S(1)} %collective-permute-done.4.refs_1_), channel_id=1, source_target_pairs={{0,4},{1,3},{4,8},{5,1},{8,12},{9,5},{12,14},{13,9},{14,10},{15,13... | collective-permute-start | bytes 3145736 | tf_op jit(solution)/shard_map/ppermute | solution.py:382
  30.5 4.7 %shard_map.117 = (f32[16,1,384]{2,1,0:T(1,128)S(1)}, bf16[64,384]{1,0:T(8,128)(2,1)S(1)}, f32[64,384]{1,0:T(8,128)S(1)}) custom-call(f32[16,1,384]{2,1,0:T(1,128)S(1)} %get-tuple-element.58.refs_0_, bf16[256,2048]{1,0:T(8,128)(2,1)S(1)} %collective-permute-done.4.refs_1_, bf16[256,2048]{1,0:T(8,128)(2,1)S(1)} %collective-permute-done.5.refs_2_, ...), custom_call_target="tpu_custom_call" | custom-call | flops 3623878656 | bytes 3145728 | tf_op jit(solution)/shard_map/pallas_call | solution.py:170
  35.2 4.4 %collective-permute-done.6.refs_1_ = bf16[256,2048]{1,0:T(8,128)(2,1)S(1)} collective-permute-done((bf16[256,2048]{1,0:T(8,128)(2,1)S(1)}, bf16[256,2048]{1,0:T(8,128)(2,1)S(1)}, u32[]{:S(2)}, u32[]{:S(2)}) %collective-permute-start.6) | collective-permute-done | bytes 1048608 | tf_op jit(solution)/shard_map/ppermute | solution.py:382
  39.6 2.1 %collective-permute-start.10 = (bf16[256,2048]{1,0:T(8,128)(2,1)S(1)}, bf16[256,2048]{1,0:T(8,128)(2,1)S(1)}, u32[]{:S(2)}, u32[]{:S(2)}) collective-permute-start(bf16[256,2048]{1,0:T(8,128)(2,1)S(1)} %collective-permute-done.6.refs_1_), channel_id=1, source_target_pairs={{0,4},{1,3},{4,8},{5,1},{8,12},{9,5},{12,14},{13,9},{14,10},{15,13... | collective-permute-start | bytes 3145736 | tf_op jit(solution)/shard_map/ppermute | solution.py:382
  41.7 3.0 %shard_map.118 = (f32[16,1,384]{2,1,0:T(1,128)S(1)}, bf16[64,256]{1,0:T(8,128)(2,1)S(1)}, f32[64,256]{1,0:T(8,128)S(1)}) custom-call(f32[16,1,384]{2,1,0:T(1,128)S(1)} %get-tuple-element.67.refs_0_, bf16[256,2048]{1,0:T(8,128)(2,1)S(1)} %collective-permute-done.6.refs_1_, bf16[256,2048]{1,0:T(8,128)(2,1)S(1)} %collective-permute-done.7.refs_2_, ...), custom_call_target="tpu_custom_call" | custom-call | flops 2415919104 | bytes 2097152 | tf_op jit(solution)/shard_map/pallas_call | solution.py:170
  44.8 6.1 %collective-permute-done.8.refs_1_ = bf16[256,2048]{1,0:T(8,128)(2,1)S(1)} collective-permute-done((bf16[256,2048]{1,0:T(8,128)(2,1)S(1)}, bf16[256,2048]{1,0:T(8,128)(2,1)S(1)}, u32[]{:S(2)}, u32[]{:S(2)}) %collective-permute-start.8) | collective-permute-done | bytes 1048608 | tf_op jit(solution)/shard_map/ppermute | solution.py:382
  50.8 2.1 %collective-permute-start.12 = (bf16[256,2048]{1,0:T(8,128)(2,1)S(1)}, bf16[256,2048]{1,0:T(8,128)(2,1)S(1)}, u32[]{:S(2)}, u32[]{:S(2)}) collective-permute-start(bf16[256,2048]{1,0:T(8,128)(2,1)S(1)} %collective-permute-done.8.refs_1_), channel_id=1, source_target_pairs={{0,4},{1,3},{4,8},{5,1},{8,12},{9,5},{12,14},{13,9},{14,10},{15,13... | collective-permute-start | bytes 3145736 | tf_op jit(solution)/shard_map/ppermute | solution.py:382
  53.0 3.1 %shard_map.119 = (f32[16,1,384]{2,1,0:T(1,128)S(1)}, bf16[64,256]{1,0:T(8,128)(2,1)S(1)}, f32[64,256]{1,0:T(8,128)S(1)}) custom-call(f32[16,1,384]{2,1,0:T(1,128)S(1)} %get-tuple-element.70.refs_0_, bf16[256,2048]{1,0:T(8,128)(2,1)S(1)} %collective-permute-done.8.refs_1_, bf16[256,2048]{1,0:T(8,128)(2,1)S(1)} %collective-permute-done.9.refs_2_, ...), custom_call_target="tpu_custom_call" | custom-call | flops 2415919104 | bytes 2097152 | tf_op jit(solution)/shard_map/pallas_call | solution.py:170
  56.0 6.1 %collective-permute-done.10.refs_1_.block = bf16[256,2048]{1,0:T(8,128)(2,1)S(1)} collective-permute-done((bf16[256,2048]{1,0:T(8,128)(2,1)S(1)}, bf16[256,2048]{1,0:T(8,128)(2,1)S(1)}, u32[]{:S(2)}, u32[]{:S(2)}) %collective-permute-start.10) | collective-permute-done | bytes 1048608 | tf_op jit(solution)/shard_map/ppermute | solution.py:382
  62.1 0.1 shard_map.122
  62.1 2.2 %collective-permute-start.14 = (bf16[64,2048]{1,0:T(8,128)(2,1)S(1)}, bf16[64,2048]{1,0:T(8,128)(2,1)S(1)}, u32[]{:S(2)}, u32[]{:S(2)}) collective-permute-start(bf16[64,2048]{1,0:T(8,128)(2,1)S(1)} %get-tuple-element.79), channel_id=1, source_target_pairs={{0,4},{1,3},{4,8},{5,1},{8,12},{9,5},{12,14},{13,9},{14,10},{15,13... | collective-permute-start | bytes 786440 | tf_op jit(solution)/shard_map/ppermute | solution.py:382
  64.3 1.6 %collective-permute-start.15 = (bf16[64,2048]{1,0:T(8,128)(2,1)S(1)}, bf16[64,2048]{1,0:T(8,128)(2,1)S(1)}, u32[]{:S(2)}, u32[]{:S(2)}) collective-permute-start(bf16[64,2048]{1,0:T(8,128)(2,1)S(1)} %get-tuple-element.80), channel_id=1, source_target_pairs={{0,4},{1,3},{4,8},{5,1},{8,12},{9,5},{12,14},{13,9},{14,10},{15,13... | collective-permute-start | bytes 786440 | tf_op jit(solution)/shard_map/ppermute | solution.py:382
  65.9 3.0 %shard_map.120 = (f32[16,1,384]{2,1,0:T(1,128)S(1)}, bf16[64,256]{1,0:T(8,128)(2,1)S(1)}, f32[64,256]{1,0:T(8,128)S(1)}) custom-call(f32[16,1,384]{2,1,0:T(1,128)S(1)} %get-tuple-element.73.refs_0_, bf16[256,2048]{1,0:T(8,128)(2,1)S(1)} %collective-permute-done.10.refs_1_.block, bf16[256,2048]{1,0:T(8,128)(2,1)S(1)} %collective-permute-done.11.refs_2_, ...), custom_call_target="tpu_custom_call" | custom-call | flops 2415919104 | bytes 2097152 | tf_op jit(solution)/shard_map/pallas_call | solution.py:170
  68.9 4.4 %collective-permute-done.12.refs_1_.block = bf16[256,2048]{1,0:T(8,128)(2,1)S(1)} collective-permute-done((bf16[256,2048]{1,0:T(8,128)(2,1)S(1)}, bf16[256,2048]{1,0:T(8,128)(2,1)S(1)}, u32[]{:S(2)}, u32[]{:S(2)}) %collective-permute-start.12) | collective-permute-done | bytes 1048608 | tf_op jit(solution)/shard_map/ppermute | solution.py:382
  73.3 0.1 shard_map.123
  73.4 0.1 collective-permute-start.17
  73.5 2.2 %collective-permute-start.20 = (bf16[128,2048]{1,0:T(8,128)(2,1)S(1)}, bf16[128,2048]{1,0:T(8,128)(2,1)S(1)}, u32[]{:S(2)}, u32[]{:S(2)}) collective-permute-start(bf16[128,2048]{1,0:T(8,128)(2,1)S(1)} %get-tuple-element.88), channel_id=1, source_target_pairs={{0,4},{1,3},{4,8},{5,1},{8,12},{9,5},{12,14},{13,9},{14,10},{15,13... | collective-permute-start | bytes 1572872 | tf_op jit(solution)/shard_map/ppermute | solution.py:382
  75.6 3.0 %shard_map.121 = (f32[16,1,384]{2,1,0:T(1,128)S(1)}, bf16[64,256]{1,0:T(8,128)(2,1)S(1)}, f32[64,256]{1,0:T(8,128)S(1)}) custom-call(f32[16,1,384]{2,1,0:T(1,128)S(1)} %get-tuple-element.76.refs_0_, bf16[256,2048]{1,0:T(8,128)(2,1)S(1)} %collective-permute-done.12.refs_1_.block, bf16[256,2048]{1,0:T(8,128)(2,1)S(1)} %collective-permute-done.13.refs_2_, ...), custom_call_target="tpu_custom_call" | custom-call | flops 2415919104 | bytes 2097152 | tf_op jit(solution)/shard_map/pallas_call | solution.py:170
  78.7 0.2 collective-permute-done.15.refs_2_
  78.9 0.5 collective-permute-start.19
  79.4 0.0 collective-permute-start.16
  79.4 1.0 %collective-permute-done.18.refs_3_ = bf16[64,2048]{1,0:T(8,128)(2,1)S(1)} collective-permute-done((bf16[64,2048]{1,0:T(8,128)(2,1)S(1)}, bf16[64,2048]{1,0:T(8,128)(2,1)S(1)}, u32[]{:S(2)}, u32[]{:S(2)}) %collective-permute-start.18) | collective-permute-done | bytes 262176 | tf_op jit(solution)/shard_map/ppermute | solution.py:385
  80.5 0.4 collective-permute-done.19.refs_4_
  80.8 3.1 %shard_map.124 = (bf16[384,768]{1,0:T(8,128)(2,1)S(1)}, bf16[64,256]{1,0:T(8,128)(2,1)S(1)}, bf16[64,128]{1,0:T(8,128)(2,1)S(1)}) custom-call(bf16[128,2048]{1,0:T(8,128)(2,1)S(1)} %collective-permute-done.17.refs_0_, bf16[64,2048]{1,0:T(8,128)(2,1)S(1)} %collective-permute-done.14.refs_1_, bf16[64,2048]{1,0:T(8,128)(2,1)S(1)} %collective-permute-done.15.refs_2_, ...), custom_call_target="tpu_custom_call" | custom-call | flops 2415919104 | bytes 1572864 | tf_op jit(solution)/shard_map/pallas_call | solution.py:206
  83.9 0.6 collective-permute-done.20.refs_2_
  84.6 1.8 %shard_map.125 = (f32[16,1,384]{2,1,0:T(1,128)S(1)}, f32[64,256]{1,0:T(8,128)S(1)}, f32[128,2048]{1,0:T(8,128)S(1)}) custom-call(f32[16,1,384]{2,1,0:T(1,128)S(1)} %get-tuple-element.81.refs_0_, bf16[128,2048]{1,0:T(8,128)(2,1)S(1)} %collective-permute-done.16.refs_1_, bf16[128,2048]{1,0:T(8,128)(2,1)S(1)} %collective-permute-done.20.refs_2_, ...), custom_call_target="tpu_custom_call" | custom-call | flops 1207959552 | bytes 1048576 | tf_op jit(solution)/shard_map/pallas_call | solution.py:280
  86.3 0.1 collective-permute-done.21.dy
  86.5 0.3 shard_map.126
  86.8 12.8 %all_to_all.5.returned = f32[16,1,384]{2,1,0:T(1,128)S(1)} all-to-all(f32[16,1,384]{2,1,0:T(1,128)S(1)} %get-tuple-element.93), channel_id=1, replica_groups=mesh['grp'=2,'exp'=16] {'exp'}, dimensions={0} | all-to-all | bytes 49152 | tf_op jit(solution)/shard_map/all_to_all | solution.py:472
  99.6 1.1 %shard_map.127 = (f32[256,64]{1,0:T(8,128)}, f32[8,128]{1,0:T(8,128)}) custom-call(f32[16,1,384]{2,1,0:T(1,128)S(1)} %all_to_all.5.returned, s32[8,128]{1,0:T(8,128)S(1)} %bitcast.19, bf16[64,256]{1,0:T(8,128)(2,1)S(1)} %get-tuple-element.94.refs_0_, bf16[64,384]{1,0:T(8,128)(2,1)S(1)} %get-tuple-element.95.refs_1_, ...), custom_call_target="tpu_custom_call" | custom-call | tf_op jit(solution)/shard_map/pallas_call | solution.py:473
  (28 shorter events, 0.1 us)
Async XLA Ops:
  0.6 7.2 %collective-permute-start = (bf16[128,2048]{1,0:T(8,128)(2,1)}, bf16[128,2048]{1,0:T(8,128)(2,1)S(1)}, u32[]{:S(2)}, u32[]{:S(2)}) collective-permute-start(bf16[128,2048]{1,0:T(8,128)(2,1)} %refs_1_.1), channel_id=1, source_target_pairs={{0,1},{1,0},{2,3},{3,2},{4,5},{5,4},{6,7},{7,6},{8,9},{9,8},{10,11... | collective-permute-start | bytes 1572872 | tf_op jit(solution)/shard_map/ppermute | solution.py:385
  1.1 6.7 %collective-permute-start.1 = (bf16[128,2048]{1,0:T(8,128)(2,1)}, bf16[128,2048]{1,0:T(8,128)(2,1)S(1)}, u32[]{:S(2)}, u32[]{:S(2)}) collective-permute-start(bf16[128,2048]{1,0:T(8,128)(2,1)} %refs_2_.1), channel_id=1, source_target_pairs={{0,1},{1,0},{2,3},{3,2},{4,5},{5,4},{6,7},{7,6},{8,9},{9,8},{10,11... | collective-permute-start | bytes 1572872 | tf_op jit(solution)/shard_map/ppermute | solution.py:385
  1.2 18.4 %collective-permute-start.2 = (bf16[128,2048]{1,0:T(8,128)(2,1)}, bf16[128,2048]{1,0:T(8,128)(2,1)S(1)}, u32[]{:S(2)}, u32[]{:S(2)}) collective-permute-start(bf16[128,2048]{1,0:T(8,128)(2,1)} %refs_1_.1), channel_id=1, source_target_pairs={{0,4},{1,3},{4,8},{5,1},{8,12},{9,5},{12,14},{13,9},{14,10},{15,13... | collective-permute-start | bytes 1572872 | tf_op jit(solution)/shard_map/ppermute | solution.py:382
  4.2 15.4 %collective-permute-start.3 = (bf16[128,2048]{1,0:T(8,128)(2,1)}, bf16[128,2048]{1,0:T(8,128)(2,1)S(1)}, u32[]{:S(2)}, u32[]{:S(2)}) collective-permute-start(bf16[128,2048]{1,0:T(8,128)(2,1)} %refs_2_.1), channel_id=1, source_target_pairs={{0,4},{1,3},{4,8},{5,1},{8,12},{9,5},{12,14},{13,9},{14,10},{15,13... | collective-permute-start | bytes 1572872 | tf_op jit(solution)/shard_map/ppermute | solution.py:382
  5.8 0.7 copy-start.4
  6.5 0.7 copy-start.6
  7.2 0.7 copy-start.7
  8.0 20.4 %collective-permute-start.4 = (bf16[256,2048]{1,0:T(8,128)(2,1)S(1)}, bf16[256,2048]{1,0:T(8,128)(2,1)S(1)}, u32[]{:S(2)}, u32[]{:S(2)}) collective-permute-start(bf16[256,2048]{1,0:T(8,128)(2,1)S(1)} %shard_map.114.refs_3_), channel_id=1, source_target_pairs={{0,4},{1,3},{4,8},{5,1},{8,12},{9,5},{12,14},{13,9},{14,10},{15,13... | collective-permute-start | bytes 3145736 | tf_op jit(solution)/shard_map/ppermute | solution.py:382
  9.6 1.0 %copy-start = (bf16[128,2048]{1,0:T(8,128)(2,1)S(1)}, bf16[128,2048]{1,0:T(8,128)(2,1)}, u32[]{:S(2)}) copy-start(bf16[128,2048]{1,0:T(8,128)(2,1)} %refs_1_.1) | copy-start | bytes 1572868
  10.6 1.0 %copy-start.1 = (bf16[128,2048]{1,0:T(8,128)(2,1)S(1)}, bf16[128,2048]{1,0:T(8,128)(2,1)}, u32[]{:S(2)}) copy-start(bf16[128,2048]{1,0:T(8,128)(2,1)} %refs_2_.1) | copy-start | bytes 1572868
  11.7 0.9 copy-start.2
  12.6 0.9 copy-start.3
  19.7 10.8 %collective-permute-start.5 = (bf16[256,2048]{1,0:T(8,128)(2,1)S(1)}, bf16[256,2048]{1,0:T(8,128)(2,1)S(1)}, u32[]{:S(2)}, u32[]{:S(2)}) collective-permute-start(bf16[256,2048]{1,0:T(8,128)(2,1)S(1)} %shard_map.116.refs_3_), channel_id=1, source_target_pairs={{0,1},{1,0},{2,3},{3,2},{4,5},{5,4},{6,7},{7,6},{8,9},{9,8},{10,11... | collective-permute-start | bytes 3145736 | tf_op jit(solution)/shard_map/ppermute | solution.py:385
  19.8 19.8 %collective-permute-start.6 = (bf16[256,2048]{1,0:T(8,128)(2,1)S(1)}, bf16[256,2048]{1,0:T(8,128)(2,1)S(1)}, u32[]{:S(2)}, u32[]{:S(2)}) collective-permute-start(bf16[256,2048]{1,0:T(8,128)(2,1)S(1)} %shard_map.116.refs_3_), channel_id=1, source_target_pairs={{0,4},{1,3},{4,8},{5,1},{8,12},{9,5},{12,14},{13,9},{14,10},{15,13... | collective-permute-start | bytes 3145736 | tf_op jit(solution)/shard_map/ppermute | solution.py:382
  28.4 13.4 %collective-permute-start.7 = (bf16[256,2048]{1,0:T(8,128)(2,1)S(1)}, bf16[256,2048]{1,0:T(8,128)(2,1)S(1)}, u32[]{:S(2)}, u32[]{:S(2)}) collective-permute-start(bf16[256,2048]{1,0:T(8,128)(2,1)S(1)} %collective-permute-done.4.refs_1_), channel_id=1, source_target_pairs={{0,1},{1,0},{2,3},{3,2},{4,5},{5,4},{6,7},{7,6},{8,9},{9,8},{10,11... | collective-permute-start | bytes 3145736 | tf_op jit(solution)/shard_map/ppermute | solution.py:385
  28.4 22.5 %collective-permute-start.8 = (bf16[256,2048]{1,0:T(8,128)(2,1)S(1)}, bf16[256,2048]{1,0:T(8,128)(2,1)S(1)}, u32[]{:S(2)}, u32[]{:S(2)}) collective-permute-start(bf16[256,2048]{1,0:T(8,128)(2,1)S(1)} %collective-permute-done.4.refs_1_), channel_id=1, source_target_pairs={{0,4},{1,3},{4,8},{5,1},{8,12},{9,5},{12,14},{13,9},{14,10},{15,13... | collective-permute-start | bytes 3145736 | tf_op jit(solution)/shard_map/ppermute | solution.py:382
  39.6 13.4 %collective-permute-start.9 = (bf16[256,2048]{1,0:T(8,128)(2,1)S(1)}, bf16[256,2048]{1,0:T(8,128)(2,1)S(1)}, u32[]{:S(2)}, u32[]{:S(2)}) collective-permute-start(bf16[256,2048]{1,0:T(8,128)(2,1)S(1)} %collective-permute-done.6.refs_1_), channel_id=1, source_target_pairs={{0,1},{1,0},{2,3},{3,2},{4,5},{5,4},{6,7},{7,6},{8,9},{9,8},{10,11... | collective-permute-start | bytes 3145736 | tf_op jit(solution)/shard_map/ppermute | solution.py:385
  39.6 22.5 %collective-permute-start.10 = (bf16[256,2048]{1,0:T(8,128)(2,1)S(1)}, bf16[256,2048]{1,0:T(8,128)(2,1)S(1)}, u32[]{:S(2)}, u32[]{:S(2)}) collective-permute-start(bf16[256,2048]{1,0:T(8,128)(2,1)S(1)} %collective-permute-done.6.refs_1_), channel_id=1, source_target_pairs={{0,4},{1,3},{4,8},{5,1},{8,12},{9,5},{12,14},{13,9},{14,10},{15,13... | collective-permute-start | bytes 3145736 | tf_op jit(solution)/shard_map/ppermute | solution.py:382
  50.8 15.1 %collective-permute-start.11 = (bf16[256,2048]{1,0:T(8,128)(2,1)S(1)}, bf16[256,2048]{1,0:T(8,128)(2,1)S(1)}, u32[]{:S(2)}, u32[]{:S(2)}) collective-permute-start(bf16[256,2048]{1,0:T(8,128)(2,1)S(1)} %collective-permute-done.8.refs_1_), channel_id=1, source_target_pairs={{0,1},{1,0},{2,3},{3,2},{4,5},{5,4},{6,7},{7,6},{8,9},{9,8},{10,11... | collective-permute-start | bytes 3145736 | tf_op jit(solution)/shard_map/ppermute | solution.py:385
  50.8 22.5 %collective-permute-start.12 = (bf16[256,2048]{1,0:T(8,128)(2,1)S(1)}, bf16[256,2048]{1,0:T(8,128)(2,1)S(1)}, u32[]{:S(2)}, u32[]{:S(2)}) collective-permute-start(bf16[256,2048]{1,0:T(8,128)(2,1)S(1)} %collective-permute-done.8.refs_1_), channel_id=1, source_target_pairs={{0,4},{1,3},{4,8},{5,1},{8,12},{9,5},{12,14},{13,9},{14,10},{15,13... | collective-permute-start | bytes 3145736 | tf_op jit(solution)/shard_map/ppermute | solution.py:382
  62.1 13.6 %collective-permute-start.13 = (bf16[256,2048]{1,0:T(8,128)(2,1)S(1)}, bf16[256,2048]{1,0:T(8,128)(2,1)S(1)}, u32[]{:S(2)}, u32[]{:S(2)}) collective-permute-start(bf16[256,2048]{1,0:T(8,128)(2,1)S(1)} %collective-permute-done.10.refs_1_.block), channel_id=1, source_target_pairs={{0,1},{1,0},{2,3},{3,2},{4,5},{5,4},{6,7},{7,6},{8,9},{9,8},{10,11... | collective-permute-start | bytes 3145736 | tf_op jit(solution)/shard_map/ppermute | solution.py:385
  62.1 16.5 %collective-permute-start.14 = (bf16[64,2048]{1,0:T(8,128)(2,1)S(1)}, bf16[64,2048]{1,0:T(8,128)(2,1)S(1)}, u32[]{:S(2)}, u32[]{:S(2)}) collective-permute-start(bf16[64,2048]{1,0:T(8,128)(2,1)S(1)} %get-tuple-element.79), channel_id=1, source_target_pairs={{0,4},{1,3},{4,8},{5,1},{8,12},{9,5},{12,14},{13,9},{14,10},{15,13... | collective-permute-start | bytes 786440 | tf_op jit(solution)/shard_map/ppermute | solution.py:382
  64.3 14.6 %collective-permute-start.15 = (bf16[64,2048]{1,0:T(8,128)(2,1)S(1)}, bf16[64,2048]{1,0:T(8,128)(2,1)S(1)}, u32[]{:S(2)}, u32[]{:S(2)}) collective-permute-start(bf16[64,2048]{1,0:T(8,128)(2,1)S(1)} %get-tuple-element.80), channel_id=1, source_target_pairs={{0,4},{1,3},{4,8},{5,1},{8,12},{9,5},{12,14},{13,9},{14,10},{15,13... | collective-permute-start | bytes 786440 | tf_op jit(solution)/shard_map/ppermute | solution.py:382
  73.4 7.5 %collective-permute-start.17 = (bf16[128,2048]{1,0:T(8,128)(2,1)S(1)}, bf16[128,2048]{1,0:T(8,128)(2,1)S(1)}, u32[]{:S(2)}, u32[]{:S(2)}) collective-permute-start(bf16[128,2048]{1,0:T(8,128)(2,1)S(1)} %get-tuple-element.83), channel_id=1, source_target_pairs={{0,1},{1,0},{2,3},{3,2},{4,5},{5,4},{6,7},{7,6},{8,9},{9,8},{10,11... | collective-permute-start | bytes 1572872 | tf_op jit(solution)/shard_map/ppermute | solution.py:385
  73.5 11.1 %collective-permute-start.20 = (bf16[128,2048]{1,0:T(8,128)(2,1)S(1)}, bf16[128,2048]{1,0:T(8,128)(2,1)S(1)}, u32[]{:S(2)}, u32[]{:S(2)}) collective-permute-start(bf16[128,2048]{1,0:T(8,128)(2,1)S(1)} %get-tuple-element.88), channel_id=1, source_target_pairs={{0,4},{1,3},{4,8},{5,1},{8,12},{9,5},{12,14},{13,9},{14,10},{15,13... | collective-permute-start | bytes 1572872 | tf_op jit(solution)/shard_map/ppermute | solution.py:382
  78.9 1.5 %collective-permute-start.18 = (bf16[64,2048]{1,0:T(8,128)(2,1)S(1)}, bf16[64,2048]{1,0:T(8,128)(2,1)S(1)}, u32[]{:S(2)}, u32[]{:S(2)}) collective-permute-start(bf16[64,2048]{1,0:T(8,128)(2,1)S(1)} %collective-permute-done.14.refs_1_), channel_id=1, source_target_pairs={{0,1},{1,0},{2,3},{3,2},{4,5},{5,4},{6,7},{7,6},{8,9},{9,8},{10,11... | collective-permute-start | bytes 786440 | tf_op jit(solution)/shard_map/ppermute | solution.py:385
  78.9 1.9 %collective-permute-start.19 = (bf16[64,2048]{1,0:T(8,128)(2,1)S(1)}, bf16[64,2048]{1,0:T(8,128)(2,1)S(1)}, u32[]{:S(2)}, u32[]{:S(2)}) collective-permute-start(bf16[64,2048]{1,0:T(8,128)(2,1)S(1)} %collective-permute-done.15.refs_2_), channel_id=1, source_target_pairs={{0,1},{1,0},{2,3},{3,2},{4,5},{5,4},{6,7},{7,6},{8,9},{9,8},{10,11... | collective-permute-start | bytes 786440 | tf_op jit(solution)/shard_map/ppermute | solution.py:385
  79.4 5.1 %collective-permute-start.16 = (bf16[128,2048]{1,0:T(8,128)(2,1)S(1)}, bf16[128,2048]{1,0:T(8,128)(2,1)S(1)}, u32[]{:S(2)}, u32[]{:S(2)}) collective-permute-start(bf16[128,2048]{1,0:T(8,128)(2,1)S(1)} %get-tuple-element.82), channel_id=1, source_target_pairs={{0,1},{1,0},{2,3},{3,2},{4,5},{5,4},{6,7},{7,6},{8,9},{9,8},{10,11... | collective-permute-start | bytes 1572872 | tf_op jit(solution)/shard_map/ppermute | solution.py:385
  84.5 15.1 %copy-start.5 = (s32[128,8]{0,1:T(8,128)S(1)}, s32[128,8]{0,1:T(8,128)}, u32[]{:S(2)}) copy-start(s32[128,8]{0,1:T(8,128)} %param.12) | copy-start | bytes 12292
  84.5 1.9 %collective-permute-start.21 = (bf16[128,2048]{1,0:T(8,128)(2,1)S(1)}, bf16[128,2048]{1,0:T(8,128)(2,1)S(1)}, u32[]{:S(2)}, u32[]{:S(2)}) collective-permute-start(bf16[128,2048]{1,0:T(8,128)(2,1)S(1)} %collective-permute-done.20.refs_2_), channel_id=1, source_target_pairs={{0,1},{1,0},{2,3},{3,2},{4,5},{5,4},{6,7},{7,6},{8,9},{9,8},{10,11... | collective-permute-start | bytes 1572872 | tf_op jit(solution)/shard_map/ppermute | solution.py:385

commit v21 on v19

--- a/solution.py
+++ b/solution.py
@@ -240,7 +240,7 @@
     rows = dy_in[0].shape[0]
     across = (((1,), (1,)), ((), ()))
     width = w_down.shape[1]
-    tile = 512 if width % 512 == 0 else width
+    tile = 256 if width % 256 == 0 else width
     totals = [0.0] * blocks
     for cut in range(0, width, tile):
         part = pl.ds(cut, tile)

time: 101 us -> 101 us (level)
  no operation moved by 1% of the time
where the time goes in v21:
time: 101 us
  Pallas kernels  30.2 us (30%)
  waiting for transfers between devices  29.3 us (29%)
  starting transfers between devices  21.6 us (21%)
  blocking collectives  12.8 us (13%)
  local copies, waits for them, and re-layouts  5.95 us (6%)
    ppermute x10, waiting for transfers between devices, hop(): return lax.ppermute(block, 'exp', onward)  29.1 us
    pallas_call x6, Pallas kernels, work(): return call(sheet, *apart, *block_in, *weights)  23 us
    ppermute x10, starting transfers between devices, hop(): return lax.ppermute(block, 'exp', onward)  20.2 us
    all_to_all x1, blocking collectives, by_ring(): lax.all_to_all(sheet, 'exp', split_axis=0, concat_axis=0, tiled=True)  12.8 us
    unnamed x16, local copies, waits for them, and re-layouts  5.95 us
    pallas_call x2, Pallas kernels, front(): pl.pallas_call(kernel, out_shape=[jax.ShapeDtypeStruct((room, units), jnp...  3.75 us
    pallas_call x2, Pallas kernels, on_core(): pl.pallas_call(kernel, out_shape=[jax.ShapeDtypeStruct(shape, jnp.float32...  2.07 us
  transfers between devices with their start and end apart: 22, of which 7 were waited for; matrix products, arithmetic and copies ran while one was open for 0% of the time, Pallas kernels for 29%

profile of v21, /device:TPU:0, one launch (start us, length us, event | category | flops | bytes accessed | tf_op | source)
XLA Modules:
  0.0 100.7 jit_solution(7889987648821527971)
XLA Ops:
  0.6 0.5 collective-permute-start
  1.1 0.1 collective-permute-start.1
  1.2 3.0 %collective-permute-start.2 = (bf16[128,2048]{1,0:T(8,128)(2,1)}, bf16[128,2048]{1,0:T(8,128)(2,1)S(1)}, u32[]{:S(2)}, u32[]{:S(2)}) collective-permute-start(bf16[128,2048]{1,0:T(8,128)(2,1)} %refs_1_.1), channel_id=1, source_target_pairs={{0,4},{1,3},{4,8},{5,1},{8,12},{9,5},{12,14},{13,9},{14,10},{15,13... | collective-permute-start | bytes 1572872 | tf_op jit(solution)/shard_map/ppermute | solution.py:378
  4.2 1.6 %collective-permute-start.3 = (bf16[128,2048]{1,0:T(8,128)(2,1)}, bf16[128,2048]{1,0:T(8,128)(2,1)S(1)}, u32[]{:S(2)}, u32[]{:S(2)}) collective-permute-start(bf16[128,2048]{1,0:T(8,128)(2,1)} %refs_2_.1), channel_id=1, source_target_pairs={{0,4},{1,3},{4,8},{5,1},{8,12},{9,5},{12,14},{13,9},{14,10},{15,13... | collective-permute-start | bytes 1572872 | tf_op jit(solution)/shard_map/ppermute | solution.py:378
  5.8 0.7 copy-done.4
  6.5 0.7 copy-done.6
  7.2 0.7 copy-done.7
  7.9 0.1 shard_map.114.refs_3_
  8.0 1.6 %collective-permute-start.4 = (bf16[256,2048]{1,0:T(8,128)(2,1)S(1)}, bf16[256,2048]{1,0:T(8,128)(2,1)S(1)}, u32[]{:S(2)}, u32[]{:S(2)}) collective-permute-start(bf16[256,2048]{1,0:T(8,128)(2,1)S(1)} %shard_map.114.refs_3_), channel_id=1, source_target_pairs={{0,4},{1,3},{4,8},{5,1},{8,12},{9,5},{12,14},{13,9},{14,10},{15,13... | collective-permute-start | bytes 3145736 | tf_op jit(solution)/shard_map/ppermute | solution.py:378
  9.6 1.0 %copy-done = bf16[128,2048]{1,0:T(8,128)(2,1)S(1)} copy-done((bf16[128,2048]{1,0:T(8,128)(2,1)S(1)}, bf16[128,2048]{1,0:T(8,128)(2,1)}, u32[]{:S(2)}) %copy-start) | copy-done | bytes 524312
  10.6 1.0 %copy-done.1 = bf16[128,2048]{1,0:T(8,128)(2,1)S(1)} copy-done((bf16[128,2048]{1,0:T(8,128)(2,1)S(1)}, bf16[128,2048]{1,0:T(8,128)(2,1)}, u32[]{:S(2)}) %copy-start.1) | copy-done | bytes 524312
  11.7 0.9 copy-done.2
  12.6 0.9 copy-done.3
  13.5 6.1 %shard_map.115 = (f32[16,1,384]{2,1,0:T(1,128)S(1)}, bf16[64,256]{1,0:T(8,128)(2,1)S(1)}, f32[64,256]{1,0:T(8,128)S(1)}, bf16[2048,768]{1,0:T(8,128)(2,1)S(1)}, ...) custom-call(f32[16,1,384]{2,1,0:T(1,128)S(1)} %shard_map.113.refs_0_, ...), custom_call_target="tpu_custom_call" | custom-call | flops 2415919104 | bytes 2097152 | tf_op jit(solution)/shard_map/pallas_call | solution.py:170
  19.6 0.1 shard_map.116.refs_3_
  19.7 0.1 collective-permute-start.5
  19.8 1.5 %collective-permute-start.6 = (bf16[256,2048]{1,0:T(8,128)(2,1)S(1)}, bf16[256,2048]{1,0:T(8,128)(2,1)S(1)}, u32[]{:S(2)}, u32[]{:S(2)}) collective-permute-start(bf16[256,2048]{1,0:T(8,128)(2,1)S(1)} %shard_map.116.refs_3_), channel_id=1, source_target_pairs={{0,4},{1,3},{4,8},{5,1},{8,12},{9,5},{12,14},{13,9},{14,10},{15,13... | collective-permute-start | bytes 3145736 | tf_op jit(solution)/shard_map/ppermute | solution.py:378
  21.3 7.1 %collective-permute-done.4.refs_1_ = bf16[256,2048]{1,0:T(8,128)(2,1)S(1)} collective-permute-done((bf16[256,2048]{1,0:T(8,128)(2,1)S(1)}, bf16[256,2048]{1,0:T(8,128)(2,1)S(1)}, u32[]{:S(2)}, u32[]{:S(2)}) %collective-permute-start.4) | collective-permute-done | bytes 1048608 | tf_op jit(solution)/shard_map/ppermute | solution.py:378
  28.4 2.1 %collective-permute-start.8 = (bf16[256,2048]{1,0:T(8,128)(2,1)S(1)}, bf16[256,2048]{1,0:T(8,128)(2,1)S(1)}, u32[]{:S(2)}, u32[]{:S(2)}) collective-permute-start(bf16[256,2048]{1,0:T(8,128)(2,1)S(1)} %collective-permute-done.4.refs_1_), channel_id=1, source_target_pairs={{0,4},{1,3},{4,8},{5,1},{8,12},{9,5},{12,14},{13,9},{14,10},{15,13... | collective-permute-start | bytes 3145736 | tf_op jit(solution)/shard_map/ppermute | solution.py:378
  30.5 4.7 %shard_map.117 = (f32[16,1,384]{2,1,0:T(1,128)S(1)}, bf16[64,384]{1,0:T(8,128)(2,1)S(1)}, f32[64,384]{1,0:T(8,128)S(1)}) custom-call(f32[16,1,384]{2,1,0:T(1,128)S(1)} %get-tuple-element.59.refs_0_, bf16[256,2048]{1,0:T(8,128)(2,1)S(1)} %collective-permute-done.4.refs_1_, bf16[256,2048]{1,0:T(8,128)(2,1)S(1)} %collective-permute-done.5.refs_2_, ...), custom_call_target="tpu_custom_call" | custom-call | flops 3623878656 | bytes 3145728 | tf_op jit(solution)/shard_map/pallas_call | solution.py:170
  35.2 4.4 %collective-permute-done.6.refs_1_ = bf16[256,2048]{1,0:T(8,128)(2,1)S(1)} collective-permute-done((bf16[256,2048]{1,0:T(8,128)(2,1)S(1)}, bf16[256,2048]{1,0:T(8,128)(2,1)S(1)}, u32[]{:S(2)}, u32[]{:S(2)}) %collective-permute-start.6) | collective-permute-done | bytes 1048608 | tf_op jit(solution)/shard_map/ppermute | solution.py:378
  39.6 2.1 %collective-permute-start.10 = (bf16[256,2048]{1,0:T(8,128)(2,1)S(1)}, bf16[256,2048]{1,0:T(8,128)(2,1)S(1)}, u32[]{:S(2)}, u32[]{:S(2)}) collective-permute-start(bf16[256,2048]{1,0:T(8,128)(2,1)S(1)} %collective-permute-done.6.refs_1_), channel_id=1, source_target_pairs={{0,4},{1,3},{4,8},{5,1},{8,12},{9,5},{12,14},{13,9},{14,10},{15,13... | collective-permute-start | bytes 3145736 | tf_op jit(solution)/shard_map/ppermute | solution.py:378
  41.7 3.0 %shard_map.118 = (f32[16,1,384]{2,1,0:T(1,128)S(1)}, bf16[64,256]{1,0:T(8,128)(2,1)S(1)}, f32[64,256]{1,0:T(8,128)S(1)}) custom-call(f32[16,1,384]{2,1,0:T(1,128)S(1)} %get-tuple-element.68.refs_0_, bf16[256,2048]{1,0:T(8,128)(2,1)S(1)} %collective-permute-done.6.refs_1_, bf16[256,2048]{1,0:T(8,128)(2,1)S(1)} %collective-permute-done.7.refs_2_, ...), custom_call_target="tpu_custom_call" | custom-call | flops 2415919104 | bytes 2097152 | tf_op jit(solution)/shard_map/pallas_call | solution.py:170
  44.8 6.1 %collective-permute-done.8.refs_1_ = bf16[256,2048]{1,0:T(8,128)(2,1)S(1)} collective-permute-done((bf16[256,2048]{1,0:T(8,128)(2,1)S(1)}, bf16[256,2048]{1,0:T(8,128)(2,1)S(1)}, u32[]{:S(2)}, u32[]{:S(2)}) %collective-permute-start.8) | collective-permute-done | bytes 1048608 | tf_op jit(solution)/shard_map/ppermute | solution.py:378
  50.8 2.1 %collective-permute-start.12 = (bf16[256,2048]{1,0:T(8,128)(2,1)S(1)}, bf16[256,2048]{1,0:T(8,128)(2,1)S(1)}, u32[]{:S(2)}, u32[]{:S(2)}) collective-permute-start(bf16[256,2048]{1,0:T(8,128)(2,1)S(1)} %collective-permute-done.8.refs_1_), channel_id=1, source_target_pairs={{0,4},{1,3},{4,8},{5,1},{8,12},{9,5},{12,14},{13,9},{14,10},{15,13... | collective-permute-start | bytes 3145736 | tf_op jit(solution)/shard_map/ppermute | solution.py:378
  53.0 3.1 %shard_map.119 = (f32[16,1,384]{2,1,0:T(1,128)S(1)}, bf16[64,256]{1,0:T(8,128)(2,1)S(1)}, f32[64,256]{1,0:T(8,128)S(1)}) custom-call(f32[16,1,384]{2,1,0:T(1,128)S(1)} %get-tuple-element.71.refs_0_, bf16[256,2048]{1,0:T(8,128)(2,1)S(1)} %collective-permute-done.8.refs_1_, bf16[256,2048]{1,0:T(8,128)(2,1)S(1)} %collective-permute-done.9.refs_2_, ...), custom_call_target="tpu_custom_call" | custom-call | flops 2415919104 | bytes 2097152 | tf_op jit(solution)/shard_map/pallas_call | solution.py:170
  56.0 6.1 %collective-permute-done.10.refs_1_.block = bf16[256,2048]{1,0:T(8,128)(2,1)S(1)} collective-permute-done((bf16[256,2048]{1,0:T(8,128)(2,1)S(1)}, bf16[256,2048]{1,0:T(8,128)(2,1)S(1)}, u32[]{:S(2)}, u32[]{:S(2)}) %collective-permute-start.10) | collective-permute-done | bytes 1048608 | tf_op jit(solution)/shard_map/ppermute | solution.py:378
  62.1 0.1 shard_map.122
  62.1 2.2 %collective-permute-start.14 = (bf16[64,2048]{1,0:T(8,128)(2,1)S(1)}, bf16[64,2048]{1,0:T(8,128)(2,1)S(1)}, u32[]{:S(2)}, u32[]{:S(2)}) collective-permute-start(bf16[64,2048]{1,0:T(8,128)(2,1)S(1)} %get-tuple-element.80), channel_id=1, source_target_pairs={{0,4},{1,3},{4,8},{5,1},{8,12},{9,5},{12,14},{13,9},{14,10},{15,13... | collective-permute-start | bytes 786440 | tf_op jit(solution)/shard_map/ppermute | solution.py:378
  64.3 1.6 %collective-permute-start.15 = (bf16[64,2048]{1,0:T(8,128)(2,1)S(1)}, bf16[64,2048]{1,0:T(8,128)(2,1)S(1)}, u32[]{:S(2)}, u32[]{:S(2)}) collective-permute-start(bf16[64,2048]{1,0:T(8,128)(2,1)S(1)} %get-tuple-element.81), channel_id=1, source_target_pairs={{0,4},{1,3},{4,8},{5,1},{8,12},{9,5},{12,14},{13,9},{14,10},{15,13... | collective-permute-start | bytes 786440 | tf_op jit(solution)/shard_map/ppermute | solution.py:378
  65.9 3.0 %shard_map.120 = (f32[16,1,384]{2,1,0:T(1,128)S(1)}, bf16[64,256]{1,0:T(8,128)(2,1)S(1)}, f32[64,256]{1,0:T(8,128)S(1)}) custom-call(f32[16,1,384]{2,1,0:T(1,128)S(1)} %get-tuple-element.74.refs_0_, bf16[256,2048]{1,0:T(8,128)(2,1)S(1)} %collective-permute-done.10.refs_1_.block, bf16[256,2048]{1,0:T(8,128)(2,1)S(1)} %collective-permute-done.11.refs_2_, ...), custom_call_target="tpu_custom_call" | custom-call | flops 2415919104 | bytes 2097152 | tf_op jit(solution)/shard_map/pallas_call | solution.py:170
  68.9 4.4 %collective-permute-done.12.refs_1_.block = bf16[256,2048]{1,0:T(8,128)(2,1)S(1)} collective-permute-done((bf16[256,2048]{1,0:T(8,128)(2,1)S(1)}, bf16[256,2048]{1,0:T(8,128)(2,1)S(1)}, u32[]{:S(2)}, u32[]{:S(2)}) %collective-permute-start.12) | collective-permute-done | bytes 1048608 | tf_op jit(solution)/shard_map/ppermute | solution.py:378
  73.3 0.1 shard_map.123
  73.4 0.1 collective-permute-start.19
  73.5 2.4 %collective-permute-start.20 = (bf16[128,2048]{1,0:T(8,128)(2,1)S(1)}, bf16[128,2048]{1,0:T(8,128)(2,1)S(1)}, u32[]{:S(2)}, u32[]{:S(2)}) collective-permute-start(bf16[128,2048]{1,0:T(8,128)(2,1)S(1)} %get-tuple-element.90), channel_id=1, source_target_pairs={{0,4},{1,3},{4,8},{5,1},{8,12},{9,5},{12,14},{13,9},{14,10},{15,13... | collective-permute-start | bytes 1572872 | tf_op jit(solution)/shard_map/ppermute | solution.py:378
  75.8 3.1 %shard_map.121 = (f32[16,1,384]{2,1,0:T(1,128)S(1)}, bf16[64,256]{1,0:T(8,128)(2,1)S(1)}, f32[64,256]{1,0:T(8,128)S(1)}) custom-call(f32[16,1,384]{2,1,0:T(1,128)S(1)} %get-tuple-element.77.refs_0_, bf16[256,2048]{1,0:T(8,128)(2,1)S(1)} %collective-permute-done.12.refs_1_.block, bf16[256,2048]{1,0:T(8,128)(2,1)S(1)} %collective-permute-done.13.refs_2_, ...), custom_call_target="tpu_custom_call" | custom-call | flops 2415919104 | bytes 2097152 | tf_op jit(solution)/shard_map/pallas_call | solution.py:170
  78.9 0.0 collective-permute-done.15.refs_2_
  78.9 0.1 collective-permute-start.17
  79.0 0.5 collective-permute-start.18
  79.5 0.1 collective-permute-start.16
  79.6 2.3 %shard_map.124 = (bf16[384,768]{1,0:T(8,128)(2,1)S(1)}, bf16[64,256]{1,0:T(8,128)(2,1)S(1)}) custom-call(bf16[128,2048]{1,0:T(8,128)(2,1)S(1)} %collective-permute-done.19.refs_0_, bf16[64,2048]{1,0:T(8,128)(2,1)S(1)} %collective-permute-done.14.refs_1_, bf16[64,2048]{1,0:T(8,128)(2,1)S(1)} %collective-permute-done.15.refs_2_, ...), custom_call_target="tpu_custom_call" | custom-call | tf_op jit(solution)/shard_map/pallas_call | solution.py:206
  81.9 1.5 %shard_map.125 = (bf16[384,768]{1,0:T(8,128)(2,1)S(1)}, bf16[64,128]{1,0:T(8,128)(2,1)S(1)}) custom-call(bf16[64,2048]{1,0:T(8,128)(2,1)S(1)} %collective-permute-done.17.refs_0_, bf16[64,2048]{1,0:T(8,128)(2,1)S(1)} %collective-permute-done.18.refs_1_, ...), custom_call_target="tpu_custom_call", output_to_operand_aliasing={{0}: (5, {})} | custom-call | tf_op jit(solution)/shard_map/pallas_call | solution.py:206
  83.4 1.2 %collective-permute-done.20.refs_2_ = bf16[128,2048]{1,0:T(8,128)(2,1)S(1)} collective-permute-done((bf16[128,2048]{1,0:T(8,128)(2,1)S(1)}, bf16[128,2048]{1,0:T(8,128)(2,1)S(1)}, u32[]{:S(2)}, u32[]{:S(2)}) %collective-permute-start.20) | collective-permute-done | bytes 524320 | tf_op jit(solution)/shard_map/ppermute | solution.py:378
  84.6 1.7 %shard_map.126 = (f32[16,1,384]{2,1,0:T(1,128)S(1)}, f32[64,256]{1,0:T(8,128)S(1)}, f32[128,2048]{1,0:T(8,128)S(1)}) custom-call(f32[16,1,384]{2,1,0:T(1,128)S(1)} %get-tuple-element.82.refs_0_, bf16[128,2048]{1,0:T(8,128)(2,1)S(1)} %collective-permute-done.16.refs_1_, bf16[128,2048]{1,0:T(8,128)(2,1)S(1)} %collective-permute-done.20.refs_2_, ...), custom_call_target="tpu_custom_call" | custom-call | flops 1207959552 | bytes 1048576 | tf_op jit(solution)/shard_map/pallas_call | solution.py:276
  86.3 0.2 collective-permute-done.21.dy
  86.5 0.3 shard_map.127
  86.8 12.8 %all_to_all.5.returned = f32[16,1,384]{2,1,0:T(1,128)S(1)} all-to-all(f32[16,1,384]{2,1,0:T(1,128)S(1)} %get-tuple-element.95), channel_id=1, replica_groups=mesh['grp'=2,'exp'=16] {'exp'}, dimensions={0} | all-to-all | bytes 49152 | tf_op jit(solution)/shard_map/all_to_all | solution.py:468
  99.6 1.1 %shard_map.128 = (f32[256,64]{1,0:T(8,128)}, f32[8,128]{1,0:T(8,128)}) custom-call(f32[16,1,384]{2,1,0:T(1,128)S(1)} %all_to_all.5.returned, s32[8,128]{1,0:T(8,128)S(1)} %bitcast.19, bf16[64,256]{1,0:T(8,128)(2,1)S(1)} %get-tuple-element.96.refs_0_, bf16[64,384]{1,0:T(8,128)(2,1)S(1)} %get-tuple-element.97.refs_1_, ...), custom_call_target="tpu_custom_call" | custom-call | tf_op jit(solution)/shard_map/pallas_call | solution.py:469
  (29 shorter events, 0.1 us)
Async XLA Ops:
  0.6 7.2 %collective-permute-start = (bf16[128,2048]{1,0:T(8,128)(2,1)}, bf16[128,2048]{1,0:T(8,128)(2,1)S(1)}, u32[]{:S(2)}, u32[]{:S(2)}) collective-permute-start(bf16[128,2048]{1,0:T(8,128)(2,1)} %refs_1_.1), channel_id=1, source_target_pairs={{0,1},{1,0},{2,3},{3,2},{4,5},{5,4},{6,7},{7,6},{8,9},{9,8},{10,11... | collective-permute-start | bytes 1572872 | tf_op jit(solution)/shard_map/ppermute | solution.py:381
  1.1 6.7 %collective-permute-start.1 = (bf16[128,2048]{1,0:T(8,128)(2,1)}, bf16[128,2048]{1,0:T(8,128)(2,1)S(1)}, u32[]{:S(2)}, u32[]{:S(2)}) collective-permute-start(bf16[128,2048]{1,0:T(8,128)(2,1)} %refs_2_.1), channel_id=1, source_target_pairs={{0,1},{1,0},{2,3},{3,2},{4,5},{5,4},{6,7},{7,6},{8,9},{9,8},{10,11... | collective-permute-start | bytes 1572872 | tf_op jit(solution)/shard_map/ppermute | solution.py:381
  1.2 18.4 %collective-permute-start.2 = (bf16[128,2048]{1,0:T(8,128)(2,1)}, bf16[128,2048]{1,0:T(8,128)(2,1)S(1)}, u32[]{:S(2)}, u32[]{:S(2)}) collective-permute-start(bf16[128,2048]{1,0:T(8,128)(2,1)} %refs_1_.1), channel_id=1, source_target_pairs={{0,4},{1,3},{4,8},{5,1},{8,12},{9,5},{12,14},{13,9},{14,10},{15,13... | collective-permute-start | bytes 1572872 | tf_op jit(solution)/shard_map/ppermute | solution.py:378
  4.2 15.4 %collective-permute-start.3 = (bf16[128,2048]{1,0:T(8,128)(2,1)}, bf16[128,2048]{1,0:T(8,128)(2,1)S(1)}, u32[]{:S(2)}, u32[]{:S(2)}) collective-permute-start(bf16[128,2048]{1,0:T(8,128)(2,1)} %refs_2_.1), channel_id=1, source_target_pairs={{0,4},{1,3},{4,8},{5,1},{8,12},{9,5},{12,14},{13,9},{14,10},{15,13... | collective-permute-start | bytes 1572872 | tf_op jit(solution)/shard_map/ppermute | solution.py:378
  5.8 0.7 copy-start.4
  6.5 0.7 copy-start.6
  7.2 0.7 copy-start.7
  8.0 20.4 %collective-permute-start.4 = (bf16[256,2048]{1,0:T(8,128)(2,1)S(1)}, bf16[256,2048]{1,0:T(8,128)(2,1)S(1)}, u32[]{:S(2)}, u32[]{:S(2)}) collective-permute-start(bf16[256,2048]{1,0:T(8,128)(2,1)S(1)} %shard_map.114.refs_3_), channel_id=1, source_target_pairs={{0,4},{1,3},{4,8},{5,1},{8,12},{9,5},{12,14},{13,9},{14,10},{15,13... | collective-permute-start | bytes 3145736 | tf_op jit(solution)/shard_map/ppermute | solution.py:378
  9.6 1.0 %copy-start = (bf16[128,2048]{1,0:T(8,128)(2,1)S(1)}, bf16[128,2048]{1,0:T(8,128)(2,1)}, u32[]{:S(2)}) copy-start(bf16[128,2048]{1,0:T(8,128)(2,1)} %refs_1_.1) | copy-start | bytes 1572868
  10.6 1.0 %copy-start.1 = (bf16[128,2048]{1,0:T(8,128)(2,1)S(1)}, bf16[128,2048]{1,0:T(8,128)(2,1)}, u32[]{:S(2)}) copy-start(bf16[128,2048]{1,0:T(8,128)(2,1)} %refs_2_.1) | copy-start | bytes 1572868
  11.7 0.9 copy-start.2
  12.6 0.9 copy-start.3
  19.7 10.8 %collective-permute-start.5 = (bf16[256,2048]{1,0:T(8,128)(2,1)S(1)}, bf16[256,2048]{1,0:T(8,128)(2,1)S(1)}, u32[]{:S(2)}, u32[]{:S(2)}) collective-permute-start(bf16[256,2048]{1,0:T(8,128)(2,1)S(1)} %shard_map.116.refs_3_), channel_id=1, source_target_pairs={{0,1},{1,0},{2,3},{3,2},{4,5},{5,4},{6,7},{7,6},{8,9},{9,8},{10,11... | collective-permute-start | bytes 3145736 | tf_op jit(solution)/shard_map/ppermute | solution.py:381
  19.8 19.8 %collective-permute-start.6 = (bf16[256,2048]{1,0:T(8,128)(2,1)S(1)}, bf16[256,2048]{1,0:T(8,128)(2,1)S(1)}, u32[]{:S(2)}, u32[]{:S(2)}) collective-permute-start(bf16[256,2048]{1,0:T(8,128)(2,1)S(1)} %shard_map.116.refs_3_), channel_id=1, source_target_pairs={{0,4},{1,3},{4,8},{5,1},{8,12},{9,5},{12,14},{13,9},{14,10},{15,13... | collective-permute-start | bytes 3145736 | tf_op jit(solution)/shard_map/ppermute | solution.py:378
  28.4 13.4 %collective-permute-start.7 = (bf16[256,2048]{1,0:T(8,128)(2,1)S(1)}, bf16[256,2048]{1,0:T(8,128)(2,1)S(1)}, u32[]{:S(2)}, u32[]{:S(2)}) collective-permute-start(bf16[256,2048]{1,0:T(8,128)(2,1)S(1)} %collective-permute-done.4.refs_1_), channel_id=1, source_target_pairs={{0,1},{1,0},{2,3},{3,2},{4,5},{5,4},{6,7},{7,6},{8,9},{9,8},{10,11... | collective-permute-start | bytes 3145736 | tf_op jit(solution)/shard_map/ppermute | solution.py:381
  28.4 22.5 %collective-permute-start.8 = (bf16[256,2048]{1,0:T(8,128)(2,1)S(1)}, bf16[256,2048]{1,0:T(8,128)(2,1)S(1)}, u32[]{:S(2)}, u32[]{:S(2)}) collective-permute-start(bf16[256,2048]{1,0:T(8,128)(2,1)S(1)} %collective-permute-done.4.refs_1_), channel_id=1, source_target_pairs={{0,4},{1,3},{4,8},{5,1},{8,12},{9,5},{12,14},{13,9},{14,10},{15,13... | collective-permute-start | bytes 3145736 | tf_op jit(solution)/shard_map/ppermute | solution.py:378
  39.6 13.4 %collective-permute-start.9 = (bf16[256,2048]{1,0:T(8,128)(2,1)S(1)}, bf16[256,2048]{1,0:T(8,128)(2,1)S(1)}, u32[]{:S(2)}, u32[]{:S(2)}) collective-permute-start(bf16[256,2048]{1,0:T(8,128)(2,1)S(1)} %collective-permute-done.6.refs_1_), channel_id=1, source_target_pairs={{0,1},{1,0},{2,3},{3,2},{4,5},{5,4},{6,7},{7,6},{8,9},{9,8},{10,11... | collective-permute-start | bytes 3145736 | tf_op jit(solution)/shard_map/ppermute | solution.py:381
  39.6 22.5 %collective-permute-start.10 = (bf16[256,2048]{1,0:T(8,128)(2,1)S(1)}, bf16[256,2048]{1,0:T(8,128)(2,1)S(1)}, u32[]{:S(2)}, u32[]{:S(2)}) collective-permute-start(bf16[256,2048]{1,0:T(8,128)(2,1)S(1)} %collective-permute-done.6.refs_1_), channel_id=1, source_target_pairs={{0,4},{1,3},{4,8},{5,1},{8,12},{9,5},{12,14},{13,9},{14,10},{15,13... | collective-permute-start | bytes 3145736 | tf_op jit(solution)/shard_map/ppermute | solution.py:378
  50.8 15.1 %collective-permute-start.11 = (bf16[256,2048]{1,0:T(8,128)(2,1)S(1)}, bf16[256,2048]{1,0:T(8,128)(2,1)S(1)}, u32[]{:S(2)}, u32[]{:S(2)}) collective-permute-start(bf16[256,2048]{1,0:T(8,128)(2,1)S(1)} %collective-permute-done.8.refs_1_), channel_id=1, source_target_pairs={{0,1},{1,0},{2,3},{3,2},{4,5},{5,4},{6,7},{7,6},{8,9},{9,8},{10,11... | collective-permute-start | bytes 3145736 | tf_op jit(solution)/shard_map/ppermute | solution.py:381
  50.8 22.5 %collective-permute-start.12 = (bf16[256,2048]{1,0:T(8,128)(2,1)S(1)}, bf16[256,2048]{1,0:T(8,128)(2,1)S(1)}, u32[]{:S(2)}, u32[]{:S(2)}) collective-permute-start(bf16[256,2048]{1,0:T(8,128)(2,1)S(1)} %collective-permute-done.8.refs_1_), channel_id=1, source_target_pairs={{0,4},{1,3},{4,8},{5,1},{8,12},{9,5},{12,14},{13,9},{14,10},{15,13... | collective-permute-start | bytes 3145736 | tf_op jit(solution)/shard_map/ppermute | solution.py:378
  62.1 13.8 %collective-permute-start.13 = (bf16[256,2048]{1,0:T(8,128)(2,1)S(1)}, bf16[256,2048]{1,0:T(8,128)(2,1)S(1)}, u32[]{:S(2)}, u32[]{:S(2)}) collective-permute-start(bf16[256,2048]{1,0:T(8,128)(2,1)S(1)} %collective-permute-done.10.refs_1_.block), channel_id=1, source_target_pairs={{0,1},{1,0},{2,3},{3,2},{4,5},{5,4},{6,7},{7,6},{8,9},{9,8},{10,11... | collective-permute-start | bytes 3145736 | tf_op jit(solution)/shard_map/ppermute | solution.py:381
  62.1 16.8 %collective-permute-start.14 = (bf16[64,2048]{1,0:T(8,128)(2,1)S(1)}, bf16[64,2048]{1,0:T(8,128)(2,1)S(1)}, u32[]{:S(2)}, u32[]{:S(2)}) collective-permute-start(bf16[64,2048]{1,0:T(8,128)(2,1)S(1)} %get-tuple-element.80), channel_id=1, source_target_pairs={{0,4},{1,3},{4,8},{5,1},{8,12},{9,5},{12,14},{13,9},{14,10},{15,13... | collective-permute-start | bytes 786440 | tf_op jit(solution)/shard_map/ppermute | solution.py:378
  64.3 14.6 %collective-permute-start.15 = (bf16[64,2048]{1,0:T(8,128)(2,1)S(1)}, bf16[64,2048]{1,0:T(8,128)(2,1)S(1)}, u32[]{:S(2)}, u32[]{:S(2)}) collective-permute-start(bf16[64,2048]{1,0:T(8,128)(2,1)S(1)} %get-tuple-element.81), channel_id=1, source_target_pairs={{0,4},{1,3},{4,8},{5,1},{8,12},{9,5},{12,14},{13,9},{14,10},{15,13... | collective-permute-start | bytes 786440 | tf_op jit(solution)/shard_map/ppermute | solution.py:378
  73.4 6.2 %collective-permute-start.19 = (bf16[128,2048]{1,0:T(8,128)(2,1)S(1)}, bf16[128,2048]{1,0:T(8,128)(2,1)S(1)}, u32[]{:S(2)}, u32[]{:S(2)}) collective-permute-start(bf16[128,2048]{1,0:T(8,128)(2,1)S(1)} %get-tuple-element.86), channel_id=1, source_target_pairs={{0,1},{1,0},{2,3},{3,2},{4,5},{5,4},{6,7},{7,6},{8,9},{9,8},{10,11... | collective-permute-start | bytes 1572872 | tf_op jit(solution)/shard_map/ppermute | solution.py:381
  73.5 11.1 %collective-permute-start.20 = (bf16[128,2048]{1,0:T(8,128)(2,1)S(1)}, bf16[128,2048]{1,0:T(8,128)(2,1)S(1)}, u32[]{:S(2)}, u32[]{:S(2)}) collective-permute-start(bf16[128,2048]{1,0:T(8,128)(2,1)S(1)} %get-tuple-element.90), channel_id=1, source_target_pairs={{0,4},{1,3},{4,8},{5,1},{8,12},{9,5},{12,14},{13,9},{14,10},{15,13... | collective-permute-start | bytes 1572872 | tf_op jit(solution)/shard_map/ppermute | solution.py:378
  78.9 2.9 %collective-permute-start.17 = (bf16[64,2048]{1,0:T(8,128)(2,1)S(1)}, bf16[64,2048]{1,0:T(8,128)(2,1)S(1)}, u32[]{:S(2)}, u32[]{:S(2)}) collective-permute-start(bf16[64,2048]{1,0:T(8,128)(2,1)S(1)} %collective-permute-done.14.refs_1_), channel_id=1, source_target_pairs={{0,1},{1,0},{2,3},{3,2},{4,5},{5,4},{6,7},{7,6},{8,9},{9,8},{10,11... | collective-permute-start | bytes 786440 | tf_op jit(solution)/shard_map/ppermute | solution.py:381
  79.0 2.9 %collective-permute-start.18 = (bf16[64,2048]{1,0:T(8,128)(2,1)S(1)}, bf16[64,2048]{1,0:T(8,128)(2,1)S(1)}, u32[]{:S(2)}, u32[]{:S(2)}) collective-permute-start(bf16[64,2048]{1,0:T(8,128)(2,1)S(1)} %collective-permute-done.15.refs_2_), channel_id=1, source_target_pairs={{0,1},{1,0},{2,3},{3,2},{4,5},{5,4},{6,7},{7,6},{8,9},{9,8},{10,11... | collective-permute-start | bytes 786440 | tf_op jit(solution)/shard_map/ppermute | solution.py:381
  79.5 5.0 %collective-permute-start.16 = (bf16[128,2048]{1,0:T(8,128)(2,1)S(1)}, bf16[128,2048]{1,0:T(8,128)(2,1)S(1)}, u32[]{:S(2)}, u32[]{:S(2)}) collective-permute-start(bf16[128,2048]{1,0:T(8,128)(2,1)S(1)} %get-tuple-element.83), channel_id=1, source_target_pairs={{0,1},{1,0},{2,3},{3,2},{4,5},{5,4},{6,7},{7,6},{8,9},{9,8},{10,11... | collective-permute-start | bytes 1572872 | tf_op jit(solution)/shard_map/ppermute | solution.py:381
  84.5 15.1 %copy-start.5 = (s32[128,8]{0,1:T(8,128)S(1)}, s32[128,8]{0,1:T(8,128)}, u32[]{:S(2)}) copy-start(s32[128,8]{0,1:T(8,128)} %param.12) | copy-start | bytes 12292
  84.5 1.9 %collective-permute-start.21 = (bf16[128,2048]{1,0:T(8,128)(2,1)S(1)}, bf16[128,2048]{1,0:T(8,128)(2,1)S(1)}, u32[]{:S(2)}, u32[]{:S(2)}) collective-permute-start(bf16[128,2048]{1,0:T(8,128)(2,1)S(1)} %collective-permute-done.20.refs_2_), channel_id=1, source_target_pairs={{0,1},{1,0},{2,3},{3,2},{4,5},{5,4},{6,7},{7,6},{8,9},{9,8},{10,11... | collective-permute-start | bytes 1572872 | tf_op jit(solution)/shard_map/ppermute | solution.py:381

commit v22 on v21

--- a/solution.py
+++ b/solution.py
@@ -249,7 +249,6 @@
             dy = dy_in[i][:, part].astype(jnp.float32)
             totals[i] += fold(dy * out_val[i * rows : (i + 1) * rows, :])
         rest[:, part] = out_val[blocks * rows :, :]
-    sheet[...] = sheet_in[...]
     for i in range(blocks):
         enter(sheet, names[i], totals[i])
         proj_cot[:, i * rows : (i + 1) * rows] = lax.dot_general(
@@ -264,7 +263,6 @@
     for cut in range(0, width, tile):
         part = pl.ds(cut, tile)
         total += fold(dy[:, part].astype(jnp.float32) * out_val[:, part])
-    sheet[...] = sheet_in[...]
     enter(sheet, name, total)
     proj_cot[...] = lax.dot_general(
         high_proj[...], dy[...], (((1,), (1,)), ((), ())), preferred_element_type=jnp.float32
@@ -278,6 +276,7 @@
         out_shape=[jax.ShapeDtypeStruct(shape, jnp.float32) for shape in out_shape],
         in_specs=[inside] * len(args),
         out_specs=[inside] * len(out_shape),
+        input_output_aliases={0: 0},
         compiler_params=pltpu.CompilerParams(vmem_limit_bytes=16 * 1024 * 1024),
         cost_estimate=pl.CostEstimate(flops=flops, bytes_accessed=2**20, transcendentals=0),
     )(*args)

time: 101 us -> 101 us (level)
  no operation moved by 1% of the time
where the time goes in v22:
time: 101 us
  Pallas kernels  30.2 us (30%)
  waiting for transfers between devices  29.3 us (29%)
  starting transfers between devices  21.6 us (21%)
  blocking collectives  12.8 us (13%)
  local copies, waits for them, and re-layouts  5.95 us (6%)
    ppermute x10, waiting for transfers between devices, hop(): return lax.ppermute(block, 'exp', onward)  29.1 us
    pallas_call x6, Pallas kernels, work(): return call(sheet, *apart, *block_in, *weights)  23 us
    ppermute x10, starting transfers between devices, hop(): return lax.ppermute(block, 'exp', onward)  20.2 us
    all_to_all x1, blocking collectives, by_ring(): lax.all_to_all(sheet, 'exp', split_axis=0, concat_axis=0, tiled=True)  12.8 us
    unnamed x16, local copies, waits for them, and re-layouts  5.95 us
    pallas_call x2, Pallas kernels, front(): pl.pallas_call(kernel, out_shape=[jax.ShapeDtypeStruct((room, units), jnp...  3.75 us
    pallas_call x2, Pallas kernels, on_core(): pl.pallas_call(kernel, out_shape=[jax.ShapeDtypeStruct(shape, jnp.float32...  2.06 us
  transfers between devices with their start and end apart: 22, of which 7 were waited for; matrix products, arithmetic and copies ran while one was open for 0% of the time, Pallas kernels for 29%

profile of v22, /device:TPU:0, one launch (start us, length us, event | category | flops | bytes accessed | tf_op | source)
XLA Modules:
  0.0 100.7 jit_solution(17280702160795820488)
XLA Ops:
  0.6 0.5 collective-permute-start
  1.1 0.1 collective-permute-start.1
  1.2 3.0 %collective-permute-start.2 = (bf16[128,2048]{1,0:T(8,128)(2,1)}, bf16[128,2048]{1,0:T(8,128)(2,1)S(1)}, u32[]{:S(2)}, u32[]{:S(2)}) collective-permute-start(bf16[128,2048]{1,0:T(8,128)(2,1)} %refs_1_.1), channel_id=1, source_target_pairs={{0,4},{1,3},{4,8},{5,1},{8,12},{9,5},{12,14},{13,9},{14,10},{15,13... | collective-permute-start | bytes 1572872 | tf_op jit(solution)/shard_map/ppermute | solution.py:377
  4.2 1.6 %collective-permute-start.3 = (bf16[128,2048]{1,0:T(8,128)(2,1)}, bf16[128,2048]{1,0:T(8,128)(2,1)S(1)}, u32[]{:S(2)}, u32[]{:S(2)}) collective-permute-start(bf16[128,2048]{1,0:T(8,128)(2,1)} %refs_2_.1), channel_id=1, source_target_pairs={{0,4},{1,3},{4,8},{5,1},{8,12},{9,5},{12,14},{13,9},{14,10},{15,13... | collective-permute-start | bytes 1572872 | tf_op jit(solution)/shard_map/ppermute | solution.py:377
  5.8 0.7 copy-done.4
  6.5 0.7 copy-done.6
  7.2 0.7 copy-done.7
  7.9 0.1 shard_map.114.refs_3_
  8.0 1.6 %collective-permute-start.4 = (bf16[256,2048]{1,0:T(8,128)(2,1)S(1)}, bf16[256,2048]{1,0:T(8,128)(2,1)S(1)}, u32[]{:S(2)}, u32[]{:S(2)}) collective-permute-start(bf16[256,2048]{1,0:T(8,128)(2,1)S(1)} %shard_map.114.refs_3_), channel_id=1, source_target_pairs={{0,4},{1,3},{4,8},{5,1},{8,12},{9,5},{12,14},{13,9},{14,10},{15,13... | collective-permute-start | bytes 3145736 | tf_op jit(solution)/shard_map/ppermute | solution.py:377
  9.6 1.0 %copy-done = bf16[128,2048]{1,0:T(8,128)(2,1)S(1)} copy-done((bf16[128,2048]{1,0:T(8,128)(2,1)S(1)}, bf16[128,2048]{1,0:T(8,128)(2,1)}, u32[]{:S(2)}) %copy-start) | copy-done | bytes 524312
  10.6 1.0 %copy-done.1 = bf16[128,2048]{1,0:T(8,128)(2,1)S(1)} copy-done((bf16[128,2048]{1,0:T(8,128)(2,1)S(1)}, bf16[128,2048]{1,0:T(8,128)(2,1)}, u32[]{:S(2)}) %copy-start.1) | copy-done | bytes 524312
  11.7 0.9 copy-done.2
  12.6 0.9 copy-done.3
  13.5 6.1 %shard_map.115 = (f32[16,1,384]{2,1,0:T(1,128)S(1)}, bf16[64,256]{1,0:T(8,128)(2,1)S(1)}, f32[64,256]{1,0:T(8,128)S(1)}, bf16[2048,768]{1,0:T(8,128)(2,1)S(1)}, ...) custom-call(f32[16,1,384]{2,1,0:T(1,128)S(1)} %shard_map.113.refs_0_, ...), custom_call_target="tpu_custom_call" | custom-call | flops 2415919104 | bytes 2097152 | tf_op jit(solution)/shard_map/pallas_call | solution.py:170
  19.6 0.1 shard_map.116.refs_3_
  19.7 0.1 collective-permute-start.5
  19.8 1.5 %collective-permute-start.6 = (bf16[256,2048]{1,0:T(8,128)(2,1)S(1)}, bf16[256,2048]{1,0:T(8,128)(2,1)S(1)}, u32[]{:S(2)}, u32[]{:S(2)}) collective-permute-start(bf16[256,2048]{1,0:T(8,128)(2,1)S(1)} %shard_map.116.refs_3_), channel_id=1, source_target_pairs={{0,4},{1,3},{4,8},{5,1},{8,12},{9,5},{12,14},{13,9},{14,10},{15,13... | collective-permute-start | bytes 3145736 | tf_op jit(solution)/shard_map/ppermute | solution.py:377
  21.3 7.1 %collective-permute-done.4.refs_1_ = bf16[256,2048]{1,0:T(8,128)(2,1)S(1)} collective-permute-done((bf16[256,2048]{1,0:T(8,128)(2,1)S(1)}, bf16[256,2048]{1,0:T(8,128)(2,1)S(1)}, u32[]{:S(2)}, u32[]{:S(2)}) %collective-permute-start.4) | collective-permute-done | bytes 1048608 | tf_op jit(solution)/shard_map/ppermute | solution.py:377
  28.4 2.1 %collective-permute-start.8 = (bf16[256,2048]{1,0:T(8,128)(2,1)S(1)}, bf16[256,2048]{1,0:T(8,128)(2,1)S(1)}, u32[]{:S(2)}, u32[]{:S(2)}) collective-permute-start(bf16[256,2048]{1,0:T(8,128)(2,1)S(1)} %collective-permute-done.4.refs_1_), channel_id=1, source_target_pairs={{0,4},{1,3},{4,8},{5,1},{8,12},{9,5},{12,14},{13,9},{14,10},{15,13... | collective-permute-start | bytes 3145736 | tf_op jit(solution)/shard_map/ppermute | solution.py:377
  30.5 4.7 %shard_map.117 = (f32[16,1,384]{2,1,0:T(1,128)S(1)}, bf16[64,384]{1,0:T(8,128)(2,1)S(1)}, f32[64,384]{1,0:T(8,128)S(1)}) custom-call(f32[16,1,384]{2,1,0:T(1,128)S(1)} %get-tuple-element.59.refs_0_, bf16[256,2048]{1,0:T(8,128)(2,1)S(1)} %collective-permute-done.4.refs_1_, bf16[256,2048]{1,0:T(8,128)(2,1)S(1)} %collective-permute-done.5.refs_2_, ...), custom_call_target="tpu_custom_call" | custom-call | flops 3623878656 | bytes 3145728 | tf_op jit(solution)/shard_map/pallas_call | solution.py:170
  35.2 4.4 %collective-permute-done.6.refs_1_ = bf16[256,2048]{1,0:T(8,128)(2,1)S(1)} collective-permute-done((bf16[256,2048]{1,0:T(8,128)(2,1)S(1)}, bf16[256,2048]{1,0:T(8,128)(2,1)S(1)}, u32[]{:S(2)}, u32[]{:S(2)}) %collective-permute-start.6) | collective-permute-done | bytes 1048608 | tf_op jit(solution)/shard_map/ppermute | solution.py:377
  39.6 2.1 %collective-permute-start.10 = (bf16[256,2048]{1,0:T(8,128)(2,1)S(1)}, bf16[256,2048]{1,0:T(8,128)(2,1)S(1)}, u32[]{:S(2)}, u32[]{:S(2)}) collective-permute-start(bf16[256,2048]{1,0:T(8,128)(2,1)S(1)} %collective-permute-done.6.refs_1_), channel_id=1, source_target_pairs={{0,4},{1,3},{4,8},{5,1},{8,12},{9,5},{12,14},{13,9},{14,10},{15,13... | collective-permute-start | bytes 3145736 | tf_op jit(solution)/shard_map/ppermute | solution.py:377
  41.7 3.0 %shard_map.118 = (f32[16,1,384]{2,1,0:T(1,128)S(1)}, bf16[64,256]{1,0:T(8,128)(2,1)S(1)}, f32[64,256]{1,0:T(8,128)S(1)}) custom-call(f32[16,1,384]{2,1,0:T(1,128)S(1)} %get-tuple-element.68.refs_0_, bf16[256,2048]{1,0:T(8,128)(2,1)S(1)} %collective-permute-done.6.refs_1_, bf16[256,2048]{1,0:T(8,128)(2,1)S(1)} %collective-permute-done.7.refs_2_, ...), custom_call_target="tpu_custom_call" | custom-call | flops 2415919104 | bytes 2097152 | tf_op jit(solution)/shard_map/pallas_call | solution.py:170
  44.8 6.1 %collective-permute-done.8.refs_1_ = bf16[256,2048]{1,0:T(8,128)(2,1)S(1)} collective-permute-done((bf16[256,2048]{1,0:T(8,128)(2,1)S(1)}, bf16[256,2048]{1,0:T(8,128)(2,1)S(1)}, u32[]{:S(2)}, u32[]{:S(2)}) %collective-permute-start.8) | collective-permute-done | bytes 1048608 | tf_op jit(solution)/shard_map/ppermute | solution.py:377
  50.8 2.1 %collective-permute-start.12 = (bf16[256,2048]{1,0:T(8,128)(2,1)S(1)}, bf16[256,2048]{1,0:T(8,128)(2,1)S(1)}, u32[]{:S(2)}, u32[]{:S(2)}) collective-permute-start(bf16[256,2048]{1,0:T(8,128)(2,1)S(1)} %collective-permute-done.8.refs_1_), channel_id=1, source_target_pairs={{0,4},{1,3},{4,8},{5,1},{8,12},{9,5},{12,14},{13,9},{14,10},{15,13... | collective-permute-start | bytes 3145736 | tf_op jit(solution)/shard_map/ppermute | solution.py:377
  53.0 3.1 %shard_map.119 = (f32[16,1,384]{2,1,0:T(1,128)S(1)}, bf16[64,256]{1,0:T(8,128)(2,1)S(1)}, f32[64,256]{1,0:T(8,128)S(1)}) custom-call(f32[16,1,384]{2,1,0:T(1,128)S(1)} %get-tuple-element.71.refs_0_, bf16[256,2048]{1,0:T(8,128)(2,1)S(1)} %collective-permute-done.8.refs_1_, bf16[256,2048]{1,0:T(8,128)(2,1)S(1)} %collective-permute-done.9.refs_2_, ...), custom_call_target="tpu_custom_call" | custom-call | flops 2415919104 | bytes 2097152 | tf_op jit(solution)/shard_map/pallas_call | solution.py:170
  56.0 6.1 %collective-permute-done.10.refs_1_.block = bf16[256,2048]{1,0:T(8,128)(2,1)S(1)} collective-permute-done((bf16[256,2048]{1,0:T(8,128)(2,1)S(1)}, bf16[256,2048]{1,0:T(8,128)(2,1)S(1)}, u32[]{:S(2)}, u32[]{:S(2)}) %collective-permute-start.10) | collective-permute-done | bytes 1048608 | tf_op jit(solution)/shard_map/ppermute | solution.py:377
  62.1 0.1 shard_map.122
  62.1 2.2 %collective-permute-start.14 = (bf16[64,2048]{1,0:T(8,128)(2,1)S(1)}, bf16[64,2048]{1,0:T(8,128)(2,1)S(1)}, u32[]{:S(2)}, u32[]{:S(2)}) collective-permute-start(bf16[64,2048]{1,0:T(8,128)(2,1)S(1)} %get-tuple-element.80), channel_id=1, source_target_pairs={{0,4},{1,3},{4,8},{5,1},{8,12},{9,5},{12,14},{13,9},{14,10},{15,13... | collective-permute-start | bytes 786440 | tf_op jit(solution)/shard_map/ppermute | solution.py:377
  64.3 1.6 %collective-permute-start.15 = (bf16[64,2048]{1,0:T(8,128)(2,1)S(1)}, bf16[64,2048]{1,0:T(8,128)(2,1)S(1)}, u32[]{:S(2)}, u32[]{:S(2)}) collective-permute-start(bf16[64,2048]{1,0:T(8,128)(2,1)S(1)} %get-tuple-element.81), channel_id=1, source_target_pairs={{0,4},{1,3},{4,8},{5,1},{8,12},{9,5},{12,14},{13,9},{14,10},{15,13... | collective-permute-start | bytes 786440 | tf_op jit(solution)/shard_map/ppermute | solution.py:377
  65.9 3.0 %shard_map.120 = (f32[16,1,384]{2,1,0:T(1,128)S(1)}, bf16[64,256]{1,0:T(8,128)(2,1)S(1)}, f32[64,256]{1,0:T(8,128)S(1)}) custom-call(f32[16,1,384]{2,1,0:T(1,128)S(1)} %get-tuple-element.74.refs_0_, bf16[256,2048]{1,0:T(8,128)(2,1)S(1)} %collective-permute-done.10.refs_1_.block, bf16[256,2048]{1,0:T(8,128)(2,1)S(1)} %collective-permute-done.11.refs_2_, ...), custom_call_target="tpu_custom_call" | custom-call | flops 2415919104 | bytes 2097152 | tf_op jit(solution)/shard_map/pallas_call | solution.py:170
  68.9 4.4 %collective-permute-done.12.refs_1_.block = bf16[256,2048]{1,0:T(8,128)(2,1)S(1)} collective-permute-done((bf16[256,2048]{1,0:T(8,128)(2,1)S(1)}, bf16[256,2048]{1,0:T(8,128)(2,1)S(1)}, u32[]{:S(2)}, u32[]{:S(2)}) %collective-permute-start.12) | collective-permute-done | bytes 1048608 | tf_op jit(solution)/shard_map/ppermute | solution.py:377
  73.3 0.1 shard_map.123
  73.4 0.1 collective-permute-start.19
  73.5 2.4 %collective-permute-start.20 = (bf16[128,2048]{1,0:T(8,128)(2,1)S(1)}, bf16[128,2048]{1,0:T(8,128)(2,1)S(1)}, u32[]{:S(2)}, u32[]{:S(2)}) collective-permute-start(bf16[128,2048]{1,0:T(8,128)(2,1)S(1)} %get-tuple-element.90), channel_id=1, source_target_pairs={{0,4},{1,3},{4,8},{5,1},{8,12},{9,5},{12,14},{13,9},{14,10},{15,13... | collective-permute-start | bytes 1572872 | tf_op jit(solution)/shard_map/ppermute | solution.py:377
  75.8 3.1 %shard_map.121 = (f32[16,1,384]{2,1,0:T(1,128)S(1)}, bf16[64,256]{1,0:T(8,128)(2,1)S(1)}, f32[64,256]{1,0:T(8,128)S(1)}) custom-call(f32[16,1,384]{2,1,0:T(1,128)S(1)} %get-tuple-element.77.refs_0_, bf16[256,2048]{1,0:T(8,128)(2,1)S(1)} %collective-permute-done.12.refs_1_.block, bf16[256,2048]{1,0:T(8,128)(2,1)S(1)} %collective-permute-done.13.refs_2_, ...), custom_call_target="tpu_custom_call" | custom-call | flops 2415919104 | bytes 2097152 | tf_op jit(solution)/shard_map/pallas_call | solution.py:170
  78.9 0.0 collective-permute-done.15.refs_2_
  78.9 0.1 collective-permute-start.17
  79.0 0.5 collective-permute-start.18
  79.5 0.1 collective-permute-start.16
  79.6 2.3 %shard_map.124 = (bf16[384,768]{1,0:T(8,128)(2,1)S(1)}, bf16[64,256]{1,0:T(8,128)(2,1)S(1)}) custom-call(bf16[128,2048]{1,0:T(8,128)(2,1)S(1)} %collective-permute-done.19.refs_0_, bf16[64,2048]{1,0:T(8,128)(2,1)S(1)} %collective-permute-done.14.refs_1_, bf16[64,2048]{1,0:T(8,128)(2,1)S(1)} %collective-permute-done.15.refs_2_, ...), custom_call_target="tpu_custom_call" | custom-call | tf_op jit(solution)/shard_map/pallas_call | solution.py:206
  81.9 1.5 %shard_map.125 = (bf16[384,768]{1,0:T(8,128)(2,1)S(1)}, bf16[64,128]{1,0:T(8,128)(2,1)S(1)}) custom-call(bf16[64,2048]{1,0:T(8,128)(2,1)S(1)} %collective-permute-done.17.refs_0_, bf16[64,2048]{1,0:T(8,128)(2,1)S(1)} %collective-permute-done.18.refs_1_, ...), custom_call_target="tpu_custom_call", output_to_operand_aliasing={{0}: (5, {})} | custom-call | tf_op jit(solution)/shard_map/pallas_call | solution.py:206
  83.4 1.2 %collective-permute-done.20.refs_2_ = bf16[128,2048]{1,0:T(8,128)(2,1)S(1)} collective-permute-done((bf16[128,2048]{1,0:T(8,128)(2,1)S(1)}, bf16[128,2048]{1,0:T(8,128)(2,1)S(1)}, u32[]{:S(2)}, u32[]{:S(2)}) %collective-permute-start.20) | collective-permute-done | bytes 524320 | tf_op jit(solution)/shard_map/ppermute | solution.py:377
  84.6 1.7 %shard_map.126 = (f32[16,1,384]{2,1,0:T(1,128)S(1)}, f32[64,256]{1,0:T(8,128)S(1)}, f32[128,2048]{1,0:T(8,128)S(1)}) custom-call(f32[16,1,384]{2,1,0:T(1,128)S(1)} %get-tuple-element.82.refs_0_, bf16[128,2048]{1,0:T(8,128)(2,1)S(1)} %collective-permute-done.16.refs_1_, ...), custom_call_target="tpu_custom_call", output_to_operand_aliasing={{0}: (0, {})} | custom-call | flops 1207959552 | bytes 1048576 | tf_op jit(solution)/shard_map/pallas_call | solution.py:274
  86.3 0.2 collective-permute-done.21.dy
  86.5 0.3 shard_map.127
  86.8 12.8 %all_to_all.5.returned = f32[16,1,384]{2,1,0:T(1,128)S(1)} all-to-all(f32[16,1,384]{2,1,0:T(1,128)S(1)} %get-tuple-element.95), channel_id=1, replica_groups=mesh['grp'=2,'exp'=16] {'exp'}, dimensions={0} | all-to-all | bytes 49152 | tf_op jit(solution)/shard_map/all_to_all | solution.py:467
  99.6 1.1 %shard_map.128 = (f32[256,64]{1,0:T(8,128)}, f32[8,128]{1,0:T(8,128)}) custom-call(f32[16,1,384]{2,1,0:T(1,128)S(1)} %all_to_all.5.returned, s32[8,128]{1,0:T(8,128)S(1)} %bitcast.19, bf16[64,256]{1,0:T(8,128)(2,1)S(1)} %get-tuple-element.96.refs_0_, bf16[64,384]{1,0:T(8,128)(2,1)S(1)} %get-tuple-element.97.refs_1_, ...), custom_call_target="tpu_custom_call" | custom-call | tf_op jit(solution)/shard_map/pallas_call | solution.py:468
  (29 shorter events, 0.1 us)
Async XLA Ops:
  0.6 7.2 %collective-permute-start = (bf16[128,2048]{1,0:T(8,128)(2,1)}, bf16[128,2048]{1,0:T(8,128)(2,1)S(1)}, u32[]{:S(2)}, u32[]{:S(2)}) collective-permute-start(bf16[128,2048]{1,0:T(8,128)(2,1)} %refs_1_.1), channel_id=1, source_target_pairs={{0,1},{1,0},{2,3},{3,2},{4,5},{5,4},{6,7},{7,6},{8,9},{9,8},{10,11... | collective-permute-start | bytes 1572872 | tf_op jit(solution)/shard_map/ppermute | solution.py:380
  1.1 6.7 %collective-permute-start.1 = (bf16[128,2048]{1,0:T(8,128)(2,1)}, bf16[128,2048]{1,0:T(8,128)(2,1)S(1)}, u32[]{:S(2)}, u32[]{:S(2)}) collective-permute-start(bf16[128,2048]{1,0:T(8,128)(2,1)} %refs_2_.1), channel_id=1, source_target_pairs={{0,1},{1,0},{2,3},{3,2},{4,5},{5,4},{6,7},{7,6},{8,9},{9,8},{10,11... | collective-permute-start | bytes 1572872 | tf_op jit(solution)/shard_map/ppermute | solution.py:380
  1.2 18.4 %collective-permute-start.2 = (bf16[128,2048]{1,0:T(8,128)(2,1)}, bf16[128,2048]{1,0:T(8,128)(2,1)S(1)}, u32[]{:S(2)}, u32[]{:S(2)}) collective-permute-start(bf16[128,2048]{1,0:T(8,128)(2,1)} %refs_1_.1), channel_id=1, source_target_pairs={{0,4},{1,3},{4,8},{5,1},{8,12},{9,5},{12,14},{13,9},{14,10},{15,13... | collective-permute-start | bytes 1572872 | tf_op jit(solution)/shard_map/ppermute | solution.py:377
  4.2 15.4 %collective-permute-start.3 = (bf16[128,2048]{1,0:T(8,128)(2,1)}, bf16[128,2048]{1,0:T(8,128)(2,1)S(1)}, u32[]{:S(2)}, u32[]{:S(2)}) collective-permute-start(bf16[128,2048]{1,0:T(8,128)(2,1)} %refs_2_.1), channel_id=1, source_target_pairs={{0,4},{1,3},{4,8},{5,1},{8,12},{9,5},{12,14},{13,9},{14,10},{15,13... | collective-permute-start | bytes 1572872 | tf_op jit(solution)/shard_map/ppermute | solution.py:377
  5.8 0.7 copy-start.4
  6.5 0.7 copy-start.6
  7.2 0.7 copy-start.7
  8.0 20.4 %collective-permute-start.4 = (bf16[256,2048]{1,0:T(8,128)(2,1)S(1)}, bf16[256,2048]{1,0:T(8,128)(2,1)S(1)}, u32[]{:S(2)}, u32[]{:S(2)}) collective-permute-start(bf16[256,2048]{1,0:T(8,128)(2,1)S(1)} %shard_map.114.refs_3_), channel_id=1, source_target_pairs={{0,4},{1,3},{4,8},{5,1},{8,12},{9,5},{12,14},{13,9},{14,10},{15,13... | collective-permute-start | bytes 3145736 | tf_op jit(solution)/shard_map/ppermute | solution.py:377
  9.6 1.0 %copy-start = (bf16[128,2048]{1,0:T(8,128)(2,1)S(1)}, bf16[128,2048]{1,0:T(8,128)(2,1)}, u32[]{:S(2)}) copy-start(bf16[128,2048]{1,0:T(8,128)(2,1)} %refs_1_.1) | copy-start | bytes 1572868
  10.6 1.0 %copy-start.1 = (bf16[128,2048]{1,0:T(8,128)(2,1)S(1)}, bf16[128,2048]{1,0:T(8,128)(2,1)}, u32[]{:S(2)}) copy-start(bf16[128,2048]{1,0:T(8,128)(2,1)} %refs_2_.1) | copy-start | bytes 1572868
  11.7 0.9 copy-start.2
  12.6 0.9 copy-start.3
  19.7 10.8 %collective-permute-start.5 = (bf16[256,2048]{1,0:T(8,128)(2,1)S(1)}, bf16[256,2048]{1,0:T(8,128)(2,1)S(1)}, u32[]{:S(2)}, u32[]{:S(2)}) collective-permute-start(bf16[256,2048]{1,0:T(8,128)(2,1)S(1)} %shard_map.116.refs_3_), channel_id=1, source_target_pairs={{0,1},{1,0},{2,3},{3,2},{4,5},{5,4},{6,7},{7,6},{8,9},{9,8},{10,11... | collective-permute-start | bytes 3145736 | tf_op jit(solution)/shard_map/ppermute | solution.py:380
  19.8 19.8 %collective-permute-start.6 = (bf16[256,2048]{1,0:T(8,128)(2,1)S(1)}, bf16[256,2048]{1,0:T(8,128)(2,1)S(1)}, u32[]{:S(2)}, u32[]{:S(2)}) collective-permute-start(bf16[256,2048]{1,0:T(8,128)(2,1)S(1)} %shard_map.116.refs_3_), channel_id=1, source_target_pairs={{0,4},{1,3},{4,8},{5,1},{8,12},{9,5},{12,14},{13,9},{14,10},{15,13... | collective-permute-start | bytes 3145736 | tf_op jit(solution)/shard_map/ppermute | solution.py:377
  28.4 13.4 %collective-permute-start.7 = (bf16[256,2048]{1,0:T(8,128)(2,1)S(1)}, bf16[256,2048]{1,0:T(8,128)(2,1)S(1)}, u32[]{:S(2)}, u32[]{:S(2)}) collective-permute-start(bf16[256,2048]{1,0:T(8,128)(2,1)S(1)} %collective-permute-done.4.refs_1_), channel_id=1, source_target_pairs={{0,1},{1,0},{2,3},{3,2},{4,5},{5,4},{6,7},{7,6},{8,9},{9,8},{10,11... | collective-permute-start | bytes 3145736 | tf_op jit(solution)/shard_map/ppermute | solution.py:380
  28.4 22.5 %collective-permute-start.8 = (bf16[256,2048]{1,0:T(8,128)(2,1)S(1)}, bf16[256,2048]{1,0:T(8,128)(2,1)S(1)}, u32[]{:S(2)}, u32[]{:S(2)}) collective-permute-start(bf16[256,2048]{1,0:T(8,128)(2,1)S(1)} %collective-permute-done.4.refs_1_), channel_id=1, source_target_pairs={{0,4},{1,3},{4,8},{5,1},{8,12},{9,5},{12,14},{13,9},{14,10},{15,13... | collective-permute-start | bytes 3145736 | tf_op jit(solution)/shard_map/ppermute | solution.py:377
  39.6 13.4 %collective-permute-start.9 = (bf16[256,2048]{1,0:T(8,128)(2,1)S(1)}, bf16[256,2048]{1,0:T(8,128)(2,1)S(1)}, u32[]{:S(2)}, u32[]{:S(2)}) collective-permute-start(bf16[256,2048]{1,0:T(8,128)(2,1)S(1)} %collective-permute-done.6.refs_1_), channel_id=1, source_target_pairs={{0,1},{1,0},{2,3},{3,2},{4,5},{5,4},{6,7},{7,6},{8,9},{9,8},{10,11... | collective-permute-start | bytes 3145736 | tf_op jit(solution)/shard_map/ppermute | solution.py:380
  39.6 22.5 %collective-permute-start.10 = (bf16[256,2048]{1,0:T(8,128)(2,1)S(1)}, bf16[256,2048]{1,0:T(8,128)(2,1)S(1)}, u32[]{:S(2)}, u32[]{:S(2)}) collective-permute-start(bf16[256,2048]{1,0:T(8,128)(2,1)S(1)} %collective-permute-done.6.refs_1_), channel_id=1, source_target_pairs={{0,4},{1,3},{4,8},{5,1},{8,12},{9,5},{12,14},{13,9},{14,10},{15,13... | collective-permute-start | bytes 3145736 | tf_op jit(solution)/shard_map/ppermute | solution.py:377
  50.8 15.1 %collective-permute-start.11 = (bf16[256,2048]{1,0:T(8,128)(2,1)S(1)}, bf16[256,2048]{1,0:T(8,128)(2,1)S(1)}, u32[]{:S(2)}, u32[]{:S(2)}) collective-permute-start(bf16[256,2048]{1,0:T(8,128)(2,1)S(1)} %collective-permute-done.8.refs_1_), channel_id=1, source_target_pairs={{0,1},{1,0},{2,3},{3,2},{4,5},{5,4},{6,7},{7,6},{8,9},{9,8},{10,11... | collective-permute-start | bytes 3145736 | tf_op jit(solution)/shard_map/ppermute | solution.py:380
  50.8 22.5 %collective-permute-start.12 = (bf16[256,2048]{1,0:T(8,128)(2,1)S(1)}, bf16[256,2048]{1,0:T(8,128)(2,1)S(1)}, u32[]{:S(2)}, u32[]{:S(2)}) collective-permute-start(bf16[256,2048]{1,0:T(8,128)(2,1)S(1)} %collective-permute-done.8.refs_1_), channel_id=1, source_target_pairs={{0,4},{1,3},{4,8},{5,1},{8,12},{9,5},{12,14},{13,9},{14,10},{15,13... | collective-permute-start | bytes 3145736 | tf_op jit(solution)/shard_map/ppermute | solution.py:377
  62.1 13.8 %collective-permute-start.13 = (bf16[256,2048]{1,0:T(8,128)(2,1)S(1)}, bf16[256,2048]{1,0:T(8,128)(2,1)S(1)}, u32[]{:S(2)}, u32[]{:S(2)}) collective-permute-start(bf16[256,2048]{1,0:T(8,128)(2,1)S(1)} %collective-permute-done.10.refs_1_.block), channel_id=1, source_target_pairs={{0,1},{1,0},{2,3},{3,2},{4,5},{5,4},{6,7},{7,6},{8,9},{9,8},{10,11... | collective-permute-start | bytes 3145736 | tf_op jit(solution)/shard_map/ppermute | solution.py:380
  62.1 16.8 %collective-permute-start.14 = (bf16[64,2048]{1,0:T(8,128)(2,1)S(1)}, bf16[64,2048]{1,0:T(8,128)(2,1)S(1)}, u32[]{:S(2)}, u32[]{:S(2)}) collective-permute-start(bf16[64,2048]{1,0:T(8,128)(2,1)S(1)} %get-tuple-element.80), channel_id=1, source_target_pairs={{0,4},{1,3},{4,8},{5,1},{8,12},{9,5},{12,14},{13,9},{14,10},{15,13... | collective-permute-start | bytes 786440 | tf_op jit(solution)/shard_map/ppermute | solution.py:377
  64.3 14.6 %collective-permute-start.15 = (bf16[64,2048]{1,0:T(8,128)(2,1)S(1)}, bf16[64,2048]{1,0:T(8,128)(2,1)S(1)}, u32[]{:S(2)}, u32[]{:S(2)}) collective-permute-start(bf16[64,2048]{1,0:T(8,128)(2,1)S(1)} %get-tuple-element.81), channel_id=1, source_target_pairs={{0,4},{1,3},{4,8},{5,1},{8,12},{9,5},{12,14},{13,9},{14,10},{15,13... | collective-permute-start | bytes 786440 | tf_op jit(solution)/shard_map/ppermute | solution.py:377
  73.4 6.2 %collective-permute-start.19 = (bf16[128,2048]{1,0:T(8,128)(2,1)S(1)}, bf16[128,2048]{1,0:T(8,128)(2,1)S(1)}, u32[]{:S(2)}, u32[]{:S(2)}) collective-permute-start(bf16[128,2048]{1,0:T(8,128)(2,1)S(1)} %get-tuple-element.86), channel_id=1, source_target_pairs={{0,1},{1,0},{2,3},{3,2},{4,5},{5,4},{6,7},{7,6},{8,9},{9,8},{10,11... | collective-permute-start | bytes 1572872 | tf_op jit(solution)/shard_map/ppermute | solution.py:380
  73.5 11.1 %collective-permute-start.20 = (bf16[128,2048]{1,0:T(8,128)(2,1)S(1)}, bf16[128,2048]{1,0:T(8,128)(2,1)S(1)}, u32[]{:S(2)}, u32[]{:S(2)}) collective-permute-start(bf16[128,2048]{1,0:T(8,128)(2,1)S(1)} %get-tuple-element.90), channel_id=1, source_target_pairs={{0,4},{1,3},{4,8},{5,1},{8,12},{9,5},{12,14},{13,9},{14,10},{15,13... | collective-permute-start | bytes 1572872 | tf_op jit(solution)/shard_map/ppermute | solution.py:377
  78.9 2.9 %collective-permute-start.17 = (bf16[64,2048]{1,0:T(8,128)(2,1)S(1)}, bf16[64,2048]{1,0:T(8,128)(2,1)S(1)}, u32[]{:S(2)}, u32[]{:S(2)}) collective-permute-start(bf16[64,2048]{1,0:T(8,128)(2,1)S(1)} %collective-permute-done.14.refs_1_), channel_id=1, source_target_pairs={{0,1},{1,0},{2,3},{3,2},{4,5},{5,4},{6,7},{7,6},{8,9},{9,8},{10,11... | collective-permute-start | bytes 786440 | tf_op jit(solution)/shard_map/ppermute | solution.py:380
  79.0 2.9 %collective-permute-start.18 = (bf16[64,2048]{1,0:T(8,128)(2,1)S(1)}, bf16[64,2048]{1,0:T(8,128)(2,1)S(1)}, u32[]{:S(2)}, u32[]{:S(2)}) collective-permute-start(bf16[64,2048]{1,0:T(8,128)(2,1)S(1)} %collective-permute-done.15.refs_2_), channel_id=1, source_target_pairs={{0,1},{1,0},{2,3},{3,2},{4,5},{5,4},{6,7},{7,6},{8,9},{9,8},{10,11... | collective-permute-start | bytes 786440 | tf_op jit(solution)/shard_map/ppermute | solution.py:380
  79.5 5.0 %collective-permute-start.16 = (bf16[128,2048]{1,0:T(8,128)(2,1)S(1)}, bf16[128,2048]{1,0:T(8,128)(2,1)S(1)}, u32[]{:S(2)}, u32[]{:S(2)}) collective-permute-start(bf16[128,2048]{1,0:T(8,128)(2,1)S(1)} %get-tuple-element.83), channel_id=1, source_target_pairs={{0,1},{1,0},{2,3},{3,2},{4,5},{5,4},{6,7},{7,6},{8,9},{9,8},{10,11... | collective-permute-start | bytes 1572872 | tf_op jit(solution)/shard_map/ppermute | solution.py:380
  84.5 15.1 %copy-start.5 = (s32[128,8]{0,1:T(8,128)S(1)}, s32[128,8]{0,1:T(8,128)}, u32[]{:S(2)}) copy-start(s32[128,8]{0,1:T(8,128)} %param.12) | copy-start | bytes 12292
  84.5 1.9 %collective-permute-start.21 = (bf16[128,2048]{1,0:T(8,128)(2,1)S(1)}, bf16[128,2048]{1,0:T(8,128)(2,1)S(1)}, u32[]{:S(2)}, u32[]{:S(2)}) collective-permute-start(bf16[128,2048]{1,0:T(8,128)(2,1)S(1)} %collective-permute-done.20.refs_2_), channel_id=1, source_target_pairs={{0,1},{1,0},{2,3},{3,2},{4,5},{5,4},{6,7},{7,6},{8,9},{9,8},{10,11... | collective-permute-start | bytes 1572872 | tf_op jit(solution)/shard_map/ppermute | solution.py:380
